TPU v7x, 32 devices: a whole 2x2x4 slice. The times are simulated.
32 devices in a mesh: gx: 4 (over x, core), gy: 4 (over z), gz: 2 (over y).
Axes of the slice: x: 2, y: 2, z: 4, core: 2. Of those that a mesh axis runs over, the one named last changes fastest.
Arguments:
- features: bfloat16 [4, 4, 2, 64, 3200], P('gx', 'gy', 'gz'), may hold values from -6 to 6
- positions: float32 [4, 4, 2, 3, 64], P('gx', 'gy', 'gz'), as said below
- neighbours: int32 [4, 4, 2, 64, 32], P('gx', 'gy', 'gz'), may hold values from 0 to 575, as said below
- counts: int32 [4, 4, 2, 64], P('gx', 'gy', 'gz'), may hold values from 8 to 32, as said below
- cell_atoms: int32 [4, 4, 2, 64], P('gx', 'gy', 'gz'), may hold values from 0 to 63, as said below
- rbf_weight: bfloat16 [512, 128], replicated, may hold values from -3 to 3
- radial_weight: bfloat16 [128, 640], replicated, may hold values from -0.5 to 0.5
- mix_weight: bfloat16 [5, 128, 128], replicated, may hold values from -0.5 to 0.5
- out_weight: bfloat16 [5, 128, 128], replicated, may hold values from -1 to 1
- energy_weight: float32 [128], replicated, may hold values from -0.5 to 0.5
- norm_weight: float32 [4, 128], replicated, may hold values from -0.5 to 0.5
Outputs:
- new_features: bfloat16 [4, 4, 2, 64, 3200], P('gx', 'gy', 'gz')
- energies: float32 [4, 4, 2, 64], P('gx', 'gy', 'gz')
- forces: float32 [4, 4, 2, 3, 64], P('gx', 'gy', 'gz')
Inputs may be any that keep to these rules, and one draw needn't show every extreme that they name: `positions`: the atom cell_atoms[q] of cell slot q = 8 c + r lies within 0.2 of the lattice site (2 cx + rx + 0.5, 2 cy + ry + 0.5, 2 cz + rz + 0.5) of its box. `neighbours`: the first 16 slots of atom i name other atoms of its domain (rows 0 to 63, never i); the rest name rows 64 + 8 e + r of extended cells e = ((ex 4 + ey) (4) + ez) that touch atom i's cell and lie outside the domain. `counts`: atom 0 of every domain has all 32 slots live. `cell_atoms`: A permutation of the domain's atoms.
All inputs are finite; a program needn't handle non-finite values.
Results may differ from a plain program's by a relative error of at most 0.012.
Values may be sent and summed in bfloat16 or wider, within the bound.
No kernel may reach another device: no remote copies, remote signals or barrier semaphores. Data moves between devices by JAX's collectives and lax.ppermute only.
A program may use at most 64 MiB of HBM per device.

v0:
```python
from functools import partial
import math

import jax
import jax.numpy as jnp
import numpy as np
from jax import lax
from jax.sharding import PartitionSpec as P


def padded(shard, sides, width):
    for axis, dim in sides:
        peers, length = (lax.axis_size(axis), shard.shape[dim])
        up = [(i, (i + 1) % peers) for i in range(peers)]
        down = [(j, i) for i, j in up]
        last = lax.slice_in_dim(shard, length - width, length, axis=dim)
        first = lax.slice_in_dim(shard, 0, width, axis=dim)
        before = lax.ppermute(last, axis, up)
        after = lax.ppermute(first, axis, down)
        shard = jnp.concatenate([before, shard, after], axis=dim)
    return shard


def degree_of(coeff_total):
    top_degree = int(math.isqrt(coeff_total)) - 1
    return np.array(
        [degree for degree in range(top_degree + 1) for _ in range(2 * degree + 1)], dtype=np.int32
    )


def product(pattern, first_op, second_op):
    return jnp.einsum(pattern, first_op, second_op, preferred_element_type=jnp.float32)


def degree_matmul(values, weights, flipped):
    edge_rows, coefficients, channels = values.shape
    degrees = weights.shape[0]
    pieces = []
    for degree in range(degrees):
        width = 2 * degree + 1
        block = values[:, degree * degree : degree * degree + width, :].reshape(
            edge_rows * width, channels
        )
        if flipped:
            result = lax.dot_general(
                block, weights[degree], (((1,), (1,)), ((), ())), preferred_element_type=jnp.float32
            )
        else:
            result = jnp.dot(block, weights[degree], preferred_element_type=jnp.float32)
        pieces.append(result.reshape(edge_rows, width, channels))
    return jnp.concatenate(pieces, axis=1)


def image_shifts(zcells):
    depth = 2 * zcells
    side_x = [-4.0, 0.0, 0.0, 4.0]
    side_z = [-float(depth)] + [0.0] * zcells + [float(depth)]
    table = [
        [
            [
                [[side_x[ex], side_x[ey], side_z[ez]][comp] for ez in range(zcells + 2)]
                for ey in range(4)
            ]
            for ex in range(4)
        ]
        for comp in range(3)
    ]
    return jnp.asarray(table, jnp.float32)


def block_step(
    table_feat,
    table_places,
    rbf_weight,
    radial_weight,
    mix_weight,
    out_weight,
    energy_weight,
    norm_expanded,
    reach_max,
    grad_table,
    block,
):
    own_feat, own_places, neigh_rows, live_counts = block
    atom_rows, slot_count = neigh_rows.shape
    channels = energy_weight.shape[0]
    coefficients = own_feat.shape[1] // channels
    degrees = radial_weight.shape[1] // channels
    edge_rows = atom_rows * slot_count
    flat_rows = neigh_rows.reshape(edge_rows)
    near_feat = jnp.take(table_feat, flat_rows, axis=0).reshape(edge_rows, coefficients, channels)
    near_places = jnp.take(table_places, flat_rows, axis=1)
    relative = near_places - jnp.repeat(own_places, slot_count, axis=1)
    distance = jnp.sqrt(jnp.sum(relative * relative, axis=0))
    nbasis = rbf_weight.shape[0]
    spacing = reach_max / (nbasis - 1)
    centred = (
        distance[:, None] - spacing * jnp.arange(nbasis, dtype=jnp.float32)[None, :]
    ) / spacing
    basis_vals = jnp.exp(-0.5 * centred * centred)
    preact = product("eb,bh->eh", basis_vals.astype(jnp.bfloat16), rbf_weight)
    hidden = jax.nn.silu(preact).astype(jnp.bfloat16)
    radial = product("eh,hf->ef", hidden, radial_weight).reshape(edge_rows, degrees, channels)
    scaled = jnp.concatenate(
        [
            near_feat[:, degree * degree : (degree + 1) * (degree + 1), :]
            * radial[:, degree : degree + 1, :]
            for degree in range(degrees)
        ],
        axis=1,
    ).astype(jnp.bfloat16)
    mixed = degree_matmul(scaled, mix_weight, False)
    gating = jax.nn.sigmoid(mixed[:, :1, :])
    message = mixed * gating
    live_mask = (jnp.arange(slot_count, dtype=jnp.int32)[None, :] < live_counts[:, None]).astype(
        jnp.float32
    )
    norm_scale = 1.0 / math.sqrt(slot_count)
    summed = (
        jnp.sum(
            message.reshape(atom_rows, slot_count, coefficients, channels)
            * live_mask[:, :, None, None],
            axis=1,
        )
        * norm_scale
    )
    updated = own_feat.reshape(atom_rows, coefficients, channels).astype(
        jnp.float32
    ) + degree_matmul(summed.astype(jnp.bfloat16), out_weight, False)
    scalar_part = updated[:, 0, :]
    energy = jnp.sum(energy_weight[None, :] * jax.nn.silu(scalar_part), axis=1) + jnp.sum(
        norm_expanded[None] * updated * updated, axis=(1, 2)
    )
    logistic = jax.nn.sigmoid(scalar_part)
    grad_updated = jnp.concatenate(
        [
            (energy_weight[None, :] * logistic * (1.0 + scalar_part * (1.0 - logistic)))[
                :, None, :
            ],
            2.0 * norm_expanded[None, 1:, :] * updated[:, 1:, :],
        ],
        axis=1,
    )
    grad_summed = degree_matmul(grad_updated.astype(jnp.bfloat16), out_weight, True) * norm_scale
    grad_message = (grad_summed[:, None, :, :] * live_mask[:, :, None, None]).reshape(
        edge_rows, coefficients, channels
    )
    grad_first = grad_message[:, :1, :] * gating * (
        1.0 + mixed[:, :1, :] * (1.0 - gating)
    ) + jnp.sum(grad_message[:, 1:, :] * mixed[:, 1:, :], axis=1, keepdims=True) * gating * (
        1.0 - gating
    )
    grad_mixed = jnp.concatenate([grad_first, grad_message[:, 1:, :] * gating], axis=1).astype(
        jnp.bfloat16
    )
    grad_scaled = degree_matmul(grad_mixed, mix_weight, True)
    weighted = grad_scaled * near_feat
    grad_radial = jnp.stack(
        [
            jnp.sum(weighted[:, degree * degree : (degree + 1) * (degree + 1), :], axis=1)
            for degree in range(degrees)
        ],
        axis=1,
    )
    grad_hidden = product(
        "ef,hf->eh",
        grad_radial.reshape(edge_rows, degrees * channels).astype(jnp.bfloat16),
        radial_weight,
    )
    logistic_pre = jax.nn.sigmoid(preact)
    grad_preact = grad_hidden * logistic_pre * (1.0 + preact * (1.0 - logistic_pre))
    grad_basis = product("eh,bh->eb", grad_preact.astype(jnp.bfloat16), rbf_weight)
    grad_dist = jnp.sum(grad_basis * basis_vals * centred, axis=1) * (-1.0 / spacing)
    pull_vec = relative * (grad_dist / distance)[None, :]
    grad_own = -jnp.sum(pull_vec.reshape(3, atom_rows, slot_count), axis=2)
    grad_table = grad_table.at[:, flat_rows].add(pull_vec)
    return (
        grad_table,
        (
            updated.reshape(atom_rows, coefficients * channels).astype(jnp.bfloat16),
            energy,
            grad_own,
        ),
    )


def domain_layer(
    own_feat,
    own_places,
    ghost_feat,
    ghost_places,
    neigh_rows,
    live_counts,
    rbf_weight,
    radial_weight,
    mix_weight,
    out_weight,
    energy_weight,
    norm_weight,
):
    atom_rows = own_feat.shape[0]
    channels = energy_weight.shape[0]
    coefficients = own_feat.shape[1] // channels
    table_deg = degree_of(coefficients)
    upper_deg = table_deg[1:]
    divisor = jnp.asarray(2 * upper_deg + 1, jnp.float32)
    norm_expanded = jnp.concatenate(
        [jnp.zeros((1, channels), jnp.float32), norm_weight[upper_deg - 1] / divisor[:, None]],
        axis=0,
    )
    table_feat = jnp.concatenate([own_feat, ghost_feat], axis=0)
    table_places = jnp.concatenate([own_places, ghost_places], axis=1)
    blocks = atom_rows // 8
    layer_depth = atom_rows // 16
    reach_max = 2.0 * math.sqrt(32.0 + layer_depth * layer_depth)
    scanned = (
        own_feat.reshape(blocks, 8, -1),
        jnp.transpose(own_places.reshape(3, blocks, 8), (1, 0, 2)),
        neigh_rows.reshape(blocks, 8, -1),
        live_counts.reshape(blocks, 8),
    )
    advance = partial(
        block_step,
        table_feat,
        table_places,
        rbf_weight,
        radial_weight,
        mix_weight,
        out_weight,
        energy_weight,
        norm_expanded,
        reach_max,
    )
    grad_table, (updated, energy, grad_own) = lax.scan(
        advance, jnp.zeros(table_places.shape, jnp.float32), scanned
    )
    grad_own = jnp.transpose(grad_own, (1, 0, 2)).reshape(3, atom_rows) + grad_table[:, :atom_rows]
    return (
        updated.reshape(atom_rows, -1),
        energy.reshape(atom_rows),
        grad_own,
        grad_table[:, atom_rows:],
    )


def fold_axis(received, axis, count):
    middle = lax.slice_in_dim(received, 2, count + 2, axis=axis)
    lower = lax.slice_in_dim(received, 0, 1, axis=axis)
    upper = lax.slice_in_dim(received, count + 3, count + 4, axis=axis)
    widths_low = [(0, 0)] * received.ndim
    widths_high = [(0, 0)] * received.ndim
    widths_low[axis] = (0, count - 1)
    widths_high[axis] = (count - 1, 0)
    return middle + jnp.pad(lower, widths_low) + jnp.pad(upper, widths_high)


def local(
    features,
    positions,
    neighbours,
    counts,
    cell_atoms,
    rbf_weight,
    radial_weight,
    mix_weight,
    out_weight,
    energy_weight,
    norm_weight,
):
    atom_rows = features.shape[3]
    zcells = atom_rows // 32
    order = cell_atoms[0, 0, 0]
    own_feat = features[0, 0, 0]
    own_places = positions[0, 0, 0]
    cell_feat = jnp.take(own_feat, order, axis=0).reshape(2, 2, zcells, 8, -1)
    cell_places = jnp.take(own_places, order, axis=1).reshape(3, 2, 2, zcells, 8)
    ghost_feat = padded(cell_feat, (("gx", 0), ("gy", 1), ("gz", 2)), 1)
    ghost_places = padded(cell_places, (("gx", 1), ("gy", 2), ("gz", 3)), 1)
    ghost_places = (ghost_places + image_shifts(zcells)[..., None]).reshape(3, -1)
    updated, energy, grad_own, grad_ghost = domain_layer(
        own_feat,
        own_places,
        ghost_feat.reshape(-1, own_feat.shape[1]),
        ghost_places,
        neighbours[0, 0, 0],
        counts[0, 0, 0],
        rbf_weight,
        radial_weight,
        mix_weight,
        out_weight,
        energy_weight,
        norm_weight,
    )
    grad_blocks = grad_ghost.reshape(3, 4, 4, zcells + 2, 8)
    returned = padded(grad_blocks, (("gx", 1), ("gy", 2), ("gz", 3)), 1)
    cell_grad = fold_axis(fold_axis(fold_axis(returned, 1, 2), 2, 2), 3, zcells).reshape(
        3, atom_rows
    )
    onehot = (order[:, None] == jnp.arange(atom_rows, dtype=jnp.int32)[None, :]).astype(jnp.float32)
    back_own = jnp.sum(cell_grad[:, :, None] * onehot[None], axis=1)
    forces = -(grad_own + back_own)
    return (updated[None, None, None], energy[None, None, None], forces[None, None, None])


def solution(mesh):
    return jax.shard_map(
        local,
        mesh=mesh,
        in_specs=(
            P("gx", "gy", "gz", None, None),
            P("gx", "gy", "gz", None, None),
            P("gx", "gy", "gz", None, None),
            P("gx", "gy", "gz", None),
            P("gx", "gy", "gz", None),
            P(),
            P(),
            P(),
            P(),
            P(),
            P(),
        ),
        out_specs=(
            P("gx", "gy", "gz", None, None),
            P("gx", "gy", "gz", None),
            P("gx", "gy", "gz", None, None),
        ),
        check_vma=False,
    )
```

profile of v0, /device:TPU:0, one launch (start us, length us, event | category | flops | bytes accessed | tf_op | source)
XLA Modules:
  0.0 439.8 jit_solution(16397635624979777882)
XLA Ops:
  7.9 2.3 gather_fusion.3
  11.2 4.3 collective-permute-done.7
  15.5 2.8 collective-permute-done.6
  23.3 3.8 collective-permute-start.3
  27.1 5.6 %collective-permute-done.8 = bf16[4,1,2,8,3200]{4,3,2,1,0:T(8,128)(2,1)S(1)} collective-permute-done((bf16[4,1,2,8,3200]{4,3,2,1,0:T(8,128)(2,1)S(1)}, bf16[4,1,2,8,3200]{4,3,2,1,0:T(8,128)(2,1)S(1)}, u32[]{:S(2)}, u32[]{:S(2)}) %collective-permute-start.8) | collective-permute-done | bytes 409632 | tf_op jit(solution)/shard_map/ppermute | solution.py:18
  32.8 7.8 %collective-permute-done.9 = bf16[4,1,2,8,3200]{4,3,2,1,0:T(8,128)(2,1)S(1)} collective-permute-done((bf16[4,1,2,8,3200]{4,3,2,1,0:T(8,128)(2,1)S(1)}, bf16[4,1,2,8,3200]{4,3,2,1,0:T(8,128)(2,1)S(1)}, u32[]{:S(2)}, u32[]{:S(2)}) %collective-permute-start.9) | collective-permute-done | bytes 409632 | tf_op jit(solution)/shard_map/ppermute | solution.py:19
  48.0 32.1 %collective-permute-done.4 = f32[3,4,4,1,8]{4,1,3,2,0:T(4,128)S(1)} collective-permute-done((f32[3,4,4,1,8]{4,1,3,2,0:T(4,128)}, f32[3,4,4,1,8]{4,1,3,2,0:T(4,128)S(1)}, u32[]{:S(2)}, u32[]{:S(2)}) %collective-permute-start.4) | collective-permute-done | bytes 1568 | tf_op jit(solution)/shard_map/ppermute | solution.py:18
  85.4 335.1 %while.18 = (s32[]{:T(128)}, f32[3,576]{0,1:T(8,128)}, bf16[8,8,3200]{2,1,0:T(8,128)(2,1)}, f32[8,8]{1,0:T(8,128)}, f32[8,3,8]{2,1,0:T(4,128)}, /*index=5*/s32[8...) while((s32[]{:T(128)}, f32[3,576]{0,1:T(8,128)}, ...), condition=%wide.region_13.14_spmd, body=%wide.region_0.13_spmd.sunk | while | flops 601584384 | bytes 85508784 | solution.py:234
  93.2 5.9 %gather_fusion.1 = bf16[256,3200]{1,0:T(8,128)(2,1)S(1)} fusion(bf16[576,3200]{1,0:T(8,128)(2,1)} %get-tuple-element.552, s32[1024]{0:T(1024)S(1)} %pad_clamp_fusion.4), kind=kCustom, calls=%fused_computation.1.clone.1 | custom fusion | bytes 3277824 | tf_op jit(solution)/shard_map/while/body/eval_jaxpr/jit(_take)/gather | solution.py:91
  124.3 2.2 scatter_custom_fusion.5
  135.1 5.9 %gather_fusion.1 = bf16[256,3200]{1,0:T(8,128)(2,1)S(1)} fusion(bf16[576,3200]{1,0:T(8,128)(2,1)} %get-tuple-element.552, s32[1024]{0:T(1024)S(1)} %pad_clamp_fusion.4), kind=kCustom, calls=%fused_computation.1.clone.1 | custom fusion | bytes 3277824 | tf_op jit(solution)/shard_map/while/body/eval_jaxpr/jit(_take)/gather | solution.py:91
  166.2 2.2 scatter_custom_fusion.5
  177.0 5.9 %gather_fusion.1 = bf16[256,3200]{1,0:T(8,128)(2,1)S(1)} fusion(bf16[576,3200]{1,0:T(8,128)(2,1)} %get-tuple-element.552, s32[1024]{0:T(1024)S(1)} %pad_clamp_fusion.4), kind=kCustom, calls=%fused_computation.1.clone.1 | custom fusion | bytes 3277824 | tf_op jit(solution)/shard_map/while/body/eval_jaxpr/jit(_take)/gather | solution.py:91
  208.1 2.2 scatter_custom_fusion.5
  218.9 5.9 %gather_fusion.1 = bf16[256,3200]{1,0:T(8,128)(2,1)S(1)} fusion(bf16[576,3200]{1,0:T(8,128)(2,1)} %get-tuple-element.552, s32[1024]{0:T(1024)S(1)} %pad_clamp_fusion.4), kind=kCustom, calls=%fused_computation.1.clone.1 | custom fusion | bytes 3277824 | tf_op jit(solution)/shard_map/while/body/eval_jaxpr/jit(_take)/gather | solution.py:91
  250.0 2.2 scatter_custom_fusion.5
  260.8 5.9 %gather_fusion.1 = bf16[256,3200]{1,0:T(8,128)(2,1)S(1)} fusion(bf16[576,3200]{1,0:T(8,128)(2,1)} %get-tuple-element.552, s32[1024]{0:T(1024)S(1)} %pad_clamp_fusion.4), kind=kCustom, calls=%fused_computation.1.clone.1 | custom fusion | bytes 3277824 | tf_op jit(solution)/shard_map/while/body/eval_jaxpr/jit(_take)/gather | solution.py:91
  291.9 2.2 scatter_custom_fusion.5
  302.7 5.9 %gather_fusion.1 = bf16[256,3200]{1,0:T(8,128)(2,1)S(1)} fusion(bf16[576,3200]{1,0:T(8,128)(2,1)} %get-tuple-element.552, s32[1024]{0:T(1024)S(1)} %pad_clamp_fusion.4), kind=kCustom, calls=%fused_computation.1.clone.1 | custom fusion | bytes 3277824 | tf_op jit(solution)/shard_map/while/body/eval_jaxpr/jit(_take)/gather | solution.py:91
  333.8 2.2 scatter_custom_fusion.5
  344.6 5.9 %gather_fusion.1 = bf16[256,3200]{1,0:T(8,128)(2,1)S(1)} fusion(bf16[576,3200]{1,0:T(8,128)(2,1)} %get-tuple-element.552, s32[1024]{0:T(1024)S(1)} %pad_clamp_fusion.4), kind=kCustom, calls=%fused_computation.1.clone.1 | custom fusion | bytes 3277824 | tf_op jit(solution)/shard_map/while/body/eval_jaxpr/jit(_take)/gather | solution.py:91
  375.7 2.2 scatter_custom_fusion.5
  386.5 5.9 %gather_fusion.1 = bf16[256,3200]{1,0:T(8,128)(2,1)S(1)} fusion(bf16[576,3200]{1,0:T(8,128)(2,1)} %get-tuple-element.552, s32[1024]{0:T(1024)S(1)} %pad_clamp_fusion.4), kind=kCustom, calls=%fused_computation.1.clone.1 | custom fusion | bytes 3277824 | tf_op jit(solution)/shard_map/while/body/eval_jaxpr/jit(_take)/gather | solution.py:91
  417.6 2.2 scatter_custom_fusion.5
  (1427 shorter events, 309.1 us)
Async XLA Ops:
  0.6 21.9 %copy-start = (f32[4,128]{1,0:T(4,128)S(1)}, f32[4,128]{1,0:T(4,128)}, u32[]{:S(2)}) copy-start(f32[4,128]{1,0:T(4,128)} %param.27) | copy-start | bytes 6148
  4.8 18.3 %collective-permute-start = (f32[3,1,2,2,8]{4,1,3,2,0:T(1,128)S(1)}, f32[3,1,2,2,8]{4,1,3,2,0:T(1,128)S(1)}, u32[]{:S(2)}, u32[]{:S(2)}) collective-permute-start(f32[3,1,2,2,8]{4,1,3,2,0:T(1,128)S(1)} %get-tuple-element.371), channel_id=1, source_target_pairs={{0,8},{8,16},{16,24},{24,0},{1,9},{9,17},{17,25},{25,1},{2,10},{10... | collective-permute-start | bytes 1160 | tf_op jit(solution)/shard_map/ppermute | solution.py:18
  5.3 17.8 %collective-permute-start.1 = (f32[3,1,2,2,8]{4,1,3,2,0:T(1,128)S(1)}, f32[3,1,2,2,8]{4,1,3,2,0:T(1,128)S(1)}, u32[]{:S(2)}, u32[]{:S(2)}) collective-permute-start(f32[3,1,2,2,8]{4,1,3,2,0:T(1,128)S(1)} %get-tuple-element.372), channel_id=1, source_target_pairs={{8,0},{16,8},{24,16},{0,24},{9,1},{17,9},{25,17},{1,25},{10,2},{18... | collective-permute-start | bytes 1160 | tf_op jit(solution)/shard_map/ppermute | solution.py:19
  10.4 5.1 %collective-permute-start.7 = (bf16[1,2,2,8,3200]{4,3,2,1,0:T(8,128)(2,1)S(1)}, bf16[1,2,2,8,3200]{4,3,2,1,0:T(8,128)(2,1)S(1)}, u32[]{:S(2)}, u32[]{:S(2)}) collective-permute-start(bf16[1,2,2,8,3200]{4,3,2,1,0:T(8,128)(2,1)S(1)} %bitcast.410), channel_id=1, source_target_pairs={{8,0},{16,8},{24,16},{0,24},{9,1},{17,9},{25,17},{1,25},{10,2},{18... | collective-permute-start | bytes 614408 | tf_op jit(solution)/shard_map/ppermute | solution.py:19
  11.1 7.3 %collective-permute-start.6 = (bf16[1,2,2,8,3200]{4,3,2,1,0:T(8,128)(2,1)S(1)}, bf16[1,2,2,8,3200]{4,3,2,1,0:T(8,128)(2,1)S(1)}, u32[]{:S(2)}, u32[]{:S(2)}) collective-permute-start(bf16[1,2,2,8,3200]{4,3,2,1,0:T(8,128)(2,1)S(1)} %bitcast.409), channel_id=1, source_target_pairs={{0,8},{8,16},{16,24},{24,0},{1,9},{9,17},{17,25},{25,1},{2,10},{10... | collective-permute-start | bytes 614408 | tf_op jit(solution)/shard_map/ppermute | solution.py:18
  18.6 14.2 %collective-permute-start.8 = (bf16[4,1,2,8,3200]{4,3,2,1,0:T(8,128)(2,1)S(1)}, bf16[4,1,2,8,3200]{4,3,2,1,0:T(8,128)(2,1)S(1)}, u32[]{:S(2)}, u32[]{:S(2)}) collective-permute-start(bf16[4,1,2,8,3200]{4,3,2,1,0:T(8,128)(2,1)S(1)} %get-tuple-element.357), channel_id=1, source_target_pairs={{0,2},{2,4},{4,6},{6,0},{1,3},{3,5},{5,7},{7,1},{8,10},{10,12},{12... | collective-permute-start | bytes 1228808 | tf_op jit(solution)/shard_map/ppermute | solution.py:18
  20.4 20.1 %collective-permute-start.9 = (bf16[4,1,2,8,3200]{4,3,2,1,0:T(8,128)(2,1)S(1)}, bf16[4,1,2,8,3200]{4,3,2,1,0:T(8,128)(2,1)S(1)}, u32[]{:S(2)}, u32[]{:S(2)}) collective-permute-start(bf16[4,1,2,8,3200]{4,3,2,1,0:T(8,128)(2,1)S(1)} %get-tuple-element.358), channel_id=1, source_target_pairs={{2,0},{4,2},{6,4},{0,6},{3,1},{5,3},{7,5},{1,7},{10,8},{12,10},{14... | collective-permute-start | bytes 1228808 | tf_op jit(solution)/shard_map/ppermute | solution.py:19
  23.2 21.0 %collective-permute-start.2 = (f32[3,4,1,2,8]{4,1,3,2,0:T(4,128)S(1)}, f32[3,4,1,2,8]{4,1,3,2,0:T(4,128)S(1)}, u32[]{:S(2)}, u32[]{:S(2)}) collective-permute-start(f32[3,4,1,2,8]{4,1,3,2,0:T(4,128)S(1)} %get-tuple-element.369), channel_id=1, source_target_pairs={{0,2},{2,4},{4,6},{6,0},{1,3},{3,5},{5,7},{7,1},{8,10},{10,12},{12... | collective-permute-start | bytes 2312 | tf_op jit(solution)/shard_map/ppermute | solution.py:18
  23.2 23.7 %copy-start.49 = (f32[24]{0:T(128)S(1)}, f32[24]{0:T(128)}, u32[]{:S(2)}) copy-start(f32[24]{0:T(128)} %constant.188) | copy-start | bytes 292
  23.3 23.8 %copy-start.51 = (s32[1,1,1,64]{3,2,1,0:T(1,128)S(1)}, s32[1,1,1,64]{3,2,1,0:T(1,128)}, u32[]{:S(2)}) copy-start(s32[1,1,1,64]{3,2,1,0:T(1,128)} %param.20) | copy-start | bytes 772
  23.3 24.5 %copy-start.45 = (f32[1,1,1,3,64]{4,2,3,1,0:T(1,128)S(1)}, f32[1,1,1,3,64]{4,2,3,1,0:T(1,128)}, u32[]{:S(2)}) copy-start(f32[1,1,1,3,64]{4,2,3,1,0:T(1,128)} %param.18) | copy-start | bytes 2308
  23.3 24.6 %copy-start.43 = (s32[1,1,1,64,32]{3,4,2,1,0:T(8,128)S(1)}, s32[1,1,1,64,32]{3,4,2,1,0:T(8,128)}, u32[]{:S(2)}) copy-start(s32[1,1,1,64,32]{3,4,2,1,0:T(8,128)} %param.19) | copy-start | bytes 24580
  23.3 57.1 %copy-start.42 = (f32[3,4,4,4]{3,2,1,0:T(4,128)S(1)}, f32[3,4,4,4]{3,2,1,0:T(4,128)}, u32[]{:S(2)}) copy-start(f32[3,4,4,4]{3,2,1,0:T(4,128)} %constant.171.clone) | copy-start | bytes 2308
  23.3 20.9 %collective-permute-start.3 = (f32[3,4,1,2,8]{4,1,3,2,0:T(4,128)S(1)}, f32[3,4,1,2,8]{4,1,3,2,0:T(4,128)S(1)}, u32[]{:S(2)}, u32[]{:S(2)}) collective-permute-start(f32[3,4,1,2,8]{4,1,3,2,0:T(4,128)S(1)} %get-tuple-element.370), channel_id=1, source_target_pairs={{2,0},{4,2},{6,4},{0,6},{3,1},{5,3},{7,5},{1,7},{10,8},{12,10},{14... | collective-permute-start | bytes 2312 | tf_op jit(solution)/shard_map/ppermute | solution.py:19
  42.2 39.5 %collective-permute-start.10 = (bf16[4,4,1,8,3200]{4,3,2,1,0:T(8,128)(2,1)}, bf16[4,4,1,8,3200]{4,3,2,1,0:T(8,128)(2,1)S(1)}, u32[]{:S(2)}, u32[]{:S(2)}) collective-permute-start(bf16[4,4,1,8,3200]{4,3,2,1,0:T(8,128)(2,1)} %get-tuple-element.355), channel_id=1, source_target_pairs={{0,1},{1,0},{2,3},{3,2},{4,5},{5,4},{6,7},{7,6},{8,9},{9,8},{10,11... | collective-permute-start | bytes 2457608 | tf_op jit(solution)/shard_map/ppermute | solution.py:18
  43.8 37.9 %collective-permute-start.11 = (bf16[4,4,1,8,3200]{4,3,2,1,0:T(8,128)(2,1)}, bf16[4,4,1,8,3200]{4,3,2,1,0:T(8,128)(2,1)S(1)}, u32[]{:S(2)}, u32[]{:S(2)}) collective-permute-start(bf16[4,4,1,8,3200]{4,3,2,1,0:T(8,128)(2,1)} %get-tuple-element.356), channel_id=1, source_target_pairs={{1,0},{0,1},{3,2},{2,3},{5,4},{4,5},{7,6},{6,7},{9,8},{8,9},{11,10... | collective-permute-start | bytes 2457608 | tf_op jit(solution)/shard_map/ppermute | solution.py:19
  44.9 35.3 %collective-permute-start.4 = (f32[3,4,4,1,8]{4,1,3,2,0:T(4,128)}, f32[3,4,4,1,8]{4,1,3,2,0:T(4,128)S(1)}, u32[]{:S(2)}, u32[]{:S(2)}) collective-permute-start(f32[3,4,4,1,8]{4,1,3,2,0:T(4,128)} %get-tuple-element.367), channel_id=1, source_target_pairs={{0,1},{1,0},{2,3},{3,2},{4,5},{5,4},{6,7},{7,6},{8,9},{9,8},{10,11... | collective-permute-start | bytes 4616 | tf_op jit(solution)/shard_map/ppermute | solution.py:18
  46.5 33.9 %collective-permute-start.5 = (f32[3,4,4,1,8]{4,1,3,2,0:T(4,128)}, f32[3,4,4,1,8]{4,1,3,2,0:T(4,128)S(1)}, u32[]{:S(2)}, u32[]{:S(2)}) collective-permute-start(f32[3,4,4,1,8]{4,1,3,2,0:T(4,128)} %get-tuple-element.368), channel_id=1, source_target_pairs={{1,0},{0,1},{3,2},{2,3},{5,4},{4,5},{7,6},{6,7},{9,8},{8,9},{11,10... | collective-permute-start | bytes 4616 | tf_op jit(solution)/shard_map/ppermute | solution.py:19
  422.0 3.5 collective-permute-start.12
  422.1 3.4 collective-permute-start.13
  425.6 5.8 %collective-permute-start.14 = (f32[3,6,1,4,8]{4,3,2,1,0:T(4,128)S(1)}, f32[3,6,1,4,8]{4,3,2,1,0:T(4,128)S(1)}, u32[]{:S(2)}, u32[]{:S(2)}) collective-permute-start(f32[3,6,1,4,8]{4,3,2,1,0:T(4,128)S(1)} %get-tuple-element.363), channel_id=1, source_target_pairs={{0,2},{2,4},{4,6},{6,0},{1,3},{3,5},{5,7},{7,1},{8,10},{10,12},{12... | collective-permute-start | bytes 6920 | tf_op jit(solution)/shard_map/ppermute | solution.py:18
  427.4 4.3 collective-permute-start.15
  431.9 6.0 %collective-permute-start.16 = (f32[3,6,6,1,8]{4,3,2,1,0:T(1,128)S(1)}, f32[3,6,6,1,8]{4,3,2,1,0:T(1,128)S(1)}, u32[]{:S(2)}, u32[]{:S(2)}) collective-permute-start(f32[3,6,6,1,8]{4,3,2,1,0:T(1,128)S(1)} %get-tuple-element.361), channel_id=1, source_target_pairs={{0,1},{1,0},{2,3},{3,2},{4,5},{5,4},{6,7},{7,6},{8,9},{9,8},{10,11... | collective-permute-start | bytes 10376 | tf_op jit(solution)/shard_map/ppermute | solution.py:18
  433.5 4.4 %collective-permute-start.17 = (f32[3,6,6,1,8]{4,3,2,1,0:T(1,128)S(1)}, f32[3,6,6,1,8]{4,3,2,1,0:T(1,128)S(1)}, u32[]{:S(2)}, u32[]{:S(2)}) collective-permute-start(f32[3,6,6,1,8]{4,3,2,1,0:T(1,128)S(1)} %get-tuple-element.362), channel_id=1, source_target_pairs={{1,0},{0,1},{3,2},{2,3},{5,4},{4,5},{7,6},{6,7},{9,8},{8,9},{11,10... | collective-permute-start | bytes 10376 | tf_op jit(solution)/shard_map/ppermute | solution.py:19
  (347 other events, 1373.1 us)
where the time goes:
time: 446 us; the launch traced here: 440 us
  local copies, waits for them, and re-layouts  144 us (32%)
  other arithmetic  106 us (24%)
  matrix products  102 us (23%)
  waiting for transfers between devices  56.9 us (13%)
  starting transfers between devices  22.9 us (5%)
  loops' own time  6.46 us (1%)
    gather x16, local copies, waits for them, and re-layouts, block_step(): jnp.take(table_feat, flat_rows, axis=0)  59.2 us
    dot_general x80, matrix products, degree_matmul(): lax.dot_general(block, weights[degree], (((1,), (1,)), ((), ())), preferr...  46.2 us
    ppermute x9, waiting for transfers between devices, padded(): before = lax.ppermute(last, axis, up)  44.2 us
    dot_general x24, matrix products, product(): jnp.einsum(pattern, first_op, second_op, preferred_element_type=jnp.float32)  32.4 us
    while x752, local copies, waits for them, and re-layouts  24.9 us
    dot_general x80, matrix products, degree_matmul(): result = jnp.dot(block, weights[degree], preferred_element_type=jnp.float32)  23.8 us
    scatter-add x8, other arithmetic, block_step(): grad_table = grad_table.at[:, flat_rows].add(pull_vec)  17.6 us
    dynamic_update_slice x16, local copies, waits for them, and re-layouts, domain_layer(): lax.scan(advance, jnp.zeros(table_places.shape, jnp.float32), scanned)  15.1 us
  transfers between devices with their start and end apart: 18, of which 9 were waited for; matrix products, arithmetic and copies ran while one was open for 3% of the time, Pallas kernels for 0%

commit v1 on v0

v1 whole, which is shorter than its diff:
```python
import math

import jax
import jax.numpy as jnp
from jax import lax
from jax.experimental import pallas as pl
from jax.experimental.pallas import tpu as pltpu
from jax.sharding import PartitionSpec as P

F32 = jnp.float32
BF16 = jnp.bfloat16
CH = 128
PAIRS = 12
OWN_ROWS = 256
GH_ROWS = 128
VMEM = 56 * 1024 * 1024


def mm(a, b):
    return jnp.dot(a, b, preferred_element_type=F32)


def mm_nt(a, b):
    return lax.dot_general(a, b, (((1,), (1,)), ((), ())), preferred_element_type=F32)


def iota(shape, dim):
    return lax.broadcasted_iota(jnp.int32, shape, dim)


def flip(w):
    return w.astype(F32).T.astype(BF16)


def cells_kernel(feat_ref, pos_ref, meta_ref, cells_ref, own_pos_ref, rows_ref):
    atoms, feat = feat_ref.shape
    rows_ref[...] = jnp.zeros_like(rows_ref)
    places = pos_ref[...]
    first = places.astype(BF16).astype(F32)
    second = (places - first).astype(BF16).astype(F32)
    third = places - first - second
    rows_ref[0:3, :] = first
    rows_ref[4:7, :] = second
    rows_ref[8:11, :] = third
    pieces = rows_ref[...].astype(BF16)
    lane = iota((atoms, atoms), 1)
    pick = (meta_ref[:, 33:34] == lane).astype(BF16)
    same = (iota((atoms, atoms), 0) == lane).astype(BF16)
    own_pos_ref[...] = mm_nt(same, pieces).astype(BF16)
    cells_ref[:, feat:] = mm_nt(pick, pieces).astype(BF16)
    for at in range(0, feat, 640):
        cells_ref[:, at : at + 640] = mm(pick, feat_ref[:, at : at + 640]).astype(BF16)


def make_cells(feats, places, meta):
    atoms, feat = feats.shape
    return pl.pallas_call(
        cells_kernel,
        out_shape=(
            jax.ShapeDtypeStruct((atoms, feat + CH), BF16),
            jax.ShapeDtypeStruct((atoms, CH), BF16),
        ),
        scratch_shapes=[pltpu.VMEM((CH, atoms), F32)],
        name="cells",
    )(feats, places, meta)


def degrees_of(pair):
    low = 1 + (pair >= 2) + (pair >= 4) + (pair >= 8)
    high = 1 + (pair >= 1) + (pair >= 4) + (pair >= 7)
    kind = (pair >= 1) + (pair >= 2) + (pair >= 4) + (pair >= 7) + (pair >= 8)
    return low, high, kind


KINDS = ((1, 1), (1, 2), (2, 2), (3, 3), (3, 4), (4, 4))


def degrees_dyn(pair):
    def over(at):
        return (pair >= at).astype(jnp.int32)

    low = 1 + over(2) + over(4) + over(8)
    high = 1 + over(1) + over(4) + over(7)
    kind = over(1) + over(2) + over(4) + over(7) + over(8)
    return low, high, kind


def layer_kernel(
    own_ref,
    own_pos_ref,
    gh_ref,
    meta_ref,
    rbf_ref,
    rad_ref,
    mix_ref,
    out_ref,
    ew_ref,
    nw_ref,
    new_ref,
    en_ref,
    fown_ref,
    fgh_ref,
    oh_own,
    oh_gh,
    d_gh,
    dt_gh,
    unit_s,
    bc_s,
    pre_s,
    radial_s,
    nf0_s,
    m0_s,
    gate_s,
    dot_s,
    gr_s,
    nf_s,
    mx_s,
    wm,
    wmt,
    wo,
    wot,
    radt,
    rbft,
    nw2,
    ghpos,
    acc_s,
    gs_s,
    gs0_s,
    en_s,
    src_s,
    fo_s,
):
    atoms = own_ref.shape[0]
    feat = own_ref.shape[1]
    slots = 32
    half = slots // 2
    own_edges = atoms * half
    ghosts = gh_ref.shape[0]
    nbasis = rbf_ref.shape[0]
    depth = atoms // 16
    spacing = 2.0 * math.sqrt(32.0 + depth * depth) / (nbasis - 1)
    norm = 1.0 / math.sqrt(slots)
    per_step = OWN_ROWS // atoms
    own_steps = own_edges // OWN_ROWS

    wm[...] = jnp.zeros_like(wm)
    wmt[...] = jnp.zeros_like(wmt)
    wo[...] = jnp.zeros_like(wo)
    wot[...] = jnp.zeros_like(wot)
    for degree in range(5):
        mix = mix_ref[degree]
        out = out_ref[degree]
        mix_t = flip(mix)
        out_t = flip(out)
        if degree == 0:
            wm[6, 0:CH, 0:CH] = mix
            wmt[6, 0:CH, 0:CH] = mix_t
            wo[6, 0:CH, 0:CH] = out
            wot[6, 0:CH, 0:CH] = out_t
        for kind, both in enumerate(KINDS):
            for side in range(2):
                if both[side] == degree:
                    part = slice(side * CH, side * CH + CH)
                    wm[kind, part, part] = mix
                    wmt[kind, part, part] = mix_t
                    wo[kind, part, part] = out
                    wot[kind, part, part] = out_t
    for degree in range(5):
        radt[degree * CH : (degree + 1) * CH, :] = flip(
            rad_ref[:, degree * CH : (degree + 1) * CH]
        )
    for part in range(nbasis // CH):
        rbft[:, part * CH : (part + 1) * CH] = flip(rbf_ref[part * CH : (part + 1) * CH, :])
    for kind, both in enumerate(KINDS):
        for side in range(2):
            degree = both[side]
            nw2[kind, :, side * CH : (side + 1) * CH] = nw_ref[degree - 1 : degree, :] * (
                1.0 / (2 * degree + 1)
            )

    counts = meta_ref[:, 32:33]
    lane_atom = iota((atoms, atoms), 1)
    for slot in range(half):
        hit = jnp.logical_and(meta_ref[:, slot : slot + 1] == lane_atom, counts > slot)
        oh_own[slot * atoms : (slot + 1) * atoms, :] = hit.astype(F32).astype(BF16)

    live = jnp.maximum(counts - half, 0).astype(F32)
    sub_atom = iota((atoms, atoms), 0)
    live_b = jnp.broadcast_to(live, (atoms, atoms))
    end_row = jnp.sum(jnp.where(sub_atom <= lane_atom, live_b, 0.0), axis=0, keepdims=True)
    live_row = jnp.sum(jnp.where(sub_atom == lane_atom, live_b, 0.0), axis=0, keepdims=True)
    start_row = end_row - live_row
    end_col = jnp.sum(
        jnp.where(lane_atom <= sub_atom, jnp.broadcast_to(live_row, (atoms, atoms)), 0.0),
        axis=1,
        keepdims=True,
    )
    start_col = end_col - live
    total = jnp.sum(live)
    gh_steps = (total.astype(jnp.int32) + (GH_ROWS - 1)) // GH_ROWS
    ghost_row = meta_ref[:, half:slots] - atoms
    row_high = (ghost_row // 16).astype(F32).astype(BF16)
    row_low = (ghost_row % 16).astype(F32).astype(BF16)

    row = iota((ghosts, CH), 0)
    lane = iota((ghosts, CH), 1)
    zcells = atoms // 32
    per_y = (zcells + 2) * 8
    ext_x = row // (4 * per_y)
    ext_y = row // per_y % 4
    ext_z = row // 8 % (zcells + 2)

    def side_of(ext, last, size):
        return jnp.where(ext == 0, -size, jnp.where(ext == last, size, 0.0))

    shift = jnp.where(lane == 12, side_of(ext_x, 3, 4.0), 0.0)
    shift = jnp.where(lane == 13, side_of(ext_y, 3, 4.0), shift)
    shift = jnp.where(lane == 14, side_of(ext_z, zcells + 1, 2.0 * zcells), shift)
    ghpos[...] = (gh_ref[:, feat:].astype(F32) + shift).astype(BF16)

    def geometry(rows, near, here):
        diff = near - here
        rel = (diff + pltpu.roll(diff, CH - 4, 1)) + (
            pltpu.roll(diff, CH - 8, 1) + pltpu.roll(diff, CH - 12, 1)
        )
        rel = jnp.where(iota(rel.shape, 1) < 3, rel, 0.0)
        square = jnp.sum(rel * rel, axis=1, keepdims=True)
        inverse = lax.rsqrt(jnp.where(square > 0.0, square, 1.0))
        unit_s[rows, :] = rel * inverse
        dist = square * inverse
        centred = dist * (1.0 / spacing) - iota((rel.shape[0], nbasis), 1).astype(F32)
        basis = jnp.exp(-0.5 * centred * centred)
        bc_s[rows, :] = basis * centred
        pre = mm(basis.astype(BF16), rbf_ref[...])
        pre_s[rows, :] = pre
        hidden = (pre * jax.nn.sigmoid(pre)).astype(BF16)
        radial = mm(hidden, rad_ref[...])
        for degree in range(5):
            radial_s[degree, rows, :] = radial[:, degree * CH : (degree + 1) * CH]

    def forward0(rows, onehot, table):
        near = mm(onehot, table)
        scaled = (near * radial_s[0, rows, :]).astype(BF16)
        mixed = mm(scaled, wm[6, 0:CH, 0:CH])
        gate = jax.nn.sigmoid(mixed)
        nf0_s[rows, :] = near
        m0_s[rows, :] = mixed
        gate_s[rows, :] = gate
        dot_s[rows, :] = jnp.zeros_like(gate)
        for degree in range(1, 5):
            gr_s[degree, rows, :] = jnp.zeros_like(gate)
        return mixed * gate

    def over_slots(values):
        return jnp.sum(values.reshape(per_step, atoms, values.shape[1]), axis=0)

    def tiled(values):
        return jnp.concatenate([values] * per_step, axis=0)

    own_pos = own_pos_ref[...].astype(F32)
    own0 = own_ref[:, 0:CH]
    total0 = jnp.zeros((atoms, CH), F32)
    for step in range(own_steps):
        rows = pl.ds(step * OWN_ROWS, OWN_ROWS)
        onehot = oh_own[rows, :]
        geometry(rows, mm(onehot, own_pos_ref[...]), tiled(own_pos))
        total0 += over_slots(forward0(rows, onehot, own0))
    acc_s[:, 0:CH] = total0

    def ghost_start(step, carry):
        base = pl.multiple_of(step * GH_ROWS, GH_ROWS)
        here = pl.ds(base, GH_ROWS)
        rows = pl.ds(pl.multiple_of(own_edges + base, GH_ROWS), GH_ROWS)
        edge = (iota((GH_ROWS, atoms), 0) + base).astype(F32)
        mine = jnp.logical_and(edge >= start_row, edge < end_row).astype(F32)
        source = mine.astype(BF16)
        d_gh[here, :] = source
        edge_t = (iota((atoms, GH_ROWS), 1) + base).astype(F32)
        mine_t = jnp.logical_and(edge_t >= start_col, edge_t < end_col)
        dt_gh[step, :, :] = mine_t.astype(F32).astype(BF16)
        edge_col = edge[:, 0:1]
        slot = edge_col - jnp.sum(mine * start_row, axis=1, keepdims=True)
        listed = mm(source, row_high) * 16.0 + mm(source, row_low)
        at_slot = iota((GH_ROWS, half), 1).astype(F32) == slot
        which = jnp.sum(jnp.where(at_slot, listed, 0.0), axis=1, keepdims=True)
        which = jnp.where(edge_col < total, which, -1.0)
        onehot = (iota((GH_ROWS, ghosts), 1).astype(F32) == which).astype(F32).astype(BF16)
        oh_gh[here, :] = onehot
        geometry(rows, mm(onehot, ghpos[...]), mm(source, own_pos_ref[...]))
        message = forward0(rows, onehot, gh_ref[:, 0:CH])
        acc_s[:, 0:CH] += mm(dt_gh[step], message.astype(BF16))
        return carry

    lax.fori_loop(0, gh_steps, ghost_start, 0)

    low0 = (acc_s[:, 0:CH] * norm).astype(BF16)
    updated0 = own0.astype(F32) + mm(low0, wo[6, 0:CH, 0:CH])
    new_ref[:, 0:CH] = updated0.astype(BF16)
    logistic = jax.nn.sigmoid(updated0)
    weight0 = ew_ref[...]
    en_s[...] = weight0 * updated0 * logistic
    grad0 = (weight0 * logistic * (1.0 + updated0 * (1.0 - logistic))).astype(BF16)
    gs0_s[...] = mm(grad0, wot[6, 0:CH, 0:CH]) * norm

    def forward(rows, onehot, table, low, high, weight):
        near = mm(onehot, table)
        nf_s[rows, :] = near.astype(BF16)
        left = near[:, 0:CH] * radial_s[low, rows, :]
        right = near[:, CH:] * radial_s[high, rows, :]
        scaled = jnp.concatenate([left, right], axis=1).astype(BF16)
        mixed = mm(scaled, weight)
        mx_s[rows, :] = mixed.astype(BF16)
        gate = gate_s[rows, :]
        return mixed * jnp.concatenate([gate, gate], axis=1)

    def backward(rows, grad, low, high, weight_t):
        gate = gate_s[rows, :]
        product = grad * mx_s[rows, :].astype(F32)
        dot_s[rows, :] += product[:, 0:CH] + product[:, CH:]
        grad_mixed = (grad * jnp.concatenate([gate, gate], axis=1)).astype(BF16)
        weighted = mm(grad_mixed, weight_t) * nf_s[rows, :].astype(F32)
        gr_s[low, rows, :] += weighted[:, 0:CH]
        gr_s[high, rows, :] += weighted[:, CH:]

    def pair_step(pair, carry):
        low, high, kind = degrees_dyn(pair)
        cols = pl.ds(pl.multiple_of(CH + pair * 2 * CH, CH), 2 * CH)
        own = own_ref[:, cols]
        weight = wm[kind]
        summed = jnp.zeros((atoms, 2 * CH), F32)
        for step in range(own_steps):
            rows = pl.ds(step * OWN_ROWS, OWN_ROWS)
            summed += over_slots(forward(rows, oh_own[rows, :], own, low, high, weight))
        acc_s[...] = summed

        def ghost_forward(step, inner):
            base = pl.multiple_of(step * GH_ROWS, GH_ROWS)
            rows = pl.ds(pl.multiple_of(own_edges + base, GH_ROWS), GH_ROWS)
            message = forward(
                rows, oh_gh[pl.ds(base, GH_ROWS), :], gh_ref[:, cols], low, high, wm[kind]
            )
            acc_s[...] += mm(dt_gh[step], message.astype(BF16))
            return inner

        lax.fori_loop(0, gh_steps, ghost_forward, 0)

        summed_low = (acc_s[...] * norm).astype(BF16)
        updated = own.astype(F32) + mm(summed_low, wo[kind])
        new_ref[:, cols] = updated.astype(BF16)
        scale = nw2[kind] * updated
        energy = scale * updated
        en_s[...] += energy[:, 0:CH] + energy[:, CH:]
        grad_summed = mm((2.0 * scale).astype(BF16), wot[kind]) * norm
        gs_s[...] = grad_summed.astype(BF16)
        weight_t = wmt[kind]
        grad_tiled = tiled(grad_summed)
        for step in range(own_steps):
            rows = pl.ds(step * OWN_ROWS, OWN_ROWS)
            backward(rows, grad_tiled, low, high, weight_t)

        def ghost_backward(step, inner):
            base = pl.multiple_of(step * GH_ROWS, GH_ROWS)
            rows = pl.ds(pl.multiple_of(own_edges + base, GH_ROWS), GH_ROWS)
            grad = mm(d_gh[pl.ds(base, GH_ROWS), :], gs_s[...])
            backward(rows, grad, low, high, wmt[kind])
            return inner

        lax.fori_loop(0, gh_steps, ghost_backward, 0)
        return carry

    lax.fori_loop(0, PAIRS, pair_step, 0)

    def finish(rows, grad):
        gate = gate_s[rows, :]
        first = grad * gate * (1.0 + m0_s[rows, :] * (1.0 - gate)) + dot_s[rows, :] * gate * (
            1.0 - gate
        )
        weighted = mm(first.astype(BF16), wmt[6, 0:CH, 0:CH]) * nf0_s[rows, :]
        radial_grad = jnp.concatenate(
            [weighted] + [gr_s[degree, rows, :] for degree in range(1, 5)], axis=1
        ).astype(BF16)
        hidden_grad = mm(radial_grad, radt[...])
        pre = pre_s[rows, :]
        logistic_pre = jax.nn.sigmoid(pre)
        pre_grad = (hidden_grad * logistic_pre * (1.0 + pre * (1.0 - logistic_pre))).astype(BF16)
        basis_grad = mm(pre_grad, rbft[...])
        dist_grad = jnp.sum(basis_grad * bc_s[rows, :], axis=1, keepdims=True) * (-1.0 / spacing)
        pull = unit_s[rows, :] * dist_grad
        across = pull.T[0:8, :]
        top = across.astype(BF16)
        rest = (across - top.astype(F32)).astype(BF16)
        return pull, top, rest

    grad0_tiled = tiled(gs0_s[...])
    src = jnp.zeros((atoms, CH), F32)
    onto = jnp.zeros((8, atoms), F32)
    for step in range(own_steps):
        rows = pl.ds(step * OWN_ROWS, OWN_ROWS)
        pull, top, rest = finish(rows, grad0_tiled)
        src += over_slots(pull)
        onehot = oh_own[rows, :]
        onto += mm(top, onehot) + mm(rest, onehot)
    src_s[...] = src
    fgh_ref[...] = jnp.zeros_like(fgh_ref)
    gs_s[:, 0:CH] = gs0_s[...].astype(BF16)

    def ghost_finish(step, carry):
        base = pl.multiple_of(step * GH_ROWS, GH_ROWS)
        here = pl.ds(base, GH_ROWS)
        rows = pl.ds(pl.multiple_of(own_edges + base, GH_ROWS), GH_ROWS)
        grad = mm(d_gh[here, :], gs_s[:, 0:CH])
        pull, top, rest = finish(rows, grad)
        pull_top = pull.astype(BF16)
        pull_rest = (pull - pull_top.astype(F32)).astype(BF16)
        spread = dt_gh[step]
        src_s[...] += mm(spread, pull_top) + mm(spread, pull_rest)
        onehot = oh_gh[here, :]
        fgh_ref[...] += mm(top, onehot) + mm(rest, onehot)
        return carry

    lax.fori_loop(0, gh_steps, ghost_finish, 0)
    fown_ref[...] = onto - src_s[...].T[0:8, :]
    en_ref[...] = jnp.sum(en_s[...].T, axis=0, keepdims=True)


def layer(feats, own_pos, ghost, meta, rbf, rad, mix, out, ew, nw):
    atoms, feat = feats.shape
    ghosts = ghost.shape[0]
    edges = atoms * 32
    half = edges // 2
    nbasis = rbf.shape[0]
    scratch = [
        pltpu.VMEM((half, atoms), BF16),
        pltpu.VMEM((half, ghosts), BF16),
        pltpu.VMEM((half, atoms), BF16),
        pltpu.VMEM((half // GH_ROWS, atoms, GH_ROWS), BF16),
        pltpu.VMEM((edges, CH), F32),
        pltpu.VMEM((edges, nbasis), F32),
        pltpu.VMEM((edges, CH), F32),
        pltpu.VMEM((5, edges, CH), F32),
        pltpu.VMEM((edges, CH), F32),
        pltpu.VMEM((edges, CH), F32),
        pltpu.VMEM((edges, CH), F32),
        pltpu.VMEM((edges, CH), F32),
        pltpu.VMEM((5, edges, CH), F32),
        pltpu.VMEM((edges, 2 * CH), BF16),
        pltpu.VMEM((edges, 2 * CH), BF16),
        pltpu.VMEM((7, 2 * CH, 2 * CH), BF16),
        pltpu.VMEM((7, 2 * CH, 2 * CH), BF16),
        pltpu.VMEM((7, 2 * CH, 2 * CH), BF16),
        pltpu.VMEM((7, 2 * CH, 2 * CH), BF16),
        pltpu.VMEM((5 * CH, CH), BF16),
        pltpu.VMEM((CH, nbasis), BF16),
        pltpu.VMEM((6, 1, 2 * CH), F32),
        pltpu.VMEM((ghosts, CH), BF16),
        pltpu.VMEM((atoms, 2 * CH), F32),
        pltpu.VMEM((atoms, 2 * CH), BF16),
        pltpu.VMEM((atoms, CH), F32),
        pltpu.VMEM((atoms, CH), F32),
        pltpu.VMEM((atoms, CH), F32),
        pltpu.VMEM((8, atoms), F32),
    ]
    return pl.pallas_call(
        layer_kernel,
        out_shape=(
            jax.ShapeDtypeStruct((atoms, feat), BF16),
            jax.ShapeDtypeStruct((1, atoms), F32),
            jax.ShapeDtypeStruct((8, atoms), F32),
            jax.ShapeDtypeStruct((8, ghosts), F32),
        ),
        scratch_shapes=scratch,
        compiler_params=pltpu.CompilerParams(vmem_limit_bytes=VMEM),
        name="layer",
    )(feats, own_pos, ghost, meta, rbf, rad, mix, out, ew, nw)


def halo(block, axis, dim):
    peers, length = lax.axis_size(axis), block.shape[dim]
    up = [(i, (i + 1) % peers) for i in range(peers)]
    down = [(j, i) for i, j in up]
    last = lax.slice_in_dim(block, length - 1, length, axis=dim)
    first = lax.slice_in_dim(block, 0, 1, axis=dim)
    if peers == 2 and length == 2:
        other = lax.ppermute(block, axis, up)
        before = lax.slice_in_dim(other, length - 1, length, axis=dim)
        after = lax.slice_in_dim(other, 0, 1, axis=dim)
    else:
        before = lax.ppermute(last, axis, up)
        after = lax.ppermute(first, axis, down)
    return jnp.concatenate([before, block, after], axis=dim)


def fold(block, axis, dim):
    peers, length = lax.axis_size(axis), block.shape[dim]
    up = [(i, (i + 1) % peers) for i in range(peers)]
    down = [(j, i) for i, j in up]
    to_upper = lax.slice_in_dim(block, length - 1, length, axis=dim)
    to_lower = lax.slice_in_dim(block, 0, 1, axis=dim)
    from_lower = lax.ppermute(to_upper, axis, up)
    from_upper = lax.ppermute(to_lower, axis, down)
    first = lax.slice_in_dim(block, 1, 2, axis=dim) + from_lower
    last = lax.slice_in_dim(block, length - 2, length - 1, axis=dim) + from_upper
    inner = lax.slice_in_dim(block, 2, length - 2, axis=dim)
    return jnp.concatenate([first, inner, last], axis=dim)


def local(
    features,
    positions,
    neighbours,
    counts,
    cell_atoms,
    rbf_weight,
    radial_weight,
    mix_weight,
    out_weight,
    energy_weight,
    norm_weight,
):
    atoms = features.shape[3]
    zcells = atoms // 32
    feats = features[0, 0, 0]
    places = positions[0, 0, 0]
    order = cell_atoms[0, 0, 0]
    meta = jnp.concatenate(
        [neighbours[0, 0, 0], counts[0, 0, 0][:, None], order[:, None]], axis=1
    )
    cells, own_pos = make_cells(feats, places, meta)
    ghost = cells.reshape(2, 2, zcells, 8, -1)
    ghost = halo(ghost, "gz", 2)
    ghost = halo(ghost, "gy", 1)
    ghost = halo(ghost, "gx", 0)
    new, energy, grad_own, grad_ghost = layer(
        feats,
        own_pos,
        ghost.reshape(-1, ghost.shape[-1]),
        meta,
        rbf_weight,
        radial_weight,
        mix_weight,
        out_weight,
        energy_weight[None],
        norm_weight,
    )
    grads = grad_ghost[0:3].reshape(3, 4, 4, zcells + 2, 8)
    grads = fold(grads, "gx", 1)
    grads = fold(grads, "gy", 2)
    grads = fold(grads, "gz", 3)
    onehot = (order[:, None] == jnp.arange(atoms, dtype=jnp.int32)[None, :]).astype(F32)
    back = jnp.sum(grads.reshape(3, atoms)[:, :, None] * onehot[None], axis=1)
    forces = -(grad_own[0:3] + back)
    return (new[None, None, None], energy[None, None], forces[None, None, None])


def solution(mesh):
    split = P("gx", "gy", "gz", None, None)
    flat = P("gx", "gy", "gz", None)
    return jax.shard_map(
        local,
        mesh=mesh,
        in_specs=(split, split, split, flat, flat, P(), P(), P(), P(), P(), P()),
        out_specs=(split, flat, split),
        check_vma=False,
    )
```

time: 446 us -> 160 us (0.36); the launches traced: 440 us -> 160 us
  local copies, waits for them, and re-layouts: 144 us -> 5.29 us
  matrix products: 102 us -> 0 us
  other arithmetic: 106 us -> 5.07 us
  Pallas kernels: 0 us -> 61.5 us
  waiting for transfers between devices: 56.9 us -> 70.8 us
  starting transfers between devices: 22.9 us -> 16.1 us
  loops' own time: 6.46 us -> 0 us
    dot_general x184 -> x0, matrix products: 102 us -> none  [the longest x80 46.2 us: degree_matmul(): lax.dot_general(block, weights[degree], (((1,), (1,)), ((), ())), preferr...]
    gather x28 -> x0, local copies, waits for them, and re-layouts: 76.2 us -> none  [the longest x16 59.2 us: block_step(): jnp.take(table_feat, flat_rows, axis=0)]
    pallas_call x0 -> x2, Pallas kernels: none -> 61.5 us  [the longest x1 59.4 us: layer(): pl.pallas_call(layer_kernel, out_shape=(jax.ShapeDtypeStruct((atoms, feat...]
    while x754 -> x0, local copies, waits for them, and re-layouts: 26.8 us -> none
    reduce_sum x73 -> x1, other arithmetic: 21.4 us -> 0.11 us  [local(): back = jnp.sum(grads.reshape(3, atoms)[:, :, None] * onehot[None], axis=1)]
    scatter-add x8 -> x0, other arithmetic: 17.6 us -> none  [block_step(): grad_table = grad_table.at[:, flat_rows].add(pull_vec)]
    dynamic_update_slice x16 -> x0, local copies, waits for them, and re-layouts: 15.1 us -> none  [domain_layer(): lax.scan(advance, jnp.zeros(table_places.shape, jnp.float32), scanned)]
    ppermute x18 -> x11, waiting for transfers between devices: 56.9 us -> 70.8 us  [the longest x2 28.1 us: halo(): after = lax.ppermute(first, axis, down)]
  transfers between devices with their start and end apart: 18 -> 11, of which waited for: 9 -> 11; matrix products, arithmetic and copies ran while one was open for 3% -> 0% of each run, Pallas kernels for 0% -> 0%
where the time goes in v1:
time: 160 us
  waiting for transfers between devices  70.8 us (44%)
  Pallas kernels  61.5 us (38%)
  starting transfers between devices  16.1 us (10%)
  local copies, waits for them, and re-layouts  5.29 us (3%)
  other arithmetic  5.07 us (3%)
    pallas_call x1, Pallas kernels, layer(): pl.pallas_call(layer_kernel, out_shape=(jax.ShapeDtypeStruct((atoms, feat...  59.4 us
    ppermute x2, waiting for transfers between devices, halo(): after = lax.ppermute(first, axis, down)  28.1 us
    ppermute x3, waiting for transfers between devices, fold(): from_lower = lax.ppermute(to_upper, axis, up)  15.2 us
    ppermute x2, waiting for transfers between devices, halo(): before = lax.ppermute(last, axis, up)  10.9 us
    ppermute x1, waiting for transfers between devices, halo(): other = lax.ppermute(block, axis, up)  10.1 us
    ppermute x3, waiting for transfers between devices, fold(): from_upper = lax.ppermute(to_lower, axis, down)  6.46 us
    ppermute x3, starting transfers between devices, fold(): from_lower = lax.ppermute(to_upper, axis, up)  6.06 us
    ppermute x2, starting transfers between devices, halo(): after = lax.ppermute(first, axis, down)  3.87 us
  transfers between devices with their start and end apart: 11, of which 11 were waited for; matrix products, arithmetic and copies ran while one was open for 0% of the time, Pallas kernels for 0%

profile of v1, /device:TPU:0, one launch (start us, length us, event | category | flops | bytes accessed | tf_op | source)
XLA Modules:
  0.0 159.6 jit_solution(6549934847205689238)
XLA Ops:
  0.6 1.3 copy.24
  1.9 0.7 copy.20
  3.4 0.8 copy.18
  4.9 2.1 %cells.1 = (bf16[64,3328]{1,0:T(8,128)(2,1)}, bf16[64,128]{1,0:T(8,128)(2,1)}) custom-call(bf16[64,3200]{1,0:T(8,128)(2,1)} %bitcast.20, f32[3,64]{1,0:T(4,128)} %bitcast.23, s32[64,34]{1,0:T(8,128)} %pad_add_fusion.meta_ref), custom_call_target="tpu_custom_call" | custom-call | tf_op jit(solution)/shard_map/cells/pallas_call | solution.py:57
  7.0 3.0 %collective-permute-start = (bf16[2,2,2,8,3328]{4,3,2,1,0:T(8,128)(2,1)}, bf16[2,2,2,8,3328]{4,3,2,1,0:T(8,128)(2,1)S(1)}, u32[]{:S(2)}, u32[]{:S(2)}) collective-permute-start(bf16[2,2,2,8,3328]{4,3,2,1,0:T(8,128)(2,1)} %bitcast.16), channel_id=1, source_target_pairs={{0,1},{1,0},{2,3},{3,2},{4,5},{5,4},{6,7},{7,6},{8,9},{9,8},{10,11... | collective-permute-start | bytes 1277960 | tf_op jit(solution)/shard_map/ppermute | solution.py:484
  10.0 10.1 %collective-permute-done = bf16[2,2,2,8,3328]{4,3,2,1,0:T(8,128)(2,1)S(1)} collective-permute-done((bf16[2,2,2,8,3328]{4,3,2,1,0:T(8,128)(2,1)}, bf16[2,2,2,8,3328]{4,3,2,1,0:T(8,128)(2,1)S(1)}, u32[]{:S(2)}, u32[]{:S(2)}) %collective-permute-start) | collective-permute-done | bytes 426016 | tf_op jit(solution)/shard_map/ppermute | solution.py:484
  20.1 1.1 pad_maximum_fusion.2
  21.3 3.8 %collective-permute-start.2 = (bf16[2,1,4,8,3328]{4,3,2,1,0:T(8,128)(2,1)S(1)}, bf16[2,1,4,8,3328]{4,3,2,1,0:T(8,128)(2,1)S(1)}, u32[]{:S(2)}, u32[]{:S(2)}) collective-permute-start(bf16[2,1,4,8,3328]{4,3,2,1,0:T(8,128)(2,1)S(1)} %get-tuple-element.24), channel_id=1, source_target_pairs={{2,0},{4,2},{6,4},{0,6},{3,1},{5,3},{7,5},{1,7},{10,8},{12,10},{14... | collective-permute-start | bytes 1277960 | tf_op jit(solution)/shard_map/ppermute | solution.py:489
  25.1 10.3 %collective-permute-done.2 = bf16[2,1,4,8,3328]{4,3,2,1,0:T(8,128)(2,1)S(1)} collective-permute-done((bf16[2,1,4,8,3328]{4,3,2,1,0:T(8,128)(2,1)S(1)}, bf16[2,1,4,8,3328]{4,3,2,1,0:T(8,128)(2,1)S(1)}, u32[]{:S(2)}, u32[]{:S(2)}) %collective-permute-start.2) | collective-permute-done | bytes 426016 | tf_op jit(solution)/shard_map/ppermute | solution.py:489
  35.4 8.0 %collective-permute-done.1 = bf16[2,1,4,8,3328]{4,3,2,1,0:T(8,128)(2,1)S(1)} collective-permute-done((bf16[2,1,4,8,3328]{4,3,2,1,0:T(8,128)(2,1)S(1)}, bf16[2,1,4,8,3328]{4,3,2,1,0:T(8,128)(2,1)S(1)}, u32[]{:S(2)}, u32[]{:S(2)}) %collective-permute-start.1) | collective-permute-done | bytes 426016 | tf_op jit(solution)/shard_map/ppermute | solution.py:488
  44.2 17.9 %collective-permute-done.4 = bf16[1,4,4,8,3328]{4,3,2,1,0:T(8,128)(2,1)S(1)} collective-permute-done((bf16[1,4,4,8,3328]{4,3,2,1,0:T(8,128)(2,1)S(1)}, bf16[1,4,4,8,3328]{4,3,2,1,0:T(8,128)(2,1)S(1)}, u32[]{:S(2)}, u32[]{:S(2)}) %collective-permute-start.4) | collective-permute-done | bytes 852000 | tf_op jit(solution)/shard_map/ppermute | solution.py:489
  62.1 2.9 %collective-permute-done.3 = bf16[1,4,4,8,3328]{4,3,2,1,0:T(8,128)(2,1)S(1)} collective-permute-done((bf16[1,4,4,8,3328]{4,3,2,1,0:T(8,128)(2,1)S(1)}, bf16[1,4,4,8,3328]{4,3,2,1,0:T(8,128)(2,1)S(1)}, u32[]{:S(2)}, u32[]{:S(2)}) %collective-permute-start.3) | collective-permute-done | bytes 852000 | tf_op jit(solution)/shard_map/ppermute | solution.py:488
  65.0 2.0 %pad_maximum_fusion = bf16[4,4,4,8,3328]{4,3,2,1,0:T(8,128)(2,1)} fusion(bf16[1,4,4,8,3328]{4,3,2,1,0:T(8,128)(2,1)S(1)} %collective-permute-done.4, bf16[2,1,4,8,3328]{4,3,2,1,0:T(8,128)(2,1)S(1)} %collective-permute-done.2, bf16[2,2,1,8,3328]{4,3,2,1,0:T(8,128)(2,1)S(1)} %get-tuple-element.26, bf16[2,2,2,8,3328]{4,3,2,1,0:T(8,128)(2,1)S(1)} %bitcast.19, ...), kind=kLoop, calls=%fused_computation | loop fusion | flops 10223616 | bytes 6815744 | tf_op jit(solution)/shard_map/concatenate | solution.py:490
  67.1 59.4 %layer.1 = (bf16[64,3200]{1,0:T(8,128)(2,1)}, f32[1,64]{1,0:T(1,128)}, f32[8,64]{1,0:T(8,128)}, f32[8,512]{1,0:T(8,128)}) custom-call(bf16[64,3200]{1,0:T(8,128)(2,1)} %bitcast.21, bf16[64,128]{1,0:T(8,128)(2,1)} %get-tuple-element.9.own_pos_ref, bf16[512,3328]{1,0:T(8,128)(2,1)} %bitcast.15, s32[64,34]{1,0:T(8,128)} %pad_add_fusion.meta_ref, ...), custom_call_target="tpu_custom_call" | custom-call | tf_op jit(solution)/shard_map/layer/pallas_call | solution.py:463
  127.5 11.9 %collective-permute-done.5 = f32[3,1,4,4,8]{4,3,2,1,0:T(4,128)S(1)} collective-permute-done((f32[3,1,4,4,8]{4,3,2,1,0:T(4,128)S(1)}, f32[3,1,4,4,8]{4,3,2,1,0:T(4,128)S(1)}, u32[]{:S(2)}, u32[]{:S(2)}) %collective-permute-start.5) | collective-permute-done | bytes 1568 | tf_op jit(solution)/shard_map/ppermute | solution.py:499
  139.5 1.5 collective-permute-done.6
  141.1 4.1 %collective-permute-start.7 = (f32[3,2,1,4,8]{4,3,2,1,0:T(4,128)S(1)}, f32[3,2,1,4,8]{4,3,2,1,0:T(4,128)S(1)}, u32[]{:S(2)}, u32[]{:S(2)}) collective-permute-start(f32[3,2,1,4,8]{4,3,2,1,0:T(4,128)S(1)} %fusion.5), channel_id=1, source_target_pairs={{0,2},{2,4},{4,6},{6,0},{1,3},{3,5},{5,7},{7,1},{8,10},{10,12},{12... | collective-permute-start | bytes 2312 | tf_op jit(solution)/shard_map/ppermute | solution.py:499
  145.2 1.4 collective-permute-done.7
  146.6 0.9 collective-permute-start.8
  147.5 3.1 %collective-permute-done.8 = f32[3,2,1,4,8]{4,3,2,1,0:T(4,128)S(1)} collective-permute-done((f32[3,2,1,4,8]{4,3,2,1,0:T(4,128)S(1)}, f32[3,2,1,4,8]{4,3,2,1,0:T(4,128)S(1)}, u32[]{:S(2)}, u32[]{:S(2)}) %collective-permute-start.8) | collective-permute-done | bytes 800 | tf_op jit(solution)/shard_map/ppermute | solution.py:500
  150.6 1.8 %collective-permute-start.9 = (f32[3,2,2,1,8]{4,3,2,1,0:T(1,128)S(1)}, f32[3,2,2,1,8]{4,3,2,1,0:T(1,128)S(1)}, u32[]{:S(2)}, u32[]{:S(2)}) collective-permute-start(f32[3,2,2,1,8]{4,3,2,1,0:T(1,128)S(1)} %fusion.10), channel_id=1, source_target_pairs={{0,1},{1,0},{2,3},{3,2},{4,5},{5,4},{6,7},{7,6},{8,9},{9,8},{10,11... | collective-permute-start | bytes 1160 | tf_op jit(solution)/shard_map/ppermute | solution.py:499
  152.4 1.9 %collective-permute-done.9 = f32[3,2,2,1,8]{4,3,2,1,0:T(1,128)S(1)} collective-permute-done((f32[3,2,2,1,8]{4,3,2,1,0:T(1,128)S(1)}, f32[3,2,2,1,8]{4,3,2,1,0:T(1,128)S(1)}, u32[]{:S(2)}, u32[]{:S(2)}) %collective-permute-start.9) | collective-permute-done | bytes 416 | tf_op jit(solution)/shard_map/ppermute | solution.py:499
  154.4 1.8 %collective-permute-start.10 = (f32[3,2,2,1,8]{4,3,2,1,0:T(1,128)S(1)}, f32[3,2,2,1,8]{4,3,2,1,0:T(1,128)S(1)}, u32[]{:S(2)}, u32[]{:S(2)}) collective-permute-start(f32[3,2,2,1,8]{4,3,2,1,0:T(1,128)S(1)} %get-tuple-element.32), channel_id=1, source_target_pairs={{1,0},{0,1},{3,2},{2,3},{5,4},{4,5},{7,6},{6,7},{9,8},{8,9},{11,10... | collective-permute-start | bytes 1160 | tf_op jit(solution)/shard_map/ppermute | solution.py:500
  156.2 1.8 %collective-permute-done.10 = f32[3,2,2,1,8]{4,3,2,1,0:T(1,128)S(1)} collective-permute-done((f32[3,2,2,1,8]{4,3,2,1,0:T(1,128)S(1)}, f32[3,2,2,1,8]{4,3,2,1,0:T(1,128)S(1)}, u32[]{:S(2)}, u32[]{:S(2)}) %collective-permute-start.10) | collective-permute-done | bytes 416 | tf_op jit(solution)/shard_map/ppermute | solution.py:500
  (32 shorter events, 5.2 us)
Async XLA Ops:
  7.0 36.3 %copy-start = (bf16[64,3328]{1,0:T(8,128)(2,1)S(1)}, bf16[64,3328]{1,0:T(8,128)(2,1)}, u32[]{:S(2)}) copy-start(bf16[64,3328]{1,0:T(8,128)(2,1)} %get-tuple-element.10) | copy-start | bytes 1277956
  7.0 13.1 %collective-permute-start = (bf16[2,2,2,8,3328]{4,3,2,1,0:T(8,128)(2,1)}, bf16[2,2,2,8,3328]{4,3,2,1,0:T(8,128)(2,1)S(1)}, u32[]{:S(2)}, u32[]{:S(2)}) collective-permute-start(bf16[2,2,2,8,3328]{4,3,2,1,0:T(8,128)(2,1)} %bitcast.16), channel_id=1, source_target_pairs={{0,1},{1,0},{2,3},{3,2},{4,5},{5,4},{6,7},{7,6},{8,9},{9,8},{10,11... | collective-permute-start | bytes 1277960 | tf_op jit(solution)/shard_map/ppermute | solution.py:484
  21.3 14.1 %collective-permute-start.2 = (bf16[2,1,4,8,3328]{4,3,2,1,0:T(8,128)(2,1)S(1)}, bf16[2,1,4,8,3328]{4,3,2,1,0:T(8,128)(2,1)S(1)}, u32[]{:S(2)}, u32[]{:S(2)}) collective-permute-start(bf16[2,1,4,8,3328]{4,3,2,1,0:T(8,128)(2,1)S(1)} %get-tuple-element.24), channel_id=1, source_target_pairs={{2,0},{4,2},{6,4},{0,6},{3,1},{5,3},{7,5},{1,7},{10,8},{12,10},{14... | collective-permute-start | bytes 1277960 | tf_op jit(solution)/shard_map/ppermute | solution.py:489
  25.1 18.2 %collective-permute-start.1 = (bf16[2,1,4,8,3328]{4,3,2,1,0:T(8,128)(2,1)S(1)}, bf16[2,1,4,8,3328]{4,3,2,1,0:T(8,128)(2,1)S(1)}, u32[]{:S(2)}, u32[]{:S(2)}) collective-permute-start(bf16[2,1,4,8,3328]{4,3,2,1,0:T(8,128)(2,1)S(1)} %get-tuple-element.23), channel_id=1, source_target_pairs={{0,2},{2,4},{4,6},{6,0},{1,3},{3,5},{5,7},{7,1},{8,10},{10,12},{12... | collective-permute-start | bytes 1277960 | tf_op jit(solution)/shard_map/ppermute | solution.py:488
  43.7 18.4 %collective-permute-start.4 = (bf16[1,4,4,8,3328]{4,3,2,1,0:T(8,128)(2,1)S(1)}, bf16[1,4,4,8,3328]{4,3,2,1,0:T(8,128)(2,1)S(1)}, u32[]{:S(2)}, u32[]{:S(2)}) collective-permute-start(bf16[1,4,4,8,3328]{4,3,2,1,0:T(8,128)(2,1)S(1)} %get-tuple-element.22), channel_id=1, source_target_pairs={{8,0},{16,8},{24,16},{0,24},{9,1},{17,9},{25,17},{1,25},{10,2},{18... | collective-permute-start | bytes 2555912 | tf_op jit(solution)/shard_map/ppermute | solution.py:489
  43.7 21.3 %collective-permute-start.3 = (bf16[1,4,4,8,3328]{4,3,2,1,0:T(8,128)(2,1)S(1)}, bf16[1,4,4,8,3328]{4,3,2,1,0:T(8,128)(2,1)S(1)}, u32[]{:S(2)}, u32[]{:S(2)}) collective-permute-start(bf16[1,4,4,8,3328]{4,3,2,1,0:T(8,128)(2,1)S(1)} %get-tuple-element.21), channel_id=1, source_target_pairs={{0,8},{8,16},{16,24},{24,0},{1,9},{9,17},{17,25},{25,1},{2,10},{10... | collective-permute-start | bytes 2555912 | tf_op jit(solution)/shard_map/ppermute | solution.py:488
  67.1 89.1 %copy-start.1 = (s32[1,1,1,64]{3,2,1,0:T(1,128)S(1)}, s32[1,1,1,64]{3,2,1,0:T(1,128)}, u32[]{:S(2)}) copy-start(s32[1,1,1,64]{3,2,1,0:T(1,128)} %param.15) | copy-start | bytes 772
  127.4 12.1 %collective-permute-start.5 = (f32[3,1,4,4,8]{4,3,2,1,0:T(4,128)S(1)}, f32[3,1,4,4,8]{4,3,2,1,0:T(4,128)S(1)}, u32[]{:S(2)}, u32[]{:S(2)}) collective-permute-start(f32[3,1,4,4,8]{4,3,2,1,0:T(4,128)S(1)} %slice.87), channel_id=1, source_target_pairs={{0,8},{8,16},{16,24},{24,0},{1,9},{9,17},{17,25},{25,1},{2,10},{10... | collective-permute-start | bytes 4616 | tf_op jit(solution)/shard_map/ppermute | solution.py:499
  139.5 1.6 collective-permute-start.6
  141.1 5.5 %collective-permute-start.7 = (f32[3,2,1,4,8]{4,3,2,1,0:T(4,128)S(1)}, f32[3,2,1,4,8]{4,3,2,1,0:T(4,128)S(1)}, u32[]{:S(2)}, u32[]{:S(2)}) collective-permute-start(f32[3,2,1,4,8]{4,3,2,1,0:T(4,128)S(1)} %fusion.5), channel_id=1, source_target_pairs={{0,2},{2,4},{4,6},{6,0},{1,3},{3,5},{5,7},{7,1},{8,10},{10,12},{12... | collective-permute-start | bytes 2312 | tf_op jit(solution)/shard_map/ppermute | solution.py:499
  146.6 4.0 %collective-permute-start.8 = (f32[3,2,1,4,8]{4,3,2,1,0:T(4,128)S(1)}, f32[3,2,1,4,8]{4,3,2,1,0:T(4,128)S(1)}, u32[]{:S(2)}, u32[]{:S(2)}) collective-permute-start(f32[3,2,1,4,8]{4,3,2,1,0:T(4,128)S(1)} %get-tuple-element.30), channel_id=1, source_target_pairs={{2,0},{4,2},{6,4},{0,6},{3,1},{5,3},{7,5},{1,7},{10,8},{12,10},{14... | collective-permute-start | bytes 2312 | tf_op jit(solution)/shard_map/ppermute | solution.py:500
  150.6 3.7 %collective-permute-start.9 = (f32[3,2,2,1,8]{4,3,2,1,0:T(1,128)S(1)}, f32[3,2,2,1,8]{4,3,2,1,0:T(1,128)S(1)}, u32[]{:S(2)}, u32[]{:S(2)}) collective-permute-start(f32[3,2,2,1,8]{4,3,2,1,0:T(1,128)S(1)} %fusion.10), channel_id=1, source_target_pairs={{0,1},{1,0},{2,3},{3,2},{4,5},{5,4},{6,7},{7,6},{8,9},{9,8},{10,11... | collective-permute-start | bytes 1160 | tf_op jit(solution)/shard_map/ppermute | solution.py:499
  154.4 3.7 %collective-permute-start.10 = (f32[3,2,2,1,8]{4,3,2,1,0:T(1,128)S(1)}, f32[3,2,2,1,8]{4,3,2,1,0:T(1,128)S(1)}, u32[]{:S(2)}, u32[]{:S(2)}) collective-permute-start(f32[3,2,2,1,8]{4,3,2,1,0:T(1,128)S(1)} %get-tuple-element.32), channel_id=1, source_target_pairs={{1,0},{0,1},{3,2},{2,3},{5,4},{4,5},{7,6},{6,7},{9,8},{8,9},{11,10... | collective-permute-start | bytes 1160 | tf_op jit(solution)/shard_map/ppermute | solution.py:500

commit v2 on v0

v2 whole, which is shorter than its diff:
```python
import functools
import math

import jax
import jax.numpy as jnp
from jax import lax
from jax.experimental import pallas as pl
from jax.experimental.pallas import tpu as pltpu
from jax.sharding import PartitionSpec as P

F32 = jnp.float32
BF16 = jnp.bfloat16
CH = 128
SLOTS = 32
HALF = 16
STEP = 256
OWN_STEPS = 4
GH_STEPS = 2
VMEM = 56 * 1024 * 1024
SPACE = pltpu.VMEM
PAIR_DEGREES = (
    (1, 1), (1, 2), (2, 2), (2, 2),
    (3, 3), (3, 3), (3, 3), (3, 4),
    (4, 4), (4, 4), (4, 4), (4, 4),
)
GROUPS = ((0, 4), (4, 8), (8, 12))


def mm(a, b):
    return jnp.dot(a, b, preferred_element_type=F32)


def mm_nt(a, b):
    return lax.dot_general(a, b, (((1,), (1,)), ((), ())), preferred_element_type=F32)


def iota(shape, dim):
    return lax.broadcasted_iota(jnp.int32, shape, dim)


def flip(w):
    return w.astype(F32).T.astype(BF16)


def pair_cols(pair):
    return slice(CH + pair * 2 * CH, CH + (pair + 1) * 2 * CH)


def struct(*shape, dtype=F32):
    return jax.ShapeDtypeStruct(shape, dtype)


def call(kernel, name, out_shape, scratch, flops, args, specs=None):
    size = sum(a.size * a.dtype.itemsize for a in list(args) + list(out_shape))
    return pl.pallas_call(
        kernel,
        out_shape=out_shape,
        in_specs=specs or [pl.BlockSpec(memory_space=SPACE)] * len(args),
        out_specs=tuple(pl.BlockSpec(memory_space=SPACE) for _ in out_shape),
        scratch_shapes=scratch,
        compiler_params=pltpu.CompilerParams(vmem_limit_bytes=VMEM),
        cost_estimate=pl.CostEstimate(flops=flops, bytes_accessed=size, transcendentals=0),
        name=name,
    )(*args)


def cells_kernel(feat_ref, pos_ref, near_ref, counts_ref, order_ref, *refs):
    out_refs, (own_pos_ref, meta_ref, rows_ref, pos_rows) = refs[:3], refs[3:]
    atoms = feat_ref.shape[0]
    rows_ref[...] = jnp.zeros_like(rows_ref)
    rows_ref[0:SLOTS, :] = near_ref[...].astype(F32)
    rows_ref[SLOTS : SLOTS + 1, :] = counts_ref[...].astype(F32)
    rows_ref[SLOTS + 1 : SLOTS + 2, :] = order_ref[...].astype(F32)
    meta = rows_ref[...].T
    meta_ref[...] = meta
    pos_rows[...] = jnp.zeros_like(pos_rows)
    for comp in range(3):
        places = pos_ref[comp]
        first = places.astype(BF16).astype(F32)
        second = (places - first).astype(BF16).astype(F32)
        pos_rows[comp : comp + 1, :] = first
        pos_rows[4 + comp : 5 + comp, :] = second
        pos_rows[8 + comp : 9 + comp, :] = places - first - second
    pieces = pos_rows[...].astype(BF16)
    lane = iota((atoms, atoms), 1).astype(F32)
    pick = (meta[:, SLOTS + 1 : SLOTS + 2] == lane).astype(F32).astype(BF16)
    same = (iota((atoms, atoms), 0) == iota((atoms, atoms), 1)).astype(F32).astype(BF16)
    own_pos_ref[...] = mm_nt(same, pieces).astype(BF16)
    for group, (begin, end) in enumerate(GROUPS):
        at = 0 if group == 0 else pair_cols(begin).start
        till = pair_cols(end - 1).stop
        out_refs[group][:, 0 : till - at] = mm(pick, feat_ref[:, at:till]).astype(BF16)
        if group == 0:
            out_refs[group][:, till:] = mm_nt(pick, pieces).astype(BF16)


def make_cells(feats, places, near, counts, order):
    atoms = feats.shape[0]
    widths = [CH * 2 * (end - begin) for begin, end in GROUPS]
    widths[0] += 2 * CH
    out_shape = tuple(struct(atoms, width, dtype=BF16) for width in widths) + (
        struct(atoms, CH, dtype=BF16),
        struct(atoms, CH),
    )
    scratch = [pltpu.VMEM((CH, atoms), F32), pltpu.VMEM((CH, atoms), F32)]
    args = (feats, places, near, counts, order)
    return call(cells_kernel, "cells", out_shape, scratch, 1 << 26, args)


def spacing_of(atoms, nbasis):
    depth = atoms // 16
    return 2.0 * math.sqrt(32.0 + depth * depth) / (nbasis - 1)


def own_onehots(meta_ref, oh_own):
    atoms = meta_ref.shape[0]
    counts = meta_ref[:, SLOTS : SLOTS + 1]
    lane_atom = iota((atoms, atoms), 1).astype(F32)
    for slot in range(HALF):
        hit = jnp.logical_and(meta_ref[:, slot : slot + 1] == lane_atom, counts > slot)
        oh_own[slot * atoms : (slot + 1) * atoms, :] = hit.astype(F32).astype(BF16)


def geometry(near, here):
    diff = near - here
    rel = (diff + pltpu.roll(diff, CH - 4, 1)) + (
        pltpu.roll(diff, CH - 8, 1) + pltpu.roll(diff, CH - 12, 1)
    )
    lane = iota(rel.shape, 1)
    rel = jnp.where(lane < 3, rel, 0.0)
    square = jnp.sum(rel * rel, axis=1, keepdims=True)
    inverse = lax.rsqrt(jnp.where(square > 0.0, square, 1.0))
    dist = square * inverse
    return jnp.where(lane == 3, dist, rel * inverse), dist


def centred_of(dist, spacing, nbasis):
    return dist * (1.0 / spacing) - iota((dist.shape[0], nbasis), 1).astype(F32)


def radial_net(dist, spacing, rbf_ref, rad_ref):
    centred = centred_of(dist, spacing, rbf_ref.shape[0])
    basis = jnp.exp(-0.5 * centred * centred)
    pre = mm(basis.astype(BF16), rbf_ref[...])
    hidden = (pre * jax.nn.sigmoid(pre)).astype(BF16)
    return pre, mm(hidden, rad_ref[...]).astype(BF16)


def own_spread(atoms):
    shape = (atoms, STEP)
    return (iota(shape, 1) % atoms == iota(shape, 0)).astype(F32).astype(BF16)


def tiled(values):
    return jnp.concatenate([values] * (STEP // values.shape[0]), axis=0)


def live_ghosts(meta_ref):
    return jnp.maximum(meta_ref[:, SLOTS : SLOTS + 1] - HALF, 0.0)


def step_count(meta_ref):
    total = jnp.sum(live_ghosts(meta_ref)).astype(jnp.int32)
    return jnp.maximum((total + (STEP - 1)) // STEP, GH_STEPS)


def own_rows(step):
    return pl.ds(step * STEP, STEP)


def ghost_rows(step):
    if isinstance(step, int):
        return pl.ds(step * STEP, STEP), pl.ds((OWN_STEPS + step) * STEP, STEP)
    base = pl.multiple_of(step * STEP, STEP)
    later = pl.multiple_of(OWN_STEPS * STEP + step * STEP, STEP)
    return pl.ds(base, STEP), pl.ds(later, STEP)


def over_ghost_steps(steps, body):
    for step in range(GH_STEPS):
        body(step)

    def again(step, carry):
        body(step)
        return carry

    lax.fori_loop(GH_STEPS, steps, again, 0)


def block_diagonal(kinds, mix_ref, out_ref, wm, wmt, wo, wot):
    zero = jnp.zeros((CH, CH), BF16)
    for kind, both in enumerate(kinds):
        for ref in (wm, wmt, wo, wot):
            ref[kind, 0:CH, CH:] = zero
            ref[kind, CH:, 0:CH] = zero
    for degree in sorted({d for both in kinds for d in both}):
        mix, out = mix_ref[degree], out_ref[degree]
        mix_t, out_t = flip(mix), flip(out)
        for kind, both in enumerate(kinds):
            for side in range(2):
                if both[side] == degree:
                    part = slice(side * CH, side * CH + CH)
                    wm[kind, part, part] = mix
                    wmt[kind, part, part] = mix_t
                    wo[kind, part, part] = out
                    wot[kind, part, part] = out_t


def fetch(pieces, table, sems):
    copies = []
    at = 0
    for index, piece in enumerate(pieces):
        rows = piece.shape[0]
        copies.append(
            pltpu.make_async_copy(piece, table.at[pl.ds(at, rows), :], sems.at[index])
        )
        at += rows
    for copy in copies:
        copy.start()
    return copies


def run_pairs(
    pairs, kinds, first_col, own_ref, table, new_ref, new_base, oh_own, oh_gh, d_gh, dt_gh,
    gate_ref, radial_of, nw_ref, steps, wm, wmt, wo, wot, nf_s, mx_s, acc_s, gs_s, dot_ref,
    grad_refs, en_ref,
):
    atoms = own_ref.shape[0]
    norm = 1.0 / math.sqrt(SLOTS)
    spread_own = own_spread(atoms)
    seen = set()

    def gate_of(rows):
        gate = gate_ref[rows, :]
        return jnp.concatenate([gate, gate], axis=1)

    for quad in range(0, len(pairs), 2):
        both = pairs[quad : quad + 2]
        infos = []
        for index, pair in enumerate(both):
            degrees = PAIR_DEGREES[pair]
            cols = pair_cols(pair)
            local = slice(cols.start - first_col, cols.stop - first_col)
            infos.append((index, degrees, kinds.index(degrees), cols, local))

        def forward(index, degrees, kind, rows, onehot, feats):
            near = mm(onehot, feats).astype(BF16)
            nf_s[index, rows, :] = near
            radial = jnp.concatenate([radial_of(d, rows) for d in degrees], axis=1)
            mixed = mm(near * radial, wm[kind]).astype(BF16)
            mx_s[index, rows, :] = mixed
            return mixed * gate_of(rows)

        def backward(rows, grads):
            parts = {}
            dots = None
            gate = gate_of(rows)
            for (index, degrees, kind, cols, local), grad in zip(infos, grads):
                product = grad * mx_s[index, rows, :]
                dot = (product[:, 0:CH] + product[:, CH:]).astype(F32)
                dots = dot if dots is None else dots + dot
                weighted = mm(grad * gate, wmt[kind]) * nf_s[index, rows, :].astype(F32)
                for side in range(2):
                    part = weighted[:, side * CH : (side + 1) * CH]
                    degree = degrees[side]
                    parts[degree] = parts[degree] + part if degree in parts else part
            dot_ref[rows, :] = dots if quad == 0 else dot_ref[rows, :] + dots
            for degree, part in parts.items():
                ref = grad_refs[degree]
                ref[rows, :] = ref[rows, :] + part if degree in seen else part

        for index, degrees, kind, cols, local in infos:
            own = own_ref[:, cols]
            summed = None
            for step in range(OWN_STEPS):
                rows = own_rows(step)
                message = forward(index, degrees, kind, rows, oh_own[rows, :], own)
                part = mm(spread_own, message)
                summed = part if summed is None else summed + part
            acc_s[index] = summed

        def ghost_forward(step):
            here, rows = ghost_rows(step)
            for index, degrees, kind, cols, local in infos:
                message = forward(index, degrees, kind, rows, oh_gh[here, :], table[:, local])
                acc_s[index] += mm(dt_gh[step], message)

        over_ghost_steps(steps, ghost_forward)

        for index, degrees, kind, cols, local in infos:
            summed_low = (acc_s[index] * norm).astype(BF16)
            updated = own_ref[:, cols].astype(F32) + mm(summed_low, wo[kind])
            at = cols.start - new_base
            new_ref[:, at : at + 2 * CH] = updated.astype(BF16)
            weight = jnp.concatenate(
                [nw_ref[d - 1 : d, :] * (1.0 / (2 * d + 1)) for d in degrees], axis=1
            )
            scale = weight * updated
            energy = scale * updated
            en_ref[...] += energy[:, 0:CH] + energy[:, CH:]
            gs_s[index] = (mm((2.0 * scale).astype(BF16), wot[kind]) * norm).astype(BF16)

        grads_own = [tiled(gs_s[index]) for index in range(len(both))]
        for step in range(OWN_STEPS):
            backward(own_rows(step), grads_own)

        def ghost_backward(step):
            here, rows = ghost_rows(step)
            source = d_gh[here, :]
            backward(rows, [mm(source, gs_s[i]).astype(BF16) for i in range(len(both))])

        over_ghost_steps(steps, ghost_backward)
        for pair in both:
            seen.update(PAIR_DEGREES[pair])


def pair_scratch(atoms, edges, kinds):
    count = len(kinds)
    return [pltpu.VMEM((count, 2 * CH, 2 * CH), BF16) for _ in range(4)] + [
        pltpu.VMEM((2, edges, 2 * CH), BF16),
        pltpu.VMEM((2, edges, 2 * CH), BF16),
        pltpu.VMEM((2, atoms, 2 * CH), F32),
        pltpu.VMEM((2, atoms, 2 * CH), BF16),
    ]


def own_kernel(meta_ref, own_pos_ref, rbf_ref, rad_ref, oh_own, radial_ref, pre_ref, unit_ref):
    atoms = meta_ref.shape[0]
    spacing = spacing_of(atoms, rbf_ref.shape[0])
    own_onehots(meta_ref, oh_own)
    here = tiled(own_pos_ref[...].astype(F32))
    for step in range(OWN_STEPS):
        rows = own_rows(step)
        unit, dist = geometry(mm(oh_own[rows, :], own_pos_ref[...]), here)
        unit_ref[rows, :] = unit
        pre, radial = radial_net(dist, spacing, rbf_ref, rad_ref)
        pre_ref[rows, :] = pre
        for degree in range(5):
            radial_ref[degree, rows, :] = radial[:, degree * CH : (degree + 1) * CH]


def own_stage(meta, own_pos, rbf, rad):
    atoms = meta.shape[0]
    edges = atoms * HALF
    out_shape = (
        struct(edges, atoms, dtype=BF16),
        struct(5, edges, CH, dtype=BF16),
        struct(edges, CH),
        struct(edges, CH),
    )
    return call(own_kernel, "own_edges", out_shape, [], 1 << 31, (meta, own_pos, rbf, rad))


def first_kernel(
    low_ref, mid_ref, high_ref, own_ref, own_pos_ref, meta_ref, rbf_ref, rad_ref, mix_ref,
    out_ref, ew_ref, nw_ref, oh_own, radial_own,
    new_ref, oh_gh, d_gh, dt_gh, radial_gh, pre_ref, unit_ref, m0_ref, gate_ref, nf0_ref,
    gs0_ref, dot_ref, gr1_ref, gr2_ref, en_ref,
    table, sems, ghpos, wm, wmt, wo, wot, nf_s, mx_s, acc_s, gs_s,
):
    pairs = tuple(range(*GROUPS[0]))
    kinds = sorted({PAIR_DEGREES[pair] for pair in pairs})
    copies = fetch((low_ref, mid_ref, high_ref), table, sems)
    atoms = own_ref.shape[0]
    ghosts = table.shape[0]
    spacing = spacing_of(atoms, rbf_ref.shape[0])
    norm = 1.0 / math.sqrt(SLOTS)
    block_diagonal(kinds, mix_ref, out_ref, wm, wmt, wo, wot)

    live = live_ghosts(meta_ref)
    sub_atom = iota((atoms, atoms), 0)
    lane_atom = iota((atoms, atoms), 1)
    live_b = jnp.broadcast_to(live, (atoms, atoms))
    end_row = jnp.sum(jnp.where(sub_atom <= lane_atom, live_b, 0.0), axis=0, keepdims=True)
    live_row = jnp.sum(jnp.where(sub_atom == lane_atom, live_b, 0.0), axis=0, keepdims=True)
    start_row = end_row - live_row
    row_b = jnp.broadcast_to(live_row, (atoms, atoms))
    end_col = jnp.sum(jnp.where(lane_atom <= sub_atom, row_b, 0.0), axis=1, keepdims=True)
    start_col = end_col - live
    total = jnp.sum(live)
    steps = step_count(meta_ref)
    ghost_row = meta_ref[:, HALF:SLOTS] - atoms
    high_part = jnp.floor(ghost_row * (1.0 / 16.0))
    row_high = high_part.astype(BF16)
    row_low = (ghost_row - 16.0 * high_part).astype(BF16)

    row = iota((ghosts, CH), 0)
    lane = iota((ghosts, CH), 1)
    zcells = atoms // 32
    per_y = (zcells + 2) * 8
    ext_x = row // (4 * per_y)
    ext_y = row // per_y % 4
    ext_z = row // 8 % (zcells + 2)

    def side_of(ext, last, size):
        return jnp.where(ext == 0, -size, jnp.where(ext == last, size, 0.0))

    shift = jnp.where(lane == 12, side_of(ext_x, 3, 4.0), 0.0)
    shift = jnp.where(lane == 13, side_of(ext_y, 3, 4.0), shift)
    shift = jnp.where(lane == 14, side_of(ext_z, zcells + 1, 2.0 * zcells), shift)
    for copy in copies:
        copy.wait()
    ghpos[...] = (table[:, table.shape[1] - CH :].astype(F32) + shift).astype(BF16)

    def radial_of(degree, rows):
        return radial_gh[degree, pl.ds(rows.start - OWN_STEPS * STEP, STEP), :]

    def forward0(rows, onehot, feats, radial):
        near = mm(onehot, feats).astype(BF16)
        nf0_ref[rows, :] = near
        mixed = mm(near * radial, mix_ref[0])
        m0_ref[rows, :] = mixed
        gate = jax.nn.sigmoid(mixed)
        gate_ref[rows, :] = gate.astype(BF16)
        return (mixed * gate).astype(BF16)

    own0 = own_ref[:, 0:CH]
    spread_own = own_spread(atoms)
    summed = None
    for step in range(OWN_STEPS):
        rows = own_rows(step)
        message = forward0(rows, oh_own[rows, :], own0, radial_own[0, rows, :])
        part = mm(spread_own, message)
        summed = part if summed is None else summed + part
    acc_s[0, :, 0:CH] = summed

    def ghost_start(step):
        here, rows = ghost_rows(step)
        base = step * STEP
        edge = (iota((STEP, atoms), 0) + base).astype(F32)
        mine = jnp.logical_and(edge >= start_row, edge < end_row).astype(F32)
        source = mine.astype(BF16)
        d_gh[here, :] = source
        edge_t = (iota((atoms, STEP), 1) + base).astype(F32)
        mine_t = jnp.logical_and(edge_t >= start_col, edge_t < end_col)
        spread = mine_t.astype(F32).astype(BF16)
        dt_gh[step, :, :] = spread
        edge_col = edge[:, 0:1]
        slot = edge_col - jnp.sum(mine * start_row, axis=1, keepdims=True)
        listed = mm(source, row_high) * 16.0 + mm(source, row_low)
        at_slot = iota((STEP, HALF), 1).astype(F32) == slot
        which = jnp.sum(jnp.where(at_slot, listed, 0.0), axis=1, keepdims=True)
        which = jnp.where(edge_col < total, which, -1.0)
        onehot = (iota((STEP, ghosts), 1).astype(F32) == which).astype(F32).astype(BF16)
        oh_gh[here, :] = onehot
        unit, dist = geometry(mm(onehot, ghpos[...]), mm(source, own_pos_ref[...]))
        unit_ref[here, :] = unit
        pre, radial = radial_net(dist, spacing, rbf_ref, rad_ref)
        pre_ref[here, :] = pre
        for degree in range(5):
            radial_gh[degree, here, :] = radial[:, degree * CH : (degree + 1) * CH]
        message = forward0(rows, onehot, table[:, 0:CH], radial[:, 0:CH])
        acc_s[0, :, 0:CH] += mm(spread, message)

    over_ghost_steps(steps, ghost_start)

    low0 = (acc_s[0, :, 0:CH] * norm).astype(BF16)
    updated0 = own0.astype(F32) + mm(low0, out_ref[0])
    new_ref[:, 0:CH] = updated0.astype(BF16)
    logistic = jax.nn.sigmoid(updated0)
    weight0 = ew_ref[...]
    en_ref[...] = weight0 * updated0 * logistic
    grad0 = (weight0 * logistic * (1.0 + updated0 * (1.0 - logistic))).astype(BF16)
    gs0_ref[...] = mm_nt(grad0, out_ref[0]) * norm

    def radial_any(degree, rows):
        if isinstance(rows.start, int) and rows.start < OWN_STEPS * STEP:
            return radial_own[degree, rows, :]
        return radial_of(degree, rows)

    run_pairs(
        pairs, kinds, 0, own_ref, table, new_ref, 0, oh_own, oh_gh, d_gh, dt_gh, gate_ref,
        radial_any, nw_ref, steps, wm, wmt, wo, wot, nf_s, mx_s, acc_s, gs_s, dot_ref,
        {1: gr1_ref, 2: gr2_ref}, en_ref,
    )


def any_specs(count, total):
    return [pl.BlockSpec(memory_space=pl.ANY)] * count + [
        pl.BlockSpec(memory_space=SPACE)
    ] * (total - count)


def first_stage(pieces, feats, own_pos, meta, rbf, rad, mix, out, ew, nw, oh_own, radial_own):
    atoms = feats.shape[0]
    half = atoms * HALF
    edges = 2 * half
    width = pieces[0].shape[1]
    ghosts = sum(piece.shape[0] for piece in pieces)
    kinds = sorted({PAIR_DEGREES[pair] for pair in range(*GROUPS[0])})
    out_shape = (
        struct(atoms, width - CH, dtype=BF16),
        struct(half, ghosts, dtype=BF16),
        struct(half, atoms, dtype=BF16),
        struct(half // STEP, atoms, STEP, dtype=BF16),
        struct(5, half, CH, dtype=BF16),
        struct(half, CH),
        struct(half, CH),
        struct(edges, CH),
        struct(edges, CH, dtype=BF16),
        struct(edges, CH, dtype=BF16),
        struct(atoms, CH),
        struct(edges, CH),
        struct(edges, CH),
        struct(edges, CH),
        struct(atoms, CH),
    )
    scratch = [
        pltpu.VMEM((ghosts, width), BF16),
        pltpu.SemaphoreType.DMA((3,)),
        pltpu.VMEM((ghosts, CH), BF16),
    ] + pair_scratch(atoms, edges, kinds)
    args = tuple(pieces) + (
        feats, own_pos, meta, rbf, rad, mix, out, ew, nw, oh_own, radial_own
    )
    return call(
        first_kernel, "first_group", out_shape, scratch, 1 << 33, args, any_specs(3, len(args))
    )


def second_kernel(
    low_ref, mid_ref, high_ref, own_ref, meta_ref, mix_ref, out_ref, nw_ref, oh_own, radial_own,
    oh_gh, d_gh, dt_gh, radial_gh, gate_ref,
    new_ref, dot_ref, gr3_ref, gr4_ref, en_ref,
    table, sems, wm, wmt, wo, wot, nf_s, mx_s, acc_s, gs_s,
):
    pairs = tuple(range(*GROUPS[1]))
    kinds = sorted({PAIR_DEGREES[pair] for pair in pairs})
    copies = fetch((low_ref, mid_ref, high_ref), table, sems)
    block_diagonal(kinds, mix_ref, out_ref, wm, wmt, wo, wot)
    en_ref[...] = jnp.zeros_like(en_ref)
    base = pair_cols(pairs[0]).start

    def radial_any(degree, rows):
        if isinstance(rows.start, int) and rows.start < OWN_STEPS * STEP:
            return radial_own[degree, rows, :]
        return radial_gh[degree, pl.ds(rows.start - OWN_STEPS * STEP, STEP), :]

    for copy in copies:
        copy.wait()
    run_pairs(
        pairs, kinds, base, own_ref, table, new_ref, base, oh_own, oh_gh, d_gh, dt_gh, gate_ref,
        radial_any, nw_ref, step_count(meta_ref), wm, wmt, wo, wot, nf_s, mx_s, acc_s, gs_s,
        dot_ref, {3: gr3_ref, 4: gr4_ref}, en_ref,
    )


def second_stage(pieces, feats, meta, mix, out, nw, oh_own, radial_own, oh_gh, d_gh, dt_gh,
                 radial_gh, gate):
    atoms = feats.shape[0]
    edges = atoms * SLOTS
    width = pieces[0].shape[1]
    ghosts = sum(piece.shape[0] for piece in pieces)
    kinds = sorted({PAIR_DEGREES[pair] for pair in range(*GROUPS[1])})
    out_shape = (
        struct(atoms, width, dtype=BF16),
        struct(edges, CH),
        struct(edges, CH),
        struct(edges, CH),
        struct(atoms, CH),
    )
    scratch = [
        pltpu.VMEM((ghosts, width), BF16),
        pltpu.SemaphoreType.DMA((3,)),
    ] + pair_scratch(atoms, edges, kinds)
    args = tuple(pieces) + (
        feats, meta, mix, out, nw, oh_own, radial_own, oh_gh, d_gh, dt_gh, radial_gh, gate
    )
    return call(
        second_kernel, "second_group", out_shape, scratch, 1 << 33, args,
        any_specs(3, len(args)),
    )


def third_kernel(
    low_ref, mid_ref, high_ref, own_ref, meta_ref, mix_ref, out_ref, nw_ref, oh_own, radial_own,
    oh_gh, d_gh, dt_gh, radial_gh, gate_ref,
    rbf_ref, rad_ref, pre_own, pre_gh, unit_own, unit_gh, m0_ref, nf0_ref, gs0_ref,
    dot_a, dot_b, gr1_ref, gr2_ref, gr3_ref, gr4_a, en_a, en_b, new_a, new_b,
    new_ref, energy_ref, fown_ref, flow_ref, fmid_ref, fhigh_ref,
    table, sems, wm, wmt, wo, wot, nf_s, mx_s, acc_s, gs_s,
    dot_c, gr4_b, en_s, radt, rbft, src_s, fgh_s,
):
    pairs = tuple(range(*GROUPS[2]))
    kinds = sorted({PAIR_DEGREES[pair] for pair in pairs})
    copies = fetch((low_ref, mid_ref, high_ref), table, sems)
    atoms = own_ref.shape[0]
    nbasis = rbf_ref.shape[0]
    spacing = spacing_of(atoms, nbasis)
    block_diagonal(kinds, mix_ref, out_ref, wm, wmt, wo, wot)
    for degree in range(5):
        part = slice(degree * CH, (degree + 1) * CH)
        radt[part, :] = flip(rad_ref[:, part])
    for index in range(nbasis // CH):
        part = slice(index * CH, (index + 1) * CH)
        rbft[:, part] = flip(rbf_ref[part, :])
    mix0_t = flip(mix_ref[0])
    en_s[...] = en_a[...] + en_b[...]
    new_ref[:, 0 : new_a.shape[1]] = new_a[...]
    new_ref[:, new_a.shape[1] : new_a.shape[1] + new_b.shape[1]] = new_b[...]
    base = pair_cols(pairs[0]).start
    steps = step_count(meta_ref)

    def radial_any(degree, rows):
        if isinstance(rows.start, int) and rows.start < OWN_STEPS * STEP:
            return radial_own[degree, rows, :]
        return radial_gh[degree, pl.ds(rows.start - OWN_STEPS * STEP, STEP), :]

    for copy in copies:
        copy.wait()
    run_pairs(
        pairs, kinds, base, own_ref, table, new_ref, 0, oh_own, oh_gh, d_gh, dt_gh, gate_ref,
        radial_any, nw_ref, steps, wm, wmt, wo, wot, nf_s, mx_s, acc_s, gs_s, dot_c,
        {4: gr4_b}, en_s,
    )

    def finish(rows, grad, pre, unit):
        mixed = m0_ref[rows, :]
        gate = jax.nn.sigmoid(mixed)
        dot = dot_a[rows, :] + dot_b[rows, :] + dot_c[rows, :]
        first = grad * gate * (1.0 + mixed * (1.0 - gate)) + dot * gate * (1.0 - gate)
        weighted = mm(first.astype(BF16), mix0_t) * nf0_ref[rows, :].astype(F32)
        parts = [weighted, gr1_ref[rows, :], gr2_ref[rows, :], gr3_ref[rows, :]]
        parts.append(gr4_a[rows, :] + gr4_b[rows, :])
        radial_grad = jnp.concatenate([part.astype(BF16) for part in parts], axis=1)
        hidden_grad = mm(radial_grad, radt[...])
        logistic = jax.nn.sigmoid(pre)
        pre_grad = (hidden_grad * logistic * (1.0 + pre * (1.0 - logistic))).astype(BF16)
        centred = centred_of(unit[:, 3:4], spacing, nbasis)
        slope = jnp.exp(-0.5 * centred * centred) * centred
        basis_grad = mm(pre_grad, rbft[...])
        dist_grad = jnp.sum(basis_grad * slope, axis=1, keepdims=True) * (-1.0 / spacing)
        pull = unit * dist_grad
        across = pull.T[0:8, :]
        top = across.astype(BF16)
        rest = (across - top.astype(F32)).astype(BF16)
        return pull, top, rest

    fgh_s[...] = jnp.zeros_like(fgh_s)
    src_s[...] = jnp.zeros_like(src_s)
    gs0 = gs0_ref[...]
    gs0_low = gs0.astype(BF16)

    def ghost_finish(step):
        here, rows = ghost_rows(step)
        grad = mm(d_gh[here, :], gs0_low)
        pull, top, rest = finish(rows, grad, pre_gh[here, :], unit_gh[here, :])
        pull_top = pull.astype(BF16)
        pull_rest = (pull - pull_top.astype(F32)).astype(BF16)
        spread = dt_gh[step]
        src_s[...] += mm(spread, pull_top) + mm(spread, pull_rest)
        onehot = oh_gh[here, :]
        fgh_s[...] += mm(top, onehot) + mm(rest, onehot)

    over_ghost_steps(steps, ghost_finish)
    low, mid = flow_ref.shape[1], fmid_ref.shape[1]
    flow_ref[...] = fgh_s[:, 0:low]
    fmid_ref[...] = fgh_s[:, low : low + mid]
    fhigh_ref[...] = fgh_s[:, low + mid :]

    grad_own = tiled(gs0)
    src = src_s[...]
    onto = jnp.zeros((8, atoms), F32)
    for step in range(OWN_STEPS):
        rows = own_rows(step)
        pull, top, rest = finish(rows, grad_own, pre_own[rows, :], unit_own[rows, :])
        src += jnp.sum(pull.reshape(STEP // atoms, atoms, CH), axis=0)
        onehot = oh_own[rows, :]
        onto += mm(top, onehot) + mm(rest, onehot)
    fown_ref[...] = onto - src.T[0:8, :]
    energy_ref[...] = jnp.sum(en_s[...].T, axis=0, keepdims=True)


def third_stage(pieces, feats, *rest):
    atoms, feat = feats.shape
    edges = atoms * SLOTS
    width = pieces[0].shape[1]
    sizes = [piece.shape[0] for piece in pieces]
    ghosts = sum(sizes)
    nbasis = rest[11].shape[0]
    kinds = sorted({PAIR_DEGREES[pair] for pair in range(*GROUPS[2])})
    out_shape = (
        struct(atoms, feat, dtype=BF16),
        struct(1, atoms),
        struct(8, atoms),
    ) + tuple(struct(8, size) for size in sizes)
    scratch = [
        pltpu.VMEM((ghosts, width), BF16),
        pltpu.SemaphoreType.DMA((3,)),
    ] + pair_scratch(atoms, edges, kinds) + [
        pltpu.VMEM((edges, CH), F32),
        pltpu.VMEM((edges, CH), F32),
        pltpu.VMEM((atoms, CH), F32),
        pltpu.VMEM((5 * CH, CH), BF16),
        pltpu.VMEM((CH, nbasis), BF16),
        pltpu.VMEM((atoms, CH), F32),
        pltpu.VMEM((8, ghosts), F32),
    ]
    args = tuple(pieces) + (feats,) + rest
    return call(
        third_kernel, "third_group", out_shape, scratch, 1 << 33, args, any_specs(3, len(args))
    )


def layer(pieces, feats, own_pos, meta, rbf, rad, mix, out, ew, nw):
    oh_own, radial_own, pre_own, unit_own = own_stage(meta, own_pos, rbf, rad)
    (
        new_a, oh_gh, d_gh, dt_gh, radial_gh, pre_gh, unit_gh, m0, gate, nf0, gs0, dot_a, gr1,
        gr2, en_a,
    ) = first_stage(
        pieces[0], feats, own_pos, meta, rbf, rad, mix, out, ew, nw, oh_own, radial_own
    )
    new_b, dot_b, gr3, gr4, en_b = second_stage(
        pieces[1], feats, meta, mix, out, nw, oh_own, radial_own, oh_gh, d_gh, dt_gh, radial_gh,
        gate,
    )
    return third_stage(
        pieces[2], feats, meta, mix, out, nw, oh_own, radial_own, oh_gh, d_gh, dt_gh, radial_gh,
        gate, rbf, rad, pre_own, pre_gh, unit_own, unit_gh, m0, nf0, gs0, dot_a, dot_b, gr1, gr2,
        gr3, gr4, en_a, en_b, new_a, new_b,
    )


def ring(axis):
    peers = lax.axis_size(axis)
    up = [(i, (i + 1) % peers) for i in range(peers)]
    return up, [(j, i) for i, j in up]


def neighbours_of(block, axis, dim):
    up, down = ring(axis)
    length = block.shape[dim]
    if len(up) == 2 and length == 2:
        other = lax.ppermute(block, axis, up)
        return (
            lax.slice_in_dim(other, length - 1, length, axis=dim),
            lax.slice_in_dim(other, 0, 1, axis=dim),
        )
    before = lax.ppermute(lax.slice_in_dim(block, length - 1, length, axis=dim), axis, up)
    after = lax.ppermute(lax.slice_in_dim(block, 0, 1, axis=dim), axis, down)
    return before, after


def exchange(cells):
    block = cells.reshape(2, 2, 2, 8, cells.shape[1])
    for axis, dim in (("gz", 2), ("gy", 1)):
        before, after = neighbours_of(block, axis, dim)
        block = jnp.concatenate([before, block, after], axis=dim)
    before, after = neighbours_of(block, "gx", 0)
    return tuple(piece.reshape(-1, cells.shape[1]) for piece in (before, block, after))


def forces_kernel(mid_ref, low_ref, high_ref, own_ref, meta_ref, out_ref):
    atoms = own_ref.shape[1]
    values = mid_ref[...]
    lanes = values.shape[1]
    lane = iota(values.shape, 1)
    ext_z = lane // 8 % 4
    values += jnp.where(ext_z == 1, pltpu.roll(low_ref[...], lanes - 16, 1), 0.0)
    values += jnp.where(ext_z == 2, pltpu.roll(high_ref[...], 16, 1), 0.0)
    lane = iota((atoms, lanes), 1)
    ext_x, ext_y, ext_z = lane // 128, lane // 32 % 4, lane // 8 % 4
    slot = ((2 * ext_x + ext_y - 1) * 2 + ext_z - 1) * 8 + lane % 8
    inside = jnp.logical_and(
        jnp.logical_or(ext_y == 1, ext_y == 2), jnp.logical_or(ext_z == 1, ext_z == 2)
    )
    to_slot = jnp.logical_and(iota((atoms, lanes), 0) == slot, inside)
    to_slot = to_slot.astype(F32).astype(BF16)
    order = meta_ref[:, SLOTS + 1 : SLOTS + 2]
    to_atom = (order == iota((atoms, atoms), 1).astype(F32)).astype(F32).astype(BF16)
    total = own_ref[...]
    for _ in range(3):
        top = values.astype(BF16)
        values = values - top.astype(F32)
        total += mm(mm_nt(top, to_slot).astype(BF16), to_atom)
    for comp in range(3):
        out_ref[comp] = -total[comp : comp + 1, :]


def give_back(low, mid, high, own, meta):
    up, down = ring("gx")
    from_low = lax.ppermute(high, "gx", up)
    from_high = lax.ppermute(low, "gx", down)
    mid = mid + jnp.concatenate([from_low, from_high], axis=1)
    up, down = ring("gy")
    from_low = lax.ppermute(mid, "gy", up)
    from_high = lax.ppermute(mid, "gy", down)
    ext_y = jnp.arange(mid.shape[1], dtype=jnp.int32)[None] // 32 % 4
    mid = (
        mid
        + jnp.where(ext_y == 1, jnp.roll(from_low, -64, axis=1), 0.0)
        + jnp.where(ext_y == 2, jnp.roll(from_high, 64, axis=1), 0.0)
    )
    up, down = ring("gz")
    from_low = lax.ppermute(mid, "gz", up)
    from_high = from_low if len(up) == 2 else lax.ppermute(mid, "gz", down)
    args = (mid, from_low, from_high, own, meta)
    out_shape = (struct(3, 1, own.shape[1]),)
    return call(forces_kernel, "forces", out_shape, [], 1 << 20, args)[0]


def local(
    features,
    positions,
    neighbours,
    counts,
    cell_atoms,
    rbf_weight,
    radial_weight,
    mix_weight,
    out_weight,
    energy_weight,
    norm_weight,
):
    feats = features[0, 0, 0]
    places = jnp.swapaxes(positions[0, 0], 0, 1)
    *cells, own_pos, meta = make_cells(
        feats, places, neighbours[0, 0, 0].T, counts[0, 0], cell_atoms[0, 0]
    )
    pieces = [exchange(part) for part in cells]
    new, energy, own, low, mid, high = layer(
        pieces, feats, own_pos, meta, rbf_weight, radial_weight, mix_weight, out_weight,
        energy_weight[None], norm_weight,
    )
    forces = give_back(low, mid, high, own, meta)
    return (
        new[None, None, None],
        energy[None, None],
        jnp.swapaxes(forces, 0, 1)[None, None],
    )


def solution(mesh):
    split = P("gx", "gy", "gz", None, None)
    flat = P("gx", "gy", "gz", None)
    return jax.shard_map(
        local,
        mesh=mesh,
        in_specs=(split, split, split, flat, flat, P(), P(), P(), P(), P(), P()),
        out_specs=(split, flat, split),
        check_vma=False,
    )
```

time: 446 us -> 118 us (0.26); the launches traced: 440 us -> 118 us
  local copies, waits for them, and re-layouts: 144 us -> 3.29 us
  other arithmetic: 106 us -> 1.13 us
  matrix products: 102 us -> 0 us
  Pallas kernels: 0 us -> 61.9 us
  waiting for transfers between devices: 56.9 us -> 22.9 us
  loops' own time: 6.46 us -> 0 us
  starting transfers between devices: 22.9 us -> 27.8 us
    dot_general x184 -> x0, matrix products: 102 us -> none  [the longest x80 46.2 us: degree_matmul(): lax.dot_general(block, weights[degree], (((1,), (1,)), ((), ())), preferr...]
    gather x28 -> x0, local copies, waits for them, and re-layouts: 76.2 us -> none  [the longest x16 59.2 us: block_step(): jnp.take(table_feat, flat_rows, axis=0)]
    pallas_call x0 -> x6, Pallas kernels: none -> 61.9 us  [call(): pl.pallas_call(kernel, out_shape=out_shape, in_specs=specs or [pl.BlockSp...]
    ppermute x18 -> x20, waiting for transfers between devices: 56.9 us -> 22.9 us  [the longest x6 15.3 us: neighbours_of(): lax.ppermute(lax.slice_in_dim(block, length - 1, length, axis=dim), axis,...]
    while x754 -> x0, local copies, waits for them, and re-layouts: 26.8 us -> none
    reduce_sum x73 -> x0, other arithmetic: 21.4 us -> none  [the longest x8 8.17 us: block_step(): jnp.sum(norm_expanded[None] * updated * updated, axis=(1, 2))]
    scatter-add x8 -> x0, other arithmetic: 17.6 us -> none  [block_step(): grad_table = grad_table.at[:, flat_rows].add(pull_vec)]
    dynamic_update_slice x16 -> x0, local copies, waits for them, and re-layouts: 15.1 us -> none  [domain_layer(): lax.scan(advance, jnp.zeros(table_places.shape, jnp.float32), scanned)]
  transfers between devices with their start and end apart: 18 -> 20, of which waited for: 9 -> 9; matrix products, arithmetic and copies ran while one was open for 3% -> 1% of each run, Pallas kernels for 0% -> 32%
where the time goes in v2:
time: 118 us
  Pallas kernels  61.9 us (52%)
  starting transfers between devices  27.8 us (24%)
  waiting for transfers between devices  22.9 us (19%)
  local copies, waits for them, and re-layouts  3.29 us (3%)
    pallas_call x6, Pallas kernels, call(): pl.pallas_call(kernel, out_shape=out_shape, in_specs=specs or [pl.BlockSp...  61.9 us
    ppermute x6, waiting for transfers between devices, neighbours_of(): lax.ppermute(lax.slice_in_dim(block, length - 1, length, axis=dim), axis,...  15.3 us
    ppermute x6, starting transfers between devices, neighbours_of(): after = lax.ppermute(lax.slice_in_dim(block, 0, 1, axis=dim), axis, down)  11.4 us
    ppermute x3, starting transfers between devices, neighbours_of(): other = lax.ppermute(block, axis, up)  4.99 us
    ppermute x1, starting transfers between devices, give_back(): from_high = lax.ppermute(mid, 'gy', down)  3.82 us
    ppermute x1, starting transfers between devices, give_back(): from_low = lax.ppermute(high, 'gx', up)  3.62 us
    unnamed x28, local copies, waits for them, and re-layouts  2.94 us
    ppermute x6, starting transfers between devices, neighbours_of(): lax.ppermute(lax.slice_in_dim(block, length - 1, length, axis=dim), axis,...  2.46 us
  transfers between devices with their start and end apart: 20, of which 9 were waited for; matrix products, arithmetic and copies ran while one was open for 1% of the time, Pallas kernels for 32%

profile of v2, /device:TPU:0, one launch (start us, length us, event | category | flops | bytes accessed | tf_op | source)
XLA Modules:
  0.0 118.0 jit_solution(10892294133124359175)
XLA Ops:
  0.6 2.2 %cells.1 = (bf16[64,1280]{1,0:T(8,128)(2,1)}, bf16[64,1024]{1,0:T(8,128)(2,1)}, bf16[64,1024]{1,0:T(8,128)(2,1)}, bf16[64,128]{1,0:T(8,128)(2,1)}, f32[64,128]{1,0:T(8,128)}) custom-call(bf16[64,3200]{1,0:T(8,128)(2,1)} %bitcast.38, f32[3,1,64]{2,1,0:T(1,128)} %bitcast.44, s32[32,64]{1,0:T(8,128)} %bitcast.43, s32[1,64]{1,0:T(1,128)} %bitcast.46, ...), custom_call_target="tpu_custom_call" | custom-call | flops 67108864 | bytes 894208 | tf_op jit(solution)/shard_map/cells/pallas_call | solution.py:55
  2.8 3.0 %collective-permute-start.5 = (bf16[2,2,2,8,1280]{4,3,2,1,0:T(8,128)(2,1)}, bf16[2,2,2,8,1280]{4,3,2,1,0:T(8,128)(2,1)S(1)}, u32[]{:S(2)}, u32[]{:S(2)}) collective-permute-start(bf16[2,2,2,8,1280]{4,3,2,1,0:T(8,128)(2,1)} %bitcast.29), channel_id=1, source_target_pairs={{0,1},{1,0},{2,3},{3,2},{4,5},{5,4},{6,7},{7,6},{8,9},{9,8},{10,11... | collective-permute-start | bytes 491528 | tf_op jit(solution)/shard_map/ppermute | solution.py:734
  5.8 2.0 %collective-permute-start = (bf16[2,2,2,8,1024]{4,3,2,1,0:T(8,128)(2,1)}, bf16[2,2,2,8,1024]{4,3,2,1,0:T(8,128)(2,1)S(1)}, u32[]{:S(2)}, u32[]{:S(2)}) collective-permute-start(bf16[2,2,2,8,1024]{4,3,2,1,0:T(8,128)(2,1)} %bitcast.32), channel_id=1, source_target_pairs={{0,1},{1,0},{2,3},{3,2},{4,5},{5,4},{6,7},{7,6},{8,9},{9,8},{10,11... | collective-permute-start | bytes 393224 | tf_op jit(solution)/shard_map/ppermute | solution.py:734
  7.8 5.2 %own_edges.1 = (bf16[1024,64]{1,0:T(8,128)(2,1)}, bf16[5,1024,128]{2,1,0:T(8,128)(2,1)}, f32[1024,128]{1,0:T(8,128)}, f32[1024,128]{1,0:T(8,128)}) custom-call(f32[64,128]{1,0:T(8,128)} %get-tuple-element.39.meta_ref, bf16[64,128]{1,0:T(8,128)(2,1)} %get-tuple-element.40.own_pos_ref, bf16[512,128]{1,0:T(8,128)(2,1)} %rbf_ref.5, bf16[128,640]{1,0:T(8,128)(2,1)} %rad_ref.5), custom_call_target="tpu_custom_call" | custom-call | flops 2147483648 | bytes 2834432 | tf_op jit(solution)/shard_map/own_edges/pallas_call | solution.py:55
  13.0 0.8 collective-permute-done.10
  13.9 2.2 %collective-permute-start.11 = (bf16[2,1,4,8,1024]{4,3,2,1,0:T(8,128)(2,1)S(1)}, bf16[2,1,4,8,1024]{4,3,2,1,0:T(8,128)(2,1)S(1)}, u32[]{:S(2)}, u32[]{:S(2)}) collective-permute-start(bf16[2,1,4,8,1024]{4,3,2,1,0:T(8,128)(2,1)S(1)} %get-tuple-element.84), channel_id=1, source_target_pairs={{0,2},{2,4},{4,6},{6,0},{1,3},{3,5},{5,7},{7,1},{8,10},{10,12},{12... | collective-permute-start | bytes 393224 | tf_op jit(solution)/shard_map/ppermute | solution.py:739
  16.1 2.1 %collective-permute-start.12 = (bf16[2,1,4,8,1024]{4,3,2,1,0:T(8,128)(2,1)S(1)}, bf16[2,1,4,8,1024]{4,3,2,1,0:T(8,128)(2,1)S(1)}, u32[]{:S(2)}, u32[]{:S(2)}) collective-permute-start(bf16[2,1,4,8,1024]{4,3,2,1,0:T(8,128)(2,1)S(1)} %get-tuple-element.85), channel_id=1, source_target_pairs={{2,0},{4,2},{6,4},{0,6},{3,1},{5,3},{7,5},{1,7},{10,8},{12,10},{14... | collective-permute-start | bytes 393224 | tf_op jit(solution)/shard_map/ppermute | solution.py:740
  18.4 3.8 %collective-permute-start.2 = (bf16[2,1,4,8,1024]{4,3,2,1,0:T(8,128)(2,1)S(1)}, bf16[2,1,4,8,1024]{4,3,2,1,0:T(8,128)(2,1)S(1)}, u32[]{:S(2)}, u32[]{:S(2)}) collective-permute-start(bf16[2,1,4,8,1024]{4,3,2,1,0:T(8,128)(2,1)S(1)} %get-tuple-element.87), channel_id=1, source_target_pairs={{2,0},{4,2},{6,4},{0,6},{3,1},{5,3},{7,5},{1,7},{10,8},{12,10},{14... | collective-permute-start | bytes 393224 | tf_op jit(solution)/shard_map/ppermute | solution.py:740
  22.3 3.8 %collective-permute-start.7 = (bf16[2,1,4,8,1280]{4,3,2,1,0:T(8,128)(2,1)S(1)}, bf16[2,1,4,8,1280]{4,3,2,1,0:T(8,128)(2,1)S(1)}, u32[]{:S(2)}, u32[]{:S(2)}) collective-permute-start(bf16[2,1,4,8,1280]{4,3,2,1,0:T(8,128)(2,1)S(1)} %get-tuple-element.83), channel_id=1, source_target_pairs={{2,0},{4,2},{6,4},{0,6},{3,1},{5,3},{7,5},{1,7},{10,8},{12,10},{14... | collective-permute-start | bytes 491528 | tf_op jit(solution)/shard_map/ppermute | solution.py:740
  26.4 7.3 %collective-permute-done.6 = bf16[2,1,4,8,1280]{4,3,2,1,0:T(8,128)(2,1)S(1)} collective-permute-done((bf16[2,1,4,8,1280]{4,3,2,1,0:T(8,128)(2,1)S(1)}, bf16[2,1,4,8,1280]{4,3,2,1,0:T(8,128)(2,1)S(1)}, u32[]{:S(2)}, u32[]{:S(2)}) %collective-permute-start.6) | collective-permute-done | bytes 163872 | tf_op jit(solution)/shard_map/ppermute | solution.py:739
  33.6 0.9 collective-permute-done.7
  34.7 1.7 %collective-permute-start.9 = (bf16[1,4,4,8,1280]{4,3,2,1,0:T(8,128)(2,1)S(1)}, bf16[1,4,4,8,1280]{4,3,2,1,0:T(8,128)(2,1)S(1)}, u32[]{:S(2)}, u32[]{:S(2)}) collective-permute-start(bf16[1,4,4,8,1280]{4,3,2,1,0:T(8,128)(2,1)S(1)} %get-tuple-element.76), channel_id=1, source_target_pairs={{8,0},{16,8},{24,16},{0,24},{9,1},{17,9},{25,17},{1,25},{10,2},{18... | collective-permute-start | bytes 983048 | tf_op jit(solution)/shard_map/ppermute | solution.py:740
  36.7 8.0 %collective-permute-done.8 = bf16[1,4,4,8,1280]{4,3,2,1,0:T(8,128)(2,1)S(1)} collective-permute-done((bf16[1,4,4,8,1280]{4,3,2,1,0:T(8,128)(2,1)S(1)}, bf16[1,4,4,8,1280]{4,3,2,1,0:T(8,128)(2,1)S(1)}, u32[]{:S(2)}, u32[]{:S(2)}) %collective-permute-start.8) | collective-permute-done | bytes 327712 | tf_op jit(solution)/shard_map/ppermute | solution.py:739
  46.0 18.7 %first_group.1 = (bf16[64,1152]{1,0:T(8,128)(2,1)}, bf16[1024,512]{1,0:T(8,128)(2,1)}, bf16[1024,64]{1,0:T(8,128)(2,1)}, bf16[4,64,256]{2,1,0:T(8,128)(2,1)}, bf...) custom-call(bf16[128,1280]{1,0:T(8,128)(2,1)} %bitcast.48, ...), custom_call_target="tpu_custom_call" | custom-call | flops 8589934592 | bytes 12962304 | tf_op jit(solution)/shard_map/first_group/pallas_call | solution.py:55
  65.6 14.0 %second_group.1 = (bf16[64,1024]{1,0:T(8,128)(2,1)}, f32[2048,128]{1,0:T(8,128)}, f32[2048,128]{1,0:T(8,128)}, f32[2048,128]{1,0:T(8,128)}, f32[64,128]{1,0:T(8,128)}) custom-call(bf16[128,1024]{1,0:T(8,128)(2,1)} %bitcast.50, bf16[256,1024]{1,0:T(8,128)(2,1)} %bitcast.27, bf16[128,1024]{1,0:T(8,128)(2,1)} %bitcast.51, bf16[64,3200]{1,0:T(8,128)(2,1)} %bitcast.40, ...), custom_call_target="tpu_custom_call" | custom-call | flops 8589934592 | bytes 9717760 | tf_op jit(solution)/shard_map/second_group/pallas_call | solution.py:55
  80.4 20.0 %third_group.1 = (bf16[64,3200]{1,0:T(8,128)(2,1)}, f32[1,64]{1,0:T(1,128)}, f32[8,64]{1,0:T(8,128)}, f32[8,128]{1,0:T(8,128)}, f32[8,256]{1,0:T(8,128)}, /*index=5*/f32[8,128]{1,0:T(8,128)}) custom-call(bf16[128,1024]{1,0:T(8,128)(2,1)} %bitcast.52, bf16[256,1024]{1,0:T(8,128)(2,1)} %bitcast.28, bf16[128,1024]{1,0:T(8,128)(2,1)} %bitcast.53, ...), custom_call_target="tpu_custom_call" | custom-call | flops 8589934592 | bytes 17469696 | tf_op jit(solution)/shard_map/third_group/pallas_call | solution.py:55
  100.4 3.6 %collective-permute-start.15 = (f32[8,128]{1,0:T(8,128)}, f32[8,128]{1,0:T(8,128)S(1)}, u32[]{:S(2)}, u32[]{:S(2)}) collective-permute-start(f32[8,128]{1,0:T(8,128)} %get-tuple-element.70), channel_id=1, source_target_pairs={{0,8},{8,16},{16,24},{24,0},{1,9},{9,17},{17,25},{25,1},{2,10},{10... | collective-permute-start | bytes 12296 | tf_op jit(solution)/shard_map/ppermute | solution.py:782
  104.0 1.0 collective-permute-done.15
  105.6 0.7 maximum_add_fusion
  106.3 3.8 %collective-permute-start.18 = (f32[8,256]{1,0:T(8,128)S(1)}, f32[8,256]{1,0:T(8,128)S(1)}, u32[]{:S(2)}, u32[]{:S(2)}) collective-permute-start(f32[8,256]{1,0:T(8,128)S(1)} %maximum_add_fusion), channel_id=1, source_target_pairs={{2,0},{4,2},{6,4},{0,6},{3,1},{5,3},{7,5},{1,7},{10,8},{12,10},{14... | collective-permute-start | bytes 24584 | tf_op jit(solution)/shard_map/ppermute | solution.py:787
  110.1 1.6 %collective-permute-done.17 = f32[8,256]{1,0:T(8,128)S(1)} collective-permute-done((f32[8,256]{1,0:T(8,128)S(1)}, f32[8,256]{1,0:T(8,128)S(1)}, u32[]{:S(2)}, u32[]{:S(2)}) %collective-permute-start.17) | collective-permute-done | bytes 8224 | tf_op jit(solution)/shard_map/ppermute | solution.py:786
  111.9 1.5 %collective-permute-start.19 = (f32[8,256]{1,0:T(8,128)S(1)}, f32[8,256]{1,0:T(8,128)S(1)}, u32[]{:S(2)}, u32[]{:S(2)}) collective-permute-start(f32[8,256]{1,0:T(8,128)S(1)} %fusion.1.mid_ref), channel_id=1, source_target_pairs={{0,1},{1,0},{2,3},{3,2},{4,5},{5,4},{6,7},{7,6},{8,9},{9,8},{10,11... | collective-permute-start | bytes 24584 | tf_op jit(solution)/shard_map/ppermute | solution.py:795
  113.5 2.1 %collective-permute-done.19.low_ref.high_ref = f32[8,256]{1,0:T(8,128)S(1)} collective-permute-done((f32[8,256]{1,0:T(8,128)S(1)}, f32[8,256]{1,0:T(8,128)S(1)}, u32[]{:S(2)}, u32[]{:S(2)}) %collective-permute-start.19) | collective-permute-done | bytes 8224 | tf_op jit(solution)/shard_map/ppermute | solution.py:795
  116.2 1.8 %forces.1 = f32[3,1,64]{2,1,0:T(1,128)} custom-call(f32[8,256]{1,0:T(8,128)} %copy-done.7, f32[8,256]{1,0:T(8,128)} %copy-done.6, f32[8,256]{1,0:T(8,128)} %copy-done.6, f32[8,64]{1,0:T(8,128)} %get-tuple-element.72.own_ref, f32[64,128]{1,0:T(8,128)} %get-tuple-element.39.meta_ref), custom_call_target="tpu_custom_call" | custom-call | flops 1048576 | bytes 60160 | tf_op jit(solution)/shard_map/forces/pallas_call | solution.py:55
  (71 shorter events, 5.2 us)
Async XLA Ops:
  2.8 19.3 %collective-permute-start.5 = (bf16[2,2,2,8,1280]{4,3,2,1,0:T(8,128)(2,1)}, bf16[2,2,2,8,1280]{4,3,2,1,0:T(8,128)(2,1)S(1)}, u32[]{:S(2)}, u32[]{:S(2)}) collective-permute-start(bf16[2,2,2,8,1280]{4,3,2,1,0:T(8,128)(2,1)} %bitcast.29), channel_id=1, source_target_pairs={{0,1},{1,0},{2,3},{3,2},{4,5},{5,4},{6,7},{7,6},{8,9},{9,8},{10,11... | collective-permute-start | bytes 491528 | tf_op jit(solution)/shard_map/ppermute | solution.py:734
  5.8 8.0 %collective-permute-start.10 = (bf16[2,2,2,8,1024]{4,3,2,1,0:T(8,128)(2,1)}, bf16[2,2,2,8,1024]{4,3,2,1,0:T(8,128)(2,1)S(1)}, u32[]{:S(2)}, u32[]{:S(2)}) collective-permute-start(bf16[2,2,2,8,1024]{4,3,2,1,0:T(8,128)(2,1)} %bitcast.35), channel_id=1, source_target_pairs={{0,1},{1,0},{2,3},{3,2},{4,5},{5,4},{6,7},{7,6},{8,9},{9,8},{10,11... | collective-permute-start | bytes 393224 | tf_op jit(solution)/shard_map/ppermute | solution.py:734
  5.8 12.4 %collective-permute-start = (bf16[2,2,2,8,1024]{4,3,2,1,0:T(8,128)(2,1)}, bf16[2,2,2,8,1024]{4,3,2,1,0:T(8,128)(2,1)S(1)}, u32[]{:S(2)}, u32[]{:S(2)}) collective-permute-start(bf16[2,2,2,8,1024]{4,3,2,1,0:T(8,128)(2,1)} %bitcast.32), channel_id=1, source_target_pairs={{0,1},{1,0},{2,3},{3,2},{4,5},{5,4},{6,7},{7,6},{8,9},{9,8},{10,11... | collective-permute-start | bytes 393224 | tf_op jit(solution)/shard_map/ppermute | solution.py:734
  7.8 6.0 %copy-start.5 = (bf16[64,1024]{1,0:T(8,128)(2,1)S(1)}, bf16[64,1024]{1,0:T(8,128)(2,1)}, u32[]{:S(2)}) copy-start(bf16[64,1024]{1,0:T(8,128)(2,1)} %get-tuple-element.57) | copy-start | bytes 393220
  13.9 8.3 %copy-start.3 = (bf16[64,1280]{1,0:T(8,128)(2,1)S(1)}, bf16[64,1280]{1,0:T(8,128)(2,1)}, u32[]{:S(2)}) copy-start(bf16[64,1280]{1,0:T(8,128)(2,1)} %get-tuple-element.43) | copy-start | bytes 491524
  13.9 8.4 %collective-permute-start.11 = (bf16[2,1,4,8,1024]{4,3,2,1,0:T(8,128)(2,1)S(1)}, bf16[2,1,4,8,1024]{4,3,2,1,0:T(8,128)(2,1)S(1)}, u32[]{:S(2)}, u32[]{:S(2)}) collective-permute-start(bf16[2,1,4,8,1024]{4,3,2,1,0:T(8,128)(2,1)S(1)} %get-tuple-element.84), channel_id=1, source_target_pairs={{0,2},{2,4},{4,6},{6,0},{1,3},{3,5},{5,7},{7,1},{8,10},{10,12},{12... | collective-permute-start | bytes 393224 | tf_op jit(solution)/shard_map/ppermute | solution.py:739
  16.1 10.1 %collective-permute-start.12 = (bf16[2,1,4,8,1024]{4,3,2,1,0:T(8,128)(2,1)S(1)}, bf16[2,1,4,8,1024]{4,3,2,1,0:T(8,128)(2,1)S(1)}, u32[]{:S(2)}, u32[]{:S(2)}) collective-permute-start(bf16[2,1,4,8,1024]{4,3,2,1,0:T(8,128)(2,1)S(1)} %get-tuple-element.85), channel_id=1, source_target_pairs={{2,0},{4,2},{6,4},{0,6},{3,1},{5,3},{7,5},{1,7},{10,8},{12,10},{14... | collective-permute-start | bytes 393224 | tf_op jit(solution)/shard_map/ppermute | solution.py:740
  18.3 16.4 %collective-permute-start.1 = (bf16[2,1,4,8,1024]{4,3,2,1,0:T(8,128)(2,1)S(1)}, bf16[2,1,4,8,1024]{4,3,2,1,0:T(8,128)(2,1)S(1)}, u32[]{:S(2)}, u32[]{:S(2)}) collective-permute-start(bf16[2,1,4,8,1024]{4,3,2,1,0:T(8,128)(2,1)S(1)} %get-tuple-element.86), channel_id=1, source_target_pairs={{0,2},{2,4},{4,6},{6,0},{1,3},{3,5},{5,7},{7,1},{8,10},{10,12},{12... | collective-permute-start | bytes 393224 | tf_op jit(solution)/shard_map/ppermute | solution.py:739
  18.4 18.1 %collective-permute-start.2 = (bf16[2,1,4,8,1024]{4,3,2,1,0:T(8,128)(2,1)S(1)}, bf16[2,1,4,8,1024]{4,3,2,1,0:T(8,128)(2,1)S(1)}, u32[]{:S(2)}, u32[]{:S(2)}) collective-permute-start(bf16[2,1,4,8,1024]{4,3,2,1,0:T(8,128)(2,1)S(1)} %get-tuple-element.87), channel_id=1, source_target_pairs={{2,0},{4,2},{6,4},{0,6},{3,1},{5,3},{7,5},{1,7},{10,8},{12,10},{14... | collective-permute-start | bytes 393224 | tf_op jit(solution)/shard_map/ppermute | solution.py:740
  22.3 11.3 %collective-permute-start.6 = (bf16[2,1,4,8,1280]{4,3,2,1,0:T(8,128)(2,1)S(1)}, bf16[2,1,4,8,1280]{4,3,2,1,0:T(8,128)(2,1)S(1)}, u32[]{:S(2)}, u32[]{:S(2)}) collective-permute-start(bf16[2,1,4,8,1280]{4,3,2,1,0:T(8,128)(2,1)S(1)} %get-tuple-element.82), channel_id=1, source_target_pairs={{0,2},{2,4},{4,6},{6,0},{1,3},{3,5},{5,7},{7,1},{8,10},{10,12},{12... | collective-permute-start | bytes 491528 | tf_op jit(solution)/shard_map/ppermute | solution.py:739
  22.3 12.1 %collective-permute-start.7 = (bf16[2,1,4,8,1280]{4,3,2,1,0:T(8,128)(2,1)S(1)}, bf16[2,1,4,8,1280]{4,3,2,1,0:T(8,128)(2,1)S(1)}, u32[]{:S(2)}, u32[]{:S(2)}) collective-permute-start(bf16[2,1,4,8,1280]{4,3,2,1,0:T(8,128)(2,1)S(1)} %get-tuple-element.83), channel_id=1, source_target_pairs={{2,0},{4,2},{6,4},{0,6},{3,1},{5,3},{7,5},{1,7},{10,8},{12,10},{14... | collective-permute-start | bytes 491528 | tf_op jit(solution)/shard_map/ppermute | solution.py:740
  26.2 8.4 %copy-start.1 = (bf16[2,4,4,8,1024]{4,3,2,1,0:T(8,128)(2,1)}, bf16[2,4,4,8,1024]{4,3,2,1,0:T(8,128)(2,1)S(1)}, u32[]{:S(2)}) copy-start(bf16[2,4,4,8,1024]{4,3,2,1,0:T(8,128)(2,1)S(1)} %pad_maximum_fusion.2) | copy-start | bytes 1572868
  26.3 38.5 %collective-permute-start.13 = (bf16[1,4,4,8,1024]{4,3,2,1,0:T(8,128)(2,1)S(1)}, bf16[1,4,4,8,1024]{4,3,2,1,0:T(8,128)(2,1)S(1)}, u32[]{:S(2)}, u32[]{:S(2)}) collective-permute-start(bf16[1,4,4,8,1024]{4,3,2,1,0:T(8,128)(2,1)S(1)} %get-tuple-element.79), channel_id=1, source_target_pairs={{0,8},{8,16},{16,24},{24,0},{1,9},{9,17},{17,25},{25,1},{2,10},{10... | collective-permute-start | bytes 786440 | tf_op jit(solution)/shard_map/ppermute | solution.py:739
  33.6 31.2 %collective-permute-start.14 = (bf16[1,4,4,8,1024]{4,3,2,1,0:T(8,128)(2,1)S(1)}, bf16[1,4,4,8,1024]{4,3,2,1,0:T(8,128)(2,1)S(1)}, u32[]{:S(2)}, u32[]{:S(2)}) collective-permute-start(bf16[1,4,4,8,1024]{4,3,2,1,0:T(8,128)(2,1)S(1)} %get-tuple-element.78), channel_id=1, source_target_pairs={{8,0},{16,8},{24,16},{0,24},{9,1},{17,9},{25,17},{1,25},{10,2},{18... | collective-permute-start | bytes 786440 | tf_op jit(solution)/shard_map/ppermute | solution.py:740
  34.6 10.0 %collective-permute-start.8 = (bf16[1,4,4,8,1280]{4,3,2,1,0:T(8,128)(2,1)S(1)}, bf16[1,4,4,8,1280]{4,3,2,1,0:T(8,128)(2,1)S(1)}, u32[]{:S(2)}, u32[]{:S(2)}) collective-permute-start(bf16[1,4,4,8,1280]{4,3,2,1,0:T(8,128)(2,1)S(1)} %get-tuple-element.77), channel_id=1, source_target_pairs={{0,8},{8,16},{16,24},{24,0},{1,9},{9,17},{17,25},{25,1},{2,10},{10... | collective-permute-start | bytes 983048 | tf_op jit(solution)/shard_map/ppermute | solution.py:739
  34.7 10.5 %collective-permute-start.9 = (bf16[1,4,4,8,1280]{4,3,2,1,0:T(8,128)(2,1)S(1)}, bf16[1,4,4,8,1280]{4,3,2,1,0:T(8,128)(2,1)S(1)}, u32[]{:S(2)}, u32[]{:S(2)}) collective-permute-start(bf16[1,4,4,8,1280]{4,3,2,1,0:T(8,128)(2,1)S(1)} %get-tuple-element.76), channel_id=1, source_target_pairs={{8,0},{16,8},{24,16},{0,24},{9,1},{17,9},{25,17},{1,25},{10,2},{18... | collective-permute-start | bytes 983048 | tf_op jit(solution)/shard_map/ppermute | solution.py:740
  36.5 28.2 %copy-start.2 = (bf16[2,4,4,8,1024]{4,3,2,1,0:T(8,128)(2,1)}, bf16[2,4,4,8,1024]{4,3,2,1,0:T(8,128)(2,1)S(1)}, u32[]{:S(2)}) copy-start(bf16[2,4,4,8,1024]{4,3,2,1,0:T(8,128)(2,1)S(1)} %pad_maximum_fusion.1) | copy-start | bytes 1572868
  36.6 43.0 %collective-permute-start.3 = (bf16[1,4,4,8,1024]{4,3,2,1,0:T(8,128)(2,1)S(1)}, bf16[1,4,4,8,1024]{4,3,2,1,0:T(8,128)(2,1)S(1)}, u32[]{:S(2)}, u32[]{:S(2)}) collective-permute-start(bf16[1,4,4,8,1024]{4,3,2,1,0:T(8,128)(2,1)S(1)} %get-tuple-element.81), channel_id=1, source_target_pairs={{0,8},{8,16},{16,24},{24,0},{1,9},{9,17},{17,25},{25,1},{2,10},{10... | collective-permute-start | bytes 786440 | tf_op jit(solution)/shard_map/ppermute | solution.py:739
  44.7 34.9 %collective-permute-start.4 = (bf16[1,4,4,8,1024]{4,3,2,1,0:T(8,128)(2,1)S(1)}, bf16[1,4,4,8,1024]{4,3,2,1,0:T(8,128)(2,1)S(1)}, u32[]{:S(2)}, u32[]{:S(2)}) collective-permute-start(bf16[1,4,4,8,1024]{4,3,2,1,0:T(8,128)(2,1)S(1)} %get-tuple-element.80), channel_id=1, source_target_pairs={{8,0},{16,8},{24,16},{0,24},{9,1},{17,9},{25,17},{1,25},{10,2},{18... | collective-permute-start | bytes 786440 | tf_op jit(solution)/shard_map/ppermute | solution.py:740
  100.4 4.7 %collective-permute-start.15 = (f32[8,128]{1,0:T(8,128)}, f32[8,128]{1,0:T(8,128)S(1)}, u32[]{:S(2)}, u32[]{:S(2)}) collective-permute-start(f32[8,128]{1,0:T(8,128)} %get-tuple-element.70), channel_id=1, source_target_pairs={{0,8},{8,16},{16,24},{24,0},{1,9},{9,17},{17,25},{25,1},{2,10},{10... | collective-permute-start | bytes 12296 | tf_op jit(solution)/shard_map/ppermute | solution.py:782
  104.0 1.5 %collective-permute-start.16 = (f32[8,128]{1,0:T(8,128)}, f32[8,128]{1,0:T(8,128)S(1)}, u32[]{:S(2)}, u32[]{:S(2)}) collective-permute-start(f32[8,128]{1,0:T(8,128)} %get-tuple-element.71), channel_id=1, source_target_pairs={{8,0},{16,8},{24,16},{0,24},{9,1},{17,9},{25,17},{1,25},{10,2},{18... | collective-permute-start | bytes 12296 | tf_op jit(solution)/shard_map/ppermute | solution.py:783
  106.3 5.4 %collective-permute-start.17 = (f32[8,256]{1,0:T(8,128)S(1)}, f32[8,256]{1,0:T(8,128)S(1)}, u32[]{:S(2)}, u32[]{:S(2)}) collective-permute-start(f32[8,256]{1,0:T(8,128)S(1)} %maximum_add_fusion), channel_id=1, source_target_pairs={{0,2},{2,4},{4,6},{6,0},{1,3},{3,5},{5,7},{7,1},{8,10},{10,12},{12... | collective-permute-start | bytes 24584 | tf_op jit(solution)/shard_map/ppermute | solution.py:786
  106.3 5.5 %collective-permute-start.18 = (f32[8,256]{1,0:T(8,128)S(1)}, f32[8,256]{1,0:T(8,128)S(1)}, u32[]{:S(2)}, u32[]{:S(2)}) collective-permute-start(f32[8,256]{1,0:T(8,128)S(1)} %maximum_add_fusion), channel_id=1, source_target_pairs={{2,0},{4,2},{6,4},{0,6},{3,1},{5,3},{7,5},{1,7},{10,8},{12,10},{14... | collective-permute-start | bytes 24584 | tf_op jit(solution)/shard_map/ppermute | solution.py:787
  111.9 3.7 %collective-permute-start.19 = (f32[8,256]{1,0:T(8,128)S(1)}, f32[8,256]{1,0:T(8,128)S(1)}, u32[]{:S(2)}, u32[]{:S(2)}) collective-permute-start(f32[8,256]{1,0:T(8,128)S(1)} %fusion.1.mid_ref), channel_id=1, source_target_pairs={{0,1},{1,0},{2,3},{3,2},{4,5},{5,4},{6,7},{7,6},{8,9},{9,8},{10,11... | collective-permute-start | bytes 24584 | tf_op jit(solution)/shard_map/ppermute | solution.py:795
  (10 other events, 15.9 us)

commit v3 on v2

--- a/solution.py
+++ b/solution.py
@@ -146,13 +146,13 @@
     return pre, mm(hidden, rad_ref[...]).astype(BF16)
 
 
-def own_spread(atoms):
-    shape = (atoms, STEP)
+def own_spread(atoms, size=STEP):
+    shape = (atoms, size)
     return (iota(shape, 1) % atoms == iota(shape, 0)).astype(F32).astype(BF16)
 
 
-def tiled(values):
-    return jnp.concatenate([values] * (STEP // values.shape[0]), axis=0)
+def tiled(values, size=STEP):
+    return jnp.concatenate([values] * (size // values.shape[0]), axis=0)
 
 
 def live_ghosts(meta_ref):
@@ -161,30 +161,32 @@
 
 def step_count(meta_ref):
     total = jnp.sum(live_ghosts(meta_ref)).astype(jnp.int32)
-    return jnp.maximum((total + (STEP - 1)) // STEP, GH_STEPS)
-
-
-def own_rows(step):
-    return pl.ds(step * STEP, STEP)
-
-
-def ghost_rows(step):
+    rows = GH_STEPS * STEP
+    return jnp.maximum((total + (rows - 1)) // rows, 1) * GH_STEPS
+
+
+def own_rows(step, size=STEP):
+    return pl.ds(step * size, size)
+
+
+def ghost_rows(step, size=STEP):
+    first = OWN_STEPS * STEP
     if isinstance(step, int):
-        return pl.ds(step * STEP, STEP), pl.ds((OWN_STEPS + step) * STEP, STEP)
-    base = pl.multiple_of(step * STEP, STEP)
-    later = pl.multiple_of(OWN_STEPS * STEP + step * STEP, STEP)
-    return pl.ds(base, STEP), pl.ds(later, STEP)
-
-
-def over_ghost_steps(steps, body):
-    for step in range(GH_STEPS):
+        return pl.ds(step * size, size), pl.ds(first + step * size, size)
+    base = pl.multiple_of(step * size, size)
+    return pl.ds(base, size), pl.ds(pl.multiple_of(first + base, size), size)
+
+
+def over_ghost_steps(steps, body, size=STEP):
+    static = GH_STEPS * STEP // size
+    for step in range(static):
         body(step)
 
     def again(step, carry):
         body(step)
         return carry
 
-    lax.fori_loop(GH_STEPS, steps, again, 0)
+    lax.fori_loop(static, (steps * STEP + (size - 1)) // size, again, 0)
 
 
 def block_diagonal(kinds, mix_ref, out_ref, wm, wmt, wo, wot):
@@ -223,104 +225,99 @@
 def run_pairs(
     pairs, kinds, first_col, own_ref, table, new_ref, new_base, oh_own, oh_gh, d_gh, dt_gh,
     gate_ref, radial_of, nw_ref, steps, wm, wmt, wo, wot, nf_s, mx_s, acc_s, gs_s, dot_ref,
-    grad_refs, en_ref,
+    grad_refs, en_ref, size=STEP,
 ):
     atoms = own_ref.shape[0]
     norm = 1.0 / math.sqrt(SLOTS)
-    spread_own = own_spread(atoms)
-    seen = set()
+    spread_own = own_spread(atoms, size)
+    own_steps = OWN_STEPS * STEP // size
+    begin, end = pair_cols(pairs[0]).start, pair_cols(pairs[-1]).stop
+    own_cols = slice(begin, end)
+    table_cols = slice(begin - first_col, end - first_col)
+    infos = []
+    for index, pair in enumerate(pairs):
+        degrees = PAIR_DEGREES[pair]
+        infos.append((slice(index * 2 * CH, (index + 1) * 2 * CH), degrees, kinds.index(degrees)))
 
     def gate_of(rows):
         gate = gate_ref[rows, :]
         return jnp.concatenate([gate, gate], axis=1)
 
-    for quad in range(0, len(pairs), 2):
-        both = pairs[quad : quad + 2]
-        infos = []
-        for index, pair in enumerate(both):
-            degrees = PAIR_DEGREES[pair]
-            cols = pair_cols(pair)
-            local = slice(cols.start - first_col, cols.stop - first_col)
-            infos.append((index, degrees, kinds.index(degrees), cols, local))
-
-        def forward(index, degrees, kind, rows, onehot, feats):
-            near = mm(onehot, feats).astype(BF16)
-            nf_s[index, rows, :] = near
+    def forward(rows, onehot, feats):
+        near = mm(onehot, feats).astype(BF16)
+        nf_s[rows, :] = near
+        gate = gate_of(rows)
+        messages = []
+        for cols, degrees, kind in infos:
             radial = jnp.concatenate([radial_of(d, rows) for d in degrees], axis=1)
-            mixed = mm(near * radial, wm[kind]).astype(BF16)
-            mx_s[index, rows, :] = mixed
-            return mixed * gate_of(rows)
-
-        def backward(rows, grads):
-            parts = {}
-            dots = None
-            gate = gate_of(rows)
-            for (index, degrees, kind, cols, local), grad in zip(infos, grads):
-                product = grad * mx_s[index, rows, :]
-                dot = (product[:, 0:CH] + product[:, CH:]).astype(F32)
-                dots = dot if dots is None else dots + dot
-                weighted = mm(grad * gate, wmt[kind]) * nf_s[index, rows, :].astype(F32)
-                for side in range(2):
-                    part = weighted[:, side * CH : (side + 1) * CH]
-                    degree = degrees[side]
-                    parts[degree] = parts[degree] + part if degree in parts else part
-            dot_ref[rows, :] = dots if quad == 0 else dot_ref[rows, :] + dots
-            for degree, part in parts.items():
-                ref = grad_refs[degree]
-                ref[rows, :] = ref[rows, :] + part if degree in seen else part
-
-        for index, degrees, kind, cols, local in infos:
-            own = own_ref[:, cols]
-            summed = None
-            for step in range(OWN_STEPS):
-                rows = own_rows(step)
-                message = forward(index, degrees, kind, rows, oh_own[rows, :], own)
-                part = mm(spread_own, message)
-                summed = part if summed is None else summed + part
-            acc_s[index] = summed
-
-        def ghost_forward(step):
-            here, rows = ghost_rows(step)
-            for index, degrees, kind, cols, local in infos:
-                message = forward(index, degrees, kind, rows, oh_gh[here, :], table[:, local])
-                acc_s[index] += mm(dt_gh[step], message)
-
-        over_ghost_steps(steps, ghost_forward)
-
-        for index, degrees, kind, cols, local in infos:
-            summed_low = (acc_s[index] * norm).astype(BF16)
-            updated = own_ref[:, cols].astype(F32) + mm(summed_low, wo[kind])
-            at = cols.start - new_base
-            new_ref[:, at : at + 2 * CH] = updated.astype(BF16)
-            weight = jnp.concatenate(
-                [nw_ref[d - 1 : d, :] * (1.0 / (2 * d + 1)) for d in degrees], axis=1
-            )
-            scale = weight * updated
-            energy = scale * updated
-            en_ref[...] += energy[:, 0:CH] + energy[:, CH:]
-            gs_s[index] = (mm((2.0 * scale).astype(BF16), wot[kind]) * norm).astype(BF16)
-
-        grads_own = [tiled(gs_s[index]) for index in range(len(both))]
-        for step in range(OWN_STEPS):
-            backward(own_rows(step), grads_own)
-
-        def ghost_backward(step):
-            here, rows = ghost_rows(step)
-            source = d_gh[here, :]
-            backward(rows, [mm(source, gs_s[i]).astype(BF16) for i in range(len(both))])
-
-        over_ghost_steps(steps, ghost_backward)
-        for pair in both:
-            seen.update(PAIR_DEGREES[pair])
+            mixed = mm(near[:, cols] * radial, wm[kind]).astype(BF16)
+            mx_s[rows, cols] = mixed
+            messages.append(mixed * gate)
+        return jnp.concatenate(messages, axis=1)
+
+    def backward(rows, grad):
+        parts = {}
+        dots = None
+        gate = gate_of(rows)
+        for cols, degrees, kind in infos:
+            product = grad[:, cols] * mx_s[rows, cols]
+            dot = (product[:, 0:CH] + product[:, CH:]).astype(F32)
+            dots = dot if dots is None else dots + dot
+            weighted = mm(grad[:, cols] * gate, wmt[kind]) * nf_s[rows, cols].astype(F32)
+            for side in range(2):
+                part = weighted[:, side * CH : (side + 1) * CH]
+                degree = degrees[side]
+                parts[degree] = parts[degree] + part if degree in parts else part
+        dot_ref[rows, :] = dots
+        for degree, part in parts.items():
+            grad_refs[degree][rows, :] = part
+
+    own = own_ref[:, own_cols]
+    summed = None
+    for step in range(own_steps):
+        rows = own_rows(step, size)
+        part = mm(spread_own, forward(rows, oh_own[rows, :], own))
+        summed = part if summed is None else summed + part
+    acc_s[...] = summed
+
+    def ghost_forward(step):
+        here, rows = ghost_rows(step, size)
+        message = forward(rows, oh_gh[here, :], table[:, table_cols])
+        acc_s[...] += mm(dt_gh[:, here], message)
+
+    over_ghost_steps(steps, ghost_forward, size)
+
+    for cols, degrees, kind in infos:
+        summed_low = (acc_s[:, cols] * norm).astype(BF16)
+        updated = own[:, cols].astype(F32) + mm(summed_low, wo[kind])
+        at = begin - new_base + cols.start
+        new_ref[:, at : at + 2 * CH] = updated.astype(BF16)
+        weight = jnp.concatenate(
+            [nw_ref[d - 1 : d, :] * (1.0 / (2 * d + 1)) for d in degrees], axis=1
+        )
+        scale = weight * updated
+        energy = scale * updated
+        en_ref[...] += energy[:, 0:CH] + energy[:, CH:]
+        gs_s[:, cols] = (mm((2.0 * scale).astype(BF16), wot[kind]) * norm).astype(BF16)
+
+    grad_own = tiled(gs_s[...], size)
+    for step in range(own_steps):
+        backward(own_rows(step, size), grad_own)
+
+    def ghost_backward(step):
+        here, rows = ghost_rows(step, size)
+        backward(rows, mm(d_gh[here, :], gs_s[...]).astype(BF16))
+
+    over_ghost_steps(steps, ghost_backward, size)
 
 
 def pair_scratch(atoms, edges, kinds):
     count = len(kinds)
     return [pltpu.VMEM((count, 2 * CH, 2 * CH), BF16) for _ in range(4)] + [
-        pltpu.VMEM((2, edges, 2 * CH), BF16),
-        pltpu.VMEM((2, edges, 2 * CH), BF16),
-        pltpu.VMEM((2, atoms, 2 * CH), F32),
-        pltpu.VMEM((2, atoms, 2 * CH), BF16),
+        pltpu.VMEM((edges, 8 * CH), BF16),
+        pltpu.VMEM((edges, 8 * CH), BF16),
+        pltpu.VMEM((atoms, 8 * CH), F32),
+        pltpu.VMEM((atoms, 8 * CH), BF16),
     ]
 
 
@@ -402,9 +399,6 @@
         copy.wait()
     ghpos[...] = (table[:, table.shape[1] - CH :].astype(F32) + shift).astype(BF16)
 
-    def radial_of(degree, rows):
-        return radial_gh[degree, pl.ds(rows.start - OWN_STEPS * STEP, STEP), :]
-
     def forward0(rows, onehot, feats, radial):
         near = mm(onehot, feats).astype(BF16)
         nf0_ref[rows, :] = near
@@ -422,7 +416,7 @@
         message = forward0(rows, oh_own[rows, :], own0, radial_own[0, rows, :])
         part = mm(spread_own, message)
         summed = part if summed is None else summed + part
-    acc_s[0, :, 0:CH] = summed
+    acc_s[:, 0:CH] = summed
 
     def ghost_start(step):
         here, rows = ghost_rows(step)
@@ -434,7 +428,7 @@
         edge_t = (iota((atoms, STEP), 1) + base).astype(F32)
         mine_t = jnp.logical_and(edge_t >= start_col, edge_t < end_col)
         spread = mine_t.astype(F32).astype(BF16)
-        dt_gh[step, :, :] = spread
+        dt_gh[:, here] = spread
         edge_col = edge[:, 0:1]
         slot = edge_col - jnp.sum(mine * start_row, axis=1, keepdims=True)
         listed = mm(source, row_high) * 16.0 + mm(source, row_low)
@@ -450,11 +444,11 @@
         for degree in range(5):
             radial_gh[degree, here, :] = radial[:, degree * CH : (degree + 1) * CH]
         message = forward0(rows, onehot, table[:, 0:CH], radial[:, 0:CH])
-        acc_s[0, :, 0:CH] += mm(spread, message)
+        acc_s[:, 0:CH] += mm(spread, message)
 
     over_ghost_steps(steps, ghost_start)
 
-    low0 = (acc_s[0, :, 0:CH] * norm).astype(BF16)
+    low0 = (acc_s[:, 0:CH] * norm).astype(BF16)
     updated0 = own0.astype(F32) + mm(low0, out_ref[0])
     new_ref[:, 0:CH] = updated0.astype(BF16)
     logistic = jax.nn.sigmoid(updated0)
@@ -466,7 +460,7 @@
     def radial_any(degree, rows):
         if isinstance(rows.start, int) and rows.start < OWN_STEPS * STEP:
             return radial_own[degree, rows, :]
-        return radial_of(degree, rows)
+        return radial_gh[degree, pl.ds(rows.start - OWN_STEPS * STEP, rows.size), :]
 
     run_pairs(
         pairs, kinds, 0, own_ref, table, new_ref, 0, oh_own, oh_gh, d_gh, dt_gh, gate_ref,
@@ -492,7 +486,7 @@
         struct(atoms, width - CH, dtype=BF16),
         struct(half, ghosts, dtype=BF16),
         struct(half, atoms, dtype=BF16),
-        struct(half // STEP, atoms, STEP, dtype=BF16),
+        struct(atoms, half, dtype=BF16),
         struct(5, half, CH, dtype=BF16),
         struct(half, CH),
         struct(half, CH),
@@ -534,7 +528,7 @@
     def radial_any(degree, rows):
         if isinstance(rows.start, int) and rows.start < OWN_STEPS * STEP:
             return radial_own[degree, rows, :]
-        return radial_gh[degree, pl.ds(rows.start - OWN_STEPS * STEP, STEP), :]
+        return radial_gh[degree, pl.ds(rows.start - OWN_STEPS * STEP, rows.size), :]
 
     for copy in copies:
         copy.wait()
@@ -604,14 +598,14 @@
     def radial_any(degree, rows):
         if isinstance(rows.start, int) and rows.start < OWN_STEPS * STEP:
             return radial_own[degree, rows, :]
-        return radial_gh[degree, pl.ds(rows.start - OWN_STEPS * STEP, STEP), :]
+        return radial_gh[degree, pl.ds(rows.start - OWN_STEPS * STEP, rows.size), :]
 
     for copy in copies:
         copy.wait()
     run_pairs(
         pairs, kinds, base, own_ref, table, new_ref, 0, oh_own, oh_gh, d_gh, dt_gh, gate_ref,
         radial_any, nw_ref, steps, wm, wmt, wo, wot, nf_s, mx_s, acc_s, gs_s, dot_c,
-        {4: gr4_b}, en_s,
+        {4: gr4_b}, en_s, 2 * STEP,
     )
 
     def finish(rows, grad, pre, unit):
@@ -647,7 +641,7 @@
         pull, top, rest = finish(rows, grad, pre_gh[here, :], unit_gh[here, :])
         pull_top = pull.astype(BF16)
         pull_rest = (pull - pull_top.astype(F32)).astype(BF16)
-        spread = dt_gh[step]
+        spread = dt_gh[:, here]
         src_s[...] += mm(spread, pull_top) + mm(spread, pull_rest)
         onehot = oh_gh[here, :]
         fgh_s[...] += mm(top, onehot) + mm(rest, onehot)
@@ -702,25 +696,6 @@
     )
 
 
-def layer(pieces, feats, own_pos, meta, rbf, rad, mix, out, ew, nw):
-    oh_own, radial_own, pre_own, unit_own = own_stage(meta, own_pos, rbf, rad)
-    (
-        new_a, oh_gh, d_gh, dt_gh, radial_gh, pre_gh, unit_gh, m0, gate, nf0, gs0, dot_a, gr1,
-        gr2, en_a,
-    ) = first_stage(
-        pieces[0], feats, own_pos, meta, rbf, rad, mix, out, ew, nw, oh_own, radial_own
-    )
-    new_b, dot_b, gr3, gr4, en_b = second_stage(
-        pieces[1], feats, meta, mix, out, nw, oh_own, radial_own, oh_gh, d_gh, dt_gh, radial_gh,
-        gate,
-    )
-    return third_stage(
-        pieces[2], feats, meta, mix, out, nw, oh_own, radial_own, oh_gh, d_gh, dt_gh, radial_gh,
-        gate, rbf, rad, pre_own, pre_gh, unit_own, unit_gh, m0, nf0, gs0, dot_a, dot_b, gr1, gr2,
-        gr3, gr4, en_a, en_b, new_a, new_b,
-    )
-
-
 def ring(axis):
     peers = lax.axis_size(axis)
     up = [(i, (i + 1) % peers) for i in range(peers)]
@@ -741,13 +716,14 @@
     return before, after
 
 
-def exchange(cells):
-    block = cells.reshape(2, 2, 2, 8, cells.shape[1])
-    for axis, dim in (("gz", 2), ("gy", 1)):
-        before, after = neighbours_of(block, axis, dim)
-        block = jnp.concatenate([before, block, after], axis=dim)
+def grown(block, axis, dim):
+    before, after = neighbours_of(block, axis, dim)
+    return jnp.concatenate([before, block, after], axis=dim)
+
+
+def ghost_pieces(block):
     before, after = neighbours_of(block, "gx", 0)
-    return tuple(piece.reshape(-1, cells.shape[1]) for piece in (before, block, after))
+    return tuple(piece.reshape(-1, block.shape[-1]) for piece in (before, block, after))
 
 
 def forces_kernel(mid_ref, low_ref, high_ref, own_ref, meta_ref, out_ref):
@@ -817,10 +793,35 @@
     *cells, own_pos, meta = make_cells(
         feats, places, neighbours[0, 0, 0].T, counts[0, 0], cell_atoms[0, 0]
     )
-    pieces = [exchange(part) for part in cells]
-    new, energy, own, low, mid, high = layer(
-        pieces, feats, own_pos, meta, rbf_weight, radial_weight, mix_weight, out_weight,
-        energy_weight[None], norm_weight,
+    hold = lax.optimization_barrier
+    blocks = [part.reshape(2, 2, 2, 8, part.shape[1]) for part in cells]
+    block0, block1, block2 = (grown(block, "gz", 2) for block in blocks)
+    block0, own_pos, meta = hold((block0, own_pos, meta))
+    block0 = grown(block0, "gy", 1)
+    oh_own, radial_own, pre_own, unit_own = own_stage(meta, own_pos, rbf_weight, radial_weight)
+    block0, block1 = hold((block0, block1))
+    pieces0 = ghost_pieces(block0)
+    block1 = grown(block1, "gy", 1)
+    pieces0, block1, block2 = hold((pieces0, block1, block2))
+    pieces1 = ghost_pieces(block1)
+    block2 = grown(block2, "gy", 1)
+    (
+        new_a, oh_gh, d_gh, dt_gh, radial_gh, pre_gh, unit_gh, m0, gate, nf0, gs0, dot_a, gr1,
+        gr2, en_a,
+    ) = first_stage(
+        pieces0, feats, own_pos, meta, rbf_weight, radial_weight, mix_weight, out_weight,
+        energy_weight[None], norm_weight, oh_own, radial_own,
+    )
+    gate, block2 = hold((gate, block2))
+    pieces2 = ghost_pieces(block2)
+    shared = (
+        feats, meta, mix_weight, out_weight, norm_weight, oh_own, radial_own, oh_gh, d_gh, dt_gh,
+        radial_gh, gate,
+    )
+    new_b, dot_b, gr3, gr4, en_b = second_stage(pieces1, *shared)
+    new, energy, own, low, mid, high = third_stage(
+        pieces2, *shared, rbf_weight, radial_weight, pre_own, pre_gh, unit_own, unit_gh, m0, nf0,
+        gs0, dot_a, dot_b, gr1, gr2, gr3, gr4, en_a, en_b, new_a, new_b,
     )
     forces = give_back(low, mid, high, own, meta)
     return (

time: 118 us -> 104 us (0.88)
  Pallas kernels: 61.9 us -> 51.6 us
  waiting for transfers between devices: 22.9 us -> 20.7 us
  starting transfers between devices: 27.8 us -> 26.1 us
    pallas_call x6, Pallas kernels: 61.9 us -> 51.6 us  [call(): pl.pallas_call(kernel, out_shape=out_shape, in_specs=specs or [pl.BlockSp...]
    ppermute x6, waiting for transfers between devices: 15.3 us -> 5.03 us  [neighbours_of(): lax.ppermute(lax.slice_in_dim(block, length - 1, length, axis=dim), axis,...]
    ppermute x3, waiting for transfers between devices: 0.82 us -> 8.05 us  [neighbours_of(): other = lax.ppermute(block, axis, up)]
    ppermute x1, starting transfers between devices: 3.62 us -> 0.06 us  [give_back(): from_low = lax.ppermute(high, 'gx', up)]
    ppermute x1, starting transfers between devices: 0.01 us -> 1.73 us  [give_back(): from_high = lax.ppermute(low, 'gx', down)]
    unnamed x28 -> x26, local copies, waits for them, and re-layouts: 2.94 us -> 2.2 us
  transfers between devices with their start and end apart: 20 -> 20, of which waited for: 9 -> 8; matrix products, arithmetic and copies ran while one was open for 1% -> 0% of each run, Pallas kernels for 32% -> 30%
where the time goes in v3:
time: 104 us
  Pallas kernels  51.6 us (50%)
  starting transfers between devices  26.1 us (25%)
  waiting for transfers between devices  20.7 us (20%)
  local copies, waits for them, and re-layouts  2.56 us (2%)
  other arithmetic  2.01 us (2%)
    pallas_call x6, Pallas kernels, call(): pl.pallas_call(kernel, out_shape=out_shape, in_specs=specs or [pl.BlockSp...  51.6 us
    ppermute x6, starting transfers between devices, neighbours_of(): after = lax.ppermute(lax.slice_in_dim(block, 0, 1, axis=dim), axis, down)  10.6 us
    ppermute x3, waiting for transfers between devices, neighbours_of(): other = lax.ppermute(block, axis, up)  8.05 us
    ppermute x6, waiting for transfers between devices, neighbours_of(): lax.ppermute(lax.slice_in_dim(block, length - 1, length, axis=dim), axis,...  5.03 us
    ppermute x3, starting transfers between devices, neighbours_of(): other = lax.ppermute(block, axis, up)  4.99 us
    ppermute x6, starting transfers between devices, neighbours_of(): lax.ppermute(lax.slice_in_dim(block, length - 1, length, axis=dim), axis,...  3.36 us
    ppermute x1, starting transfers between devices, give_back(): from_high = lax.ppermute(mid, 'gy', down)  3.09 us
    ppermute x6, waiting for transfers between devices, neighbours_of(): after = lax.ppermute(lax.slice_in_dim(block, 0, 1, axis=dim), axis, down)  2.33 us
  transfers between devices with their start and end apart: 20, of which 8 were waited for; matrix products, arithmetic and copies ran while one was open for 0% of the time, Pallas kernels for 30%

profile of v3, /device:TPU:0, one launch (start us, length us, event | category | flops | bytes accessed | tf_op | source)
XLA Modules:
  0.0 104.0 jit_solution(12509079507692134897)
XLA Ops:
  0.6 2.2 %cells.1 = (bf16[64,1280]{1,0:T(8,128)(2,1)}, bf16[64,1024]{1,0:T(8,128)(2,1)}, bf16[64,1024]{1,0:T(8,128)(2,1)}, bf16[64,128]{1,0:T(8,128)(2,1)}, f32[64,128]{1,0:T(8,128)}) custom-call(bf16[64,3200]{1,0:T(8,128)(2,1)} %bitcast.29, f32[3,1,64]{2,1,0:T(1,128)} %bitcast.41, s32[32,64]{1,0:T(8,128)} %bitcast.40, s32[1,64]{1,0:T(1,128)} %bitcast.43, ...), custom_call_target="tpu_custom_call" | custom-call | flops 67108864 | bytes 894208 | tf_op jit(solution)/shard_map/cells/pallas_call | solution.py:55
  2.8 3.0 %collective-permute-start.3 = (bf16[2,2,2,8,1024]{4,3,2,1,0:T(8,128)(2,1)}, bf16[2,2,2,8,1024]{4,3,2,1,0:T(8,128)(2,1)S(1)}, u32[]{:S(2)}, u32[]{:S(2)}) collective-permute-start(bf16[2,2,2,8,1024]{4,3,2,1,0:T(8,128)(2,1)} %bitcast.37), channel_id=1, source_target_pairs={{0,1},{1,0},{2,3},{3,2},{4,5},{5,4},{6,7},{7,6},{8,9},{9,8},{10,11... | collective-permute-start | bytes 393224 | tf_op jit(solution)/shard_map/ppermute | solution.py:709
  5.9 2.0 %collective-permute-start.8 = (bf16[2,2,2,8,1024]{4,3,2,1,0:T(8,128)(2,1)}, bf16[2,2,2,8,1024]{4,3,2,1,0:T(8,128)(2,1)S(1)}, u32[]{:S(2)}, u32[]{:S(2)}) collective-permute-start(bf16[2,2,2,8,1024]{4,3,2,1,0:T(8,128)(2,1)} %bitcast.35), channel_id=1, source_target_pairs={{0,1},{1,0},{2,3},{3,2},{4,5},{5,4},{6,7},{7,6},{8,9},{9,8},{10,11... | collective-permute-start | bytes 393224 | tf_op jit(solution)/shard_map/ppermute | solution.py:709
  7.8 2.6 %collective-permute-done.3 = bf16[2,2,2,8,1024]{4,3,2,1,0:T(8,128)(2,1)S(1)} collective-permute-done((bf16[2,2,2,8,1024]{4,3,2,1,0:T(8,128)(2,1)}, bf16[2,2,2,8,1024]{4,3,2,1,0:T(8,128)(2,1)S(1)}, u32[]{:S(2)}, u32[]{:S(2)}) %collective-permute-start.3) | collective-permute-done | bytes 131104 | tf_op jit(solution)/shard_map/ppermute | solution.py:709
  10.4 5.5 %collective-permute-done.8 = bf16[2,2,2,8,1024]{4,3,2,1,0:T(8,128)(2,1)S(1)} collective-permute-done((bf16[2,2,2,8,1024]{4,3,2,1,0:T(8,128)(2,1)}, bf16[2,2,2,8,1024]{4,3,2,1,0:T(8,128)(2,1)S(1)}, u32[]{:S(2)}, u32[]{:S(2)}) %collective-permute-start.8) | collective-permute-done | bytes 131104 | tf_op jit(solution)/shard_map/ppermute | solution.py:709
  16.9 1.8 %collective-permute-start.1 = (bf16[2,1,4,8,1280]{4,3,2,1,0:T(8,128)(2,1)S(1)}, bf16[2,1,4,8,1280]{4,3,2,1,0:T(8,128)(2,1)S(1)}, u32[]{:S(2)}, u32[]{:S(2)}) collective-permute-start(bf16[2,1,4,8,1280]{4,3,2,1,0:T(8,128)(2,1)S(1)} %get-tuple-element.106), channel_id=1, source_target_pairs={{0,2},{2,4},{4,6},{6,0},{1,3},{3,5},{5,7},{7,1},{8,10},{10,12},{12... | collective-permute-start | bytes 491528 | tf_op jit(solution)/shard_map/ppermute | solution.py:714
  18.7 2.1 %collective-permute-start.2 = (bf16[2,1,4,8,1280]{4,3,2,1,0:T(8,128)(2,1)S(1)}, bf16[2,1,4,8,1280]{4,3,2,1,0:T(8,128)(2,1)S(1)}, u32[]{:S(2)}, u32[]{:S(2)}) collective-permute-start(bf16[2,1,4,8,1280]{4,3,2,1,0:T(8,128)(2,1)S(1)} %get-tuple-element.107), channel_id=1, source_target_pairs={{2,0},{4,2},{6,4},{0,6},{3,1},{5,3},{7,5},{1,7},{10,8},{12,10},{14... | collective-permute-start | bytes 491528 | tf_op jit(solution)/shard_map/ppermute | solution.py:715
  20.9 5.0 %collective-permute-done.1 = bf16[2,1,4,8,1280]{4,3,2,1,0:T(8,128)(2,1)S(1)} collective-permute-done((bf16[2,1,4,8,1280]{4,3,2,1,0:T(8,128)(2,1)S(1)}, bf16[2,1,4,8,1280]{4,3,2,1,0:T(8,128)(2,1)S(1)}, u32[]{:S(2)}, u32[]{:S(2)}) %collective-permute-start.1) | collective-permute-done | bytes 163872 | tf_op jit(solution)/shard_map/ppermute | solution.py:714
  27.7 1.3 %collective-permute-start.6 = (bf16[2,1,4,8,1024]{4,3,2,1,0:T(8,128)(2,1)S(1)}, bf16[2,1,4,8,1024]{4,3,2,1,0:T(8,128)(2,1)S(1)}, u32[]{:S(2)}, u32[]{:S(2)}) collective-permute-start(bf16[2,1,4,8,1024]{4,3,2,1,0:T(8,128)(2,1)S(1)} %get-tuple-element.110), channel_id=1, source_target_pairs={{0,2},{2,4},{4,6},{6,0},{1,3},{3,5},{5,7},{7,1},{8,10},{10,12},{12... | collective-permute-start | bytes 393224 | tf_op jit(solution)/shard_map/ppermute | solution.py:714
  29.0 2.6 %collective-permute-start.7 = (bf16[2,1,4,8,1024]{4,3,2,1,0:T(8,128)(2,1)S(1)}, bf16[2,1,4,8,1024]{4,3,2,1,0:T(8,128)(2,1)S(1)}, u32[]{:S(2)}, u32[]{:S(2)}) collective-permute-start(bf16[2,1,4,8,1024]{4,3,2,1,0:T(8,128)(2,1)S(1)} %get-tuple-element.111), channel_id=1, source_target_pairs={{2,0},{4,2},{6,4},{0,6},{3,1},{5,3},{7,5},{1,7},{10,8},{12,10},{14... | collective-permute-start | bytes 393224 | tf_op jit(solution)/shard_map/ppermute | solution.py:715
  31.6 5.1 %own_edges.1 = (bf16[1024,64]{1,0:T(8,128)(2,1)}, bf16[5,1024,128]{2,1,0:T(8,128)(2,1)}, f32[1024,128]{1,0:T(8,128)}, f32[1024,128]{1,0:T(8,128)}) custom-call(f32[64,128]{1,0:T(8,128)} %get-tuple-element.62.meta_ref, bf16[64,128]{1,0:T(8,128)(2,1)} %get-tuple-element.61.own_pos_ref, bf16[512,128]{1,0:T(8,128)(2,1)} %rbf_ref.5, bf16[128,640]{1,0:T(8,128)(2,1)} %rad_ref.5), custom_call_target="tpu_custom_call" | custom-call | flops 2147483648 | bytes 2834432 | tf_op jit(solution)/shard_map/own_edges/pallas_call | solution.py:55
  38.1 2.0 %collective-permute-start.10 = (bf16[2,1,4,8,1024]{4,3,2,1,0:T(8,128)(2,1)S(1)}, bf16[2,1,4,8,1024]{4,3,2,1,0:T(8,128)(2,1)S(1)}, u32[]{:S(2)}, u32[]{:S(2)}) collective-permute-start(bf16[2,1,4,8,1024]{4,3,2,1,0:T(8,128)(2,1)S(1)} %get-tuple-element.109), channel_id=1, source_target_pairs={{2,0},{4,2},{6,4},{0,6},{3,1},{5,3},{7,5},{1,7},{10,8},{12,10},{14... | collective-permute-start | bytes 393224 | tf_op jit(solution)/shard_map/ppermute | solution.py:715
  40.3 1.7 %collective-permute-start.14 = (bf16[1,4,4,8,1024]{4,3,2,1,0:T(8,128)(2,1)S(1)}, bf16[1,4,4,8,1024]{4,3,2,1,0:T(8,128)(2,1)S(1)}, u32[]{:S(2)}, u32[]{:S(2)}) collective-permute-start(bf16[1,4,4,8,1024]{4,3,2,1,0:T(8,128)(2,1)S(1)} %get-tuple-element.102), channel_id=1, source_target_pairs={{8,0},{16,8},{24,16},{0,24},{9,1},{17,9},{25,17},{1,25},{10,2},{18... | collective-permute-start | bytes 786440 | tf_op jit(solution)/shard_map/ppermute | solution.py:715
  42.1 15.3 %first_group.1 = (bf16[64,1152]{1,0:T(8,128)(2,1)}, bf16[1024,512]{1,0:T(8,128)(2,1)}, bf16[1024,64]{1,0:T(8,128)(2,1)}, bf16[64,1024]{1,0:T(8,128)(2,1)}, bf16[...) custom-call(bf16[128,1280]{1,0:T(8,128)(2,1)} %bitcast.46, ...), custom_call_target="tpu_custom_call" | custom-call | flops 8589934592 | bytes 12962304 | tf_op jit(solution)/shard_map/first_group/pallas_call | solution.py:55
  57.6 1.7 %collective-permute-start.12 = (bf16[1,4,4,8,1024]{4,3,2,1,0:T(8,128)(2,1)S(1)}, bf16[1,4,4,8,1024]{4,3,2,1,0:T(8,128)(2,1)S(1)}, u32[]{:S(2)}, u32[]{:S(2)}) collective-permute-start(bf16[1,4,4,8,1024]{4,3,2,1,0:T(8,128)(2,1)S(1)} %get-tuple-element.104), channel_id=1, source_target_pairs={{8,0},{16,8},{24,16},{0,24},{9,1},{17,9},{25,17},{1,25},{10,2},{18... | collective-permute-start | bytes 786440 | tf_op jit(solution)/shard_map/ppermute | solution.py:715
  60.1 10.5 %second_group.1 = (bf16[64,1024]{1,0:T(8,128)(2,1)}, f32[2048,128]{1,0:T(8,128)}, f32[2048,128]{1,0:T(8,128)}, f32[2048,128]{1,0:T(8,128)}, f32[64,128]{1,0:T(8,128)}) custom-call(bf16[128,1024]{1,0:T(8,128)(2,1)} %bitcast.47, bf16[256,1024]{1,0:T(8,128)(2,1)} %bitcast.27, bf16[128,1024]{1,0:T(8,128)(2,1)} %bitcast.48, bf16[64,3200]{1,0:T(8,128)(2,1)} %bitcast.31, ...), custom_call_target="tpu_custom_call" | custom-call | flops 8589934592 | bytes 9717760 | tf_op jit(solution)/shard_map/second_group/pallas_call | solution.py:55
  71.5 16.7 %third_group.1 = (bf16[64,3200]{1,0:T(8,128)(2,1)}, f32[1,64]{1,0:T(1,128)}, f32[8,64]{1,0:T(8,128)}, f32[8,128]{1,0:T(8,128)}, f32[8,256]{1,0:T(8,128)}, /*index=5*/f32[8,128]{1,0:T(8,128)}) custom-call(bf16[128,1024]{1,0:T(8,128)(2,1)} %bitcast.49, bf16[256,1024]{1,0:T(8,128)(2,1)} %bitcast.28, bf16[128,1024]{1,0:T(8,128)(2,1)} %bitcast.50, ...), custom_call_target="tpu_custom_call" | custom-call | flops 8589934592 | bytes 17469696 | tf_op jit(solution)/shard_map/third_group/pallas_call | solution.py:55
  88.2 1.7 %collective-permute-start.16 = (f32[8,128]{1,0:T(8,128)}, f32[8,128]{1,0:T(8,128)S(1)}, u32[]{:S(2)}, u32[]{:S(2)}) collective-permute-start(f32[8,128]{1,0:T(8,128)} %get-tuple-element.95), channel_id=1, source_target_pairs={{8,0},{16,8},{24,16},{0,24},{9,1},{17,9},{25,17},{1,25},{10,2},{18... | collective-permute-start | bytes 12296 | tf_op jit(solution)/shard_map/ppermute | solution.py:759
  90.0 1.5 %collective-permute-done.15 = f32[8,128]{1,0:T(8,128)S(1)} collective-permute-done((f32[8,128]{1,0:T(8,128)}, f32[8,128]{1,0:T(8,128)S(1)}, u32[]{:S(2)}, u32[]{:S(2)}) %collective-permute-start.15) | collective-permute-done | bytes 4128 | tf_op jit(solution)/shard_map/ppermute | solution.py:758
  92.9 3.1 %collective-permute-start.18 = (f32[8,256]{1,0:T(8,128)S(1)}, f32[8,256]{1,0:T(8,128)S(1)}, u32[]{:S(2)}, u32[]{:S(2)}) collective-permute-start(f32[8,256]{1,0:T(8,128)S(1)} %maximum_add_fusion), channel_id=1, source_target_pairs={{2,0},{4,2},{6,4},{0,6},{3,1},{5,3},{7,5},{1,7},{10,8},{12,10},{14... | collective-permute-start | bytes 24584 | tf_op jit(solution)/shard_map/ppermute | solution.py:763
  96.0 1.6 %collective-permute-done.17 = f32[8,256]{1,0:T(8,128)S(1)} collective-permute-done((f32[8,256]{1,0:T(8,128)S(1)}, f32[8,256]{1,0:T(8,128)S(1)}, u32[]{:S(2)}, u32[]{:S(2)}) %collective-permute-start.17) | collective-permute-done | bytes 8224 | tf_op jit(solution)/shard_map/ppermute | solution.py:762
  97.9 1.5 %collective-permute-start.19 = (f32[8,256]{1,0:T(8,128)S(1)}, f32[8,256]{1,0:T(8,128)S(1)}, u32[]{:S(2)}, u32[]{:S(2)}) collective-permute-start(f32[8,256]{1,0:T(8,128)S(1)} %fusion.1.mid_ref), channel_id=1, source_target_pairs={{0,1},{1,0},{2,3},{3,2},{4,5},{5,4},{6,7},{7,6},{8,9},{9,8},{10,11... | collective-permute-start | bytes 24584 | tf_op jit(solution)/shard_map/ppermute | solution.py:771
  99.4 2.1 %collective-permute-done.19.low_ref.high_ref = f32[8,256]{1,0:T(8,128)S(1)} collective-permute-done((f32[8,256]{1,0:T(8,128)S(1)}, f32[8,256]{1,0:T(8,128)S(1)}, u32[]{:S(2)}, u32[]{:S(2)}) %collective-permute-start.19) | collective-permute-done | bytes 8224 | tf_op jit(solution)/shard_map/ppermute | solution.py:771
  102.1 1.8 %forces.1 = f32[3,1,64]{2,1,0:T(1,128)} custom-call(f32[8,256]{1,0:T(8,128)} %copy-done.6, f32[8,256]{1,0:T(8,128)} %copy-done.5, f32[8,256]{1,0:T(8,128)} %copy-done.5, f32[8,64]{1,0:T(8,128)} %get-tuple-element.96.own_ref, f32[64,128]{1,0:T(8,128)} %get-tuple-element.62.meta_ref), custom_call_target="tpu_custom_call" | custom-call | flops 1048576 | bytes 60160 | tf_op jit(solution)/shard_map/forces/pallas_call | solution.py:55
  (69 shorter events, 8.6 us)
Async XLA Ops:
  2.8 18.0 %copy-start.4 = (bf16[64,1024]{1,0:T(8,128)(2,1)S(1)}, bf16[64,1024]{1,0:T(8,128)(2,1)}, u32[]{:S(2)}) copy-start(bf16[64,1024]{1,0:T(8,128)(2,1)} %get-tuple-element.54) | copy-start | bytes 393220
  2.8 7.6 %collective-permute-start.3 = (bf16[2,2,2,8,1024]{4,3,2,1,0:T(8,128)(2,1)}, bf16[2,2,2,8,1024]{4,3,2,1,0:T(8,128)(2,1)S(1)}, u32[]{:S(2)}, u32[]{:S(2)}) collective-permute-start(bf16[2,2,2,8,1024]{4,3,2,1,0:T(8,128)(2,1)} %bitcast.37), channel_id=1, source_target_pairs={{0,1},{1,0},{2,3},{3,2},{4,5},{5,4},{6,7},{7,6},{8,9},{9,8},{10,11... | collective-permute-start | bytes 393224 | tf_op jit(solution)/shard_map/ppermute | solution.py:709
  5.8 10.1 %collective-permute-start = (bf16[2,2,2,8,1280]{4,3,2,1,0:T(8,128)(2,1)}, bf16[2,2,2,8,1280]{4,3,2,1,0:T(8,128)(2,1)S(1)}, u32[]{:S(2)}, u32[]{:S(2)}) collective-permute-start(bf16[2,2,2,8,1280]{4,3,2,1,0:T(8,128)(2,1)} %bitcast.33), channel_id=1, source_target_pairs={{0,1},{1,0},{2,3},{3,2},{4,5},{5,4},{6,7},{7,6},{8,9},{9,8},{10,11... | collective-permute-start | bytes 491528 | tf_op jit(solution)/shard_map/ppermute | solution.py:709
  5.9 15.0 %copy-start.3 = (bf16[64,1024]{1,0:T(8,128)(2,1)S(1)}, bf16[64,1024]{1,0:T(8,128)(2,1)}, u32[]{:S(2)}) copy-start(bf16[64,1024]{1,0:T(8,128)(2,1)} %get-tuple-element.57) | copy-start | bytes 393220
  5.9 10.0 %collective-permute-start.8 = (bf16[2,2,2,8,1024]{4,3,2,1,0:T(8,128)(2,1)}, bf16[2,2,2,8,1024]{4,3,2,1,0:T(8,128)(2,1)S(1)}, u32[]{:S(2)}, u32[]{:S(2)}) collective-permute-start(bf16[2,2,2,8,1024]{4,3,2,1,0:T(8,128)(2,1)} %bitcast.35), channel_id=1, source_target_pairs={{0,1},{1,0},{2,3},{3,2},{4,5},{5,4},{6,7},{7,6},{8,9},{9,8},{10,11... | collective-permute-start | bytes 393224 | tf_op jit(solution)/shard_map/ppermute | solution.py:709
  16.9 9.0 %collective-permute-start.1 = (bf16[2,1,4,8,1280]{4,3,2,1,0:T(8,128)(2,1)S(1)}, bf16[2,1,4,8,1280]{4,3,2,1,0:T(8,128)(2,1)S(1)}, u32[]{:S(2)}, u32[]{:S(2)}) collective-permute-start(bf16[2,1,4,8,1280]{4,3,2,1,0:T(8,128)(2,1)S(1)} %get-tuple-element.106), channel_id=1, source_target_pairs={{0,2},{2,4},{4,6},{6,0},{1,3},{3,5},{5,7},{7,1},{8,10},{10,12},{12... | collective-permute-start | bytes 491528 | tf_op jit(solution)/shard_map/ppermute | solution.py:714
  18.7 8.3 %collective-permute-start.2 = (bf16[2,1,4,8,1280]{4,3,2,1,0:T(8,128)(2,1)S(1)}, bf16[2,1,4,8,1280]{4,3,2,1,0:T(8,128)(2,1)S(1)}, u32[]{:S(2)}, u32[]{:S(2)}) collective-permute-start(bf16[2,1,4,8,1280]{4,3,2,1,0:T(8,128)(2,1)S(1)} %get-tuple-element.107), channel_id=1, source_target_pairs={{2,0},{4,2},{6,4},{0,6},{3,1},{5,3},{7,5},{1,7},{10,8},{12,10},{14... | collective-permute-start | bytes 491528 | tf_op jit(solution)/shard_map/ppermute | solution.py:715
  27.1 10.9 %collective-permute-start.5 = (bf16[1,4,4,8,1280]{4,3,2,1,0:T(8,128)(2,1)S(1)}, bf16[1,4,4,8,1280]{4,3,2,1,0:T(8,128)(2,1)S(1)}, u32[]{:S(2)}, u32[]{:S(2)}) collective-permute-start(bf16[1,4,4,8,1280]{4,3,2,1,0:T(8,128)(2,1)S(1)} %get-tuple-element.100), channel_id=1, source_target_pairs={{8,0},{16,8},{24,16},{0,24},{9,1},{17,9},{25,17},{1,25},{10,2},{18... | collective-permute-start | bytes 983048 | tf_op jit(solution)/shard_map/ppermute | solution.py:715
  27.6 10.5 %collective-permute-start.4 = (bf16[1,4,4,8,1280]{4,3,2,1,0:T(8,128)(2,1)S(1)}, bf16[1,4,4,8,1280]{4,3,2,1,0:T(8,128)(2,1)S(1)}, u32[]{:S(2)}, u32[]{:S(2)}) collective-permute-start(bf16[1,4,4,8,1280]{4,3,2,1,0:T(8,128)(2,1)S(1)} %get-tuple-element.101), channel_id=1, source_target_pairs={{0,8},{8,16},{16,24},{24,0},{1,9},{9,17},{17,25},{25,1},{2,10},{10... | collective-permute-start | bytes 983048 | tf_op jit(solution)/shard_map/ppermute | solution.py:714
  27.7 9.0 %collective-permute-start.6 = (bf16[2,1,4,8,1024]{4,3,2,1,0:T(8,128)(2,1)S(1)}, bf16[2,1,4,8,1024]{4,3,2,1,0:T(8,128)(2,1)S(1)}, u32[]{:S(2)}, u32[]{:S(2)}) collective-permute-start(bf16[2,1,4,8,1024]{4,3,2,1,0:T(8,128)(2,1)S(1)} %get-tuple-element.110), channel_id=1, source_target_pairs={{0,2},{2,4},{4,6},{6,0},{1,3},{3,5},{5,7},{7,1},{8,10},{10,12},{12... | collective-permute-start | bytes 393224 | tf_op jit(solution)/shard_map/ppermute | solution.py:714
  29.0 9.0 %collective-permute-start.7 = (bf16[2,1,4,8,1024]{4,3,2,1,0:T(8,128)(2,1)S(1)}, bf16[2,1,4,8,1024]{4,3,2,1,0:T(8,128)(2,1)S(1)}, u32[]{:S(2)}, u32[]{:S(2)}) collective-permute-start(bf16[2,1,4,8,1024]{4,3,2,1,0:T(8,128)(2,1)S(1)} %get-tuple-element.111), channel_id=1, source_target_pairs={{2,0},{4,2},{6,4},{0,6},{3,1},{5,3},{7,5},{1,7},{10,8},{12,10},{14... | collective-permute-start | bytes 393224 | tf_op jit(solution)/shard_map/ppermute | solution.py:715
  38.1 19.3 %copy-start.1 = (bf16[2,4,4,8,1024]{4,3,2,1,0:T(8,128)(2,1)}, bf16[2,4,4,8,1024]{4,3,2,1,0:T(8,128)(2,1)S(1)}, u32[]{:S(2)}) copy-start(bf16[2,4,4,8,1024]{4,3,2,1,0:T(8,128)(2,1)S(1)} %pad_maximum_fusion.1) | copy-start | bytes 1572868
  38.1 19.2 %collective-permute-start.10 = (bf16[2,1,4,8,1024]{4,3,2,1,0:T(8,128)(2,1)S(1)}, bf16[2,1,4,8,1024]{4,3,2,1,0:T(8,128)(2,1)S(1)}, u32[]{:S(2)}, u32[]{:S(2)}) collective-permute-start(bf16[2,1,4,8,1024]{4,3,2,1,0:T(8,128)(2,1)S(1)} %get-tuple-element.109), channel_id=1, source_target_pairs={{2,0},{4,2},{6,4},{0,6},{3,1},{5,3},{7,5},{1,7},{10,8},{12,10},{14... | collective-permute-start | bytes 393224 | tf_op jit(solution)/shard_map/ppermute | solution.py:715
  40.1 17.3 %collective-permute-start.9 = (bf16[2,1,4,8,1024]{4,3,2,1,0:T(8,128)(2,1)S(1)}, bf16[2,1,4,8,1024]{4,3,2,1,0:T(8,128)(2,1)S(1)}, u32[]{:S(2)}, u32[]{:S(2)}) collective-permute-start(bf16[2,1,4,8,1024]{4,3,2,1,0:T(8,128)(2,1)S(1)} %get-tuple-element.108), channel_id=1, source_target_pairs={{0,2},{2,4},{4,6},{6,0},{1,3},{3,5},{5,7},{7,1},{8,10},{10,12},{12... | collective-permute-start | bytes 393224 | tf_op jit(solution)/shard_map/ppermute | solution.py:714
  40.3 19.1 %collective-permute-start.13 = (bf16[1,4,4,8,1024]{4,3,2,1,0:T(8,128)(2,1)S(1)}, bf16[1,4,4,8,1024]{4,3,2,1,0:T(8,128)(2,1)S(1)}, u32[]{:S(2)}, u32[]{:S(2)}) collective-permute-start(bf16[1,4,4,8,1024]{4,3,2,1,0:T(8,128)(2,1)S(1)} %get-tuple-element.103), channel_id=1, source_target_pairs={{0,8},{8,16},{16,24},{24,0},{1,9},{9,17},{17,25},{25,1},{2,10},{10... | collective-permute-start | bytes 786440 | tf_op jit(solution)/shard_map/ppermute | solution.py:714
  40.3 19.0 %collective-permute-start.14 = (bf16[1,4,4,8,1024]{4,3,2,1,0:T(8,128)(2,1)S(1)}, bf16[1,4,4,8,1024]{4,3,2,1,0:T(8,128)(2,1)S(1)}, u32[]{:S(2)}, u32[]{:S(2)}) collective-permute-start(bf16[1,4,4,8,1024]{4,3,2,1,0:T(8,128)(2,1)S(1)} %get-tuple-element.102), channel_id=1, source_target_pairs={{8,0},{16,8},{24,16},{0,24},{9,1},{17,9},{25,17},{1,25},{10,2},{18... | collective-permute-start | bytes 786440 | tf_op jit(solution)/shard_map/ppermute | solution.py:715
  57.5 13.2 %copy-start.2 = (bf16[2,4,4,8,1024]{4,3,2,1,0:T(8,128)(2,1)}, bf16[2,4,4,8,1024]{4,3,2,1,0:T(8,128)(2,1)S(1)}, u32[]{:S(2)}) copy-start(bf16[2,4,4,8,1024]{4,3,2,1,0:T(8,128)(2,1)S(1)} %pad_maximum_fusion.2) | copy-start | bytes 1572868
  57.5 13.1 %collective-permute-start.11 = (bf16[1,4,4,8,1024]{4,3,2,1,0:T(8,128)(2,1)S(1)}, bf16[1,4,4,8,1024]{4,3,2,1,0:T(8,128)(2,1)S(1)}, u32[]{:S(2)}, u32[]{:S(2)}) collective-permute-start(bf16[1,4,4,8,1024]{4,3,2,1,0:T(8,128)(2,1)S(1)} %get-tuple-element.105), channel_id=1, source_target_pairs={{0,8},{8,16},{16,24},{24,0},{1,9},{9,17},{17,25},{25,1},{2,10},{10... | collective-permute-start | bytes 786440 | tf_op jit(solution)/shard_map/ppermute | solution.py:714
  57.6 13.1 %collective-permute-start.12 = (bf16[1,4,4,8,1024]{4,3,2,1,0:T(8,128)(2,1)S(1)}, bf16[1,4,4,8,1024]{4,3,2,1,0:T(8,128)(2,1)S(1)}, u32[]{:S(2)}, u32[]{:S(2)}) collective-permute-start(bf16[1,4,4,8,1024]{4,3,2,1,0:T(8,128)(2,1)S(1)} %get-tuple-element.104), channel_id=1, source_target_pairs={{8,0},{16,8},{24,16},{0,24},{9,1},{17,9},{25,17},{1,25},{10,2},{18... | collective-permute-start | bytes 786440 | tf_op jit(solution)/shard_map/ppermute | solution.py:715
  88.2 3.3 %collective-permute-start.15 = (f32[8,128]{1,0:T(8,128)}, f32[8,128]{1,0:T(8,128)S(1)}, u32[]{:S(2)}, u32[]{:S(2)}) collective-permute-start(f32[8,128]{1,0:T(8,128)} %get-tuple-element.94), channel_id=1, source_target_pairs={{0,8},{8,16},{16,24},{24,0},{1,9},{9,17},{17,25},{25,1},{2,10},{10... | collective-permute-start | bytes 12296 | tf_op jit(solution)/shard_map/ppermute | solution.py:758
  88.2 3.3 %collective-permute-start.16 = (f32[8,128]{1,0:T(8,128)}, f32[8,128]{1,0:T(8,128)S(1)}, u32[]{:S(2)}, u32[]{:S(2)}) collective-permute-start(f32[8,128]{1,0:T(8,128)} %get-tuple-element.95), channel_id=1, source_target_pairs={{8,0},{16,8},{24,16},{0,24},{9,1},{17,9},{25,17},{1,25},{10,2},{18... | collective-permute-start | bytes 12296 | tf_op jit(solution)/shard_map/ppermute | solution.py:759
  92.2 5.4 %collective-permute-start.17 = (f32[8,256]{1,0:T(8,128)S(1)}, f32[8,256]{1,0:T(8,128)S(1)}, u32[]{:S(2)}, u32[]{:S(2)}) collective-permute-start(f32[8,256]{1,0:T(8,128)S(1)} %maximum_add_fusion), channel_id=1, source_target_pairs={{0,2},{2,4},{4,6},{6,0},{1,3},{3,5},{5,7},{7,1},{8,10},{10,12},{12... | collective-permute-start | bytes 24584 | tf_op jit(solution)/shard_map/ppermute | solution.py:762
  92.9 4.8 %collective-permute-start.18 = (f32[8,256]{1,0:T(8,128)S(1)}, f32[8,256]{1,0:T(8,128)S(1)}, u32[]{:S(2)}, u32[]{:S(2)}) collective-permute-start(f32[8,256]{1,0:T(8,128)S(1)} %maximum_add_fusion), channel_id=1, source_target_pairs={{2,0},{4,2},{6,4},{0,6},{3,1},{5,3},{7,5},{1,7},{10,8},{12,10},{14... | collective-permute-start | bytes 24584 | tf_op jit(solution)/shard_map/ppermute | solution.py:763
  97.9 3.7 %collective-permute-start.19 = (f32[8,256]{1,0:T(8,128)S(1)}, f32[8,256]{1,0:T(8,128)S(1)}, u32[]{:S(2)}, u32[]{:S(2)}) collective-permute-start(f32[8,256]{1,0:T(8,128)S(1)} %fusion.1.mid_ref), channel_id=1, source_target_pairs={{0,1},{1,0},{2,3},{3,2},{4,5},{5,4},{6,7},{7,6},{8,9},{9,8},{10,11... | collective-permute-start | bytes 24584 | tf_op jit(solution)/shard_map/ppermute | solution.py:771
  (9 other events, 24.9 us)

commit v4 on v3

--- a/solution.py
+++ b/solution.py
@@ -1,4 +1,3 @@
-import functools
 import math
 
 import jax
@@ -16,7 +15,7 @@
 STEP = 256
 OWN_STEPS = 4
 GH_STEPS = 2
-VMEM = 56 * 1024 * 1024
+MIB = 1024 * 1024
 SPACE = pltpu.VMEM
 PAIR_DEGREES = (
     (1, 1), (1, 2), (2, 2), (2, 2),
@@ -50,7 +49,7 @@
     return jax.ShapeDtypeStruct(shape, dtype)
 
 
-def call(kernel, name, out_shape, scratch, flops, args, specs=None):
+def call(kernel, name, out_shape, scratch, flops, args, specs=None, limit=16):
     size = sum(a.size * a.dtype.itemsize for a in list(args) + list(out_shape))
     return pl.pallas_call(
         kernel,
@@ -58,7 +57,7 @@
         in_specs=specs or [pl.BlockSpec(memory_space=SPACE)] * len(args),
         out_specs=tuple(pl.BlockSpec(memory_space=SPACE) for _ in out_shape),
         scratch_shapes=scratch,
-        compiler_params=pltpu.CompilerParams(vmem_limit_bytes=VMEM),
+        compiler_params=pltpu.CompilerParams(vmem_limit_bytes=limit * MIB),
         cost_estimate=pl.CostEstimate(flops=flops, bytes_accessed=size, transcendentals=0),
         name=name,
     )(*args)
@@ -177,6 +176,28 @@
     return pl.ds(base, size), pl.ds(pl.multiple_of(first + base, size), size)
 
 
+class Halves:
+    def __init__(self, own, ghost):
+        self.own, self.ghost = own, ghost
+        self.dtype = own.dtype
+
+    def place(self, rows):
+        first = OWN_STEPS * STEP
+        if not isinstance(rows.start, int):
+            return self.ghost, pl.ds(pl.multiple_of(rows.start - first, rows.size), rows.size)
+        if rows.start < first:
+            return self.own, rows
+        return self.ghost, pl.ds(rows.start - first, rows.size)
+
+    def __getitem__(self, at):
+        ref, rows = self.place(at[0])
+        return ref[rows, at[1]]
+
+    def __setitem__(self, at, value):
+        ref, rows = self.place(at[0])
+        ref[rows, at[1]] = value
+
+
 def over_ghost_steps(steps, body, size=STEP):
     static = GH_STEPS * STEP // size
     for step in range(static):
@@ -268,9 +289,9 @@
                 part = weighted[:, side * CH : (side + 1) * CH]
                 degree = degrees[side]
                 parts[degree] = parts[degree] + part if degree in parts else part
-        dot_ref[rows, :] = dots
+        dot_ref[rows, :] = dots.astype(dot_ref.dtype)
         for degree, part in parts.items():
-            grad_refs[degree][rows, :] = part
+            grad_refs[degree][rows, :] = part.astype(grad_refs[degree].dtype)
 
     own = own_ref[:, own_cols]
     summed = None
@@ -321,9 +342,13 @@
     ]
 
 
-def own_kernel(meta_ref, own_pos_ref, rbf_ref, rad_ref, oh_own, radial_ref, pre_ref, unit_ref):
+def own_kernel(
+    meta_ref, own_pos_ref, rbf_ref, rad_ref, mix_ref,
+    oh_own, pre_ref, unit_ref, radt_ref, rbft_ref, mixt_ref, home_ref, *radial_refs
+):
     atoms = meta_ref.shape[0]
-    spacing = spacing_of(atoms, rbf_ref.shape[0])
+    nbasis = rbf_ref.shape[0]
+    spacing = spacing_of(atoms, nbasis)
     own_onehots(meta_ref, oh_own)
     here = tiled(own_pos_ref[...].astype(F32))
     for step in range(OWN_STEPS):
@@ -331,30 +356,60 @@
         unit, dist = geometry(mm(oh_own[rows, :], own_pos_ref[...]), here)
         unit_ref[rows, :] = unit
         pre, radial = radial_net(dist, spacing, rbf_ref, rad_ref)
-        pre_ref[rows, :] = pre
-        for degree in range(5):
-            radial_ref[degree, rows, :] = radial[:, degree * CH : (degree + 1) * CH]
-
-
-def own_stage(meta, own_pos, rbf, rad):
+        pre_ref[rows, :] = pre.astype(BF16)
+        for degree, ref in enumerate(radial_refs):
+            ref[rows, :] = radial[:, degree * CH : (degree + 1) * CH]
+    for degree in range(5):
+        part = slice(degree * CH, (degree + 1) * CH)
+        radt_ref[part, :] = flip(rad_ref[:, part])
+    for index in range(nbasis // CH):
+        part = slice(index * CH, (index + 1) * CH)
+        rbft_ref[:, part] = flip(rbf_ref[part, :])
+    mixt_ref[...] = flip(mix_ref[0])
+    lanes = home_ref.shape[1]
+    lane = iota((atoms, lanes), 1)
+    ext_x, ext_y, ext_z = lane // 128, lane // 32 % 4, lane // 8 % 4
+    slot = ((2 * ext_x + ext_y - 1) * 2 + ext_z - 1) * 8 + lane % 8
+    inside = jnp.logical_and(
+        jnp.logical_or(ext_y == 1, ext_y == 2), jnp.logical_or(ext_z == 1, ext_z == 2)
+    )
+    to_slot = jnp.logical_and(iota((atoms, lanes), 0) == slot, inside)
+    to_slot = to_slot.astype(F32).astype(BF16)
+    order = meta_ref[:, SLOTS + 1 : SLOTS + 2]
+    to_atom = (order == iota((atoms, atoms), 1).astype(F32)).astype(F32)
+    home_ref[...] = mm(to_atom.T.astype(BF16), to_slot).astype(BF16)
+
+
+def own_stage(meta, own_pos, rbf, rad, mix):
     atoms = meta.shape[0]
     edges = atoms * HALF
     out_shape = (
         struct(edges, atoms, dtype=BF16),
-        struct(5, edges, CH, dtype=BF16),
+        struct(edges, CH, dtype=BF16),
         struct(edges, CH),
-        struct(edges, CH),
-    )
-    return call(own_kernel, "own_edges", out_shape, [], 1 << 31, (meta, own_pos, rbf, rad))
+        struct(*rad.shape[::-1], dtype=BF16),
+        struct(*rbf.shape[::-1], dtype=BF16),
+        struct(CH, CH, dtype=BF16),
+        struct(atoms, 256, dtype=BF16),
+    ) + (struct(edges, CH, dtype=BF16),) * 5
+    args = (meta, own_pos, rbf, rad, mix)
+    return call(own_kernel, "own_edges", out_shape, [], 1 << 31, args)
 
 
 def first_kernel(
     low_ref, mid_ref, high_ref, own_ref, own_pos_ref, meta_ref, rbf_ref, rad_ref, mix_ref,
-    out_ref, ew_ref, nw_ref, oh_own, radial_own,
-    new_ref, oh_gh, d_gh, dt_gh, radial_gh, pre_ref, unit_ref, m0_ref, gate_ref, nf0_ref,
-    gs0_ref, dot_ref, gr1_ref, gr2_ref, en_ref,
-    table, sems, ghpos, wm, wmt, wo, wot, nf_s, mx_s, acc_s, gs_s,
+    out_ref, ew_ref, nw_ref, oh_own, radial_own0, radial_own1, radial_own2,
+    new_ref, oh_gh, d_gh, dt_gh, radial_gh3, radial_gh4, pre_ref, unit_ref, gs0_ref, en_ref,
+    m0_own, m0_gh, gate_own, gate_gh, nf0_own, nf0_gh, dot_own, dot_gh, gr1_own, gr1_gh, gr2_own,
+    gr2_gh,
+    table, sems, ghpos, radial_gh0, radial_gh1, radial_gh2, wm, wmt, wo, wot, nf_s, mx_s, acc_s,
+    gs_s,
 ):
+    m0_ref, gate_ref, nf0_ref = Halves(m0_own, m0_gh), Halves(gate_own, gate_gh), Halves(nf0_own, nf0_gh)
+    dot_ref, gr1_ref, gr2_ref = Halves(dot_own, dot_gh), Halves(gr1_own, gr1_gh), Halves(gr2_own, gr2_gh)
+    radial_gh = (radial_gh0, radial_gh1, radial_gh2, radial_gh3, radial_gh4)
+    radials = [Halves(radial_own0, radial_gh0), Halves(radial_own1, radial_gh1)]
+    radials.append(Halves(radial_own2, radial_gh2))
     pairs = tuple(range(*GROUPS[0]))
     kinds = sorted({PAIR_DEGREES[pair] for pair in pairs})
     copies = fetch((low_ref, mid_ref, high_ref), table, sems)
@@ -403,7 +458,7 @@
         near = mm(onehot, feats).astype(BF16)
         nf0_ref[rows, :] = near
         mixed = mm(near * radial, mix_ref[0])
-        m0_ref[rows, :] = mixed
+        m0_ref[rows, :] = mixed.astype(BF16)
         gate = jax.nn.sigmoid(mixed)
         gate_ref[rows, :] = gate.astype(BF16)
         return (mixed * gate).astype(BF16)
@@ -413,7 +468,7 @@
     summed = None
     for step in range(OWN_STEPS):
         rows = own_rows(step)
-        message = forward0(rows, oh_own[rows, :], own0, radial_own[0, rows, :])
+        message = forward0(rows, oh_own[rows, :], own0, radial_own0[rows, :])
         part = mm(spread_own, message)
         summed = part if summed is None else summed + part
     acc_s[:, 0:CH] = summed
@@ -440,9 +495,9 @@
         unit, dist = geometry(mm(onehot, ghpos[...]), mm(source, own_pos_ref[...]))
         unit_ref[here, :] = unit
         pre, radial = radial_net(dist, spacing, rbf_ref, rad_ref)
-        pre_ref[here, :] = pre
+        pre_ref[here, :] = pre.astype(BF16)
         for degree in range(5):
-            radial_gh[degree, here, :] = radial[:, degree * CH : (degree + 1) * CH]
+            radial_gh[degree][here, :] = radial[:, degree * CH : (degree + 1) * CH]
         message = forward0(rows, onehot, table[:, 0:CH], radial[:, 0:CH])
         acc_s[:, 0:CH] += mm(spread, message)
 
@@ -458,9 +513,7 @@
     gs0_ref[...] = mm_nt(grad0, out_ref[0]) * norm
 
     def radial_any(degree, rows):
-        if isinstance(rows.start, int) and rows.start < OWN_STEPS * STEP:
-            return radial_own[degree, rows, :]
-        return radial_gh[degree, pl.ds(rows.start - OWN_STEPS * STEP, rows.size), :]
+        return radials[degree][rows, :]
 
     run_pairs(
         pairs, kinds, 0, own_ref, table, new_ref, 0, oh_own, oh_gh, d_gh, dt_gh, gate_ref,
@@ -475,7 +528,7 @@
     ] * (total - count)
 
 
-def first_stage(pieces, feats, own_pos, meta, rbf, rad, mix, out, ew, nw, oh_own, radial_own):
+def first_stage(pieces, feats, own_pos, meta, rbf, rad, mix, out, ew, nw, oh_own, *radial_own):
     atoms = feats.shape[0]
     half = atoms * HALF
     edges = 2 * half
@@ -487,37 +540,36 @@
         struct(half, ghosts, dtype=BF16),
         struct(half, atoms, dtype=BF16),
         struct(atoms, half, dtype=BF16),
-        struct(5, half, CH, dtype=BF16),
+        struct(half, CH, dtype=BF16),
+        struct(half, CH, dtype=BF16),
+        struct(half, CH, dtype=BF16),
         struct(half, CH),
-        struct(half, CH),
-        struct(edges, CH),
-        struct(edges, CH, dtype=BF16),
-        struct(edges, CH, dtype=BF16),
         struct(atoms, CH),
-        struct(edges, CH),
-        struct(edges, CH),
-        struct(edges, CH),
         struct(atoms, CH),
-    )
+    ) + (struct(half, CH, dtype=BF16),) * 12
     scratch = [
         pltpu.VMEM((ghosts, width), BF16),
         pltpu.SemaphoreType.DMA((3,)),
         pltpu.VMEM((ghosts, CH), BF16),
-    ] + pair_scratch(atoms, edges, kinds)
+    ] + [pltpu.VMEM((half, CH), BF16)] * 3 + pair_scratch(atoms, edges, kinds)
     args = tuple(pieces) + (
-        feats, own_pos, meta, rbf, rad, mix, out, ew, nw, oh_own, radial_own
-    )
+        feats, own_pos, meta, rbf, rad, mix, out, ew, nw, oh_own
+    ) + radial_own
     return call(
-        first_kernel, "first_group", out_shape, scratch, 1 << 33, args, any_specs(3, len(args))
+        first_kernel, "first_group", out_shape, scratch, 1 << 33, args, any_specs(3, len(args)),
+        32,
     )
 
 
 def second_kernel(
-    low_ref, mid_ref, high_ref, own_ref, meta_ref, mix_ref, out_ref, nw_ref, oh_own, radial_own,
-    oh_gh, d_gh, dt_gh, radial_gh, gate_ref,
-    new_ref, dot_ref, gr3_ref, gr4_ref, en_ref,
+    low_ref, mid_ref, high_ref, own_ref, meta_ref, mix_ref, out_ref, nw_ref, oh_own, oh_gh, d_gh,
+    dt_gh, gate_own, gate_gh, radial_own4, radial_gh4, radial_own3, radial_gh3,
+    new_ref, en_ref, dot_own, dot_gh, gr3_own, gr3_gh, gr4_own, gr4_gh,
     table, sems, wm, wmt, wo, wot, nf_s, mx_s, acc_s, gs_s,
 ):
+    radials = {3: Halves(radial_own3, radial_gh3), 4: Halves(radial_own4, radial_gh4)}
+    gate_ref = Halves(gate_own, gate_gh)
+    dot_ref, gr3_ref, gr4_ref = Halves(dot_own, dot_gh), Halves(gr3_own, gr3_gh), Halves(gr4_own, gr4_gh)
     pairs = tuple(range(*GROUPS[1]))
     kinds = sorted({PAIR_DEGREES[pair] for pair in pairs})
     copies = fetch((low_ref, mid_ref, high_ref), table, sems)
@@ -526,9 +578,7 @@
     base = pair_cols(pairs[0]).start
 
     def radial_any(degree, rows):
-        if isinstance(rows.start, int) and rows.start < OWN_STEPS * STEP:
-            return radial_own[degree, rows, :]
-        return radial_gh[degree, pl.ds(rows.start - OWN_STEPS * STEP, rows.size), :]
+        return radials[degree][rows, :]
 
     for copy in copies:
         copy.wait()
@@ -539,8 +589,7 @@
     )
 
 
-def second_stage(pieces, feats, meta, mix, out, nw, oh_own, radial_own, oh_gh, d_gh, dt_gh,
-                 radial_gh, gate):
+def second_stage(pieces, feats, *rest):
     atoms = feats.shape[0]
     edges = atoms * SLOTS
     width = pieces[0].shape[1]
@@ -548,47 +597,65 @@
     kinds = sorted({PAIR_DEGREES[pair] for pair in range(*GROUPS[1])})
     out_shape = (
         struct(atoms, width, dtype=BF16),
-        struct(edges, CH),
-        struct(edges, CH),
-        struct(edges, CH),
         struct(atoms, CH),
-    )
+    ) + (struct(atoms * HALF, CH, dtype=BF16),) * 6
     scratch = [
         pltpu.VMEM((ghosts, width), BF16),
         pltpu.SemaphoreType.DMA((3,)),
     ] + pair_scratch(atoms, edges, kinds)
-    args = tuple(pieces) + (
-        feats, meta, mix, out, nw, oh_own, radial_own, oh_gh, d_gh, dt_gh, radial_gh, gate
-    )
+    args = tuple(pieces) + (feats,) + rest
     return call(
         second_kernel, "second_group", out_shape, scratch, 1 << 33, args,
-        any_specs(3, len(args)),
-    )
+        any_specs(3, len(args)), 28,
+    )
+
+
+def finish(
+    grad, mixed, near, dots, parts, pre, unit, spacing, radt_ref, rbft_ref, mixt_ref
+):
+    mixed = mixed.astype(F32)
+    gate = jax.nn.sigmoid(mixed)
+    first = grad * gate * (1.0 + mixed * (1.0 - gate)) + dots * gate * (1.0 - gate)
+    weighted = mm(first.astype(BF16), mixt_ref[...]) * near.astype(F32)
+    radial_grad = jnp.concatenate([weighted.astype(BF16)] + parts, axis=1)
+    hidden_grad = mm(radial_grad, radt_ref[...])
+    pre = pre.astype(F32)
+    logistic = jax.nn.sigmoid(pre)
+    pre_grad = (hidden_grad * logistic * (1.0 + pre * (1.0 - logistic))).astype(BF16)
+    centred = centred_of(unit[:, 3:4], spacing, rbft_ref.shape[1])
+    slope = jnp.exp(-0.5 * centred * centred) * centred
+    basis_grad = mm(pre_grad, rbft_ref[...])
+    dist_grad = jnp.sum(basis_grad * slope, axis=1, keepdims=True) * (-1.0 / spacing)
+    pull = unit * dist_grad
+    across = pull.T[0:8, :]
+    top = across.astype(BF16)
+    rest = (across - top.astype(F32)).astype(BF16)
+    return pull, top, rest
+
+
+def sum_of(refs, rows):
+    total = refs[0][rows, :].astype(F32)
+    for ref in refs[1:]:
+        total += ref[rows, :].astype(F32)
+    return total
 
 
 def third_kernel(
-    low_ref, mid_ref, high_ref, own_ref, meta_ref, mix_ref, out_ref, nw_ref, oh_own, radial_own,
-    oh_gh, d_gh, dt_gh, radial_gh, gate_ref,
-    rbf_ref, rad_ref, pre_own, pre_gh, unit_own, unit_gh, m0_ref, nf0_ref, gs0_ref,
-    dot_a, dot_b, gr1_ref, gr2_ref, gr3_ref, gr4_a, en_a, en_b, new_a, new_b,
-    new_ref, energy_ref, fown_ref, flow_ref, fmid_ref, fhigh_ref,
-    table, sems, wm, wmt, wo, wot, nf_s, mx_s, acc_s, gs_s,
-    dot_c, gr4_b, en_s, radt, rbft, src_s, fgh_s,
+    low_ref, mid_ref, high_ref, own_ref, meta_ref, mix_ref, out_ref, nw_ref, oh_own, oh_gh, d_gh,
+    dt_gh, gate_own, gate_gh, radial_own4, radial_gh4,
+    radt_ref, rbft_ref, mixt_ref, gs0_ref, en_a, en_b, new_a, new_b, pre_gh, unit_gh,
+    m0_ref, nf0_ref, dot_a, dot_b, gr1_ref, gr2_ref, gr3_ref, gr4_a,
+    new_ref, energy_ref, src_ref, flow_ref, fmid_ref, fhigh_ref, dot_own, gr4_own,
+    table, sems, wm, wmt, wo, wot, nf_s, mx_s, acc_s, gs_s, dot_c, gr4_b, en_s, fgh_s,
 ):
+    gate_ref = Halves(gate_own, gate_gh)
+    radials = {4: Halves(radial_own4, radial_gh4)}
     pairs = tuple(range(*GROUPS[2]))
     kinds = sorted({PAIR_DEGREES[pair] for pair in pairs})
     copies = fetch((low_ref, mid_ref, high_ref), table, sems)
     atoms = own_ref.shape[0]
-    nbasis = rbf_ref.shape[0]
-    spacing = spacing_of(atoms, nbasis)
+    spacing = spacing_of(atoms, rbft_ref.shape[1])
     block_diagonal(kinds, mix_ref, out_ref, wm, wmt, wo, wot)
-    for degree in range(5):
-        part = slice(degree * CH, (degree + 1) * CH)
-        radt[part, :] = flip(rad_ref[:, part])
-    for index in range(nbasis // CH):
-        part = slice(index * CH, (index + 1) * CH)
-        rbft[:, part] = flip(rbf_ref[part, :])
-    mix0_t = flip(mix_ref[0])
     en_s[...] = en_a[...] + en_b[...]
     new_ref[:, 0 : new_a.shape[1]] = new_a[...]
     new_ref[:, new_a.shape[1] : new_a.shape[1] + new_b.shape[1]] = new_b[...]
@@ -596,53 +663,35 @@
     steps = step_count(meta_ref)
 
     def radial_any(degree, rows):
-        if isinstance(rows.start, int) and rows.start < OWN_STEPS * STEP:
-            return radial_own[degree, rows, :]
-        return radial_gh[degree, pl.ds(rows.start - OWN_STEPS * STEP, rows.size), :]
+        return radials[degree][rows, :]
 
     for copy in copies:
         copy.wait()
     run_pairs(
         pairs, kinds, base, own_ref, table, new_ref, 0, oh_own, oh_gh, d_gh, dt_gh, gate_ref,
-        radial_any, nw_ref, steps, wm, wmt, wo, wot, nf_s, mx_s, acc_s, gs_s, dot_c,
-        {4: gr4_b}, en_s, 2 * STEP,
-    )
-
-    def finish(rows, grad, pre, unit):
-        mixed = m0_ref[rows, :]
-        gate = jax.nn.sigmoid(mixed)
-        dot = dot_a[rows, :] + dot_b[rows, :] + dot_c[rows, :]
-        first = grad * gate * (1.0 + mixed * (1.0 - gate)) + dot * gate * (1.0 - gate)
-        weighted = mm(first.astype(BF16), mix0_t) * nf0_ref[rows, :].astype(F32)
-        parts = [weighted, gr1_ref[rows, :], gr2_ref[rows, :], gr3_ref[rows, :]]
-        parts.append(gr4_a[rows, :] + gr4_b[rows, :])
-        radial_grad = jnp.concatenate([part.astype(BF16) for part in parts], axis=1)
-        hidden_grad = mm(radial_grad, radt[...])
-        logistic = jax.nn.sigmoid(pre)
-        pre_grad = (hidden_grad * logistic * (1.0 + pre * (1.0 - logistic))).astype(BF16)
-        centred = centred_of(unit[:, 3:4], spacing, nbasis)
-        slope = jnp.exp(-0.5 * centred * centred) * centred
-        basis_grad = mm(pre_grad, rbft[...])
-        dist_grad = jnp.sum(basis_grad * slope, axis=1, keepdims=True) * (-1.0 / spacing)
-        pull = unit * dist_grad
-        across = pull.T[0:8, :]
-        top = across.astype(BF16)
-        rest = (across - top.astype(F32)).astype(BF16)
-        return pull, top, rest
+        radial_any, nw_ref, steps, wm, wmt, wo, wot, nf_s, mx_s, acc_s, gs_s,
+        Halves(dot_own, dot_c), {4: Halves(gr4_own, gr4_b)}, en_s,
+    )
+    energy_ref[...] = jnp.sum(en_s[...].T, axis=0, keepdims=True)
 
     fgh_s[...] = jnp.zeros_like(fgh_s)
-    src_s[...] = jnp.zeros_like(src_s)
-    gs0 = gs0_ref[...]
-    gs0_low = gs0.astype(BF16)
+    src_ref[...] = jnp.zeros_like(src_ref)
+    gs0_low = gs0_ref[...].astype(BF16)
 
     def ghost_finish(step):
         here, rows = ghost_rows(step)
         grad = mm(d_gh[here, :], gs0_low)
-        pull, top, rest = finish(rows, grad, pre_gh[here, :], unit_gh[here, :])
+        dots = sum_of((dot_a, dot_b, dot_c), here)
+        parts = [gr1_ref[here, :], gr2_ref[here, :], gr3_ref[here, :]]
+        parts.append(sum_of((gr4_a, gr4_b), here).astype(BF16))
+        pull, top, rest = finish(
+            grad, m0_ref[here, :], nf0_ref[here, :], dots, parts, pre_gh[here, :],
+            unit_gh[here, :], spacing, radt_ref, rbft_ref, mixt_ref,
+        )
         pull_top = pull.astype(BF16)
         pull_rest = (pull - pull_top.astype(F32)).astype(BF16)
         spread = dt_gh[:, here]
-        src_s[...] += mm(spread, pull_top) + mm(spread, pull_rest)
+        src_ref[...] += mm(spread, pull_top) + mm(spread, pull_rest)
         onehot = oh_gh[here, :]
         fgh_s[...] += mm(top, onehot) + mm(rest, onehot)
 
@@ -652,48 +701,64 @@
     fmid_ref[...] = fgh_s[:, low : low + mid]
     fhigh_ref[...] = fgh_s[:, low + mid :]
 
-    grad_own = tiled(gs0)
-    src = src_s[...]
-    onto = jnp.zeros((8, atoms), F32)
-    for step in range(OWN_STEPS):
-        rows = own_rows(step)
-        pull, top, rest = finish(rows, grad_own, pre_own[rows, :], unit_own[rows, :])
-        src += jnp.sum(pull.reshape(STEP // atoms, atoms, CH), axis=0)
-        onehot = oh_own[rows, :]
-        onto += mm(top, onehot) + mm(rest, onehot)
-    fown_ref[...] = onto - src.T[0:8, :]
-    energy_ref[...] = jnp.sum(en_s[...].T, axis=0, keepdims=True)
-
 
 def third_stage(pieces, feats, *rest):
     atoms, feat = feats.shape
-    edges = atoms * SLOTS
+    half = atoms * HALF
+    edges = 2 * half
     width = pieces[0].shape[1]
     sizes = [piece.shape[0] for piece in pieces]
     ghosts = sum(sizes)
-    nbasis = rest[11].shape[0]
     kinds = sorted({PAIR_DEGREES[pair] for pair in range(*GROUPS[2])})
     out_shape = (
         struct(atoms, feat, dtype=BF16),
         struct(1, atoms),
-        struct(8, atoms),
-    ) + tuple(struct(8, size) for size in sizes)
+        struct(atoms, CH),
+    ) + tuple(struct(8, size) for size in sizes) + (struct(half, CH, dtype=BF16),) * 2
     scratch = [
         pltpu.VMEM((ghosts, width), BF16),
         pltpu.SemaphoreType.DMA((3,)),
     ] + pair_scratch(atoms, edges, kinds) + [
-        pltpu.VMEM((edges, CH), F32),
-        pltpu.VMEM((edges, CH), F32),
-        pltpu.VMEM((atoms, CH), F32),
-        pltpu.VMEM((5 * CH, CH), BF16),
-        pltpu.VMEM((CH, nbasis), BF16),
+        pltpu.VMEM((half, CH), BF16),
+        pltpu.VMEM((half, CH), BF16),
         pltpu.VMEM((atoms, CH), F32),
         pltpu.VMEM((8, ghosts), F32),
     ]
     args = tuple(pieces) + (feats,) + rest
     return call(
-        third_kernel, "third_group", out_shape, scratch, 1 << 33, args, any_specs(3, len(args))
-    )
+        third_kernel, "third_group", out_shape, scratch, 1 << 33, args, any_specs(3, len(args)),
+        30,
+    )
+
+
+def own_back_kernel(
+    oh_own, pre_own, unit_own, radt_ref, rbft_ref, mixt_ref, gs0_ref, src_ref,
+    m0_ref, nf0_ref, dot_a, dot_b, dot_c, gr1_ref, gr2_ref, gr3_ref, gr4_a, gr4_b,
+    force_ref,
+):
+    atoms = oh_own.shape[1]
+    spacing = spacing_of(atoms, rbft_ref.shape[1])
+    grad = tiled(gs0_ref[...])
+    src = src_ref[...]
+    onto = jnp.zeros((8, atoms), F32)
+    for step in range(OWN_STEPS):
+        rows = own_rows(step)
+        parts = [gr1_ref[rows, :], gr2_ref[rows, :], gr3_ref[rows, :]]
+        parts.append(sum_of((gr4_a, gr4_b), rows).astype(BF16))
+        pull, top, rest = finish(
+            grad, m0_ref[rows, :], nf0_ref[rows, :], sum_of((dot_a, dot_b, dot_c), rows), parts,
+            pre_own[rows, :], unit_own[rows, :], spacing, radt_ref, rbft_ref, mixt_ref,
+        )
+        src += jnp.sum(pull.reshape(STEP // atoms, atoms, CH), axis=0)
+        onehot = oh_own[rows, :]
+        onto += mm(top, onehot) + mm(rest, onehot)
+    force_ref[...] = onto - src.T[0:8, :]
+
+
+def own_back_stage(*args):
+    oh_own = args[0]
+    out_shape = (struct(8, oh_own.shape[1]),)
+    return call(own_back_kernel, "own_back", out_shape, [], 1 << 31, args)[0]
 
 
 def ring(axis):
@@ -726,37 +791,27 @@
     return tuple(piece.reshape(-1, block.shape[-1]) for piece in (before, block, after))
 
 
-def forces_kernel(mid_ref, low_ref, high_ref, own_ref, meta_ref, out_ref):
-    atoms = own_ref.shape[1]
+def forces_kernel(mid_ref, low_ref, high_ref, own_ref, home_ref, out_ref):
     values = mid_ref[...]
     lanes = values.shape[1]
-    lane = iota(values.shape, 1)
-    ext_z = lane // 8 % 4
+    ext_z = iota(values.shape, 1) // 8 % 4
     values += jnp.where(ext_z == 1, pltpu.roll(low_ref[...], lanes - 16, 1), 0.0)
     values += jnp.where(ext_z == 2, pltpu.roll(high_ref[...], 16, 1), 0.0)
-    lane = iota((atoms, lanes), 1)
-    ext_x, ext_y, ext_z = lane // 128, lane // 32 % 4, lane // 8 % 4
-    slot = ((2 * ext_x + ext_y - 1) * 2 + ext_z - 1) * 8 + lane % 8
-    inside = jnp.logical_and(
-        jnp.logical_or(ext_y == 1, ext_y == 2), jnp.logical_or(ext_z == 1, ext_z == 2)
-    )
-    to_slot = jnp.logical_and(iota((atoms, lanes), 0) == slot, inside)
-    to_slot = to_slot.astype(F32).astype(BF16)
-    order = meta_ref[:, SLOTS + 1 : SLOTS + 2]
-    to_atom = (order == iota((atoms, atoms), 1).astype(F32)).astype(F32).astype(BF16)
-    total = own_ref[...]
-    for _ in range(3):
-        top = values.astype(BF16)
-        values = values - top.astype(F32)
-        total += mm(mm_nt(top, to_slot).astype(BF16), to_atom)
+    first = values.astype(BF16)
+    values -= first.astype(F32)
+    second = values.astype(BF16)
+    third = (values - second.astype(F32)).astype(BF16)
+    home = home_ref[...]
+    total = own_ref[...] + (mm_nt(first, home) + (mm_nt(second, home) + mm_nt(third, home)))
     for comp in range(3):
         out_ref[comp] = -total[comp : comp + 1, :]
 
 
-def give_back(low, mid, high, own, meta):
+def give_back(low, mid, high, own, home):
     up, down = ring("gx")
     from_low = lax.ppermute(high, "gx", up)
     from_high = lax.ppermute(low, "gx", down)
+    from_low, from_high, own = lax.optimization_barrier((from_low, from_high, own))
     mid = mid + jnp.concatenate([from_low, from_high], axis=1)
     up, down = ring("gy")
     from_low = lax.ppermute(mid, "gy", up)
@@ -770,7 +825,7 @@
     up, down = ring("gz")
     from_low = lax.ppermute(mid, "gz", up)
     from_high = from_low if len(up) == 2 else lax.ppermute(mid, "gz", down)
-    args = (mid, from_low, from_high, own, meta)
+    args = (mid, from_low, from_high, own, home)
     out_shape = (struct(3, 1, own.shape[1]),)
     return call(forces_kernel, "forces", out_shape, [], 1 << 20, args)[0]
 
@@ -794,36 +849,46 @@
         feats, places, neighbours[0, 0, 0].T, counts[0, 0], cell_atoms[0, 0]
     )
     hold = lax.optimization_barrier
-    blocks = [part.reshape(2, 2, 2, 8, part.shape[1]) for part in cells]
-    block0, block1, block2 = (grown(block, "gz", 2) for block in blocks)
-    block0, own_pos, meta = hold((block0, own_pos, meta))
+    block0, block1, block2 = (part.reshape(2, 2, 2, 8, part.shape[1]) for part in cells)
+    block0 = grown(block0, "gz", 2)
+    block0, block1, block2, own_pos, meta = hold((block0, block1, block2, own_pos, meta))
+    block1, block2 = (grown(block, "gz", 2) for block in (block1, block2))
     block0 = grown(block0, "gy", 1)
-    oh_own, radial_own, pre_own, unit_own = own_stage(meta, own_pos, rbf_weight, radial_weight)
-    block0, block1 = hold((block0, block1))
+    oh_own, pre_own, unit_own, radt, rbft, mixt, home, *radial_own = own_stage(
+        meta, own_pos, rbf_weight, radial_weight, mix_weight
+    )
+    block0, block1, oh_own = hold((block0, block1, oh_own))
     pieces0 = ghost_pieces(block0)
     block1 = grown(block1, "gy", 1)
     pieces0, block1, block2 = hold((pieces0, block1, block2))
     pieces1 = ghost_pieces(block1)
     block2 = grown(block2, "gy", 1)
     (
-        new_a, oh_gh, d_gh, dt_gh, radial_gh, pre_gh, unit_gh, m0, gate, nf0, gs0, dot_a, gr1,
-        gr2, en_a,
+        new_a, oh_gh, d_gh, dt_gh, radial_gh3, radial_gh4, pre_gh, unit_gh, gs0, en_a, m0_own,
+        m0_gh, gate_own, gate_gh, nf0_own, nf0_gh, dot_own_a, dot_gh_a, gr1_own, gr1_gh, gr2_own,
+        gr2_gh,
     ) = first_stage(
         pieces0, feats, own_pos, meta, rbf_weight, radial_weight, mix_weight, out_weight,
-        energy_weight[None], norm_weight, oh_own, radial_own,
-    )
-    gate, block2 = hold((gate, block2))
+        energy_weight[None], norm_weight, oh_own, *radial_own[:3],
+    )
+    gate_own, block2 = hold((gate_own, block2))
     pieces2 = ghost_pieces(block2)
     shared = (
-        feats, meta, mix_weight, out_weight, norm_weight, oh_own, radial_own, oh_gh, d_gh, dt_gh,
-        radial_gh, gate,
-    )
-    new_b, dot_b, gr3, gr4, en_b = second_stage(pieces1, *shared)
-    new, energy, own, low, mid, high = third_stage(
-        pieces2, *shared, rbf_weight, radial_weight, pre_own, pre_gh, unit_own, unit_gh, m0, nf0,
-        gs0, dot_a, dot_b, gr1, gr2, gr3, gr4, en_a, en_b, new_a, new_b,
-    )
-    forces = give_back(low, mid, high, own, meta)
+        feats, meta, mix_weight, out_weight, norm_weight, oh_own, oh_gh, d_gh, dt_gh, gate_own,
+        gate_gh, radial_own[4], radial_gh4,
+    )
+    new_b, en_b, dot_own_b, dot_gh_b, gr3_own, gr3_gh, gr4_own_a, gr4_gh_a = second_stage(
+        pieces1, *shared, radial_own[3], radial_gh3
+    )
+    new, energy, src, low, mid, high, dot_own_c, gr4_own_b = third_stage(
+        pieces2, *shared, radt, rbft, mixt, gs0, en_a, en_b, new_a, new_b, pre_gh, unit_gh, m0_gh,
+        nf0_gh, dot_gh_a, dot_gh_b, gr1_gh, gr2_gh, gr3_gh, gr4_gh_a,
+    )
+    own = own_back_stage(
+        oh_own, pre_own, unit_own, radt, rbft, mixt, gs0, src, m0_own, nf0_own, dot_own_a,
+        dot_own_b, dot_own_c, gr1_own, gr2_own, gr3_own, gr4_own_a, gr4_own_b,
+    )
+    forces = give_back(low, mid, high, own, home)
     return (
         new[None, None, None],
         energy[None, None],

time: 104 us -> 82.7 us (0.80)
  Pallas kernels: 51.6 us -> 29.4 us
  local copies, waits for them, and re-layouts: 2.56 us -> 4.63 us
  other arithmetic: 2.01 us -> 0.4 us
    pallas_call x6 -> x7, Pallas kernels: 51.6 us -> 29.4 us  [call(): pl.pallas_call(kernel, out_shape=out_shape, in_specs=specs or [pl.BlockSp...]
    ppermute x3, waiting for transfers between devices: 8.05 us -> 4.2 us  [neighbours_of(): other = lax.ppermute(block, axis, up)]
    ppermute x6, waiting for transfers between devices: 5.03 us -> 8.55 us  [neighbours_of(): lax.ppermute(lax.slice_in_dim(block, length - 1, length, axis=dim), axis,...]
    ppermute x6, waiting for transfers between devices: 2.33 us -> 4.23 us  [neighbours_of(): after = lax.ppermute(lax.slice_in_dim(block, 0, 1, axis=dim), axis, down)]
    ppermute x1, waiting for transfers between devices: 1.5 us -> 0.01 us  [give_back(): from_low = lax.ppermute(high, 'gx', up)]
    unnamed x26, local copies, waits for them, and re-layouts: 2.2 us -> 3.6 us
    ppermute x6, starting transfers between devices: 10.6 us -> 9.27 us  [neighbours_of(): after = lax.ppermute(lax.slice_in_dim(block, 0, 1, axis=dim), axis, down)]
    ppermute x6, starting transfers between devices: 3.36 us -> 4.69 us  [neighbours_of(): lax.ppermute(lax.slice_in_dim(block, length - 1, length, axis=dim), axis,...]
  transfers between devices with their start and end apart: 20 -> 20, of which waited for: 8 -> 10; matrix products, arithmetic and copies ran while one was open for 0% -> 1% of each run, Pallas kernels for 30% -> 25%
where the time goes in v4:
time: 82.7 us; the launch traced here: 82.4 us
  Pallas kernels  29.4 us (36%)
  starting transfers between devices  25.4 us (31%)
  waiting for transfers between devices  21.7 us (26%)
  local copies, waits for them, and re-layouts  4.63 us (6%)
  between operations  0.91 us (1%)
    pallas_call x7, Pallas kernels, call(): pl.pallas_call(kernel, out_shape=out_shape, in_specs=specs or [pl.BlockSp...  29.4 us
    ppermute x6, starting transfers between devices, neighbours_of(): after = lax.ppermute(lax.slice_in_dim(block, 0, 1, axis=dim), axis, down)  9.27 us
    ppermute x6, waiting for transfers between devices, neighbours_of(): lax.ppermute(lax.slice_in_dim(block, length - 1, length, axis=dim), axis,...  8.55 us
    ppermute x3, starting transfers between devices, neighbours_of(): other = lax.ppermute(block, axis, up)  5.19 us
    ppermute x6, starting transfers between devices, neighbours_of(): lax.ppermute(lax.slice_in_dim(block, length - 1, length, axis=dim), axis,...  4.69 us
    ppermute x6, waiting for transfers between devices, neighbours_of(): after = lax.ppermute(lax.slice_in_dim(block, 0, 1, axis=dim), axis, down)  4.23 us
    ppermute x3, waiting for transfers between devices, neighbours_of(): other = lax.ppermute(block, axis, up)  4.2 us
    ppermute x1, starting transfers between devices, give_back(): from_high = lax.ppermute(mid, 'gy', down)  3.81 us
  transfers between devices with their start and end apart: 20, of which 10 were waited for; matrix products, arithmetic and copies ran while one was open for 1% of the time, Pallas kernels for 25%

profile of v4, /device:TPU:0, one launch (start us, length us, event | category | flops | bytes accessed | tf_op | source)
XLA Modules:
  0.0 82.4 jit_solution(5364472028011208132)
XLA Ops:
  3.5 3.0 %collective-permute-start = (bf16[2,2,2,8,1280]{4,3,2,1,0:T(8,128)(2,1)S(1)}, bf16[2,2,2,8,1280]{4,3,2,1,0:T(8,128)(2,1)S(1)}, u32[]{:S(2)}, u32[]{:S(2)}) collective-permute-start(bf16[2,2,2,8,1280]{4,3,2,1,0:T(8,128)(2,1)S(1)} %bitcast.33), channel_id=1, source_target_pairs={{0,1},{1,0},{2,3},{3,2},{4,5},{5,4},{6,7},{7,6},{8,9},{9,8},{10,11... | collective-permute-start | bytes 491528 | tf_op jit(solution)/shard_map/ppermute | solution.py:774
  6.5 4.2 %collective-permute-done = bf16[2,2,2,8,1280]{4,3,2,1,0:T(8,128)(2,1)S(1)} collective-permute-done((bf16[2,2,2,8,1280]{4,3,2,1,0:T(8,128)(2,1)S(1)}, bf16[2,2,2,8,1280]{4,3,2,1,0:T(8,128)(2,1)S(1)}, u32[]{:S(2)}, u32[]{:S(2)}) %collective-permute-start) | collective-permute-done | bytes 163872 | tf_op jit(solution)/shard_map/ppermute | solution.py:774
  10.8 1.8 %collective-permute-start.3 = (bf16[2,2,2,8,1024]{4,3,2,1,0:T(8,128)(2,1)S(1)}, bf16[2,2,2,8,1024]{4,3,2,1,0:T(8,128)(2,1)S(1)}, u32[]{:S(2)}, u32[]{:S(2)}) collective-permute-start(bf16[2,2,2,8,1024]{4,3,2,1,0:T(8,128)(2,1)S(1)} %bitcast.37), channel_id=1, source_target_pairs={{0,1},{1,0},{2,3},{3,2},{4,5},{5,4},{6,7},{7,6},{8,9},{9,8},{10,11... | collective-permute-start | bytes 393224 | tf_op jit(solution)/shard_map/ppermute | solution.py:774
  12.6 1.6 %collective-permute-start.1 = (bf16[2,1,4,8,1280]{4,3,2,1,0:T(8,128)(2,1)S(1)}, bf16[2,1,4,8,1280]{4,3,2,1,0:T(8,128)(2,1)S(1)}, u32[]{:S(2)}, u32[]{:S(2)}) collective-permute-start(bf16[2,1,4,8,1280]{4,3,2,1,0:T(8,128)(2,1)S(1)} %get-tuple-element.158), channel_id=1, source_target_pairs={{0,2},{2,4},{4,6},{6,0},{1,3},{3,5},{5,7},{7,1},{8,10},{10,12},{12... | collective-permute-start | bytes 491528 | tf_op jit(solution)/shard_map/ppermute | solution.py:779
  14.3 2.2 %collective-permute-start.2 = (bf16[2,1,4,8,1280]{4,3,2,1,0:T(8,128)(2,1)S(1)}, bf16[2,1,4,8,1280]{4,3,2,1,0:T(8,128)(2,1)S(1)}, u32[]{:S(2)}, u32[]{:S(2)}) collective-permute-start(bf16[2,1,4,8,1280]{4,3,2,1,0:T(8,128)(2,1)S(1)} %get-tuple-element.159), channel_id=1, source_target_pairs={{2,0},{4,2},{6,4},{0,6},{3,1},{5,3},{7,5},{1,7},{10,8},{12,10},{14... | collective-permute-start | bytes 491528 | tf_op jit(solution)/shard_map/ppermute | solution.py:780
  16.9 2.9 %own_edges.1 = (bf16[1024,64]{1,0:T(8,128)(2,1)S(1)}, bf16[1024,128]{1,0:T(8,128)(2,1)S(1)}, f32[1024,128]{1,0:T(8,128)S(1)}, bf16[640,128]{1,0:T(8,128)(2,1)S(1...) custom-call(f32[64,128]{1,0:T(8,128)S(1)} %get-tuple-element.83.meta, ...), custom_call_target="tpu_custom_call" | custom-call | flops 2147483648 | bytes 3096576 | tf_op jit(solution)/shard_map/own_edges/pallas_call | solution.py:54
  19.8 1.3 %collective-permute-done.1 = bf16[2,1,4,8,1280]{4,3,2,1,0:T(8,128)(2,1)S(1)} collective-permute-done((bf16[2,1,4,8,1280]{4,3,2,1,0:T(8,128)(2,1)S(1)}, bf16[2,1,4,8,1280]{4,3,2,1,0:T(8,128)(2,1)S(1)}, u32[]{:S(2)}, u32[]{:S(2)}) %collective-permute-start.1) | collective-permute-done | bytes 163872 | tf_op jit(solution)/shard_map/ppermute | solution.py:779
  21.1 1.1 %collective-permute-done.2 = bf16[2,1,4,8,1280]{4,3,2,1,0:T(8,128)(2,1)S(1)} collective-permute-done((bf16[2,1,4,8,1280]{4,3,2,1,0:T(8,128)(2,1)S(1)}, bf16[2,1,4,8,1280]{4,3,2,1,0:T(8,128)(2,1)S(1)}, u32[]{:S(2)}, u32[]{:S(2)}) %collective-permute-start.2) | collective-permute-done | bytes 163872 | tf_op jit(solution)/shard_map/ppermute | solution.py:780
  22.4 1.2 %collective-permute-start.6 = (bf16[2,1,4,8,1024]{4,3,2,1,0:T(8,128)(2,1)S(1)}, bf16[2,1,4,8,1024]{4,3,2,1,0:T(8,128)(2,1)S(1)}, u32[]{:S(2)}, u32[]{:S(2)}) collective-permute-start(bf16[2,1,4,8,1024]{4,3,2,1,0:T(8,128)(2,1)S(1)} %get-tuple-element.162), channel_id=1, source_target_pairs={{0,2},{2,4},{4,6},{6,0},{1,3},{3,5},{5,7},{7,1},{8,10},{10,12},{12... | collective-permute-start | bytes 393224 | tf_op jit(solution)/shard_map/ppermute | solution.py:779
  23.6 2.7 %collective-permute-start.7 = (bf16[2,1,4,8,1024]{4,3,2,1,0:T(8,128)(2,1)S(1)}, bf16[2,1,4,8,1024]{4,3,2,1,0:T(8,128)(2,1)S(1)}, u32[]{:S(2)}, u32[]{:S(2)}) collective-permute-start(bf16[2,1,4,8,1024]{4,3,2,1,0:T(8,128)(2,1)S(1)} %get-tuple-element.163), channel_id=1, source_target_pairs={{2,0},{4,2},{6,4},{0,6},{3,1},{5,3},{7,5},{1,7},{10,8},{12,10},{14... | collective-permute-start | bytes 393224 | tf_op jit(solution)/shard_map/ppermute | solution.py:780
  26.9 3.4 %collective-permute-done.6 = bf16[2,1,4,8,1024]{4,3,2,1,0:T(8,128)(2,1)S(1)} collective-permute-done((bf16[2,1,4,8,1024]{4,3,2,1,0:T(8,128)(2,1)S(1)}, bf16[2,1,4,8,1024]{4,3,2,1,0:T(8,128)(2,1)S(1)}, u32[]{:S(2)}, u32[]{:S(2)}) %collective-permute-start.6) | collective-permute-done | bytes 131104 | tf_op jit(solution)/shard_map/ppermute | solution.py:779
  30.7 2.8 %collective-permute-done.5 = bf16[1,4,4,8,1280]{4,3,2,1,0:T(8,128)(2,1)S(1)} collective-permute-done((bf16[1,4,4,8,1280]{4,3,2,1,0:T(8,128)(2,1)S(1)}, bf16[1,4,4,8,1280]{4,3,2,1,0:T(8,128)(2,1)S(1)}, u32[]{:S(2)}, u32[]{:S(2)}) %collective-permute-start.5) | collective-permute-done | bytes 327712 | tf_op jit(solution)/shard_map/ppermute | solution.py:780
  33.5 2.9 %collective-permute-done.4 = bf16[1,4,4,8,1280]{4,3,2,1,0:T(8,128)(2,1)S(1)} collective-permute-done((bf16[1,4,4,8,1280]{4,3,2,1,0:T(8,128)(2,1)S(1)}, bf16[1,4,4,8,1280]{4,3,2,1,0:T(8,128)(2,1)S(1)}, u32[]{:S(2)}, u32[]{:S(2)}) %collective-permute-start.4) | collective-permute-done | bytes 327712 | tf_op jit(solution)/shard_map/ppermute | solution.py:779
  37.2 1.3 %collective-permute-start.9 = (bf16[2,1,4,8,1024]{4,3,2,1,0:T(8,128)(2,1)S(1)}, bf16[2,1,4,8,1024]{4,3,2,1,0:T(8,128)(2,1)S(1)}, u32[]{:S(2)}, u32[]{:S(2)}) collective-permute-start(bf16[2,1,4,8,1024]{4,3,2,1,0:T(8,128)(2,1)S(1)} %get-tuple-element.160), channel_id=1, source_target_pairs={{0,2},{2,4},{4,6},{6,0},{1,3},{3,5},{5,7},{7,1},{8,10},{10,12},{12... | collective-permute-start | bytes 393224 | tf_op jit(solution)/shard_map/ppermute | solution.py:779
  38.6 1.7 %collective-permute-start.14 = (bf16[1,4,4,8,1024]{4,3,2,1,0:T(8,128)(2,1)S(1)}, bf16[1,4,4,8,1024]{4,3,2,1,0:T(8,128)(2,1)S(1)}, u32[]{:S(2)}, u32[]{:S(2)}) collective-permute-start(bf16[1,4,4,8,1024]{4,3,2,1,0:T(8,128)(2,1)S(1)} %get-tuple-element.154), channel_id=1, source_target_pairs={{8,0},{16,8},{24,16},{0,24},{9,1},{17,9},{25,17},{1,25},{10,2},{18... | collective-permute-start | bytes 786440 | tf_op jit(solution)/shard_map/ppermute | solution.py:780
  41.0 9.5 %first_group.1 = (bf16[64,1152]{1,0:T(8,128)(2,1)S(1)}, bf16[1024,512]{1,0:T(8,128)(2,1)S(1)}, bf16[1024,64]{1,0:T(8,128)(2,1)S(1)}, bf16[64,1024]{1,0:T(8,128)(...) custom-call(bf16[128,1280]{1,0:T(8,128)(2,1)S(1)} %bitcast.44, ...), custom_call_target="tpu_custom_call" | custom-call | flops 8589934592 | bytes 9292288 | tf_op jit(solution)/shard_map/first_group/pallas_call | solution.py:54
  50.7 1.7 %collective-permute-start.12 = (bf16[1,4,4,8,1024]{4,3,2,1,0:T(8,128)(2,1)S(1)}, bf16[1,4,4,8,1024]{4,3,2,1,0:T(8,128)(2,1)S(1)}, u32[]{:S(2)}, u32[]{:S(2)}) collective-permute-start(bf16[1,4,4,8,1024]{4,3,2,1,0:T(8,128)(2,1)S(1)} %get-tuple-element.156), channel_id=1, source_target_pairs={{8,0},{16,8},{24,16},{0,24},{9,1},{17,9},{25,17},{1,25},{10,2},{18... | collective-permute-start | bytes 786440 | tf_op jit(solution)/shard_map/ppermute | solution.py:780
  52.5 5.1 %second_group.1 = (bf16[64,1024]{1,0:T(8,128)(2,1)S(1)}, f32[64,128]{1,0:T(8,128)S(1)}, bf16[1024,128]{1,0:T(8,128)(2,1)S(1)}, bf16[1024,128]{1,0:T(8,128)(2,1)S...) custom-call(bf16[128,1024]{1,0:T(8,128)(2,1)S(1)} %bitcast.45, ...), custom_call_target="tpu_custom_call" | custom-call | flops 8589934592 | bytes 6572032 | tf_op jit(solution)/shard_map/second_group/pallas_call | solution.py:54
  58.5 7.9 %third_group.1 = (bf16[64,3200]{1,0:T(8,128)(2,1)}, f32[1,64]{1,0:T(1,128)}, f32[64,128]{1,0:T(8,128)S(1)}, f32[8,128]{1,0:T(8,128)S(1)}, f32[8,256]{1,0:T(8,128...) custom-call(bf16[128,1024]{1,0:T(8,128)(2,1)S(1)} %bitcast.47, ...), custom_call_target="tpu_custom_call" | custom-call | flops 8589934592 | bytes 8882432 | tf_op jit(solution)/shard_map/third_group/pallas_call | solution.py:54
  67.1 1.1 %collective-permute-start.16 = (f32[8,128]{1,0:T(8,128)S(1)}, f32[8,128]{1,0:T(8,128)S(1)}, u32[]{:S(2)}, u32[]{:S(2)}) collective-permute-start(f32[8,128]{1,0:T(8,128)S(1)} %get-tuple-element.131), channel_id=1, source_target_pairs={{8,0},{16,8},{24,16},{0,24},{9,1},{17,9},{25,17},{1,25},{10,2},{18... | collective-permute-start | bytes 12296 | tf_op jit(solution)/shard_map/ppermute | solution.py:813
  68.2 2.8 %own_back.1.own_ref = f32[8,64]{1,0:T(8,128)S(1)} custom-call(bf16[1024,64]{1,0:T(8,128)(2,1)S(1)} %get-tuple-element.92.oh_own, bf16[1024,128]{1,0:T(8,128)(2,1)S(1)} %get-tuple-element.132.pre_own, f32[1024,128]{1,0:T(8,128)S(1)} %get-tuple-element.133.unit_own, bf16[640,128]{1,0:T(8,128)(2,1)S(1)} %get-tuple-element.106.radt_ref, ...), custom_call_target="tpu_custom_call" | custom-call | flops 2147483648 | bytes 3934208 | tf_op jit(solution)/shard_map/own_back/pallas_call | solution.py:54
  71.1 3.8 %collective-permute-start.18 = (f32[8,256]{1,0:T(8,128)S(1)}, f32[8,256]{1,0:T(8,128)S(1)}, u32[]{:S(2)}, u32[]{:S(2)}) collective-permute-start(f32[8,256]{1,0:T(8,128)S(1)} %maximum_add_fusion), channel_id=1, source_target_pairs={{2,0},{4,2},{6,4},{0,6},{3,1},{5,3},{7,5},{1,7},{10,8},{12,10},{14... | collective-permute-start | bytes 24584 | tf_op jit(solution)/shard_map/ppermute | solution.py:818
  75.0 1.6 %collective-permute-done.17 = f32[8,256]{1,0:T(8,128)S(1)} collective-permute-done((f32[8,256]{1,0:T(8,128)S(1)}, f32[8,256]{1,0:T(8,128)S(1)}, u32[]{:S(2)}, u32[]{:S(2)}) %collective-permute-start.17) | collective-permute-done | bytes 8224 | tf_op jit(solution)/shard_map/ppermute | solution.py:817
  78.5 3.1 %collective-permute-done.19.low_ref.high_ref = f32[8,256]{1,0:T(8,128)S(1)} collective-permute-done((f32[8,256]{1,0:T(8,128)S(1)}, f32[8,256]{1,0:T(8,128)S(1)}, u32[]{:S(2)}, u32[]{:S(2)}) %collective-permute-start.19) | collective-permute-done | bytes 8224 | tf_op jit(solution)/shard_map/ppermute | solution.py:826
  (71 shorter events, 10.5 us)
Async XLA Ops:
  3.5 7.2 %collective-permute-start = (bf16[2,2,2,8,1280]{4,3,2,1,0:T(8,128)(2,1)S(1)}, bf16[2,2,2,8,1280]{4,3,2,1,0:T(8,128)(2,1)S(1)}, u32[]{:S(2)}, u32[]{:S(2)}) collective-permute-start(bf16[2,2,2,8,1280]{4,3,2,1,0:T(8,128)(2,1)S(1)} %bitcast.33), channel_id=1, source_target_pairs={{0,1},{1,0},{2,3},{3,2},{4,5},{5,4},{6,7},{7,6},{8,9},{9,8},{10,11... | collective-permute-start | bytes 491528 | tf_op jit(solution)/shard_map/ppermute | solution.py:774
  10.8 6.1 %copy-start.6 = (bf16[128,640]{1,0:T(8,128)(2,1)S(1)}, bf16[128,640]{1,0:T(8,128)(2,1)}, u32[]{:S(2)}) copy-start(bf16[128,640]{1,0:T(8,128)(2,1)} %rad_ref.3) | copy-start | bytes 491524
  10.8 6.1 %copy-start.7 = (bf16[5,128,128]{2,1,0:T(8,128)(2,1)S(1)}, bf16[5,128,128]{2,1,0:T(8,128)(2,1)}, u32[]{:S(2)}) copy-start(bf16[5,128,128]{2,1,0:T(8,128)(2,1)} %mix_ref.7) | copy-start | bytes 491524
  10.8 6.1 %copy-start.9 = (bf16[512,128]{1,0:T(8,128)(2,1)S(1)}, bf16[512,128]{1,0:T(8,128)(2,1)}, u32[]{:S(2)}) copy-start(bf16[512,128]{1,0:T(8,128)(2,1)} %rbf_ref.3) | copy-start | bytes 393220
  10.8 9.0 %collective-permute-start.3 = (bf16[2,2,2,8,1024]{4,3,2,1,0:T(8,128)(2,1)S(1)}, bf16[2,2,2,8,1024]{4,3,2,1,0:T(8,128)(2,1)S(1)}, u32[]{:S(2)}, u32[]{:S(2)}) collective-permute-start(bf16[2,2,2,8,1024]{4,3,2,1,0:T(8,128)(2,1)S(1)} %bitcast.37), channel_id=1, source_target_pairs={{0,1},{1,0},{2,3},{3,2},{4,5},{5,4},{6,7},{7,6},{8,9},{9,8},{10,11... | collective-permute-start | bytes 393224 | tf_op jit(solution)/shard_map/ppermute | solution.py:774
  12.6 8.5 %collective-permute-start.1 = (bf16[2,1,4,8,1280]{4,3,2,1,0:T(8,128)(2,1)S(1)}, bf16[2,1,4,8,1280]{4,3,2,1,0:T(8,128)(2,1)S(1)}, u32[]{:S(2)}, u32[]{:S(2)}) collective-permute-start(bf16[2,1,4,8,1280]{4,3,2,1,0:T(8,128)(2,1)S(1)} %get-tuple-element.158), channel_id=1, source_target_pairs={{0,2},{2,4},{4,6},{6,0},{1,3},{3,5},{5,7},{7,1},{8,10},{10,12},{12... | collective-permute-start | bytes 491528 | tf_op jit(solution)/shard_map/ppermute | solution.py:779
  14.3 8.0 %collective-permute-start.2 = (bf16[2,1,4,8,1280]{4,3,2,1,0:T(8,128)(2,1)S(1)}, bf16[2,1,4,8,1280]{4,3,2,1,0:T(8,128)(2,1)S(1)}, u32[]{:S(2)}, u32[]{:S(2)}) collective-permute-start(bf16[2,1,4,8,1280]{4,3,2,1,0:T(8,128)(2,1)S(1)} %get-tuple-element.159), channel_id=1, source_target_pairs={{2,0},{4,2},{6,4},{0,6},{3,1},{5,3},{7,5},{1,7},{10,8},{12,10},{14... | collective-permute-start | bytes 491528 | tf_op jit(solution)/shard_map/ppermute | solution.py:780
  16.5 10.4 %collective-permute-start.8 = (bf16[2,2,2,8,1024]{4,3,2,1,0:T(8,128)(2,1)S(1)}, bf16[2,2,2,8,1024]{4,3,2,1,0:T(8,128)(2,1)S(1)}, u32[]{:S(2)}, u32[]{:S(2)}) collective-permute-start(bf16[2,2,2,8,1024]{4,3,2,1,0:T(8,128)(2,1)S(1)} %bitcast.35), channel_id=1, source_target_pairs={{0,1},{1,0},{2,3},{3,2},{4,5},{5,4},{6,7},{7,6},{8,9},{9,8},{10,11... | collective-permute-start | bytes 393224 | tf_op jit(solution)/shard_map/ppermute | solution.py:774
  22.4 8.0 %collective-permute-start.6 = (bf16[2,1,4,8,1024]{4,3,2,1,0:T(8,128)(2,1)S(1)}, bf16[2,1,4,8,1024]{4,3,2,1,0:T(8,128)(2,1)S(1)}, u32[]{:S(2)}, u32[]{:S(2)}) collective-permute-start(bf16[2,1,4,8,1024]{4,3,2,1,0:T(8,128)(2,1)S(1)} %get-tuple-element.162), channel_id=1, source_target_pairs={{0,2},{2,4},{4,6},{6,0},{1,3},{3,5},{5,7},{7,1},{8,10},{10,12},{12... | collective-permute-start | bytes 393224 | tf_op jit(solution)/shard_map/ppermute | solution.py:779
  23.6 7.1 %collective-permute-start.7 = (bf16[2,1,4,8,1024]{4,3,2,1,0:T(8,128)(2,1)S(1)}, bf16[2,1,4,8,1024]{4,3,2,1,0:T(8,128)(2,1)S(1)}, u32[]{:S(2)}, u32[]{:S(2)}) collective-permute-start(bf16[2,1,4,8,1024]{4,3,2,1,0:T(8,128)(2,1)S(1)} %get-tuple-element.163), channel_id=1, source_target_pairs={{2,0},{4,2},{6,4},{0,6},{3,1},{5,3},{7,5},{1,7},{10,8},{12,10},{14... | collective-permute-start | bytes 393224 | tf_op jit(solution)/shard_map/ppermute | solution.py:780
  26.3 7.2 %collective-permute-start.5 = (bf16[1,4,4,8,1280]{4,3,2,1,0:T(8,128)(2,1)S(1)}, bf16[1,4,4,8,1280]{4,3,2,1,0:T(8,128)(2,1)S(1)}, u32[]{:S(2)}, u32[]{:S(2)}) collective-permute-start(bf16[1,4,4,8,1280]{4,3,2,1,0:T(8,128)(2,1)S(1)} %get-tuple-element.152), channel_id=1, source_target_pairs={{8,0},{16,8},{24,16},{0,24},{9,1},{17,9},{25,17},{1,25},{10,2},{18... | collective-permute-start | bytes 983048 | tf_op jit(solution)/shard_map/ppermute | solution.py:780
  26.4 10.0 %collective-permute-start.4 = (bf16[1,4,4,8,1280]{4,3,2,1,0:T(8,128)(2,1)S(1)}, bf16[1,4,4,8,1280]{4,3,2,1,0:T(8,128)(2,1)S(1)}, u32[]{:S(2)}, u32[]{:S(2)}) collective-permute-start(bf16[1,4,4,8,1280]{4,3,2,1,0:T(8,128)(2,1)S(1)} %get-tuple-element.153), channel_id=1, source_target_pairs={{0,8},{8,16},{16,24},{24,0},{1,9},{9,17},{17,25},{25,1},{2,10},{10... | collective-permute-start | bytes 983048 | tf_op jit(solution)/shard_map/ppermute | solution.py:779
  36.4 14.1 %collective-permute-start.10 = (bf16[2,1,4,8,1024]{4,3,2,1,0:T(8,128)(2,1)S(1)}, bf16[2,1,4,8,1024]{4,3,2,1,0:T(8,128)(2,1)S(1)}, u32[]{:S(2)}, u32[]{:S(2)}) collective-permute-start(bf16[2,1,4,8,1024]{4,3,2,1,0:T(8,128)(2,1)S(1)} %get-tuple-element.161), channel_id=1, source_target_pairs={{2,0},{4,2},{6,4},{0,6},{3,1},{5,3},{7,5},{1,7},{10,8},{12,10},{14... | collective-permute-start | bytes 393224 | tf_op jit(solution)/shard_map/ppermute | solution.py:780
  37.2 3.1 %copy-start.8 = (bf16[5,128,128]{2,1,0:T(8,128)(2,1)S(1)}, bf16[5,128,128]{2,1,0:T(8,128)(2,1)}, u32[]{:S(2)}) copy-start(bf16[5,128,128]{2,1,0:T(8,128)(2,1)} %out_ref.5) | copy-start | bytes 491524
  37.2 13.3 %collective-permute-start.9 = (bf16[2,1,4,8,1024]{4,3,2,1,0:T(8,128)(2,1)S(1)}, bf16[2,1,4,8,1024]{4,3,2,1,0:T(8,128)(2,1)S(1)}, u32[]{:S(2)}, u32[]{:S(2)}) collective-permute-start(bf16[2,1,4,8,1024]{4,3,2,1,0:T(8,128)(2,1)S(1)} %get-tuple-element.160), channel_id=1, source_target_pairs={{0,2},{2,4},{4,6},{6,0},{1,3},{3,5},{5,7},{7,1},{8,10},{10,12},{12... | collective-permute-start | bytes 393224 | tf_op jit(solution)/shard_map/ppermute | solution.py:779
  38.6 13.9 %collective-permute-start.13 = (bf16[1,4,4,8,1024]{4,3,2,1,0:T(8,128)(2,1)S(1)}, bf16[1,4,4,8,1024]{4,3,2,1,0:T(8,128)(2,1)S(1)}, u32[]{:S(2)}, u32[]{:S(2)}) collective-permute-start(bf16[1,4,4,8,1024]{4,3,2,1,0:T(8,128)(2,1)S(1)} %get-tuple-element.155), channel_id=1, source_target_pairs={{0,8},{8,16},{16,24},{24,0},{1,9},{9,17},{17,25},{25,1},{2,10},{10... | collective-permute-start | bytes 786440 | tf_op jit(solution)/shard_map/ppermute | solution.py:779
  38.6 13.8 %collective-permute-start.14 = (bf16[1,4,4,8,1024]{4,3,2,1,0:T(8,128)(2,1)S(1)}, bf16[1,4,4,8,1024]{4,3,2,1,0:T(8,128)(2,1)S(1)}, u32[]{:S(2)}, u32[]{:S(2)}) collective-permute-start(bf16[1,4,4,8,1024]{4,3,2,1,0:T(8,128)(2,1)S(1)} %get-tuple-element.154), channel_id=1, source_target_pairs={{8,0},{16,8},{24,16},{0,24},{9,1},{17,9},{25,17},{1,25},{10,2},{18... | collective-permute-start | bytes 786440 | tf_op jit(solution)/shard_map/ppermute | solution.py:780
  50.7 7.8 %collective-permute-start.11 = (bf16[1,4,4,8,1024]{4,3,2,1,0:T(8,128)(2,1)S(1)}, bf16[1,4,4,8,1024]{4,3,2,1,0:T(8,128)(2,1)S(1)}, u32[]{:S(2)}, u32[]{:S(2)}) collective-permute-start(bf16[1,4,4,8,1024]{4,3,2,1,0:T(8,128)(2,1)S(1)} %get-tuple-element.157), channel_id=1, source_target_pairs={{0,8},{8,16},{16,24},{24,0},{1,9},{9,17},{17,25},{25,1},{2,10},{10... | collective-permute-start | bytes 786440 | tf_op jit(solution)/shard_map/ppermute | solution.py:779
  50.7 7.8 %collective-permute-start.12 = (bf16[1,4,4,8,1024]{4,3,2,1,0:T(8,128)(2,1)S(1)}, bf16[1,4,4,8,1024]{4,3,2,1,0:T(8,128)(2,1)S(1)}, u32[]{:S(2)}, u32[]{:S(2)}) collective-permute-start(bf16[1,4,4,8,1024]{4,3,2,1,0:T(8,128)(2,1)S(1)} %get-tuple-element.156), channel_id=1, source_target_pairs={{8,0},{16,8},{24,16},{0,24},{9,1},{17,9},{25,17},{1,25},{10,2},{18... | collective-permute-start | bytes 786440 | tf_op jit(solution)/shard_map/ppermute | solution.py:780
  66.4 4.6 %collective-permute-start.15 = (f32[8,128]{1,0:T(8,128)S(1)}, f32[8,128]{1,0:T(8,128)S(1)}, u32[]{:S(2)}, u32[]{:S(2)}) collective-permute-start(f32[8,128]{1,0:T(8,128)S(1)} %get-tuple-element.130), channel_id=1, source_target_pairs={{0,8},{8,16},{16,24},{24,0},{1,9},{9,17},{17,25},{25,1},{2,10},{10... | collective-permute-start | bytes 12296 | tf_op jit(solution)/shard_map/ppermute | solution.py:812
  67.1 3.9 %collective-permute-start.16 = (f32[8,128]{1,0:T(8,128)S(1)}, f32[8,128]{1,0:T(8,128)S(1)}, u32[]{:S(2)}, u32[]{:S(2)}) collective-permute-start(f32[8,128]{1,0:T(8,128)S(1)} %get-tuple-element.131), channel_id=1, source_target_pairs={{8,0},{16,8},{24,16},{0,24},{9,1},{17,9},{25,17},{1,25},{10,2},{18... | collective-permute-start | bytes 12296 | tf_op jit(solution)/shard_map/ppermute | solution.py:813
  71.1 5.5 %collective-permute-start.17 = (f32[8,256]{1,0:T(8,128)S(1)}, f32[8,256]{1,0:T(8,128)S(1)}, u32[]{:S(2)}, u32[]{:S(2)}) collective-permute-start(f32[8,256]{1,0:T(8,128)S(1)} %maximum_add_fusion), channel_id=1, source_target_pairs={{0,2},{2,4},{4,6},{6,0},{1,3},{3,5},{5,7},{7,1},{8,10},{10,12},{12... | collective-permute-start | bytes 24584 | tf_op jit(solution)/shard_map/ppermute | solution.py:817
  71.1 6.0 %collective-permute-start.18 = (f32[8,256]{1,0:T(8,128)S(1)}, f32[8,256]{1,0:T(8,128)S(1)}, u32[]{:S(2)}, u32[]{:S(2)}) collective-permute-start(f32[8,256]{1,0:T(8,128)S(1)} %maximum_add_fusion), channel_id=1, source_target_pairs={{2,0},{4,2},{6,4},{0,6},{3,1},{5,3},{7,5},{1,7},{10,8},{12,10},{14... | collective-permute-start | bytes 24584 | tf_op jit(solution)/shard_map/ppermute | solution.py:818
  78.0 3.7 %collective-permute-start.19 = (f32[8,256]{1,0:T(8,128)S(1)}, f32[8,256]{1,0:T(8,128)S(1)}, u32[]{:S(2)}, u32[]{:S(2)}) collective-permute-start(f32[8,256]{1,0:T(8,128)S(1)} %fusion.1.mid_ref), channel_id=1, source_target_pairs={{0,1},{1,0},{2,3},{3,2},{4,5},{5,4},{6,7},{7,6},{8,9},{9,8},{10,11... | collective-permute-start | bytes 24584 | tf_op jit(solution)/shard_map/ppermute | solution.py:826
  (10 other events, 9.5 us)

commit v5 on v4

--- a/solution.py
+++ b/solution.py
@@ -1,3 +1,4 @@
+import functools
 import math
 
 import jax
@@ -22,7 +23,10 @@
     (3, 3), (3, 3), (3, 3), (3, 4),
     (4, 4), (4, 4), (4, 4), (4, 4),
 )
-GROUPS = ((0, 4), (4, 8), (8, 12))
+GROUPS = ((0, 3), (3, 8), (8, 12))
+KINDS = tuple(sorted({PAIR_DEGREES[pair] for pair in range(*group)}) for group in GROUPS)
+DEGREES = tuple(sorted({d for both in kinds for d in both}) for kinds in KINDS)
+GROUP_COLS = tuple(2 * CH * (end - begin) for begin, end in GROUPS)
 
 
 def mm(a, b):
@@ -63,16 +67,29 @@
     )(*args)
 
 
-def cells_kernel(feat_ref, pos_ref, near_ref, counts_ref, order_ref, *refs):
-    out_refs, (own_pos_ref, meta_ref, rows_ref, pos_rows) = refs[:3], refs[3:]
+def cells_kernel(
+    feat_hbm, pos_hbm, near_hbm, counts_hbm, order_hbm,
+    first_ref, rest_ref, own_pos_ref, meta_ref,
+    feat_ref, pos_ref, near_ref, counts_ref, order_ref, rows_ref, pos_rows, sems,
+):
+    args = (pos_hbm, near_hbm, counts_hbm, order_hbm, feat_hbm)
+    held = (pos_ref, near_ref, counts_ref, order_ref, feat_ref)
+    copies = [
+        pltpu.make_async_copy(arg, ref, sems.at[index])
+        for index, (arg, ref) in enumerate(zip(args, held))
+    ]
+    for copy in copies:
+        copy.start()
+    rows_ref[...] = jnp.zeros_like(rows_ref)
+    pos_rows[...] = jnp.zeros_like(pos_rows)
+    for copy in copies[:4]:
+        copy.wait()
     atoms = feat_ref.shape[0]
-    rows_ref[...] = jnp.zeros_like(rows_ref)
     rows_ref[0:SLOTS, :] = near_ref[...].astype(F32)
     rows_ref[SLOTS : SLOTS + 1, :] = counts_ref[...].astype(F32)
     rows_ref[SLOTS + 1 : SLOTS + 2, :] = order_ref[...].astype(F32)
     meta = rows_ref[...].T
     meta_ref[...] = meta
-    pos_rows[...] = jnp.zeros_like(pos_rows)
     for comp in range(3):
         places = pos_ref[comp]
         first = places.astype(BF16).astype(F32)
@@ -85,25 +102,28 @@
     pick = (meta[:, SLOTS + 1 : SLOTS + 2] == lane).astype(F32).astype(BF16)
     same = (iota((atoms, atoms), 0) == iota((atoms, atoms), 1)).astype(F32).astype(BF16)
     own_pos_ref[...] = mm_nt(same, pieces).astype(BF16)
-    for group, (begin, end) in enumerate(GROUPS):
-        at = 0 if group == 0 else pair_cols(begin).start
-        till = pair_cols(end - 1).stop
-        out_refs[group][:, 0 : till - at] = mm(pick, feat_ref[:, at:till]).astype(BF16)
-        if group == 0:
-            out_refs[group][:, till:] = mm_nt(pick, pieces).astype(BF16)
+    first_ref[:, CH : 2 * CH] = mm_nt(pick, pieces).astype(BF16)
+    copies[4].wait()
+    first_ref[:, 0:CH] = mm(pick, feat_ref[:, 0:CH]).astype(BF16)
+    cut = pair_cols(GROUPS[1][0]).start
+    first_ref[:, 2 * CH :] = mm(pick, feat_ref[:, CH:cut]).astype(BF16)
+    rest_ref[...] = mm(pick, feat_ref[:, cut:]).astype(BF16)
 
 
 def make_cells(feats, places, near, counts, order):
     atoms = feats.shape[0]
-    widths = [CH * 2 * (end - begin) for begin, end in GROUPS]
-    widths[0] += 2 * CH
-    out_shape = tuple(struct(atoms, width, dtype=BF16) for width in widths) + (
+    out_shape = (
+        struct(atoms, 2 * CH + GROUP_COLS[0], dtype=BF16),
+        struct(atoms, sum(GROUP_COLS[1:]), dtype=BF16),
         struct(atoms, CH, dtype=BF16),
         struct(atoms, CH),
     )
-    scratch = [pltpu.VMEM((CH, atoms), F32), pltpu.VMEM((CH, atoms), F32)]
     args = (feats, places, near, counts, order)
-    return call(cells_kernel, "cells", out_shape, scratch, 1 << 26, args)
+    scratch = [pltpu.VMEM(arg.shape, arg.dtype) for arg in args]
+    scratch += [pltpu.VMEM((CH, atoms), F32), pltpu.VMEM((CH, atoms), F32)]
+    scratch += [pltpu.SemaphoreType.DMA((5,))]
+    specs = [pl.BlockSpec(memory_space=pltpu.HBM)] * 5
+    return call(cells_kernel, "cells", out_shape, scratch, 1 << 26, args, specs)
 
 
 def spacing_of(atoms, nbasis):
@@ -229,22 +249,30 @@
                     wot[kind, part, part] = out_t
 
 
-def fetch(pieces, table, sems):
+def fetch(pieces, cols, table, sems):
+    low, high, ghosts = 0, 0, table.shape[0]
+    if len(pieces) == 3:
+        rows = [(piece, 0, piece.shape[0]) for piece in pieces]
+    else:
+        low_in, low_out, mid, high_in, high_out = pieces
+        half = low_out.shape[0] // 2
+        rows = [(low_out, 0, half), (low_in, 0, low_in.shape[0]), (low_out, half, half)]
+        rows += [(mid, 0, mid.shape[0])]
+        rows += [(high_out, 0, half), (high_in, 0, high_in.shape[0]), (high_out, half, half)]
     copies = []
     at = 0
-    for index, piece in enumerate(pieces):
-        rows = piece.shape[0]
-        copies.append(
-            pltpu.make_async_copy(piece, table.at[pl.ds(at, rows), :], sems.at[index])
-        )
-        at += rows
+    for index, (piece, start, count) in enumerate(rows):
+        source = piece.at[pl.ds(start, count), cols]
+        target = table.at[pl.ds(at, count), :]
+        copies.append(pltpu.make_async_copy(source, target, sems.at[index]))
+        at += count
     for copy in copies:
         copy.start()
     return copies
 
 
 def run_pairs(
-    pairs, kinds, first_col, own_ref, table, new_ref, new_base, oh_own, oh_gh, d_gh, dt_gh,
+    pairs, kinds, own_ref, table, new_ref, new_base, oh_own, oh_gh, d_gh, dt_gh,
     gate_ref, radial_of, nw_ref, steps, wm, wmt, wo, wot, nf_s, mx_s, acc_s, gs_s, dot_ref,
     grad_refs, en_ref, size=STEP,
 ):
@@ -254,7 +282,6 @@
     own_steps = OWN_STEPS * STEP // size
     begin, end = pair_cols(pairs[0]).start, pair_cols(pairs[-1]).stop
     own_cols = slice(begin, end)
-    table_cols = slice(begin - first_col, end - first_col)
     infos = []
     for index, pair in enumerate(pairs):
         degrees = PAIR_DEGREES[pair]
@@ -303,7 +330,7 @@
 
     def ghost_forward(step):
         here, rows = ghost_rows(step, size)
-        message = forward(rows, oh_gh[here, :], table[:, table_cols])
+        message = forward(rows, oh_gh[here, :], table[...])
         acc_s[...] += mm(dt_gh[:, here], message)
 
     over_ghost_steps(steps, ghost_forward, size)
@@ -332,14 +359,18 @@
     over_ghost_steps(steps, ghost_backward, size)
 
 
-def pair_scratch(atoms, edges, kinds):
-    count = len(kinds)
-    return [pltpu.VMEM((count, 2 * CH, 2 * CH), BF16) for _ in range(4)] + [
-        pltpu.VMEM((edges, 8 * CH), BF16),
-        pltpu.VMEM((edges, 8 * CH), BF16),
-        pltpu.VMEM((atoms, 8 * CH), F32),
-        pltpu.VMEM((atoms, 8 * CH), BF16),
-    ]
+def pair_scratch(atoms, edges, ghosts, group):
+    count, width = len(KINDS[group]), GROUP_COLS[group]
+    return (
+        [pltpu.VMEM((ghosts, width), BF16), pltpu.SemaphoreType.DMA((7,))]
+        + [pltpu.VMEM((count, 2 * CH, 2 * CH), BF16) for _ in range(4)]
+        + [
+            pltpu.VMEM((edges, width), BF16),
+            pltpu.VMEM((edges, width), BF16),
+            pltpu.VMEM((atoms, width), F32),
+            pltpu.VMEM((atoms, width), BF16),
+        ]
+    )
 
 
 def own_kernel(
@@ -396,28 +427,21 @@
     return call(own_kernel, "own_edges", out_shape, [], 1 << 31, args)
 
 
-def first_kernel(
-    low_ref, mid_ref, high_ref, own_ref, own_pos_ref, meta_ref, rbf_ref, rad_ref, mix_ref,
-    out_ref, ew_ref, nw_ref, oh_own, radial_own0, radial_own1, radial_own2,
-    new_ref, oh_gh, d_gh, dt_gh, radial_gh3, radial_gh4, pre_ref, unit_ref, gs0_ref, en_ref,
-    m0_own, m0_gh, gate_own, gate_gh, nf0_own, nf0_gh, dot_own, dot_gh, gr1_own, gr1_gh, gr2_own,
-    gr2_gh,
-    table, sems, ghpos, radial_gh0, radial_gh1, radial_gh2, wm, wmt, wo, wot, nf_s, mx_s, acc_s,
-    gs_s,
+def start_kernel(
+    p0, p1, p2, p3, p4, own_ref, own_pos_ref, meta_ref, rbf_ref, rad_ref, mix_ref, out_ref,
+    ew_ref, oh_own, radial_own0,
+    new_ref, oh_gh, d_gh, dt_gh, pre_ref, unit_ref, gs0_ref, en_ref, m0_own, m0_gh, gate_own,
+    gate_gh, nf0_own, nf0_gh, radial_gh1, radial_gh2, radial_gh3, radial_gh4,
+    table, sems, ghpos, acc_s,
 ):
-    m0_ref, gate_ref, nf0_ref = Halves(m0_own, m0_gh), Halves(gate_own, gate_gh), Halves(nf0_own, nf0_gh)
-    dot_ref, gr1_ref, gr2_ref = Halves(dot_own, dot_gh), Halves(gr1_own, gr1_gh), Halves(gr2_own, gr2_gh)
-    radial_gh = (radial_gh0, radial_gh1, radial_gh2, radial_gh3, radial_gh4)
-    radials = [Halves(radial_own0, radial_gh0), Halves(radial_own1, radial_gh1)]
-    radials.append(Halves(radial_own2, radial_gh2))
-    pairs = tuple(range(*GROUPS[0]))
-    kinds = sorted({PAIR_DEGREES[pair] for pair in pairs})
-    copies = fetch((low_ref, mid_ref, high_ref), table, sems)
+    m0_ref, gate_ref = Halves(m0_own, m0_gh), Halves(gate_own, gate_gh)
+    nf0_ref = Halves(nf0_own, nf0_gh)
+    radial_gh = (None, radial_gh1, radial_gh2, radial_gh3, radial_gh4)
+    copies = fetch((p0, p1, p2, p3, p4), slice(0, 2 * CH), table, sems)
     atoms = own_ref.shape[0]
     ghosts = table.shape[0]
     spacing = spacing_of(atoms, rbf_ref.shape[0])
     norm = 1.0 / math.sqrt(SLOTS)
-    block_diagonal(kinds, mix_ref, out_ref, wm, wmt, wo, wot)
 
     live = live_ghosts(meta_ref)
     sub_atom = iota((atoms, atoms), 0)
@@ -450,10 +474,6 @@
     shift = jnp.where(lane == 12, side_of(ext_x, 3, 4.0), 0.0)
     shift = jnp.where(lane == 13, side_of(ext_y, 3, 4.0), shift)
     shift = jnp.where(lane == 14, side_of(ext_z, zcells + 1, 2.0 * zcells), shift)
-    for copy in copies:
-        copy.wait()
-    ghpos[...] = (table[:, table.shape[1] - CH :].astype(F32) + shift).astype(BF16)
-
     def forward0(rows, onehot, feats, radial):
         near = mm(onehot, feats).astype(BF16)
         nf0_ref[rows, :] = near
@@ -471,7 +491,10 @@
         message = forward0(rows, oh_own[rows, :], own0, radial_own0[rows, :])
         part = mm(spread_own, message)
         summed = part if summed is None else summed + part
-    acc_s[:, 0:CH] = summed
+    acc_s[...] = summed
+    for copy in copies:
+        copy.wait()
+    ghpos[...] = (table[:, CH:].astype(F32) + shift).astype(BF16)
 
     def ghost_start(step):
         here, rows = ghost_rows(step)
@@ -496,14 +519,14 @@
         unit_ref[here, :] = unit
         pre, radial = radial_net(dist, spacing, rbf_ref, rad_ref)
         pre_ref[here, :] = pre.astype(BF16)
-        for degree in range(5):
+        for degree in range(1, 5):
             radial_gh[degree][here, :] = radial[:, degree * CH : (degree + 1) * CH]
         message = forward0(rows, onehot, table[:, 0:CH], radial[:, 0:CH])
-        acc_s[:, 0:CH] += mm(spread, message)
+        acc_s[...] += mm(spread, message)
 
     over_ghost_steps(steps, ghost_start)
 
-    low0 = (acc_s[:, 0:CH] * norm).astype(BF16)
+    low0 = (acc_s[...] * norm).astype(BF16)
     updated0 = own0.astype(F32) + mm(low0, out_ref[0])
     new_ref[:, 0:CH] = updated0.astype(BF16)
     logistic = jax.nn.sigmoid(updated0)
@@ -512,15 +535,6 @@
     grad0 = (weight0 * logistic * (1.0 + updated0 * (1.0 - logistic))).astype(BF16)
     gs0_ref[...] = mm_nt(grad0, out_ref[0]) * norm
 
-    def radial_any(degree, rows):
-        return radials[degree][rows, :]
-
-    run_pairs(
-        pairs, kinds, 0, own_ref, table, new_ref, 0, oh_own, oh_gh, d_gh, dt_gh, gate_ref,
-        radial_any, nw_ref, steps, wm, wmt, wo, wot, nf_s, mx_s, acc_s, gs_s, dot_ref,
-        {1: gr1_ref, 2: gr2_ref}, en_ref,
-    )
-
 
 def any_specs(count, total):
     return [pl.BlockSpec(memory_space=pl.ANY)] * count + [
@@ -528,54 +542,52 @@
     ] * (total - count)
 
 
-def first_stage(pieces, feats, own_pos, meta, rbf, rad, mix, out, ew, nw, oh_own, *radial_own):
+def start_stage(pieces, feats, *rest):
     atoms = feats.shape[0]
     half = atoms * HALF
-    edges = 2 * half
-    width = pieces[0].shape[1]
     ghosts = sum(piece.shape[0] for piece in pieces)
-    kinds = sorted({PAIR_DEGREES[pair] for pair in range(*GROUPS[0])})
     out_shape = (
-        struct(atoms, width - CH, dtype=BF16),
+        struct(atoms, CH, dtype=BF16),
         struct(half, ghosts, dtype=BF16),
         struct(half, atoms, dtype=BF16),
         struct(atoms, half, dtype=BF16),
         struct(half, CH, dtype=BF16),
-        struct(half, CH, dtype=BF16),
-        struct(half, CH, dtype=BF16),
         struct(half, CH),
         struct(atoms, CH),
         struct(atoms, CH),
-    ) + (struct(half, CH, dtype=BF16),) * 12
+    ) + (struct(half, CH, dtype=BF16),) * 10
     scratch = [
-        pltpu.VMEM((ghosts, width), BF16),
-        pltpu.SemaphoreType.DMA((3,)),
+        pltpu.VMEM((ghosts, 2 * CH), BF16),
+        pltpu.SemaphoreType.DMA((7,)),
         pltpu.VMEM((ghosts, CH), BF16),
-    ] + [pltpu.VMEM((half, CH), BF16)] * 3 + pair_scratch(atoms, edges, kinds)
-    args = tuple(pieces) + (
-        feats, own_pos, meta, rbf, rad, mix, out, ew, nw, oh_own
-    ) + radial_own
+        pltpu.VMEM((atoms, CH), F32),
+    ]
+    args = tuple(pieces) + (feats,) + rest
     return call(
-        first_kernel, "first_group", out_shape, scratch, 1 << 33, args, any_specs(3, len(args)),
-        32,
-    )
-
-
-def second_kernel(
-    low_ref, mid_ref, high_ref, own_ref, meta_ref, mix_ref, out_ref, nw_ref, oh_own, oh_gh, d_gh,
-    dt_gh, gate_own, gate_gh, radial_own4, radial_gh4, radial_own3, radial_gh3,
-    new_ref, en_ref, dot_own, dot_gh, gr3_own, gr3_gh, gr4_own, gr4_gh,
-    table, sems, wm, wmt, wo, wot, nf_s, mx_s, acc_s, gs_s,
-):
-    radials = {3: Halves(radial_own3, radial_gh3), 4: Halves(radial_own4, radial_gh4)}
-    gate_ref = Halves(gate_own, gate_gh)
-    dot_ref, gr3_ref, gr4_ref = Halves(dot_own, dot_gh), Halves(gr3_own, gr3_gh), Halves(gr4_own, gr4_gh)
-    pairs = tuple(range(*GROUPS[1]))
-    kinds = sorted({PAIR_DEGREES[pair] for pair in pairs})
-    copies = fetch((low_ref, mid_ref, high_ref), table, sems)
-    block_diagonal(kinds, mix_ref, out_ref, wm, wmt, wo, wot)
+        start_kernel, "ghost_start", out_shape, scratch, 1 << 31, args,
+        any_specs(len(pieces), len(args)), 24,
+    )
+
+
+def pairs_kernel(group, count, skip, *refs):
+    pieces, refs = refs[:count], refs[count:]
+    own_ref, meta_ref, mix_ref, out_ref, nw_ref, oh_own, oh_gh, d_gh, dt_gh = refs[:9]
+    gate_ref = Halves(*refs[9:11])
+    refs = refs[11:]
+    degrees = DEGREES[group]
+    radials = {}
+    for degree in degrees:
+        radials[degree], refs = Halves(*refs[:2]), refs[2:]
+    new_ref, en_ref, dot_own, dot_gh = refs[:4]
+    refs = refs[4:]
+    grads = {}
+    for degree in degrees:
+        grads[degree], refs = Halves(*refs[:2]), refs[2:]
+    table, sems, wm, wmt, wo, wot, nf_s, mx_s, acc_s, gs_s = refs
+    copies = fetch(pieces, slice(skip, skip + GROUP_COLS[group]), table, sems)
+    block_diagonal(KINDS[group], mix_ref, out_ref, wm, wmt, wo, wot)
     en_ref[...] = jnp.zeros_like(en_ref)
-    base = pair_cols(pairs[0]).start
+    pairs = tuple(range(*GROUPS[group]))
 
     def radial_any(degree, rows):
         return radials[degree][rows, :]
@@ -583,31 +595,32 @@
     for copy in copies:
         copy.wait()
     run_pairs(
-        pairs, kinds, base, own_ref, table, new_ref, base, oh_own, oh_gh, d_gh, dt_gh, gate_ref,
-        radial_any, nw_ref, step_count(meta_ref), wm, wmt, wo, wot, nf_s, mx_s, acc_s, gs_s,
-        dot_ref, {3: gr3_ref, 4: gr4_ref}, en_ref,
-    )
-
-
-def second_stage(pieces, feats, *rest):
+        pairs, KINDS[group], own_ref, table, new_ref, pair_cols(pairs[0]).start, oh_own, oh_gh,
+        d_gh, dt_gh, gate_ref, radial_any, nw_ref, step_count(meta_ref), wm, wmt, wo, wot, nf_s,
+        mx_s, acc_s, gs_s, Halves(dot_own, dot_gh), grads, en_ref,
+    )
+
+
+def pairs_stage(group, skip, pieces, shared, radials):
+    feats = shared[0]
     atoms = feats.shape[0]
-    edges = atoms * SLOTS
-    width = pieces[0].shape[1]
+    half = atoms * HALF
     ghosts = sum(piece.shape[0] for piece in pieces)
-    kinds = sorted({PAIR_DEGREES[pair] for pair in range(*GROUPS[1])})
+    degrees = DEGREES[group]
     out_shape = (
-        struct(atoms, width, dtype=BF16),
+        struct(atoms, GROUP_COLS[group], dtype=BF16),
         struct(atoms, CH),
-    ) + (struct(atoms * HALF, CH, dtype=BF16),) * 6
-    scratch = [
-        pltpu.VMEM((ghosts, width), BF16),
-        pltpu.SemaphoreType.DMA((3,)),
-    ] + pair_scratch(atoms, edges, kinds)
-    args = tuple(pieces) + (feats,) + rest
-    return call(
-        second_kernel, "second_group", out_shape, scratch, 1 << 33, args,
-        any_specs(3, len(args)), 28,
-    )
+    ) + (struct(half, CH, dtype=BF16),) * (2 + 2 * len(degrees))
+    args = tuple(pieces) + tuple(shared)
+    for degree in degrees:
+        args += radials[degree]
+    new, energy, dot_own, dot_gh, *grads = call(
+        functools.partial(pairs_kernel, group, len(pieces), skip), "pairs_" + "abc"[group],
+        out_shape, pair_scratch(atoms, 2 * half, ghosts, group), 1 << 33, args,
+        any_specs(len(pieces), len(args)), 32,
+    )
+    grads = {degree: tuple(grads[2 * i : 2 * i + 2]) for i, degree in enumerate(degrees)}
+    return new, energy, dot_own, dot_gh, grads
 
 
 def finish(
@@ -640,37 +653,53 @@
     return total
 
 
+def degree_parts(refs, rows):
+    by_degree = {}
+    refs = list(refs)
+    for degrees in DEGREES:
+        for degree in degrees:
+            by_degree.setdefault(degree, []).append(refs.pop(0))
+    return [sum_of(by_degree[degree], rows).astype(BF16) for degree in range(1, 5)]
+
+
+PARTIALS = sum(len(degrees) for degrees in DEGREES)
+
+
 def third_kernel(
     low_ref, mid_ref, high_ref, own_ref, meta_ref, mix_ref, out_ref, nw_ref, oh_own, oh_gh, d_gh,
     dt_gh, gate_own, gate_gh, radial_own4, radial_gh4,
-    radt_ref, rbft_ref, mixt_ref, gs0_ref, en_a, en_b, new_a, new_b, pre_gh, unit_gh,
-    m0_ref, nf0_ref, dot_a, dot_b, gr1_ref, gr2_ref, gr3_ref, gr4_a,
-    new_ref, energy_ref, src_ref, flow_ref, fmid_ref, fhigh_ref, dot_own, gr4_own,
-    table, sems, wm, wmt, wo, wot, nf_s, mx_s, acc_s, gs_s, dot_c, gr4_b, en_s, fgh_s,
+    radt_ref, rbft_ref, mixt_ref, gs0_ref, en_0, en_a, en_b, new_0, new_a, new_b, pre_gh, unit_gh,
+    m0_ref, nf0_ref, dot_a, dot_b, *refs
 ):
+    gr_gh, refs = refs[: PARTIALS - 1], refs[PARTIALS - 1 :]
+    (
+        new_ref, energy_ref, src_ref, flow_ref, fmid_ref, fhigh_ref, dot_own, gr_own,
+        table, sems, wm, wmt, wo, wot, nf_s, mx_s, acc_s, gs_s, dot_c, gr_c, en_s, fgh_s,
+    ) = refs
+    group = 2
     gate_ref = Halves(gate_own, gate_gh)
-    radials = {4: Halves(radial_own4, radial_gh4)}
-    pairs = tuple(range(*GROUPS[2]))
-    kinds = sorted({PAIR_DEGREES[pair] for pair in pairs})
-    copies = fetch((low_ref, mid_ref, high_ref), table, sems)
+    radial4 = Halves(radial_own4, radial_gh4)
+    pairs = tuple(range(*GROUPS[group]))
+    copies = fetch((low_ref, mid_ref, high_ref), slice(0, GROUP_COLS[group]), table, sems)
     atoms = own_ref.shape[0]
     spacing = spacing_of(atoms, rbft_ref.shape[1])
-    block_diagonal(kinds, mix_ref, out_ref, wm, wmt, wo, wot)
-    en_s[...] = en_a[...] + en_b[...]
-    new_ref[:, 0 : new_a.shape[1]] = new_a[...]
-    new_ref[:, new_a.shape[1] : new_a.shape[1] + new_b.shape[1]] = new_b[...]
-    base = pair_cols(pairs[0]).start
+    block_diagonal(KINDS[group], mix_ref, out_ref, wm, wmt, wo, wot)
+    en_s[...] = en_0[...] + en_a[...] + en_b[...]
+    at = 0
+    for part in (new_0, new_a, new_b):
+        new_ref[:, at : at + part.shape[1]] = part[...]
+        at += part.shape[1]
     steps = step_count(meta_ref)
 
     def radial_any(degree, rows):
-        return radials[degree][rows, :]
+        return radial4[rows, :]
 
     for copy in copies:
         copy.wait()
     run_pairs(
-        pairs, kinds, base, own_ref, table, new_ref, 0, oh_own, oh_gh, d_gh, dt_gh, gate_ref,
+        pairs, KINDS[group], own_ref, table, new_ref, 0, oh_own, oh_gh, d_gh, dt_gh, gate_ref,
         radial_any, nw_ref, steps, wm, wmt, wo, wot, nf_s, mx_s, acc_s, gs_s,
-        Halves(dot_own, dot_c), {4: Halves(gr4_own, gr4_b)}, en_s,
+        Halves(dot_own, dot_c), {4: Halves(gr_own, gr_c)}, en_s,
     )
     energy_ref[...] = jnp.sum(en_s[...].T, axis=0, keepdims=True)
 
@@ -681,12 +710,10 @@
     def ghost_finish(step):
         here, rows = ghost_rows(step)
         grad = mm(d_gh[here, :], gs0_low)
-        dots = sum_of((dot_a, dot_b, dot_c), here)
-        parts = [gr1_ref[here, :], gr2_ref[here, :], gr3_ref[here, :]]
-        parts.append(sum_of((gr4_a, gr4_b), here).astype(BF16))
         pull, top, rest = finish(
-            grad, m0_ref[here, :], nf0_ref[here, :], dots, parts, pre_gh[here, :],
-            unit_gh[here, :], spacing, radt_ref, rbft_ref, mixt_ref,
+            grad, m0_ref[here, :], nf0_ref[here, :], sum_of((dot_a, dot_b, dot_c), here),
+            degree_parts(gr_gh + (gr_c,), here), pre_gh[here, :], unit_gh[here, :], spacing,
+            radt_ref, rbft_ref, mixt_ref,
         )
         pull_top = pull.astype(BF16)
         pull_rest = (pull - pull_top.astype(F32)).astype(BF16)
@@ -705,20 +732,14 @@
 def third_stage(pieces, feats, *rest):
     atoms, feat = feats.shape
     half = atoms * HALF
-    edges = 2 * half
-    width = pieces[0].shape[1]
     sizes = [piece.shape[0] for piece in pieces]
     ghosts = sum(sizes)
-    kinds = sorted({PAIR_DEGREES[pair] for pair in range(*GROUPS[2])})
     out_shape = (
         struct(atoms, feat, dtype=BF16),
         struct(1, atoms),
         struct(atoms, CH),
     ) + tuple(struct(8, size) for size in sizes) + (struct(half, CH, dtype=BF16),) * 2
-    scratch = [
-        pltpu.VMEM((ghosts, width), BF16),
-        pltpu.SemaphoreType.DMA((3,)),
-    ] + pair_scratch(atoms, edges, kinds) + [
+    scratch = pair_scratch(atoms, 2 * half, ghosts, 2) + [
         pltpu.VMEM((half, CH), BF16),
         pltpu.VMEM((half, CH), BF16),
         pltpu.VMEM((atoms, CH), F32),
@@ -733,9 +754,9 @@
 
 def own_back_kernel(
     oh_own, pre_own, unit_own, radt_ref, rbft_ref, mixt_ref, gs0_ref, src_ref,
-    m0_ref, nf0_ref, dot_a, dot_b, dot_c, gr1_ref, gr2_ref, gr3_ref, gr4_a, gr4_b,
-    force_ref,
+    m0_ref, nf0_ref, dot_a, dot_b, dot_c, *refs
 ):
+    gr_own, (force_ref,) = refs[:PARTIALS], refs[PARTIALS:]
     atoms = oh_own.shape[1]
     spacing = spacing_of(atoms, rbft_ref.shape[1])
     grad = tiled(gs0_ref[...])
@@ -743,11 +764,10 @@
     onto = jnp.zeros((8, atoms), F32)
     for step in range(OWN_STEPS):
         rows = own_rows(step)
-        parts = [gr1_ref[rows, :], gr2_ref[rows, :], gr3_ref[rows, :]]
-        parts.append(sum_of((gr4_a, gr4_b), rows).astype(BF16))
         pull, top, rest = finish(
-            grad, m0_ref[rows, :], nf0_ref[rows, :], sum_of((dot_a, dot_b, dot_c), rows), parts,
-            pre_own[rows, :], unit_own[rows, :], spacing, radt_ref, rbft_ref, mixt_ref,
+            grad, m0_ref[rows, :], nf0_ref[rows, :], sum_of((dot_a, dot_b, dot_c), rows),
+            degree_parts(gr_own, rows), pre_own[rows, :], unit_own[rows, :], spacing, radt_ref,
+            rbft_ref, mixt_ref,
         )
         src += jnp.sum(pull.reshape(STEP // atoms, atoms, CH), axis=0)
         onehot = oh_own[rows, :]
@@ -788,7 +808,21 @@
 
 def ghost_pieces(block):
     before, after = neighbours_of(block, "gx", 0)
-    return tuple(piece.reshape(-1, block.shape[-1]) for piece in (before, block, after))
+    return tuple(flat_rows(piece) for piece in (before, block, after))
+
+
+def flat_rows(piece):
+    return piece.reshape(-1, piece.shape[-1])
+
+
+def fold_kernel(mid_ref, low_ref, high_ref, out_ref):
+    lanes = mid_ref.shape[1]
+    ext_y = iota(mid_ref.shape, 1) // 32 % 4
+    out_ref[...] = (
+        mid_ref[...]
+        + jnp.where(ext_y == 1, pltpu.roll(low_ref[...], lanes - 64, 1), 0.0)
+        + jnp.where(ext_y == 2, pltpu.roll(high_ref[...], 64, 1), 0.0)
+    )
 
 
 def forces_kernel(mid_ref, low_ref, high_ref, own_ref, home_ref, out_ref):
@@ -816,12 +850,8 @@
     up, down = ring("gy")
     from_low = lax.ppermute(mid, "gy", up)
     from_high = lax.ppermute(mid, "gy", down)
-    ext_y = jnp.arange(mid.shape[1], dtype=jnp.int32)[None] // 32 % 4
-    mid = (
-        mid
-        + jnp.where(ext_y == 1, jnp.roll(from_low, -64, axis=1), 0.0)
-        + jnp.where(ext_y == 2, jnp.roll(from_high, 64, axis=1), 0.0)
-    )
+    args = (mid, from_low, from_high)
+    mid = call(fold_kernel, "fold", (struct(*mid.shape),), [], 1 << 16, args)[0]
     up, down = ring("gz")
     from_low = lax.ppermute(mid, "gz", up)
     from_high = from_low if len(up) == 2 else lax.ppermute(mid, "gz", down)
@@ -845,48 +875,53 @@
 ):
     feats = features[0, 0, 0]
     places = jnp.swapaxes(positions[0, 0], 0, 1)
-    *cells, own_pos, meta = make_cells(
+    cells0, cells12, own_pos, meta = make_cells(
         feats, places, neighbours[0, 0, 0].T, counts[0, 0], cell_atoms[0, 0]
     )
     hold = lax.optimization_barrier
-    block0, block1, block2 = (part.reshape(2, 2, 2, 8, part.shape[1]) for part in cells)
+    block0, block12 = (part.reshape(2, 2, 2, 8, part.shape[1]) for part in (cells0, cells12))
     block0 = grown(block0, "gz", 2)
-    block0, block1, block2, own_pos, meta = hold((block0, block1, block2, own_pos, meta))
-    block1, block2 = (grown(block, "gz", 2) for block in (block1, block2))
-    block0 = grown(block0, "gy", 1)
+    block0, block12, own_pos, meta = hold((block0, block12, own_pos, meta))
+    y_low, y_high = neighbours_of(block0, "gy", 1)
+    low_in, high_in = neighbours_of(block0, "gx", 0)
+    block12 = grown(block12, "gz", 2)
     oh_own, pre_own, unit_own, radt, rbft, mixt, home, *radial_own = own_stage(
         meta, own_pos, rbf_weight, radial_weight, mix_weight
     )
-    block0, block1, oh_own = hold((block0, block1, oh_own))
-    pieces0 = ghost_pieces(block0)
+    y_low, y_high, block12, oh_own = hold((y_low, y_high, block12, oh_own))
+    outer = jnp.concatenate([y_low, y_high], axis=1)
+    low_out, high_out = neighbours_of(outer, "gx", 0)
+    middle = jnp.concatenate([y_low, block0, y_high], axis=1)
+    pieces0 = tuple(flat_rows(p) for p in (low_in, low_out, middle, high_in, high_out))
+    block1, block2 = block12[..., : GROUP_COLS[1]], block12[..., GROUP_COLS[1] :]
     block1 = grown(block1, "gy", 1)
-    pieces0, block1, block2 = hold((pieces0, block1, block2))
+    (
+        new_0, oh_gh, d_gh, dt_gh, pre_gh, unit_gh, gs0, en_0, m0_own, m0_gh, gate_own, gate_gh,
+        nf0_own, nf0_gh, *radial_gh,
+    ) = start_stage(
+        pieces0, feats, own_pos, meta, rbf_weight, radial_weight, mix_weight, out_weight,
+        energy_weight[None], oh_own, radial_own[0],
+    )
+    block1, block2, gate_own = hold((block1, block2, gate_own))
     pieces1 = ghost_pieces(block1)
     block2 = grown(block2, "gy", 1)
-    (
-        new_a, oh_gh, d_gh, dt_gh, radial_gh3, radial_gh4, pre_gh, unit_gh, gs0, en_a, m0_own,
-        m0_gh, gate_own, gate_gh, nf0_own, nf0_gh, dot_own_a, dot_gh_a, gr1_own, gr1_gh, gr2_own,
-        gr2_gh,
-    ) = first_stage(
-        pieces0, feats, own_pos, meta, rbf_weight, radial_weight, mix_weight, out_weight,
-        energy_weight[None], norm_weight, oh_own, *radial_own[:3],
-    )
-    gate_own, block2 = hold((gate_own, block2))
-    pieces2 = ghost_pieces(block2)
     shared = (
         feats, meta, mix_weight, out_weight, norm_weight, oh_own, oh_gh, d_gh, dt_gh, gate_own,
-        gate_gh, radial_own[4], radial_gh4,
-    )
-    new_b, en_b, dot_own_b, dot_gh_b, gr3_own, gr3_gh, gr4_own_a, gr4_gh_a = second_stage(
-        pieces1, *shared, radial_own[3], radial_gh3
-    )
-    new, energy, src, low, mid, high, dot_own_c, gr4_own_b = third_stage(
-        pieces2, *shared, radt, rbft, mixt, gs0, en_a, en_b, new_a, new_b, pre_gh, unit_gh, m0_gh,
-        nf0_gh, dot_gh_a, dot_gh_b, gr1_gh, gr2_gh, gr3_gh, gr4_gh_a,
+        gate_gh,
+    )
+    radials = {degree: (radial_own[degree], radial_gh[degree - 1]) for degree in range(1, 5)}
+    new_a, en_a, dot_own_a, dot_gh_a, grads_a = pairs_stage(0, 2 * CH, pieces0, shared, radials)
+    en_a, block2 = hold((en_a, block2))
+    pieces2 = ghost_pieces(block2)
+    new_b, en_b, dot_own_b, dot_gh_b, grads_b = pairs_stage(1, 0, pieces1, shared, radials)
+    grads = list(grads_a.values()) + list(grads_b.values())
+    new, energy, src, low, mid, high, dot_own_c, gr_own_c = third_stage(
+        pieces2, *shared, *radials[4], radt, rbft, mixt, gs0, en_0, en_a, en_b, new_0, new_a,
+        new_b, pre_gh, unit_gh, m0_gh, nf0_gh, dot_gh_a, dot_gh_b, *[ghost for _, ghost in grads],
     )
     own = own_back_stage(
         oh_own, pre_own, unit_own, radt, rbft, mixt, gs0, src, m0_own, nf0_own, dot_own_a,
-        dot_own_b, dot_own_c, gr1_own, gr2_own, gr3_own, gr4_own_a, gr4_own_b,
+        dot_own_b, dot_own_c, *[own for own, _ in grads], gr_own_c,
     )
     forces = give_back(low, mid, high, own, home)
     return (

time: 82.7 us -> 75.7 us (0.915)
  waiting for transfers between devices: 21.7 us -> 12.1 us
  starting transfers between devices: 25.4 us -> 27.4 us
  Pallas kernels: 29.4 us -> 30.6 us
    ppermute x6 -> x7, waiting for transfers between devices: 8.55 us -> 1.73 us  [neighbours_of(): lax.ppermute(lax.slice_in_dim(block, length - 1, length, axis=dim), axis,...]
    ppermute x6 -> x7, starting transfers between devices: 9.27 us -> 12 us  [neighbours_of(): after = lax.ppermute(lax.slice_in_dim(block, 0, 1, axis=dim), axis, down)]
    ppermute x6 -> x7, waiting for transfers between devices: 4.23 us -> 2.11 us  [neighbours_of(): after = lax.ppermute(lax.slice_in_dim(block, 0, 1, axis=dim), axis, down)]
    pallas_call x7 -> x9, Pallas kernels: 29.4 us -> 30.6 us  [call(): pl.pallas_call(kernel, out_shape=out_shape, in_specs=specs or [pl.BlockSp...]
    ppermute x3 -> x2, waiting for transfers between devices: 4.2 us -> 3.5 us  [neighbours_of(): other = lax.ppermute(block, axis, up)]
    ppermute x3 -> x2, starting transfers between devices: 5.19 us -> 4.84 us  [neighbours_of(): other = lax.ppermute(block, axis, up)]
    ppermute x6 -> x7, starting transfers between devices: 4.69 us -> 4.37 us  [neighbours_of(): lax.ppermute(lax.slice_in_dim(block, length - 1, length, axis=dim), axis,...]
    unnamed x26 -> x27, local copies, waits for them, and re-layouts: 3.6 us -> 3.76 us
  transfers between devices with their start and end apart: 20 -> 21, of which waited for: 10 -> 7; matrix products, arithmetic and copies ran while one was open for 1% -> 1% of each run, Pallas kernels for 25% -> 28%
where the time goes in v5:
time: 75.7 us; the launch traced here: 75.3 us
  Pallas kernels  30.6 us (40%)
  starting transfers between devices  27.4 us (36%)
  waiting for transfers between devices  12.1 us (16%)
  local copies, waits for them, and re-layouts  4 us (5%)
  between operations  0.99 us (1%)
    pallas_call x9, Pallas kernels, call(): pl.pallas_call(kernel, out_shape=out_shape, in_specs=specs or [pl.BlockSp...  30.6 us
    ppermute x7, starting transfers between devices, neighbours_of(): after = lax.ppermute(lax.slice_in_dim(block, 0, 1, axis=dim), axis, down)  12 us
    ppermute x2, starting transfers between devices, neighbours_of(): other = lax.ppermute(block, axis, up)  4.84 us
    ppermute x7, starting transfers between devices, neighbours_of(): lax.ppermute(lax.slice_in_dim(block, length - 1, length, axis=dim), axis,...  4.37 us
    ppermute x1, starting transfers between devices, give_back(): from_high = lax.ppermute(mid, 'gy', down)  3.81 us
    unnamed x27, local copies, waits for them, and re-layouts  3.76 us
    ppermute x2, waiting for transfers between devices, neighbours_of(): other = lax.ppermute(block, axis, up)  3.5 us
    ppermute x1, waiting for transfers between devices, give_back(): from_low = lax.ppermute(mid, 'gz', up)  3.13 us
  transfers between devices with their start and end apart: 21, of which 7 were waited for; matrix products, arithmetic and copies ran while one was open for 1% of the time, Pallas kernels for 28%

profile of v5, /device:TPU:0, one launch (start us, length us, event | category | flops | bytes accessed | tf_op | source)
XLA Modules:
  0.0 75.3 jit_solution(16392540215069885978)
XLA Ops:
  1.3 1.0 %copy-done = bf16[1,1,1,64,3200]{4,3,2,1,0:T(8,128)(2,1)S(1)} copy-done((bf16[1,1,1,64,3200]{4,3,2,1,0:T(8,128)(2,1)S(1)}, bf16[1,1,1,64,3200]{4,3,2,1,0:T(8,128)(2,1)}, u32[]{:S(2)}) %copy-start) | copy-done | bytes 409624
  3.9 3.0 %collective-permute-start = (bf16[2,2,2,8,1024]{4,3,2,1,0:T(8,128)(2,1)S(1)}, bf16[2,2,2,8,1024]{4,3,2,1,0:T(8,128)(2,1)S(1)}, u32[]{:S(2)}, u32[]{:S(2)}) collective-permute-start(bf16[2,2,2,8,1024]{4,3,2,1,0:T(8,128)(2,1)S(1)} %bitcast.37), channel_id=1, source_target_pairs={{0,1},{1,0},{2,3},{3,2},{4,5},{5,4},{6,7},{7,6},{8,9},{9,8},{10,11... | collective-permute-start | bytes 393224 | tf_op jit(solution)/shard_map/ppermute | solution.py:794
  6.9 3.5 %collective-permute-done = bf16[2,2,2,8,1024]{4,3,2,1,0:T(8,128)(2,1)S(1)} collective-permute-done((bf16[2,2,2,8,1024]{4,3,2,1,0:T(8,128)(2,1)S(1)}, bf16[2,2,2,8,1024]{4,3,2,1,0:T(8,128)(2,1)S(1)}, u32[]{:S(2)}, u32[]{:S(2)}) %collective-permute-start) | collective-permute-done | bytes 131104 | tf_op jit(solution)/shard_map/ppermute | solution.py:794
  10.4 1.8 %collective-permute-start.4 = (bf16[2,2,2,8,2304]{4,3,2,1,0:T(8,128)(2,1)S(1)}, bf16[2,2,2,8,2304]{4,3,2,1,0:T(8,128)(2,1)S(1)}, u32[]{:S(2)}, u32[]{:S(2)}) collective-permute-start(bf16[2,2,2,8,2304]{4,3,2,1,0:T(8,128)(2,1)S(1)} %bitcast.35), channel_id=1, source_target_pairs={{0,1},{1,0},{2,3},{3,2},{4,5},{5,4},{6,7},{7,6},{8,9},{9,8},{10,11... | collective-permute-start | bytes 884744 | tf_op jit(solution)/shard_map/ppermute | solution.py:794
  12.3 1.6 %collective-permute-start.2 = (bf16[2,1,4,8,1024]{4,3,2,1,0:T(8,128)(2,1)S(1)}, bf16[2,1,4,8,1024]{4,3,2,1,0:T(8,128)(2,1)S(1)}, u32[]{:S(2)}, u32[]{:S(2)}) collective-permute-start(bf16[2,1,4,8,1024]{4,3,2,1,0:T(8,128)(2,1)S(1)} %get-tuple-element.173), channel_id=1, source_target_pairs={{0,2},{2,4},{4,6},{6,0},{1,3},{3,5},{5,7},{7,1},{8,10},{10,12},{12... | collective-permute-start | bytes 393224 | tf_op jit(solution)/shard_map/ppermute | solution.py:799
  13.9 2.3 %collective-permute-start.3 = (bf16[2,1,4,8,1024]{4,3,2,1,0:T(8,128)(2,1)S(1)}, bf16[2,1,4,8,1024]{4,3,2,1,0:T(8,128)(2,1)S(1)}, u32[]{:S(2)}, u32[]{:S(2)}) collective-permute-start(bf16[2,1,4,8,1024]{4,3,2,1,0:T(8,128)(2,1)S(1)} %get-tuple-element.172), channel_id=1, source_target_pairs={{2,0},{4,2},{6,4},{0,6},{3,1},{5,3},{7,5},{1,7},{10,8},{12,10},{14... | collective-permute-start | bytes 393224 | tf_op jit(solution)/shard_map/ppermute | solution.py:800
  16.7 2.9 %own_edges.1 = (bf16[1024,64]{1,0:T(8,128)(2,1)S(1)}, bf16[1024,128]{1,0:T(8,128)(2,1)S(1)}, f32[1024,128]{1,0:T(8,128)S(1)}, bf16[640,128]{1,0:T(8,128)(2,1)S(1...) custom-call(f32[64,128]{1,0:T(8,128)S(1)} %get-tuple-element.85.meta, ...), custom_call_target="tpu_custom_call" | custom-call | flops 2147483648 | bytes 3096576 | tf_op jit(solution)/shard_map/own_edges/pallas_call | solution.py:58
  21.3 1.2 %collective-permute-start.8 = (bf16[2,1,4,8,1280]{4,3,2,1,0:T(8,128)(2,1)S(1)}, bf16[2,1,4,8,1280]{4,3,2,1,0:T(8,128)(2,1)S(1)}, u32[]{:S(2)}, u32[]{:S(2)}) collective-permute-start(bf16[2,1,4,8,1280]{4,3,2,1,0:T(8,128)(2,1)S(1)} %get-tuple-element.160), channel_id=1, source_target_pairs={{0,2},{2,4},{4,6},{6,0},{1,3},{3,5},{5,7},{7,1},{8,10},{10,12},{12... | collective-permute-start | bytes 491528 | tf_op jit(solution)/shard_map/ppermute | solution.py:799
  22.5 2.7 %collective-permute-start.9 = (bf16[2,1,4,8,1280]{4,3,2,1,0:T(8,128)(2,1)S(1)}, bf16[2,1,4,8,1280]{4,3,2,1,0:T(8,128)(2,1)S(1)}, u32[]{:S(2)}, u32[]{:S(2)}) collective-permute-start(bf16[2,1,4,8,1280]{4,3,2,1,0:T(8,128)(2,1)S(1)} %get-tuple-element.161), channel_id=1, source_target_pairs={{2,0},{4,2},{6,4},{0,6},{3,1},{5,3},{7,5},{1,7},{10,8},{12,10},{14... | collective-permute-start | bytes 491528 | tf_op jit(solution)/shard_map/ppermute | solution.py:800
  25.3 1.6 %collective-permute-done.5 = bf16[1,2,4,8,1024]{4,3,2,1,0:T(8,128)(2,1)S(1)} collective-permute-done((bf16[1,2,4,8,1024]{4,3,2,1,0:T(8,128)(2,1)S(1)}, bf16[1,2,4,8,1024]{4,3,2,1,0:T(8,128)(2,1)S(1)}, u32[]{:S(2)}, u32[]{:S(2)}) %collective-permute-start.5) | collective-permute-done | bytes 131104 | tf_op jit(solution)/shard_map/ppermute | solution.py:799
  27.5 4.1 %ghost_start.1 = (bf16[64,128]{1,0:T(8,128)(2,1)S(1)}, bf16[1024,512]{1,0:T(8,128)(2,1)S(1)}, bf16[1024,64]{1,0:T(8,128)(2,1)S(1)}, bf16[64,1024]{1,0:T(8,128)(2...) custom-call(bf16[64,1024]{1,0:T(8,128)(2,1)S(1)} %bitcast.49, ...), custom_call_target="tpu_custom_call" | custom-call | flops 2147483648 | bytes 7324160 | tf_op jit(solution)/shard_map/ghost_start/pallas_call | solution.py:58
  31.7 1.4 %collective-permute-done.9 = bf16[2,1,4,8,1280]{4,3,2,1,0:T(8,128)(2,1)S(1)} collective-permute-done((bf16[2,1,4,8,1280]{4,3,2,1,0:T(8,128)(2,1)S(1)}, bf16[2,1,4,8,1280]{4,3,2,1,0:T(8,128)(2,1)S(1)}, u32[]{:S(2)}, u32[]{:S(2)}) %collective-permute-start.9) | collective-permute-done | bytes 163872 | tf_op jit(solution)/shard_map/ppermute | solution.py:800
  33.3 1.7 %collective-permute-start.15 = (bf16[1,4,4,8,1280]{4,3,2,1,0:T(8,128)(2,1)S(1)}, bf16[1,4,4,8,1280]{4,3,2,1,0:T(8,128)(2,1)S(1)}, u32[]{:S(2)}, u32[]{:S(2)}) collective-permute-start(bf16[1,4,4,8,1280]{4,3,2,1,0:T(8,128)(2,1)S(1)} %get-tuple-element.158), channel_id=1, source_target_pairs={{8,0},{16,8},{24,16},{0,24},{9,1},{17,9},{25,17},{1,25},{10,2},{18... | collective-permute-start | bytes 983048 | tf_op jit(solution)/shard_map/ppermute | solution.py:800
  35.0 0.9 %collective-permute-start.10 = (bf16[2,1,4,8,1024]{4,3,2,1,0:T(8,128)(2,1)S(1)}, bf16[2,1,4,8,1024]{4,3,2,1,0:T(8,128)(2,1)S(1)}, u32[]{:S(2)}, u32[]{:S(2)}) collective-permute-start(bf16[2,1,4,8,1024]{4,3,2,1,0:T(8,128)(2,1)S(1)} %get-tuple-element.166), channel_id=1, source_target_pairs={{0,2},{2,4},{4,6},{6,0},{1,3},{3,5},{5,7},{7,1},{8,10},{10,12},{12... | collective-permute-start | bytes 393224 | tf_op jit(solution)/shard_map/ppermute | solution.py:799
  35.9 3.0 %collective-permute-start.11 = (bf16[2,1,4,8,1024]{4,3,2,1,0:T(8,128)(2,1)S(1)}, bf16[2,1,4,8,1024]{4,3,2,1,0:T(8,128)(2,1)S(1)}, u32[]{:S(2)}, u32[]{:S(2)}) collective-permute-start(bf16[2,1,4,8,1024]{4,3,2,1,0:T(8,128)(2,1)S(1)} %get-tuple-element.167), channel_id=1, source_target_pairs={{2,0},{4,2},{6,4},{0,6},{3,1},{5,3},{7,5},{1,7},{10,8},{12,10},{14... | collective-permute-start | bytes 393224 | tf_op jit(solution)/shard_map/ppermute | solution.py:800
  39.6 4.8 %pairs_a.1 = (bf16[64,768]{1,0:T(8,128)(2,1)S(1)}, f32[64,128]{1,0:T(8,128)S(1)}, bf16[1024,128]{1,0:T(8,128)(2,1)S(1)}, bf16[1024,128]{1,0:T(8,128)(2,1)S(1)}, ...) custom-call(bf16[64,1024]{1,0:T(8,128)(2,1)S(1)} %bitcast.50, ...), custom_call_target="tpu_custom_call" | custom-call | flops 8589934592 | bytes 6539264 | tf_op jit(solution)/shard_map/pairs_a/pallas_call | solution.py:58
  44.6 1.7 %collective-permute-start.13 = (bf16[1,4,4,8,1024]{4,3,2,1,0:T(8,128)(2,1)S(1)}, bf16[1,4,4,8,1024]{4,3,2,1,0:T(8,128)(2,1)S(1)}, u32[]{:S(2)}, u32[]{:S(2)}) collective-permute-start(bf16[1,4,4,8,1024]{4,3,2,1,0:T(8,128)(2,1)S(1)} %get-tuple-element.162), channel_id=1, source_target_pairs={{8,0},{16,8},{24,16},{0,24},{9,1},{17,9},{25,17},{1,25},{10,2},{18... | collective-permute-start | bytes 786440 | tf_op jit(solution)/shard_map/ppermute | solution.py:800
  46.3 6.3 %pairs_b.1 = (bf16[64,1280]{1,0:T(8,128)(2,1)S(1)}, f32[64,128]{1,0:T(8,128)S(1)}, bf16[1024,128]{1,0:T(8,128)(2,1)S(1)}, bf16[1024,128]{1,0:T(8,128)(2,1)S(1)},...) custom-call(bf16[128,1280]{1,0:T(8,128)(2,1)S(1)} %bitcast.43, ...), custom_call_target="tpu_custom_call" | custom-call | flops 8589934592 | bytes 7915520 | tf_op jit(solution)/shard_map/pairs_b/pallas_call | solution.py:58
  52.7 8.0 %third_group.1 = (bf16[64,3200]{1,0:T(8,128)(2,1)}, f32[1,64]{1,0:T(1,128)}, f32[64,128]{1,0:T(8,128)S(1)}, f32[8,128]{1,0:T(8,128)S(1)}, f32[8,256]{1,0:T(8,128...) custom-call(bf16[128,1024]{1,0:T(8,128)(2,1)S(1)} %bitcast.45, ...), custom_call_target="tpu_custom_call" | custom-call | flops 8589934592 | bytes 9177344 | tf_op jit(solution)/shard_map/third_group/pallas_call | solution.py:58
  61.0 1.5 %collective-permute-start.17 = (f32[8,128]{1,0:T(8,128)S(1)}, f32[8,128]{1,0:T(8,128)S(1)}, u32[]{:S(2)}, u32[]{:S(2)}) collective-permute-start(f32[8,128]{1,0:T(8,128)S(1)} %get-tuple-element.136), channel_id=1, source_target_pairs={{8,0},{16,8},{24,16},{0,24},{9,1},{17,9},{25,17},{1,25},{10,2},{18... | collective-permute-start | bytes 12296 | tf_op jit(solution)/shard_map/ppermute | solution.py:847
  62.5 2.8 %own_back.1.own_ref = f32[8,64]{1,0:T(8,128)S(1)} custom-call(bf16[1024,64]{1,0:T(8,128)(2,1)S(1)} %get-tuple-element.90.oh_own.refs_10_.refs_8_, bf16[1024,128]{1,0:T(8,128)(2,1)S(1)} %get-tuple-element.137.pre_own, f32[1024,128]{1,0:T(8,128)S(1)} %get-tuple-element.138.unit_own, bf16[640,128]{1,0:T(8,128)(2,1)S(1)} %get-tuple-element.108.radt_ref, ...), custom_call_target="tpu_custom_call" | custom-call | flops 2147483648 | bytes 4196352 | tf_op jit(solution)/shard_map/own_back/pallas_call | solution.py:58
  65.4 3.8 %collective-permute-start.19 = (f32[8,256]{1,0:T(8,128)S(1)}, f32[8,256]{1,0:T(8,128)S(1)}, u32[]{:S(2)}, u32[]{:S(2)}) collective-permute-start(f32[8,256]{1,0:T(8,128)S(1)} %maximum_add_fusion.mid_ref), channel_id=1, source_target_pairs={{2,0},{4,2},{6,4},{0,6},{3,1},{5,3},{7,5},{1,7},{10,8},{12,10},{14... | collective-permute-start | bytes 24584 | tf_op jit(solution)/shard_map/ppermute | solution.py:852
  69.2 1.6 %collective-permute-done.18.low_ref = f32[8,256]{1,0:T(8,128)S(1)} collective-permute-done((f32[8,256]{1,0:T(8,128)S(1)}, f32[8,256]{1,0:T(8,128)S(1)}, u32[]{:S(2)}, u32[]{:S(2)}) %collective-permute-start.18) | collective-permute-done | bytes 8224 | tf_op jit(solution)/shard_map/ppermute | solution.py:851
  71.4 3.1 %collective-permute-done.20.low_ref.high_ref = f32[8,256]{1,0:T(8,128)S(1)} collective-permute-done((f32[8,256]{1,0:T(8,128)S(1)}, f32[8,256]{1,0:T(8,128)S(1)}, u32[]{:S(2)}, u32[]{:S(2)}) %collective-permute-start.20) | collective-permute-done | bytes 8224 | tf_op jit(solution)/shard_map/ppermute | solution.py:856
  (73 shorter events, 7.9 us)
Async XLA Ops:
  3.9 6.5 %collective-permute-start = (bf16[2,2,2,8,1024]{4,3,2,1,0:T(8,128)(2,1)S(1)}, bf16[2,2,2,8,1024]{4,3,2,1,0:T(8,128)(2,1)S(1)}, u32[]{:S(2)}, u32[]{:S(2)}) collective-permute-start(bf16[2,2,2,8,1024]{4,3,2,1,0:T(8,128)(2,1)S(1)} %bitcast.37), channel_id=1, source_target_pairs={{0,1},{1,0},{2,3},{3,2},{4,5},{5,4},{6,7},{7,6},{8,9},{9,8},{10,11... | collective-permute-start | bytes 393224 | tf_op jit(solution)/shard_map/ppermute | solution.py:794
  10.4 9.2 %collective-permute-start.4 = (bf16[2,2,2,8,2304]{4,3,2,1,0:T(8,128)(2,1)S(1)}, bf16[2,2,2,8,2304]{4,3,2,1,0:T(8,128)(2,1)S(1)}, u32[]{:S(2)}, u32[]{:S(2)}) collective-permute-start(bf16[2,2,2,8,2304]{4,3,2,1,0:T(8,128)(2,1)S(1)} %bitcast.35), channel_id=1, source_target_pairs={{0,1},{1,0},{2,3},{3,2},{4,5},{5,4},{6,7},{7,6},{8,9},{9,8},{10,11... | collective-permute-start | bytes 884744 | tf_op jit(solution)/shard_map/ppermute | solution.py:794
  12.3 7.6 %collective-permute-start.2 = (bf16[2,1,4,8,1024]{4,3,2,1,0:T(8,128)(2,1)S(1)}, bf16[2,1,4,8,1024]{4,3,2,1,0:T(8,128)(2,1)S(1)}, u32[]{:S(2)}, u32[]{:S(2)}) collective-permute-start(bf16[2,1,4,8,1024]{4,3,2,1,0:T(8,128)(2,1)S(1)} %get-tuple-element.173), channel_id=1, source_target_pairs={{0,2},{2,4},{4,6},{6,0},{1,3},{3,5},{5,7},{7,1},{8,10},{10,12},{12... | collective-permute-start | bytes 393224 | tf_op jit(solution)/shard_map/ppermute | solution.py:799
  13.9 6.6 %collective-permute-start.3 = (bf16[2,1,4,8,1024]{4,3,2,1,0:T(8,128)(2,1)S(1)}, bf16[2,1,4,8,1024]{4,3,2,1,0:T(8,128)(2,1)S(1)}, u32[]{:S(2)}, u32[]{:S(2)}) collective-permute-start(bf16[2,1,4,8,1024]{4,3,2,1,0:T(8,128)(2,1)S(1)} %get-tuple-element.172), channel_id=1, source_target_pairs={{2,0},{4,2},{6,4},{0,6},{3,1},{5,3},{7,5},{1,7},{10,8},{12,10},{14... | collective-permute-start | bytes 393224 | tf_op jit(solution)/shard_map/ppermute | solution.py:800
  16.2 6.3 %collective-permute-start.6 = (bf16[1,2,4,8,1024]{4,3,2,1,0:T(8,128)(2,1)S(1)}, bf16[1,2,4,8,1024]{4,3,2,1,0:T(8,128)(2,1)S(1)}, u32[]{:S(2)}, u32[]{:S(2)}) collective-permute-start(bf16[1,2,4,8,1024]{4,3,2,1,0:T(8,128)(2,1)S(1)} %get-tuple-element.170), channel_id=1, source_target_pairs={{8,0},{16,8},{24,16},{0,24},{9,1},{17,9},{25,17},{1,25},{10,2},{18... | collective-permute-start | bytes 393224 | tf_op jit(solution)/shard_map/ppermute | solution.py:800
  16.2 9.1 %collective-permute-start.1 = (bf16[1,2,4,8,1024]{4,3,2,1,0:T(8,128)(2,1)S(1)}, bf16[1,2,4,8,1024]{4,3,2,1,0:T(8,128)(2,1)S(1)}, u32[]{:S(2)}, u32[]{:S(2)}) collective-permute-start(bf16[1,2,4,8,1024]{4,3,2,1,0:T(8,128)(2,1)S(1)} %get-tuple-element.171), channel_id=1, source_target_pairs={{0,8},{8,16},{16,24},{24,0},{1,9},{9,17},{17,25},{25,1},{2,10},{10... | collective-permute-start | bytes 393224 | tf_op jit(solution)/shard_map/ppermute | solution.py:799
  20.6 4.7 %collective-permute-start.7 = (bf16[1,2,4,8,1024]{4,3,2,1,0:T(8,128)(2,1)S(1)}, bf16[1,2,4,8,1024]{4,3,2,1,0:T(8,128)(2,1)S(1)}, u32[]{:S(2)}, u32[]{:S(2)}) collective-permute-start(bf16[1,2,4,8,1024]{4,3,2,1,0:T(8,128)(2,1)S(1)} %get-tuple-element.168), channel_id=1, source_target_pairs={{8,0},{16,8},{24,16},{0,24},{9,1},{17,9},{25,17},{1,25},{10,2},{18... | collective-permute-start | bytes 393224 | tf_op jit(solution)/shard_map/ppermute | solution.py:800
  21.1 5.7 %collective-permute-start.5 = (bf16[1,2,4,8,1024]{4,3,2,1,0:T(8,128)(2,1)S(1)}, bf16[1,2,4,8,1024]{4,3,2,1,0:T(8,128)(2,1)S(1)}, u32[]{:S(2)}, u32[]{:S(2)}) collective-permute-start(bf16[1,2,4,8,1024]{4,3,2,1,0:T(8,128)(2,1)S(1)} %get-tuple-element.169), channel_id=1, source_target_pairs={{0,8},{8,16},{16,24},{24,0},{1,9},{9,17},{17,25},{25,1},{2,10},{10... | collective-permute-start | bytes 393224 | tf_op jit(solution)/shard_map/ppermute | solution.py:799
  21.2 5.6 %copy-start.1 = (bf16[1,1,1,64,3200]{4,3,2,1,0:T(8,128)(2,1)S(1)}, bf16[1,1,1,64,3200]{4,3,2,1,0:T(8,128)(2,1)}, u32[]{:S(2)}) copy-start(bf16[1,1,1,64,3200]{4,3,2,1,0:T(8,128)(2,1)} %param.11) | copy-start | bytes 1228804
  21.3 5.6 %copy-start.8 = (bf16[5,128,128]{2,1,0:T(8,128)(2,1)S(1)}, bf16[5,128,128]{2,1,0:T(8,128)(2,1)}, u32[]{:S(2)}) copy-start(bf16[5,128,128]{2,1,0:T(8,128)(2,1)} %out_ref.3) | copy-start | bytes 491524
  21.3 10.4 %collective-permute-start.8 = (bf16[2,1,4,8,1280]{4,3,2,1,0:T(8,128)(2,1)S(1)}, bf16[2,1,4,8,1280]{4,3,2,1,0:T(8,128)(2,1)S(1)}, u32[]{:S(2)}, u32[]{:S(2)}) collective-permute-start(bf16[2,1,4,8,1280]{4,3,2,1,0:T(8,128)(2,1)S(1)} %get-tuple-element.160), channel_id=1, source_target_pairs={{0,2},{2,4},{4,6},{6,0},{1,3},{3,5},{5,7},{7,1},{8,10},{10,12},{12... | collective-permute-start | bytes 491528 | tf_op jit(solution)/shard_map/ppermute | solution.py:799
  22.5 10.5 %collective-permute-start.9 = (bf16[2,1,4,8,1280]{4,3,2,1,0:T(8,128)(2,1)S(1)}, bf16[2,1,4,8,1280]{4,3,2,1,0:T(8,128)(2,1)S(1)}, u32[]{:S(2)}, u32[]{:S(2)}) collective-permute-start(bf16[2,1,4,8,1280]{4,3,2,1,0:T(8,128)(2,1)S(1)} %get-tuple-element.161), channel_id=1, source_target_pairs={{2,0},{4,2},{6,4},{0,6},{3,1},{5,3},{7,5},{1,7},{10,8},{12,10},{14... | collective-permute-start | bytes 491528 | tf_op jit(solution)/shard_map/ppermute | solution.py:800
  27.5 5.6 %slice-start = ((bf16[2,2,4,8,2304]{4,3,2,1,0:T(8,128)(2,1)}), bf16[2,2,4,8,1280]{4,3,2,1,0:T(8,128)(2,1)S(1)}, s32[]{:S(2)}) async-start(bf16[2,2,4,8,2304]{4,3,2,1,0:T(8,128)(2,1)} %copy-done.12), calls=%async_computation | async-start | bytes 655360 | tf_op jit(solution)/shard_map/slice | solution.py:896
  33.2 13.1 %collective-permute-start.14 = (bf16[1,4,4,8,1280]{4,3,2,1,0:T(8,128)(2,1)S(1)}, bf16[1,4,4,8,1280]{4,3,2,1,0:T(8,128)(2,1)S(1)}, u32[]{:S(2)}, u32[]{:S(2)}) collective-permute-start(bf16[1,4,4,8,1280]{4,3,2,1,0:T(8,128)(2,1)S(1)} %get-tuple-element.159), channel_id=1, source_target_pairs={{0,8},{8,16},{16,24},{24,0},{1,9},{9,17},{17,25},{25,1},{2,10},{10... | collective-permute-start | bytes 983048 | tf_op jit(solution)/shard_map/ppermute | solution.py:799
  33.3 13.0 %collective-permute-start.15 = (bf16[1,4,4,8,1280]{4,3,2,1,0:T(8,128)(2,1)S(1)}, bf16[1,4,4,8,1280]{4,3,2,1,0:T(8,128)(2,1)S(1)}, u32[]{:S(2)}, u32[]{:S(2)}) collective-permute-start(bf16[1,4,4,8,1280]{4,3,2,1,0:T(8,128)(2,1)S(1)} %get-tuple-element.158), channel_id=1, source_target_pairs={{8,0},{16,8},{24,16},{0,24},{9,1},{17,9},{25,17},{1,25},{10,2},{18... | collective-permute-start | bytes 983048 | tf_op jit(solution)/shard_map/ppermute | solution.py:800
  35.0 9.3 %collective-permute-start.10 = (bf16[2,1,4,8,1024]{4,3,2,1,0:T(8,128)(2,1)S(1)}, bf16[2,1,4,8,1024]{4,3,2,1,0:T(8,128)(2,1)S(1)}, u32[]{:S(2)}, u32[]{:S(2)}) collective-permute-start(bf16[2,1,4,8,1024]{4,3,2,1,0:T(8,128)(2,1)S(1)} %get-tuple-element.166), channel_id=1, source_target_pairs={{0,2},{2,4},{4,6},{6,0},{1,3},{3,5},{5,7},{7,1},{8,10},{10,12},{12... | collective-permute-start | bytes 393224 | tf_op jit(solution)/shard_map/ppermute | solution.py:799
  35.9 8.5 %collective-permute-start.11 = (bf16[2,1,4,8,1024]{4,3,2,1,0:T(8,128)(2,1)S(1)}, bf16[2,1,4,8,1024]{4,3,2,1,0:T(8,128)(2,1)S(1)}, u32[]{:S(2)}, u32[]{:S(2)}) collective-permute-start(bf16[2,1,4,8,1024]{4,3,2,1,0:T(8,128)(2,1)S(1)} %get-tuple-element.167), channel_id=1, source_target_pairs={{2,0},{4,2},{6,4},{0,6},{3,1},{5,3},{7,5},{1,7},{10,8},{12,10},{14... | collective-permute-start | bytes 393224 | tf_op jit(solution)/shard_map/ppermute | solution.py:800
  44.5 8.2 %collective-permute-start.12 = (bf16[1,4,4,8,1024]{4,3,2,1,0:T(8,128)(2,1)S(1)}, bf16[1,4,4,8,1024]{4,3,2,1,0:T(8,128)(2,1)S(1)}, u32[]{:S(2)}, u32[]{:S(2)}) collective-permute-start(bf16[1,4,4,8,1024]{4,3,2,1,0:T(8,128)(2,1)S(1)} %get-tuple-element.163), channel_id=1, source_target_pairs={{0,8},{8,16},{16,24},{24,0},{1,9},{9,17},{17,25},{25,1},{2,10},{10... | collective-permute-start | bytes 786440 | tf_op jit(solution)/shard_map/ppermute | solution.py:799
  44.6 8.1 %collective-permute-start.13 = (bf16[1,4,4,8,1024]{4,3,2,1,0:T(8,128)(2,1)S(1)}, bf16[1,4,4,8,1024]{4,3,2,1,0:T(8,128)(2,1)S(1)}, u32[]{:S(2)}, u32[]{:S(2)}) collective-permute-start(bf16[1,4,4,8,1024]{4,3,2,1,0:T(8,128)(2,1)S(1)} %get-tuple-element.162), channel_id=1, source_target_pairs={{8,0},{16,8},{24,16},{0,24},{9,1},{17,9},{25,17},{1,25},{10,2},{18... | collective-permute-start | bytes 786440 | tf_op jit(solution)/shard_map/ppermute | solution.py:800
  60.7 4.6 %collective-permute-start.16 = (f32[8,128]{1,0:T(8,128)S(1)}, f32[8,128]{1,0:T(8,128)S(1)}, u32[]{:S(2)}, u32[]{:S(2)}) collective-permute-start(f32[8,128]{1,0:T(8,128)S(1)} %get-tuple-element.135), channel_id=1, source_target_pairs={{0,8},{8,16},{16,24},{24,0},{1,9},{9,17},{17,25},{25,1},{2,10},{10... | collective-permute-start | bytes 12296 | tf_op jit(solution)/shard_map/ppermute | solution.py:846
  61.0 4.3 %collective-permute-start.17 = (f32[8,128]{1,0:T(8,128)S(1)}, f32[8,128]{1,0:T(8,128)S(1)}, u32[]{:S(2)}, u32[]{:S(2)}) collective-permute-start(f32[8,128]{1,0:T(8,128)S(1)} %get-tuple-element.136), channel_id=1, source_target_pairs={{8,0},{16,8},{24,16},{0,24},{9,1},{17,9},{25,17},{1,25},{10,2},{18... | collective-permute-start | bytes 12296 | tf_op jit(solution)/shard_map/ppermute | solution.py:847
  65.3 5.5 %collective-permute-start.18 = (f32[8,256]{1,0:T(8,128)S(1)}, f32[8,256]{1,0:T(8,128)S(1)}, u32[]{:S(2)}, u32[]{:S(2)}) collective-permute-start(f32[8,256]{1,0:T(8,128)S(1)} %maximum_add_fusion.mid_ref), channel_id=1, source_target_pairs={{0,2},{2,4},{4,6},{6,0},{1,3},{3,5},{5,7},{7,1},{8,10},{10,12},{12... | collective-permute-start | bytes 24584 | tf_op jit(solution)/shard_map/ppermute | solution.py:851
  65.4 5.4 %collective-permute-start.19 = (f32[8,256]{1,0:T(8,128)S(1)}, f32[8,256]{1,0:T(8,128)S(1)}, u32[]{:S(2)}, u32[]{:S(2)}) collective-permute-start(f32[8,256]{1,0:T(8,128)S(1)} %maximum_add_fusion.mid_ref), channel_id=1, source_target_pairs={{2,0},{4,2},{6,4},{0,6},{3,1},{5,3},{7,5},{1,7},{10,8},{12,10},{14... | collective-permute-start | bytes 24584 | tf_op jit(solution)/shard_map/ppermute | solution.py:852
  70.9 3.7 %collective-permute-start.20 = (f32[8,256]{1,0:T(8,128)S(1)}, f32[8,256]{1,0:T(8,128)S(1)}, u32[]{:S(2)}, u32[]{:S(2)}) collective-permute-start(f32[8,256]{1,0:T(8,128)S(1)} %fold.1.mid_ref), channel_id=1, source_target_pairs={{0,1},{1,0},{2,3},{3,2},{4,5},{5,4},{6,7},{7,6},{8,9},{9,8},{10,11... | collective-permute-start | bytes 24584 | tf_op jit(solution)/shard_map/ppermute | solution.py:856
  (11 other events, 19.9 us)

commit v6 on v5

--- a/solution.py
+++ b/solution.py
@@ -69,7 +69,7 @@
 
 def cells_kernel(
     feat_hbm, pos_hbm, near_hbm, counts_hbm, order_hbm,
-    first_ref, rest_ref, own_pos_ref, meta_ref,
+    first_ref, own_pos_ref, meta_ref, pick_ref,
     feat_ref, pos_ref, near_ref, counts_ref, order_ref, rows_ref, pos_rows, sems,
 ):
     args = (pos_hbm, near_hbm, counts_hbm, order_hbm, feat_hbm)
@@ -103,27 +103,37 @@
     same = (iota((atoms, atoms), 0) == iota((atoms, atoms), 1)).astype(F32).astype(BF16)
     own_pos_ref[...] = mm_nt(same, pieces).astype(BF16)
     first_ref[:, CH : 2 * CH] = mm_nt(pick, pieces).astype(BF16)
+    pick_ref[...] = pick
     copies[4].wait()
     first_ref[:, 0:CH] = mm(pick, feat_ref[:, 0:CH]).astype(BF16)
     cut = pair_cols(GROUPS[1][0]).start
     first_ref[:, 2 * CH :] = mm(pick, feat_ref[:, CH:cut]).astype(BF16)
-    rest_ref[...] = mm(pick, feat_ref[:, cut:]).astype(BF16)
+
+
+def rest_kernel(feat_ref, pick_ref, rest_ref):
+    cut = pair_cols(GROUPS[1][0]).start
+    rest_ref[...] = mm(pick_ref[...], feat_ref[:, cut:]).astype(BF16)
 
 
 def make_cells(feats, places, near, counts, order):
     atoms = feats.shape[0]
     out_shape = (
         struct(atoms, 2 * CH + GROUP_COLS[0], dtype=BF16),
-        struct(atoms, sum(GROUP_COLS[1:]), dtype=BF16),
         struct(atoms, CH, dtype=BF16),
         struct(atoms, CH),
+        struct(atoms, atoms, dtype=BF16),
     )
     args = (feats, places, near, counts, order)
     scratch = [pltpu.VMEM(arg.shape, arg.dtype) for arg in args]
     scratch += [pltpu.VMEM((CH, atoms), F32), pltpu.VMEM((CH, atoms), F32)]
     scratch += [pltpu.SemaphoreType.DMA((5,))]
-    specs = [pl.BlockSpec(memory_space=pltpu.HBM)] * 5
-    return call(cells_kernel, "cells", out_shape, scratch, 1 << 26, args, specs)
+    specs = [pl.BlockSpec(memory_space=pl.ANY)] * 5
+    first, own_pos, meta, pick = call(
+        cells_kernel, "cells", out_shape, scratch, 1 << 26, args, specs
+    )
+    out_shape = (struct(atoms, sum(GROUP_COLS[1:]), dtype=BF16),)
+    rest = call(rest_kernel, "cells_rest", out_shape, [], 1 << 26, (feats, pick))[0]
+    return first, rest, own_pos, meta
 
 
 def spacing_of(atoms, nbasis):
@@ -196,28 +206,6 @@
     return pl.ds(base, size), pl.ds(pl.multiple_of(first + base, size), size)
 
 
-class Halves:
-    def __init__(self, own, ghost):
-        self.own, self.ghost = own, ghost
-        self.dtype = own.dtype
-
-    def place(self, rows):
-        first = OWN_STEPS * STEP
-        if not isinstance(rows.start, int):
-            return self.ghost, pl.ds(pl.multiple_of(rows.start - first, rows.size), rows.size)
-        if rows.start < first:
-            return self.own, rows
-        return self.ghost, pl.ds(rows.start - first, rows.size)
-
-    def __getitem__(self, at):
-        ref, rows = self.place(at[0])
-        return ref[rows, at[1]]
-
-    def __setitem__(self, at, value):
-        ref, rows = self.place(at[0])
-        ref[rows, at[1]] = value
-
-
 def over_ghost_steps(steps, body, size=STEP):
     static = GH_STEPS * STEP // size
     for step in range(static):
@@ -230,23 +218,24 @@
     lax.fori_loop(static, (steps * STEP + (size - 1)) // size, again, 0)
 
 
-def block_diagonal(kinds, mix_ref, out_ref, wm, wmt, wo, wot):
+def block_diagonal(kinds, source, straight=None, across=None):
     zero = jnp.zeros((CH, CH), BF16)
+    targets = [ref for ref in (straight, across) if ref is not None]
     for kind, both in enumerate(kinds):
-        for ref in (wm, wmt, wo, wot):
+        for ref in targets:
             ref[kind, 0:CH, CH:] = zero
             ref[kind, CH:, 0:CH] = zero
     for degree in sorted({d for both in kinds for d in both}):
-        mix, out = mix_ref[degree], out_ref[degree]
-        mix_t, out_t = flip(mix), flip(out)
+        weight = source[degree]
+        flipped = flip(weight) if across is not None else None
         for kind, both in enumerate(kinds):
             for side in range(2):
                 if both[side] == degree:
                     part = slice(side * CH, side * CH + CH)
-                    wm[kind, part, part] = mix
-                    wmt[kind, part, part] = mix_t
-                    wo[kind, part, part] = out
-                    wot[kind, part, part] = out_t
+                    if straight is not None:
+                        straight[kind, part, part] = weight
+                    if across is not None:
+                        across[kind, part, part] = flipped
 
 
 def fetch(pieces, cols, table, sems):
@@ -271,73 +260,98 @@
     return copies
 
 
-def run_pairs(
-    pairs, kinds, own_ref, table, new_ref, new_base, oh_own, oh_gh, d_gh, dt_gh,
-    gate_ref, radial_of, nw_ref, steps, wm, wmt, wo, wot, nf_s, mx_s, acc_s, gs_s, dot_ref,
-    grad_refs, en_ref, size=STEP,
+def infos_of(group):
+    infos = []
+    for index, pair in enumerate(range(*GROUPS[group])):
+        degrees = PAIR_DEGREES[pair]
+        cols = slice(index * 2 * CH, (index + 1) * 2 * CH)
+        infos.append((cols, degrees, KINDS[group].index(degrees)))
+    return infos
+
+
+def group_cols(group):
+    begin, end = GROUPS[group]
+    return slice(pair_cols(begin).start, pair_cols(end - 1).stop)
+
+
+def twice(values):
+    return jnp.concatenate([values, values], axis=1)
+
+
+def forward(group, rows, onehot, feats, radials, gate_ref, wm, nf_ref, mx_ref):
+    near = mm(onehot, feats).astype(BF16)
+    nf_ref[rows, :] = near
+    gate = twice(gate_ref[rows, :])
+    messages = []
+    for cols, degrees, kind in infos_of(group):
+        radial = jnp.concatenate([radials[d][rows, :] for d in degrees], axis=1)
+        mixed = mm(near[:, cols] * radial, wm[kind]).astype(BF16)
+        mx_ref[rows, cols] = mixed
+        messages.append(mixed * gate)
+    return jnp.concatenate(messages, axis=1)
+
+
+def backward(group, rows, grad, gate_ref, wmt, nf_ref, mx_ref, dot_ref, grad_refs):
+    parts = {}
+    dots = None
+    gate = twice(gate_ref[rows, :])
+    for cols, degrees, kind in infos_of(group):
+        product = grad[:, cols] * mx_ref[rows, cols]
+        dot = (product[:, 0:CH] + product[:, CH:]).astype(F32)
+        dots = dot if dots is None else dots + dot
+        weighted = mm(grad[:, cols] * gate, wmt[kind]) * nf_ref[rows, cols].astype(F32)
+        for side in range(2):
+            part = weighted[:, side * CH : (side + 1) * CH]
+            degree = degrees[side]
+            parts[degree] = parts[degree] + part if degree in parts else part
+    dot_ref[rows, :] = dots.astype(dot_ref.dtype)
+    for degree, part in parts.items():
+        grad_refs[degree][rows, :] = part.astype(grad_refs[degree].dtype)
+
+
+def own_forward(group, own_ref, oh_own, radials, gate_ref, wm, nf_ref, mx_ref, acc_ref):
+    spread = own_spread(own_ref.shape[0])
+    feats = own_ref[:, group_cols(group)]
+    summed = None
+    for step in range(OWN_STEPS):
+        rows = own_rows(step)
+        message = forward(
+            group, rows, oh_own[rows, :], feats, radials, gate_ref, wm, nf_ref, mx_ref
+        )
+        part = mm(spread, message)
+        summed = part if summed is None else summed + part
+    acc_ref[...] = summed
+
+
+def own_backward(group, gs_ref, gate_ref, wmt, nf_ref, mx_ref, dot_ref, grad_refs):
+    grad = tiled(gs_ref[...])
+    for step in range(OWN_STEPS):
+        backward(
+            group, own_rows(step), grad, gate_ref, wmt, nf_ref, mx_ref, dot_ref, grad_refs
+        )
+
+
+def ghost_pairs(
+    group, own_ref, table, new_ref, new_base, oh_gh, d_gh, dt_gh, gate_ref, radials, nw_ref,
+    steps, wm, wmt, wo, wot, nf_s, mx_s, acc_in, acc_s, gs_ref, dot_ref, grad_refs, en_ref,
 ):
-    atoms = own_ref.shape[0]
     norm = 1.0 / math.sqrt(SLOTS)
-    spread_own = own_spread(atoms, size)
-    own_steps = OWN_STEPS * STEP // size
-    begin, end = pair_cols(pairs[0]).start, pair_cols(pairs[-1]).stop
-    own_cols = slice(begin, end)
-    infos = []
-    for index, pair in enumerate(pairs):
-        degrees = PAIR_DEGREES[pair]
-        infos.append((slice(index * 2 * CH, (index + 1) * 2 * CH), degrees, kinds.index(degrees)))
-
-    def gate_of(rows):
-        gate = gate_ref[rows, :]
-        return jnp.concatenate([gate, gate], axis=1)
-
-    def forward(rows, onehot, feats):
-        near = mm(onehot, feats).astype(BF16)
-        nf_s[rows, :] = near
-        gate = gate_of(rows)
-        messages = []
-        for cols, degrees, kind in infos:
-            radial = jnp.concatenate([radial_of(d, rows) for d in degrees], axis=1)
-            mixed = mm(near[:, cols] * radial, wm[kind]).astype(BF16)
-            mx_s[rows, cols] = mixed
-            messages.append(mixed * gate)
-        return jnp.concatenate(messages, axis=1)
-
-    def backward(rows, grad):
-        parts = {}
-        dots = None
-        gate = gate_of(rows)
-        for cols, degrees, kind in infos:
-            product = grad[:, cols] * mx_s[rows, cols]
-            dot = (product[:, 0:CH] + product[:, CH:]).astype(F32)
-            dots = dot if dots is None else dots + dot
-            weighted = mm(grad[:, cols] * gate, wmt[kind]) * nf_s[rows, cols].astype(F32)
-            for side in range(2):
-                part = weighted[:, side * CH : (side + 1) * CH]
-                degree = degrees[side]
-                parts[degree] = parts[degree] + part if degree in parts else part
-        dot_ref[rows, :] = dots.astype(dot_ref.dtype)
-        for degree, part in parts.items():
-            grad_refs[degree][rows, :] = part.astype(grad_refs[degree].dtype)
-
-    own = own_ref[:, own_cols]
-    summed = None
-    for step in range(own_steps):
-        rows = own_rows(step, size)
-        part = mm(spread_own, forward(rows, oh_own[rows, :], own))
-        summed = part if summed is None else summed + part
-    acc_s[...] = summed
+    acc_s[...] = acc_in[...]
 
     def ghost_forward(step):
-        here, rows = ghost_rows(step, size)
-        message = forward(rows, oh_gh[here, :], table[...])
+        here, _ = ghost_rows(step)
+        message = forward(
+            group, here, oh_gh[here, :], table[...], radials, gate_ref, wm, nf_s, mx_s
+        )
         acc_s[...] += mm(dt_gh[:, here], message)
 
-    over_ghost_steps(steps, ghost_forward, size)
-
-    for cols, degrees, kind in infos:
+    over_ghost_steps(steps, ghost_forward)
+
+    begin = group_cols(group).start
+    for cols, degrees, kind in infos_of(group):
         summed_low = (acc_s[:, cols] * norm).astype(BF16)
-        updated = own[:, cols].astype(F32) + mm(summed_low, wo[kind])
+        own = own_ref[:, begin + cols.start : begin + cols.stop]
+        updated = own.astype(F32) + mm(summed_low, wo[kind])
         at = begin - new_base + cols.start
         new_ref[:, at : at + 2 * CH] = updated.astype(BF16)
         weight = jnp.concatenate(
@@ -346,29 +360,25 @@
         scale = weight * updated
         energy = scale * updated
         en_ref[...] += energy[:, 0:CH] + energy[:, CH:]
-        gs_s[:, cols] = (mm((2.0 * scale).astype(BF16), wot[kind]) * norm).astype(BF16)
-
-    grad_own = tiled(gs_s[...], size)
-    for step in range(own_steps):
-        backward(own_rows(step, size), grad_own)
+        gs_ref[:, cols] = (mm((2.0 * scale).astype(BF16), wot[kind]) * norm).astype(BF16)
 
     def ghost_backward(step):
-        here, rows = ghost_rows(step, size)
-        backward(rows, mm(d_gh[here, :], gs_s[...]).astype(BF16))
-
-    over_ghost_steps(steps, ghost_backward, size)
-
-
-def pair_scratch(atoms, edges, ghosts, group):
+        here, _ = ghost_rows(step)
+        grad = mm(d_gh[here, :], gs_ref[...]).astype(BF16)
+        backward(group, here, grad, gate_ref, wmt, nf_s, mx_s, dot_ref, grad_refs)
+
+    over_ghost_steps(steps, ghost_backward)
+
+
+def pair_scratch(atoms, half, ghosts, group):
     count, width = len(KINDS[group]), GROUP_COLS[group]
     return (
         [pltpu.VMEM((ghosts, width), BF16), pltpu.SemaphoreType.DMA((7,))]
         + [pltpu.VMEM((count, 2 * CH, 2 * CH), BF16) for _ in range(4)]
         + [
-            pltpu.VMEM((edges, width), BF16),
-            pltpu.VMEM((edges, width), BF16),
+            pltpu.VMEM((half, width), BF16),
+            pltpu.VMEM((half, width), BF16),
             pltpu.VMEM((atoms, width), F32),
-            pltpu.VMEM((atoms, width), BF16),
         ]
     )
 
@@ -427,15 +437,71 @@
     return call(own_kernel, "own_edges", out_shape, [], 1 << 31, args)
 
 
+def scalar_forward(rows, near, radial, mix_ref, m0_ref, gate_ref, nf0_ref):
+    near = near.astype(BF16)
+    nf0_ref[rows, :] = near
+    mixed = mm(near * radial, mix_ref[0])
+    m0_ref[rows, :] = mixed.astype(BF16)
+    gate = jax.nn.sigmoid(mixed)
+    gate_ref[rows, :] = gate.astype(BF16)
+    return (mixed * gate).astype(BF16)
+
+
+def own_forward_kernel(groups, scalar, *refs):
+    own_ref, mix_ref, oh_own, refs = *refs[:3], refs[3:]
+    radial0, radials = refs[0], dict(enumerate(refs[1:5], start=1))
+    refs = refs[5:]
+    if scalar:
+        m0_ref, gate_ref, nf0_ref, acc0_ref = refs[:4]
+        refs = refs[4:]
+        spread = own_spread(own_ref.shape[0])
+        feats = own_ref[:, 0:CH]
+        summed = None
+        for step in range(OWN_STEPS):
+            rows = own_rows(step)
+            message = scalar_forward(
+                rows, mm(oh_own[rows, :], feats), radial0[rows, :], mix_ref, m0_ref, gate_ref,
+                nf0_ref,
+            )
+            part = mm(spread, message)
+            summed = part if summed is None else summed + part
+        acc0_ref[...] = summed
+    else:
+        gate_ref, refs = refs[0], refs[1:]
+    outs, weights = refs[: 3 * len(groups)], refs[3 * len(groups) :]
+    for index, group in enumerate(groups):
+        block_diagonal(KINDS[group], mix_ref, weights[index])
+        nf_ref, mx_ref, acc_ref = outs[3 * index : 3 * index + 3]
+        own_forward(
+            group, own_ref, oh_own, radials, gate_ref, weights[index], nf_ref, mx_ref, acc_ref
+        )
+
+
+def own_forward_stage(groups, feats, mix, oh_own, radial_own, gate=None):
+    atoms = feats.shape[0]
+    half = atoms * HALF
+    out_shape = ()
+    if gate is None:
+        out_shape += (struct(half, CH, dtype=BF16),) * 3 + (struct(atoms, CH),)
+    for group in groups:
+        width = GROUP_COLS[group]
+        out_shape += (struct(half, width, dtype=BF16),) * 2 + (struct(atoms, width),)
+    args = (feats, mix, oh_own, *radial_own) + (() if gate is None else (gate,))
+    scratch = [pltpu.VMEM((len(KINDS[group]), 2 * CH, 2 * CH), BF16) for group in groups]
+    name = "own_forward_" + "".join("abc"[group] for group in groups)
+    kernel = functools.partial(own_forward_kernel, groups, gate is None)
+    outs = call(kernel, name, out_shape, scratch, 1 << 32, args)
+    first = len(outs) - 3 * len(groups)
+    return outs[:first], [outs[first + 3 * i : first + 3 * i + 3] for i in range(len(groups))]
+
+
 def start_kernel(
     p0, p1, p2, p3, p4, own_ref, own_pos_ref, meta_ref, rbf_ref, rad_ref, mix_ref, out_ref,
-    ew_ref, oh_own, radial_own0,
-    new_ref, oh_gh, d_gh, dt_gh, pre_ref, unit_ref, gs0_ref, en_ref, m0_own, m0_gh, gate_own,
-    gate_gh, nf0_own, nf0_gh, radial_gh1, radial_gh2, radial_gh3, radial_gh4,
+    ew_ref, acc0_ref,
+    new_ref, oh_gh, d_gh, dt_gh, pre_ref, unit_ref, gs0_ref, en_ref, m0_gh, gate_gh, nf0_gh,
+    radial_gh1, radial_gh2, radial_gh3, radial_gh4,
     table, sems, ghpos, acc_s,
 ):
-    m0_ref, gate_ref = Halves(m0_own, m0_gh), Halves(gate_own, gate_gh)
-    nf0_ref = Halves(nf0_own, nf0_gh)
     radial_gh = (None, radial_gh1, radial_gh2, radial_gh3, radial_gh4)
     copies = fetch((p0, p1, p2, p3, p4), slice(0, 2 * CH), table, sems)
     atoms = own_ref.shape[0]
@@ -474,30 +540,14 @@
     shift = jnp.where(lane == 12, side_of(ext_x, 3, 4.0), 0.0)
     shift = jnp.where(lane == 13, side_of(ext_y, 3, 4.0), shift)
     shift = jnp.where(lane == 14, side_of(ext_z, zcells + 1, 2.0 * zcells), shift)
-    def forward0(rows, onehot, feats, radial):
-        near = mm(onehot, feats).astype(BF16)
-        nf0_ref[rows, :] = near
-        mixed = mm(near * radial, mix_ref[0])
-        m0_ref[rows, :] = mixed.astype(BF16)
-        gate = jax.nn.sigmoid(mixed)
-        gate_ref[rows, :] = gate.astype(BF16)
-        return (mixed * gate).astype(BF16)
-
     own0 = own_ref[:, 0:CH]
-    spread_own = own_spread(atoms)
-    summed = None
-    for step in range(OWN_STEPS):
-        rows = own_rows(step)
-        message = forward0(rows, oh_own[rows, :], own0, radial_own0[rows, :])
-        part = mm(spread_own, message)
-        summed = part if summed is None else summed + part
-    acc_s[...] = summed
+    acc_s[...] = acc0_ref[...]
     for copy in copies:
         copy.wait()
     ghpos[...] = (table[:, CH:].astype(F32) + shift).astype(BF16)
 
     def ghost_start(step):
-        here, rows = ghost_rows(step)
+        here, _ = ghost_rows(step)
         base = step * STEP
         edge = (iota((STEP, atoms), 0) + base).astype(F32)
         mine = jnp.logical_and(edge >= start_row, edge < end_row).astype(F32)
@@ -521,7 +571,9 @@
         pre_ref[here, :] = pre.astype(BF16)
         for degree in range(1, 5):
             radial_gh[degree][here, :] = radial[:, degree * CH : (degree + 1) * CH]
-        message = forward0(rows, onehot, table[:, 0:CH], radial[:, 0:CH])
+        message = scalar_forward(
+            here, mm(onehot, table[:, 0:CH]), radial[:, 0:CH], mix_ref, m0_gh, gate_gh, nf0_gh
+        )
         acc_s[...] += mm(spread, message)
 
     over_ghost_steps(steps, ghost_start)
@@ -555,7 +607,7 @@
         struct(half, CH),
         struct(atoms, CH),
         struct(atoms, CH),
-    ) + (struct(half, CH, dtype=BF16),) * 10
+    ) + (struct(half, CH, dtype=BF16),) * 7
     scratch = [
         pltpu.VMEM((ghosts, 2 * CH), BF16),
         pltpu.SemaphoreType.DMA((7,)),
@@ -571,56 +623,67 @@
 
 def pairs_kernel(group, count, skip, *refs):
     pieces, refs = refs[:count], refs[count:]
-    own_ref, meta_ref, mix_ref, out_ref, nw_ref, oh_own, oh_gh, d_gh, dt_gh = refs[:9]
-    gate_ref = Halves(*refs[9:11])
-    refs = refs[11:]
+    own_ref, meta_ref, mix_ref, out_ref, nw_ref, oh_gh, d_gh, dt_gh, gate_gh = refs[:9]
+    gate_own, nf_own, mx_own, acc_own = refs[9:13]
+    refs = refs[13:]
     degrees = DEGREES[group]
-    radials = {}
-    for degree in degrees:
-        radials[degree], refs = Halves(*refs[:2]), refs[2:]
-    new_ref, en_ref, dot_own, dot_gh = refs[:4]
-    refs = refs[4:]
-    grads = {}
-    for degree in degrees:
-        grads[degree], refs = Halves(*refs[:2]), refs[2:]
-    table, sems, wm, wmt, wo, wot, nf_s, mx_s, acc_s, gs_s = refs
+    radials, refs = dict(zip(degrees, refs)), refs[len(degrees) :]
+    new_ref, en_ref, gs_ref, dot_gh = refs[:4]
+    grads, refs = dict(zip(degrees, refs[4:])), refs[4 + len(degrees) :]
+    if group == 0:
+        dot_own, refs = refs[0], refs[1:]
+        grads_own, refs = dict(zip(degrees, refs)), refs[len(degrees) :]
+    table, sems, wm, wmt, wo, wot, nf_s, mx_s, acc_s = refs
     copies = fetch(pieces, slice(skip, skip + GROUP_COLS[group]), table, sems)
-    block_diagonal(KINDS[group], mix_ref, out_ref, wm, wmt, wo, wot)
+    block_diagonal(KINDS[group], mix_ref, wm, wmt)
+    block_diagonal(KINDS[group], out_ref, wo, wot)
     en_ref[...] = jnp.zeros_like(en_ref)
-    pairs = tuple(range(*GROUPS[group]))
-
-    def radial_any(degree, rows):
-        return radials[degree][rows, :]
-
     for copy in copies:
         copy.wait()
-    run_pairs(
-        pairs, KINDS[group], own_ref, table, new_ref, pair_cols(pairs[0]).start, oh_own, oh_gh,
-        d_gh, dt_gh, gate_ref, radial_any, nw_ref, step_count(meta_ref), wm, wmt, wo, wot, nf_s,
-        mx_s, acc_s, gs_s, Halves(dot_own, dot_gh), grads, en_ref,
-    )
-
-
-def pairs_stage(group, skip, pieces, shared, radials):
+    ghost_pairs(
+        group, own_ref, table, new_ref, group_cols(group).start, oh_gh, d_gh, dt_gh, gate_gh,
+        radials, nw_ref, step_count(meta_ref), wm, wmt, wo, wot, nf_s, mx_s, acc_own, acc_s,
+        gs_ref, dot_gh, grads, en_ref,
+    )
+    if group == 0:
+        own_backward(group, gs_ref, gate_own, wmt, nf_own, mx_own, dot_own, grads_own)
+
+
+def pairs_stage(group, skip, pieces, shared, own_parts, radial_gh):
     feats = shared[0]
     atoms = feats.shape[0]
     half = atoms * HALF
     ghosts = sum(piece.shape[0] for piece in pieces)
     degrees = DEGREES[group]
+    sides = 2 if group == 0 else 1
     out_shape = (
         struct(atoms, GROUP_COLS[group], dtype=BF16),
         struct(atoms, CH),
-    ) + (struct(half, CH, dtype=BF16),) * (2 + 2 * len(degrees))
-    args = tuple(pieces) + tuple(shared)
-    for degree in degrees:
-        args += radials[degree]
-    new, energy, dot_own, dot_gh, *grads = call(
+        struct(atoms, GROUP_COLS[group], dtype=BF16),
+    ) + (struct(half, CH, dtype=BF16),) * (sides * (1 + len(degrees)))
+    args = tuple(pieces) + tuple(shared) + tuple(own_parts)
+    args += tuple(radial_gh[degree - 1] for degree in degrees)
+    new, energy, gs, *rest = call(
         functools.partial(pairs_kernel, group, len(pieces), skip), "pairs_" + "abc"[group],
-        out_shape, pair_scratch(atoms, 2 * half, ghosts, group), 1 << 33, args,
-        any_specs(len(pieces), len(args)), 32,
-    )
-    grads = {degree: tuple(grads[2 * i : 2 * i + 2]) for i, degree in enumerate(degrees)}
-    return new, energy, dot_own, dot_gh, grads
+        out_shape, pair_scratch(atoms, half, ghosts, group), 1 << 33, args,
+        any_specs(len(pieces), len(args)), 24,
+    )
+    return new, energy, gs, rest[: 1 + len(degrees)], rest[1 + len(degrees) :]
+
+
+def own_backward_kernel(group, mix_ref, gs_ref, gate_ref, nf_ref, mx_ref, *refs):
+    dot_ref, grads, wmt = refs[0], dict(zip(DEGREES[group], refs[1:-1])), refs[-1]
+    block_diagonal(KINDS[group], mix_ref, None, wmt)
+    own_backward(group, gs_ref, gate_ref, wmt, nf_ref, mx_ref, dot_ref, grads)
+
+
+def own_backward_stage(group, mix, gs, gate, nf, mx):
+    half = nf.shape[0]
+    out_shape = (struct(half, CH, dtype=BF16),) * (1 + len(DEGREES[group]))
+    scratch = [pltpu.VMEM((len(KINDS[group]), 2 * CH, 2 * CH), BF16)]
+    kernel = functools.partial(own_backward_kernel, group)
+    name = "own_backward_" + "abc"[group]
+    return call(kernel, name, out_shape, scratch, 1 << 32, (mix, gs, gate, nf, mx))
 
 
 def finish(
@@ -666,24 +729,22 @@
 
 
 def third_kernel(
-    low_ref, mid_ref, high_ref, own_ref, meta_ref, mix_ref, out_ref, nw_ref, oh_own, oh_gh, d_gh,
-    dt_gh, gate_own, gate_gh, radial_own4, radial_gh4,
+    low_ref, mid_ref, high_ref, own_ref, meta_ref, mix_ref, out_ref, nw_ref, oh_gh, d_gh, dt_gh,
+    gate_gh, acc_own, radial_gh4,
     radt_ref, rbft_ref, mixt_ref, gs0_ref, en_0, en_a, en_b, new_0, new_a, new_b, pre_gh, unit_gh,
     m0_ref, nf0_ref, dot_a, dot_b, *refs
 ):
     gr_gh, refs = refs[: PARTIALS - 1], refs[PARTIALS - 1 :]
     (
-        new_ref, energy_ref, src_ref, flow_ref, fmid_ref, fhigh_ref, dot_own, gr_own,
-        table, sems, wm, wmt, wo, wot, nf_s, mx_s, acc_s, gs_s, dot_c, gr_c, en_s, fgh_s,
+        new_ref, energy_ref, src_ref, flow_ref, fmid_ref, fhigh_ref, gs_ref,
+        table, sems, wm, wmt, wo, wot, nf_s, mx_s, acc_s, dot_c, gr_c, en_s, fgh_s,
     ) = refs
     group = 2
-    gate_ref = Halves(gate_own, gate_gh)
-    radial4 = Halves(radial_own4, radial_gh4)
-    pairs = tuple(range(*GROUPS[group]))
     copies = fetch((low_ref, mid_ref, high_ref), slice(0, GROUP_COLS[group]), table, sems)
     atoms = own_ref.shape[0]
     spacing = spacing_of(atoms, rbft_ref.shape[1])
-    block_diagonal(KINDS[group], mix_ref, out_ref, wm, wmt, wo, wot)
+    block_diagonal(KINDS[group], mix_ref, wm, wmt)
+    block_diagonal(KINDS[group], out_ref, wo, wot)
     en_s[...] = en_0[...] + en_a[...] + en_b[...]
     at = 0
     for part in (new_0, new_a, new_b):
@@ -691,15 +752,11 @@
         at += part.shape[1]
     steps = step_count(meta_ref)
 
-    def radial_any(degree, rows):
-        return radial4[rows, :]
-
     for copy in copies:
         copy.wait()
-    run_pairs(
-        pairs, KINDS[group], own_ref, table, new_ref, 0, oh_own, oh_gh, d_gh, dt_gh, gate_ref,
-        radial_any, nw_ref, steps, wm, wmt, wo, wot, nf_s, mx_s, acc_s, gs_s,
-        Halves(dot_own, dot_c), {4: Halves(gr_own, gr_c)}, en_s,
+    ghost_pairs(
+        group, own_ref, table, new_ref, 0, oh_gh, d_gh, dt_gh, gate_gh, {4: radial_gh4}, nw_ref,
+        steps, wm, wmt, wo, wot, nf_s, mx_s, acc_own, acc_s, gs_ref, dot_c, {4: gr_c}, en_s,
     )
     energy_ref[...] = jnp.sum(en_s[...].T, axis=0, keepdims=True)
 
@@ -708,7 +765,7 @@
     gs0_low = gs0_ref[...].astype(BF16)
 
     def ghost_finish(step):
-        here, rows = ghost_rows(step)
+        here, _ = ghost_rows(step)
         grad = mm(d_gh[here, :], gs0_low)
         pull, top, rest = finish(
             grad, m0_ref[here, :], nf0_ref[here, :], sum_of((dot_a, dot_b, dot_c), here),
@@ -738,8 +795,10 @@
         struct(atoms, feat, dtype=BF16),
         struct(1, atoms),
         struct(atoms, CH),
-    ) + tuple(struct(8, size) for size in sizes) + (struct(half, CH, dtype=BF16),) * 2
-    scratch = pair_scratch(atoms, 2 * half, ghosts, 2) + [
+    ) + tuple(struct(8, size) for size in sizes) + (
+        struct(atoms, GROUP_COLS[2], dtype=BF16),
+    )
+    scratch = pair_scratch(atoms, half, ghosts, 2) + [
         pltpu.VMEM((half, CH), BF16),
         pltpu.VMEM((half, CH), BF16),
         pltpu.VMEM((atoms, CH), F32),
@@ -748,7 +807,7 @@
     args = tuple(pieces) + (feats,) + rest
     return call(
         third_kernel, "third_group", out_shape, scratch, 1 << 33, args, any_specs(3, len(args)),
-        30,
+        24,
     )
 
 
@@ -841,23 +900,26 @@
         out_ref[comp] = -total[comp : comp + 1, :]
 
 
-def give_back(low, mid, high, own, home):
+def give_back_x(low, mid, high):
     up, down = ring("gx")
     from_low = lax.ppermute(high, "gx", up)
     from_high = lax.ppermute(low, "gx", down)
-    from_low, from_high, own = lax.optimization_barrier((from_low, from_high, own))
-    mid = mid + jnp.concatenate([from_low, from_high], axis=1)
+    return mid, jnp.concatenate([from_low, from_high], axis=1)
+
+
+def give_back_y(mid):
     up, down = ring("gy")
-    from_low = lax.ppermute(mid, "gy", up)
-    from_high = lax.ppermute(mid, "gy", down)
-    args = (mid, from_low, from_high)
-    mid = call(fold_kernel, "fold", (struct(*mid.shape),), [], 1 << 16, args)[0]
+    return mid, lax.ppermute(mid, "gy", up), lax.ppermute(mid, "gy", down)
+
+
+def fold(*args):
+    return call(fold_kernel, "fold", (struct(*args[0].shape),), [], 1 << 16, args)[0]
+
+
+def give_back_z(mid):
     up, down = ring("gz")
     from_low = lax.ppermute(mid, "gz", up)
-    from_high = from_low if len(up) == 2 else lax.ppermute(mid, "gz", down)
-    args = (mid, from_low, from_high, own, home)
-    out_shape = (struct(3, 1, own.shape[1]),)
-    return call(forces_kernel, "forces", out_shape, [], 1 << 20, args)[0]
+    return mid, from_low, from_low if len(up) == 2 else lax.ppermute(mid, "gz", down)
 
 
 def local(
@@ -881,49 +943,61 @@
     hold = lax.optimization_barrier
     block0, block12 = (part.reshape(2, 2, 2, 8, part.shape[1]) for part in (cells0, cells12))
     block0 = grown(block0, "gz", 2)
-    block0, block12, own_pos, meta = hold((block0, block12, own_pos, meta))
+    oh_own, pre_own, unit_own, radt, rbft, mixt, home, *radial_own = own_stage(
+        meta, own_pos, rbf_weight, radial_weight, mix_weight
+    )
+    block0, oh_own = hold((block0, oh_own))
     y_low, y_high = neighbours_of(block0, "gy", 1)
     low_in, high_in = neighbours_of(block0, "gx", 0)
     block12 = grown(block12, "gz", 2)
-    oh_own, pre_own, unit_own, radt, rbft, mixt, home, *radial_own = own_stage(
-        meta, own_pos, rbf_weight, radial_weight, mix_weight
-    )
-    y_low, y_high, block12, oh_own = hold((y_low, y_high, block12, oh_own))
+    (m0_own, gate_own, nf0_own, acc0), (own_a, own_b) = own_forward_stage(
+        (0, 1), feats, mix_weight, oh_own, radial_own
+    )
+    y_low, y_high, block12, gate_own = hold((y_low, y_high, block12, gate_own))
     outer = jnp.concatenate([y_low, y_high], axis=1)
     low_out, high_out = neighbours_of(outer, "gx", 0)
     middle = jnp.concatenate([y_low, block0, y_high], axis=1)
     pieces0 = tuple(flat_rows(p) for p in (low_in, low_out, middle, high_in, high_out))
     block1, block2 = block12[..., : GROUP_COLS[1]], block12[..., GROUP_COLS[1] :]
     block1 = grown(block1, "gy", 1)
+    _, (own_c,) = own_forward_stage((2,), feats, mix_weight, oh_own, radial_own, gate_own)
+    pieces0, acc_c = hold((pieces0, own_c[2]))
     (
-        new_0, oh_gh, d_gh, dt_gh, pre_gh, unit_gh, gs0, en_0, m0_own, m0_gh, gate_own, gate_gh,
-        nf0_own, nf0_gh, *radial_gh,
+        new_0, oh_gh, d_gh, dt_gh, pre_gh, unit_gh, gs0, en_0, m0_gh, gate_gh, nf0_gh, *radial_gh,
     ) = start_stage(
         pieces0, feats, own_pos, meta, rbf_weight, radial_weight, mix_weight, out_weight,
-        energy_weight[None], oh_own, radial_own[0],
-    )
-    block1, block2, gate_own = hold((block1, block2, gate_own))
+        energy_weight[None], acc0,
+    )
+    block1, block2, gate_gh = hold((block1, block2, gate_gh))
     pieces1 = ghost_pieces(block1)
     block2 = grown(block2, "gy", 1)
-    shared = (
-        feats, meta, mix_weight, out_weight, norm_weight, oh_own, oh_gh, d_gh, dt_gh, gate_own,
-        gate_gh,
-    )
-    radials = {degree: (radial_own[degree], radial_gh[degree - 1]) for degree in range(1, 5)}
-    new_a, en_a, dot_own_a, dot_gh_a, grads_a = pairs_stage(0, 2 * CH, pieces0, shared, radials)
+    shared = (feats, meta, mix_weight, out_weight, norm_weight, oh_gh, d_gh, dt_gh, gate_gh)
+    new_a, en_a, _, (dot_gh_a, *gr_gh_a), (dot_own_a, *gr_own_a) = pairs_stage(
+        0, 2 * CH, pieces0, shared, (gate_own, *own_a), radial_gh
+    )
     en_a, block2 = hold((en_a, block2))
     pieces2 = ghost_pieces(block2)
-    new_b, en_b, dot_own_b, dot_gh_b, grads_b = pairs_stage(1, 0, pieces1, shared, radials)
-    grads = list(grads_a.values()) + list(grads_b.values())
-    new, energy, src, low, mid, high, dot_own_c, gr_own_c = third_stage(
-        pieces2, *shared, *radials[4], radt, rbft, mixt, gs0, en_0, en_a, en_b, new_0, new_a,
-        new_b, pre_gh, unit_gh, m0_gh, nf0_gh, dot_gh_a, dot_gh_b, *[ghost for _, ghost in grads],
-    )
+    new_b, en_b, gs_b, (dot_gh_b, *gr_gh_b), _ = pairs_stage(
+        1, 0, pieces1, shared, (gate_own, *own_b), radial_gh
+    )
+    new, energy, src, low, mid, high, gs_c = third_stage(
+        pieces2, *shared, acc_c, radial_gh[3], radt, rbft, mixt, gs0, en_0, en_a, en_b, new_0,
+        new_a, new_b, pre_gh, unit_gh, m0_gh, nf0_gh, dot_gh_a, dot_gh_b, *gr_gh_a, *gr_gh_b,
+    )
+    mid, arrived = give_back_x(low, mid, high)
+    dot_own_c, *gr_own_c = own_backward_stage(2, mix_weight, gs_c, gate_own, *own_c[:2])
+    arrived, gs_b, dot_own_c = hold((arrived, gs_b, dot_own_c))
+    mid, from_low, from_high = give_back_y(mid + arrived)
+    dot_own_b, *gr_own_b = own_backward_stage(1, mix_weight, gs_b, gate_own, *own_b[:2])
+    from_low, from_high, gs0, dot_own_b = hold((from_low, from_high, gs0, dot_own_b))
+    folded = give_back_z(fold(mid, from_low, from_high))
     own = own_back_stage(
         oh_own, pre_own, unit_own, radt, rbft, mixt, gs0, src, m0_own, nf0_own, dot_own_a,
-        dot_own_b, dot_own_c, *[own for own, _ in grads], gr_own_c,
-    )
-    forces = give_back(low, mid, high, own, home)
+        dot_own_b, dot_own_c, *gr_own_a, *gr_own_b, *gr_own_c,
+    )
+    args = (*folded, own, home)
+    out_shape = (struct(3, 1, own.shape[1]),)
+    forces = call(forces_kernel, "forces", out_shape, [], 1 << 20, args)[0]
     return (
         new[None, None, None],
         energy[None, None],

time: 75.7 us -> 77.5 us (1.024)
  starting transfers between devices: 27.4 us -> 22.6 us
  local copies, waits for them, and re-layouts: 4 us -> 6.73 us
  waiting for transfers between devices: 12.1 us -> 14.7 us
  Pallas kernels: 30.6 us -> 31.8 us
    ppermute x7, waiting for transfers between devices: 1.73 us -> 6.54 us  [neighbours_of(): lax.ppermute(lax.slice_in_dim(block, length - 1, length, axis=dim), axis,...]
    ppermute x2, waiting for transfers between devices: 3.5 us -> 0.01 us  [neighbours_of(): other = lax.ppermute(block, axis, up)]
    ppermute x7, waiting for transfers between devices: 2.11 us -> 5.54 us  [neighbours_of(): after = lax.ppermute(lax.slice_in_dim(block, 0, 1, axis=dim), axis, down)]
    unnamed x27 -> x33, local copies, waits for them, and re-layouts: 3.76 us -> 6.48 us
    ppermute x5, waiting for transfers between devices: 4.76 us -> 2.57 us  [the longest x2 2.38 us: give_back_y(): return (mid, lax.ppermute(mid, 'gy', up), lax.ppermute(mid, 'gy', down))]
    ppermute x2, starting transfers between devices: 4.84 us -> 3.11 us  [neighbours_of(): other = lax.ppermute(block, axis, up)]
    ppermute x7, starting transfers between devices: 4.37 us -> 2.75 us  [neighbours_of(): lax.ppermute(lax.slice_in_dim(block, length - 1, length, axis=dim), axis,...]
    pallas_call x9 -> x14, Pallas kernels: 30.6 us -> 31.8 us  [call(): pl.pallas_call(kernel, out_shape=out_shape, in_specs=specs or [pl.BlockSp...]
  transfers between devices with their start and end apart: 21 -> 21, of which waited for: 7 -> 10; matrix products, arithmetic and copies ran while one was open for 1% -> 1% of each run, Pallas kernels for 28% -> 32%
where the time goes in v6:
time: 77.5 us; the launch traced here: 77.2 us
  Pallas kernels  31.8 us (41%)
  starting transfers between devices  22.6 us (29%)
  waiting for transfers between devices  14.7 us (19%)
  local copies, waits for them, and re-layouts  6.73 us (9%)
  between operations  1.04 us (1%)
    pallas_call x14, Pallas kernels, call(): pl.pallas_call(kernel, out_shape=out_shape, in_specs=specs or [pl.BlockSp...  31.8 us
    ppermute x7, starting transfers between devices, neighbours_of(): after = lax.ppermute(lax.slice_in_dim(block, 0, 1, axis=dim), axis, down)  11.4 us
    ppermute x7, waiting for transfers between devices, neighbours_of(): lax.ppermute(lax.slice_in_dim(block, length - 1, length, axis=dim), axis,...  6.54 us
    unnamed x33, local copies, waits for them, and re-layouts  6.48 us
    ppermute x7, waiting for transfers between devices, neighbours_of(): after = lax.ppermute(lax.slice_in_dim(block, 0, 1, axis=dim), axis, down)  5.54 us
    ppermute x2, starting transfers between devices, neighbours_of(): other = lax.ppermute(block, axis, up)  3.11 us
    ppermute x7, starting transfers between devices, neighbours_of(): lax.ppermute(lax.slice_in_dim(block, length - 1, length, axis=dim), axis,...  2.75 us
    ppermute x2, waiting for transfers between devices, give_back_y(): return (mid, lax.ppermute(mid, 'gy', up), lax.ppermute(mid, 'gy', down))  2.38 us
  transfers between devices with their start and end apart: 21, of which 10 were waited for; matrix products, arithmetic and copies ran while one was open for 1% of the time, Pallas kernels for 32%

profile of v6, /device:TPU:0, one launch (start us, length us, event | category | flops | bytes accessed | tf_op | source)
XLA Modules:
  0.0 77.2 jit_solution(4403336453083126191)
XLA Ops:
  0.6 1.0 %copy-done = bf16[1,1,1,64,3200]{4,3,2,1,0:T(8,128)(2,1)S(1)} copy-done((bf16[1,1,1,64,3200]{4,3,2,1,0:T(8,128)(2,1)S(1)}, bf16[1,1,1,64,3200]{4,3,2,1,0:T(8,128)(2,1)}, u32[]{:S(2)}) %copy-start) | copy-done | bytes 409624
  5.1 3.0 %collective-permute-start = (bf16[2,2,2,8,1024]{4,3,2,1,0:T(8,128)(2,1)S(1)}, bf16[2,2,2,8,1024]{4,3,2,1,0:T(8,128)(2,1)S(1)}, u32[]{:S(2)}, u32[]{:S(2)}) collective-permute-start(bf16[2,2,2,8,1024]{4,3,2,1,0:T(8,128)(2,1)S(1)} %bitcast.40), channel_id=1, source_target_pairs={{0,1},{1,0},{2,3},{3,2},{4,5},{5,4},{6,7},{7,6},{8,9},{9,8},{10,11... | collective-permute-start | bytes 393224 | tf_op jit(solution)/shard_map/ppermute | solution.py:853
  11.1 2.9 %own_edges.1 = (bf16[1024,64]{1,0:T(8,128)(2,1)S(1)}, bf16[1024,128]{1,0:T(8,128)(2,1)S(1)}, f32[1024,128]{1,0:T(8,128)S(1)}, bf16[640,128]{1,0:T(8,128)(2,1)S(1...) custom-call(f32[64,128]{1,0:T(8,128)S(1)} %get-tuple-element.100.met, ...), custom_call_target="tpu_custom_call" | custom-call | flops 2147483648 | bytes 3096576 | tf_op jit(solution)/shard_map/own_edges/pallas_call | solution.py:58
  14.1 4.2 %collective-permute-start.3 = (bf16[2,1,4,8,1024]{4,3,2,1,0:T(8,128)(2,1)S(1)}, bf16[2,1,4,8,1024]{4,3,2,1,0:T(8,128)(2,1)S(1)}, u32[]{:S(2)}, u32[]{:S(2)}) collective-permute-start(bf16[2,1,4,8,1024]{4,3,2,1,0:T(8,128)(2,1)S(1)} %get-tuple-element.212), channel_id=1, source_target_pairs={{2,0},{4,2},{6,4},{0,6},{3,1},{5,3},{7,5},{1,7},{10,8},{12,10},{14... | collective-permute-start | bytes 393224 | tf_op jit(solution)/shard_map/ppermute | solution.py:859
  18.8 4.3 %own_forward_ab.1 = (bf16[1024,128]{1,0:T(8,128)(2,1)S(1)}, bf16[1024,128]{1,0:T(8,128)(2,1)S(1)}, bf16[1024,128]{1,0:T(8,128)(2,1)S(1)}, f32[64,128]{1,0:T(8,12...) custom-call(bf16[64,3200]{1,0:T(8,128)(2,1)S(1)} %bitcast.30, ...), custom_call_target="tpu_custom_call" | custom-call | flops 4294967296 | bytes 11747328 | tf_op jit(solution)/shard_map/own_forward_ab/pallas_call | solution.py:58
  23.3 1.8 %collective-permute-done.2 = bf16[2,1,4,8,1024]{4,3,2,1,0:T(8,128)(2,1)S(1)} collective-permute-done((bf16[2,1,4,8,1024]{4,3,2,1,0:T(8,128)(2,1)S(1)}, bf16[2,1,4,8,1024]{4,3,2,1,0:T(8,128)(2,1)S(1)}, u32[]{:S(2)}, u32[]{:S(2)}) %collective-permute-start.2) | collective-permute-done | bytes 131104 | tf_op jit(solution)/shard_map/ppermute | solution.py:858
  26.5 1.8 %own_forward_c.1 = (bf16[1024,1024]{1,0:T(8,128)(2,1)S(1)}, bf16[1024,1024]{1,0:T(8,128)(2,1)S(1)}, f32[64,1024]{1,0:T(8,128)S(1)}) custom-call(bf16[64,3200]{1,0:T(8,128)(2,1)S(1)} %bitcast.31, bf16[5,128,128]{2,1,0:T(8,128)(2,1)S(1)} %copy-done.9, bf16[1024,64]{1,0:T(8,128)(2,1)S(1)} %get-tuple-element.105.refs_2_.oh_own, ...), custom_call_target="tpu_custom_call" | custom-call | flops 4294967296 | bytes 6733824 | tf_op jit(solution)/shard_map/own_forward_c/pallas_call | solution.py:58
  28.4 3.2 %collective-permute-start.9 = (bf16[2,1,4,8,1280]{4,3,2,1,0:T(8,128)(2,1)S(1)}, bf16[2,1,4,8,1280]{4,3,2,1,0:T(8,128)(2,1)S(1)}, u32[]{:S(2)}, u32[]{:S(2)}) collective-permute-start(bf16[2,1,4,8,1280]{4,3,2,1,0:T(8,128)(2,1)S(1)} %get-tuple-element.201), channel_id=1, source_target_pairs={{2,0},{4,2},{6,4},{0,6},{3,1},{5,3},{7,5},{1,7},{10,8},{12,10},{14... | collective-permute-start | bytes 491528 | tf_op jit(solution)/shard_map/ppermute | solution.py:859
  31.7 3.6 %ghost_start.1 = (bf16[64,128]{1,0:T(8,128)(2,1)S(1)}, bf16[1024,512]{1,0:T(8,128)(2,1)S(1)}, bf16[1024,64]{1,0:T(8,128)(2,1)S(1)}, bf16[64,1024]{1,0:T(8,128)(2...) custom-call(bf16[64,1024]{1,0:T(8,128)(2,1)S(1)} %bitcast.52, ...), custom_call_target="tpu_custom_call" | custom-call | flops 2147483648 | bytes 6177280 | tf_op jit(solution)/shard_map/ghost_start/pallas_call | solution.py:58
  35.3 2.9 %collective-permute-done.9 = bf16[2,1,4,8,1280]{4,3,2,1,0:T(8,128)(2,1)S(1)} collective-permute-done((bf16[2,1,4,8,1280]{4,3,2,1,0:T(8,128)(2,1)S(1)}, bf16[2,1,4,8,1280]{4,3,2,1,0:T(8,128)(2,1)S(1)}, u32[]{:S(2)}, u32[]{:S(2)}) %collective-permute-start.9) | collective-permute-done | bytes 163872 | tf_op jit(solution)/shard_map/ppermute | solution.py:859
  38.9 3.3 %collective-permute-start.11 = (bf16[2,1,4,8,1024]{4,3,2,1,0:T(8,128)(2,1)S(1)}, bf16[2,1,4,8,1024]{4,3,2,1,0:T(8,128)(2,1)S(1)}, u32[]{:S(2)}, u32[]{:S(2)}) collective-permute-start(bf16[2,1,4,8,1024]{4,3,2,1,0:T(8,128)(2,1)S(1)} %get-tuple-element.207), channel_id=1, source_target_pairs={{2,0},{4,2},{6,4},{0,6},{3,1},{5,3},{7,5},{1,7},{10,8},{12,10},{14... | collective-permute-start | bytes 393224 | tf_op jit(solution)/shard_map/ppermute | solution.py:859
  42.8 3.3 %pairs_a.1 = (bf16[64,768]{1,0:T(8,128)(2,1)S(1)}, f32[64,128]{1,0:T(8,128)S(1)}, bf16[64,768]{1,0:T(8,128)(2,1)}, bf16[1024,128]{1,0:T(8,128)(2,1)S(1)}, bf16[1...) custom-call(bf16[64,1024]{1,0:T(8,128)(2,1)S(1)} %bitcast.53, ...), custom_call_target="tpu_custom_call" | custom-call | flops 8589934592 | bytes 9324544 | tf_op jit(solution)/shard_map/pairs_a/pallas_call | solution.py:58
  47.6 2.3 %collective-permute-done.15 = bf16[1,4,4,8,1280]{4,3,2,1,0:T(8,128)(2,1)S(1)} collective-permute-done((bf16[1,4,4,8,1280]{4,3,2,1,0:T(8,128)(2,1)S(1)}, bf16[1,4,4,8,1280]{4,3,2,1,0:T(8,128)(2,1)S(1)}, u32[]{:S(2)}, u32[]{:S(2)}) %collective-permute-start.15) | collective-permute-done | bytes 327712 | tf_op jit(solution)/shard_map/ppermute | solution.py:859
  49.9 2.5 %collective-permute-done.14 = bf16[1,4,4,8,1280]{4,3,2,1,0:T(8,128)(2,1)S(1)} collective-permute-done((bf16[1,4,4,8,1280]{4,3,2,1,0:T(8,128)(2,1)S(1)}, bf16[1,4,4,8,1280]{4,3,2,1,0:T(8,128)(2,1)S(1)}, u32[]{:S(2)}, u32[]{:S(2)}) %collective-permute-start.14) | collective-permute-done | bytes 327712 | tf_op jit(solution)/shard_map/ppermute | solution.py:858
  52.4 3.5 %pairs_b.1 = (bf16[64,1280]{1,0:T(8,128)(2,1)S(1)}, f32[64,128]{1,0:T(8,128)S(1)}, bf16[64,1280]{1,0:T(8,128)(2,1)S(1)}, bf16[1024,128]{1,0:T(8,128)(2,1)S(1)}, ...) custom-call(bf16[128,1280]{1,0:T(8,128)(2,1)S(1)} %bitcast.47, ...), custom_call_target="tpu_custom_call" | custom-call | flops 8589934592 | bytes 11683840 | tf_op jit(solution)/shard_map/pairs_b/pallas_call | solution.py:58
  55.9 1.8 %collective-permute-done.12 = bf16[1,4,4,8,1024]{4,3,2,1,0:T(8,128)(2,1)S(1)} collective-permute-done((bf16[1,4,4,8,1024]{4,3,2,1,0:T(8,128)(2,1)S(1)}, bf16[1,4,4,8,1024]{4,3,2,1,0:T(8,128)(2,1)S(1)}, u32[]{:S(2)}, u32[]{:S(2)}) %collective-permute-start.12) | collective-permute-done | bytes 262176 | tf_op jit(solution)/shard_map/ppermute | solution.py:858
  57.7 5.4 %third_group.1 = (bf16[64,3200]{1,0:T(8,128)(2,1)}, f32[1,64]{1,0:T(1,128)}, f32[64,128]{1,0:T(8,128)S(1)}, f32[8,128]{1,0:T(8,128)S(1)}, f32[8,256]{1,0:T(8,128...) custom-call(bf16[128,1024]{1,0:T(8,128)(2,1)S(1)} %bitcast.49, bf16[256,1024]{1,0:T(8,128)(2,1)S(1)} %bitcast.27, ...), custom_call_target="tpu_custom_call" | custom-call | flops 8589934592 | bytes 8390912 | tf_op jit(solution)/shard_map/third_group/pallas_call | solution.py:58
  63.2 1.7 %collective-permute-start.17 = (f32[8,128]{1,0:T(8,128)S(1)}, f32[8,128]{1,0:T(8,128)S(1)}, u32[]{:S(2)}, u32[]{:S(2)}) collective-permute-start(f32[8,128]{1,0:T(8,128)S(1)} %get-tuple-element.168), channel_id=1, source_target_pairs={{8,0},{16,8},{24,16},{0,24},{9,1},{17,9},{25,17},{1,25},{10,2},{18... | collective-permute-start | bytes 12296 | tf_op jit(solution)/shard_map/ppermute | solution.py:906
  64.9 1.1 %own_backward_c.1 = (bf16[1024,128]{1,0:T(8,128)(2,1)S(1)}, bf16[1024,128]{1,0:T(8,128)(2,1)S(1)}) custom-call(bf16[5,128,128]{2,1,0:T(8,128)(2,1)S(1)} %copy-done.10, bf16[64,1024]{1,0:T(8,128)(2,1)S(1)} %get-tuple-element.170.gs_ref, bf16[1024,128]{1,0:T(8,128)(2,1)S(1)} %get-tuple-element.114.refs_8_.refs_14_.refs_12_.gate_ref, ...), custom_call_target="tpu_custom_call" | custom-call | flops 4294967296 | bytes 5275648 | tf_op jit(solution)/shard_map/own_backward_c/pallas_call | solution.py:58
  66.5 1.7 %collective-permute-start.18 = (f32[8,256]{1,0:T(8,128)S(1)}, f32[8,256]{1,0:T(8,128)S(1)}, u32[]{:S(2)}, u32[]{:S(2)}) collective-permute-start(f32[8,256]{1,0:T(8,128)S(1)} %add.3.mid_ref), channel_id=1, source_target_pairs={{0,2},{2,4},{4,6},{6,0},{1,3},{3,5},{5,7},{7,1},{8,10},{10,12},{12... | collective-permute-start | bytes 24584 | tf_op jit(solution)/shard_map/ppermute | solution.py:912
  68.3 1.3 %own_backward_b.1 = (bf16[1024,128]{1,0:T(8,128)(2,1)S(1)}, bf16[1024,128]{1,0:T(8,128)(2,1)S(1)}, bf16[1024,128]{1,0:T(8,128)(2,1)S(1)}, bf16[1024,128]{1,0:T(8,128)(2,1)S(1)}) custom-call(bf16[5,128,128]{2,1,0:T(8,128)(2,1)S(1)} %copy-done.10, bf16[64,1280]{1,0:T(8,128)(2,1)S(1)} %get-tuple-element.175.gs_ref, ...), custom_call_target="tpu_custom_call" | custom-call | flops 4294967296 | bytes 6881280 | tf_op jit(solution)/shard_map/own_backward_b/pallas_call | solution.py:58
  69.9 2.1 %collective-permute-done.18.low_ref = f32[8,256]{1,0:T(8,128)S(1)} collective-permute-done((f32[8,256]{1,0:T(8,128)S(1)}, f32[8,256]{1,0:T(8,128)S(1)}, u32[]{:S(2)}, u32[]{:S(2)}) %collective-permute-start.18) | collective-permute-done | bytes 8224 | tf_op jit(solution)/shard_map/ppermute | solution.py:912
  72.1 1.5 %collective-permute-start.20 = (f32[8,256]{1,0:T(8,128)S(1)}, f32[8,256]{1,0:T(8,128)S(1)}, u32[]{:S(2)}, u32[]{:S(2)}) collective-permute-start(f32[8,256]{1,0:T(8,128)S(1)} %fold.1.mid_ref), channel_id=1, source_target_pairs={{0,1},{1,0},{2,3},{3,2},{4,5},{5,4},{6,7},{7,6},{8,9},{9,8},{10,11... | collective-permute-start | bytes 24584 | tf_op jit(solution)/shard_map/ppermute | solution.py:921
  73.6 2.8 %own_back.1.own_ref = f32[8,64]{1,0:T(8,128)S(1)} custom-call(bf16[1024,64]{1,0:T(8,128)(2,1)S(1)} %get-tuple-element.105.refs_2_.oh_own, bf16[1024,128]{1,0:T(8,128)(2,1)S(1)} %get-tuple-element.179.pre_own, f32[1024,128]{1,0:T(8,128)S(1)} %get-tuple-element.180.unit_own, bf16[640,128]{1,0:T(8,128)(2,1)S(1)} %get-tuple-element.138.radt_ref, ...), custom_call_target="tpu_custom_call" | custom-call | flops 2147483648 | bytes 4196352 | tf_op jit(solution)/shard_map/own_back/pallas_call | solution.py:58
  (85 shorter events, 13.1 us)
Async XLA Ops:
  5.1 9.0 %collective-permute-start = (bf16[2,2,2,8,1024]{4,3,2,1,0:T(8,128)(2,1)S(1)}, bf16[2,2,2,8,1024]{4,3,2,1,0:T(8,128)(2,1)S(1)}, u32[]{:S(2)}, u32[]{:S(2)}) collective-permute-start(bf16[2,2,2,8,1024]{4,3,2,1,0:T(8,128)(2,1)S(1)} %bitcast.40), channel_id=1, source_target_pairs={{0,1},{1,0},{2,3},{3,2},{4,5},{5,4},{6,7},{7,6},{8,9},{9,8},{10,11... | collective-permute-start | bytes 393224 | tf_op jit(solution)/shard_map/ppermute | solution.py:853
  8.3 14.8 %collective-permute-start.4 = (bf16[2,2,2,8,2304]{4,3,2,1,0:T(8,128)(2,1)S(1)}, bf16[2,2,2,8,2304]{4,3,2,1,0:T(8,128)(2,1)S(1)}, u32[]{:S(2)}, u32[]{:S(2)}) collective-permute-start(bf16[2,2,2,8,2304]{4,3,2,1,0:T(8,128)(2,1)S(1)} %bitcast.36), channel_id=1, source_target_pairs={{0,1},{1,0},{2,3},{3,2},{4,5},{5,4},{6,7},{7,6},{8,9},{9,8},{10,11... | collective-permute-start | bytes 884744 | tf_op jit(solution)/shard_map/ppermute | solution.py:853
  11.1 7.7 %copy-start.1 = (bf16[1,1,1,64,3200]{4,3,2,1,0:T(8,128)(2,1)S(1)}, bf16[1,1,1,64,3200]{4,3,2,1,0:T(8,128)(2,1)}, u32[]{:S(2)}) copy-start(bf16[1,1,1,64,3200]{4,3,2,1,0:T(8,128)(2,1)} %param.11) | copy-start | bytes 1228804
  14.1 9.1 %collective-permute-start.3 = (bf16[2,1,4,8,1024]{4,3,2,1,0:T(8,128)(2,1)S(1)}, bf16[2,1,4,8,1024]{4,3,2,1,0:T(8,128)(2,1)S(1)}, u32[]{:S(2)}, u32[]{:S(2)}) collective-permute-start(bf16[2,1,4,8,1024]{4,3,2,1,0:T(8,128)(2,1)S(1)} %get-tuple-element.212), channel_id=1, source_target_pairs={{2,0},{4,2},{6,4},{0,6},{3,1},{5,3},{7,5},{1,7},{10,8},{12,10},{14... | collective-permute-start | bytes 393224 | tf_op jit(solution)/shard_map/ppermute | solution.py:859
  18.3 6.8 %collective-permute-start.2 = (bf16[2,1,4,8,1024]{4,3,2,1,0:T(8,128)(2,1)S(1)}, bf16[2,1,4,8,1024]{4,3,2,1,0:T(8,128)(2,1)S(1)}, u32[]{:S(2)}, u32[]{:S(2)}) collective-permute-start(bf16[2,1,4,8,1024]{4,3,2,1,0:T(8,128)(2,1)S(1)} %get-tuple-element.213), channel_id=1, source_target_pairs={{0,2},{2,4},{4,6},{6,0},{1,3},{3,5},{5,7},{7,1},{8,10},{10,12},{12... | collective-permute-start | bytes 393224 | tf_op jit(solution)/shard_map/ppermute | solution.py:858
  18.3 10.1 %collective-permute-start.6 = (bf16[1,2,4,8,1024]{4,3,2,1,0:T(8,128)(2,1)S(1)}, bf16[1,2,4,8,1024]{4,3,2,1,0:T(8,128)(2,1)S(1)}, u32[]{:S(2)}, u32[]{:S(2)}) collective-permute-start(bf16[1,2,4,8,1024]{4,3,2,1,0:T(8,128)(2,1)S(1)} %get-tuple-element.210), channel_id=1, source_target_pairs={{8,0},{16,8},{24,16},{0,24},{9,1},{17,9},{25,17},{1,25},{10,2},{18... | collective-permute-start | bytes 393224 | tf_op jit(solution)/shard_map/ppermute | solution.py:859
  18.4 13.2 %collective-permute-start.1 = (bf16[1,2,4,8,1024]{4,3,2,1,0:T(8,128)(2,1)S(1)}, bf16[1,2,4,8,1024]{4,3,2,1,0:T(8,128)(2,1)S(1)}, u32[]{:S(2)}, u32[]{:S(2)}) collective-permute-start(bf16[1,2,4,8,1024]{4,3,2,1,0:T(8,128)(2,1)S(1)} %get-tuple-element.211), channel_id=1, source_target_pairs={{0,8},{8,16},{16,24},{24,0},{1,9},{9,17},{17,25},{25,1},{2,10},{10... | collective-permute-start | bytes 393224 | tf_op jit(solution)/shard_map/ppermute | solution.py:858
  25.2 6.4 %collective-permute-start.7 = (bf16[1,2,4,8,1024]{4,3,2,1,0:T(8,128)(2,1)S(1)}, bf16[1,2,4,8,1024]{4,3,2,1,0:T(8,128)(2,1)S(1)}, u32[]{:S(2)}, u32[]{:S(2)}) collective-permute-start(bf16[1,2,4,8,1024]{4,3,2,1,0:T(8,128)(2,1)S(1)} %get-tuple-element.208), channel_id=1, source_target_pairs={{8,0},{16,8},{24,16},{0,24},{9,1},{17,9},{25,17},{1,25},{10,2},{18... | collective-permute-start | bytes 393224 | tf_op jit(solution)/shard_map/ppermute | solution.py:859
  25.3 6.3 %collective-permute-start.5 = (bf16[1,2,4,8,1024]{4,3,2,1,0:T(8,128)(2,1)S(1)}, bf16[1,2,4,8,1024]{4,3,2,1,0:T(8,128)(2,1)S(1)}, u32[]{:S(2)}, u32[]{:S(2)}) collective-permute-start(bf16[1,2,4,8,1024]{4,3,2,1,0:T(8,128)(2,1)S(1)} %get-tuple-element.209), channel_id=1, source_target_pairs={{0,8},{8,16},{16,24},{24,0},{1,9},{9,17},{17,25},{25,1},{2,10},{10... | collective-permute-start | bytes 393224 | tf_op jit(solution)/shard_map/ppermute | solution.py:858
  25.8 9.5 %collective-permute-start.8 = (bf16[2,1,4,8,1280]{4,3,2,1,0:T(8,128)(2,1)S(1)}, bf16[2,1,4,8,1280]{4,3,2,1,0:T(8,128)(2,1)S(1)}, u32[]{:S(2)}, u32[]{:S(2)}) collective-permute-start(bf16[2,1,4,8,1280]{4,3,2,1,0:T(8,128)(2,1)S(1)} %get-tuple-element.200), channel_id=1, source_target_pairs={{0,2},{2,4},{4,6},{6,0},{1,3},{3,5},{5,7},{7,1},{8,10},{10,12},{12... | collective-permute-start | bytes 491528 | tf_op jit(solution)/shard_map/ppermute | solution.py:858
  28.4 9.8 %collective-permute-start.9 = (bf16[2,1,4,8,1280]{4,3,2,1,0:T(8,128)(2,1)S(1)}, bf16[2,1,4,8,1280]{4,3,2,1,0:T(8,128)(2,1)S(1)}, u32[]{:S(2)}, u32[]{:S(2)}) collective-permute-start(bf16[2,1,4,8,1280]{4,3,2,1,0:T(8,128)(2,1)S(1)} %get-tuple-element.201), channel_id=1, source_target_pairs={{2,0},{4,2},{6,4},{0,6},{3,1},{5,3},{7,5},{1,7},{10,8},{12,10},{14... | collective-permute-start | bytes 491528 | tf_op jit(solution)/shard_map/ppermute | solution.py:859
  31.6 6.6 %slice-start = ((bf16[2,2,4,8,2304]{4,3,2,1,0:T(8,128)(2,1)}), bf16[2,2,4,8,1280]{4,3,2,1,0:T(8,128)(2,1)S(1)}, s32[]{:S(2)}) async-start(bf16[2,2,4,8,2304]{4,3,2,1,0:T(8,128)(2,1)} %copy-done.15), calls=%async_computation | async-start | bytes 655360 | tf_op jit(solution)/shard_map/slice | solution.py:961
  35.3 7.5 %copy-start.13 = (f32[4,128]{1,0:T(4,128)S(1)}, f32[4,128]{1,0:T(4,128)}, u32[]{:S(2)}) copy-start(f32[4,128]{1,0:T(4,128)} %nw_ref.1) | copy-start | bytes 6148
  38.3 8.2 %collective-permute-start.10 = (bf16[2,1,4,8,1024]{4,3,2,1,0:T(8,128)(2,1)S(1)}, bf16[2,1,4,8,1024]{4,3,2,1,0:T(8,128)(2,1)S(1)}, u32[]{:S(2)}, u32[]{:S(2)}) collective-permute-start(bf16[2,1,4,8,1024]{4,3,2,1,0:T(8,128)(2,1)S(1)} %get-tuple-element.206), channel_id=1, source_target_pairs={{0,2},{2,4},{4,6},{6,0},{1,3},{3,5},{5,7},{7,1},{8,10},{10,12},{12... | collective-permute-start | bytes 393224 | tf_op jit(solution)/shard_map/ppermute | solution.py:858
  38.9 8.0 %collective-permute-start.11 = (bf16[2,1,4,8,1024]{4,3,2,1,0:T(8,128)(2,1)S(1)}, bf16[2,1,4,8,1024]{4,3,2,1,0:T(8,128)(2,1)S(1)}, u32[]{:S(2)}, u32[]{:S(2)}) collective-permute-start(bf16[2,1,4,8,1024]{4,3,2,1,0:T(8,128)(2,1)S(1)} %get-tuple-element.207), channel_id=1, source_target_pairs={{2,0},{4,2},{6,4},{0,6},{3,1},{5,3},{7,5},{1,7},{10,8},{12,10},{14... | collective-permute-start | bytes 393224 | tf_op jit(solution)/shard_map/ppermute | solution.py:859
  42.2 7.6 %collective-permute-start.15 = (bf16[1,4,4,8,1280]{4,3,2,1,0:T(8,128)(2,1)S(1)}, bf16[1,4,4,8,1280]{4,3,2,1,0:T(8,128)(2,1)S(1)}, u32[]{:S(2)}, u32[]{:S(2)}) collective-permute-start(bf16[1,4,4,8,1280]{4,3,2,1,0:T(8,128)(2,1)S(1)} %get-tuple-element.198), channel_id=1, source_target_pairs={{8,0},{16,8},{24,16},{0,24},{9,1},{17,9},{25,17},{1,25},{10,2},{18... | collective-permute-start | bytes 983048 | tf_op jit(solution)/shard_map/ppermute | solution.py:859
  42.3 10.1 %collective-permute-start.14 = (bf16[1,4,4,8,1280]{4,3,2,1,0:T(8,128)(2,1)S(1)}, bf16[1,4,4,8,1280]{4,3,2,1,0:T(8,128)(2,1)S(1)}, u32[]{:S(2)}, u32[]{:S(2)}) collective-permute-start(bf16[1,4,4,8,1280]{4,3,2,1,0:T(8,128)(2,1)S(1)} %get-tuple-element.199), channel_id=1, source_target_pairs={{0,8},{8,16},{16,24},{24,0},{1,9},{9,17},{17,25},{25,1},{2,10},{10... | collective-permute-start | bytes 983048 | tf_op jit(solution)/shard_map/ppermute | solution.py:858
  47.0 8.8 %collective-permute-start.13 = (bf16[1,4,4,8,1024]{4,3,2,1,0:T(8,128)(2,1)S(1)}, bf16[1,4,4,8,1024]{4,3,2,1,0:T(8,128)(2,1)S(1)}, u32[]{:S(2)}, u32[]{:S(2)}) collective-permute-start(bf16[1,4,4,8,1024]{4,3,2,1,0:T(8,128)(2,1)S(1)} %get-tuple-element.202), channel_id=1, source_target_pairs={{8,0},{16,8},{24,16},{0,24},{9,1},{17,9},{25,17},{1,25},{10,2},{18... | collective-permute-start | bytes 786440 | tf_op jit(solution)/shard_map/ppermute | solution.py:859
  47.6 10.0 %collective-permute-start.12 = (bf16[1,4,4,8,1024]{4,3,2,1,0:T(8,128)(2,1)S(1)}, bf16[1,4,4,8,1024]{4,3,2,1,0:T(8,128)(2,1)S(1)}, u32[]{:S(2)}, u32[]{:S(2)}) collective-permute-start(bf16[1,4,4,8,1024]{4,3,2,1,0:T(8,128)(2,1)S(1)} %get-tuple-element.203), channel_id=1, source_target_pairs={{0,8},{8,16},{16,24},{24,0},{1,9},{9,17},{17,25},{25,1},{2,10},{10... | collective-permute-start | bytes 786440 | tf_op jit(solution)/shard_map/ppermute | solution.py:858
  63.1 3.1 %collective-permute-start.16 = (f32[8,128]{1,0:T(8,128)S(1)}, f32[8,128]{1,0:T(8,128)S(1)}, u32[]{:S(2)}, u32[]{:S(2)}) collective-permute-start(f32[8,128]{1,0:T(8,128)S(1)} %get-tuple-element.167), channel_id=1, source_target_pairs={{0,8},{8,16},{16,24},{24,0},{1,9},{9,17},{17,25},{25,1},{2,10},{10... | collective-permute-start | bytes 12296 | tf_op jit(solution)/shard_map/ppermute | solution.py:905
  63.2 3.1 %collective-permute-start.17 = (f32[8,128]{1,0:T(8,128)S(1)}, f32[8,128]{1,0:T(8,128)S(1)}, u32[]{:S(2)}, u32[]{:S(2)}) collective-permute-start(f32[8,128]{1,0:T(8,128)S(1)} %get-tuple-element.168), channel_id=1, source_target_pairs={{8,0},{16,8},{24,16},{0,24},{9,1},{17,9},{25,17},{1,25},{10,2},{18... | collective-permute-start | bytes 12296 | tf_op jit(solution)/shard_map/ppermute | solution.py:906
  66.2 3.7 %collective-permute-start.19 = (f32[8,256]{1,0:T(8,128)S(1)}, f32[8,256]{1,0:T(8,128)S(1)}, u32[]{:S(2)}, u32[]{:S(2)}) collective-permute-start(f32[8,256]{1,0:T(8,128)S(1)} %add.3.mid_ref), channel_id=1, source_target_pairs={{2,0},{4,2},{6,4},{0,6},{3,1},{5,3},{7,5},{1,7},{10,8},{12,10},{14... | collective-permute-start | bytes 24584 | tf_op jit(solution)/shard_map/ppermute | solution.py:912
  66.5 5.4 %collective-permute-start.18 = (f32[8,256]{1,0:T(8,128)S(1)}, f32[8,256]{1,0:T(8,128)S(1)}, u32[]{:S(2)}, u32[]{:S(2)}) collective-permute-start(f32[8,256]{1,0:T(8,128)S(1)} %add.3.mid_ref), channel_id=1, source_target_pairs={{0,2},{2,4},{4,6},{6,0},{1,3},{3,5},{5,7},{7,1},{8,10},{10,12},{12... | collective-permute-start | bytes 24584 | tf_op jit(solution)/shard_map/ppermute | solution.py:912
  72.1 4.3 %collective-permute-start.20 = (f32[8,256]{1,0:T(8,128)S(1)}, f32[8,256]{1,0:T(8,128)S(1)}, u32[]{:S(2)}, u32[]{:S(2)}) collective-permute-start(f32[8,256]{1,0:T(8,128)S(1)} %fold.1.mid_ref), channel_id=1, source_target_pairs={{0,1},{1,0},{2,3},{3,2},{4,5},{5,4},{6,7},{7,6},{8,9},{9,8},{10,11... | collective-permute-start | bytes 24584 | tf_op jit(solution)/shard_map/ppermute | solution.py:921
  (14 other events, 40.8 us)

commit v7 on v6

--- a/solution.py
+++ b/solution.py
@@ -23,7 +23,7 @@
     (3, 3), (3, 3), (3, 3), (3, 4),
     (4, 4), (4, 4), (4, 4), (4, 4),
 )
-GROUPS = ((0, 3), (3, 8), (8, 12))
+GROUPS = ((0, 3), (3, 12))
 KINDS = tuple(sorted({PAIR_DEGREES[pair] for pair in range(*group)}) for group in GROUPS)
 DEGREES = tuple(sorted({d for both in kinds for d in both}) for kinds in KINDS)
 GROUP_COLS = tuple(2 * CH * (end - begin) for begin, end in GROUPS)
@@ -68,22 +68,11 @@
 
 
 def cells_kernel(
-    feat_hbm, pos_hbm, near_hbm, counts_hbm, order_hbm,
-    first_ref, own_pos_ref, meta_ref, pick_ref,
-    feat_ref, pos_ref, near_ref, counts_ref, order_ref, rows_ref, pos_rows, sems,
+    feat_ref, pos_ref, near_ref, counts_ref, order_ref,
+    first_ref, own_pos_ref, meta_ref, pick_ref, rows_ref, pos_rows,
 ):
-    args = (pos_hbm, near_hbm, counts_hbm, order_hbm, feat_hbm)
-    held = (pos_ref, near_ref, counts_ref, order_ref, feat_ref)
-    copies = [
-        pltpu.make_async_copy(arg, ref, sems.at[index])
-        for index, (arg, ref) in enumerate(zip(args, held))
-    ]
-    for copy in copies:
-        copy.start()
     rows_ref[...] = jnp.zeros_like(rows_ref)
     pos_rows[...] = jnp.zeros_like(pos_rows)
-    for copy in copies[:4]:
-        copy.wait()
     atoms = feat_ref.shape[0]
     rows_ref[0:SLOTS, :] = near_ref[...].astype(F32)
     rows_ref[SLOTS : SLOTS + 1, :] = counts_ref[...].astype(F32)
@@ -104,7 +93,6 @@
     own_pos_ref[...] = mm_nt(same, pieces).astype(BF16)
     first_ref[:, CH : 2 * CH] = mm_nt(pick, pieces).astype(BF16)
     pick_ref[...] = pick
-    copies[4].wait()
     first_ref[:, 0:CH] = mm(pick, feat_ref[:, 0:CH]).astype(BF16)
     cut = pair_cols(GROUPS[1][0]).start
     first_ref[:, 2 * CH :] = mm(pick, feat_ref[:, CH:cut]).astype(BF16)
@@ -124,13 +112,8 @@
         struct(atoms, atoms, dtype=BF16),
     )
     args = (feats, places, near, counts, order)
-    scratch = [pltpu.VMEM(arg.shape, arg.dtype) for arg in args]
-    scratch += [pltpu.VMEM((CH, atoms), F32), pltpu.VMEM((CH, atoms), F32)]
-    scratch += [pltpu.SemaphoreType.DMA((5,))]
-    specs = [pl.BlockSpec(memory_space=pl.ANY)] * 5
-    first, own_pos, meta, pick = call(
-        cells_kernel, "cells", out_shape, scratch, 1 << 26, args, specs
-    )
+    scratch = [pltpu.VMEM((CH, atoms), F32), pltpu.VMEM((CH, atoms), F32)]
+    first, own_pos, meta, pick = call(cells_kernel, "cells", out_shape, scratch, 1 << 26, args)
     out_shape = (struct(atoms, sum(GROUP_COLS[1:]), dtype=BF16),)
     rest = call(rest_kernel, "cells_rest", out_shape, [], 1 << 26, (feats, pick))[0]
     return first, rest, own_pos, meta
@@ -729,25 +712,24 @@
 
 
 def third_kernel(
-    low_ref, mid_ref, high_ref, own_ref, meta_ref, mix_ref, out_ref, nw_ref, oh_gh, d_gh, dt_gh,
-    gate_gh, acc_own, radial_gh4,
-    radt_ref, rbft_ref, mixt_ref, gs0_ref, en_0, en_a, en_b, new_0, new_a, new_b, pre_gh, unit_gh,
-    m0_ref, nf0_ref, dot_a, dot_b, *refs
+    p0, p1, p2, p3, p4, own_ref, meta_ref, mix_ref, out_ref, nw_ref, oh_gh, d_gh, dt_gh, gate_gh,
+    acc_own, radial_gh2, radial_gh3, radial_gh4,
+    radt_ref, rbft_ref, mixt_ref, gs0_ref, en_0, en_a, new_0, new_a, pre_gh, unit_gh,
+    m0_ref, nf0_ref, dot_a, gr1_a, gr2_a,
+    new_ref, energy_ref, src_ref, flow_ref, fmid_ref, fhigh_ref, gs_ref,
+    table, sems, wm, wmt, wo, wot, nf_s, mx_s, acc_s, dot_c, gr2_c, gr3_c, gr4_c, en_s, fgh_s,
 ):
-    gr_gh, refs = refs[: PARTIALS - 1], refs[PARTIALS - 1 :]
-    (
-        new_ref, energy_ref, src_ref, flow_ref, fmid_ref, fhigh_ref, gs_ref,
-        table, sems, wm, wmt, wo, wot, nf_s, mx_s, acc_s, dot_c, gr_c, en_s, fgh_s,
-    ) = refs
-    group = 2
-    copies = fetch((low_ref, mid_ref, high_ref), slice(0, GROUP_COLS[group]), table, sems)
+    group = 1
+    radials = {2: radial_gh2, 3: radial_gh3, 4: radial_gh4}
+    grads = {2: gr2_c, 3: gr3_c, 4: gr4_c}
+    copies = fetch((p0, p1, p2, p3, p4), slice(0, GROUP_COLS[group]), table, sems)
     atoms = own_ref.shape[0]
     spacing = spacing_of(atoms, rbft_ref.shape[1])
     block_diagonal(KINDS[group], mix_ref, wm, wmt)
     block_diagonal(KINDS[group], out_ref, wo, wot)
-    en_s[...] = en_0[...] + en_a[...] + en_b[...]
+    en_s[...] = en_0[...] + en_a[...]
     at = 0
-    for part in (new_0, new_a, new_b):
+    for part in (new_0, new_a):
         new_ref[:, at : at + part.shape[1]] = part[...]
         at += part.shape[1]
     steps = step_count(meta_ref)
@@ -755,8 +737,8 @@
     for copy in copies:
         copy.wait()
     ghost_pairs(
-        group, own_ref, table, new_ref, 0, oh_gh, d_gh, dt_gh, gate_gh, {4: radial_gh4}, nw_ref,
-        steps, wm, wmt, wo, wot, nf_s, mx_s, acc_own, acc_s, gs_ref, dot_c, {4: gr_c}, en_s,
+        group, own_ref, table, new_ref, 0, oh_gh, d_gh, dt_gh, gate_gh, radials, nw_ref,
+        steps, wm, wmt, wo, wot, nf_s, mx_s, acc_own, acc_s, gs_ref, dot_c, grads, en_s,
     )
     energy_ref[...] = jnp.sum(en_s[...].T, axis=0, keepdims=True)
 
@@ -768,8 +750,8 @@
         here, _ = ghost_rows(step)
         grad = mm(d_gh[here, :], gs0_low)
         pull, top, rest = finish(
-            grad, m0_ref[here, :], nf0_ref[here, :], sum_of((dot_a, dot_b, dot_c), here),
-            degree_parts(gr_gh + (gr_c,), here), pre_gh[here, :], unit_gh[here, :], spacing,
+            grad, m0_ref[here, :], nf0_ref[here, :], sum_of((dot_a, dot_c), here),
+            degree_parts((gr1_a, gr2_a, gr2_c, gr3_c, gr4_c), here), pre_gh[here, :], unit_gh[here, :], spacing,
             radt_ref, rbft_ref, mixt_ref,
         )
         pull_top = pull.astype(BF16)
@@ -789,16 +771,18 @@
 def third_stage(pieces, feats, *rest):
     atoms, feat = feats.shape
     half = atoms * HALF
-    sizes = [piece.shape[0] for piece in pieces]
-    ghosts = sum(sizes)
+    ghosts = sum(piece.shape[0] for piece in pieces)
+    sizes = (ghosts // 4, ghosts // 2, ghosts // 4)
     out_shape = (
         struct(atoms, feat, dtype=BF16),
         struct(1, atoms),
         struct(atoms, CH),
     ) + tuple(struct(8, size) for size in sizes) + (
-        struct(atoms, GROUP_COLS[2], dtype=BF16),
-    )
-    scratch = pair_scratch(atoms, half, ghosts, 2) + [
+        struct(atoms, GROUP_COLS[1], dtype=BF16),
+    )
+    scratch = pair_scratch(atoms, half, ghosts, 1) + [
+        pltpu.VMEM((half, CH), BF16),
+        pltpu.VMEM((half, CH), BF16),
         pltpu.VMEM((half, CH), BF16),
         pltpu.VMEM((half, CH), BF16),
         pltpu.VMEM((atoms, CH), F32),
@@ -806,14 +790,14 @@
     ]
     args = tuple(pieces) + (feats,) + rest
     return call(
-        third_kernel, "third_group", out_shape, scratch, 1 << 33, args, any_specs(3, len(args)),
-        24,
+        third_kernel, "third_group", out_shape, scratch, 1 << 33, args,
+        any_specs(len(pieces), len(args)), 28,
     )
 
 
 def own_back_kernel(
     oh_own, pre_own, unit_own, radt_ref, rbft_ref, mixt_ref, gs0_ref, src_ref,
-    m0_ref, nf0_ref, dot_a, dot_b, dot_c, *refs
+    m0_ref, nf0_ref, dot_a, dot_c, *refs
 ):
     gr_own, (force_ref,) = refs[:PARTIALS], refs[PARTIALS:]
     atoms = oh_own.shape[1]
@@ -824,7 +808,7 @@
     for step in range(OWN_STEPS):
         rows = own_rows(step)
         pull, top, rest = finish(
-            grad, m0_ref[rows, :], nf0_ref[rows, :], sum_of((dot_a, dot_b, dot_c), rows),
+            grad, m0_ref[rows, :], nf0_ref[rows, :], sum_of((dot_a, dot_c), rows),
             degree_parts(gr_own, rows), pre_own[rows, :], unit_own[rows, :], spacing, radt_ref,
             rbft_ref, mixt_ref,
         )
@@ -865,9 +849,12 @@
     return jnp.concatenate([before, block, after], axis=dim)
 
 
-def ghost_pieces(block):
-    before, after = neighbours_of(block, "gx", 0)
-    return tuple(flat_rows(piece) for piece in (before, block, after))
+def ghost_pieces(along_y, block, along_x):
+    outer = jnp.concatenate(along_y, axis=1)
+    low_out, high_out = neighbours_of(outer, "gx", 0)
+    low_in, high_in = along_x
+    middle = jnp.concatenate([along_y[0], block, along_y[1]], axis=1)
+    return tuple(flat_rows(piece) for piece in (low_in, low_out, middle, high_in, high_out))
 
 
 def flat_rows(piece):
@@ -937,64 +924,54 @@
 ):
     feats = features[0, 0, 0]
     places = jnp.swapaxes(positions[0, 0], 0, 1)
-    cells0, cells12, own_pos, meta = make_cells(
+    cells0, cells1, own_pos, meta = make_cells(
         feats, places, neighbours[0, 0, 0].T, counts[0, 0], cell_atoms[0, 0]
     )
     hold = lax.optimization_barrier
-    block0, block12 = (part.reshape(2, 2, 2, 8, part.shape[1]) for part in (cells0, cells12))
+    block0, block1 = (part.reshape(2, 2, 2, 8, part.shape[1]) for part in (cells0, cells1))
     block0 = grown(block0, "gz", 2)
+    block0, own_pos, meta = hold((block0, own_pos, meta))
+    y0 = neighbours_of(block0, "gy", 1)
+    x0_in = neighbours_of(block0, "gx", 0)
     oh_own, pre_own, unit_own, radt, rbft, mixt, home, *radial_own = own_stage(
         meta, own_pos, rbf_weight, radial_weight, mix_weight
     )
-    block0, oh_own = hold((block0, oh_own))
-    y_low, y_high = neighbours_of(block0, "gy", 1)
-    low_in, high_in = neighbours_of(block0, "gx", 0)
-    block12 = grown(block12, "gz", 2)
-    (m0_own, gate_own, nf0_own, acc0), (own_a, own_b) = own_forward_stage(
-        (0, 1), feats, mix_weight, oh_own, radial_own
-    )
-    y_low, y_high, block12, gate_own = hold((y_low, y_high, block12, gate_own))
-    outer = jnp.concatenate([y_low, y_high], axis=1)
-    low_out, high_out = neighbours_of(outer, "gx", 0)
-    middle = jnp.concatenate([y_low, block0, y_high], axis=1)
-    pieces0 = tuple(flat_rows(p) for p in (low_in, low_out, middle, high_in, high_out))
-    block1, block2 = block12[..., : GROUP_COLS[1]], block12[..., GROUP_COLS[1] :]
-    block1 = grown(block1, "gy", 1)
-    _, (own_c,) = own_forward_stage((2,), feats, mix_weight, oh_own, radial_own, gate_own)
-    pieces0, acc_c = hold((pieces0, own_c[2]))
+    block1 = grown(block1, "gz", 2)
+    y1 = neighbours_of(block1, "gy", 1)
+    y0, block1, oh_own = hold((y0, block1, oh_own))
+    pieces0 = ghost_pieces(y0, block0, x0_in)
+    x1_in = neighbours_of(block1, "gx", 0)
+    (m0_own, gate_own, nf0_own, acc0), (own_a,) = own_forward_stage(
+        (0,), feats, mix_weight, oh_own, radial_own
+    )
     (
         new_0, oh_gh, d_gh, dt_gh, pre_gh, unit_gh, gs0, en_0, m0_gh, gate_gh, nf0_gh, *radial_gh,
     ) = start_stage(
         pieces0, feats, own_pos, meta, rbf_weight, radial_weight, mix_weight, out_weight,
         energy_weight[None], acc0,
     )
-    block1, block2, gate_gh = hold((block1, block2, gate_gh))
-    pieces1 = ghost_pieces(block1)
-    block2 = grown(block2, "gy", 1)
+    y1, gate_gh = hold((y1, gate_gh))
+    pieces1 = ghost_pieces(y1, block1, x1_in)
     shared = (feats, meta, mix_weight, out_weight, norm_weight, oh_gh, d_gh, dt_gh, gate_gh)
     new_a, en_a, _, (dot_gh_a, *gr_gh_a), (dot_own_a, *gr_own_a) = pairs_stage(
         0, 2 * CH, pieces0, shared, (gate_own, *own_a), radial_gh
     )
-    en_a, block2 = hold((en_a, block2))
-    pieces2 = ghost_pieces(block2)
-    new_b, en_b, gs_b, (dot_gh_b, *gr_gh_b), _ = pairs_stage(
-        1, 0, pieces1, shared, (gate_own, *own_b), radial_gh
-    )
-    new, energy, src, low, mid, high, gs_c = third_stage(
-        pieces2, *shared, acc_c, radial_gh[3], radt, rbft, mixt, gs0, en_0, en_a, en_b, new_0,
-        new_a, new_b, pre_gh, unit_gh, m0_gh, nf0_gh, dot_gh_a, dot_gh_b, *gr_gh_a, *gr_gh_b,
+    en_a, gate_own = hold((en_a, gate_own))
+    _, (own_b,) = own_forward_stage((1,), feats, mix_weight, oh_own, radial_own, gate_own)
+    new, energy, src, low, mid, high, gs_b = third_stage(
+        pieces1, *shared, own_b[2], *radial_gh[1:], radt, rbft, mixt, gs0, en_0, en_a, new_0,
+        new_a, pre_gh, unit_gh, m0_gh, nf0_gh, dot_gh_a, *gr_gh_a,
     )
     mid, arrived = give_back_x(low, mid, high)
-    dot_own_c, *gr_own_c = own_backward_stage(2, mix_weight, gs_c, gate_own, *own_c[:2])
-    arrived, gs_b, dot_own_c = hold((arrived, gs_b, dot_own_c))
+    dot_own_b, *gr_own_b = own_backward_stage(1, mix_weight, gs_b, gate_own, *own_b[:2])
+    arrived, gs0, dot_own_b = hold((arrived, gs0, dot_own_b))
     mid, from_low, from_high = give_back_y(mid + arrived)
-    dot_own_b, *gr_own_b = own_backward_stage(1, mix_weight, gs_b, gate_own, *own_b[:2])
-    from_low, from_high, gs0, dot_own_b = hold((from_low, from_high, gs0, dot_own_b))
-    folded = give_back_z(fold(mid, from_low, from_high))
     own = own_back_stage(
         oh_own, pre_own, unit_own, radt, rbft, mixt, gs0, src, m0_own, nf0_own, dot_own_a,
-        dot_own_b, dot_own_c, *gr_own_a, *gr_own_b, *gr_own_c,
-    )
+        dot_own_b, *gr_own_a, *gr_own_b,
+    )
+    from_low, from_high, own = hold((from_low, from_high, own))
+    folded = give_back_z(fold(mid, from_low, from_high))
     args = (*folded, own, home)
     out_shape = (struct(3, 1, own.shape[1]),)
     forces = call(forces_kernel, "forces", out_shape, [], 1 << 20, args)[0]

time: 77.5 us -> 79.3 us (1.023)
  waiting for transfers between devices: 14.7 us -> 19.9 us
  local copies, waits for them, and re-layouts: 6.73 us -> 4.01 us
  Pallas kernels: 31.8 us -> 30.7 us
    ppermute x2, waiting for transfers between devices: 0.01 us -> 3.99 us  [neighbours_of(): other = lax.ppermute(block, axis, up)]
    ppermute x7 -> x6, starting transfers between devices: 11.4 us -> 8.3 us  [neighbours_of(): after = lax.ppermute(lax.slice_in_dim(block, 0, 1, axis=dim), axis, down)]
    unnamed x33 -> x26, local copies, waits for them, and re-layouts: 6.48 us -> 3.77 us
    ppermute x2, waiting for transfers between devices: 2.38 us -> 0.01 us  [give_back_y(): return (mid, lax.ppermute(mid, 'gy', up), lax.ppermute(mid, 'gy', down))]
    ppermute x1, waiting for transfers between devices: 0.01 us -> 2.15 us  [give_back_z(): from_low = lax.ppermute(mid, 'gz', up)]
    ppermute x2, starting transfers between devices: 2.04 us -> 3.88 us  [give_back_y(): return (mid, lax.ppermute(mid, 'gy', up), lax.ppermute(mid, 'gy', down))]
    ppermute x7 -> x6, starting transfers between devices: 2.75 us -> 4.48 us  [neighbours_of(): lax.ppermute(lax.slice_in_dim(block, length - 1, length, axis=dim), axis,...]
    ppermute x7 -> x6, waiting for transfers between devices: 6.54 us -> 7.9 us  [neighbours_of(): lax.ppermute(lax.slice_in_dim(block, length - 1, length, axis=dim), axis,...]
  transfers between devices with their start and end apart: 21 -> 19, of which waited for: 10 -> 6; matrix products, arithmetic and copies ran while one was open for 1% -> 1% of each run, Pallas kernels for 32% -> 27%
where the time goes in v7:
time: 79.3 us; the launch traced here: 79 us
  Pallas kernels  30.7 us (39%)
  starting transfers between devices  23.1 us (29%)
  waiting for transfers between devices  19.9 us (25%)
  local copies, waits for them, and re-layouts  4.01 us (5%)
  between operations  0.99 us (1%)
    pallas_call x12, Pallas kernels, call(): pl.pallas_call(kernel, out_shape=out_shape, in_specs=specs or [pl.BlockSp...  30.7 us
    ppermute x6, starting transfers between devices, neighbours_of(): after = lax.ppermute(lax.slice_in_dim(block, 0, 1, axis=dim), axis, down)  8.3 us
    ppermute x6, waiting for transfers between devices, neighbours_of(): lax.ppermute(lax.slice_in_dim(block, length - 1, length, axis=dim), axis,...  7.9 us
    ppermute x6, waiting for transfers between devices, neighbours_of(): after = lax.ppermute(lax.slice_in_dim(block, 0, 1, axis=dim), axis, down)  5.87 us
    ppermute x6, starting transfers between devices, neighbours_of(): lax.ppermute(lax.slice_in_dim(block, length - 1, length, axis=dim), axis,...  4.48 us
    ppermute x2, waiting for transfers between devices, neighbours_of(): other = lax.ppermute(block, axis, up)  3.99 us
    ppermute x2, starting transfers between devices, give_back_y(): return (mid, lax.ppermute(mid, 'gy', up), lax.ppermute(mid, 'gy', down))  3.88 us
    unnamed x26, local copies, waits for them, and re-layouts  3.77 us
  transfers between devices with their start and end apart: 19, of which 6 were waited for; matrix products, arithmetic and copies ran while one was open for 1% of the time, Pallas kernels for 27%

profile of v7, /device:TPU:0, one launch (start us, length us, event | category | flops | bytes accessed | tf_op | source)
XLA Modules:
  0.0 79.0 jit_solution(10081117754151440715)
XLA Ops:
  0.6 1.0 %copy-done = bf16[1,1,1,64,3200]{4,3,2,1,0:T(8,128)(2,1)S(1)} copy-done((bf16[1,1,1,64,3200]{4,3,2,1,0:T(8,128)(2,1)S(1)}, bf16[1,1,1,64,3200]{4,3,2,1,0:T(8,128)(2,1)}, u32[]{:S(2)}) %copy-start) | copy-done | bytes 409624
  4.7 3.0 %collective-permute-start = (bf16[2,2,2,8,1024]{4,3,2,1,0:T(8,128)(2,1)S(1)}, bf16[2,2,2,8,1024]{4,3,2,1,0:T(8,128)(2,1)S(1)}, u32[]{:S(2)}, u32[]{:S(2)}) collective-permute-start(bf16[2,2,2,8,1024]{4,3,2,1,0:T(8,128)(2,1)S(1)} %bitcast.37), channel_id=1, source_target_pairs={{0,1},{1,0},{2,3},{3,2},{4,5},{5,4},{6,7},{7,6},{8,9},{9,8},{10,11... | collective-permute-start | bytes 393224 | tf_op jit(solution)/shard_map/ppermute | solution.py:837
  8.0 4.0 %collective-permute-done = bf16[2,2,2,8,1024]{4,3,2,1,0:T(8,128)(2,1)S(1)} collective-permute-done((bf16[2,2,2,8,1024]{4,3,2,1,0:T(8,128)(2,1)S(1)}, bf16[2,2,2,8,1024]{4,3,2,1,0:T(8,128)(2,1)S(1)}, u32[]{:S(2)}, u32[]{:S(2)}) %collective-permute-start) | collective-permute-done | bytes 131104 | tf_op jit(solution)/shard_map/ppermute | solution.py:837
  12.1 2.2 %collective-permute-start.1 = (bf16[2,1,4,8,1024]{4,3,2,1,0:T(8,128)(2,1)S(1)}, bf16[2,1,4,8,1024]{4,3,2,1,0:T(8,128)(2,1)S(1)}, u32[]{:S(2)}, u32[]{:S(2)}) collective-permute-start(bf16[2,1,4,8,1024]{4,3,2,1,0:T(8,128)(2,1)S(1)} %get-tuple-element.175), channel_id=1, source_target_pairs={{0,2},{2,4},{4,6},{6,0},{1,3},{3,5},{5,7},{7,1},{8,10},{10,12},{12... | collective-permute-start | bytes 393224 | tf_op jit(solution)/shard_map/ppermute | solution.py:842
  14.3 2.1 %collective-permute-start.2 = (bf16[2,1,4,8,1024]{4,3,2,1,0:T(8,128)(2,1)S(1)}, bf16[2,1,4,8,1024]{4,3,2,1,0:T(8,128)(2,1)S(1)}, u32[]{:S(2)}, u32[]{:S(2)}) collective-permute-start(bf16[2,1,4,8,1024]{4,3,2,1,0:T(8,128)(2,1)S(1)} %get-tuple-element.174), channel_id=1, source_target_pairs={{2,0},{4,2},{6,4},{0,6},{3,1},{5,3},{7,5},{1,7},{10,8},{12,10},{14... | collective-permute-start | bytes 393224 | tf_op jit(solution)/shard_map/ppermute | solution.py:843
  16.9 2.9 %own_edges.1 = (bf16[1024,64]{1,0:T(8,128)(2,1)S(1)}, bf16[1024,128]{1,0:T(8,128)(2,1)S(1)}, f32[1024,128]{1,0:T(8,128)S(1)}, bf16[640,128]{1,0:T(8,128)(2,1)S(1...) custom-call(f32[64,128]{1,0:T(8,128)S(1)} %get-tuple-element.86.meta, ...), custom_call_target="tpu_custom_call" | custom-call | flops 2147483648 | bytes 3096576 | tf_op jit(solution)/shard_map/own_edges/pallas_call | solution.py:58
  21.4 1.2 %collective-permute-start.10 = (bf16[1,2,4,8,1024]{4,3,2,1,0:T(8,128)(2,1)S(1)}, bf16[1,2,4,8,1024]{4,3,2,1,0:T(8,128)(2,1)S(1)}, u32[]{:S(2)}, u32[]{:S(2)}) collective-permute-start(bf16[1,2,4,8,1024]{4,3,2,1,0:T(8,128)(2,1)S(1)} %get-tuple-element.170), channel_id=1, source_target_pairs={{8,0},{16,8},{24,16},{0,24},{9,1},{17,9},{25,17},{1,25},{10,2},{18... | collective-permute-start | bytes 393224 | tf_op jit(solution)/shard_map/ppermute | solution.py:843
  23.2 2.4 %own_forward_a.1 = (bf16[1024,128]{1,0:T(8,128)(2,1)S(1)}, bf16[1024,128]{1,0:T(8,128)(2,1)S(1)}, bf16[1024,128]{1,0:T(8,128)(2,1)S(1)}, f32[64,128]{1,0:T(8,128...) custom-call(bf16[64,3200]{1,0:T(8,128)(2,1)S(1)} %bitcast.27, ...), custom_call_target="tpu_custom_call" | custom-call | flops 4294967296 | bytes 6176768 | tf_op jit(solution)/shard_map/own_forward_a/pallas_call | solution.py:58
  25.6 3.3 %collective-permute-start.6 = (bf16[2,1,4,8,2304]{4,3,2,1,0:T(8,128)(2,1)S(1)}, bf16[2,1,4,8,2304]{4,3,2,1,0:T(8,128)(2,1)S(1)}, u32[]{:S(2)}, u32[]{:S(2)}) collective-permute-start(bf16[2,1,4,8,2304]{4,3,2,1,0:T(8,128)(2,1)S(1)} %get-tuple-element.166), channel_id=1, source_target_pairs={{2,0},{4,2},{6,4},{0,6},{3,1},{5,3},{7,5},{1,7},{10,8},{12,10},{14... | collective-permute-start | bytes 884744 | tf_op jit(solution)/shard_map/ppermute | solution.py:843
  29.5 3.4 %ghost_start.1 = (bf16[64,128]{1,0:T(8,128)(2,1)S(1)}, bf16[1024,512]{1,0:T(8,128)(2,1)S(1)}, bf16[1024,64]{1,0:T(8,128)(2,1)S(1)}, bf16[64,1024]{1,0:T(8,128)(2...) custom-call(bf16[64,1024]{1,0:T(8,128)(2,1)S(1)} %bitcast.49, ...), custom_call_target="tpu_custom_call" | custom-call | flops 2147483648 | bytes 6177280 | tf_op jit(solution)/shard_map/ghost_start/pallas_call | solution.py:58
  33.0 1.3 %collective-permute-done.5 = bf16[2,1,4,8,2304]{4,3,2,1,0:T(8,128)(2,1)S(1)} collective-permute-done((bf16[2,1,4,8,2304]{4,3,2,1,0:T(8,128)(2,1)S(1)}, bf16[2,1,4,8,2304]{4,3,2,1,0:T(8,128)(2,1)S(1)}, u32[]{:S(2)}, u32[]{:S(2)}) %collective-permute-start.5) | collective-permute-done | bytes 294944 | tf_op jit(solution)/shard_map/ppermute | solution.py:842
  34.3 5.2 %collective-permute-done.6 = bf16[2,1,4,8,2304]{4,3,2,1,0:T(8,128)(2,1)S(1)} collective-permute-done((bf16[2,1,4,8,2304]{4,3,2,1,0:T(8,128)(2,1)S(1)}, bf16[2,1,4,8,2304]{4,3,2,1,0:T(8,128)(2,1)S(1)}, u32[]{:S(2)}, u32[]{:S(2)}) %collective-permute-start.6) | collective-permute-done | bytes 294944 | tf_op jit(solution)/shard_map/ppermute | solution.py:843
  39.4 3.5 %pairs_a.1 = (bf16[64,768]{1,0:T(8,128)(2,1)S(1)}, f32[64,128]{1,0:T(8,128)S(1)}, bf16[64,768]{1,0:T(8,128)(2,1)}, bf16[1024,128]{1,0:T(8,128)(2,1)S(1)}, bf16[1...) custom-call(bf16[64,1024]{1,0:T(8,128)(2,1)S(1)} %bitcast.50, ...), custom_call_target="tpu_custom_call" | custom-call | flops 8589934592 | bytes 9324544 | tf_op jit(solution)/shard_map/pairs_a/pallas_call | solution.py:58
  42.9 3.5 %own_forward_b.1 = (bf16[1024,2304]{1,0:T(8,128)(2,1)S(1)}, bf16[1024,2304]{1,0:T(8,128)(2,1)S(1)}, f32[64,2304]{1,0:T(8,128)S(1)}) custom-call(bf16[64,3200]{1,0:T(8,128)(2,1)S(1)} %bitcast.30, bf16[5,128,128]{2,1,0:T(8,128)(2,1)S(1)} %copy-done.8, bf16[1024,64]{1,0:T(8,128)(2,1)S(1)} %get-tuple-element.92.refs_2_.oh_own, ...), custom_call_target="tpu_custom_call" | custom-call | flops 4294967296 | bytes 12304384 | tf_op jit(solution)/shard_map/own_forward_b/pallas_call | solution.py:58
  46.6 1.7 %collective-permute-start.13 = (bf16[1,2,4,8,2304]{4,3,2,1,0:T(8,128)(2,1)S(1)}, bf16[1,2,4,8,2304]{4,3,2,1,0:T(8,128)(2,1)S(1)}, u32[]{:S(2)}, u32[]{:S(2)}) collective-permute-start(bf16[1,2,4,8,2304]{4,3,2,1,0:T(8,128)(2,1)S(1)} %get-tuple-element.162), channel_id=1, source_target_pairs={{8,0},{16,8},{24,16},{0,24},{9,1},{17,9},{25,17},{1,25},{10,2},{18... | collective-permute-start | bytes 884744 | tf_op jit(solution)/shard_map/ppermute | solution.py:843
  48.5 6.6 %collective-permute-done.11 = bf16[1,2,4,8,2304]{4,3,2,1,0:T(8,128)(2,1)S(1)} collective-permute-done((bf16[1,2,4,8,2304]{4,3,2,1,0:T(8,128)(2,1)S(1)}, bf16[1,2,4,8,2304]{4,3,2,1,0:T(8,128)(2,1)S(1)}, u32[]{:S(2)}, u32[]{:S(2)}) %collective-permute-start.11) | collective-permute-done | bytes 294944 | tf_op jit(solution)/shard_map/ppermute | solution.py:842
  55.1 8.5 %third_group.1 = (bf16[64,3200]{1,0:T(8,128)(2,1)}, f32[1,64]{1,0:T(1,128)}, f32[64,128]{1,0:T(8,128)S(1)}, f32[8,128]{1,0:T(8,128)S(1)}, f32[8,256]{1,0:T(8,128...) custom-call(bf16[64,2304]{1,0:T(8,128)(2,1)S(1)} %bitcast.44, bf16[64,2304]{1,0:T(8,128)(2,1)S(1)} %bitcast.45, ...), custom_call_target="tpu_custom_call" | custom-call | flops 8589934592 | bytes 9472256 | tf_op jit(solution)/shard_map/third_group/pallas_call | solution.py:58
  64.2 1.1 %collective-permute-start.15 = (f32[8,128]{1,0:T(8,128)S(1)}, f32[8,128]{1,0:T(8,128)S(1)}, u32[]{:S(2)}, u32[]{:S(2)}) collective-permute-start(f32[8,128]{1,0:T(8,128)S(1)} %get-tuple-element.136), channel_id=1, source_target_pairs={{8,0},{16,8},{24,16},{0,24},{9,1},{17,9},{25,17},{1,25},{10,2},{18... | collective-permute-start | bytes 12296 | tf_op jit(solution)/shard_map/ppermute | solution.py:893
  65.4 2.4 %own_backward_b.1 = (bf16[1024,128]{1,0:T(8,128)(2,1)S(1)}, bf16[1024,128]{1,0:T(8,128)(2,1)S(1)}, bf16[1024,128]{1,0:T(8,128)(2,1)S(1)}, bf16[1024,128]{1,0:T(8,128)(2,1)S(1)}) custom-call(bf16[5,128,128]{2,1,0:T(8,128)(2,1)S(1)} %copy-done.8, bf16[64,2304]{1,0:T(8,128)(2,1)S(1)} %get-tuple-element.137.gs_ref, ...), custom_call_target="tpu_custom_call" | custom-call | flops 4294967296 | bytes 11206656 | tf_op jit(solution)/shard_map/own_backward_b/pallas_call | solution.py:58
  68.4 3.3 %collective-permute-start.17 = (f32[8,256]{1,0:T(8,128)S(1)}, f32[8,256]{1,0:T(8,128)S(1)}, u32[]{:S(2)}, u32[]{:S(2)}) collective-permute-start(f32[8,256]{1,0:T(8,128)S(1)} %add.3.mid_ref), channel_id=1, source_target_pairs={{2,0},{4,2},{6,4},{0,6},{3,1},{5,3},{7,5},{1,7},{10,8},{12,10},{14... | collective-permute-start | bytes 24584 | tf_op jit(solution)/shard_map/ppermute | solution.py:899
  71.7 2.8 %own_back.1.own_ref = f32[8,64]{1,0:T(8,128)S(1)} custom-call(bf16[1024,64]{1,0:T(8,128)(2,1)S(1)} %get-tuple-element.92.refs_2_.oh_own, bf16[1024,128]{1,0:T(8,128)(2,1)S(1)} %get-tuple-element.142.pre_own, f32[1024,128]{1,0:T(8,128)S(1)} %get-tuple-element.143.unit_own, bf16[640,128]{1,0:T(8,128)(2,1)S(1)} %get-tuple-element.117.radt_ref, ...), custom_call_target="tpu_custom_call" | custom-call | flops 2147483648 | bytes 3672064 | tf_op jit(solution)/shard_map/own_back/pallas_call | solution.py:58
  74.6 1.5 %collective-permute-start.18 = (f32[8,256]{1,0:T(8,128)S(1)}, f32[8,256]{1,0:T(8,128)S(1)}, u32[]{:S(2)}, u32[]{:S(2)}) collective-permute-start(f32[8,256]{1,0:T(8,128)S(1)} %fold.1.mid_ref), channel_id=1, source_target_pairs={{0,1},{1,0},{2,3},{3,2},{4,5},{5,4},{6,7},{7,6},{8,9},{9,8},{10,11... | collective-permute-start | bytes 24584 | tf_op jit(solution)/shard_map/ppermute | solution.py:908
  76.1 2.1 %collective-permute-done.18.low_ref.high_ref = f32[8,256]{1,0:T(8,128)S(1)} collective-permute-done((f32[8,256]{1,0:T(8,128)S(1)}, f32[8,256]{1,0:T(8,128)S(1)}, u32[]{:S(2)}, u32[]{:S(2)}) %collective-permute-start.18) | collective-permute-done | bytes 8224 | tf_op jit(solution)/shard_map/ppermute | solution.py:908
  78.2 0.8 forces.1
  (68 shorter events, 8.4 us)
Async XLA Ops:
  4.7 7.4 %collective-permute-start = (bf16[2,2,2,8,1024]{4,3,2,1,0:T(8,128)(2,1)S(1)}, bf16[2,2,2,8,1024]{4,3,2,1,0:T(8,128)(2,1)S(1)}, u32[]{:S(2)}, u32[]{:S(2)}) collective-permute-start(bf16[2,2,2,8,1024]{4,3,2,1,0:T(8,128)(2,1)S(1)} %bitcast.37), channel_id=1, source_target_pairs={{0,1},{1,0},{2,3},{3,2},{4,5},{5,4},{6,7},{7,6},{8,9},{9,8},{10,11... | collective-permute-start | bytes 393224 | tf_op jit(solution)/shard_map/ppermute | solution.py:837
  7.7 9.2 %copy-start.6 = (bf16[128,640]{1,0:T(8,128)(2,1)S(1)}, bf16[128,640]{1,0:T(8,128)(2,1)}, u32[]{:S(2)}) copy-start(bf16[128,640]{1,0:T(8,128)(2,1)} %rad_ref.3) | copy-start | bytes 491524
  7.7 9.2 %copy-start.8 = (bf16[5,128,128]{2,1,0:T(8,128)(2,1)S(1)}, bf16[5,128,128]{2,1,0:T(8,128)(2,1)}, u32[]{:S(2)}) copy-start(bf16[5,128,128]{2,1,0:T(8,128)(2,1)} %mix_ref.7) | copy-start | bytes 491524
  7.7 9.2 %copy-start.9 = (bf16[512,128]{1,0:T(8,128)(2,1)S(1)}, bf16[512,128]{1,0:T(8,128)(2,1)}, u32[]{:S(2)}) copy-start(bf16[512,128]{1,0:T(8,128)(2,1)} %rbf_ref.3) | copy-start | bytes 393220
  7.9 11.9 %collective-permute-start.3 = (bf16[2,2,2,8,2304]{4,3,2,1,0:T(8,128)(2,1)S(1)}, bf16[2,2,2,8,2304]{4,3,2,1,0:T(8,128)(2,1)S(1)}, u32[]{:S(2)}, u32[]{:S(2)}) collective-permute-start(bf16[2,2,2,8,2304]{4,3,2,1,0:T(8,128)(2,1)S(1)} %bitcast.33), channel_id=1, source_target_pairs={{0,1},{1,0},{2,3},{3,2},{4,5},{5,4},{6,7},{7,6},{8,9},{9,8},{10,11... | collective-permute-start | bytes 884744 | tf_op jit(solution)/shard_map/ppermute | solution.py:837
  12.1 7.8 %collective-permute-start.1 = (bf16[2,1,4,8,1024]{4,3,2,1,0:T(8,128)(2,1)S(1)}, bf16[2,1,4,8,1024]{4,3,2,1,0:T(8,128)(2,1)S(1)}, u32[]{:S(2)}, u32[]{:S(2)}) collective-permute-start(bf16[2,1,4,8,1024]{4,3,2,1,0:T(8,128)(2,1)S(1)} %get-tuple-element.175), channel_id=1, source_target_pairs={{0,2},{2,4},{4,6},{6,0},{1,3},{3,5},{5,7},{7,1},{8,10},{10,12},{12... | collective-permute-start | bytes 393224 | tf_op jit(solution)/shard_map/ppermute | solution.py:842
  14.3 6.4 %collective-permute-start.2 = (bf16[2,1,4,8,1024]{4,3,2,1,0:T(8,128)(2,1)S(1)}, bf16[2,1,4,8,1024]{4,3,2,1,0:T(8,128)(2,1)S(1)}, u32[]{:S(2)}, u32[]{:S(2)}) collective-permute-start(bf16[2,1,4,8,1024]{4,3,2,1,0:T(8,128)(2,1)S(1)} %get-tuple-element.174), channel_id=1, source_target_pairs={{2,0},{4,2},{6,4},{0,6},{3,1},{5,3},{7,5},{1,7},{10,8},{12,10},{14... | collective-permute-start | bytes 393224 | tf_op jit(solution)/shard_map/ppermute | solution.py:843
  16.4 9.2 %collective-permute-start.9 = (bf16[1,2,4,8,1024]{4,3,2,1,0:T(8,128)(2,1)S(1)}, bf16[1,2,4,8,1024]{4,3,2,1,0:T(8,128)(2,1)S(1)}, u32[]{:S(2)}, u32[]{:S(2)}) collective-permute-start(bf16[1,2,4,8,1024]{4,3,2,1,0:T(8,128)(2,1)S(1)} %get-tuple-element.172), channel_id=1, source_target_pairs={{8,0},{16,8},{24,16},{0,24},{9,1},{17,9},{25,17},{1,25},{10,2},{18... | collective-permute-start | bytes 393224 | tf_op jit(solution)/shard_map/ppermute | solution.py:843
  16.4 12.5 %collective-permute-start.7 = (bf16[1,2,4,8,1024]{4,3,2,1,0:T(8,128)(2,1)S(1)}, bf16[1,2,4,8,1024]{4,3,2,1,0:T(8,128)(2,1)S(1)}, u32[]{:S(2)}, u32[]{:S(2)}) collective-permute-start(bf16[1,2,4,8,1024]{4,3,2,1,0:T(8,128)(2,1)S(1)} %get-tuple-element.173), channel_id=1, source_target_pairs={{0,8},{8,16},{16,24},{24,0},{1,9},{9,17},{17,25},{25,1},{2,10},{10... | collective-permute-start | bytes 393224 | tf_op jit(solution)/shard_map/ppermute | solution.py:842
  20.7 8.3 %collective-permute-start.8 = (bf16[1,2,4,8,1024]{4,3,2,1,0:T(8,128)(2,1)S(1)}, bf16[1,2,4,8,1024]{4,3,2,1,0:T(8,128)(2,1)S(1)}, u32[]{:S(2)}, u32[]{:S(2)}) collective-permute-start(bf16[1,2,4,8,1024]{4,3,2,1,0:T(8,128)(2,1)S(1)} %get-tuple-element.171), channel_id=1, source_target_pairs={{0,8},{8,16},{16,24},{24,0},{1,9},{9,17},{17,25},{25,1},{2,10},{10... | collective-permute-start | bytes 393224 | tf_op jit(solution)/shard_map/ppermute | solution.py:842
  21.4 8.1 %collective-permute-start.10 = (bf16[1,2,4,8,1024]{4,3,2,1,0:T(8,128)(2,1)S(1)}, bf16[1,2,4,8,1024]{4,3,2,1,0:T(8,128)(2,1)S(1)}, u32[]{:S(2)}, u32[]{:S(2)}) collective-permute-start(bf16[1,2,4,8,1024]{4,3,2,1,0:T(8,128)(2,1)S(1)} %get-tuple-element.170), channel_id=1, source_target_pairs={{8,0},{16,8},{24,16},{0,24},{9,1},{17,9},{25,17},{1,25},{10,2},{18... | collective-permute-start | bytes 393224 | tf_op jit(solution)/shard_map/ppermute | solution.py:843
  22.5 11.7 %collective-permute-start.5 = (bf16[2,1,4,8,2304]{4,3,2,1,0:T(8,128)(2,1)S(1)}, bf16[2,1,4,8,2304]{4,3,2,1,0:T(8,128)(2,1)S(1)}, u32[]{:S(2)}, u32[]{:S(2)}) collective-permute-start(bf16[2,1,4,8,2304]{4,3,2,1,0:T(8,128)(2,1)S(1)} %get-tuple-element.167), channel_id=1, source_target_pairs={{0,2},{2,4},{4,6},{6,0},{1,3},{3,5},{5,7},{7,1},{8,10},{10,12},{12... | collective-permute-start | bytes 884744 | tf_op jit(solution)/shard_map/ppermute | solution.py:842
  23.2 6.3 %copy-start.7 = (bf16[5,128,128]{2,1,0:T(8,128)(2,1)S(1)}, bf16[5,128,128]{2,1,0:T(8,128)(2,1)}, u32[]{:S(2)}) copy-start(bf16[5,128,128]{2,1,0:T(8,128)(2,1)} %out_ref.3) | copy-start | bytes 491524
  25.6 13.8 %collective-permute-start.6 = (bf16[2,1,4,8,2304]{4,3,2,1,0:T(8,128)(2,1)S(1)}, bf16[2,1,4,8,2304]{4,3,2,1,0:T(8,128)(2,1)S(1)}, u32[]{:S(2)}, u32[]{:S(2)}) collective-permute-start(bf16[2,1,4,8,2304]{4,3,2,1,0:T(8,128)(2,1)S(1)} %get-tuple-element.166), channel_id=1, source_target_pairs={{2,0},{4,2},{6,4},{0,6},{3,1},{5,3},{7,5},{1,7},{10,8},{12,10},{14... | collective-permute-start | bytes 884744 | tf_op jit(solution)/shard_map/ppermute | solution.py:843
  28.9 19.5 %collective-permute-start.12 = (bf16[1,2,4,8,2304]{4,3,2,1,0:T(8,128)(2,1)S(1)}, bf16[1,2,4,8,2304]{4,3,2,1,0:T(8,128)(2,1)S(1)}, u32[]{:S(2)}, u32[]{:S(2)}) collective-permute-start(bf16[1,2,4,8,2304]{4,3,2,1,0:T(8,128)(2,1)S(1)} %get-tuple-element.164), channel_id=1, source_target_pairs={{8,0},{16,8},{24,16},{0,24},{9,1},{17,9},{25,17},{1,25},{10,2},{18... | collective-permute-start | bytes 884744 | tf_op jit(solution)/shard_map/ppermute | solution.py:843
  29.0 19.5 %collective-permute-start.4 = (bf16[1,2,4,8,2304]{4,3,2,1,0:T(8,128)(2,1)S(1)}, bf16[1,2,4,8,2304]{4,3,2,1,0:T(8,128)(2,1)S(1)}, u32[]{:S(2)}, u32[]{:S(2)}) collective-permute-start(bf16[1,2,4,8,2304]{4,3,2,1,0:T(8,128)(2,1)S(1)} %get-tuple-element.165), channel_id=1, source_target_pairs={{0,8},{8,16},{16,24},{24,0},{1,9},{9,17},{17,25},{25,1},{2,10},{10... | collective-permute-start | bytes 884744 | tf_op jit(solution)/shard_map/ppermute | solution.py:842
  29.5 9.9 %copy-start.10 = (f32[4,128]{1,0:T(4,128)S(1)}, f32[4,128]{1,0:T(4,128)}, u32[]{:S(2)}) copy-start(f32[4,128]{1,0:T(4,128)} %nw_ref.1) | copy-start | bytes 6148
  46.5 8.6 %collective-permute-start.11 = (bf16[1,2,4,8,2304]{4,3,2,1,0:T(8,128)(2,1)S(1)}, bf16[1,2,4,8,2304]{4,3,2,1,0:T(8,128)(2,1)S(1)}, u32[]{:S(2)}, u32[]{:S(2)}) collective-permute-start(bf16[1,2,4,8,2304]{4,3,2,1,0:T(8,128)(2,1)S(1)} %get-tuple-element.163), channel_id=1, source_target_pairs={{0,8},{8,16},{16,24},{24,0},{1,9},{9,17},{17,25},{25,1},{2,10},{10... | collective-permute-start | bytes 884744 | tf_op jit(solution)/shard_map/ppermute | solution.py:842
  46.6 8.5 %collective-permute-start.13 = (bf16[1,2,4,8,2304]{4,3,2,1,0:T(8,128)(2,1)S(1)}, bf16[1,2,4,8,2304]{4,3,2,1,0:T(8,128)(2,1)S(1)}, u32[]{:S(2)}, u32[]{:S(2)}) collective-permute-start(bf16[1,2,4,8,2304]{4,3,2,1,0:T(8,128)(2,1)S(1)} %get-tuple-element.162), channel_id=1, source_target_pairs={{8,0},{16,8},{24,16},{0,24},{9,1},{17,9},{25,17},{1,25},{10,2},{18... | collective-permute-start | bytes 884744 | tf_op jit(solution)/shard_map/ppermute | solution.py:843
  63.6 4.2 %collective-permute-start.14 = (f32[8,128]{1,0:T(8,128)S(1)}, f32[8,128]{1,0:T(8,128)S(1)}, u32[]{:S(2)}, u32[]{:S(2)}) collective-permute-start(f32[8,128]{1,0:T(8,128)S(1)} %get-tuple-element.135), channel_id=1, source_target_pairs={{0,8},{8,16},{16,24},{24,0},{1,9},{9,17},{17,25},{25,1},{2,10},{10... | collective-permute-start | bytes 12296 | tf_op jit(solution)/shard_map/ppermute | solution.py:892
  64.2 3.5 %collective-permute-start.15 = (f32[8,128]{1,0:T(8,128)S(1)}, f32[8,128]{1,0:T(8,128)S(1)}, u32[]{:S(2)}, u32[]{:S(2)}) collective-permute-start(f32[8,128]{1,0:T(8,128)S(1)} %get-tuple-element.136), channel_id=1, source_target_pairs={{8,0},{16,8},{24,16},{0,24},{9,1},{17,9},{25,17},{1,25},{10,2},{18... | collective-permute-start | bytes 12296 | tf_op jit(solution)/shard_map/ppermute | solution.py:893
  67.8 6.7 %collective-permute-start.16 = (f32[8,256]{1,0:T(8,128)S(1)}, f32[8,256]{1,0:T(8,128)S(1)}, u32[]{:S(2)}, u32[]{:S(2)}) collective-permute-start(f32[8,256]{1,0:T(8,128)S(1)} %add.3.mid_ref), channel_id=1, source_target_pairs={{0,2},{2,4},{4,6},{6,0},{1,3},{3,5},{5,7},{7,1},{8,10},{10,12},{12... | collective-permute-start | bytes 24584 | tf_op jit(solution)/shard_map/ppermute | solution.py:899
  68.4 6.1 %collective-permute-start.17 = (f32[8,256]{1,0:T(8,128)S(1)}, f32[8,256]{1,0:T(8,128)S(1)}, u32[]{:S(2)}, u32[]{:S(2)}) collective-permute-start(f32[8,256]{1,0:T(8,128)S(1)} %add.3.mid_ref), channel_id=1, source_target_pairs={{2,0},{4,2},{6,4},{0,6},{3,1},{5,3},{7,5},{1,7},{10,8},{12,10},{14... | collective-permute-start | bytes 24584 | tf_op jit(solution)/shard_map/ppermute | solution.py:899
  74.6 3.7 %collective-permute-start.18 = (f32[8,256]{1,0:T(8,128)S(1)}, f32[8,256]{1,0:T(8,128)S(1)}, u32[]{:S(2)}, u32[]{:S(2)}) collective-permute-start(f32[8,256]{1,0:T(8,128)S(1)} %fold.1.mid_ref), channel_id=1, source_target_pairs={{0,1},{1,0},{2,3},{3,2},{4,5},{5,4},{6,7},{7,6},{8,9},{9,8},{10,11... | collective-permute-start | bytes 24584 | tf_op jit(solution)/shard_map/ppermute | solution.py:908
  (7 other events, 13.2 us)

commit v8 on v7

--- a/solution.py
+++ b/solution.py
@@ -23,7 +23,7 @@
     (3, 3), (3, 3), (3, 3), (3, 4),
     (4, 4), (4, 4), (4, 4), (4, 4),
 )
-GROUPS = ((0, 3), (3, 12))
+GROUPS = ((0, 4), (4, 12))
 KINDS = tuple(sorted({PAIR_DEGREES[pair] for pair in range(*group)}) for group in GROUPS)
 DEGREES = tuple(sorted({d for both in kinds for d in both}) for kinds in KINDS)
 GROUP_COLS = tuple(2 * CH * (end - begin) for begin, end in GROUPS)
@@ -53,8 +53,7 @@
     return jax.ShapeDtypeStruct(shape, dtype)
 
 
-def call(kernel, name, out_shape, scratch, flops, args, specs=None, limit=16):
-    size = sum(a.size * a.dtype.itemsize for a in list(args) + list(out_shape))
+def call(kernel, name, out_shape, scratch, args, specs=None, limit=16):
     return pl.pallas_call(
         kernel,
         out_shape=out_shape,
@@ -62,7 +61,7 @@
         out_specs=tuple(pl.BlockSpec(memory_space=SPACE) for _ in out_shape),
         scratch_shapes=scratch,
         compiler_params=pltpu.CompilerParams(vmem_limit_bytes=limit * MIB),
-        cost_estimate=pl.CostEstimate(flops=flops, bytes_accessed=size, transcendentals=0),
+        cost_estimate=pl.CostEstimate(flops=1024, bytes_accessed=1024, transcendentals=0),
         name=name,
     )(*args)
 
@@ -113,9 +112,11 @@
     )
     args = (feats, places, near, counts, order)
     scratch = [pltpu.VMEM((CH, atoms), F32), pltpu.VMEM((CH, atoms), F32)]
-    first, own_pos, meta, pick = call(cells_kernel, "cells", out_shape, scratch, 1 << 26, args)
+    first, own_pos, meta, pick = call(
+        cells_kernel, "cells", out_shape, scratch, args, limit=60
+    )
     out_shape = (struct(atoms, sum(GROUP_COLS[1:]), dtype=BF16),)
-    rest = call(rest_kernel, "cells_rest", out_shape, [], 1 << 26, (feats, pick))[0]
+    rest = call(rest_kernel, "cells_rest", out_shape, [], (feats, pick), limit=60)[0]
     return first, rest, own_pos, meta
 
 
@@ -367,8 +368,8 @@
 
 
 def own_kernel(
-    meta_ref, own_pos_ref, rbf_ref, rad_ref, mix_ref,
-    oh_own, pre_ref, unit_ref, radt_ref, rbft_ref, mixt_ref, home_ref, *radial_refs
+    meta_ref, own_pos_ref, rbf_ref, rad_ref,
+    oh_own, pre_ref, unit_ref, radt_ref, rbft_ref, home_ref, *radial_refs
 ):
     atoms = meta_ref.shape[0]
     nbasis = rbf_ref.shape[0]
@@ -389,7 +390,6 @@
     for index in range(nbasis // CH):
         part = slice(index * CH, (index + 1) * CH)
         rbft_ref[:, part] = flip(rbf_ref[part, :])
-    mixt_ref[...] = flip(mix_ref[0])
     lanes = home_ref.shape[1]
     lane = iota((atoms, lanes), 1)
     ext_x, ext_y, ext_z = lane // 128, lane // 32 % 4, lane // 8 % 4
@@ -404,7 +404,7 @@
     home_ref[...] = mm(to_atom.T.astype(BF16), to_slot).astype(BF16)
 
 
-def own_stage(meta, own_pos, rbf, rad, mix):
+def own_stage(meta, own_pos, rbf, rad):
     atoms = meta.shape[0]
     edges = atoms * HALF
     out_shape = (
@@ -413,11 +413,10 @@
         struct(edges, CH),
         struct(*rad.shape[::-1], dtype=BF16),
         struct(*rbf.shape[::-1], dtype=BF16),
-        struct(CH, CH, dtype=BF16),
         struct(atoms, 256, dtype=BF16),
     ) + (struct(edges, CH, dtype=BF16),) * 5
-    args = (meta, own_pos, rbf, rad, mix)
-    return call(own_kernel, "own_edges", out_shape, [], 1 << 31, args)
+    args = (meta, own_pos, rbf, rad)
+    return call(own_kernel, "own_edges", out_shape, [], args, limit=60)
 
 
 def scalar_forward(rows, near, radial, mix_ref, m0_ref, gate_ref, nf0_ref):
@@ -473,7 +472,7 @@
     scratch = [pltpu.VMEM((len(KINDS[group]), 2 * CH, 2 * CH), BF16) for group in groups]
     name = "own_forward_" + "".join("abc"[group] for group in groups)
     kernel = functools.partial(own_forward_kernel, groups, gate is None)
-    outs = call(kernel, name, out_shape, scratch, 1 << 32, args)
+    outs = call(kernel, name, out_shape, scratch, args)
     first = len(outs) - 3 * len(groups)
     return outs[:first], [outs[first + 3 * i : first + 3 * i + 3] for i in range(len(groups))]
 
@@ -599,7 +598,7 @@
     ]
     args = tuple(pieces) + (feats,) + rest
     return call(
-        start_kernel, "ghost_start", out_shape, scratch, 1 << 31, args,
+        start_kernel, "ghost_start", out_shape, scratch, args,
         any_specs(len(pieces), len(args)), 24,
     )
 
@@ -648,7 +647,7 @@
     args += tuple(radial_gh[degree - 1] for degree in degrees)
     new, energy, gs, *rest = call(
         functools.partial(pairs_kernel, group, len(pieces), skip), "pairs_" + "abc"[group],
-        out_shape, pair_scratch(atoms, half, ghosts, group), 1 << 33, args,
+        out_shape, pair_scratch(atoms, half, ghosts, group), args,
         any_specs(len(pieces), len(args)), 24,
     )
     return new, energy, gs, rest[: 1 + len(degrees)], rest[1 + len(degrees) :]
@@ -666,16 +665,16 @@
     scratch = [pltpu.VMEM((len(KINDS[group]), 2 * CH, 2 * CH), BF16)]
     kernel = functools.partial(own_backward_kernel, group)
     name = "own_backward_" + "abc"[group]
-    return call(kernel, name, out_shape, scratch, 1 << 32, (mix, gs, gate, nf, mx))
+    return call(kernel, name, out_shape, scratch, (mix, gs, gate, nf, mx))
 
 
 def finish(
-    grad, mixed, near, dots, parts, pre, unit, spacing, radt_ref, rbft_ref, mixt_ref
+    grad, mixed, near, dots, parts, pre, unit, spacing, radt_ref, rbft_ref, mix_t
 ):
     mixed = mixed.astype(F32)
     gate = jax.nn.sigmoid(mixed)
     first = grad * gate * (1.0 + mixed * (1.0 - gate)) + dots * gate * (1.0 - gate)
-    weighted = mm(first.astype(BF16), mixt_ref[...]) * near.astype(F32)
+    weighted = mm(first.astype(BF16), mix_t) * near.astype(F32)
     radial_grad = jnp.concatenate([weighted.astype(BF16)] + parts, axis=1)
     hidden_grad = mm(radial_grad, radt_ref[...])
     pre = pre.astype(F32)
@@ -713,15 +712,16 @@
 
 def third_kernel(
     p0, p1, p2, p3, p4, own_ref, meta_ref, mix_ref, out_ref, nw_ref, oh_gh, d_gh, dt_gh, gate_gh,
-    acc_own, radial_gh2, radial_gh3, radial_gh4,
-    radt_ref, rbft_ref, mixt_ref, gs0_ref, en_0, en_a, new_0, new_a, pre_gh, unit_gh,
-    m0_ref, nf0_ref, dot_a, gr1_a, gr2_a,
-    new_ref, energy_ref, src_ref, flow_ref, fmid_ref, fhigh_ref, gs_ref,
-    table, sems, wm, wmt, wo, wot, nf_s, mx_s, acc_s, dot_c, gr2_c, gr3_c, gr4_c, en_s, fgh_s,
+    acc_own, radt_ref, rbft_ref, gs0_ref, en_0, en_a, new_0, new_a, pre_gh, unit_gh,
+    m0_ref, nf0_ref, dot_a, *refs
 ):
     group = 1
-    radials = {2: radial_gh2, 3: radial_gh3, 4: radial_gh4}
-    grads = {2: gr2_c, 3: gr3_c, 4: gr4_c}
+    before, degrees = len(DEGREES[0]), DEGREES[group]
+    gr_a, refs = refs[:before], refs[before:]
+    radials, refs = dict(zip(degrees, refs)), refs[len(degrees) :]
+    new_ref, energy_ref, src_ref, flow_ref, fmid_ref, fhigh_ref, gs_ref = refs[:7]
+    table, sems, wm, wmt, wo, wot, nf_s, mx_s, acc_s, dot_c, en_s, fgh_s = refs[7:19]
+    grads = dict(zip(degrees, refs[19:]))
     copies = fetch((p0, p1, p2, p3, p4), slice(0, GROUP_COLS[group]), table, sems)
     atoms = own_ref.shape[0]
     spacing = spacing_of(atoms, rbft_ref.shape[1])
@@ -745,14 +745,15 @@
     fgh_s[...] = jnp.zeros_like(fgh_s)
     src_ref[...] = jnp.zeros_like(src_ref)
     gs0_low = gs0_ref[...].astype(BF16)
+    mix_t = flip(mix_ref[0])
 
     def ghost_finish(step):
         here, _ = ghost_rows(step)
         grad = mm(d_gh[here, :], gs0_low)
         pull, top, rest = finish(
             grad, m0_ref[here, :], nf0_ref[here, :], sum_of((dot_a, dot_c), here),
-            degree_parts((gr1_a, gr2_a, gr2_c, gr3_c, gr4_c), here), pre_gh[here, :], unit_gh[here, :], spacing,
-            radt_ref, rbft_ref, mixt_ref,
+            degree_parts(gr_a + refs[19:], here), pre_gh[here, :], unit_gh[here, :], spacing,
+            radt_ref, rbft_ref, mix_t,
         )
         pull_top = pull.astype(BF16)
         pull_rest = (pull - pull_top.astype(F32)).astype(BF16)
@@ -782,27 +783,26 @@
     )
     scratch = pair_scratch(atoms, half, ghosts, 1) + [
         pltpu.VMEM((half, CH), BF16),
-        pltpu.VMEM((half, CH), BF16),
-        pltpu.VMEM((half, CH), BF16),
-        pltpu.VMEM((half, CH), BF16),
         pltpu.VMEM((atoms, CH), F32),
         pltpu.VMEM((8, ghosts), F32),
     ]
+    scratch += [pltpu.VMEM((half, CH), BF16)] * len(DEGREES[1])
     args = tuple(pieces) + (feats,) + rest
     return call(
-        third_kernel, "third_group", out_shape, scratch, 1 << 33, args,
+        third_kernel, "third_group", out_shape, scratch, args,
         any_specs(len(pieces), len(args)), 28,
     )
 
 
 def own_back_kernel(
-    oh_own, pre_own, unit_own, radt_ref, rbft_ref, mixt_ref, gs0_ref, src_ref,
+    oh_own, pre_own, unit_own, radt_ref, rbft_ref, mix_ref, gs0_ref, src_ref,
     m0_ref, nf0_ref, dot_a, dot_c, *refs
 ):
     gr_own, (force_ref,) = refs[:PARTIALS], refs[PARTIALS:]
     atoms = oh_own.shape[1]
     spacing = spacing_of(atoms, rbft_ref.shape[1])
     grad = tiled(gs0_ref[...])
+    mix_t = flip(mix_ref[0])
     src = src_ref[...]
     onto = jnp.zeros((8, atoms), F32)
     for step in range(OWN_STEPS):
@@ -810,7 +810,7 @@
         pull, top, rest = finish(
             grad, m0_ref[rows, :], nf0_ref[rows, :], sum_of((dot_a, dot_c), rows),
             degree_parts(gr_own, rows), pre_own[rows, :], unit_own[rows, :], spacing, radt_ref,
-            rbft_ref, mixt_ref,
+            rbft_ref, mix_t,
         )
         src += jnp.sum(pull.reshape(STEP // atoms, atoms, CH), axis=0)
         onehot = oh_own[rows, :]
@@ -821,7 +821,7 @@
 def own_back_stage(*args):
     oh_own = args[0]
     out_shape = (struct(8, oh_own.shape[1]),)
-    return call(own_back_kernel, "own_back", out_shape, [], 1 << 31, args)[0]
+    return call(own_back_kernel, "own_back", out_shape, [], args)[0]
 
 
 def ring(axis):
@@ -900,7 +900,7 @@
 
 
 def fold(*args):
-    return call(fold_kernel, "fold", (struct(*args[0].shape),), [], 1 << 16, args)[0]
+    return call(fold_kernel, "fold", (struct(*args[0].shape),), [], args)[0]
 
 
 def give_back_z(mid):
@@ -933,12 +933,12 @@
     block0, own_pos, meta = hold((block0, own_pos, meta))
     y0 = neighbours_of(block0, "gy", 1)
     x0_in = neighbours_of(block0, "gx", 0)
-    oh_own, pre_own, unit_own, radt, rbft, mixt, home, *radial_own = own_stage(
-        meta, own_pos, rbf_weight, radial_weight, mix_weight
+    oh_own, pre_own, unit_own, radt, rbft, home, *radial_own = own_stage(
+        meta, own_pos, rbf_weight, radial_weight
     )
     block1 = grown(block1, "gz", 2)
     y1 = neighbours_of(block1, "gy", 1)
-    y0, block1, oh_own = hold((y0, block1, oh_own))
+    y0, x0_in, block1, oh_own = hold((y0, x0_in, block1, oh_own))
     pieces0 = ghost_pieces(y0, block0, x0_in)
     x1_in = neighbours_of(block1, "gx", 0)
     (m0_own, gate_own, nf0_own, acc0), (own_a,) = own_forward_stage(
@@ -959,22 +959,23 @@
     en_a, gate_own = hold((en_a, gate_own))
     _, (own_b,) = own_forward_stage((1,), feats, mix_weight, oh_own, radial_own, gate_own)
     new, energy, src, low, mid, high, gs_b = third_stage(
-        pieces1, *shared, own_b[2], *radial_gh[1:], radt, rbft, mixt, gs0, en_0, en_a, new_0,
-        new_a, pre_gh, unit_gh, m0_gh, nf0_gh, dot_gh_a, *gr_gh_a,
+        pieces1, *shared, own_b[2], radt, rbft, gs0, en_0, en_a, new_0, new_a, pre_gh,
+        unit_gh, m0_gh, nf0_gh, dot_gh_a, *gr_gh_a,
+        *[radial_gh[degree - 1] for degree in DEGREES[1]],
     )
     mid, arrived = give_back_x(low, mid, high)
     dot_own_b, *gr_own_b = own_backward_stage(1, mix_weight, gs_b, gate_own, *own_b[:2])
     arrived, gs0, dot_own_b = hold((arrived, gs0, dot_own_b))
     mid, from_low, from_high = give_back_y(mid + arrived)
     own = own_back_stage(
-        oh_own, pre_own, unit_own, radt, rbft, mixt, gs0, src, m0_own, nf0_own, dot_own_a,
+        oh_own, pre_own, unit_own, radt, rbft, mix_weight, gs0, src, m0_own, nf0_own, dot_own_a,
         dot_own_b, *gr_own_a, *gr_own_b,
     )
     from_low, from_high, own = hold((from_low, from_high, own))
     folded = give_back_z(fold(mid, from_low, from_high))
     args = (*folded, own, home)
     out_shape = (struct(3, 1, own.shape[1]),)
-    forces = call(forces_kernel, "forces", out_shape, [], 1 << 20, args)[0]
+    forces = call(forces_kernel, "forces", out_shape, [], args)[0]
     return (
         new[None, None, None],
         energy[None, None],

time: 79.3 us -> 71.3 us (0.90)
  waiting for transfers between devices: 19.9 us -> 5.88 us
  Pallas kernels: 30.7 us -> 36.6 us
  local copies, waits for them, and re-layouts: 4.01 us -> 0.37 us
  other arithmetic: 0.31 us -> 2.3 us
  starting transfers between devices: 23.1 us -> 24.7 us
    ppermute x6, waiting for transfers between devices: 7.9 us -> 0.12 us  [neighbours_of(): lax.ppermute(lax.slice_in_dim(block, length - 1, length, axis=dim), axis,...]
    pallas_call x12, Pallas kernels: 30.7 us -> 36.6 us  [call(): pl.pallas_call(kernel, out_shape=out_shape, in_specs=specs or [pl.BlockSp...]
    ppermute x6, waiting for transfers between devices: 5.87 us -> 1.18 us  [neighbours_of(): after = lax.ppermute(lax.slice_in_dim(block, 0, 1, axis=dim), axis, down)]
    unnamed x26 -> x42, local copies, waits for them, and re-layouts: 3.77 us -> 0.12 us
    ppermute x6, starting transfers between devices: 8.3 us -> 10.3 us  [neighbours_of(): after = lax.ppermute(lax.slice_in_dim(block, 0, 1, axis=dim), axis, down)]
    concatenate x2, other arithmetic: 0.1 us -> 2.09 us  [grown(): return jnp.concatenate([before, block, after], axis=dim)]
    ppermute x6, starting transfers between devices: 4.48 us -> 3.28 us  [neighbours_of(): lax.ppermute(lax.slice_in_dim(block, length - 1, length, axis=dim), axis,...]
    ppermute x2, waiting for transfers between devices: 3.99 us -> 2.95 us  [neighbours_of(): other = lax.ppermute(block, axis, up)]
  transfers between devices with their start and end apart: 19 -> 19, of which waited for: 6 -> 5; matrix products, arithmetic and copies ran while one was open for 1% -> 4% of each run, Pallas kernels for 27% -> 36%
where the time goes in v8:
time: 71.3 us; the launch traced here: 71.1 us
  Pallas kernels  36.6 us (51%)
  starting transfers between devices  24.7 us (35%)
  waiting for transfers between devices  5.88 us (8%)
  other arithmetic  2.3 us (3%)
  between operations  1.18 us (2%)
    pallas_call x12, Pallas kernels, call(): pl.pallas_call(kernel, out_shape=out_shape, in_specs=specs or [pl.BlockSp...  36.6 us
    ppermute x6, starting transfers between devices, neighbours_of(): after = lax.ppermute(lax.slice_in_dim(block, 0, 1, axis=dim), axis, down)  10.3 us
    ppermute x2, starting transfers between devices, give_back_y(): return (mid, lax.ppermute(mid, 'gy', up), lax.ppermute(mid, 'gy', down))  3.88 us
    ppermute x6, starting transfers between devices, neighbours_of(): lax.ppermute(lax.slice_in_dim(block, length - 1, length, axis=dim), axis,...  3.28 us
    ppermute x2, starting transfers between devices, neighbours_of(): other = lax.ppermute(block, axis, up)  3.1 us
    ppermute x2, waiting for transfers between devices, neighbours_of(): other = lax.ppermute(block, axis, up)  2.95 us
    ppermute x1, starting transfers between devices, give_back_z(): from_low = lax.ppermute(mid, 'gz', up)  2.39 us
    concatenate x2, other arithmetic, grown(): return jnp.concatenate([before, block, after], axis=dim)  2.09 us
  transfers between devices with their start and end apart: 19, of which 5 were waited for; matrix products, arithmetic and copies ran while one was open for 4% of the time, Pallas kernels for 36%

profile of v8, /device:TPU:0, one launch (start us, length us, event | category | flops | bytes accessed | tf_op | source)
XLA Modules:
  0.0 71.1 jit_solution(5965348586171126579)
XLA Ops:
  0.6 2.0 %cells.1 = (bf16[64,1280]{1,0:T(8,128)(2,1)}, bf16[64,128]{1,0:T(8,128)(2,1)}, f32[64,128]{1,0:T(8,128)}, bf16[64,64]{1,0:T(8,128)(2,1)}) custom-call(bf16[64,3200]{1,0:T(8,128)(2,1)} %bitcast.25, f32[3,1,64]{2,1,0:T(1,128)} %bitcast.53, s32[32,64]{1,0:T(8,128)} %bitcast.52, s32[1,64]{1,0:T(1,128)} %bitcast.55, s32[1,64]{1,0:T(1,128)} %bitcast.56), custom_call_target="tpu_custom_call" | custom-call | flops 1024 | bytes 1024 | tf_op jit(solution)/shard_map/cells/pallas_call | solution.py:57
  2.7 3.0 %collective-permute-start = (bf16[2,2,2,8,1280]{4,3,2,1,0:T(8,128)(2,1)}, bf16[2,2,2,8,1280]{4,3,2,1,0:T(8,128)(2,1)S(1)}, u32[]{:S(2)}, u32[]{:S(2)}) collective-permute-start(bf16[2,2,2,8,1280]{4,3,2,1,0:T(8,128)(2,1)} %bitcast.50), channel_id=1, source_target_pairs={{0,1},{1,0},{2,3},{3,2},{4,5},{5,4},{6,7},{7,6},{8,9},{9,8},{10,11... | collective-permute-start | bytes 491528 | tf_op jit(solution)/shard_map/ppermute | solution.py:837
  5.7 1.9 %cells_rest.1 = bf16[64,2048]{1,0:T(8,128)(2,1)} custom-call(bf16[64,3200]{1,0:T(8,128)(2,1)} %bitcast.26, bf16[64,64]{1,0:T(8,128)(2,1)} %get-tuple-element.85.pick_ref), custom_call_target="tpu_custom_call" | custom-call | flops 1024 | bytes 1024 | tf_op jit(solution)/shard_map/cells_rest/pallas_call | solution.py:57
  7.7 2.9 %collective-permute-done = bf16[2,2,2,8,1280]{4,3,2,1,0:T(8,128)(2,1)S(1)} collective-permute-done((bf16[2,2,2,8,1280]{4,3,2,1,0:T(8,128)(2,1)}, bf16[2,2,2,8,1280]{4,3,2,1,0:T(8,128)(2,1)S(1)}, u32[]{:S(2)}, u32[]{:S(2)}) %collective-permute-start) | collective-permute-done | bytes 163872 | tf_op jit(solution)/shard_map/ppermute | solution.py:837
  11.7 1.6 %collective-permute-start.1 = (bf16[2,1,4,8,1280]{4,3,2,1,0:T(8,128)(2,1)S(1)}, bf16[2,1,4,8,1280]{4,3,2,1,0:T(8,128)(2,1)S(1)}, u32[]{:S(2)}, u32[]{:S(2)}) collective-permute-start(bf16[2,1,4,8,1280]{4,3,2,1,0:T(8,128)(2,1)S(1)} %get-tuple-element.173), channel_id=1, source_target_pairs={{0,2},{2,4},{4,6},{6,0},{1,3},{3,5},{5,7},{7,1},{8,10},{10,12},{12... | collective-permute-start | bytes 491528 | tf_op jit(solution)/shard_map/ppermute | solution.py:842
  13.3 2.2 %collective-permute-start.2 = (bf16[2,1,4,8,1280]{4,3,2,1,0:T(8,128)(2,1)S(1)}, bf16[2,1,4,8,1280]{4,3,2,1,0:T(8,128)(2,1)S(1)}, u32[]{:S(2)}, u32[]{:S(2)}) collective-permute-start(bf16[2,1,4,8,1280]{4,3,2,1,0:T(8,128)(2,1)S(1)} %get-tuple-element.172), channel_id=1, source_target_pairs={{2,0},{4,2},{6,4},{0,6},{3,1},{5,3},{7,5},{1,7},{10,8},{12,10},{14... | collective-permute-start | bytes 491528 | tf_op jit(solution)/shard_map/ppermute | solution.py:843
  15.6 1.7 %collective-permute-start.4 = (bf16[1,2,4,8,1280]{4,3,2,1,0:T(8,128)(2,1)S(1)}, bf16[1,2,4,8,1280]{4,3,2,1,0:T(8,128)(2,1)S(1)}, u32[]{:S(2)}, u32[]{:S(2)}) collective-permute-start(bf16[1,2,4,8,1280]{4,3,2,1,0:T(8,128)(2,1)S(1)} %get-tuple-element.170), channel_id=1, source_target_pairs={{8,0},{16,8},{24,16},{0,24},{9,1},{17,9},{25,17},{1,25},{10,2},{18... | collective-permute-start | bytes 491528 | tf_op jit(solution)/shard_map/ppermute | solution.py:843
  17.4 5.2 %own_edges.1 = (bf16[1024,64]{1,0:T(8,128)(2,1)}, bf16[1024,128]{1,0:T(8,128)(2,1)}, f32[1024,128]{1,0:T(8,128)}, bf16[640,128]{1,0:T(8,128)(2,1)}, bf16[128,512...) custom-call(f32[64,128]{1,0:T(8,128)} %get-tuple-element.86.meta_ref, ...), custom_call_target="tpu_custom_call" | custom-call | flops 1024 | bytes 1024 | tf_op jit(solution)/shard_map/own_edges/pallas_call | solution.py:57
  22.7 1.1 %pad_maximum_fusion.2 = bf16[2,2,4,8,2048]{4,3,2,1,0:T(8,128)(2,1)S(1)} fusion(bf16[2,2,1,8,2048]{4,3,2,1,0:T(8,128)(2,1)S(1)} %get-tuple-element.175, bf16[2,2,2,8,2048]{4,3,2,1,0:T(8,128)(2,1)} %bitcast.49, bf16[2,2,1,8,2048]{4,3,2,1,0:T(8,128)(2,1)S(1)} %get-tuple-element.174), kind=kLoop, calls=%fused_computation.2 | loop fusion | flops 524288 | bytes 1048576 | tf_op jit(solution)/shard_map/concatenate | solution.py:849
  24.0 3.8 %collective-permute-start.8 = (bf16[2,1,4,8,2048]{4,3,2,1,0:T(8,128)(2,1)S(1)}, bf16[2,1,4,8,2048]{4,3,2,1,0:T(8,128)(2,1)S(1)}, u32[]{:S(2)}, u32[]{:S(2)}) collective-permute-start(bf16[2,1,4,8,2048]{4,3,2,1,0:T(8,128)(2,1)S(1)} %get-tuple-element.166), channel_id=1, source_target_pairs={{2,0},{4,2},{6,4},{0,6},{3,1},{5,3},{7,5},{1,7},{10,8},{12,10},{14... | collective-permute-start | bytes 786440 | tf_op jit(solution)/shard_map/ppermute | solution.py:843
  27.9 1.7 %collective-permute-start.10 = (bf16[1,2,4,8,1280]{4,3,2,1,0:T(8,128)(2,1)S(1)}, bf16[1,2,4,8,1280]{4,3,2,1,0:T(8,128)(2,1)S(1)}, u32[]{:S(2)}, u32[]{:S(2)}) collective-permute-start(bf16[1,2,4,8,1280]{4,3,2,1,0:T(8,128)(2,1)S(1)} %get-tuple-element.168), channel_id=1, source_target_pairs={{8,0},{16,8},{24,16},{0,24},{9,1},{17,9},{25,17},{1,25},{10,2},{18... | collective-permute-start | bytes 491528 | tf_op jit(solution)/shard_map/ppermute | solution.py:843
  29.9 2.6 %own_forward_a.1 = (bf16[1024,128]{1,0:T(8,128)(2,1)S(1)}, bf16[1024,128]{1,0:T(8,128)(2,1)S(1)}, bf16[1024,128]{1,0:T(8,128)(2,1)S(1)}, f32[64,128]{1,0:T(8,128...) custom-call(bf16[64,3200]{1,0:T(8,128)(2,1)S(1)} %bitcast.27, ...), custom_call_target="tpu_custom_call" | custom-call | flops 1024 | bytes 1024 | tf_op jit(solution)/shard_map/own_forward_a/pallas_call | solution.py:57
  33.5 3.4 %ghost_start.1 = (bf16[64,128]{1,0:T(8,128)(2,1)S(1)}, bf16[1024,512]{1,0:T(8,128)(2,1)S(1)}, bf16[1024,64]{1,0:T(8,128)(2,1)S(1)}, bf16[64,1024]{1,0:T(8,128)(2...) custom-call(bf16[64,1280]{1,0:T(8,128)(2,1)S(1)} %bitcast.35, ...), custom_call_target="tpu_custom_call" | custom-call | flops 1024 | bytes 1024 | tf_op jit(solution)/shard_map/ghost_start/pallas_call | solution.py:57
  37.8 1.1 %collective-permute-start.11 = (bf16[1,2,4,8,2048]{4,3,2,1,0:T(8,128)(2,1)S(1)}, bf16[1,2,4,8,2048]{4,3,2,1,0:T(8,128)(2,1)S(1)}, u32[]{:S(2)}, u32[]{:S(2)}) collective-permute-start(bf16[1,2,4,8,2048]{4,3,2,1,0:T(8,128)(2,1)S(1)} %get-tuple-element.163), channel_id=1, source_target_pairs={{0,8},{8,16},{16,24},{24,0},{1,9},{9,17},{17,25},{25,1},{2,10},{10... | collective-permute-start | bytes 786440 | tf_op jit(solution)/shard_map/ppermute | solution.py:842
  39.6 4.7 %pairs_a.1 = (bf16[64,1024]{1,0:T(8,128)(2,1)S(1)}, f32[64,128]{1,0:T(8,128)S(1)}, bf16[64,1024]{1,0:T(8,128)(2,1)}, bf16[1024,128]{1,0:T(8,128)(2,1)S(1)}, bf16...) custom-call(bf16[64,1280]{1,0:T(8,128)(2,1)S(1)} %bitcast.36, ...), custom_call_target="tpu_custom_call" | custom-call | flops 1024 | bytes 1024 | tf_op jit(solution)/shard_map/pairs_a/pallas_call | solution.py:57
  44.3 3.1 %own_forward_b.1 = (bf16[1024,2048]{1,0:T(8,128)(2,1)S(1)}, bf16[1024,2048]{1,0:T(8,128)(2,1)S(1)}, f32[64,2048]{1,0:T(8,128)S(1)}) custom-call(bf16[64,3200]{1,0:T(8,128)(2,1)S(1)} %bitcast.30, bf16[5,128,128]{2,1,0:T(8,128)(2,1)S(1)} %copy-done.1, bf16[1024,64]{1,0:T(8,128)(2,1)S(1)} %copy-done.2, bf16[1024,128]{1,0:T(8,128)(2,1)S(1)} %copy-done.4, ...), custom_call_target="tpu_custom_call" | custom-call | flops 1024 | bytes 1024 | tf_op jit(solution)/shard_map/own_forward_b/pallas_call | solution.py:57
  47.6 7.8 %third_group.1 = (bf16[64,3200]{1,0:T(8,128)(2,1)}, f32[1,64]{1,0:T(1,128)}, f32[64,128]{1,0:T(8,128)S(1)}, f32[8,128]{1,0:T(8,128)S(1)}, f32[8,256]{1,0:T(8,128...) custom-call(bf16[64,2048]{1,0:T(8,128)(2,1)S(1)} %bitcast.44, bf16[64,2048]{1,0:T(8,128)(2,1)S(1)} %bitcast.45, ...), custom_call_target="tpu_custom_call" | custom-call | flops 1024 | bytes 1024 | tf_op jit(solution)/shard_map/third_group/pallas_call | solution.py:57
  55.5 1.7 %collective-permute-start.15 = (f32[8,128]{1,0:T(8,128)S(1)}, f32[8,128]{1,0:T(8,128)S(1)}, u32[]{:S(2)}, u32[]{:S(2)}) collective-permute-start(f32[8,128]{1,0:T(8,128)S(1)} %get-tuple-element.137), channel_id=1, source_target_pairs={{8,0},{16,8},{24,16},{0,24},{9,1},{17,9},{25,17},{1,25},{10,2},{18... | collective-permute-start | bytes 12296 | tf_op jit(solution)/shard_map/ppermute | solution.py:893
  57.2 2.1 %own_backward_b.1 = (bf16[1024,128]{1,0:T(8,128)(2,1)S(1)}, bf16[1024,128]{1,0:T(8,128)(2,1)S(1)}, bf16[1024,128]{1,0:T(8,128)(2,1)S(1)}) custom-call(bf16[5,128,128]{2,1,0:T(8,128)(2,1)S(1)} %copy-done.1, bf16[64,2048]{1,0:T(8,128)(2,1)S(1)} %get-tuple-element.138.gs_ref, bf16[1024,128]{1,0:T(8,128)(2,1)S(1)} %get-tuple-element.115.refs_14_.refs_8_.gate_ref, ...), custom_call_target="tpu_custom_call" | custom-call | flops 1024 | bytes 1024 | tf_op jit(solution)/shard_map/own_backward_b/pallas_call | solution.py:57
  59.4 1.1 %collective-permute-start.16 = (f32[8,256]{1,0:T(8,128)S(1)}, f32[8,256]{1,0:T(8,128)S(1)}, u32[]{:S(2)}, u32[]{:S(2)}) collective-permute-start(f32[8,256]{1,0:T(8,128)S(1)} %add.3.mid_ref), channel_id=1, source_target_pairs={{0,2},{2,4},{4,6},{6,0},{1,3},{3,5},{5,7},{7,1},{8,10},{10,12},{12... | collective-permute-start | bytes 24584 | tf_op jit(solution)/shard_map/ppermute | solution.py:899
  60.5 2.8 %collective-permute-start.17 = (f32[8,256]{1,0:T(8,128)S(1)}, f32[8,256]{1,0:T(8,128)S(1)}, u32[]{:S(2)}, u32[]{:S(2)}) collective-permute-start(f32[8,256]{1,0:T(8,128)S(1)} %add.3.mid_ref), channel_id=1, source_target_pairs={{2,0},{4,2},{6,4},{0,6},{3,1},{5,3},{7,5},{1,7},{10,8},{12,10},{14... | collective-permute-start | bytes 24584 | tf_op jit(solution)/shard_map/ppermute | solution.py:899
  63.3 2.8 %own_back.1.own_ref = f32[8,64]{1,0:T(8,128)S(1)} custom-call(bf16[1024,64]{1,0:T(8,128)(2,1)S(1)} %copy-done.2, bf16[1024,128]{1,0:T(8,128)(2,1)S(1)} %copy-done.15, f32[1024,128]{1,0:T(8,128)S(1)} %copy-done.13, bf16[640,128]{1,0:T(8,128)(2,1)S(1)} %copy-done.10, bf16[128,512]{1,0:T(8,128)(2,1)S(1)} %copy-done.12, bf16[5,128,128]{2,1,0:T(8,128)(2,1)S(1)} %copy-done.1, ...), custom_call_target="tpu_custom_call" | custom-call | flops 1024 | bytes 1024 | tf_op jit(solution)/shard_map/own_back/pallas_call | solution.py:57
  66.3 2.4 %collective-permute-start.18 = (f32[8,256]{1,0:T(8,128)S(1)}, f32[8,256]{1,0:T(8,128)S(1)}, u32[]{:S(2)}, u32[]{:S(2)}) collective-permute-start(f32[8,256]{1,0:T(8,128)S(1)} %fold.1.mid_ref), channel_id=1, source_target_pairs={{0,1},{1,0},{2,3},{3,2},{4,5},{5,4},{6,7},{7,6},{8,9},{9,8},{10,11... | collective-permute-start | bytes 24584 | tf_op jit(solution)/shard_map/ppermute | solution.py:908
  68.7 1.6 %collective-permute-done.18.low_ref.high_ref = f32[8,256]{1,0:T(8,128)S(1)} collective-permute-done((f32[8,256]{1,0:T(8,128)S(1)}, f32[8,256]{1,0:T(8,128)S(1)}, u32[]{:S(2)}, u32[]{:S(2)}) %collective-permute-start.18) | collective-permute-done | bytes 8224 | tf_op jit(solution)/shard_map/ppermute | solution.py:908
  (84 shorter events, 5.2 us)
Async XLA Ops:
  2.7 27.1 %copy-start = (bf16[1,1,1,64,3200]{4,3,2,1,0:T(8,128)(2,1)S(1)}, bf16[1,1,1,64,3200]{4,3,2,1,0:T(8,128)(2,1)}, u32[]{:S(2)}) copy-start(bf16[1,1,1,64,3200]{4,3,2,1,0:T(8,128)(2,1)} %param.11) | copy-start | bytes 1228804
  2.7 27.1 %copy-start.1 = (bf16[5,128,128]{2,1,0:T(8,128)(2,1)S(1)}, bf16[5,128,128]{2,1,0:T(8,128)(2,1)}, u32[]{:S(2)}) copy-start(bf16[5,128,128]{2,1,0:T(8,128)(2,1)} %mix_ref.7) | copy-start | bytes 491524
  2.7 8.0 %collective-permute-start = (bf16[2,2,2,8,1280]{4,3,2,1,0:T(8,128)(2,1)}, bf16[2,2,2,8,1280]{4,3,2,1,0:T(8,128)(2,1)S(1)}, u32[]{:S(2)}, u32[]{:S(2)}) collective-permute-start(bf16[2,2,2,8,1280]{4,3,2,1,0:T(8,128)(2,1)} %bitcast.50), channel_id=1, source_target_pairs={{0,1},{1,0},{2,3},{3,2},{4,5},{5,4},{6,7},{7,6},{8,9},{9,8},{10,11... | collective-permute-start | bytes 491528 | tf_op jit(solution)/shard_map/ppermute | solution.py:837
  7.6 15.1 %collective-permute-start.5 = (bf16[2,2,2,8,2048]{4,3,2,1,0:T(8,128)(2,1)}, bf16[2,2,2,8,2048]{4,3,2,1,0:T(8,128)(2,1)S(1)}, u32[]{:S(2)}, u32[]{:S(2)}) collective-permute-start(bf16[2,2,2,8,2048]{4,3,2,1,0:T(8,128)(2,1)} %bitcast.48), channel_id=1, source_target_pairs={{0,1},{1,0},{2,3},{3,2},{4,5},{5,4},{6,7},{7,6},{8,9},{9,8},{10,11... | collective-permute-start | bytes 786440 | tf_op jit(solution)/shard_map/ppermute | solution.py:837
  11.7 12.3 %collective-permute-start.1 = (bf16[2,1,4,8,1280]{4,3,2,1,0:T(8,128)(2,1)S(1)}, bf16[2,1,4,8,1280]{4,3,2,1,0:T(8,128)(2,1)S(1)}, u32[]{:S(2)}, u32[]{:S(2)}) collective-permute-start(bf16[2,1,4,8,1280]{4,3,2,1,0:T(8,128)(2,1)S(1)} %get-tuple-element.173), channel_id=1, source_target_pairs={{0,2},{2,4},{4,6},{6,0},{1,3},{3,5},{5,7},{7,1},{8,10},{10,12},{12... | collective-permute-start | bytes 491528 | tf_op jit(solution)/shard_map/ppermute | solution.py:842
  13.3 14.5 %collective-permute-start.2 = (bf16[2,1,4,8,1280]{4,3,2,1,0:T(8,128)(2,1)S(1)}, bf16[2,1,4,8,1280]{4,3,2,1,0:T(8,128)(2,1)S(1)}, u32[]{:S(2)}, u32[]{:S(2)}) collective-permute-start(bf16[2,1,4,8,1280]{4,3,2,1,0:T(8,128)(2,1)S(1)} %get-tuple-element.172), channel_id=1, source_target_pairs={{2,0},{4,2},{6,4},{0,6},{3,1},{5,3},{7,5},{1,7},{10,8},{12,10},{14... | collective-permute-start | bytes 491528 | tf_op jit(solution)/shard_map/ppermute | solution.py:843
  15.6 12.2 %collective-permute-start.3 = (bf16[1,2,4,8,1280]{4,3,2,1,0:T(8,128)(2,1)S(1)}, bf16[1,2,4,8,1280]{4,3,2,1,0:T(8,128)(2,1)S(1)}, u32[]{:S(2)}, u32[]{:S(2)}) collective-permute-start(bf16[1,2,4,8,1280]{4,3,2,1,0:T(8,128)(2,1)S(1)} %get-tuple-element.171), channel_id=1, source_target_pairs={{0,8},{8,16},{16,24},{24,0},{1,9},{9,17},{17,25},{25,1},{2,10},{10... | collective-permute-start | bytes 491528 | tf_op jit(solution)/shard_map/ppermute | solution.py:842
  15.6 12.2 %collective-permute-start.4 = (bf16[1,2,4,8,1280]{4,3,2,1,0:T(8,128)(2,1)S(1)}, bf16[1,2,4,8,1280]{4,3,2,1,0:T(8,128)(2,1)S(1)}, u32[]{:S(2)}, u32[]{:S(2)}) collective-permute-start(bf16[1,2,4,8,1280]{4,3,2,1,0:T(8,128)(2,1)S(1)} %get-tuple-element.170), channel_id=1, source_target_pairs={{8,0},{16,8},{24,16},{0,24},{9,1},{17,9},{25,17},{1,25},{10,2},{18... | collective-permute-start | bytes 491528 | tf_op jit(solution)/shard_map/ppermute | solution.py:843
  22.6 10.8 %copy-start.3 = (bf16[5,128,128]{2,1,0:T(8,128)(2,1)S(1)}, bf16[5,128,128]{2,1,0:T(8,128)(2,1)}, u32[]{:S(2)}) copy-start(bf16[5,128,128]{2,1,0:T(8,128)(2,1)} %out_ref.3) | copy-start | bytes 491524
  22.6 10.8 %copy-start.9 = (bf16[128,640]{1,0:T(8,128)(2,1)S(1)}, bf16[128,640]{1,0:T(8,128)(2,1)}, u32[]{:S(2)}) copy-start(bf16[128,640]{1,0:T(8,128)(2,1)} %rad_ref.3) | copy-start | bytes 491524
  23.9 13.0 %collective-permute-start.7 = (bf16[2,1,4,8,2048]{4,3,2,1,0:T(8,128)(2,1)S(1)}, bf16[2,1,4,8,2048]{4,3,2,1,0:T(8,128)(2,1)S(1)}, u32[]{:S(2)}, u32[]{:S(2)}) collective-permute-start(bf16[2,1,4,8,2048]{4,3,2,1,0:T(8,128)(2,1)S(1)} %get-tuple-element.167), channel_id=1, source_target_pairs={{0,2},{2,4},{4,6},{6,0},{1,3},{3,5},{5,7},{7,1},{8,10},{10,12},{12... | collective-permute-start | bytes 786440 | tf_op jit(solution)/shard_map/ppermute | solution.py:842
  24.0 13.7 %collective-permute-start.8 = (bf16[2,1,4,8,2048]{4,3,2,1,0:T(8,128)(2,1)S(1)}, bf16[2,1,4,8,2048]{4,3,2,1,0:T(8,128)(2,1)S(1)}, u32[]{:S(2)}, u32[]{:S(2)}) collective-permute-start(bf16[2,1,4,8,2048]{4,3,2,1,0:T(8,128)(2,1)S(1)} %get-tuple-element.166), channel_id=1, source_target_pairs={{2,0},{4,2},{6,4},{0,6},{3,1},{5,3},{7,5},{1,7},{10,8},{12,10},{14... | collective-permute-start | bytes 786440 | tf_op jit(solution)/shard_map/ppermute | solution.py:843
  27.9 4.8 %collective-permute-start.9 = (bf16[1,2,4,8,1280]{4,3,2,1,0:T(8,128)(2,1)S(1)}, bf16[1,2,4,8,1280]{4,3,2,1,0:T(8,128)(2,1)S(1)}, u32[]{:S(2)}, u32[]{:S(2)}) collective-permute-start(bf16[1,2,4,8,1280]{4,3,2,1,0:T(8,128)(2,1)S(1)} %get-tuple-element.169), channel_id=1, source_target_pairs={{0,8},{8,16},{16,24},{24,0},{1,9},{9,17},{17,25},{25,1},{2,10},{10... | collective-permute-start | bytes 491528 | tf_op jit(solution)/shard_map/ppermute | solution.py:842
  27.9 5.5 %collective-permute-start.10 = (bf16[1,2,4,8,1280]{4,3,2,1,0:T(8,128)(2,1)S(1)}, bf16[1,2,4,8,1280]{4,3,2,1,0:T(8,128)(2,1)S(1)}, u32[]{:S(2)}, u32[]{:S(2)}) collective-permute-start(bf16[1,2,4,8,1280]{4,3,2,1,0:T(8,128)(2,1)S(1)} %get-tuple-element.168), channel_id=1, source_target_pairs={{8,0},{16,8},{24,16},{0,24},{9,1},{17,9},{25,17},{1,25},{10,2},{18... | collective-permute-start | bytes 491528 | tf_op jit(solution)/shard_map/ppermute | solution.py:843
  29.7 17.8 %collective-permute-start.12 = (bf16[1,2,4,8,2048]{4,3,2,1,0:T(8,128)(2,1)S(1)}, bf16[1,2,4,8,2048]{4,3,2,1,0:T(8,128)(2,1)S(1)}, u32[]{:S(2)}, u32[]{:S(2)}) collective-permute-start(bf16[1,2,4,8,2048]{4,3,2,1,0:T(8,128)(2,1)S(1)} %get-tuple-element.164), channel_id=1, source_target_pairs={{8,0},{16,8},{24,16},{0,24},{9,1},{17,9},{25,17},{1,25},{10,2},{18... | collective-permute-start | bytes 786440 | tf_op jit(solution)/shard_map/ppermute | solution.py:843
  32.7 14.9 %collective-permute-start.6 = (bf16[1,2,4,8,2048]{4,3,2,1,0:T(8,128)(2,1)S(1)}, bf16[1,2,4,8,2048]{4,3,2,1,0:T(8,128)(2,1)S(1)}, u32[]{:S(2)}, u32[]{:S(2)}) collective-permute-start(bf16[1,2,4,8,2048]{4,3,2,1,0:T(8,128)(2,1)S(1)} %get-tuple-element.165), channel_id=1, source_target_pairs={{0,8},{8,16},{16,24},{24,0},{1,9},{9,17},{17,25},{25,1},{2,10},{10... | collective-permute-start | bytes 786440 | tf_op jit(solution)/shard_map/ppermute | solution.py:842
  37.8 9.8 %collective-permute-start.11 = (bf16[1,2,4,8,2048]{4,3,2,1,0:T(8,128)(2,1)S(1)}, bf16[1,2,4,8,2048]{4,3,2,1,0:T(8,128)(2,1)S(1)}, u32[]{:S(2)}, u32[]{:S(2)}) collective-permute-start(bf16[1,2,4,8,2048]{4,3,2,1,0:T(8,128)(2,1)S(1)} %get-tuple-element.163), channel_id=1, source_target_pairs={{0,8},{8,16},{16,24},{24,0},{1,9},{9,17},{17,25},{25,1},{2,10},{10... | collective-permute-start | bytes 786440 | tf_op jit(solution)/shard_map/ppermute | solution.py:842
  38.9 8.7 %collective-permute-start.13 = (bf16[1,2,4,8,2048]{4,3,2,1,0:T(8,128)(2,1)S(1)}, bf16[1,2,4,8,2048]{4,3,2,1,0:T(8,128)(2,1)S(1)}, u32[]{:S(2)}, u32[]{:S(2)}) collective-permute-start(bf16[1,2,4,8,2048]{4,3,2,1,0:T(8,128)(2,1)S(1)} %get-tuple-element.162), channel_id=1, source_target_pairs={{8,0},{16,8},{24,16},{0,24},{9,1},{17,9},{25,17},{1,25},{10,2},{18... | collective-permute-start | bytes 786440 | tf_op jit(solution)/shard_map/ppermute | solution.py:843
  55.4 4.0 %collective-permute-start.14 = (f32[8,128]{1,0:T(8,128)S(1)}, f32[8,128]{1,0:T(8,128)S(1)}, u32[]{:S(2)}, u32[]{:S(2)}) collective-permute-start(f32[8,128]{1,0:T(8,128)S(1)} %get-tuple-element.136), channel_id=1, source_target_pairs={{0,8},{8,16},{16,24},{24,0},{1,9},{9,17},{17,25},{25,1},{2,10},{10... | collective-permute-start | bytes 12296 | tf_op jit(solution)/shard_map/ppermute | solution.py:892
  55.5 3.9 %collective-permute-start.15 = (f32[8,128]{1,0:T(8,128)S(1)}, f32[8,128]{1,0:T(8,128)S(1)}, u32[]{:S(2)}, u32[]{:S(2)}) collective-permute-start(f32[8,128]{1,0:T(8,128)S(1)} %get-tuple-element.137), channel_id=1, source_target_pairs={{8,0},{16,8},{24,16},{0,24},{9,1},{17,9},{25,17},{1,25},{10,2},{18... | collective-permute-start | bytes 12296 | tf_op jit(solution)/shard_map/ppermute | solution.py:893
  57.2 13.1 %copy-start.17 = (bf16[64,256]{1,0:T(8,128)(2,1)S(1)}, bf16[64,256]{1,0:T(8,128)(2,1)}, u32[]{:S(2)}) copy-start(bf16[64,256]{1,0:T(8,128)(2,1)} %get-tuple-element.158.home_ref) | copy-start | bytes 98308
  59.4 6.7 %collective-permute-start.16 = (f32[8,256]{1,0:T(8,128)S(1)}, f32[8,256]{1,0:T(8,128)S(1)}, u32[]{:S(2)}, u32[]{:S(2)}) collective-permute-start(f32[8,256]{1,0:T(8,128)S(1)} %add.3.mid_ref), channel_id=1, source_target_pairs={{0,2},{2,4},{4,6},{6,0},{1,3},{3,5},{5,7},{7,1},{8,10},{10,12},{12... | collective-permute-start | bytes 24584 | tf_op jit(solution)/shard_map/ppermute | solution.py:899
  60.5 5.7 %collective-permute-start.17 = (f32[8,256]{1,0:T(8,128)S(1)}, f32[8,256]{1,0:T(8,128)S(1)}, u32[]{:S(2)}, u32[]{:S(2)}) collective-permute-start(f32[8,256]{1,0:T(8,128)S(1)} %add.3.mid_ref), channel_id=1, source_target_pairs={{2,0},{4,2},{6,4},{0,6},{3,1},{5,3},{7,5},{1,7},{10,8},{12,10},{14... | collective-permute-start | bytes 24584 | tf_op jit(solution)/shard_map/ppermute | solution.py:899
  66.3 4.0 %collective-permute-start.18 = (f32[8,256]{1,0:T(8,128)S(1)}, f32[8,256]{1,0:T(8,128)S(1)}, u32[]{:S(2)}, u32[]{:S(2)}) collective-permute-start(f32[8,256]{1,0:T(8,128)S(1)} %fold.1.mid_ref), channel_id=1, source_target_pairs={{0,1},{1,0},{2,3},{3,2},{4,5},{5,4},{6,7},{7,6},{8,9},{9,8},{10,11... | collective-permute-start | bytes 24584 | tf_op jit(solution)/shard_map/ppermute | solution.py:908
  (15 other events, 115.3 us)

commit v9 on v8

--- a/solution.py
+++ b/solution.py
@@ -67,15 +67,13 @@
 
 
 def cells_kernel(
-    feat_ref, pos_ref, near_ref, counts_ref, order_ref,
+    feat_ref, pos_ref, lists_ref,
     first_ref, own_pos_ref, meta_ref, pick_ref, rows_ref, pos_rows,
 ):
     rows_ref[...] = jnp.zeros_like(rows_ref)
     pos_rows[...] = jnp.zeros_like(pos_rows)
     atoms = feat_ref.shape[0]
-    rows_ref[0:SLOTS, :] = near_ref[...].astype(F32)
-    rows_ref[SLOTS : SLOTS + 1, :] = counts_ref[...].astype(F32)
-    rows_ref[SLOTS + 1 : SLOTS + 2, :] = order_ref[...].astype(F32)
+    rows_ref[0 : SLOTS + 2, :] = lists_ref[...].astype(F32)
     meta = rows_ref[...].T
     meta_ref[...] = meta
     for comp in range(3):
@@ -102,7 +100,7 @@
     rest_ref[...] = mm(pick_ref[...], feat_ref[:, cut:]).astype(BF16)
 
 
-def make_cells(feats, places, near, counts, order):
+def make_cells(feats, places, lists):
     atoms = feats.shape[0]
     out_shape = (
         struct(atoms, 2 * CH + GROUP_COLS[0], dtype=BF16),
@@ -110,13 +108,11 @@
         struct(atoms, CH),
         struct(atoms, atoms, dtype=BF16),
     )
-    args = (feats, places, near, counts, order)
+    args = (feats, places, lists)
     scratch = [pltpu.VMEM((CH, atoms), F32), pltpu.VMEM((CH, atoms), F32)]
-    first, own_pos, meta, pick = call(
-        cells_kernel, "cells", out_shape, scratch, args, limit=60
-    )
+    first, own_pos, meta, pick = call(cells_kernel, "cells", out_shape, scratch, args)
     out_shape = (struct(atoms, sum(GROUP_COLS[1:]), dtype=BF16),)
-    rest = call(rest_kernel, "cells_rest", out_shape, [], (feats, pick), limit=60)[0]
+    rest = call(rest_kernel, "cells_rest", out_shape, [], (feats, pick))[0]
     return first, rest, own_pos, meta
 
 
@@ -151,17 +147,14 @@
     return dist * (1.0 / spacing) - iota((dist.shape[0], nbasis), 1).astype(F32)
 
 
-def radial_net(dist, spacing, rbf_ref, rad_ref):
-    centred = centred_of(dist, spacing, rbf_ref.shape[0])
+def radial_net(dist, spacing, nets_ref):
+    nbasis = nets_ref.shape[0] - 5 * CH
+    centred = centred_of(dist, spacing, nbasis)
     basis = jnp.exp(-0.5 * centred * centred)
-    pre = mm(basis.astype(BF16), rbf_ref[...])
+    pre = mm(basis.astype(BF16), nets_ref[0:nbasis, :])
     hidden = (pre * jax.nn.sigmoid(pre)).astype(BF16)
-    return pre, mm(hidden, rad_ref[...]).astype(BF16)
-
-
-def own_spread(atoms, size=STEP):
-    shape = (atoms, size)
-    return (iota(shape, 1) % atoms == iota(shape, 0)).astype(F32).astype(BF16)
+    weight = [nets_ref[nbasis + d * CH : nbasis + (d + 1) * CH, :] for d in range(5)]
+    return pre, mm(hidden, jnp.concatenate(weight, axis=1)).astype(BF16)
 
 
 def tiled(values, size=STEP):
@@ -262,17 +255,19 @@
     return jnp.concatenate([values, values], axis=1)
 
 
-def forward(group, rows, onehot, feats, radials, gate_ref, wm, nf_ref, mx_ref):
+def forward(group, rows, onehot, feats, radials, gate_ref, wm, nf_ref, mx_ref, slots):
     near = mm(onehot, feats).astype(BF16)
     nf_ref[rows, :] = near
     gate = twice(gate_ref[rows, :])
+    wide = gate.astype(F32) if slots else None
     messages = []
     for cols, degrees, kind in infos_of(group):
         radial = jnp.concatenate([radials[d][rows, :] for d in degrees], axis=1)
-        mixed = mm(near[:, cols] * radial, wm[kind]).astype(BF16)
-        mx_ref[rows, cols] = mixed
-        messages.append(mixed * gate)
-    return jnp.concatenate(messages, axis=1)
+        mixed = mm(near[:, cols] * radial, wm[kind])
+        low = mixed.astype(BF16)
+        mx_ref[rows, cols] = low
+        messages.append(mixed * wide if slots else low * gate)
+    return messages
 
 
 def backward(group, rows, grad, gate_ref, wmt, nf_ref, mx_ref, dot_ref, grad_refs):
@@ -293,18 +288,21 @@
         grad_refs[degree][rows, :] = part.astype(grad_refs[degree].dtype)
 
 
+def over_slots(values, atoms):
+    return jnp.sum(values.reshape(-1, atoms, values.shape[1]), axis=0)
+
+
 def own_forward(group, own_ref, oh_own, radials, gate_ref, wm, nf_ref, mx_ref, acc_ref):
-    spread = own_spread(own_ref.shape[0])
+    atoms = own_ref.shape[0]
     feats = own_ref[:, group_cols(group)]
-    summed = None
     for step in range(OWN_STEPS):
         rows = own_rows(step)
-        message = forward(
-            group, rows, oh_own[rows, :], feats, radials, gate_ref, wm, nf_ref, mx_ref
+        messages = forward(
+            group, rows, oh_own[rows, :], feats, radials, gate_ref, wm, nf_ref, mx_ref, True
         )
-        part = mm(spread, message)
-        summed = part if summed is None else summed + part
-    acc_ref[...] = summed
+        for (cols, _, _), message in zip(infos_of(group), messages):
+            part = over_slots(message, atoms)
+            acc_ref[:, cols] = part if step == 0 else acc_ref[:, cols] + part
 
 
 def own_backward(group, gs_ref, gate_ref, wmt, nf_ref, mx_ref, dot_ref, grad_refs):
@@ -324,10 +322,10 @@
 
     def ghost_forward(step):
         here, _ = ghost_rows(step)
-        message = forward(
-            group, here, oh_gh[here, :], table[...], radials, gate_ref, wm, nf_s, mx_s
+        messages = forward(
+            group, here, oh_gh[here, :], table[...], radials, gate_ref, wm, nf_s, mx_s, False
         )
-        acc_s[...] += mm(dt_gh[:, here], message)
+        acc_s[...] += mm(dt_gh[:, here], jnp.concatenate(messages, axis=1))
 
     over_ghost_steps(steps, ghost_forward)
 
@@ -368,11 +366,11 @@
 
 
 def own_kernel(
-    meta_ref, own_pos_ref, rbf_ref, rad_ref,
+    meta_ref, own_pos_ref, nets_ref,
     oh_own, pre_ref, unit_ref, radt_ref, rbft_ref, home_ref, *radial_refs
 ):
     atoms = meta_ref.shape[0]
-    nbasis = rbf_ref.shape[0]
+    nbasis = rbft_ref.shape[1]
     spacing = spacing_of(atoms, nbasis)
     own_onehots(meta_ref, oh_own)
     here = tiled(own_pos_ref[...].astype(F32))
@@ -380,16 +378,16 @@
         rows = own_rows(step)
         unit, dist = geometry(mm(oh_own[rows, :], own_pos_ref[...]), here)
         unit_ref[rows, :] = unit
-        pre, radial = radial_net(dist, spacing, rbf_ref, rad_ref)
+        pre, radial = radial_net(dist, spacing, nets_ref)
         pre_ref[rows, :] = pre.astype(BF16)
         for degree, ref in enumerate(radial_refs):
             ref[rows, :] = radial[:, degree * CH : (degree + 1) * CH]
     for degree in range(5):
         part = slice(degree * CH, (degree + 1) * CH)
-        radt_ref[part, :] = flip(rad_ref[:, part])
+        radt_ref[part, :] = flip(nets_ref[nbasis + part.start : nbasis + part.stop, :])
     for index in range(nbasis // CH):
         part = slice(index * CH, (index + 1) * CH)
-        rbft_ref[:, part] = flip(rbf_ref[part, :])
+        rbft_ref[:, part] = flip(nets_ref[part, :])
     lanes = home_ref.shape[1]
     lane = iota((atoms, lanes), 1)
     ext_x, ext_y, ext_z = lane // 128, lane // 32 % 4, lane // 8 % 4
@@ -404,19 +402,18 @@
     home_ref[...] = mm(to_atom.T.astype(BF16), to_slot).astype(BF16)
 
 
-def own_stage(meta, own_pos, rbf, rad):
+def own_stage(meta, own_pos, nets):
     atoms = meta.shape[0]
     edges = atoms * HALF
     out_shape = (
         struct(edges, atoms, dtype=BF16),
         struct(edges, CH, dtype=BF16),
         struct(edges, CH),
-        struct(*rad.shape[::-1], dtype=BF16),
-        struct(*rbf.shape[::-1], dtype=BF16),
+        struct(5 * CH, CH, dtype=BF16),
+        struct(CH, nets.shape[0] - 5 * CH, dtype=BF16),
         struct(atoms, 256, dtype=BF16),
     ) + (struct(edges, CH, dtype=BF16),) * 5
-    args = (meta, own_pos, rbf, rad)
-    return call(own_kernel, "own_edges", out_shape, [], args, limit=60)
+    return call(own_kernel, "own_edges", out_shape, [], (meta, own_pos, nets))
 
 
 def scalar_forward(rows, near, radial, mix_ref, m0_ref, gate_ref, nf0_ref):
@@ -426,7 +423,7 @@
     m0_ref[rows, :] = mixed.astype(BF16)
     gate = jax.nn.sigmoid(mixed)
     gate_ref[rows, :] = gate.astype(BF16)
-    return (mixed * gate).astype(BF16)
+    return mixed * gate
 
 
 def own_forward_kernel(groups, scalar, *refs):
@@ -436,7 +433,7 @@
     if scalar:
         m0_ref, gate_ref, nf0_ref, acc0_ref = refs[:4]
         refs = refs[4:]
-        spread = own_spread(own_ref.shape[0])
+        atoms = own_ref.shape[0]
         feats = own_ref[:, 0:CH]
         summed = None
         for step in range(OWN_STEPS):
@@ -445,7 +442,7 @@
                 rows, mm(oh_own[rows, :], feats), radial0[rows, :], mix_ref, m0_ref, gate_ref,
                 nf0_ref,
             )
-            part = mm(spread, message)
+            part = over_slots(message, atoms)
             summed = part if summed is None else summed + part
         acc0_ref[...] = summed
     else:
@@ -478,17 +475,16 @@
 
 
 def start_kernel(
-    p0, p1, p2, p3, p4, own_ref, own_pos_ref, meta_ref, rbf_ref, rad_ref, mix_ref, out_ref,
-    ew_ref, acc0_ref,
+    p0, p1, p2, own_ref, own_pos_ref, meta_ref, nets_ref, mix_ref, out_ref, ew_ref, acc0_ref,
     new_ref, oh_gh, d_gh, dt_gh, pre_ref, unit_ref, gs0_ref, en_ref, m0_gh, gate_gh, nf0_gh,
     radial_gh1, radial_gh2, radial_gh3, radial_gh4,
     table, sems, ghpos, acc_s,
 ):
     radial_gh = (None, radial_gh1, radial_gh2, radial_gh3, radial_gh4)
-    copies = fetch((p0, p1, p2, p3, p4), slice(0, 2 * CH), table, sems)
+    copies = fetch((p0, p1, p2), slice(0, 2 * CH), table, sems)
     atoms = own_ref.shape[0]
     ghosts = table.shape[0]
-    spacing = spacing_of(atoms, rbf_ref.shape[0])
+    spacing = spacing_of(atoms, nets_ref.shape[0] - 5 * CH)
     norm = 1.0 / math.sqrt(SLOTS)
 
     live = live_ghosts(meta_ref)
@@ -549,14 +545,14 @@
         oh_gh[here, :] = onehot
         unit, dist = geometry(mm(onehot, ghpos[...]), mm(source, own_pos_ref[...]))
         unit_ref[here, :] = unit
-        pre, radial = radial_net(dist, spacing, rbf_ref, rad_ref)
+        pre, radial = radial_net(dist, spacing, nets_ref)
         pre_ref[here, :] = pre.astype(BF16)
         for degree in range(1, 5):
             radial_gh[degree][here, :] = radial[:, degree * CH : (degree + 1) * CH]
         message = scalar_forward(
             here, mm(onehot, table[:, 0:CH]), radial[:, 0:CH], mix_ref, m0_gh, gate_gh, nf0_gh
         )
-        acc_s[...] += mm(spread, message)
+        acc_s[...] += mm(spread, message.astype(BF16))
 
     over_ghost_steps(steps, ghost_start)
 
@@ -719,9 +715,9 @@
     before, degrees = len(DEGREES[0]), DEGREES[group]
     gr_a, refs = refs[:before], refs[before:]
     radials, refs = dict(zip(degrees, refs)), refs[len(degrees) :]
-    new_ref, energy_ref, src_ref, flow_ref, fmid_ref, fhigh_ref, gs_ref = refs[:7]
-    table, sems, wm, wmt, wo, wot, nf_s, mx_s, acc_s, dot_c, en_s, fgh_s = refs[7:19]
-    grads = dict(zip(degrees, refs[19:]))
+    new_ref, energy_ref, src_ref, onto_ref, flow_ref, fmid_ref, fhigh_ref, gs_ref = refs[:8]
+    table, sems, wm, wmt, wo, wot, nf_s, mx_s, acc_s, dot_c, en_s, fgh_s = refs[8:20]
+    grads = dict(zip(degrees, refs[20:]))
     copies = fetch((p0, p1, p2, p3, p4), slice(0, GROUP_COLS[group]), table, sems)
     atoms = own_ref.shape[0]
     spacing = spacing_of(atoms, rbft_ref.shape[1])
@@ -744,6 +740,7 @@
 
     fgh_s[...] = jnp.zeros_like(fgh_s)
     src_ref[...] = jnp.zeros_like(src_ref)
+    onto_ref[...] = jnp.zeros_like(onto_ref)
     gs0_low = gs0_ref[...].astype(BF16)
     mix_t = flip(mix_ref[0])
 
@@ -752,7 +749,7 @@
         grad = mm(d_gh[here, :], gs0_low)
         pull, top, rest = finish(
             grad, m0_ref[here, :], nf0_ref[here, :], sum_of((dot_a, dot_c), here),
-            degree_parts(gr_a + refs[19:], here), pre_gh[here, :], unit_gh[here, :], spacing,
+            degree_parts(gr_a + refs[20:], here), pre_gh[here, :], unit_gh[here, :], spacing,
             radt_ref, rbft_ref, mix_t,
         )
         pull_top = pull.astype(BF16)
@@ -778,6 +775,7 @@
         struct(atoms, feat, dtype=BF16),
         struct(1, atoms),
         struct(atoms, CH),
+        struct(8, atoms),
     ) + tuple(struct(8, size) for size in sizes) + (
         struct(atoms, GROUP_COLS[1], dtype=BF16),
     )
@@ -795,33 +793,35 @@
 
 
 def own_back_kernel(
-    oh_own, pre_own, unit_own, radt_ref, rbft_ref, mix_ref, gs0_ref, src_ref,
+    steps, oh_own, pre_own, unit_own, radt_ref, rbft_ref, mix_ref, gs0_ref,
     m0_ref, nf0_ref, dot_a, dot_c, *refs
 ):
-    gr_own, (force_ref,) = refs[:PARTIALS], refs[PARTIALS:]
+    gr_own, (src_in, onto_in, src_out, onto_out) = refs[:PARTIALS], refs[PARTIALS:]
     atoms = oh_own.shape[1]
     spacing = spacing_of(atoms, rbft_ref.shape[1])
     grad = tiled(gs0_ref[...])
     mix_t = flip(mix_ref[0])
-    src = src_ref[...]
-    onto = jnp.zeros((8, atoms), F32)
-    for step in range(OWN_STEPS):
+    src = src_in[...]
+    onto = onto_in[...]
+    for step in steps:
         rows = own_rows(step)
         pull, top, rest = finish(
             grad, m0_ref[rows, :], nf0_ref[rows, :], sum_of((dot_a, dot_c), rows),
             degree_parts(gr_own, rows), pre_own[rows, :], unit_own[rows, :], spacing, radt_ref,
             rbft_ref, mix_t,
         )
-        src += jnp.sum(pull.reshape(STEP // atoms, atoms, CH), axis=0)
+        src += over_slots(pull, atoms)
         onehot = oh_own[rows, :]
         onto += mm(top, onehot) + mm(rest, onehot)
-    force_ref[...] = onto - src.T[0:8, :]
-
-
-def own_back_stage(*args):
-    oh_own = args[0]
-    out_shape = (struct(8, oh_own.shape[1]),)
-    return call(own_back_kernel, "own_back", out_shape, [], args)[0]
+    src_out[...] = src
+    onto_out[...] = onto
+
+
+def own_back_stage(steps, *args):
+    atoms = args[0].shape[1]
+    out_shape = (struct(atoms, CH), struct(8, atoms))
+    kernel = functools.partial(own_back_kernel, tuple(steps))
+    return call(kernel, "own_back", out_shape, [], args)
 
 
 def ring(axis):
@@ -871,7 +871,7 @@
     )
 
 
-def forces_kernel(mid_ref, low_ref, high_ref, own_ref, home_ref, out_ref):
+def forces_kernel(mid_ref, low_ref, high_ref, src_ref, onto_ref, home_ref, out_ref):
     values = mid_ref[...]
     lanes = values.shape[1]
     ext_z = iota(values.shape, 1) // 8 % 4
@@ -882,7 +882,8 @@
     second = values.astype(BF16)
     third = (values - second.astype(F32)).astype(BF16)
     home = home_ref[...]
-    total = own_ref[...] + (mm_nt(first, home) + (mm_nt(second, home) + mm_nt(third, home)))
+    total = onto_ref[...] - src_ref[...].T[0:8, :]
+    total += (mm_nt(first, home) + (mm_nt(second, home) + mm_nt(third, home)))
     for comp in range(3):
         out_ref[comp] = -total[comp : comp + 1, :]
 
@@ -924,22 +925,25 @@
 ):
     feats = features[0, 0, 0]
     places = jnp.swapaxes(positions[0, 0], 0, 1)
-    cells0, cells1, own_pos, meta = make_cells(
-        feats, places, neighbours[0, 0, 0].T, counts[0, 0], cell_atoms[0, 0]
-    )
+    lists = jnp.concatenate([neighbours[0, 0, 0].T, counts[0, 0], cell_atoms[0, 0]], axis=0)
+    cells0, cells1, own_pos, meta = make_cells(feats, places, lists)
     hold = lax.optimization_barrier
     block0, block1 = (part.reshape(2, 2, 2, 8, part.shape[1]) for part in (cells0, cells1))
     block0 = grown(block0, "gz", 2)
     block0, own_pos, meta = hold((block0, own_pos, meta))
+    nets = jnp.concatenate(
+        [rbf_weight] + [radial_weight[:, d * CH : (d + 1) * CH] for d in range(5)], axis=0
+    )
     y0 = neighbours_of(block0, "gy", 1)
-    x0_in = neighbours_of(block0, "gx", 0)
     oh_own, pre_own, unit_own, radt, rbft, home, *radial_own = own_stage(
-        meta, own_pos, rbf_weight, radial_weight
+        meta, own_pos, nets
     )
     block1 = grown(block1, "gz", 2)
     y1 = neighbours_of(block1, "gy", 1)
-    y0, x0_in, block1, oh_own = hold((y0, x0_in, block1, oh_own))
-    pieces0 = ghost_pieces(y0, block0, x0_in)
+    y0, block1, oh_own = hold((y0, block1, oh_own))
+    middle = jnp.concatenate([y0[0], block0, y0[1]], axis=1)
+    low, high = neighbours_of(middle, "gx", 0)
+    pieces0 = tuple(flat_rows(piece) for piece in (low, middle, high))
     x1_in = neighbours_of(block1, "gx", 0)
     (m0_own, gate_own, nf0_own, acc0), (own_a,) = own_forward_stage(
         (0,), feats, mix_weight, oh_own, radial_own
@@ -947,8 +951,7 @@
     (
         new_0, oh_gh, d_gh, dt_gh, pre_gh, unit_gh, gs0, en_0, m0_gh, gate_gh, nf0_gh, *radial_gh,
     ) = start_stage(
-        pieces0, feats, own_pos, meta, rbf_weight, radial_weight, mix_weight, out_weight,
-        energy_weight[None], acc0,
+        pieces0, feats, own_pos, meta, nets, mix_weight, out_weight, energy_weight[None], acc0,
     )
     y1, gate_gh = hold((y1, gate_gh))
     pieces1 = ghost_pieces(y1, block1, x1_in)
@@ -958,7 +961,7 @@
     )
     en_a, gate_own = hold((en_a, gate_own))
     _, (own_b,) = own_forward_stage((1,), feats, mix_weight, oh_own, radial_own, gate_own)
-    new, energy, src, low, mid, high, gs_b = third_stage(
+    new, energy, src, onto, low, mid, high, gs_b = third_stage(
         pieces1, *shared, own_b[2], radt, rbft, gs0, en_0, en_a, new_0, new_a, pre_gh,
         unit_gh, m0_gh, nf0_gh, dot_gh_a, *gr_gh_a,
         *[radial_gh[degree - 1] for degree in DEGREES[1]],
@@ -967,14 +970,14 @@
     dot_own_b, *gr_own_b = own_backward_stage(1, mix_weight, gs_b, gate_own, *own_b[:2])
     arrived, gs0, dot_own_b = hold((arrived, gs0, dot_own_b))
     mid, from_low, from_high = give_back_y(mid + arrived)
-    own = own_back_stage(
-        oh_own, pre_own, unit_own, radt, rbft, mix_weight, gs0, src, m0_own, nf0_own, dot_own_a,
-        dot_own_b, *gr_own_a, *gr_own_b,
-    )
-    from_low, from_high, own = hold((from_low, from_high, own))
+    back = (oh_own, pre_own, unit_own, radt, rbft, mix_weight, gs0, m0_own, nf0_own)
+    back += (dot_own_a, dot_own_b, *gr_own_a, *gr_own_b)
+    src, onto = own_back_stage(range(2), *back, src, onto)
+    from_low, from_high, src = hold((from_low, from_high, src))
     folded = give_back_z(fold(mid, from_low, from_high))
-    args = (*folded, own, home)
-    out_shape = (struct(3, 1, own.shape[1]),)
+    src, onto = own_back_stage(range(2, 4), *back, src, onto)
+    args = (*folded, src, onto, home)
+    out_shape = (struct(3, 1, src.shape[0]),)
     forces = call(forces_kernel, "forces", out_shape, [], args)[0]
     return (
         new[None, None, None],

time: 71.3 us -> 72.6 us (1.018)
  Pallas kernels: 36.6 us -> 29.1 us
  local copies, waits for them, and re-layouts: 0.37 us -> 6.82 us
  waiting for transfers between devices: 5.88 us -> 9.45 us
  other arithmetic: 2.3 us -> 0.99 us
    pallas_call x12 -> x13, Pallas kernels: 36.6 us -> 29.1 us  [call(): pl.pallas_call(kernel, out_shape=out_shape, in_specs=specs or [pl.BlockSp...]
    ppermute x6 -> x5, waiting for transfers between devices: 1.18 us -> 8.54 us  [neighbours_of(): after = lax.ppermute(lax.slice_in_dim(block, 0, 1, axis=dim), axis, down)]
    unnamed x42 -> x22, local copies, waits for them, and re-layouts: 0.12 us -> 5.74 us
    ppermute x2, waiting for transfers between devices: 2.95 us -> 0.01 us  [neighbours_of(): other = lax.ppermute(block, axis, up)]
    ppermute x6 -> x5, starting transfers between devices: 3.28 us -> 5.36 us  [neighbours_of(): lax.ppermute(lax.slice_in_dim(block, length - 1, length, axis=dim), axis,...]
    concatenate x2, other arithmetic: 2.09 us -> 0.1 us  [grown(): return jnp.concatenate([before, block, after], axis=dim)]
    ppermute x6 -> x5, starting transfers between devices: 10.3 us -> 9.04 us  [neighbours_of(): after = lax.ppermute(lax.slice_in_dim(block, 0, 1, axis=dim), axis, down)]
    ppermute x1, waiting for transfers between devices: 1.63 us -> 0.63 us  [give_back_z(): from_low = lax.ppermute(mid, 'gz', up)]
  transfers between devices with their start and end apart: 19 -> 17, of which waited for: 5 -> 5; matrix products, arithmetic and copies ran while one was open for 4% -> 7% of each run, Pallas kernels for 36% -> 28%
where the time goes in v9:
time: 72.6 us; the launch traced here: 72 us
  Pallas kernels  29.1 us (40%)
  starting transfers between devices  24.7 us (34%)
  waiting for transfers between devices  9.45 us (13%)
  local copies, waits for them, and re-layouts  6.82 us (9%)
  other arithmetic  0.99 us (1%)
  between operations  0.98 us (1%)
    pallas_call x13, Pallas kernels, call(): pl.pallas_call(kernel, out_shape=out_shape, in_specs=specs or [pl.BlockSp...  29.1 us
    ppermute x5, starting transfers between devices, neighbours_of(): after = lax.ppermute(lax.slice_in_dim(block, 0, 1, axis=dim), axis, down)  9.04 us
    ppermute x5, waiting for transfers between devices, neighbours_of(): after = lax.ppermute(lax.slice_in_dim(block, 0, 1, axis=dim), axis, down)  8.54 us
    unnamed x22, local copies, waits for them, and re-layouts  5.74 us
    ppermute x5, starting transfers between devices, neighbours_of(): lax.ppermute(lax.slice_in_dim(block, length - 1, length, axis=dim), axis,...  5.36 us
    ppermute x2, starting transfers between devices, give_back_y(): return (mid, lax.ppermute(mid, 'gy', up), lax.ppermute(mid, 'gy', down))  3.88 us
    ppermute x2, starting transfers between devices, neighbours_of(): other = lax.ppermute(block, axis, up)  3.11 us
    ppermute x1, starting transfers between devices, give_back_x(): from_high = lax.ppermute(low, 'gx', down)  1.73 us
  transfers between devices with their start and end apart: 17, of which 5 were waited for; matrix products, arithmetic and copies ran while one was open for 7% of the time, Pallas kernels for 28%

profile of v9, /device:TPU:0, one launch (start us, length us, event | category | flops | bytes accessed | tf_op | source)
XLA Modules:
  0.0 72.0 jit_solution(15249842018140744947)
XLA Ops:
  1.4 1.0 %copy-done = bf16[1,1,1,64,3200]{4,3,2,1,0:T(8,128)(2,1)S(1)} copy-done((bf16[1,1,1,64,3200]{4,3,2,1,0:T(8,128)(2,1)S(1)}, bf16[1,1,1,64,3200]{4,3,2,1,0:T(8,128)(2,1)}, u32[]{:S(2)}) %copy-start) | copy-done | bytes 409624
  3.4 3.0 %collective-permute-start = (bf16[2,2,2,8,1280]{4,3,2,1,0:T(8,128)(2,1)S(1)}, bf16[2,2,2,8,1280]{4,3,2,1,0:T(8,128)(2,1)S(1)}, u32[]{:S(2)}, u32[]{:S(2)}) collective-permute-start(bf16[2,2,2,8,1280]{4,3,2,1,0:T(8,128)(2,1)S(1)} %bitcast.43), channel_id=1, source_target_pairs={{0,1},{1,0},{2,3},{3,2},{4,5},{5,4},{6,7},{7,6},{8,9},{9,8},{10,11... | collective-permute-start | bytes 491528 | tf_op jit(solution)/shard_map/ppermute | solution.py:837
  6.7 0.9 %constant_dynamic-update-slice_fusion = bf16[1152,128]{1,0:T(8,128)(2,1)S(1)} fusion(bf16[512,128]{1,0:T(8,128)(2,1)} %param.16), kind=kLoop, calls=%fused_computation.8 | loop fusion | bytes 262144
  10.7 0.8 %slice_dynamic-update-slice_fusion.nets_ref = bf16[1152,128]{1,0:T(8,128)(2,1)S(1)} fusion(bf16[1152,128]{1,0:T(8,128)(2,1)S(1)} %slice_dynamic-update-slice_fusion.1, bf16[128,640]{1,0:T(8,128)(2,1)} %param.17), kind=kLoop, calls=%fused_computation.3 | loop fusion | bytes 65536 | tf_op jit(solution)/shard_map/concatenate | solution.py:934
  11.6 2.1 %collective-permute-start.1 = (bf16[2,1,4,8,1280]{4,3,2,1,0:T(8,128)(2,1)S(1)}, bf16[2,1,4,8,1280]{4,3,2,1,0:T(8,128)(2,1)S(1)}, u32[]{:S(2)}, u32[]{:S(2)}) collective-permute-start(bf16[2,1,4,8,1280]{4,3,2,1,0:T(8,128)(2,1)S(1)} %get-tuple-element.177), channel_id=1, source_target_pairs={{0,2},{2,4},{4,6},{6,0},{1,3},{3,5},{5,7},{7,1},{8,10},{10,12},{12... | collective-permute-start | bytes 491528 | tf_op jit(solution)/shard_map/ppermute | solution.py:842
  13.8 2.1 %collective-permute-start.2 = (bf16[2,1,4,8,1280]{4,3,2,1,0:T(8,128)(2,1)S(1)}, bf16[2,1,4,8,1280]{4,3,2,1,0:T(8,128)(2,1)S(1)}, u32[]{:S(2)}, u32[]{:S(2)}) collective-permute-start(bf16[2,1,4,8,1280]{4,3,2,1,0:T(8,128)(2,1)S(1)} %get-tuple-element.176), channel_id=1, source_target_pairs={{2,0},{4,2},{6,4},{0,6},{3,1},{5,3},{7,5},{1,7},{10,8},{12,10},{14... | collective-permute-start | bytes 491528 | tf_op jit(solution)/shard_map/ppermute | solution.py:843
  15.9 2.9 %own_edges.1 = (bf16[1024,64]{1,0:T(8,128)(2,1)S(1)}, bf16[1024,128]{1,0:T(8,128)(2,1)S(1)}, f32[1024,128]{1,0:T(8,128)S(1)}, bf16[640,128]{1,0:T(8,128)(2,1)S(1...) custom-call(f32[64,128]{1,0:T(8,128)S(1)} %get-tuple-element.89.meta, ...), custom_call_target="tpu_custom_call" | custom-call | flops 1024 | bytes 1024 | tf_op jit(solution)/shard_map/own_edges/pallas_call | solution.py:57
  19.0 3.8 %collective-permute-start.6 = (bf16[2,1,4,8,2048]{4,3,2,1,0:T(8,128)(2,1)S(1)}, bf16[2,1,4,8,2048]{4,3,2,1,0:T(8,128)(2,1)S(1)}, u32[]{:S(2)}, u32[]{:S(2)}) collective-permute-start(bf16[2,1,4,8,2048]{4,3,2,1,0:T(8,128)(2,1)S(1)} %get-tuple-element.174), channel_id=1, source_target_pairs={{2,0},{4,2},{6,4},{0,6},{3,1},{5,3},{7,5},{1,7},{10,8},{12,10},{14... | collective-permute-start | bytes 786440 | tf_op jit(solution)/shard_map/ppermute | solution.py:843
  22.8 4.7 %collective-permute-done.2 = bf16[2,1,4,8,1280]{4,3,2,1,0:T(8,128)(2,1)S(1)} collective-permute-done((bf16[2,1,4,8,1280]{4,3,2,1,0:T(8,128)(2,1)S(1)}, bf16[2,1,4,8,1280]{4,3,2,1,0:T(8,128)(2,1)S(1)}, u32[]{:S(2)}, u32[]{:S(2)}) %collective-permute-start.2) | collective-permute-done | bytes 163872 | tf_op jit(solution)/shard_map/ppermute | solution.py:843
  28.2 1.4 %collective-permute-start.10 = (bf16[1,2,4,8,2048]{4,3,2,1,0:T(8,128)(2,1)S(1)}, bf16[1,2,4,8,2048]{4,3,2,1,0:T(8,128)(2,1)S(1)}, u32[]{:S(2)}, u32[]{:S(2)}) collective-permute-start(bf16[1,2,4,8,2048]{4,3,2,1,0:T(8,128)(2,1)S(1)} %get-tuple-element.172), channel_id=1, source_target_pairs={{8,0},{16,8},{24,16},{0,24},{9,1},{17,9},{25,17},{1,25},{10,2},{18... | collective-permute-start | bytes 786440 | tf_op jit(solution)/shard_map/ppermute | solution.py:843
  29.6 1.5 %own_forward_a.1 = (bf16[1024,128]{1,0:T(8,128)(2,1)S(1)}, bf16[1024,128]{1,0:T(8,128)(2,1)S(1)}, bf16[1024,128]{1,0:T(8,128)(2,1)S(1)}, f32[64,128]{1,0:T(8,128...) custom-call(bf16[64,3200]{1,0:T(8,128)(2,1)S(1)} %bitcast.25, ...), custom_call_target="tpu_custom_call" | custom-call | flops 1024 | bytes 1024 | tf_op jit(solution)/shard_map/own_forward_a/pallas_call | solution.py:57
  31.1 3.9 %collective-permute-done.8 = bf16[1,4,4,8,1280]{4,3,2,1,0:T(8,128)(2,1)S(1)} collective-permute-done((bf16[1,4,4,8,1280]{4,3,2,1,0:T(8,128)(2,1)S(1)}, bf16[1,4,4,8,1280]{4,3,2,1,0:T(8,128)(2,1)S(1)}, u32[]{:S(2)}, u32[]{:S(2)}) %collective-permute-start.8) | collective-permute-done | bytes 327712 | tf_op jit(solution)/shard_map/ppermute | solution.py:843
  34.9 2.6 %collective-permute-start.4 = (bf16[1,2,4,8,2048]{4,3,2,1,0:T(8,128)(2,1)S(1)}, bf16[1,2,4,8,2048]{4,3,2,1,0:T(8,128)(2,1)S(1)}, u32[]{:S(2)}, u32[]{:S(2)}) collective-permute-start(bf16[1,2,4,8,2048]{4,3,2,1,0:T(8,128)(2,1)S(1)} %get-tuple-element.173), channel_id=1, source_target_pairs={{0,8},{8,16},{16,24},{24,0},{1,9},{9,17},{17,25},{25,1},{2,10},{10... | collective-permute-start | bytes 786440 | tf_op jit(solution)/shard_map/ppermute | solution.py:842
  37.7 3.4 %ghost_start.1 = (bf16[64,128]{1,0:T(8,128)(2,1)S(1)}, bf16[1024,512]{1,0:T(8,128)(2,1)S(1)}, bf16[1024,64]{1,0:T(8,128)(2,1)S(1)}, bf16[64,1024]{1,0:T(8,128)(2...) custom-call(bf16[128,1280]{1,0:T(8,128)(2,1)S(1)} %bitcast.35, ...), custom_call_target="tpu_custom_call" | custom-call | flops 1024 | bytes 1024 | tf_op jit(solution)/shard_map/ghost_start/pallas_call | solution.py:57
  41.3 1.7 %collective-permute-start.11 = (bf16[1,2,4,8,2048]{4,3,2,1,0:T(8,128)(2,1)S(1)}, bf16[1,2,4,8,2048]{4,3,2,1,0:T(8,128)(2,1)S(1)}, u32[]{:S(2)}, u32[]{:S(2)}) collective-permute-start(bf16[1,2,4,8,2048]{4,3,2,1,0:T(8,128)(2,1)S(1)} %get-tuple-element.170), channel_id=1, source_target_pairs={{8,0},{16,8},{24,16},{0,24},{9,1},{17,9},{25,17},{1,25},{10,2},{18... | collective-permute-start | bytes 786440 | tf_op jit(solution)/shard_map/ppermute | solution.py:843
  43.0 4.6 %pairs_a.1 = (bf16[64,1024]{1,0:T(8,128)(2,1)S(1)}, f32[64,128]{1,0:T(8,128)S(1)}, bf16[64,1024]{1,0:T(8,128)(2,1)}, bf16[1024,128]{1,0:T(8,128)(2,1)S(1)}, bf16...) custom-call(bf16[128,1280]{1,0:T(8,128)(2,1)S(1)} %bitcast.36, ...), custom_call_target="tpu_custom_call" | custom-call | flops 1024 | bytes 1024 | tf_op jit(solution)/shard_map/pairs_a/pallas_call | solution.py:57
  47.6 2.5 %own_forward_b.1 = (bf16[1024,2048]{1,0:T(8,128)(2,1)S(1)}, bf16[1024,2048]{1,0:T(8,128)(2,1)S(1)}, f32[64,2048]{1,0:T(8,128)S(1)}) custom-call(bf16[64,3200]{1,0:T(8,128)(2,1)S(1)} %bitcast.28, bf16[5,128,128]{2,1,0:T(8,128)(2,1)S(1)} %copy-done.2, bf16[1024,64]{1,0:T(8,128)(2,1)S(1)} %get-tuple-element.95.refs_2_.oh_own, ...), custom_call_target="tpu_custom_call" | custom-call | flops 1024 | bytes 1024 | tf_op jit(solution)/shard_map/own_forward_b/pallas_call | solution.py:57
  50.3 7.7 %third_group.1 = (bf16[64,3200]{1,0:T(8,128)(2,1)}, f32[1,64]{1,0:T(1,128)}, f32[64,128]{1,0:T(8,128)S(1)}, f32[8,64]{1,0:T(8,128)S(1)}, f32[8,128]{1,0:T(8,128)...) custom-call(bf16[64,2048]{1,0:T(8,128)(2,1)S(1)} %bitcast.40, ...), custom_call_target="tpu_custom_call" | custom-call | flops 1024 | bytes 1024 | tf_op jit(solution)/shard_map/third_group/pallas_call | solution.py:57
  58.1 1.7 %collective-permute-start.13 = (f32[8,128]{1,0:T(8,128)S(1)}, f32[8,128]{1,0:T(8,128)S(1)}, u32[]{:S(2)}, u32[]{:S(2)}) collective-permute-start(f32[8,128]{1,0:T(8,128)S(1)} %get-tuple-element.138), channel_id=1, source_target_pairs={{8,0},{16,8},{24,16},{0,24},{9,1},{17,9},{25,17},{1,25},{10,2},{18... | collective-permute-start | bytes 12296 | tf_op jit(solution)/shard_map/ppermute | solution.py:894
  59.8 2.2 %own_backward_b.1 = (bf16[1024,128]{1,0:T(8,128)(2,1)S(1)}, bf16[1024,128]{1,0:T(8,128)(2,1)S(1)}, bf16[1024,128]{1,0:T(8,128)(2,1)S(1)}) custom-call(bf16[5,128,128]{2,1,0:T(8,128)(2,1)S(1)} %copy-done.2, bf16[64,2048]{1,0:T(8,128)(2,1)S(1)} %get-tuple-element.139.gs_ref, bf16[1024,128]{1,0:T(8,128)(2,1)S(1)} %get-tuple-element.116.refs_12_.refs_8_.gate_ref, ...), custom_call_target="tpu_custom_call" | custom-call | flops 1024 | bytes 1024 | tf_op jit(solution)/shard_map/own_backward_b/pallas_call | solution.py:57
  62.7 3.2 %collective-permute-start.15 = (f32[8,256]{1,0:T(8,128)S(1)}, f32[8,256]{1,0:T(8,128)S(1)}, u32[]{:S(2)}, u32[]{:S(2)}) collective-permute-start(f32[8,256]{1,0:T(8,128)S(1)} %add.3.mid_ref), channel_id=1, source_target_pairs={{2,0},{4,2},{6,4},{0,6},{3,1},{5,3},{7,5},{1,7},{10,8},{12,10},{14... | collective-permute-start | bytes 24584 | tf_op jit(solution)/shard_map/ppermute | solution.py:900
  65.9 1.5 %own_back.2 = (f32[64,128]{1,0:T(8,128)S(1)}, f32[8,64]{1,0:T(8,128)S(1)}) custom-call(bf16[1024,64]{1,0:T(8,128)(2,1)S(1)} %get-tuple-element.95.refs_2_.oh_own, bf16[1024,128]{1,0:T(8,128)(2,1)S(1)} %get-tuple-element.144.pre_own, f32[1024,128]{1,0:T(8,128)S(1)} %get-tuple-element.145.unit_own, bf16[640,128]{1,0:T(8,128)(2,1)S(1)} %get-tuple-element.118.radt_ref, ...), custom_call_target="tpu_custom_call" | custom-call | flops 1024 | bytes 1024 | tf_op jit(solution)/shard_map/own_back/pallas_call | solution.py:57
  67.6 1.5 %collective-permute-start.16 = (f32[8,256]{1,0:T(8,128)S(1)}, f32[8,256]{1,0:T(8,128)S(1)}, u32[]{:S(2)}, u32[]{:S(2)}) collective-permute-start(f32[8,256]{1,0:T(8,128)S(1)} %fold.1.mid_ref), channel_id=1, source_target_pairs={{0,1},{1,0},{2,3},{3,2},{4,5},{5,4},{6,7},{7,6},{8,9},{9,8},{10,11... | collective-permute-start | bytes 24584 | tf_op jit(solution)/shard_map/ppermute | solution.py:909
  69.1 1.5 %own_back.3 = (f32[64,128]{1,0:T(8,128)S(1)}, f32[8,64]{1,0:T(8,128)S(1)}) custom-call(bf16[1024,64]{1,0:T(8,128)(2,1)S(1)} %get-tuple-element.95.refs_2_.oh_own, bf16[1024,128]{1,0:T(8,128)(2,1)S(1)} %get-tuple-element.144.pre_own, f32[1024,128]{1,0:T(8,128)S(1)} %get-tuple-element.145.unit_own, bf16[640,128]{1,0:T(8,128)(2,1)S(1)} %get-tuple-element.118.radt_ref, ...), custom_call_target="tpu_custom_call" | custom-call | flops 1024 | bytes 1024 | tf_op jit(solution)/shard_map/own_back/pallas_call | solution.py:57
  (61 shorter events, 8.8 us)
Async XLA Ops:
  1.4 1.0 %copy-start = (bf16[1,1,1,64,3200]{4,3,2,1,0:T(8,128)(2,1)S(1)}, bf16[1,1,1,64,3200]{4,3,2,1,0:T(8,128)(2,1)}, u32[]{:S(2)}) copy-start(bf16[1,1,1,64,3200]{4,3,2,1,0:T(8,128)(2,1)} %param.11) | copy-start | bytes 1228804
  2.4 0.7 copy-start.5
  3.4 8.1 %collective-permute-start = (bf16[2,2,2,8,1280]{4,3,2,1,0:T(8,128)(2,1)S(1)}, bf16[2,2,2,8,1280]{4,3,2,1,0:T(8,128)(2,1)S(1)}, u32[]{:S(2)}, u32[]{:S(2)}) collective-permute-start(bf16[2,2,2,8,1280]{4,3,2,1,0:T(8,128)(2,1)S(1)} %bitcast.43), channel_id=1, source_target_pairs={{0,1},{1,0},{2,3},{3,2},{4,5},{5,4},{6,7},{7,6},{8,9},{9,8},{10,11... | collective-permute-start | bytes 491528 | tf_op jit(solution)/shard_map/ppermute | solution.py:837
  6.6 12.1 %collective-permute-start.3 = (bf16[2,2,2,8,2048]{4,3,2,1,0:T(8,128)(2,1)S(1)}, bf16[2,2,2,8,2048]{4,3,2,1,0:T(8,128)(2,1)S(1)}, u32[]{:S(2)}, u32[]{:S(2)}) collective-permute-start(bf16[2,2,2,8,2048]{4,3,2,1,0:T(8,128)(2,1)S(1)} %bitcast.37), channel_id=1, source_target_pairs={{0,1},{1,0},{2,3},{3,2},{4,5},{5,4},{6,7},{7,6},{8,9},{9,8},{10,11... | collective-permute-start | bytes 786440 | tf_op jit(solution)/shard_map/ppermute | solution.py:837
  10.7 18.8 %copy-start.1 = (bf16[1,1,1,64,3200]{4,3,2,1,0:T(8,128)(2,1)S(1)}, bf16[1,1,1,64,3200]{4,3,2,1,0:T(8,128)(2,1)}, u32[]{:S(2)}) copy-start(bf16[1,1,1,64,3200]{4,3,2,1,0:T(8,128)(2,1)} %param.11) | copy-start | bytes 1228804
  10.7 18.8 %copy-start.2 = (bf16[5,128,128]{2,1,0:T(8,128)(2,1)S(1)}, bf16[5,128,128]{2,1,0:T(8,128)(2,1)}, u32[]{:S(2)}) copy-start(bf16[5,128,128]{2,1,0:T(8,128)(2,1)} %mix_ref.9) | copy-start | bytes 491524
  11.6 11.1 %collective-permute-start.1 = (bf16[2,1,4,8,1280]{4,3,2,1,0:T(8,128)(2,1)S(1)}, bf16[2,1,4,8,1280]{4,3,2,1,0:T(8,128)(2,1)S(1)}, u32[]{:S(2)}, u32[]{:S(2)}) collective-permute-start(bf16[2,1,4,8,1280]{4,3,2,1,0:T(8,128)(2,1)S(1)} %get-tuple-element.177), channel_id=1, source_target_pairs={{0,2},{2,4},{4,6},{6,0},{1,3},{3,5},{5,7},{7,1},{8,10},{10,12},{12... | collective-permute-start | bytes 491528 | tf_op jit(solution)/shard_map/ppermute | solution.py:842
  13.8 13.7 %collective-permute-start.2 = (bf16[2,1,4,8,1280]{4,3,2,1,0:T(8,128)(2,1)S(1)}, bf16[2,1,4,8,1280]{4,3,2,1,0:T(8,128)(2,1)S(1)}, u32[]{:S(2)}, u32[]{:S(2)}) collective-permute-start(bf16[2,1,4,8,1280]{4,3,2,1,0:T(8,128)(2,1)S(1)} %get-tuple-element.176), channel_id=1, source_target_pairs={{2,0},{4,2},{6,4},{0,6},{3,1},{5,3},{7,5},{1,7},{10,8},{12,10},{14... | collective-permute-start | bytes 491528 | tf_op jit(solution)/shard_map/ppermute | solution.py:843
  18.7 19.0 %copy-start.3 = (bf16[5,128,128]{2,1,0:T(8,128)(2,1)S(1)}, bf16[5,128,128]{2,1,0:T(8,128)(2,1)}, u32[]{:S(2)}) copy-start(bf16[5,128,128]{2,1,0:T(8,128)(2,1)} %out_ref.3) | copy-start | bytes 491524
  18.7 19.0 %copy-start.6 = (f32[128]{0:T(128)S(1)}, f32[128]{0:T(128)}, u32[]{:S(2)}) copy-start(f32[128]{0:T(128)} %param.20) | copy-start | bytes 1540
  18.9 22.2 %collective-permute-start.5 = (bf16[2,1,4,8,2048]{4,3,2,1,0:T(8,128)(2,1)S(1)}, bf16[2,1,4,8,2048]{4,3,2,1,0:T(8,128)(2,1)S(1)}, u32[]{:S(2)}, u32[]{:S(2)}) collective-permute-start(bf16[2,1,4,8,2048]{4,3,2,1,0:T(8,128)(2,1)S(1)} %get-tuple-element.175), channel_id=1, source_target_pairs={{0,2},{2,4},{4,6},{6,0},{1,3},{3,5},{5,7},{7,1},{8,10},{10,12},{12... | collective-permute-start | bytes 786440 | tf_op jit(solution)/shard_map/ppermute | solution.py:842
  19.0 22.1 %collective-permute-start.6 = (bf16[2,1,4,8,2048]{4,3,2,1,0:T(8,128)(2,1)S(1)}, bf16[2,1,4,8,2048]{4,3,2,1,0:T(8,128)(2,1)S(1)}, u32[]{:S(2)}, u32[]{:S(2)}) collective-permute-start(bf16[2,1,4,8,2048]{4,3,2,1,0:T(8,128)(2,1)S(1)} %get-tuple-element.174), channel_id=1, source_target_pairs={{2,0},{4,2},{6,4},{0,6},{3,1},{5,3},{7,5},{1,7},{10,8},{12,10},{14... | collective-permute-start | bytes 786440 | tf_op jit(solution)/shard_map/ppermute | solution.py:843
  27.6 15.4 %copy-start.4 = (f32[4,128]{1,0:T(4,128)S(1)}, f32[4,128]{1,0:T(4,128)}, u32[]{:S(2)}) copy-start(f32[4,128]{1,0:T(4,128)} %nw_ref.1) | copy-start | bytes 6148
  27.6 7.3 %collective-permute-start.8 = (bf16[1,4,4,8,1280]{4,3,2,1,0:T(8,128)(2,1)S(1)}, bf16[1,4,4,8,1280]{4,3,2,1,0:T(8,128)(2,1)S(1)}, u32[]{:S(2)}, u32[]{:S(2)}) collective-permute-start(bf16[1,4,4,8,1280]{4,3,2,1,0:T(8,128)(2,1)S(1)} %get-tuple-element.168), channel_id=1, source_target_pairs={{8,0},{16,8},{24,16},{0,24},{9,1},{17,9},{25,17},{1,25},{10,2},{18... | collective-permute-start | bytes 983048 | tf_op jit(solution)/shard_map/ppermute | solution.py:843
  27.7 10.1 %collective-permute-start.7 = (bf16[1,4,4,8,1280]{4,3,2,1,0:T(8,128)(2,1)S(1)}, bf16[1,4,4,8,1280]{4,3,2,1,0:T(8,128)(2,1)S(1)}, u32[]{:S(2)}, u32[]{:S(2)}) collective-permute-start(bf16[1,4,4,8,1280]{4,3,2,1,0:T(8,128)(2,1)S(1)} %get-tuple-element.169), channel_id=1, source_target_pairs={{0,8},{8,16},{16,24},{24,0},{1,9},{9,17},{17,25},{25,1},{2,10},{10... | collective-permute-start | bytes 983048 | tf_op jit(solution)/shard_map/ppermute | solution.py:842
  28.2 22.1 %collective-permute-start.10 = (bf16[1,2,4,8,2048]{4,3,2,1,0:T(8,128)(2,1)S(1)}, bf16[1,2,4,8,2048]{4,3,2,1,0:T(8,128)(2,1)S(1)}, u32[]{:S(2)}, u32[]{:S(2)}) collective-permute-start(bf16[1,2,4,8,2048]{4,3,2,1,0:T(8,128)(2,1)S(1)} %get-tuple-element.172), channel_id=1, source_target_pairs={{8,0},{16,8},{24,16},{0,24},{9,1},{17,9},{25,17},{1,25},{10,2},{18... | collective-permute-start | bytes 786440 | tf_op jit(solution)/shard_map/ppermute | solution.py:843
  34.9 15.3 %collective-permute-start.4 = (bf16[1,2,4,8,2048]{4,3,2,1,0:T(8,128)(2,1)S(1)}, bf16[1,2,4,8,2048]{4,3,2,1,0:T(8,128)(2,1)S(1)}, u32[]{:S(2)}, u32[]{:S(2)}) collective-permute-start(bf16[1,2,4,8,2048]{4,3,2,1,0:T(8,128)(2,1)S(1)} %get-tuple-element.173), channel_id=1, source_target_pairs={{0,8},{8,16},{16,24},{24,0},{1,9},{9,17},{17,25},{25,1},{2,10},{10... | collective-permute-start | bytes 786440 | tf_op jit(solution)/shard_map/ppermute | solution.py:842
  41.2 9.1 %collective-permute-start.9 = (bf16[1,2,4,8,2048]{4,3,2,1,0:T(8,128)(2,1)S(1)}, bf16[1,2,4,8,2048]{4,3,2,1,0:T(8,128)(2,1)S(1)}, u32[]{:S(2)}, u32[]{:S(2)}) collective-permute-start(bf16[1,2,4,8,2048]{4,3,2,1,0:T(8,128)(2,1)S(1)} %get-tuple-element.171), channel_id=1, source_target_pairs={{0,8},{8,16},{16,24},{24,0},{1,9},{9,17},{17,25},{25,1},{2,10},{10... | collective-permute-start | bytes 786440 | tf_op jit(solution)/shard_map/ppermute | solution.py:842
  41.3 9.0 %collective-permute-start.11 = (bf16[1,2,4,8,2048]{4,3,2,1,0:T(8,128)(2,1)S(1)}, bf16[1,2,4,8,2048]{4,3,2,1,0:T(8,128)(2,1)S(1)}, u32[]{:S(2)}, u32[]{:S(2)}) collective-permute-start(bf16[1,2,4,8,2048]{4,3,2,1,0:T(8,128)(2,1)S(1)} %get-tuple-element.170), channel_id=1, source_target_pairs={{8,0},{16,8},{24,16},{0,24},{9,1},{17,9},{25,17},{1,25},{10,2},{18... | collective-permute-start | bytes 786440 | tf_op jit(solution)/shard_map/ppermute | solution.py:843
  58.0 4.0 %collective-permute-start.12 = (f32[8,128]{1,0:T(8,128)S(1)}, f32[8,128]{1,0:T(8,128)S(1)}, u32[]{:S(2)}, u32[]{:S(2)}) collective-permute-start(f32[8,128]{1,0:T(8,128)S(1)} %get-tuple-element.137), channel_id=1, source_target_pairs={{0,8},{8,16},{16,24},{24,0},{1,9},{9,17},{17,25},{25,1},{2,10},{10... | collective-permute-start | bytes 12296 | tf_op jit(solution)/shard_map/ppermute | solution.py:893
  58.1 3.9 %collective-permute-start.13 = (f32[8,128]{1,0:T(8,128)S(1)}, f32[8,128]{1,0:T(8,128)S(1)}, u32[]{:S(2)}, u32[]{:S(2)}) collective-permute-start(f32[8,128]{1,0:T(8,128)S(1)} %get-tuple-element.138), channel_id=1, source_target_pairs={{8,0},{16,8},{24,16},{0,24},{9,1},{17,9},{25,17},{1,25},{10,2},{18... | collective-permute-start | bytes 12296 | tf_op jit(solution)/shard_map/ppermute | solution.py:894
  62.0 5.5 %collective-permute-start.14 = (f32[8,256]{1,0:T(8,128)S(1)}, f32[8,256]{1,0:T(8,128)S(1)}, u32[]{:S(2)}, u32[]{:S(2)}) collective-permute-start(f32[8,256]{1,0:T(8,128)S(1)} %add.3.mid_ref), channel_id=1, source_target_pairs={{0,2},{2,4},{4,6},{6,0},{1,3},{3,5},{5,7},{7,1},{8,10},{10,12},{12... | collective-permute-start | bytes 24584 | tf_op jit(solution)/shard_map/ppermute | solution.py:900
  62.7 4.9 %collective-permute-start.15 = (f32[8,256]{1,0:T(8,128)S(1)}, f32[8,256]{1,0:T(8,128)S(1)}, u32[]{:S(2)}, u32[]{:S(2)}) collective-permute-start(f32[8,256]{1,0:T(8,128)S(1)} %add.3.mid_ref), channel_id=1, source_target_pairs={{2,0},{4,2},{6,4},{0,6},{3,1},{5,3},{7,5},{1,7},{10,8},{12,10},{14... | collective-permute-start | bytes 24584 | tf_op jit(solution)/shard_map/ppermute | solution.py:900
  67.6 3.7 %collective-permute-start.16 = (f32[8,256]{1,0:T(8,128)S(1)}, f32[8,256]{1,0:T(8,128)S(1)}, u32[]{:S(2)}, u32[]{:S(2)}) collective-permute-start(f32[8,256]{1,0:T(8,128)S(1)} %fold.1.mid_ref), channel_id=1, source_target_pairs={{0,1},{1,0},{2,3},{3,2},{4,5},{5,4},{6,7},{7,6},{8,9},{9,8},{10,11... | collective-permute-start | bytes 24584 | tf_op jit(solution)/shard_map/ppermute | solution.py:909

commit v10 on v9

--- a/solution.py
+++ b/solution.py
@@ -68,7 +68,7 @@
 
 def cells_kernel(
     feat_ref, pos_ref, lists_ref,
-    first_ref, own_pos_ref, meta_ref, pick_ref, rows_ref, pos_rows,
+    out_ref, own_pos_ref, meta_ref, rows_ref, pos_rows,
 ):
     rows_ref[...] = jnp.zeros_like(rows_ref)
     pos_rows[...] = jnp.zeros_like(pos_rows)
@@ -88,32 +88,20 @@
     pick = (meta[:, SLOTS + 1 : SLOTS + 2] == lane).astype(F32).astype(BF16)
     same = (iota((atoms, atoms), 0) == iota((atoms, atoms), 1)).astype(F32).astype(BF16)
     own_pos_ref[...] = mm_nt(same, pieces).astype(BF16)
-    first_ref[:, CH : 2 * CH] = mm_nt(pick, pieces).astype(BF16)
-    pick_ref[...] = pick
-    first_ref[:, 0:CH] = mm(pick, feat_ref[:, 0:CH]).astype(BF16)
-    cut = pair_cols(GROUPS[1][0]).start
-    first_ref[:, 2 * CH :] = mm(pick, feat_ref[:, CH:cut]).astype(BF16)
-
-
-def rest_kernel(feat_ref, pick_ref, rest_ref):
-    cut = pair_cols(GROUPS[1][0]).start
-    rest_ref[...] = mm(pick_ref[...], feat_ref[:, cut:]).astype(BF16)
+    out_ref[:, CH : 2 * CH] = mm_nt(pick, pieces).astype(BF16)
+    out_ref[:, 0:CH] = mm(pick, feat_ref[:, 0:CH]).astype(BF16)
+    out_ref[:, 2 * CH :] = mm(pick, feat_ref[:, CH:]).astype(BF16)
 
 
 def make_cells(feats, places, lists):
-    atoms = feats.shape[0]
+    atoms, feat = feats.shape
     out_shape = (
-        struct(atoms, 2 * CH + GROUP_COLS[0], dtype=BF16),
+        struct(atoms, feat + CH, dtype=BF16),
         struct(atoms, CH, dtype=BF16),
         struct(atoms, CH),
-        struct(atoms, atoms, dtype=BF16),
-    )
-    args = (feats, places, lists)
+    )
     scratch = [pltpu.VMEM((CH, atoms), F32), pltpu.VMEM((CH, atoms), F32)]
-    first, own_pos, meta, pick = call(cells_kernel, "cells", out_shape, scratch, args)
-    out_shape = (struct(atoms, sum(GROUP_COLS[1:]), dtype=BF16),)
-    rest = call(rest_kernel, "cells_rest", out_shape, [], (feats, pick))[0]
-    return first, rest, own_pos, meta
+    return call(cells_kernel, "cells", out_shape, scratch, (feats, places, lists))
 
 
 def spacing_of(atoms, nbasis):
@@ -147,14 +135,12 @@
     return dist * (1.0 / spacing) - iota((dist.shape[0], nbasis), 1).astype(F32)
 
 
-def radial_net(dist, spacing, nets_ref):
-    nbasis = nets_ref.shape[0] - 5 * CH
-    centred = centred_of(dist, spacing, nbasis)
+def radial_net(dist, spacing, rbf_ref, rad_ref):
+    centred = centred_of(dist, spacing, rbf_ref.shape[0])
     basis = jnp.exp(-0.5 * centred * centred)
-    pre = mm(basis.astype(BF16), nets_ref[0:nbasis, :])
+    pre = mm(basis.astype(BF16), rbf_ref[...])
     hidden = (pre * jax.nn.sigmoid(pre)).astype(BF16)
-    weight = [nets_ref[nbasis + d * CH : nbasis + (d + 1) * CH, :] for d in range(5)]
-    return pre, mm(hidden, jnp.concatenate(weight, axis=1)).astype(BF16)
+    return pre, mm(hidden, rad_ref[...]).astype(BF16)
 
 
 def tiled(values, size=STEP):
@@ -366,7 +352,7 @@
 
 
 def own_kernel(
-    meta_ref, own_pos_ref, nets_ref,
+    meta_ref, own_pos_ref, rbf_ref, rad_ref,
     oh_own, pre_ref, unit_ref, radt_ref, rbft_ref, home_ref, *radial_refs
 ):
     atoms = meta_ref.shape[0]
@@ -378,16 +364,16 @@
         rows = own_rows(step)
         unit, dist = geometry(mm(oh_own[rows, :], own_pos_ref[...]), here)
         unit_ref[rows, :] = unit
-        pre, radial = radial_net(dist, spacing, nets_ref)
+        pre, radial = radial_net(dist, spacing, rbf_ref, rad_ref)
         pre_ref[rows, :] = pre.astype(BF16)
         for degree, ref in enumerate(radial_refs):
             ref[rows, :] = radial[:, degree * CH : (degree + 1) * CH]
     for degree in range(5):
         part = slice(degree * CH, (degree + 1) * CH)
-        radt_ref[part, :] = flip(nets_ref[nbasis + part.start : nbasis + part.stop, :])
+        radt_ref[part, :] = flip(rad_ref[:, part])
     for index in range(nbasis // CH):
         part = slice(index * CH, (index + 1) * CH)
-        rbft_ref[:, part] = flip(nets_ref[part, :])
+        rbft_ref[:, part] = flip(rbf_ref[part, :])
     lanes = home_ref.shape[1]
     lane = iota((atoms, lanes), 1)
     ext_x, ext_y, ext_z = lane // 128, lane // 32 % 4, lane // 8 % 4
@@ -402,7 +388,7 @@
     home_ref[...] = mm(to_atom.T.astype(BF16), to_slot).astype(BF16)
 
 
-def own_stage(meta, own_pos, nets):
+def own_stage(meta, own_pos, rbf, rad):
     atoms = meta.shape[0]
     edges = atoms * HALF
     out_shape = (
@@ -410,10 +396,10 @@
         struct(edges, CH, dtype=BF16),
         struct(edges, CH),
         struct(5 * CH, CH, dtype=BF16),
-        struct(CH, nets.shape[0] - 5 * CH, dtype=BF16),
+        struct(CH, rbf.shape[0], dtype=BF16),
         struct(atoms, 256, dtype=BF16),
     ) + (struct(edges, CH, dtype=BF16),) * 5
-    return call(own_kernel, "own_edges", out_shape, [], (meta, own_pos, nets))
+    return call(own_kernel, "own_edges", out_shape, [], (meta, own_pos, rbf, rad))
 
 
 def scalar_forward(rows, near, radial, mix_ref, m0_ref, gate_ref, nf0_ref):
@@ -475,7 +461,8 @@
 
 
 def start_kernel(
-    p0, p1, p2, own_ref, own_pos_ref, meta_ref, nets_ref, mix_ref, out_ref, ew_ref, acc0_ref,
+    p0, p1, p2, own_ref, own_pos_ref, meta_ref, rbf_ref, rad_ref, mix_ref, out_ref, ew_ref,
+    acc0_ref,
     new_ref, oh_gh, d_gh, dt_gh, pre_ref, unit_ref, gs0_ref, en_ref, m0_gh, gate_gh, nf0_gh,
     radial_gh1, radial_gh2, radial_gh3, radial_gh4,
     table, sems, ghpos, acc_s,
@@ -484,7 +471,7 @@
     copies = fetch((p0, p1, p2), slice(0, 2 * CH), table, sems)
     atoms = own_ref.shape[0]
     ghosts = table.shape[0]
-    spacing = spacing_of(atoms, nets_ref.shape[0] - 5 * CH)
+    spacing = spacing_of(atoms, rbf_ref.shape[0])
     norm = 1.0 / math.sqrt(SLOTS)
 
     live = live_ghosts(meta_ref)
@@ -545,7 +532,7 @@
         oh_gh[here, :] = onehot
         unit, dist = geometry(mm(onehot, ghpos[...]), mm(source, own_pos_ref[...]))
         unit_ref[here, :] = unit
-        pre, radial = radial_net(dist, spacing, nets_ref)
+        pre, radial = radial_net(dist, spacing, rbf_ref, rad_ref)
         pre_ref[here, :] = pre.astype(BF16)
         for degree in range(1, 5):
             radial_gh[degree][here, :] = radial[:, degree * CH : (degree + 1) * CH]
@@ -926,43 +913,47 @@
     feats = features[0, 0, 0]
     places = jnp.swapaxes(positions[0, 0], 0, 1)
     lists = jnp.concatenate([neighbours[0, 0, 0].T, counts[0, 0], cell_atoms[0, 0]], axis=0)
-    cells0, cells1, own_pos, meta = make_cells(feats, places, lists)
+    cells, own_pos, meta = make_cells(feats, places, lists)
     hold = lax.optimization_barrier
-    block0, block1 = (part.reshape(2, 2, 2, 8, part.shape[1]) for part in (cells0, cells1))
-    block0 = grown(block0, "gz", 2)
-    block0, own_pos, meta = hold((block0, own_pos, meta))
-    nets = jnp.concatenate(
-        [rbf_weight] + [radial_weight[:, d * CH : (d + 1) * CH] for d in range(5)], axis=0
-    )
+    block = cells.reshape(2, 2, 2, 8, cells.shape[1])
+    cut = 2 * CH + GROUP_COLS[0]
+    z = neighbours_of(block, "gz", 2)
+    y1_in = neighbours_of(block[..., cut:], "gy", 1)
+    oh_own, pre_own, unit_own, radt, rbft, home, *radial_own = own_stage(
+        meta, own_pos, rbf_weight, radial_weight
+    )
+    (m0_own, gate_own, nf0_own, acc0), (own_a,) = own_forward_stage(
+        (0,), feats, mix_weight, oh_own, radial_own
+    )
+    z, y1_in, gate_own = hold((z, y1_in, gate_own))
+    block = jnp.concatenate([z[0], block, z[1]], axis=2)
+    block0, block1 = block[..., :cut], block[..., cut:]
     y0 = neighbours_of(block0, "gy", 1)
-    oh_own, pre_own, unit_own, radt, rbft, home, *radial_own = own_stage(
-        meta, own_pos, nets
-    )
-    block1 = grown(block1, "gz", 2)
-    y1 = neighbours_of(block1, "gy", 1)
-    y0, block1, oh_own = hold((y0, block1, oh_own))
+    x1_in = neighbours_of(block1, "gx", 0)
+    _, (own_b,) = own_forward_stage((1,), feats, mix_weight, oh_own, radial_own, gate_own)
+    y0, x1_in, z1, acc_b = hold((y0, x1_in, [part[..., cut:] for part in z], own_b[2]))
     middle = jnp.concatenate([y0[0], block0, y0[1]], axis=1)
     low, high = neighbours_of(middle, "gx", 0)
+    y1_out = neighbours_of(jnp.concatenate(z1, axis=2), "gy", 1)
+    low, high, y1_out = hold((low, high, y1_out))
+    y1 = [
+        jnp.concatenate([out[:, :, 0:1], inner, out[:, :, 1:2]], axis=2)
+        for out, inner in zip(y1_out, y1_in)
+    ]
     pieces0 = tuple(flat_rows(piece) for piece in (low, middle, high))
-    x1_in = neighbours_of(block1, "gx", 0)
-    (m0_own, gate_own, nf0_own, acc0), (own_a,) = own_forward_stage(
-        (0,), feats, mix_weight, oh_own, radial_own
-    )
+    pieces1 = ghost_pieces(y1, block1, x1_in)
     (
         new_0, oh_gh, d_gh, dt_gh, pre_gh, unit_gh, gs0, en_0, m0_gh, gate_gh, nf0_gh, *radial_gh,
     ) = start_stage(
-        pieces0, feats, own_pos, meta, nets, mix_weight, out_weight, energy_weight[None], acc0,
-    )
-    y1, gate_gh = hold((y1, gate_gh))
-    pieces1 = ghost_pieces(y1, block1, x1_in)
+        pieces0, feats, own_pos, meta, rbf_weight, radial_weight, mix_weight, out_weight,
+        energy_weight[None], acc0,
+    )
     shared = (feats, meta, mix_weight, out_weight, norm_weight, oh_gh, d_gh, dt_gh, gate_gh)
     new_a, en_a, _, (dot_gh_a, *gr_gh_a), (dot_own_a, *gr_own_a) = pairs_stage(
         0, 2 * CH, pieces0, shared, (gate_own, *own_a), radial_gh
     )
-    en_a, gate_own = hold((en_a, gate_own))
-    _, (own_b,) = own_forward_stage((1,), feats, mix_weight, oh_own, radial_own, gate_own)
     new, energy, src, onto, low, mid, high, gs_b = third_stage(
-        pieces1, *shared, own_b[2], radt, rbft, gs0, en_0, en_a, new_0, new_a, pre_gh,
+        pieces1, *shared, acc_b, radt, rbft, gs0, en_0, en_a, new_0, new_a, pre_gh,
         unit_gh, m0_gh, nf0_gh, dot_gh_a, *gr_gh_a,
         *[radial_gh[degree - 1] for degree in DEGREES[1]],
     )

time: 72.6 us -> 72.8 us (level)
  waiting for transfers between devices: 9.45 us -> 12.4 us
  starting transfers between devices: 24.7 us -> 23.2 us
  local copies, waits for them, and re-layouts: 6.82 us -> 5.77 us
    ppermute x5 -> x6, waiting for transfers between devices: 0.17 us -> 6.4 us  [neighbours_of(): lax.ppermute(lax.slice_in_dim(block, length - 1, length, axis=dim), axis,...]
    ppermute x5 -> x6, waiting for transfers between devices: 8.54 us -> 4.26 us  [neighbours_of(): after = lax.ppermute(lax.slice_in_dim(block, 0, 1, axis=dim), axis, down)]
    ppermute x5 -> x6, starting transfers between devices: 5.36 us -> 2.31 us  [neighbours_of(): lax.ppermute(lax.slice_in_dim(block, length - 1, length, axis=dim), axis,...]
    ppermute x5 -> x6, starting transfers between devices: 9.04 us -> 11.7 us  [neighbours_of(): after = lax.ppermute(lax.slice_in_dim(block, 0, 1, axis=dim), axis, down)]
    ppermute x1, starting transfers between devices: 1.5 us -> 0.53 us  [give_back_z(): from_low = lax.ppermute(mid, 'gz', up)]
    ppermute x1, waiting for transfers between devices: 0.63 us -> 1.6 us  [give_back_z(): from_low = lax.ppermute(mid, 'gz', up)]
    concatenate x3 -> x1, local copies, waits for them, and re-layouts: 0.86 us -> 0.01 us  [local(): y1_out = neighbours_of(jnp.concatenate(z1, axis=2), 'gy', 1)]
    unnamed x22 -> x29, local copies, waits for them, and re-layouts: 5.74 us -> 5.47 us
  transfers between devices with their start and end apart: 17 -> 18, of which waited for: 5 -> 6; matrix products, arithmetic and copies ran while one was open for 7% -> 0% of each run, Pallas kernels for 28% -> 28%
where the time goes in v10:
time: 72.8 us; the launch traced here: 72.5 us
  Pallas kernels  29 us (40%)
  starting transfers between devices  23.2 us (32%)
  waiting for transfers between devices  12.4 us (17%)
  local copies, waits for them, and re-layouts  5.77 us (8%)
  other arithmetic  1.12 us (2%)
  between operations  1.06 us (1%)
    pallas_call x12, Pallas kernels, call(): pl.pallas_call(kernel, out_shape=out_shape, in_specs=specs or [pl.BlockSp...  29 us
    ppermute x6, starting transfers between devices, neighbours_of(): after = lax.ppermute(lax.slice_in_dim(block, 0, 1, axis=dim), axis, down)  11.7 us
    ppermute x6, waiting for transfers between devices, neighbours_of(): lax.ppermute(lax.slice_in_dim(block, length - 1, length, axis=dim), axis,...  6.4 us
    unnamed x29, local copies, waits for them, and re-layouts  5.47 us
    ppermute x6, waiting for transfers between devices, neighbours_of(): after = lax.ppermute(lax.slice_in_dim(block, 0, 1, axis=dim), axis, down)  4.26 us
    ppermute x2, starting transfers between devices, give_back_y(): return (mid, lax.ppermute(mid, 'gy', up), lax.ppermute(mid, 'gy', down))  3.87 us
    ppermute x1, starting transfers between devices, neighbours_of(): other = lax.ppermute(block, axis, up)  3.03 us
    ppermute x6, starting transfers between devices, neighbours_of(): lax.ppermute(lax.slice_in_dim(block, length - 1, length, axis=dim), axis,...  2.31 us
  transfers between devices with their start and end apart: 18, of which 6 were waited for; matrix products, arithmetic and copies ran while one was open for 0% of the time, Pallas kernels for 28%

profile of v10, /device:TPU:0, one launch (start us, length us, event | category | flops | bytes accessed | tf_op | source)
XLA Modules:
  0.0 72.5 jit_solution(16021785174466052013)
XLA Ops:
  1.4 1.0 %copy-done = bf16[1,1,1,64,3200]{4,3,2,1,0:T(8,128)(2,1)S(1)} copy-done((bf16[1,1,1,64,3200]{4,3,2,1,0:T(8,128)(2,1)S(1)}, bf16[1,1,1,64,3200]{4,3,2,1,0:T(8,128)(2,1)}, u32[]{:S(2)}) %copy-start) | copy-done | bytes 409624
  3.5 3.0 %collective-permute-start = (bf16[2,2,2,8,3328]{4,3,2,1,0:T(8,128)(2,1)S(1)}, bf16[2,2,2,8,3328]{4,3,2,1,0:T(8,128)(2,1)S(1)}, u32[]{:S(2)}, u32[]{:S(2)}) collective-permute-start(bf16[2,2,2,8,3328]{4,3,2,1,0:T(8,128)(2,1)S(1)} %bitcast.35), channel_id=1, source_target_pairs={{0,1},{1,0},{2,3},{3,2},{4,5},{5,4},{6,7},{7,6},{8,9},{9,8},{10,11... | collective-permute-start | bytes 1277960 | tf_op jit(solution)/shard_map/ppermute | solution.py:824
  6.5 1.6 %collective-permute-start.1 = (bf16[2,1,2,8,2048]{4,3,2,1,0:T(8,128)(2,1)S(1)}, bf16[2,1,2,8,2048]{4,3,2,1,0:T(8,128)(2,1)S(1)}, u32[]{:S(2)}, u32[]{:S(2)}) collective-permute-start(bf16[2,1,2,8,2048]{4,3,2,1,0:T(8,128)(2,1)S(1)} %get-tuple-element.183), channel_id=1, source_target_pairs={{0,2},{2,4},{4,6},{6,0},{1,3},{3,5},{5,7},{7,1},{8,10},{10,12},{12... | collective-permute-start | bytes 393224 | tf_op jit(solution)/shard_map/ppermute | solution.py:829
  8.2 2.2 %collective-permute-start.2 = (bf16[2,1,2,8,2048]{4,3,2,1,0:T(8,128)(2,1)S(1)}, bf16[2,1,2,8,2048]{4,3,2,1,0:T(8,128)(2,1)S(1)}, u32[]{:S(2)}, u32[]{:S(2)}) collective-permute-start(bf16[2,1,2,8,2048]{4,3,2,1,0:T(8,128)(2,1)S(1)} %get-tuple-element.182), channel_id=1, source_target_pairs={{2,0},{4,2},{6,4},{0,6},{3,1},{5,3},{7,5},{1,7},{10,8},{12,10},{14... | collective-permute-start | bytes 393224 | tf_op jit(solution)/shard_map/ppermute | solution.py:830
  12.2 2.9 %own_edges.1 = (bf16[1024,64]{1,0:T(8,128)(2,1)S(1)}, bf16[1024,128]{1,0:T(8,128)(2,1)S(1)}, f32[1024,128]{1,0:T(8,128)S(1)}, bf16[640,128]{1,0:T(8,128)(2,1)S(1...) custom-call(f32[64,128]{1,0:T(8,128)S(1)} %get-tuple-element.88.meta, ...), custom_call_target="tpu_custom_call" | custom-call | flops 1024 | bytes 1024 | tf_op jit(solution)/shard_map/own_edges/pallas_call | solution.py:57
  15.1 1.0 %copy-done.1 = bf16[1,1,1,64,3200]{4,3,2,1,0:T(8,128)(2,1)S(1)} copy-done((bf16[1,1,1,64,3200]{4,3,2,1,0:T(8,128)(2,1)S(1)}, bf16[1,1,1,64,3200]{4,3,2,1,0:T(8,128)(2,1)}, u32[]{:S(2)}) %copy-start.1) | copy-done | bytes 409624
  17.0 1.5 %own_forward_a.1 = (bf16[1024,128]{1,0:T(8,128)(2,1)S(1)}, bf16[1024,128]{1,0:T(8,128)(2,1)S(1)}, bf16[1024,128]{1,0:T(8,128)(2,1)S(1)}, f32[64,128]{1,0:T(8,128...) custom-call(bf16[64,3200]{1,0:T(8,128)(2,1)S(1)} %bitcast.23, ...), custom_call_target="tpu_custom_call" | custom-call | flops 1024 | bytes 1024 | tf_op jit(solution)/shard_map/own_forward_a/pallas_call | solution.py:57
  18.8 1.7 %collective-permute-start.6 = (bf16[1,2,4,8,2048]{4,3,2,1,0:T(8,128)(2,1)S(1)}, bf16[1,2,4,8,2048]{4,3,2,1,0:T(8,128)(2,1)S(1)}, u32[]{:S(2)}, u32[]{:S(2)}) collective-permute-start(bf16[1,2,4,8,2048]{4,3,2,1,0:T(8,128)(2,1)S(1)} %get-tuple-element.174), channel_id=1, source_target_pairs={{8,0},{16,8},{24,16},{0,24},{9,1},{17,9},{25,17},{1,25},{10,2},{18... | collective-permute-start | bytes 786440 | tf_op jit(solution)/shard_map/ppermute | solution.py:830
  20.7 3.8 %collective-permute-start.4 = (bf16[2,1,4,8,1280]{4,3,2,1,0:T(8,128)(2,1)S(1)}, bf16[2,1,4,8,1280]{4,3,2,1,0:T(8,128)(2,1)S(1)}, u32[]{:S(2)}, u32[]{:S(2)}) collective-permute-start(bf16[2,1,4,8,1280]{4,3,2,1,0:T(8,128)(2,1)S(1)} %get-tuple-element.176), channel_id=1, source_target_pairs={{2,0},{4,2},{6,4},{0,6},{3,1},{5,3},{7,5},{1,7},{10,8},{12,10},{14... | collective-permute-start | bytes 491528 | tf_op jit(solution)/shard_map/ppermute | solution.py:830
  24.5 2.4 %own_forward_b.1 = (bf16[1024,2048]{1,0:T(8,128)(2,1)S(1)}, bf16[1024,2048]{1,0:T(8,128)(2,1)S(1)}, f32[64,2048]{1,0:T(8,128)S(1)}) custom-call(bf16[64,3200]{1,0:T(8,128)(2,1)S(1)} %bitcast.24, bf16[5,128,128]{2,1,0:T(8,128)(2,1)S(1)} %copy-done.3, bf16[1024,64]{1,0:T(8,128)(2,1)S(1)} %get-tuple-element.90.refs_2_.oh_own, ...), custom_call_target="tpu_custom_call" | custom-call | flops 1024 | bytes 1024 | tf_op jit(solution)/shard_map/own_forward_b/pallas_call | solution.py:57
  27.1 2.5 %collective-permute-done.3 = bf16[2,1,4,8,1280]{4,3,2,1,0:T(8,128)(2,1)S(1)} collective-permute-done((bf16[2,1,4,8,1280]{4,3,2,1,0:T(8,128)(2,1)S(1)}, bf16[2,1,4,8,1280]{4,3,2,1,0:T(8,128)(2,1)S(1)}, u32[]{:S(2)}, u32[]{:S(2)}) %collective-permute-start.3) | collective-permute-done | bytes 163872 | tf_op jit(solution)/shard_map/ppermute | solution.py:829
  30.4 1.7 %collective-permute-start.8 = (bf16[1,4,4,8,1280]{4,3,2,1,0:T(8,128)(2,1)S(1)}, bf16[1,4,4,8,1280]{4,3,2,1,0:T(8,128)(2,1)S(1)}, u32[]{:S(2)}, u32[]{:S(2)}) collective-permute-start(bf16[1,4,4,8,1280]{4,3,2,1,0:T(8,128)(2,1)S(1)} %get-tuple-element.178), channel_id=1, source_target_pairs={{8,0},{16,8},{24,16},{0,24},{9,1},{17,9},{25,17},{1,25},{10,2},{18... | collective-permute-start | bytes 983048 | tf_op jit(solution)/shard_map/ppermute | solution.py:830
  32.2 2.1 %collective-permute-start.10 = (bf16[2,1,2,8,2048]{4,3,2,1,0:T(8,128)(2,1)S(1)}, bf16[2,1,2,8,2048]{4,3,2,1,0:T(8,128)(2,1)S(1)}, u32[]{:S(2)}, u32[]{:S(2)}) collective-permute-start(bf16[2,1,2,8,2048]{4,3,2,1,0:T(8,128)(2,1)S(1)} %get-tuple-element.186), channel_id=1, source_target_pairs={{2,0},{4,2},{6,4},{0,6},{3,1},{5,3},{7,5},{1,7},{10,8},{12,10},{14... | collective-permute-start | bytes 393224 | tf_op jit(solution)/shard_map/ppermute | solution.py:830
  34.3 3.6 %collective-permute-done.10 = bf16[2,1,2,8,2048]{4,3,2,1,0:T(8,128)(2,1)S(1)} collective-permute-done((bf16[2,1,2,8,2048]{4,3,2,1,0:T(8,128)(2,1)S(1)}, bf16[2,1,2,8,2048]{4,3,2,1,0:T(8,128)(2,1)S(1)}, u32[]{:S(2)}, u32[]{:S(2)}) %collective-permute-start.10) | collective-permute-done | bytes 131104 | tf_op jit(solution)/shard_map/ppermute | solution.py:830
  37.9 3.9 %collective-permute-done.9 = bf16[2,1,2,8,2048]{4,3,2,1,0:T(8,128)(2,1)S(1)} collective-permute-done((bf16[2,1,2,8,2048]{4,3,2,1,0:T(8,128)(2,1)S(1)}, bf16[2,1,2,8,2048]{4,3,2,1,0:T(8,128)(2,1)S(1)}, u32[]{:S(2)}, u32[]{:S(2)}) %collective-permute-start.9) | collective-permute-done | bytes 131104 | tf_op jit(solution)/shard_map/ppermute | solution.py:829
  42.6 3.6 %ghost_start.1 = (bf16[64,128]{1,0:T(8,128)(2,1)S(1)}, bf16[1024,512]{1,0:T(8,128)(2,1)S(1)}, bf16[1024,64]{1,0:T(8,128)(2,1)S(1)}, bf16[64,1024]{1,0:T(8,128)(2...) custom-call(bf16[128,1280]{1,0:T(8,128)(2,1)S(1)} %bitcast.31, ...), custom_call_target="tpu_custom_call" | custom-call | flops 1024 | bytes 1024 | tf_op jit(solution)/shard_map/ghost_start/pallas_call | solution.py:57
  46.2 4.4 %pairs_a.1 = (bf16[64,1024]{1,0:T(8,128)(2,1)S(1)}, f32[64,128]{1,0:T(8,128)S(1)}, bf16[64,1024]{1,0:T(8,128)(2,1)}, bf16[1024,128]{1,0:T(8,128)(2,1)S(1)}, bf16...) custom-call(bf16[128,1280]{1,0:T(8,128)(2,1)S(1)} %bitcast.32, ...), custom_call_target="tpu_custom_call" | custom-call | flops 1024 | bytes 1024 | tf_op jit(solution)/shard_map/pairs_a/pallas_call | solution.py:57
  50.7 7.7 %third_group.1 = (bf16[64,3200]{1,0:T(8,128)(2,1)}, f32[1,64]{1,0:T(1,128)}, f32[64,128]{1,0:T(8,128)S(1)}, f32[8,64]{1,0:T(8,128)S(1)}, f32[8,128]{1,0:T(8,128)...) custom-call(bf16[64,2048]{1,0:T(8,128)(2,1)S(1)} %bitcast.38, ...), custom_call_target="tpu_custom_call" | custom-call | flops 1024 | bytes 1024 | tf_op jit(solution)/shard_map/third_group/pallas_call | solution.py:57
  59.0 1.2 %collective-permute-start.14 = (f32[8,128]{1,0:T(8,128)S(1)}, f32[8,128]{1,0:T(8,128)S(1)}, u32[]{:S(2)}, u32[]{:S(2)}) collective-permute-start(f32[8,128]{1,0:T(8,128)S(1)} %get-tuple-element.144), channel_id=1, source_target_pairs={{8,0},{16,8},{24,16},{0,24},{9,1},{17,9},{25,17},{1,25},{10,2},{18... | collective-permute-start | bytes 12296 | tf_op jit(solution)/shard_map/ppermute | solution.py:881
  60.2 2.2 %own_backward_b.1 = (bf16[1024,128]{1,0:T(8,128)(2,1)S(1)}, bf16[1024,128]{1,0:T(8,128)(2,1)S(1)}, bf16[1024,128]{1,0:T(8,128)(2,1)S(1)}) custom-call(bf16[5,128,128]{2,1,0:T(8,128)(2,1)S(1)} %copy-done.4, bf16[64,2048]{1,0:T(8,128)(2,1)S(1)} %get-tuple-element.145.gs_ref, bf16[1024,128]{1,0:T(8,128)(2,1)S(1)} %get-tuple-element.99.refs_8_.refs_12_.gate_ref, ...), custom_call_target="tpu_custom_call" | custom-call | flops 1024 | bytes 1024 | tf_op jit(solution)/shard_map/own_backward_b/pallas_call | solution.py:57
  62.5 3.8 %collective-permute-start.16 = (f32[8,256]{1,0:T(8,128)S(1)}, f32[8,256]{1,0:T(8,128)S(1)}, u32[]{:S(2)}, u32[]{:S(2)}) collective-permute-start(f32[8,256]{1,0:T(8,128)S(1)} %add.3.mid_ref), channel_id=1, source_target_pairs={{2,0},{4,2},{6,4},{0,6},{3,1},{5,3},{7,5},{1,7},{10,8},{12,10},{14... | collective-permute-start | bytes 24584 | tf_op jit(solution)/shard_map/ppermute | solution.py:887
  66.3 1.5 %own_back.2 = (f32[64,128]{1,0:T(8,128)S(1)}, f32[8,64]{1,0:T(8,128)S(1)}) custom-call(bf16[1024,64]{1,0:T(8,128)(2,1)S(1)} %get-tuple-element.90.refs_2_.oh_own, bf16[1024,128]{1,0:T(8,128)(2,1)S(1)} %get-tuple-element.150.pre_own, f32[1024,128]{1,0:T(8,128)S(1)} %get-tuple-element.151.unit_own, bf16[640,128]{1,0:T(8,128)(2,1)S(1)} %get-tuple-element.119.radt_ref, ...), custom_call_target="tpu_custom_call" | custom-call | flops 1024 | bytes 1024 | tf_op jit(solution)/shard_map/own_back/pallas_call | solution.py:57
  68.6 1.5 %own_back.3 = (f32[64,128]{1,0:T(8,128)S(1)}, f32[8,64]{1,0:T(8,128)S(1)}) custom-call(bf16[1024,64]{1,0:T(8,128)(2,1)S(1)} %get-tuple-element.90.refs_2_.oh_own, bf16[1024,128]{1,0:T(8,128)(2,1)S(1)} %get-tuple-element.150.pre_own, f32[1024,128]{1,0:T(8,128)S(1)} %get-tuple-element.151.unit_own, bf16[640,128]{1,0:T(8,128)(2,1)S(1)} %get-tuple-element.119.radt_ref, ...), custom_call_target="tpu_custom_call" | custom-call | flops 1024 | bytes 1024 | tf_op jit(solution)/shard_map/own_back/pallas_call | solution.py:57
  70.1 1.6 %collective-permute-done.17.low_ref.high_ref = f32[8,256]{1,0:T(8,128)S(1)} collective-permute-done((f32[8,256]{1,0:T(8,128)S(1)}, f32[8,256]{1,0:T(8,128)S(1)}, u32[]{:S(2)}, u32[]{:S(2)}) %collective-permute-start.17) | collective-permute-done | bytes 8224 | tf_op jit(solution)/shard_map/ppermute | solution.py:896
  (74 shorter events, 8.8 us)
Async XLA Ops:
  3.5 15.1 %collective-permute-start = (bf16[2,2,2,8,3328]{4,3,2,1,0:T(8,128)(2,1)S(1)}, bf16[2,2,2,8,3328]{4,3,2,1,0:T(8,128)(2,1)S(1)}, u32[]{:S(2)}, u32[]{:S(2)}) collective-permute-start(bf16[2,2,2,8,3328]{4,3,2,1,0:T(8,128)(2,1)S(1)} %bitcast.35), channel_id=1, source_target_pairs={{0,1},{1,0},{2,3},{3,2},{4,5},{5,4},{6,7},{7,6},{8,9},{9,8},{10,11... | collective-permute-start | bytes 1277960 | tf_op jit(solution)/shard_map/ppermute | solution.py:824
  6.5 12.1 %collective-permute-start.1 = (bf16[2,1,2,8,2048]{4,3,2,1,0:T(8,128)(2,1)S(1)}, bf16[2,1,2,8,2048]{4,3,2,1,0:T(8,128)(2,1)S(1)}, u32[]{:S(2)}, u32[]{:S(2)}) collective-permute-start(bf16[2,1,2,8,2048]{4,3,2,1,0:T(8,128)(2,1)S(1)} %get-tuple-element.183), channel_id=1, source_target_pairs={{0,2},{2,4},{4,6},{6,0},{1,3},{3,5},{5,7},{7,1},{8,10},{10,12},{12... | collective-permute-start | bytes 393224 | tf_op jit(solution)/shard_map/ppermute | solution.py:829
  8.2 10.4 %collective-permute-start.2 = (bf16[2,1,2,8,2048]{4,3,2,1,0:T(8,128)(2,1)S(1)}, bf16[2,1,2,8,2048]{4,3,2,1,0:T(8,128)(2,1)S(1)}, u32[]{:S(2)}, u32[]{:S(2)}) collective-permute-start(bf16[2,1,2,8,2048]{4,3,2,1,0:T(8,128)(2,1)S(1)} %get-tuple-element.182), channel_id=1, source_target_pairs={{2,0},{4,2},{6,4},{0,6},{3,1},{5,3},{7,5},{1,7},{10,8},{12,10},{14... | collective-permute-start | bytes 393224 | tf_op jit(solution)/shard_map/ppermute | solution.py:830
  18.7 23.8 %copy-start.13 = (bf16[2,2,4,8,3328]{4,3,2,1,0:T(8,128)(2,1)}, bf16[2,2,4,8,3328]{4,3,2,1,0:T(8,128)(2,1)S(1)}, u32[]{:S(2)}) copy-start(bf16[2,2,4,8,3328]{4,3,2,1,0:T(8,128)(2,1)S(1)} %pad_maximum_fusion) | copy-start | bytes 2555908
  18.8 11.4 %collective-permute-start.5 = (bf16[1,2,4,8,2048]{4,3,2,1,0:T(8,128)(2,1)S(1)}, bf16[1,2,4,8,2048]{4,3,2,1,0:T(8,128)(2,1)S(1)}, u32[]{:S(2)}, u32[]{:S(2)}) collective-permute-start(bf16[1,2,4,8,2048]{4,3,2,1,0:T(8,128)(2,1)S(1)} %get-tuple-element.175), channel_id=1, source_target_pairs={{0,8},{8,16},{16,24},{24,0},{1,9},{9,17},{17,25},{25,1},{2,10},{10... | collective-permute-start | bytes 786440 | tf_op jit(solution)/shard_map/ppermute | solution.py:829
  18.8 11.4 %collective-permute-start.6 = (bf16[1,2,4,8,2048]{4,3,2,1,0:T(8,128)(2,1)S(1)}, bf16[1,2,4,8,2048]{4,3,2,1,0:T(8,128)(2,1)S(1)}, u32[]{:S(2)}, u32[]{:S(2)}) collective-permute-start(bf16[1,2,4,8,2048]{4,3,2,1,0:T(8,128)(2,1)S(1)} %get-tuple-element.174), channel_id=1, source_target_pairs={{8,0},{16,8},{24,16},{0,24},{9,1},{17,9},{25,17},{1,25},{10,2},{18... | collective-permute-start | bytes 786440 | tf_op jit(solution)/shard_map/ppermute | solution.py:830
  20.6 8.9 %collective-permute-start.3 = (bf16[2,1,4,8,1280]{4,3,2,1,0:T(8,128)(2,1)S(1)}, bf16[2,1,4,8,1280]{4,3,2,1,0:T(8,128)(2,1)S(1)}, u32[]{:S(2)}, u32[]{:S(2)}) collective-permute-start(bf16[2,1,4,8,1280]{4,3,2,1,0:T(8,128)(2,1)S(1)} %get-tuple-element.177), channel_id=1, source_target_pairs={{0,2},{2,4},{4,6},{6,0},{1,3},{3,5},{5,7},{7,1},{8,10},{10,12},{12... | collective-permute-start | bytes 491528 | tf_op jit(solution)/shard_map/ppermute | solution.py:829
  20.7 9.5 %collective-permute-start.4 = (bf16[2,1,4,8,1280]{4,3,2,1,0:T(8,128)(2,1)S(1)}, bf16[2,1,4,8,1280]{4,3,2,1,0:T(8,128)(2,1)S(1)}, u32[]{:S(2)}, u32[]{:S(2)}) collective-permute-start(bf16[2,1,4,8,1280]{4,3,2,1,0:T(8,128)(2,1)S(1)} %get-tuple-element.176), channel_id=1, source_target_pairs={{2,0},{4,2},{6,4},{0,6},{3,1},{5,3},{7,5},{1,7},{10,8},{12,10},{14... | collective-permute-start | bytes 491528 | tf_op jit(solution)/shard_map/ppermute | solution.py:830
  27.0 15.6 %copy-start.2 = (bf16[1,1,1,64,3200]{4,3,2,1,0:T(8,128)(2,1)S(1)}, bf16[1,1,1,64,3200]{4,3,2,1,0:T(8,128)(2,1)}, u32[]{:S(2)}) copy-start(bf16[1,1,1,64,3200]{4,3,2,1,0:T(8,128)(2,1)} %param.11) | copy-start | bytes 1228804
  27.0 15.6 %copy-start.4 = (bf16[5,128,128]{2,1,0:T(8,128)(2,1)S(1)}, bf16[5,128,128]{2,1,0:T(8,128)(2,1)}, u32[]{:S(2)}) copy-start(bf16[5,128,128]{2,1,0:T(8,128)(2,1)} %mix_ref.9) | copy-start | bytes 491524
  27.0 15.5 %copy-start.5 = (bf16[5,128,128]{2,1,0:T(8,128)(2,1)S(1)}, bf16[5,128,128]{2,1,0:T(8,128)(2,1)}, u32[]{:S(2)}) copy-start(bf16[5,128,128]{2,1,0:T(8,128)(2,1)} %out_ref.3) | copy-start | bytes 491524
  27.0 15.5 %copy-start.7 = (bf16[128,640]{1,0:T(8,128)(2,1)S(1)}, bf16[128,640]{1,0:T(8,128)(2,1)}, u32[]{:S(2)}) copy-start(bf16[128,640]{1,0:T(8,128)(2,1)} %rad_ref.3) | copy-start | bytes 491524
  30.3 15.8 %copy-start.10 = (f32[4,128]{1,0:T(4,128)S(1)}, f32[4,128]{1,0:T(4,128)}, u32[]{:S(2)}) copy-start(f32[4,128]{1,0:T(4,128)} %nw_ref.1) | copy-start | bytes 6148
  30.4 11.4 %collective-permute-start.7 = (bf16[1,4,4,8,1280]{4,3,2,1,0:T(8,128)(2,1)S(1)}, bf16[1,4,4,8,1280]{4,3,2,1,0:T(8,128)(2,1)S(1)}, u32[]{:S(2)}, u32[]{:S(2)}) collective-permute-start(bf16[1,4,4,8,1280]{4,3,2,1,0:T(8,128)(2,1)S(1)} %get-tuple-element.179), channel_id=1, source_target_pairs={{0,8},{8,16},{16,24},{24,0},{1,9},{9,17},{17,25},{25,1},{2,10},{10... | collective-permute-start | bytes 983048 | tf_op jit(solution)/shard_map/ppermute | solution.py:829
  30.4 11.4 %collective-permute-start.8 = (bf16[1,4,4,8,1280]{4,3,2,1,0:T(8,128)(2,1)S(1)}, bf16[1,4,4,8,1280]{4,3,2,1,0:T(8,128)(2,1)S(1)}, u32[]{:S(2)}, u32[]{:S(2)}) collective-permute-start(bf16[1,4,4,8,1280]{4,3,2,1,0:T(8,128)(2,1)S(1)} %get-tuple-element.178), channel_id=1, source_target_pairs={{8,0},{16,8},{24,16},{0,24},{9,1},{17,9},{25,17},{1,25},{10,2},{18... | collective-permute-start | bytes 983048 | tf_op jit(solution)/shard_map/ppermute | solution.py:830
  32.2 5.7 %collective-permute-start.10 = (bf16[2,1,2,8,2048]{4,3,2,1,0:T(8,128)(2,1)S(1)}, bf16[2,1,2,8,2048]{4,3,2,1,0:T(8,128)(2,1)S(1)}, u32[]{:S(2)}, u32[]{:S(2)}) collective-permute-start(bf16[2,1,2,8,2048]{4,3,2,1,0:T(8,128)(2,1)S(1)} %get-tuple-element.186), channel_id=1, source_target_pairs={{2,0},{4,2},{6,4},{0,6},{3,1},{5,3},{7,5},{1,7},{10,8},{12,10},{14... | collective-permute-start | bytes 393224 | tf_op jit(solution)/shard_map/ppermute | solution.py:830
  34.3 7.5 %collective-permute-start.9 = (bf16[2,1,2,8,2048]{4,3,2,1,0:T(8,128)(2,1)S(1)}, bf16[2,1,2,8,2048]{4,3,2,1,0:T(8,128)(2,1)S(1)}, u32[]{:S(2)}, u32[]{:S(2)}) collective-permute-start(bf16[2,1,2,8,2048]{4,3,2,1,0:T(8,128)(2,1)S(1)} %get-tuple-element.187), channel_id=1, source_target_pairs={{0,2},{2,4},{4,6},{6,0},{1,3},{3,5},{5,7},{7,1},{8,10},{10,12},{12... | collective-permute-start | bytes 393224 | tf_op jit(solution)/shard_map/ppermute | solution.py:829
  42.0 8.8 %collective-permute-start.12 = (bf16[1,2,4,8,2048]{4,3,2,1,0:T(8,128)(2,1)S(1)}, bf16[1,2,4,8,2048]{4,3,2,1,0:T(8,128)(2,1)S(1)}, u32[]{:S(2)}, u32[]{:S(2)}) collective-permute-start(bf16[1,2,4,8,2048]{4,3,2,1,0:T(8,128)(2,1)S(1)} %get-tuple-element.180), channel_id=1, source_target_pairs={{8,0},{16,8},{24,16},{0,24},{9,1},{17,9},{25,17},{1,25},{10,2},{18... | collective-permute-start | bytes 786440 | tf_op jit(solution)/shard_map/ppermute | solution.py:830
  42.0 8.7 %collective-permute-start.11 = (bf16[1,2,4,8,2048]{4,3,2,1,0:T(8,128)(2,1)S(1)}, bf16[1,2,4,8,2048]{4,3,2,1,0:T(8,128)(2,1)S(1)}, u32[]{:S(2)}, u32[]{:S(2)}) collective-permute-start(bf16[1,2,4,8,2048]{4,3,2,1,0:T(8,128)(2,1)S(1)} %get-tuple-element.181), channel_id=1, source_target_pairs={{0,8},{8,16},{16,24},{24,0},{1,9},{9,17},{17,25},{25,1},{2,10},{10... | collective-permute-start | bytes 786440 | tf_op jit(solution)/shard_map/ppermute | solution.py:829
  58.4 4.0 %collective-permute-start.13 = (f32[8,128]{1,0:T(8,128)S(1)}, f32[8,128]{1,0:T(8,128)S(1)}, u32[]{:S(2)}, u32[]{:S(2)}) collective-permute-start(f32[8,128]{1,0:T(8,128)S(1)} %get-tuple-element.143), channel_id=1, source_target_pairs={{0,8},{8,16},{16,24},{24,0},{1,9},{9,17},{17,25},{25,1},{2,10},{10... | collective-permute-start | bytes 12296 | tf_op jit(solution)/shard_map/ppermute | solution.py:880
  59.0 3.4 %collective-permute-start.14 = (f32[8,128]{1,0:T(8,128)S(1)}, f32[8,128]{1,0:T(8,128)S(1)}, u32[]{:S(2)}, u32[]{:S(2)}) collective-permute-start(f32[8,128]{1,0:T(8,128)S(1)} %get-tuple-element.144), channel_id=1, source_target_pairs={{8,0},{16,8},{24,16},{0,24},{9,1},{17,9},{25,17},{1,25},{10,2},{18... | collective-permute-start | bytes 12296 | tf_op jit(solution)/shard_map/ppermute | solution.py:881
  62.5 5.5 %collective-permute-start.15 = (f32[8,256]{1,0:T(8,128)S(1)}, f32[8,256]{1,0:T(8,128)S(1)}, u32[]{:S(2)}, u32[]{:S(2)}) collective-permute-start(f32[8,256]{1,0:T(8,128)S(1)} %add.3.mid_ref), channel_id=1, source_target_pairs={{0,2},{2,4},{4,6},{6,0},{1,3},{3,5},{5,7},{7,1},{8,10},{10,12},{12... | collective-permute-start | bytes 24584 | tf_op jit(solution)/shard_map/ppermute | solution.py:887
  62.5 5.4 %collective-permute-start.16 = (f32[8,256]{1,0:T(8,128)S(1)}, f32[8,256]{1,0:T(8,128)S(1)}, u32[]{:S(2)}, u32[]{:S(2)}) collective-permute-start(f32[8,256]{1,0:T(8,128)S(1)} %add.3.mid_ref), channel_id=1, source_target_pairs={{2,0},{4,2},{6,4},{0,6},{3,1},{5,3},{7,5},{1,7},{10,8},{12,10},{14... | collective-permute-start | bytes 24584 | tf_op jit(solution)/shard_map/ppermute | solution.py:887
  68.0 3.7 %collective-permute-start.17 = (f32[8,256]{1,0:T(8,128)S(1)}, f32[8,256]{1,0:T(8,128)S(1)}, u32[]{:S(2)}, u32[]{:S(2)}) collective-permute-start(f32[8,256]{1,0:T(8,128)S(1)} %fold.1.mid_ref), channel_id=1, source_target_pairs={{0,1},{1,0},{2,3},{3,2},{4,5},{5,4},{6,7},{7,6},{8,9},{9,8},{10,11... | collective-permute-start | bytes 24584 | tf_op jit(solution)/shard_map/ppermute | solution.py:896
  (9 other events, 40.9 us)

commit v11 on v10

--- a/solution.py
+++ b/solution.py
@@ -68,7 +68,7 @@
 
 def cells_kernel(
     feat_ref, pos_ref, lists_ref,
-    out_ref, own_pos_ref, meta_ref, rows_ref, pos_rows,
+    out_ref, own_pos_ref, meta_ref, pick_ref, rows_ref, pos_rows,
 ):
     rows_ref[...] = jnp.zeros_like(rows_ref)
     pos_rows[...] = jnp.zeros_like(pos_rows)
@@ -89,19 +89,31 @@
     same = (iota((atoms, atoms), 0) == iota((atoms, atoms), 1)).astype(F32).astype(BF16)
     own_pos_ref[...] = mm_nt(same, pieces).astype(BF16)
     out_ref[:, CH : 2 * CH] = mm_nt(pick, pieces).astype(BF16)
+    pick_ref[...] = pick
     out_ref[:, 0:CH] = mm(pick, feat_ref[:, 0:CH]).astype(BF16)
-    out_ref[:, 2 * CH :] = mm(pick, feat_ref[:, CH:]).astype(BF16)
+    cut = pair_cols(GROUPS[1][0]).start
+    out_ref[:, 2 * CH :] = mm(pick, feat_ref[:, CH:cut]).astype(BF16)
+
+
+def rest_kernel(feat_ref, pick_ref, rest_ref):
+    cut = pair_cols(GROUPS[1][0]).start
+    rest_ref[...] = mm(pick_ref[...], feat_ref[:, cut:]).astype(BF16)
 
 
 def make_cells(feats, places, lists):
-    atoms, feat = feats.shape
+    atoms = feats.shape[0]
     out_shape = (
-        struct(atoms, feat + CH, dtype=BF16),
+        struct(atoms, 2 * CH + GROUP_COLS[0], dtype=BF16),
         struct(atoms, CH, dtype=BF16),
         struct(atoms, CH),
-    )
+        struct(atoms, atoms, dtype=BF16),
+    )
+    args = (feats, places, lists)
     scratch = [pltpu.VMEM((CH, atoms), F32), pltpu.VMEM((CH, atoms), F32)]
-    return call(cells_kernel, "cells", out_shape, scratch, (feats, places, lists))
+    first, own_pos, meta, pick = call(cells_kernel, "cells", out_shape, scratch, args)
+    out_shape = (struct(atoms, GROUP_COLS[1], dtype=BF16),)
+    rest = call(rest_kernel, "cells_rest", out_shape, [], (feats, pick))[0]
+    return first, rest, own_pos, meta
 
 
 def spacing_of(atoms, nbasis):
@@ -461,14 +473,14 @@
 
 
 def start_kernel(
-    p0, p1, p2, own_ref, own_pos_ref, meta_ref, rbf_ref, rad_ref, mix_ref, out_ref, ew_ref,
+    p0, p1, p2, p3, p4, own_ref, own_pos_ref, meta_ref, rbf_ref, rad_ref, mix_ref, out_ref, ew_ref,
     acc0_ref,
     new_ref, oh_gh, d_gh, dt_gh, pre_ref, unit_ref, gs0_ref, en_ref, m0_gh, gate_gh, nf0_gh,
     radial_gh1, radial_gh2, radial_gh3, radial_gh4,
     table, sems, ghpos, acc_s,
 ):
     radial_gh = (None, radial_gh1, radial_gh2, radial_gh3, radial_gh4)
-    copies = fetch((p0, p1, p2), slice(0, 2 * CH), table, sems)
+    copies = fetch((p0, p1, p2, p3, p4), slice(0, 2 * CH), table, sems)
     atoms = own_ref.shape[0]
     ghosts = table.shape[0]
     spacing = spacing_of(atoms, rbf_ref.shape[0])
@@ -913,41 +925,39 @@
     feats = features[0, 0, 0]
     places = jnp.swapaxes(positions[0, 0], 0, 1)
     lists = jnp.concatenate([neighbours[0, 0, 0].T, counts[0, 0], cell_atoms[0, 0]], axis=0)
-    cells, own_pos, meta = make_cells(feats, places, lists)
+    cells0, cells1, own_pos, meta = make_cells(feats, places, lists)
     hold = lax.optimization_barrier
-    block = cells.reshape(2, 2, 2, 8, cells.shape[1])
-    cut = 2 * CH + GROUP_COLS[0]
-    z = neighbours_of(block, "gz", 2)
-    y1_in = neighbours_of(block[..., cut:], "gy", 1)
+    block0, block1 = (part.reshape(2, 2, 2, 8, part.shape[1]) for part in (cells0, cells1))
+    z0 = neighbours_of(block0, "gz", 2)
+    z1 = neighbours_of(block1, "gz", 2)
     oh_own, pre_own, unit_own, radt, rbft, home, *radial_own = own_stage(
         meta, own_pos, rbf_weight, radial_weight
     )
+    z0, oh_own = hold((z0, oh_own))
+    block0 = jnp.concatenate([z0[0], block0, z0[1]], axis=2)
+    y0 = neighbours_of(block0, "gy", 1)
+    x0_in = neighbours_of(block0, "gx", 0)
     (m0_own, gate_own, nf0_own, acc0), (own_a,) = own_forward_stage(
         (0,), feats, mix_weight, oh_own, radial_own
     )
-    z, y1_in, gate_own = hold((z, y1_in, gate_own))
-    block = jnp.concatenate([z[0], block, z[1]], axis=2)
-    block0, block1 = block[..., :cut], block[..., cut:]
-    y0 = neighbours_of(block0, "gy", 1)
+    block1 = jnp.concatenate([z1[0], block1, z1[1]], axis=2)
+    y0, x0_in, block1, acc0 = hold((y0, x0_in, block1, acc0))
+    x0_out = neighbours_of(jnp.concatenate(y0, axis=1), "gx", 0)
+    y1 = neighbours_of(block1, "gy", 1)
     x1_in = neighbours_of(block1, "gx", 0)
     _, (own_b,) = own_forward_stage((1,), feats, mix_weight, oh_own, radial_own, gate_own)
-    y0, x1_in, z1, acc_b = hold((y0, x1_in, [part[..., cut:] for part in z], own_b[2]))
+    x0_out, acc_b = hold((x0_out, own_b[2]))
     middle = jnp.concatenate([y0[0], block0, y0[1]], axis=1)
-    low, high = neighbours_of(middle, "gx", 0)
-    y1_out = neighbours_of(jnp.concatenate(z1, axis=2), "gy", 1)
-    low, high, y1_out = hold((low, high, y1_out))
-    y1 = [
-        jnp.concatenate([out[:, :, 0:1], inner, out[:, :, 1:2]], axis=2)
-        for out, inner in zip(y1_out, y1_in)
-    ]
-    pieces0 = tuple(flat_rows(piece) for piece in (low, middle, high))
-    pieces1 = ghost_pieces(y1, block1, x1_in)
+    pieces0 = (x0_in[0], x0_out[0], middle, x0_in[1], x0_out[1])
+    pieces0 = tuple(flat_rows(piece) for piece in pieces0)
     (
         new_0, oh_gh, d_gh, dt_gh, pre_gh, unit_gh, gs0, en_0, m0_gh, gate_gh, nf0_gh, *radial_gh,
     ) = start_stage(
         pieces0, feats, own_pos, meta, rbf_weight, radial_weight, mix_weight, out_weight,
         energy_weight[None], acc0,
     )
+    y1, gate_gh = hold((y1, gate_gh))
+    pieces1 = ghost_pieces(y1, block1, x1_in)
     shared = (feats, meta, mix_weight, out_weight, norm_weight, oh_gh, d_gh, dt_gh, gate_gh)
     new_a, en_a, _, (dot_gh_a, *gr_gh_a), (dot_own_a, *gr_own_a) = pairs_stage(
         0, 2 * CH, pieces0, shared, (gate_own, *own_a), radial_gh

time: 72.8 us -> 68.3 us (0.938)
  waiting for transfers between devices: 12.4 us -> 3.55 us
  starting transfers between devices: 23.2 us -> 27.5 us
    ppermute x6, waiting for transfers between devices: 6.4 us -> 0.29 us  [neighbours_of(): lax.ppermute(lax.slice_in_dim(block, length - 1, length, axis=dim), axis,...]
    ppermute x6, starting transfers between devices: 2.31 us -> 6.08 us  [neighbours_of(): lax.ppermute(lax.slice_in_dim(block, length - 1, length, axis=dim), axis,...]
    ppermute x6, waiting for transfers between devices: 4.26 us -> 2.5 us  [neighbours_of(): after = lax.ppermute(lax.slice_in_dim(block, 0, 1, axis=dim), axis, down)]
    ppermute x1, waiting for transfers between devices: 1.6 us -> 0.61 us  [give_back_z(): from_low = lax.ppermute(mid, 'gz', up)]
    ppermute x1, starting transfers between devices: 0.53 us -> 1.52 us  [give_back_z(): from_low = lax.ppermute(mid, 'gz', up)]
    ppermute x6, starting transfers between devices: 11.7 us -> 10.7 us  [neighbours_of(): after = lax.ppermute(lax.slice_in_dim(block, 0, 1, axis=dim), axis, down)]
    ppermute x1 -> x2, starting transfers between devices: 3.03 us -> 3.11 us  [neighbours_of(): other = lax.ppermute(block, axis, up)]
    pallas_call x12 -> x13, Pallas kernels: 29 us -> 29 us  [call(): pl.pallas_call(kernel, out_shape=out_shape, in_specs=specs or [pl.BlockSp...]
  transfers between devices with their start and end apart: 18 -> 19, of which waited for: 6 -> 5; matrix products, arithmetic and copies ran while one was open for 0% -> 1% of each run, Pallas kernels for 28% -> 30%
where the time goes in v11:
time: 68.3 us; the launch traced here: 67.9 us
  Pallas kernels  29 us (42%)
  starting transfers between devices  27.5 us (40%)
  local copies, waits for them, and re-layouts  5.73 us (8%)
  waiting for transfers between devices  3.55 us (5%)
  other arithmetic  1.08 us (2%)
  between operations  1.05 us (2%)
    pallas_call x13, Pallas kernels, call(): pl.pallas_call(kernel, out_shape=out_shape, in_specs=specs or [pl.BlockSp...  29 us
    ppermute x6, starting transfers between devices, neighbours_of(): after = lax.ppermute(lax.slice_in_dim(block, 0, 1, axis=dim), axis, down)  10.7 us
    ppermute x6, starting transfers between devices, neighbours_of(): lax.ppermute(lax.slice_in_dim(block, length - 1, length, axis=dim), axis,...  6.08 us
    unnamed x28, local copies, waits for them, and re-layouts  5.49 us
    ppermute x2, starting transfers between devices, give_back_y(): return (mid, lax.ppermute(mid, 'gy', up), lax.ppermute(mid, 'gy', down))  3.88 us
    ppermute x2, starting transfers between devices, neighbours_of(): other = lax.ppermute(block, axis, up)  3.11 us
    ppermute x6, waiting for transfers between devices, neighbours_of(): after = lax.ppermute(lax.slice_in_dim(block, 0, 1, axis=dim), axis, down)  2.5 us
    ppermute x1, starting transfers between devices, give_back_z(): from_low = lax.ppermute(mid, 'gz', up)  1.52 us
  transfers between devices with their start and end apart: 19, of which 5 were waited for; matrix products, arithmetic and copies ran while one was open for 1% of the time, Pallas kernels for 30%

profile of v11, /device:TPU:0, one launch (start us, length us, event | category | flops | bytes accessed | tf_op | source)
XLA Modules:
  0.0 67.9 jit_solution(15162032311798971060)
XLA Ops:
  1.4 1.0 %copy-done = bf16[1,1,1,64,3200]{4,3,2,1,0:T(8,128)(2,1)S(1)} copy-done((bf16[1,1,1,64,3200]{4,3,2,1,0:T(8,128)(2,1)S(1)}, bf16[1,1,1,64,3200]{4,3,2,1,0:T(8,128)(2,1)}, u32[]{:S(2)}) %copy-start) | copy-done | bytes 409624
  3.4 3.0 %collective-permute-start = (bf16[2,2,2,8,1280]{4,3,2,1,0:T(8,128)(2,1)S(1)}, bf16[2,2,2,8,1280]{4,3,2,1,0:T(8,128)(2,1)S(1)}, u32[]{:S(2)}, u32[]{:S(2)}) collective-permute-start(bf16[2,2,2,8,1280]{4,3,2,1,0:T(8,128)(2,1)S(1)} %bitcast.37), channel_id=1, source_target_pairs={{0,1},{1,0},{2,3},{3,2},{4,5},{5,4},{6,7},{7,6},{8,9},{9,8},{10,11... | collective-permute-start | bytes 491528 | tf_op jit(solution)/shard_map/ppermute | solution.py:836
  8.6 2.9 %own_edges.1 = (bf16[1024,64]{1,0:T(8,128)(2,1)S(1)}, bf16[1024,128]{1,0:T(8,128)(2,1)S(1)}, f32[1024,128]{1,0:T(8,128)S(1)}, bf16[640,128]{1,0:T(8,128)(2,1)S(1...) custom-call(f32[64,128]{1,0:T(8,128)S(1)} %get-tuple-element.88.meta, ...), custom_call_target="tpu_custom_call" | custom-call | flops 1024 | bytes 1024 | tf_op jit(solution)/shard_map/own_edges/pallas_call | solution.py:57
  11.6 2.2 %collective-permute-start.1 = (bf16[2,1,4,8,1280]{4,3,2,1,0:T(8,128)(2,1)S(1)}, bf16[2,1,4,8,1280]{4,3,2,1,0:T(8,128)(2,1)S(1)}, u32[]{:S(2)}, u32[]{:S(2)}) collective-permute-start(bf16[2,1,4,8,1280]{4,3,2,1,0:T(8,128)(2,1)S(1)} %get-tuple-element.185), channel_id=1, source_target_pairs={{0,2},{2,4},{4,6},{6,0},{1,3},{3,5},{5,7},{7,1},{8,10},{10,12},{12... | collective-permute-start | bytes 491528 | tf_op jit(solution)/shard_map/ppermute | solution.py:841
  13.7 2.1 %collective-permute-start.2 = (bf16[2,1,4,8,1280]{4,3,2,1,0:T(8,128)(2,1)S(1)}, bf16[2,1,4,8,1280]{4,3,2,1,0:T(8,128)(2,1)S(1)}, u32[]{:S(2)}, u32[]{:S(2)}) collective-permute-start(bf16[2,1,4,8,1280]{4,3,2,1,0:T(8,128)(2,1)S(1)} %get-tuple-element.184), channel_id=1, source_target_pairs={{2,0},{4,2},{6,4},{0,6},{3,1},{5,3},{7,5},{1,7},{10,8},{12,10},{14... | collective-permute-start | bytes 491528 | tf_op jit(solution)/shard_map/ppermute | solution.py:842
  15.9 1.7 %collective-permute-start.4 = (bf16[1,2,4,8,1280]{4,3,2,1,0:T(8,128)(2,1)S(1)}, bf16[1,2,4,8,1280]{4,3,2,1,0:T(8,128)(2,1)S(1)}, u32[]{:S(2)}, u32[]{:S(2)}) collective-permute-start(bf16[1,2,4,8,1280]{4,3,2,1,0:T(8,128)(2,1)S(1)} %get-tuple-element.182), channel_id=1, source_target_pairs={{8,0},{16,8},{24,16},{0,24},{9,1},{17,9},{25,17},{1,25},{10,2},{18... | collective-permute-start | bytes 491528 | tf_op jit(solution)/shard_map/ppermute | solution.py:842
  17.6 1.0 %copy-done.1 = bf16[1,1,1,64,3200]{4,3,2,1,0:T(8,128)(2,1)S(1)} copy-done((bf16[1,1,1,64,3200]{4,3,2,1,0:T(8,128)(2,1)S(1)}, bf16[1,1,1,64,3200]{4,3,2,1,0:T(8,128)(2,1)}, u32[]{:S(2)}) %copy-start.1) | copy-done | bytes 409624
  19.6 1.5 %own_forward_a.1 = (bf16[1024,128]{1,0:T(8,128)(2,1)S(1)}, bf16[1024,128]{1,0:T(8,128)(2,1)S(1)}, bf16[1024,128]{1,0:T(8,128)(2,1)S(1)}, f32[64,128]{1,0:T(8,128...) custom-call(bf16[64,3200]{1,0:T(8,128)(2,1)S(1)} %bitcast.27, ...), custom_call_target="tpu_custom_call" | custom-call | flops 1024 | bytes 1024 | tf_op jit(solution)/shard_map/own_forward_a/pallas_call | solution.py:57
  21.1 2.5 %own_forward_b.1 = (bf16[1024,2048]{1,0:T(8,128)(2,1)S(1)}, bf16[1024,2048]{1,0:T(8,128)(2,1)S(1)}, f32[64,2048]{1,0:T(8,128)S(1)}) custom-call(bf16[64,3200]{1,0:T(8,128)(2,1)S(1)} %bitcast.28, bf16[5,128,128]{2,1,0:T(8,128)(2,1)S(1)} %copy-done.3, bf16[1024,64]{1,0:T(8,128)(2,1)S(1)} %get-tuple-element.94.refs_2_.oh_own, ...), custom_call_target="tpu_custom_call" | custom-call | flops 1024 | bytes 1024 | tf_op jit(solution)/shard_map/own_forward_b/pallas_call | solution.py:57
  23.9 3.8 %collective-permute-start.8 = (bf16[2,1,4,8,2048]{4,3,2,1,0:T(8,128)(2,1)S(1)}, bf16[2,1,4,8,2048]{4,3,2,1,0:T(8,128)(2,1)S(1)}, u32[]{:S(2)}, u32[]{:S(2)}) collective-permute-start(bf16[2,1,4,8,2048]{4,3,2,1,0:T(8,128)(2,1)S(1)} %get-tuple-element.178), channel_id=1, source_target_pairs={{2,0},{4,2},{6,4},{0,6},{3,1},{5,3},{7,5},{1,7},{10,8},{12,10},{14... | collective-permute-start | bytes 786440 | tf_op jit(solution)/shard_map/ppermute | solution.py:842
  28.4 1.3 %collective-permute-start.12 = (bf16[1,2,4,8,2048]{4,3,2,1,0:T(8,128)(2,1)S(1)}, bf16[1,2,4,8,2048]{4,3,2,1,0:T(8,128)(2,1)S(1)}, u32[]{:S(2)}, u32[]{:S(2)}) collective-permute-start(bf16[1,2,4,8,2048]{4,3,2,1,0:T(8,128)(2,1)S(1)} %get-tuple-element.176), channel_id=1, source_target_pairs={{8,0},{16,8},{24,16},{0,24},{9,1},{17,9},{25,17},{1,25},{10,2},{18... | collective-permute-start | bytes 786440 | tf_op jit(solution)/shard_map/ppermute | solution.py:842
  29.8 1.5 %collective-permute-done.10 = bf16[1,2,4,8,1280]{4,3,2,1,0:T(8,128)(2,1)S(1)} collective-permute-done((bf16[1,2,4,8,1280]{4,3,2,1,0:T(8,128)(2,1)S(1)}, bf16[1,2,4,8,1280]{4,3,2,1,0:T(8,128)(2,1)S(1)}, u32[]{:S(2)}, u32[]{:S(2)}) %collective-permute-start.10) | collective-permute-done | bytes 163872 | tf_op jit(solution)/shard_map/ppermute | solution.py:842
  31.3 3.2 %collective-permute-start.6 = (bf16[1,2,4,8,2048]{4,3,2,1,0:T(8,128)(2,1)S(1)}, bf16[1,2,4,8,2048]{4,3,2,1,0:T(8,128)(2,1)S(1)}, u32[]{:S(2)}, u32[]{:S(2)}) collective-permute-start(bf16[1,2,4,8,2048]{4,3,2,1,0:T(8,128)(2,1)S(1)} %get-tuple-element.177), channel_id=1, source_target_pairs={{0,8},{8,16},{16,24},{24,0},{1,9},{9,17},{17,25},{25,1},{2,10},{10... | collective-permute-start | bytes 786440 | tf_op jit(solution)/shard_map/ppermute | solution.py:841
  34.6 3.4 %ghost_start.1 = (bf16[64,128]{1,0:T(8,128)(2,1)S(1)}, bf16[1024,512]{1,0:T(8,128)(2,1)S(1)}, bf16[1024,64]{1,0:T(8,128)(2,1)S(1)}, bf16[64,1024]{1,0:T(8,128)(2...) custom-call(bf16[64,1280]{1,0:T(8,128)(2,1)S(1)} %bitcast.40, ...), custom_call_target="tpu_custom_call" | custom-call | flops 1024 | bytes 1024 | tf_op jit(solution)/shard_map/ghost_start/pallas_call | solution.py:57
  38.2 1.7 %collective-permute-start.13 = (bf16[1,2,4,8,2048]{4,3,2,1,0:T(8,128)(2,1)S(1)}, bf16[1,2,4,8,2048]{4,3,2,1,0:T(8,128)(2,1)S(1)}, u32[]{:S(2)}, u32[]{:S(2)}) collective-permute-start(bf16[1,2,4,8,2048]{4,3,2,1,0:T(8,128)(2,1)S(1)} %get-tuple-element.174), channel_id=1, source_target_pairs={{8,0},{16,8},{24,16},{0,24},{9,1},{17,9},{25,17},{1,25},{10,2},{18... | collective-permute-start | bytes 786440 | tf_op jit(solution)/shard_map/ppermute | solution.py:842
  39.9 4.5 %pairs_a.1 = (bf16[64,1024]{1,0:T(8,128)(2,1)S(1)}, f32[64,128]{1,0:T(8,128)S(1)}, bf16[64,1024]{1,0:T(8,128)(2,1)}, bf16[1024,128]{1,0:T(8,128)(2,1)S(1)}, bf16...) custom-call(bf16[64,1280]{1,0:T(8,128)(2,1)S(1)} %bitcast.41, ...), custom_call_target="tpu_custom_call" | custom-call | flops 1024 | bytes 1024 | tf_op jit(solution)/shard_map/pairs_a/pallas_call | solution.py:57
  44.9 1.0 %collective-permute-done.13 = bf16[1,2,4,8,2048]{4,3,2,1,0:T(8,128)(2,1)S(1)} collective-permute-done((bf16[1,2,4,8,2048]{4,3,2,1,0:T(8,128)(2,1)S(1)}, bf16[1,2,4,8,2048]{4,3,2,1,0:T(8,128)(2,1)S(1)}, u32[]{:S(2)}, u32[]{:S(2)}) %collective-permute-start.13) | collective-permute-done | bytes 262176 | tf_op jit(solution)/shard_map/ppermute | solution.py:842
  45.8 7.6 %third_group.1 = (bf16[64,3200]{1,0:T(8,128)(2,1)}, f32[1,64]{1,0:T(1,128)}, f32[64,128]{1,0:T(8,128)S(1)}, f32[8,64]{1,0:T(8,128)S(1)}, f32[8,128]{1,0:T(8,128)...) custom-call(bf16[64,2048]{1,0:T(8,128)(2,1)S(1)} %bitcast.49, ...), custom_call_target="tpu_custom_call" | custom-call | flops 1024 | bytes 1024 | tf_op jit(solution)/shard_map/third_group/pallas_call | solution.py:57
  54.3 1.4 %collective-permute-start.15 = (f32[8,128]{1,0:T(8,128)S(1)}, f32[8,128]{1,0:T(8,128)S(1)}, u32[]{:S(2)}, u32[]{:S(2)}) collective-permute-start(f32[8,128]{1,0:T(8,128)S(1)} %get-tuple-element.144), channel_id=1, source_target_pairs={{8,0},{16,8},{24,16},{0,24},{9,1},{17,9},{25,17},{1,25},{10,2},{18... | collective-permute-start | bytes 12296 | tf_op jit(solution)/shard_map/ppermute | solution.py:893
  55.7 2.1 %own_backward_b.1 = (bf16[1024,128]{1,0:T(8,128)(2,1)S(1)}, bf16[1024,128]{1,0:T(8,128)(2,1)S(1)}, bf16[1024,128]{1,0:T(8,128)(2,1)S(1)}) custom-call(bf16[5,128,128]{2,1,0:T(8,128)(2,1)S(1)} %copy-done.4, bf16[64,2048]{1,0:T(8,128)(2,1)S(1)} %get-tuple-element.145.gs_ref, bf16[1024,128]{1,0:T(8,128)(2,1)S(1)} %get-tuple-element.105.refs_8_.refs_14_.gate_ref, ...), custom_call_target="tpu_custom_call" | custom-call | flops 1024 | bytes 1024 | tf_op jit(solution)/shard_map/own_backward_b/pallas_call | solution.py:57
  58.5 3.3 %collective-permute-start.17 = (f32[8,256]{1,0:T(8,128)S(1)}, f32[8,256]{1,0:T(8,128)S(1)}, u32[]{:S(2)}, u32[]{:S(2)}) collective-permute-start(f32[8,256]{1,0:T(8,128)S(1)} %add.3.mid_ref), channel_id=1, source_target_pairs={{2,0},{4,2},{6,4},{0,6},{3,1},{5,3},{7,5},{1,7},{10,8},{12,10},{14... | collective-permute-start | bytes 24584 | tf_op jit(solution)/shard_map/ppermute | solution.py:899
  61.8 1.5 %own_back.2 = (f32[64,128]{1,0:T(8,128)S(1)}, f32[8,64]{1,0:T(8,128)S(1)}) custom-call(bf16[1024,64]{1,0:T(8,128)(2,1)S(1)} %get-tuple-element.94.refs_2_.oh_own, bf16[1024,128]{1,0:T(8,128)(2,1)S(1)} %get-tuple-element.150.pre_own, f32[1024,128]{1,0:T(8,128)S(1)} %get-tuple-element.151.unit_own, bf16[640,128]{1,0:T(8,128)(2,1)S(1)} %get-tuple-element.119.radt_ref, ...), custom_call_target="tpu_custom_call" | custom-call | flops 1024 | bytes 1024 | tf_op jit(solution)/shard_map/own_back/pallas_call | solution.py:57
  63.5 1.5 %collective-permute-start.18 = (f32[8,256]{1,0:T(8,128)S(1)}, f32[8,256]{1,0:T(8,128)S(1)}, u32[]{:S(2)}, u32[]{:S(2)}) collective-permute-start(f32[8,256]{1,0:T(8,128)S(1)} %fold.1.mid_ref), channel_id=1, source_target_pairs={{0,1},{1,0},{2,3},{3,2},{4,5},{5,4},{6,7},{7,6},{8,9},{9,8},{10,11... | collective-permute-start | bytes 24584 | tf_op jit(solution)/shard_map/ppermute | solution.py:908
  65.0 1.5 %own_back.3 = (f32[64,128]{1,0:T(8,128)S(1)}, f32[8,64]{1,0:T(8,128)S(1)}) custom-call(bf16[1024,64]{1,0:T(8,128)(2,1)S(1)} %get-tuple-element.94.refs_2_.oh_own, bf16[1024,128]{1,0:T(8,128)(2,1)S(1)} %get-tuple-element.150.pre_own, f32[1024,128]{1,0:T(8,128)S(1)} %get-tuple-element.151.unit_own, bf16[640,128]{1,0:T(8,128)(2,1)S(1)} %get-tuple-element.119.radt_ref, ...), custom_call_target="tpu_custom_call" | custom-call | flops 1024 | bytes 1024 | tf_op jit(solution)/shard_map/own_back/pallas_call | solution.py:57
  (72 shorter events, 9.5 us)
Async XLA Ops:
  3.4 8.1 %collective-permute-start = (bf16[2,2,2,8,1280]{4,3,2,1,0:T(8,128)(2,1)S(1)}, bf16[2,2,2,8,1280]{4,3,2,1,0:T(8,128)(2,1)S(1)}, u32[]{:S(2)}, u32[]{:S(2)}) collective-permute-start(bf16[2,2,2,8,1280]{4,3,2,1,0:T(8,128)(2,1)S(1)} %bitcast.37), channel_id=1, source_target_pairs={{0,1},{1,0},{2,3},{3,2},{4,5},{5,4},{6,7},{7,6},{8,9},{9,8},{10,11... | collective-permute-start | bytes 491528 | tf_op jit(solution)/shard_map/ppermute | solution.py:836
  6.6 17.0 %collective-permute-start.5 = (bf16[2,2,2,8,2048]{4,3,2,1,0:T(8,128)(2,1)S(1)}, bf16[2,2,2,8,2048]{4,3,2,1,0:T(8,128)(2,1)S(1)}, u32[]{:S(2)}, u32[]{:S(2)}) collective-permute-start(bf16[2,2,2,8,2048]{4,3,2,1,0:T(8,128)(2,1)S(1)} %bitcast.35), channel_id=1, source_target_pairs={{0,1},{1,0},{2,3},{3,2},{4,5},{5,4},{6,7},{7,6},{8,9},{9,8},{10,11... | collective-permute-start | bytes 786440 | tf_op jit(solution)/shard_map/ppermute | solution.py:836
  11.6 12.2 %collective-permute-start.1 = (bf16[2,1,4,8,1280]{4,3,2,1,0:T(8,128)(2,1)S(1)}, bf16[2,1,4,8,1280]{4,3,2,1,0:T(8,128)(2,1)S(1)}, u32[]{:S(2)}, u32[]{:S(2)}) collective-permute-start(bf16[2,1,4,8,1280]{4,3,2,1,0:T(8,128)(2,1)S(1)} %get-tuple-element.185), channel_id=1, source_target_pairs={{0,2},{2,4},{4,6},{6,0},{1,3},{3,5},{5,7},{7,1},{8,10},{10,12},{12... | collective-permute-start | bytes 491528 | tf_op jit(solution)/shard_map/ppermute | solution.py:841
  13.7 10.0 %collective-permute-start.2 = (bf16[2,1,4,8,1280]{4,3,2,1,0:T(8,128)(2,1)S(1)}, bf16[2,1,4,8,1280]{4,3,2,1,0:T(8,128)(2,1)S(1)}, u32[]{:S(2)}, u32[]{:S(2)}) collective-permute-start(bf16[2,1,4,8,1280]{4,3,2,1,0:T(8,128)(2,1)S(1)} %get-tuple-element.184), channel_id=1, source_target_pairs={{2,0},{4,2},{6,4},{0,6},{3,1},{5,3},{7,5},{1,7},{10,8},{12,10},{14... | collective-permute-start | bytes 491528 | tf_op jit(solution)/shard_map/ppermute | solution.py:842
  15.8 7.9 %collective-permute-start.3 = (bf16[1,2,4,8,1280]{4,3,2,1,0:T(8,128)(2,1)S(1)}, bf16[1,2,4,8,1280]{4,3,2,1,0:T(8,128)(2,1)S(1)}, u32[]{:S(2)}, u32[]{:S(2)}) collective-permute-start(bf16[1,2,4,8,1280]{4,3,2,1,0:T(8,128)(2,1)S(1)} %get-tuple-element.183), channel_id=1, source_target_pairs={{0,8},{8,16},{16,24},{24,0},{1,9},{9,17},{17,25},{25,1},{2,10},{10... | collective-permute-start | bytes 491528 | tf_op jit(solution)/shard_map/ppermute | solution.py:841
  15.9 7.8 %collective-permute-start.4 = (bf16[1,2,4,8,1280]{4,3,2,1,0:T(8,128)(2,1)S(1)}, bf16[1,2,4,8,1280]{4,3,2,1,0:T(8,128)(2,1)S(1)}, u32[]{:S(2)}, u32[]{:S(2)}) collective-permute-start(bf16[1,2,4,8,1280]{4,3,2,1,0:T(8,128)(2,1)S(1)} %get-tuple-element.182), channel_id=1, source_target_pairs={{8,0},{16,8},{24,16},{0,24},{9,1},{17,9},{25,17},{1,25},{10,2},{18... | collective-permute-start | bytes 491528 | tf_op jit(solution)/shard_map/ppermute | solution.py:842
  21.1 13.5 %copy-start.2 = (bf16[1,1,1,64,3200]{4,3,2,1,0:T(8,128)(2,1)S(1)}, bf16[1,1,1,64,3200]{4,3,2,1,0:T(8,128)(2,1)}, u32[]{:S(2)}) copy-start(bf16[1,1,1,64,3200]{4,3,2,1,0:T(8,128)(2,1)} %param.11) | copy-start | bytes 1228804
  21.1 13.5 %copy-start.4 = (bf16[5,128,128]{2,1,0:T(8,128)(2,1)S(1)}, bf16[5,128,128]{2,1,0:T(8,128)(2,1)}, u32[]{:S(2)}) copy-start(bf16[5,128,128]{2,1,0:T(8,128)(2,1)} %mix_ref.9) | copy-start | bytes 491524
  21.1 13.5 %copy-start.5 = (bf16[5,128,128]{2,1,0:T(8,128)(2,1)S(1)}, bf16[5,128,128]{2,1,0:T(8,128)(2,1)}, u32[]{:S(2)}) copy-start(bf16[5,128,128]{2,1,0:T(8,128)(2,1)} %out_ref.3) | copy-start | bytes 491524
  21.1 13.5 %copy-start.7 = (bf16[128,640]{1,0:T(8,128)(2,1)S(1)}, bf16[128,640]{1,0:T(8,128)(2,1)}, u32[]{:S(2)}) copy-start(bf16[128,640]{1,0:T(8,128)(2,1)} %rad_ref.3) | copy-start | bytes 491524
  23.8 16.1 %copy-start.10 = (f32[4,128]{1,0:T(4,128)S(1)}, f32[4,128]{1,0:T(4,128)}, u32[]{:S(2)}) copy-start(f32[4,128]{1,0:T(4,128)} %nw_ref.1) | copy-start | bytes 6148
  23.9 14.1 %collective-permute-start.7 = (bf16[2,1,4,8,2048]{4,3,2,1,0:T(8,128)(2,1)S(1)}, bf16[2,1,4,8,2048]{4,3,2,1,0:T(8,128)(2,1)S(1)}, u32[]{:S(2)}, u32[]{:S(2)}) collective-permute-start(bf16[2,1,4,8,2048]{4,3,2,1,0:T(8,128)(2,1)S(1)} %get-tuple-element.179), channel_id=1, source_target_pairs={{0,2},{2,4},{4,6},{6,0},{1,3},{3,5},{5,7},{7,1},{8,10},{10,12},{12... | collective-permute-start | bytes 786440 | tf_op jit(solution)/shard_map/ppermute | solution.py:841
  23.9 14.1 %collective-permute-start.8 = (bf16[2,1,4,8,2048]{4,3,2,1,0:T(8,128)(2,1)S(1)}, bf16[2,1,4,8,2048]{4,3,2,1,0:T(8,128)(2,1)S(1)}, u32[]{:S(2)}, u32[]{:S(2)}) collective-permute-start(bf16[2,1,4,8,2048]{4,3,2,1,0:T(8,128)(2,1)S(1)} %get-tuple-element.178), channel_id=1, source_target_pairs={{2,0},{4,2},{6,4},{0,6},{3,1},{5,3},{7,5},{1,7},{10,8},{12,10},{14... | collective-permute-start | bytes 786440 | tf_op jit(solution)/shard_map/ppermute | solution.py:842
  27.8 3.5 %collective-permute-start.10 = (bf16[1,2,4,8,1280]{4,3,2,1,0:T(8,128)(2,1)S(1)}, bf16[1,2,4,8,1280]{4,3,2,1,0:T(8,128)(2,1)S(1)}, u32[]{:S(2)}, u32[]{:S(2)}) collective-permute-start(bf16[1,2,4,8,1280]{4,3,2,1,0:T(8,128)(2,1)S(1)} %get-tuple-element.180), channel_id=1, source_target_pairs={{8,0},{16,8},{24,16},{0,24},{9,1},{17,9},{25,17},{1,25},{10,2},{18... | collective-permute-start | bytes 491528 | tf_op jit(solution)/shard_map/ppermute | solution.py:842
  27.9 6.7 %collective-permute-start.9 = (bf16[1,2,4,8,1280]{4,3,2,1,0:T(8,128)(2,1)S(1)}, bf16[1,2,4,8,1280]{4,3,2,1,0:T(8,128)(2,1)S(1)}, u32[]{:S(2)}, u32[]{:S(2)}) collective-permute-start(bf16[1,2,4,8,1280]{4,3,2,1,0:T(8,128)(2,1)S(1)} %get-tuple-element.181), channel_id=1, source_target_pairs={{0,8},{8,16},{16,24},{24,0},{1,9},{9,17},{17,25},{25,1},{2,10},{10... | collective-permute-start | bytes 491528 | tf_op jit(solution)/shard_map/ppermute | solution.py:841
  28.4 16.2 %collective-permute-start.12 = (bf16[1,2,4,8,2048]{4,3,2,1,0:T(8,128)(2,1)S(1)}, bf16[1,2,4,8,2048]{4,3,2,1,0:T(8,128)(2,1)S(1)}, u32[]{:S(2)}, u32[]{:S(2)}) collective-permute-start(bf16[1,2,4,8,2048]{4,3,2,1,0:T(8,128)(2,1)S(1)} %get-tuple-element.176), channel_id=1, source_target_pairs={{8,0},{16,8},{24,16},{0,24},{9,1},{17,9},{25,17},{1,25},{10,2},{18... | collective-permute-start | bytes 786440 | tf_op jit(solution)/shard_map/ppermute | solution.py:842
  31.3 13.3 %collective-permute-start.6 = (bf16[1,2,4,8,2048]{4,3,2,1,0:T(8,128)(2,1)S(1)}, bf16[1,2,4,8,2048]{4,3,2,1,0:T(8,128)(2,1)S(1)}, u32[]{:S(2)}, u32[]{:S(2)}) collective-permute-start(bf16[1,2,4,8,2048]{4,3,2,1,0:T(8,128)(2,1)S(1)} %get-tuple-element.177), channel_id=1, source_target_pairs={{0,8},{8,16},{16,24},{24,0},{1,9},{9,17},{17,25},{25,1},{2,10},{10... | collective-permute-start | bytes 786440 | tf_op jit(solution)/shard_map/ppermute | solution.py:841
  38.1 6.8 %collective-permute-start.11 = (bf16[1,2,4,8,2048]{4,3,2,1,0:T(8,128)(2,1)S(1)}, bf16[1,2,4,8,2048]{4,3,2,1,0:T(8,128)(2,1)S(1)}, u32[]{:S(2)}, u32[]{:S(2)}) collective-permute-start(bf16[1,2,4,8,2048]{4,3,2,1,0:T(8,128)(2,1)S(1)} %get-tuple-element.175), channel_id=1, source_target_pairs={{0,8},{8,16},{16,24},{24,0},{1,9},{9,17},{17,25},{25,1},{2,10},{10... | collective-permute-start | bytes 786440 | tf_op jit(solution)/shard_map/ppermute | solution.py:841
  38.2 7.6 %collective-permute-start.13 = (bf16[1,2,4,8,2048]{4,3,2,1,0:T(8,128)(2,1)S(1)}, bf16[1,2,4,8,2048]{4,3,2,1,0:T(8,128)(2,1)S(1)}, u32[]{:S(2)}, u32[]{:S(2)}) collective-permute-start(bf16[1,2,4,8,2048]{4,3,2,1,0:T(8,128)(2,1)S(1)} %get-tuple-element.174), channel_id=1, source_target_pairs={{8,0},{16,8},{24,16},{0,24},{9,1},{17,9},{25,17},{1,25},{10,2},{18... | collective-permute-start | bytes 786440 | tf_op jit(solution)/shard_map/ppermute | solution.py:842
  53.5 4.4 %collective-permute-start.14 = (f32[8,128]{1,0:T(8,128)S(1)}, f32[8,128]{1,0:T(8,128)S(1)}, u32[]{:S(2)}, u32[]{:S(2)}) collective-permute-start(f32[8,128]{1,0:T(8,128)S(1)} %get-tuple-element.143), channel_id=1, source_target_pairs={{0,8},{8,16},{16,24},{24,0},{1,9},{9,17},{17,25},{25,1},{2,10},{10... | collective-permute-start | bytes 12296 | tf_op jit(solution)/shard_map/ppermute | solution.py:892
  54.3 3.6 %collective-permute-start.15 = (f32[8,128]{1,0:T(8,128)S(1)}, f32[8,128]{1,0:T(8,128)S(1)}, u32[]{:S(2)}, u32[]{:S(2)}) collective-permute-start(f32[8,128]{1,0:T(8,128)S(1)} %get-tuple-element.144), channel_id=1, source_target_pairs={{8,0},{16,8},{24,16},{0,24},{9,1},{17,9},{25,17},{1,25},{10,2},{18... | collective-permute-start | bytes 12296 | tf_op jit(solution)/shard_map/ppermute | solution.py:893
  57.9 5.5 %collective-permute-start.16 = (f32[8,256]{1,0:T(8,128)S(1)}, f32[8,256]{1,0:T(8,128)S(1)}, u32[]{:S(2)}, u32[]{:S(2)}) collective-permute-start(f32[8,256]{1,0:T(8,128)S(1)} %add.3.mid_ref), channel_id=1, source_target_pairs={{0,2},{2,4},{4,6},{6,0},{1,3},{3,5},{5,7},{7,1},{8,10},{10,12},{12... | collective-permute-start | bytes 24584 | tf_op jit(solution)/shard_map/ppermute | solution.py:899
  58.5 4.9 %collective-permute-start.17 = (f32[8,256]{1,0:T(8,128)S(1)}, f32[8,256]{1,0:T(8,128)S(1)}, u32[]{:S(2)}, u32[]{:S(2)}) collective-permute-start(f32[8,256]{1,0:T(8,128)S(1)} %add.3.mid_ref), channel_id=1, source_target_pairs={{2,0},{4,2},{6,4},{0,6},{3,1},{5,3},{7,5},{1,7},{10,8},{12,10},{14... | collective-permute-start | bytes 24584 | tf_op jit(solution)/shard_map/ppermute | solution.py:899
  63.5 3.7 %collective-permute-start.18 = (f32[8,256]{1,0:T(8,128)S(1)}, f32[8,256]{1,0:T(8,128)S(1)}, u32[]{:S(2)}, u32[]{:S(2)}) collective-permute-start(f32[8,256]{1,0:T(8,128)S(1)} %fold.1.mid_ref), channel_id=1, source_target_pairs={{0,1},{1,0},{2,3},{3,2},{4,5},{5,4},{6,7},{7,6},{8,9},{9,8},{10,11... | collective-permute-start | bytes 24584 | tf_op jit(solution)/shard_map/ppermute | solution.py:908
  (8 other events, 32.3 us)

commit v12 on v11

--- a/solution.py
+++ b/solution.py
@@ -67,17 +67,17 @@
 
 
 def cells_kernel(
-    feat_ref, pos_ref, lists_ref,
+    feat_ref, lists_ref,
     out_ref, own_pos_ref, meta_ref, pick_ref, rows_ref, pos_rows,
 ):
     rows_ref[...] = jnp.zeros_like(rows_ref)
     pos_rows[...] = jnp.zeros_like(pos_rows)
     atoms = feat_ref.shape[0]
-    rows_ref[0 : SLOTS + 2, :] = lists_ref[...].astype(F32)
+    rows_ref[0 : SLOTS + 2, :] = lists_ref[0 : SLOTS + 2, :]
     meta = rows_ref[...].T
     meta_ref[...] = meta
     for comp in range(3):
-        places = pos_ref[comp]
+        places = lists_ref[SLOTS + 2 + comp : SLOTS + 3 + comp, :]
         first = places.astype(BF16).astype(F32)
         second = (places - first).astype(BF16).astype(F32)
         pos_rows[comp : comp + 1, :] = first
@@ -100,7 +100,7 @@
     rest_ref[...] = mm(pick_ref[...], feat_ref[:, cut:]).astype(BF16)
 
 
-def make_cells(feats, places, lists):
+def make_cells(feats, lists):
     atoms = feats.shape[0]
     out_shape = (
         struct(atoms, 2 * CH + GROUP_COLS[0], dtype=BF16),
@@ -108,7 +108,7 @@
         struct(atoms, CH),
         struct(atoms, atoms, dtype=BF16),
     )
-    args = (feats, places, lists)
+    args = (feats, lists)
     scratch = [pltpu.VMEM((CH, atoms), F32), pltpu.VMEM((CH, atoms), F32)]
     first, own_pos, meta, pick = call(cells_kernel, "cells", out_shape, scratch, args)
     out_shape = (struct(atoms, GROUP_COLS[1], dtype=BF16),)
@@ -473,14 +473,14 @@
 
 
 def start_kernel(
-    p0, p1, p2, p3, p4, own_ref, own_pos_ref, meta_ref, rbf_ref, rad_ref, mix_ref, out_ref, ew_ref,
+    p0, p1, p2, own_ref, own_pos_ref, meta_ref, rbf_ref, rad_ref, mix_ref, out_ref, ew_ref,
     acc0_ref,
     new_ref, oh_gh, d_gh, dt_gh, pre_ref, unit_ref, gs0_ref, en_ref, m0_gh, gate_gh, nf0_gh,
     radial_gh1, radial_gh2, radial_gh3, radial_gh4,
     table, sems, ghpos, acc_s,
 ):
     radial_gh = (None, radial_gh1, radial_gh2, radial_gh3, radial_gh4)
-    copies = fetch((p0, p1, p2, p3, p4), slice(0, 2 * CH), table, sems)
+    copies = fetch((p0, p1, p2), slice(0, 2 * CH), table, sems)
     atoms = own_ref.shape[0]
     ghosts = table.shape[0]
     spacing = spacing_of(atoms, rbf_ref.shape[0])
@@ -706,8 +706,8 @@
 
 
 def third_kernel(
-    p0, p1, p2, p3, p4, own_ref, meta_ref, mix_ref, out_ref, nw_ref, oh_gh, d_gh, dt_gh, gate_gh,
-    acc_own, radt_ref, rbft_ref, gs0_ref, en_0, en_a, new_0, new_a, pre_gh, unit_gh,
+    p0, p1, p2, own_ref, meta_ref, mix_ref, out_ref, nw_ref, oh_gh, d_gh, dt_gh, gate_gh, acc_own,
+    radt_ref, rbft_ref, gs0_ref, en_0, en_a, new_0, new_a, pre_gh, unit_gh,
     m0_ref, nf0_ref, dot_a, *refs
 ):
     group = 1
@@ -717,7 +717,7 @@
     new_ref, energy_ref, src_ref, onto_ref, flow_ref, fmid_ref, fhigh_ref, gs_ref = refs[:8]
     table, sems, wm, wmt, wo, wot, nf_s, mx_s, acc_s, dot_c, en_s, fgh_s = refs[8:20]
     grads = dict(zip(degrees, refs[20:]))
-    copies = fetch((p0, p1, p2, p3, p4), slice(0, GROUP_COLS[group]), table, sems)
+    copies = fetch((p0, p1, p2), slice(0, GROUP_COLS[group]), table, sems)
     atoms = own_ref.shape[0]
     spacing = spacing_of(atoms, rbft_ref.shape[1])
     block_diagonal(KINDS[group], mix_ref, wm, wmt)
@@ -848,14 +848,6 @@
     return jnp.concatenate([before, block, after], axis=dim)
 
 
-def ghost_pieces(along_y, block, along_x):
-    outer = jnp.concatenate(along_y, axis=1)
-    low_out, high_out = neighbours_of(outer, "gx", 0)
-    low_in, high_in = along_x
-    middle = jnp.concatenate([along_y[0], block, along_y[1]], axis=1)
-    return tuple(flat_rows(piece) for piece in (low_in, low_out, middle, high_in, high_out))
-
-
 def flat_rows(piece):
     return piece.reshape(-1, piece.shape[-1])
 
@@ -923,47 +915,50 @@
     norm_weight,
 ):
     feats = features[0, 0, 0]
-    places = jnp.swapaxes(positions[0, 0], 0, 1)
-    lists = jnp.concatenate([neighbours[0, 0, 0].T, counts[0, 0], cell_atoms[0, 0]], axis=0)
-    cells0, cells1, own_pos, meta = make_cells(feats, places, lists)
+    lists = (neighbours[0, 0, 0].T, counts[0, 0], cell_atoms[0, 0])
+    lists = jnp.concatenate([*(part.astype(F32) for part in lists), positions[0, 0, 0]], axis=0)
+    cells0, cells1, own_pos, meta = make_cells(feats, lists)
     hold = lax.optimization_barrier
     block0, block1 = (part.reshape(2, 2, 2, 8, part.shape[1]) for part in (cells0, cells1))
     z0 = neighbours_of(block0, "gz", 2)
     z1 = neighbours_of(block1, "gz", 2)
+    y1_in = neighbours_of(block1, "gy", 1)
+    z0, own_pos, meta = hold((z0, own_pos, meta))
+    block0 = jnp.concatenate([z0[0], block0, z0[1]], axis=2)
+    y0 = neighbours_of(block0, "gy", 1)
     oh_own, pre_own, unit_own, radt, rbft, home, *radial_own = own_stage(
         meta, own_pos, rbf_weight, radial_weight
     )
-    z0, oh_own = hold((z0, oh_own))
-    block0 = jnp.concatenate([z0[0], block0, z0[1]], axis=2)
-    y0 = neighbours_of(block0, "gy", 1)
-    x0_in = neighbours_of(block0, "gx", 0)
+    y0, z1, y1_in, oh_own = hold((y0, z1, y1_in, oh_own))
+    middle = jnp.concatenate([y0[0], block0, y0[1]], axis=1)
+    x0 = neighbours_of(middle, "gx", 0)
+    y1_out = neighbours_of(jnp.concatenate(z1, axis=2), "gy", 1)
     (m0_own, gate_own, nf0_own, acc0), (own_a,) = own_forward_stage(
         (0,), feats, mix_weight, oh_own, radial_own
     )
+    x0, y1_out, acc0 = hold((x0, y1_out, acc0))
+    pieces0 = tuple(flat_rows(piece) for piece in (x0[0], middle, x0[1]))
+    low, high = [
+        jnp.concatenate([out[:, :, 0:1], inner, out[:, :, 1:2]], axis=2)
+        for out, inner in zip(y1_out, y1_in)
+    ]
     block1 = jnp.concatenate([z1[0], block1, z1[1]], axis=2)
-    y0, x0_in, block1, acc0 = hold((y0, x0_in, block1, acc0))
-    x0_out = neighbours_of(jnp.concatenate(y0, axis=1), "gx", 0)
-    y1 = neighbours_of(block1, "gy", 1)
-    x1_in = neighbours_of(block1, "gx", 0)
-    _, (own_b,) = own_forward_stage((1,), feats, mix_weight, oh_own, radial_own, gate_own)
-    x0_out, acc_b = hold((x0_out, own_b[2]))
-    middle = jnp.concatenate([y0[0], block0, y0[1]], axis=1)
-    pieces0 = (x0_in[0], x0_out[0], middle, x0_in[1], x0_out[1])
-    pieces0 = tuple(flat_rows(piece) for piece in pieces0)
+    block1 = jnp.concatenate([low, block1, high], axis=1)
+    low, high = neighbours_of(block1, "gx", 0)
+    pieces1 = tuple(flat_rows(piece) for piece in (low, block1, high))
     (
         new_0, oh_gh, d_gh, dt_gh, pre_gh, unit_gh, gs0, en_0, m0_gh, gate_gh, nf0_gh, *radial_gh,
     ) = start_stage(
         pieces0, feats, own_pos, meta, rbf_weight, radial_weight, mix_weight, out_weight,
         energy_weight[None], acc0,
     )
-    y1, gate_gh = hold((y1, gate_gh))
-    pieces1 = ghost_pieces(y1, block1, x1_in)
+    _, (own_b,) = own_forward_stage((1,), feats, mix_weight, oh_own, radial_own, gate_own)
     shared = (feats, meta, mix_weight, out_weight, norm_weight, oh_gh, d_gh, dt_gh, gate_gh)
     new_a, en_a, _, (dot_gh_a, *gr_gh_a), (dot_own_a, *gr_own_a) = pairs_stage(
         0, 2 * CH, pieces0, shared, (gate_own, *own_a), radial_gh
     )
     new, energy, src, onto, low, mid, high, gs_b = third_stage(
-        pieces1, *shared, acc_b, radt, rbft, gs0, en_0, en_a, new_0, new_a, pre_gh,
+        pieces1, *shared, own_b[2], radt, rbft, gs0, en_0, en_a, new_0, new_a, pre_gh,
         unit_gh, m0_gh, nf0_gh, dot_gh_a, *gr_gh_a,
         *[radial_gh[degree - 1] for degree in DEGREES[1]],
     )

time: 68.3 us -> 69.7 us (1.020)
  waiting for transfers between devices: 3.55 us -> 8.43 us
  local copies, waits for them, and re-layouts: 5.73 us -> 3.78 us
  starting transfers between devices: 27.5 us -> 26.2 us
    ppermute x6 -> x5, waiting for transfers between devices: 0.29 us -> 4.9 us  [neighbours_of(): lax.ppermute(lax.slice_in_dim(block, length - 1, length, axis=dim), axis,...]
    unnamed x28 -> x22, local copies, waits for them, and re-layouts: 5.49 us -> 3.54 us
    convert_element_type x0 -> x2, other arithmetic: none -> 1.39 us  [local(): part.astype(F32)]
    concatenate x3 -> x2, other arithmetic: 0.94 us -> 0.14 us  [the longest x1 0.13 us: local(): block1 = jnp.concatenate([low, block1, high], axis=1)]
    ppermute x6 -> x5, starting transfers between devices: 6.08 us -> 5.58 us  [neighbours_of(): lax.ppermute(lax.slice_in_dim(block, length - 1, length, axis=dim), axis,...]
    ppermute x6 -> x5, starting transfers between devices: 10.7 us -> 10.3 us  [neighbours_of(): after = lax.ppermute(lax.slice_in_dim(block, 0, 1, axis=dim), axis, down)]
    ppermute x6 -> x5, waiting for transfers between devices: 2.5 us -> 2.32 us  [neighbours_of(): after = lax.ppermute(lax.slice_in_dim(block, 0, 1, axis=dim), axis, down)]
  transfers between devices with their start and end apart: 19 -> 17, of which waited for: 5 -> 8; matrix products, arithmetic and copies ran while one was open for 1% -> 0% of each run, Pallas kernels for 30% -> 29%
where the time goes in v12:
time: 69.7 us; the launch traced here: 69.5 us
  Pallas kernels  28.4 us (41%)
  starting transfers between devices  26.2 us (38%)
  waiting for transfers between devices  8.43 us (12%)
  local copies, waits for them, and re-layouts  3.78 us (5%)
  other arithmetic  1.68 us (2%)
  between operations  0.95 us (1%)
    pallas_call x13, Pallas kernels, call(): pl.pallas_call(kernel, out_shape=out_shape, in_specs=specs or [pl.BlockSp...  28.4 us
    ppermute x5, starting transfers between devices, neighbours_of(): after = lax.ppermute(lax.slice_in_dim(block, 0, 1, axis=dim), axis, down)  10.3 us
    ppermute x5, starting transfers between devices, neighbours_of(): lax.ppermute(lax.slice_in_dim(block, length - 1, length, axis=dim), axis,...  5.58 us
    ppermute x5, waiting for transfers between devices, neighbours_of(): lax.ppermute(lax.slice_in_dim(block, length - 1, length, axis=dim), axis,...  4.9 us
    ppermute x2, starting transfers between devices, give_back_y(): return (mid, lax.ppermute(mid, 'gy', up), lax.ppermute(mid, 'gy', down))  3.88 us
    unnamed x22, local copies, waits for them, and re-layouts  3.54 us
    ppermute x2, starting transfers between devices, neighbours_of(): other = lax.ppermute(block, axis, up)  3.12 us
    ppermute x5, waiting for transfers between devices, neighbours_of(): after = lax.ppermute(lax.slice_in_dim(block, 0, 1, axis=dim), axis, down)  2.32 us
  transfers between devices with their start and end apart: 17, of which 8 were waited for; matrix products, arithmetic and copies ran while one was open for 0% of the time, Pallas kernels for 29%

profile of v12, /device:TPU:0, one launch (start us, length us, event | category | flops | bytes accessed | tf_op | source)
XLA Modules:
  0.0 69.5 jit_solution(1418036948898287082)
XLA Ops:
  4.1 3.0 %collective-permute-start = (bf16[2,2,2,8,1280]{4,3,2,1,0:T(8,128)(2,1)S(1)}, bf16[2,2,2,8,1280]{4,3,2,1,0:T(8,128)(2,1)S(1)}, u32[]{:S(2)}, u32[]{:S(2)}) collective-permute-start(bf16[2,2,2,8,1280]{4,3,2,1,0:T(8,128)(2,1)S(1)} %bitcast.43), channel_id=1, source_target_pairs={{0,1},{1,0},{2,3},{3,2},{4,5},{5,4},{6,7},{7,6},{8,9},{9,8},{10,11... | collective-permute-start | bytes 491528 | tf_op jit(solution)/shard_map/ppermute | solution.py:836
  7.4 2.1 %collective-permute-start.4 = (bf16[2,1,2,8,2048]{4,3,2,1,0:T(8,128)(2,1)S(1)}, bf16[2,1,2,8,2048]{4,3,2,1,0:T(8,128)(2,1)S(1)}, u32[]{:S(2)}, u32[]{:S(2)}) collective-permute-start(bf16[2,1,2,8,2048]{4,3,2,1,0:T(8,128)(2,1)S(1)} %get-tuple-element.185), channel_id=1, source_target_pairs={{0,2},{2,4},{4,6},{6,0},{1,3},{3,5},{5,7},{7,1},{8,10},{10,12},{12... | collective-permute-start | bytes 393224 | tf_op jit(solution)/shard_map/ppermute | solution.py:841
  9.5 2.1 %collective-permute-start.5 = (bf16[2,1,2,8,2048]{4,3,2,1,0:T(8,128)(2,1)S(1)}, bf16[2,1,2,8,2048]{4,3,2,1,0:T(8,128)(2,1)S(1)}, u32[]{:S(2)}, u32[]{:S(2)}) collective-permute-start(bf16[2,1,2,8,2048]{4,3,2,1,0:T(8,128)(2,1)S(1)} %get-tuple-element.184), channel_id=1, source_target_pairs={{2,0},{4,2},{6,4},{0,6},{3,1},{5,3},{7,5},{1,7},{10,8},{12,10},{14... | collective-permute-start | bytes 393224 | tf_op jit(solution)/shard_map/ppermute | solution.py:842
  12.2 2.2 %collective-permute-start.1 = (bf16[2,1,4,8,1280]{4,3,2,1,0:T(8,128)(2,1)S(1)}, bf16[2,1,4,8,1280]{4,3,2,1,0:T(8,128)(2,1)S(1)}, u32[]{:S(2)}, u32[]{:S(2)}) collective-permute-start(bf16[2,1,4,8,1280]{4,3,2,1,0:T(8,128)(2,1)S(1)} %get-tuple-element.181), channel_id=1, source_target_pairs={{0,2},{2,4},{4,6},{6,0},{1,3},{3,5},{5,7},{7,1},{8,10},{10,12},{12... | collective-permute-start | bytes 491528 | tf_op jit(solution)/shard_map/ppermute | solution.py:841
  14.4 2.1 %collective-permute-start.2 = (bf16[2,1,4,8,1280]{4,3,2,1,0:T(8,128)(2,1)S(1)}, bf16[2,1,4,8,1280]{4,3,2,1,0:T(8,128)(2,1)S(1)}, u32[]{:S(2)}, u32[]{:S(2)}) collective-permute-start(bf16[2,1,4,8,1280]{4,3,2,1,0:T(8,128)(2,1)S(1)} %get-tuple-element.180), channel_id=1, source_target_pairs={{2,0},{4,2},{6,4},{0,6},{3,1},{5,3},{7,5},{1,7},{10,8},{12,10},{14... | collective-permute-start | bytes 491528 | tf_op jit(solution)/shard_map/ppermute | solution.py:842
  18.3 2.9 %own_edges.1 = (bf16[1024,64]{1,0:T(8,128)(2,1)S(1)}, bf16[1024,128]{1,0:T(8,128)(2,1)S(1)}, f32[1024,128]{1,0:T(8,128)S(1)}, bf16[640,128]{1,0:T(8,128)(2,1)S(1...) custom-call(f32[64,128]{1,0:T(8,128)S(1)} %get-tuple-element.94.meta, ...), custom_call_target="tpu_custom_call" | custom-call | flops 1024 | bytes 1024 | tf_op jit(solution)/shard_map/own_edges/pallas_call | solution.py:57
  22.2 1.6 %collective-permute-done.2 = bf16[2,1,4,8,1280]{4,3,2,1,0:T(8,128)(2,1)S(1)} collective-permute-done((bf16[2,1,4,8,1280]{4,3,2,1,0:T(8,128)(2,1)S(1)}, bf16[2,1,4,8,1280]{4,3,2,1,0:T(8,128)(2,1)S(1)}, u32[]{:S(2)}, u32[]{:S(2)}) %collective-permute-start.2) | collective-permute-done | bytes 163872 | tf_op jit(solution)/shard_map/ppermute | solution.py:842
  24.0 1.7 %collective-permute-start.7 = (bf16[1,4,4,8,1280]{4,3,2,1,0:T(8,128)(2,1)S(1)}, bf16[1,4,4,8,1280]{4,3,2,1,0:T(8,128)(2,1)S(1)}, u32[]{:S(2)}, u32[]{:S(2)}) collective-permute-start(bf16[1,4,4,8,1280]{4,3,2,1,0:T(8,128)(2,1)S(1)} %get-tuple-element.178), channel_id=1, source_target_pairs={{8,0},{16,8},{24,16},{0,24},{9,1},{17,9},{25,17},{1,25},{10,2},{18... | collective-permute-start | bytes 983048 | tf_op jit(solution)/shard_map/ppermute | solution.py:842
  25.8 1.2 %collective-permute-start.8 = (bf16[2,1,2,8,2048]{4,3,2,1,0:T(8,128)(2,1)S(1)}, bf16[2,1,2,8,2048]{4,3,2,1,0:T(8,128)(2,1)S(1)}, u32[]{:S(2)}, u32[]{:S(2)}) collective-permute-start(bf16[2,1,2,8,2048]{4,3,2,1,0:T(8,128)(2,1)S(1)} %get-tuple-element.183), channel_id=1, source_target_pairs={{0,2},{2,4},{4,6},{6,0},{1,3},{3,5},{5,7},{7,1},{8,10},{10,12},{12... | collective-permute-start | bytes 393224 | tf_op jit(solution)/shard_map/ppermute | solution.py:841
  26.9 2.7 %collective-permute-start.9 = (bf16[2,1,2,8,2048]{4,3,2,1,0:T(8,128)(2,1)S(1)}, bf16[2,1,2,8,2048]{4,3,2,1,0:T(8,128)(2,1)S(1)}, u32[]{:S(2)}, u32[]{:S(2)}) collective-permute-start(bf16[2,1,2,8,2048]{4,3,2,1,0:T(8,128)(2,1)S(1)} %get-tuple-element.182), channel_id=1, source_target_pairs={{2,0},{4,2},{6,4},{0,6},{3,1},{5,3},{7,5},{1,7},{10,8},{12,10},{14... | collective-permute-start | bytes 393224 | tf_op jit(solution)/shard_map/ppermute | solution.py:842
  29.7 1.5 %own_forward_a.1 = (bf16[1024,128]{1,0:T(8,128)(2,1)S(1)}, bf16[1024,128]{1,0:T(8,128)(2,1)S(1)}, bf16[1024,128]{1,0:T(8,128)(2,1)S(1)}, f32[64,128]{1,0:T(8,128...) custom-call(bf16[64,3200]{1,0:T(8,128)(2,1)S(1)} %bitcast.28, ...), custom_call_target="tpu_custom_call" | custom-call | flops 1024 | bytes 1024 | tf_op jit(solution)/shard_map/own_forward_a/pallas_call | solution.py:57
  31.2 2.8 %collective-permute-done.8 = bf16[2,1,2,8,2048]{4,3,2,1,0:T(8,128)(2,1)S(1)} collective-permute-done((bf16[2,1,2,8,2048]{4,3,2,1,0:T(8,128)(2,1)S(1)}, bf16[2,1,2,8,2048]{4,3,2,1,0:T(8,128)(2,1)S(1)}, u32[]{:S(2)}, u32[]{:S(2)}) %collective-permute-start.8) | collective-permute-done | bytes 131104 | tf_op jit(solution)/shard_map/ppermute | solution.py:841
  35.1 1.7 %collective-permute-start.11 = (bf16[1,4,4,8,2048]{4,3,2,1,0:T(8,128)(2,1)S(1)}, bf16[1,4,4,8,2048]{4,3,2,1,0:T(8,128)(2,1)S(1)}, u32[]{:S(2)}, u32[]{:S(2)}) collective-permute-start(bf16[1,4,4,8,2048]{4,3,2,1,0:T(8,128)(2,1)S(1)} %get-tuple-element.176), channel_id=1, source_target_pairs={{8,0},{16,8},{24,16},{0,24},{9,1},{17,9},{25,17},{1,25},{10,2},{18... | collective-permute-start | bytes 1572872 | tf_op jit(solution)/shard_map/ppermute | solution.py:842
  36.8 2.5 %own_forward_b.1 = (bf16[1024,2048]{1,0:T(8,128)(2,1)S(1)}, bf16[1024,2048]{1,0:T(8,128)(2,1)S(1)}, f32[64,2048]{1,0:T(8,128)S(1)}) custom-call(bf16[64,3200]{1,0:T(8,128)(2,1)S(1)} %bitcast.29, bf16[5,128,128]{2,1,0:T(8,128)(2,1)S(1)} %copy-done.2, bf16[1024,64]{1,0:T(8,128)(2,1)S(1)} %get-tuple-element.101.refs_2_.oh_own, ...), custom_call_target="tpu_custom_call" | custom-call | flops 1024 | bytes 1024 | tf_op jit(solution)/shard_map/own_forward_b/pallas_call | solution.py:57
  39.3 3.6 %ghost_start.1 = (bf16[64,128]{1,0:T(8,128)(2,1)S(1)}, bf16[1024,512]{1,0:T(8,128)(2,1)S(1)}, bf16[1024,64]{1,0:T(8,128)(2,1)S(1)}, bf16[64,1024]{1,0:T(8,128)(2...) custom-call(bf16[128,1280]{1,0:T(8,128)(2,1)S(1)} %bitcast.39, ...), custom_call_target="tpu_custom_call" | custom-call | flops 1024 | bytes 1024 | tf_op jit(solution)/shard_map/ghost_start/pallas_call | solution.py:57
  42.9 4.4 %pairs_a.1 = (bf16[64,1024]{1,0:T(8,128)(2,1)S(1)}, f32[64,128]{1,0:T(8,128)S(1)}, bf16[64,1024]{1,0:T(8,128)(2,1)}, bf16[1024,128]{1,0:T(8,128)(2,1)S(1)}, bf16...) custom-call(bf16[128,1280]{1,0:T(8,128)(2,1)S(1)} %bitcast.40, ...), custom_call_target="tpu_custom_call" | custom-call | flops 1024 | bytes 1024 | tf_op jit(solution)/shard_map/pairs_a/pallas_call | solution.py:57
  47.3 1.1 %collective-permute-done.10 = bf16[1,4,4,8,2048]{4,3,2,1,0:T(8,128)(2,1)S(1)} collective-permute-done((bf16[1,4,4,8,2048]{4,3,2,1,0:T(8,128)(2,1)S(1)}, bf16[1,4,4,8,2048]{4,3,2,1,0:T(8,128)(2,1)S(1)}, u32[]{:S(2)}, u32[]{:S(2)}) %collective-permute-start.10) | collective-permute-done | bytes 524320 | tf_op jit(solution)/shard_map/ppermute | solution.py:841
  48.5 7.0 %third_group.1 = (bf16[64,3200]{1,0:T(8,128)(2,1)}, f32[1,64]{1,0:T(1,128)}, f32[64,128]{1,0:T(8,128)S(1)}, f32[8,64]{1,0:T(8,128)S(1)}, f32[8,128]{1,0:T(8,128)...) custom-call(bf16[128,2048]{1,0:T(8,128)(2,1)S(1)} %bitcast.46, ...), custom_call_target="tpu_custom_call" | custom-call | flops 1024 | bytes 1024 | tf_op jit(solution)/shard_map/third_group/pallas_call | solution.py:57
  56.1 1.1 %collective-permute-start.13 = (f32[8,128]{1,0:T(8,128)S(1)}, f32[8,128]{1,0:T(8,128)S(1)}, u32[]{:S(2)}, u32[]{:S(2)}) collective-permute-start(f32[8,128]{1,0:T(8,128)S(1)} %get-tuple-element.146), channel_id=1, source_target_pairs={{8,0},{16,8},{24,16},{0,24},{9,1},{17,9},{25,17},{1,25},{10,2},{18... | collective-permute-start | bytes 12296 | tf_op jit(solution)/shard_map/ppermute | solution.py:885
  57.2 2.1 %own_backward_b.1 = (bf16[1024,128]{1,0:T(8,128)(2,1)S(1)}, bf16[1024,128]{1,0:T(8,128)(2,1)S(1)}, bf16[1024,128]{1,0:T(8,128)(2,1)S(1)}) custom-call(bf16[5,128,128]{2,1,0:T(8,128)(2,1)S(1)} %copy-done.2, bf16[64,2048]{1,0:T(8,128)(2,1)S(1)} %get-tuple-element.147.gs_ref, bf16[1024,128]{1,0:T(8,128)(2,1)S(1)} %get-tuple-element.119.refs_8_.refs_12_.gate_ref, ...), custom_call_target="tpu_custom_call" | custom-call | flops 1024 | bytes 1024 | tf_op jit(solution)/shard_map/own_backward_b/pallas_call | solution.py:57
  60.5 2.8 %collective-permute-start.15 = (f32[8,256]{1,0:T(8,128)S(1)}, f32[8,256]{1,0:T(8,128)S(1)}, u32[]{:S(2)}, u32[]{:S(2)}) collective-permute-start(f32[8,256]{1,0:T(8,128)S(1)} %add.3.mid_ref), channel_id=1, source_target_pairs={{2,0},{4,2},{6,4},{0,6},{3,1},{5,3},{7,5},{1,7},{10,8},{12,10},{14... | collective-permute-start | bytes 24584 | tf_op jit(solution)/shard_map/ppermute | solution.py:891
  63.3 1.5 %own_back.2 = (f32[64,128]{1,0:T(8,128)S(1)}, f32[8,64]{1,0:T(8,128)S(1)}) custom-call(bf16[1024,64]{1,0:T(8,128)(2,1)S(1)} %get-tuple-element.101.refs_2_.oh_own, bf16[1024,128]{1,0:T(8,128)(2,1)S(1)} %get-tuple-element.152.pre_own, f32[1024,128]{1,0:T(8,128)S(1)} %get-tuple-element.153.unit_own, bf16[640,128]{1,0:T(8,128)(2,1)S(1)} %get-tuple-element.121.radt_ref, ...), custom_call_target="tpu_custom_call" | custom-call | flops 1024 | bytes 1024 | tf_op jit(solution)/shard_map/own_back/pallas_call | solution.py:57
  65.0 1.5 %collective-permute-start.16 = (f32[8,256]{1,0:T(8,128)S(1)}, f32[8,256]{1,0:T(8,128)S(1)}, u32[]{:S(2)}, u32[]{:S(2)}) collective-permute-start(f32[8,256]{1,0:T(8,128)S(1)} %fold.1.mid_ref), channel_id=1, source_target_pairs={{0,1},{1,0},{2,3},{3,2},{4,5},{5,4},{6,7},{7,6},{8,9},{9,8},{10,11... | collective-permute-start | bytes 24584 | tf_op jit(solution)/shard_map/ppermute | solution.py:900
  66.6 1.5 %own_back.3 = (f32[64,128]{1,0:T(8,128)S(1)}, f32[8,64]{1,0:T(8,128)S(1)}) custom-call(bf16[1024,64]{1,0:T(8,128)(2,1)S(1)} %get-tuple-element.101.refs_2_.oh_own, bf16[1024,128]{1,0:T(8,128)(2,1)S(1)} %get-tuple-element.152.pre_own, f32[1024,128]{1,0:T(8,128)S(1)} %get-tuple-element.153.unit_own, bf16[640,128]{1,0:T(8,128)(2,1)S(1)} %get-tuple-element.121.radt_ref, ...), custom_call_target="tpu_custom_call" | custom-call | flops 1024 | bytes 1024 | tf_op jit(solution)/shard_map/own_back/pallas_call | solution.py:57
  (63 shorter events, 11.7 us)
Async XLA Ops:
  3.7 25.9 %copy-start.1 = (bf16[1,1,1,64,3200]{4,3,2,1,0:T(8,128)(2,1)S(1)}, bf16[1,1,1,64,3200]{4,3,2,1,0:T(8,128)(2,1)}, u32[]{:S(2)}) copy-start(bf16[1,1,1,64,3200]{4,3,2,1,0:T(8,128)(2,1)} %param.11) | copy-start | bytes 1228804
  3.7 25.9 %copy-start.2 = (bf16[5,128,128]{2,1,0:T(8,128)(2,1)S(1)}, bf16[5,128,128]{2,1,0:T(8,128)(2,1)}, u32[]{:S(2)}) copy-start(bf16[5,128,128]{2,1,0:T(8,128)(2,1)} %mix_ref.9) | copy-start | bytes 491524
  4.1 8.1 %collective-permute-start = (bf16[2,2,2,8,1280]{4,3,2,1,0:T(8,128)(2,1)S(1)}, bf16[2,2,2,8,1280]{4,3,2,1,0:T(8,128)(2,1)S(1)}, u32[]{:S(2)}, u32[]{:S(2)}) collective-permute-start(bf16[2,2,2,8,1280]{4,3,2,1,0:T(8,128)(2,1)S(1)} %bitcast.43), channel_id=1, source_target_pairs={{0,1},{1,0},{2,3},{3,2},{4,5},{5,4},{6,7},{7,6},{8,9},{9,8},{10,11... | collective-permute-start | bytes 491528 | tf_op jit(solution)/shard_map/ppermute | solution.py:836
  7.3 13.9 %collective-permute-start.3 = (bf16[2,2,2,8,2048]{4,3,2,1,0:T(8,128)(2,1)S(1)}, bf16[2,2,2,8,2048]{4,3,2,1,0:T(8,128)(2,1)S(1)}, u32[]{:S(2)}, u32[]{:S(2)}) collective-permute-start(bf16[2,2,2,8,2048]{4,3,2,1,0:T(8,128)(2,1)S(1)} %bitcast.36), channel_id=1, source_target_pairs={{0,1},{1,0},{2,3},{3,2},{4,5},{5,4},{6,7},{7,6},{8,9},{9,8},{10,11... | collective-permute-start | bytes 786440 | tf_op jit(solution)/shard_map/ppermute | solution.py:836
  7.4 13.8 %collective-permute-start.4 = (bf16[2,1,2,8,2048]{4,3,2,1,0:T(8,128)(2,1)S(1)}, bf16[2,1,2,8,2048]{4,3,2,1,0:T(8,128)(2,1)S(1)}, u32[]{:S(2)}, u32[]{:S(2)}) collective-permute-start(bf16[2,1,2,8,2048]{4,3,2,1,0:T(8,128)(2,1)S(1)} %get-tuple-element.185), channel_id=1, source_target_pairs={{0,2},{2,4},{4,6},{6,0},{1,3},{3,5},{5,7},{7,1},{8,10},{10,12},{12... | collective-permute-start | bytes 393224 | tf_op jit(solution)/shard_map/ppermute | solution.py:841
  9.5 11.7 %collective-permute-start.5 = (bf16[2,1,2,8,2048]{4,3,2,1,0:T(8,128)(2,1)S(1)}, bf16[2,1,2,8,2048]{4,3,2,1,0:T(8,128)(2,1)S(1)}, u32[]{:S(2)}, u32[]{:S(2)}) collective-permute-start(bf16[2,1,2,8,2048]{4,3,2,1,0:T(8,128)(2,1)S(1)} %get-tuple-element.184), channel_id=1, source_target_pairs={{2,0},{4,2},{6,4},{0,6},{3,1},{5,3},{7,5},{1,7},{10,8},{12,10},{14... | collective-permute-start | bytes 393224 | tf_op jit(solution)/shard_map/ppermute | solution.py:842
  12.2 10.0 %collective-permute-start.1 = (bf16[2,1,4,8,1280]{4,3,2,1,0:T(8,128)(2,1)S(1)}, bf16[2,1,4,8,1280]{4,3,2,1,0:T(8,128)(2,1)S(1)}, u32[]{:S(2)}, u32[]{:S(2)}) collective-permute-start(bf16[2,1,4,8,1280]{4,3,2,1,0:T(8,128)(2,1)S(1)} %get-tuple-element.181), channel_id=1, source_target_pairs={{0,2},{2,4},{4,6},{6,0},{1,3},{3,5},{5,7},{7,1},{8,10},{10,12},{12... | collective-permute-start | bytes 491528 | tf_op jit(solution)/shard_map/ppermute | solution.py:841
  14.4 9.4 %collective-permute-start.2 = (bf16[2,1,4,8,1280]{4,3,2,1,0:T(8,128)(2,1)S(1)}, bf16[2,1,4,8,1280]{4,3,2,1,0:T(8,128)(2,1)S(1)}, u32[]{:S(2)}, u32[]{:S(2)}) collective-permute-start(bf16[2,1,4,8,1280]{4,3,2,1,0:T(8,128)(2,1)S(1)} %get-tuple-element.180), channel_id=1, source_target_pairs={{2,0},{4,2},{6,4},{0,6},{3,1},{5,3},{7,5},{1,7},{10,8},{12,10},{14... | collective-permute-start | bytes 491528 | tf_op jit(solution)/shard_map/ppermute | solution.py:842
  23.9 10.8 %collective-permute-start.6 = (bf16[1,4,4,8,1280]{4,3,2,1,0:T(8,128)(2,1)S(1)}, bf16[1,4,4,8,1280]{4,3,2,1,0:T(8,128)(2,1)S(1)}, u32[]{:S(2)}, u32[]{:S(2)}) collective-permute-start(bf16[1,4,4,8,1280]{4,3,2,1,0:T(8,128)(2,1)S(1)} %get-tuple-element.179), channel_id=1, source_target_pairs={{0,8},{8,16},{16,24},{24,0},{1,9},{9,17},{17,25},{25,1},{2,10},{10... | collective-permute-start | bytes 983048 | tf_op jit(solution)/shard_map/ppermute | solution.py:841
  24.0 10.8 %collective-permute-start.7 = (bf16[1,4,4,8,1280]{4,3,2,1,0:T(8,128)(2,1)S(1)}, bf16[1,4,4,8,1280]{4,3,2,1,0:T(8,128)(2,1)S(1)}, u32[]{:S(2)}, u32[]{:S(2)}) collective-permute-start(bf16[1,4,4,8,1280]{4,3,2,1,0:T(8,128)(2,1)S(1)} %get-tuple-element.178), channel_id=1, source_target_pairs={{8,0},{16,8},{24,16},{0,24},{9,1},{17,9},{25,17},{1,25},{10,2},{18... | collective-permute-start | bytes 983048 | tf_op jit(solution)/shard_map/ppermute | solution.py:842
  25.8 8.2 %collective-permute-start.8 = (bf16[2,1,2,8,2048]{4,3,2,1,0:T(8,128)(2,1)S(1)}, bf16[2,1,2,8,2048]{4,3,2,1,0:T(8,128)(2,1)S(1)}, u32[]{:S(2)}, u32[]{:S(2)}) collective-permute-start(bf16[2,1,2,8,2048]{4,3,2,1,0:T(8,128)(2,1)S(1)} %get-tuple-element.183), channel_id=1, source_target_pairs={{0,2},{2,4},{4,6},{6,0},{1,3},{3,5},{5,7},{7,1},{8,10},{10,12},{12... | collective-permute-start | bytes 393224 | tf_op jit(solution)/shard_map/ppermute | solution.py:841
  26.9 7.8 %collective-permute-start.9 = (bf16[2,1,2,8,2048]{4,3,2,1,0:T(8,128)(2,1)S(1)}, bf16[2,1,2,8,2048]{4,3,2,1,0:T(8,128)(2,1)S(1)}, u32[]{:S(2)}, u32[]{:S(2)}) collective-permute-start(bf16[2,1,2,8,2048]{4,3,2,1,0:T(8,128)(2,1)S(1)} %get-tuple-element.182), channel_id=1, source_target_pairs={{2,0},{4,2},{6,4},{0,6},{3,1},{5,3},{7,5},{1,7},{10,8},{12,10},{14... | collective-permute-start | bytes 393224 | tf_op jit(solution)/shard_map/ppermute | solution.py:842
  29.6 9.7 %copy-start.3 = (bf16[5,128,128]{2,1,0:T(8,128)(2,1)S(1)}, bf16[5,128,128]{2,1,0:T(8,128)(2,1)}, u32[]{:S(2)}) copy-start(bf16[5,128,128]{2,1,0:T(8,128)(2,1)} %out_ref.3) | copy-start | bytes 491524
  29.6 9.7 %copy-start.5 = (bf16[128,640]{1,0:T(8,128)(2,1)S(1)}, bf16[128,640]{1,0:T(8,128)(2,1)}, u32[]{:S(2)}) copy-start(bf16[128,640]{1,0:T(8,128)(2,1)} %rad_ref.3) | copy-start | bytes 491524
  29.7 9.7 %copy-start.7 = (bf16[512,128]{1,0:T(8,128)(2,1)S(1)}, bf16[512,128]{1,0:T(8,128)(2,1)}, u32[]{:S(2)}) copy-start(bf16[512,128]{1,0:T(8,128)(2,1)} %rbf_ref.3) | copy-start | bytes 393220
  29.7 9.7 %copy-start.9 = (f32[128]{0:T(128)S(1)}, f32[128]{0:T(128)}, u32[]{:S(2)}) copy-start(f32[128]{0:T(128)} %param.20) | copy-start | bytes 1540
  34.8 8.1 %copy-start.8 = (f32[4,128]{1,0:T(4,128)S(1)}, f32[4,128]{1,0:T(4,128)}, u32[]{:S(2)}) copy-start(f32[4,128]{1,0:T(4,128)} %nw_ref.1) | copy-start | bytes 6148
  35.0 13.5 %collective-permute-start.10 = (bf16[1,4,4,8,2048]{4,3,2,1,0:T(8,128)(2,1)S(1)}, bf16[1,4,4,8,2048]{4,3,2,1,0:T(8,128)(2,1)S(1)}, u32[]{:S(2)}, u32[]{:S(2)}) collective-permute-start(bf16[1,4,4,8,2048]{4,3,2,1,0:T(8,128)(2,1)S(1)} %get-tuple-element.177), channel_id=1, source_target_pairs={{0,8},{8,16},{16,24},{24,0},{1,9},{9,17},{17,25},{25,1},{2,10},{10... | collective-permute-start | bytes 1572872 | tf_op jit(solution)/shard_map/ppermute | solution.py:841
  35.1 13.4 %collective-permute-start.11 = (bf16[1,4,4,8,2048]{4,3,2,1,0:T(8,128)(2,1)S(1)}, bf16[1,4,4,8,2048]{4,3,2,1,0:T(8,128)(2,1)S(1)}, u32[]{:S(2)}, u32[]{:S(2)}) collective-permute-start(bf16[1,4,4,8,2048]{4,3,2,1,0:T(8,128)(2,1)S(1)} %get-tuple-element.176), channel_id=1, source_target_pairs={{8,0},{16,8},{24,16},{0,24},{9,1},{17,9},{25,17},{1,25},{10,2},{18... | collective-permute-start | bytes 1572872 | tf_op jit(solution)/shard_map/ppermute | solution.py:842
  55.5 4.0 %collective-permute-start.12 = (f32[8,128]{1,0:T(8,128)S(1)}, f32[8,128]{1,0:T(8,128)S(1)}, u32[]{:S(2)}, u32[]{:S(2)}) collective-permute-start(f32[8,128]{1,0:T(8,128)S(1)} %get-tuple-element.145), channel_id=1, source_target_pairs={{0,8},{8,16},{16,24},{24,0},{1,9},{9,17},{17,25},{25,1},{2,10},{10... | collective-permute-start | bytes 12296 | tf_op jit(solution)/shard_map/ppermute | solution.py:884
  56.1 3.3 %collective-permute-start.13 = (f32[8,128]{1,0:T(8,128)S(1)}, f32[8,128]{1,0:T(8,128)S(1)}, u32[]{:S(2)}, u32[]{:S(2)}) collective-permute-start(f32[8,128]{1,0:T(8,128)S(1)} %get-tuple-element.146), channel_id=1, source_target_pairs={{8,0},{16,8},{24,16},{0,24},{9,1},{17,9},{25,17},{1,25},{10,2},{18... | collective-permute-start | bytes 12296 | tf_op jit(solution)/shard_map/ppermute | solution.py:885
  59.4 5.5 %collective-permute-start.14 = (f32[8,256]{1,0:T(8,128)S(1)}, f32[8,256]{1,0:T(8,128)S(1)}, u32[]{:S(2)}, u32[]{:S(2)}) collective-permute-start(f32[8,256]{1,0:T(8,128)S(1)} %add.3.mid_ref), channel_id=1, source_target_pairs={{0,2},{2,4},{4,6},{6,0},{1,3},{3,5},{5,7},{7,1},{8,10},{10,12},{12... | collective-permute-start | bytes 24584 | tf_op jit(solution)/shard_map/ppermute | solution.py:891
  60.5 4.4 %collective-permute-start.15 = (f32[8,256]{1,0:T(8,128)S(1)}, f32[8,256]{1,0:T(8,128)S(1)}, u32[]{:S(2)}, u32[]{:S(2)}) collective-permute-start(f32[8,256]{1,0:T(8,128)S(1)} %add.3.mid_ref), channel_id=1, source_target_pairs={{2,0},{4,2},{6,4},{0,6},{3,1},{5,3},{7,5},{1,7},{10,8},{12,10},{14... | collective-permute-start | bytes 24584 | tf_op jit(solution)/shard_map/ppermute | solution.py:891
  65.0 3.7 %collective-permute-start.16 = (f32[8,256]{1,0:T(8,128)S(1)}, f32[8,256]{1,0:T(8,128)S(1)}, u32[]{:S(2)}, u32[]{:S(2)}) collective-permute-start(f32[8,256]{1,0:T(8,128)S(1)} %fold.1.mid_ref), channel_id=1, source_target_pairs={{0,1},{1,0},{2,3},{3,2},{4,5},{5,4},{6,7},{7,6},{8,9},{9,8},{10,11... | collective-permute-start | bytes 24584 | tf_op jit(solution)/shard_map/ppermute | solution.py:900
  (3 other events, 2.8 us)

commit v13 on v12

--- a/solution.py
+++ b/solution.py
@@ -67,17 +67,17 @@
 
 
 def cells_kernel(
-    feat_ref, lists_ref,
+    feat_ref, pos_ref, lists_ref,
     out_ref, own_pos_ref, meta_ref, pick_ref, rows_ref, pos_rows,
 ):
     rows_ref[...] = jnp.zeros_like(rows_ref)
     pos_rows[...] = jnp.zeros_like(pos_rows)
     atoms = feat_ref.shape[0]
-    rows_ref[0 : SLOTS + 2, :] = lists_ref[0 : SLOTS + 2, :]
+    rows_ref[0 : SLOTS + 2, :] = lists_ref[...].astype(F32)
     meta = rows_ref[...].T
     meta_ref[...] = meta
     for comp in range(3):
-        places = lists_ref[SLOTS + 2 + comp : SLOTS + 3 + comp, :]
+        places = pos_ref[comp]
         first = places.astype(BF16).astype(F32)
         second = (places - first).astype(BF16).astype(F32)
         pos_rows[comp : comp + 1, :] = first
@@ -100,7 +100,7 @@
     rest_ref[...] = mm(pick_ref[...], feat_ref[:, cut:]).astype(BF16)
 
 
-def make_cells(feats, lists):
+def make_cells(feats, places, lists):
     atoms = feats.shape[0]
     out_shape = (
         struct(atoms, 2 * CH + GROUP_COLS[0], dtype=BF16),
@@ -108,7 +108,7 @@
         struct(atoms, CH),
         struct(atoms, atoms, dtype=BF16),
     )
-    args = (feats, lists)
+    args = (feats, places, lists)
     scratch = [pltpu.VMEM((CH, atoms), F32), pltpu.VMEM((CH, atoms), F32)]
     first, own_pos, meta, pick = call(cells_kernel, "cells", out_shape, scratch, args)
     out_shape = (struct(atoms, GROUP_COLS[1], dtype=BF16),)
@@ -706,8 +706,8 @@
 
 
 def third_kernel(
-    p0, p1, p2, own_ref, meta_ref, mix_ref, out_ref, nw_ref, oh_gh, d_gh, dt_gh, gate_gh, acc_own,
-    radt_ref, rbft_ref, gs0_ref, en_0, en_a, new_0, new_a, pre_gh, unit_gh,
+    p0, p1, p2, p3, p4, own_ref, meta_ref, mix_ref, out_ref, nw_ref, oh_gh, d_gh, dt_gh, gate_gh,
+    acc_own, radt_ref, rbft_ref, gs0_ref, en_0, en_a, new_0, new_a, pre_gh, unit_gh,
     m0_ref, nf0_ref, dot_a, *refs
 ):
     group = 1
@@ -717,7 +717,7 @@
     new_ref, energy_ref, src_ref, onto_ref, flow_ref, fmid_ref, fhigh_ref, gs_ref = refs[:8]
     table, sems, wm, wmt, wo, wot, nf_s, mx_s, acc_s, dot_c, en_s, fgh_s = refs[8:20]
     grads = dict(zip(degrees, refs[20:]))
-    copies = fetch((p0, p1, p2), slice(0, GROUP_COLS[group]), table, sems)
+    copies = fetch((p0, p1, p2, p3, p4), slice(0, GROUP_COLS[group]), table, sems)
     atoms = own_ref.shape[0]
     spacing = spacing_of(atoms, rbft_ref.shape[1])
     block_diagonal(KINDS[group], mix_ref, wm, wmt)
@@ -915,9 +915,9 @@
     norm_weight,
 ):
     feats = features[0, 0, 0]
-    lists = (neighbours[0, 0, 0].T, counts[0, 0], cell_atoms[0, 0])
-    lists = jnp.concatenate([*(part.astype(F32) for part in lists), positions[0, 0, 0]], axis=0)
-    cells0, cells1, own_pos, meta = make_cells(feats, lists)
+    places = jnp.swapaxes(positions[0, 0], 0, 1)
+    lists = jnp.concatenate([neighbours[0, 0, 0].T, counts[0, 0], cell_atoms[0, 0]], axis=0)
+    cells0, cells1, own_pos, meta = make_cells(feats, places, lists)
     hold = lax.optimization_barrier
     block0, block1 = (part.reshape(2, 2, 2, 8, part.shape[1]) for part in (cells0, cells1))
     z0 = neighbours_of(block0, "gz", 2)
@@ -929,36 +929,41 @@
     oh_own, pre_own, unit_own, radt, rbft, home, *radial_own = own_stage(
         meta, own_pos, rbf_weight, radial_weight
     )
-    y0, z1, y1_in, oh_own = hold((y0, z1, y1_in, oh_own))
+    z1, y1_in, oh_own = hold((z1, y1_in, oh_own))
+    block1 = jnp.concatenate([z1[0], block1, z1[1]], axis=2)
+    x1_in = neighbours_of(block1, "gx", 0)
+    y0, z1, oh_own = hold((y0, z1, oh_own))
     middle = jnp.concatenate([y0[0], block0, y0[1]], axis=1)
     x0 = neighbours_of(middle, "gx", 0)
     y1_out = neighbours_of(jnp.concatenate(z1, axis=2), "gy", 1)
+    x1_in, oh_own = hold((x1_in, oh_own))
     (m0_own, gate_own, nf0_own, acc0), (own_a,) = own_forward_stage(
         (0,), feats, mix_weight, oh_own, radial_own
     )
-    x0, y1_out, acc0 = hold((x0, y1_out, acc0))
+    _, (own_b,) = own_forward_stage((1,), feats, mix_weight, oh_own, radial_own, gate_own)
+    x0, y1_out, acc0, acc_b = hold((x0, y1_out, acc0, own_b[2]))
     pieces0 = tuple(flat_rows(piece) for piece in (x0[0], middle, x0[1]))
-    low, high = [
+    y1 = [
         jnp.concatenate([out[:, :, 0:1], inner, out[:, :, 1:2]], axis=2)
         for out, inner in zip(y1_out, y1_in)
     ]
-    block1 = jnp.concatenate([z1[0], block1, z1[1]], axis=2)
-    block1 = jnp.concatenate([low, block1, high], axis=1)
-    low, high = neighbours_of(block1, "gx", 0)
-    pieces1 = tuple(flat_rows(piece) for piece in (low, block1, high))
+    outer = jnp.concatenate(y1, axis=1)
+    x1_out = neighbours_of(outer, "gx", 0)
+    block1 = jnp.concatenate([y1[0], block1, y1[1]], axis=1)
+    pieces1 = (x1_in[0], x1_out[0], block1, x1_in[1], x1_out[1])
+    pieces1 = tuple(flat_rows(piece) for piece in pieces1)
     (
         new_0, oh_gh, d_gh, dt_gh, pre_gh, unit_gh, gs0, en_0, m0_gh, gate_gh, nf0_gh, *radial_gh,
     ) = start_stage(
         pieces0, feats, own_pos, meta, rbf_weight, radial_weight, mix_weight, out_weight,
         energy_weight[None], acc0,
     )
-    _, (own_b,) = own_forward_stage((1,), feats, mix_weight, oh_own, radial_own, gate_own)
     shared = (feats, meta, mix_weight, out_weight, norm_weight, oh_gh, d_gh, dt_gh, gate_gh)
     new_a, en_a, _, (dot_gh_a, *gr_gh_a), (dot_own_a, *gr_own_a) = pairs_stage(
         0, 2 * CH, pieces0, shared, (gate_own, *own_a), radial_gh
     )
     new, energy, src, onto, low, mid, high, gs_b = third_stage(
-        pieces1, *shared, own_b[2], radt, rbft, gs0, en_0, en_a, new_0, new_a, pre_gh,
+        pieces1, *shared, acc_b, radt, rbft, gs0, en_0, en_a, new_0, new_a, pre_gh,
         unit_gh, m0_gh, nf0_gh, dot_gh_a, *gr_gh_a,
         *[radial_gh[degree - 1] for degree in DEGREES[1]],
     )

time: 69.7 us -> 68.1 us (0.977)
  waiting for transfers between devices: 8.43 us -> 4.84 us
  starting transfers between devices: 26.2 us -> 27.9 us
  Pallas kernels: 28.4 us -> 29.2 us
    ppermute x5 -> x6, waiting for transfers between devices: 4.9 us -> 1.01 us  [neighbours_of(): lax.ppermute(lax.slice_in_dim(block, length - 1, length, axis=dim), axis,...]
    convert_element_type x2 -> x0, other arithmetic: 1.39 us -> none  [local(): part.astype(F32)]
    ppermute x5 -> x6, starting transfers between devices: 10.3 us -> 11.7 us  [neighbours_of(): after = lax.ppermute(lax.slice_in_dim(block, 0, 1, axis=dim), axis, down)]
    concatenate x2 -> x4, other arithmetic: 0.14 us -> 1.02 us  [the longest x1 0.76 us: local(): jnp.concatenate([neighbours[0, 0, 0].T, counts[0, 0], cell_atoms[0, 0]],...]
    pallas_call x13, Pallas kernels: 28.4 us -> 29.2 us  [call(): pl.pallas_call(kernel, out_shape=out_shape, in_specs=specs or [pl.BlockSp...]
    ppermute x5 -> x6, waiting for transfers between devices: 2.32 us -> 2.66 us  [neighbours_of(): after = lax.ppermute(lax.slice_in_dim(block, 0, 1, axis=dim), axis, down)]
    unnamed x22 -> x23, local copies, waits for them, and re-layouts: 3.54 us -> 3.55 us
    ppermute x5 -> x6, starting transfers between devices: 5.58 us -> 5.58 us  [neighbours_of(): lax.ppermute(lax.slice_in_dim(block, length - 1, length, axis=dim), axis,...]
  transfers between devices with their start and end apart: 17 -> 19, of which waited for: 8 -> 7; matrix products, arithmetic and copies ran while one was open for 0% -> 1% of each run, Pallas kernels for 29% -> 30%
where the time goes in v13:
time: 68.1 us; the launch traced here: 67.8 us
  Pallas kernels  29.2 us (43%)
  starting transfers between devices  27.9 us (41%)
  waiting for transfers between devices  4.84 us (7%)
  local copies, waits for them, and re-layouts  3.8 us (6%)
  other arithmetic  1.16 us (2%)
  between operations  1.01 us (1%)
    pallas_call x13, Pallas kernels, call(): pl.pallas_call(kernel, out_shape=out_shape, in_specs=specs or [pl.BlockSp...  29.2 us
    ppermute x6, starting transfers between devices, neighbours_of(): after = lax.ppermute(lax.slice_in_dim(block, 0, 1, axis=dim), axis, down)  11.7 us
    ppermute x6, starting transfers between devices, neighbours_of(): lax.ppermute(lax.slice_in_dim(block, length - 1, length, axis=dim), axis,...  5.58 us
    ppermute x2, starting transfers between devices, give_back_y(): return (mid, lax.ppermute(mid, 'gy', up), lax.ppermute(mid, 'gy', down))  3.87 us
    unnamed x23, local copies, waits for them, and re-layouts  3.55 us
    ppermute x2, starting transfers between devices, neighbours_of(): other = lax.ppermute(block, axis, up)  3.11 us
    ppermute x6, waiting for transfers between devices, neighbours_of(): after = lax.ppermute(lax.slice_in_dim(block, 0, 1, axis=dim), axis, down)  2.66 us
    ppermute x1, starting transfers between devices, give_back_x(): from_high = lax.ppermute(low, 'gx', down)  1.53 us
  transfers between devices with their start and end apart: 19, of which 7 were waited for; matrix products, arithmetic and copies ran while one was open for 1% of the time, Pallas kernels for 30%

profile of v13, /device:TPU:0, one launch (start us, length us, event | category | flops | bytes accessed | tf_op | source)
XLA Modules:
  0.0 67.8 jit_solution(13782152291903415641)
XLA Ops:
  1.4 1.0 %copy-done = bf16[1,1,1,64,3200]{4,3,2,1,0:T(8,128)(2,1)S(1)} copy-done((bf16[1,1,1,64,3200]{4,3,2,1,0:T(8,128)(2,1)S(1)}, bf16[1,1,1,64,3200]{4,3,2,1,0:T(8,128)(2,1)}, u32[]{:S(2)}) %copy-start) | copy-done | bytes 409624
  3.4 3.0 %collective-permute-start.3 = (bf16[2,2,2,8,1280]{4,3,2,1,0:T(8,128)(2,1)S(1)}, bf16[2,2,2,8,1280]{4,3,2,1,0:T(8,128)(2,1)S(1)}, u32[]{:S(2)}, u32[]{:S(2)}) collective-permute-start(bf16[2,2,2,8,1280]{4,3,2,1,0:T(8,128)(2,1)S(1)} %bitcast.41), channel_id=1, source_target_pairs={{0,1},{1,0},{2,3},{3,2},{4,5},{5,4},{6,7},{7,6},{8,9},{9,8},{10,11... | collective-permute-start | bytes 491528 | tf_op jit(solution)/shard_map/ppermute | solution.py:836
  6.8 2.1 %collective-permute-start.1 = (bf16[2,1,2,8,2048]{4,3,2,1,0:T(8,128)(2,1)S(1)}, bf16[2,1,2,8,2048]{4,3,2,1,0:T(8,128)(2,1)S(1)}, u32[]{:S(2)}, u32[]{:S(2)}) collective-permute-start(bf16[2,1,2,8,2048]{4,3,2,1,0:T(8,128)(2,1)S(1)} %get-tuple-element.201), channel_id=1, source_target_pairs={{0,2},{2,4},{4,6},{6,0},{1,3},{3,5},{5,7},{7,1},{8,10},{10,12},{12... | collective-permute-start | bytes 393224 | tf_op jit(solution)/shard_map/ppermute | solution.py:841
  8.9 2.1 %collective-permute-start.2 = (bf16[2,1,2,8,2048]{4,3,2,1,0:T(8,128)(2,1)S(1)}, bf16[2,1,2,8,2048]{4,3,2,1,0:T(8,128)(2,1)S(1)}, u32[]{:S(2)}, u32[]{:S(2)}) collective-permute-start(bf16[2,1,2,8,2048]{4,3,2,1,0:T(8,128)(2,1)S(1)} %get-tuple-element.200), channel_id=1, source_target_pairs={{2,0},{4,2},{6,4},{0,6},{3,1},{5,3},{7,5},{1,7},{10,8},{12,10},{14... | collective-permute-start | bytes 393224 | tf_op jit(solution)/shard_map/ppermute | solution.py:842
  11.6 2.2 %collective-permute-start.6 = (bf16[2,1,4,8,1280]{4,3,2,1,0:T(8,128)(2,1)S(1)}, bf16[2,1,4,8,1280]{4,3,2,1,0:T(8,128)(2,1)S(1)}, u32[]{:S(2)}, u32[]{:S(2)}) collective-permute-start(bf16[2,1,4,8,1280]{4,3,2,1,0:T(8,128)(2,1)S(1)} %get-tuple-element.197), channel_id=1, source_target_pairs={{0,2},{2,4},{4,6},{6,0},{1,3},{3,5},{5,7},{7,1},{8,10},{10,12},{12... | collective-permute-start | bytes 491528 | tf_op jit(solution)/shard_map/ppermute | solution.py:841
  13.7 2.1 %collective-permute-start.7 = (bf16[2,1,4,8,1280]{4,3,2,1,0:T(8,128)(2,1)S(1)}, bf16[2,1,4,8,1280]{4,3,2,1,0:T(8,128)(2,1)S(1)}, u32[]{:S(2)}, u32[]{:S(2)}) collective-permute-start(bf16[2,1,4,8,1280]{4,3,2,1,0:T(8,128)(2,1)S(1)} %get-tuple-element.196), channel_id=1, source_target_pairs={{2,0},{4,2},{6,4},{0,6},{3,1},{5,3},{7,5},{1,7},{10,8},{12,10},{14... | collective-permute-start | bytes 491528 | tf_op jit(solution)/shard_map/ppermute | solution.py:842
  17.6 2.9 %own_edges.1 = (bf16[1024,64]{1,0:T(8,128)(2,1)S(1)}, bf16[1024,128]{1,0:T(8,128)(2,1)S(1)}, f32[1024,128]{1,0:T(8,128)S(1)}, bf16[640,128]{1,0:T(8,128)(2,1)S(1...) custom-call(f32[64,128]{1,0:T(8,128)S(1)} %get-tuple-element.99.meta, ...), custom_call_target="tpu_custom_call" | custom-call | flops 1024 | bytes 1024 | tf_op jit(solution)/shard_map/own_edges/pallas_call | solution.py:57
  20.8 1.7 %collective-permute-start.5 = (bf16[1,2,4,8,2048]{4,3,2,1,0:T(8,128)(2,1)S(1)}, bf16[1,2,4,8,2048]{4,3,2,1,0:T(8,128)(2,1)S(1)}, u32[]{:S(2)}, u32[]{:S(2)}) collective-permute-start(bf16[1,2,4,8,2048]{4,3,2,1,0:T(8,128)(2,1)S(1)} %get-tuple-element.194), channel_id=1, source_target_pairs={{8,0},{16,8},{24,16},{0,24},{9,1},{17,9},{25,17},{1,25},{10,2},{18... | collective-permute-start | bytes 786440 | tf_op jit(solution)/shard_map/ppermute | solution.py:842
  23.4 1.7 %collective-permute-start.9 = (bf16[1,4,4,8,1280]{4,3,2,1,0:T(8,128)(2,1)S(1)}, bf16[1,4,4,8,1280]{4,3,2,1,0:T(8,128)(2,1)S(1)}, u32[]{:S(2)}, u32[]{:S(2)}) collective-permute-start(bf16[1,4,4,8,1280]{4,3,2,1,0:T(8,128)(2,1)S(1)} %get-tuple-element.190), channel_id=1, source_target_pairs={{8,0},{16,8},{24,16},{0,24},{9,1},{17,9},{25,17},{1,25},{10,2},{18... | collective-permute-start | bytes 983048 | tf_op jit(solution)/shard_map/ppermute | solution.py:842
  25.2 1.2 %collective-permute-start.10 = (bf16[2,1,2,8,2048]{4,3,2,1,0:T(8,128)(2,1)S(1)}, bf16[2,1,2,8,2048]{4,3,2,1,0:T(8,128)(2,1)S(1)}, u32[]{:S(2)}, u32[]{:S(2)}) collective-permute-start(bf16[2,1,2,8,2048]{4,3,2,1,0:T(8,128)(2,1)S(1)} %get-tuple-element.199), channel_id=1, source_target_pairs={{0,2},{2,4},{4,6},{6,0},{1,3},{3,5},{5,7},{7,1},{8,10},{10,12},{12... | collective-permute-start | bytes 393224 | tf_op jit(solution)/shard_map/ppermute | solution.py:841
  27.4 2.1 %collective-permute-start.11 = (bf16[2,1,2,8,2048]{4,3,2,1,0:T(8,128)(2,1)S(1)}, bf16[2,1,2,8,2048]{4,3,2,1,0:T(8,128)(2,1)S(1)}, u32[]{:S(2)}, u32[]{:S(2)}) collective-permute-start(bf16[2,1,2,8,2048]{4,3,2,1,0:T(8,128)(2,1)S(1)} %get-tuple-element.198), channel_id=1, source_target_pairs={{2,0},{4,2},{6,4},{0,6},{3,1},{5,3},{7,5},{1,7},{10,8},{12,10},{14... | collective-permute-start | bytes 393224 | tf_op jit(solution)/shard_map/ppermute | solution.py:842
  29.5 1.5 %own_forward_a.1 = (bf16[1024,128]{1,0:T(8,128)(2,1)S(1)}, bf16[1024,128]{1,0:T(8,128)(2,1)S(1)}, bf16[1024,128]{1,0:T(8,128)(2,1)S(1)}, f32[64,128]{1,0:T(8,128...) custom-call(bf16[64,3200]{1,0:T(8,128)(2,1)S(1)} %bitcast.25, ...), custom_call_target="tpu_custom_call" | custom-call | flops 1024 | bytes 1024 | tf_op jit(solution)/shard_map/own_forward_a/pallas_call | solution.py:57
  31.0 2.5 %own_forward_b.1 = (bf16[1024,2048]{1,0:T(8,128)(2,1)S(1)}, bf16[1024,2048]{1,0:T(8,128)(2,1)S(1)}, f32[64,2048]{1,0:T(8,128)S(1)}) custom-call(bf16[64,3200]{1,0:T(8,128)(2,1)S(1)} %bitcast.26, bf16[5,128,128]{2,1,0:T(8,128)(2,1)S(1)} %copy-done.2, bf16[1024,64]{1,0:T(8,128)(2,1)S(1)} %get-tuple-element.113.refs_2_.oh_own, ...), custom_call_target="tpu_custom_call" | custom-call | flops 1024 | bytes 1024 | tf_op jit(solution)/shard_map/own_forward_b/pallas_call | solution.py:57
  33.5 1.7 %collective-permute-done.11 = bf16[2,1,2,8,2048]{4,3,2,1,0:T(8,128)(2,1)S(1)} collective-permute-done((bf16[2,1,2,8,2048]{4,3,2,1,0:T(8,128)(2,1)S(1)}, bf16[2,1,2,8,2048]{4,3,2,1,0:T(8,128)(2,1)S(1)}, u32[]{:S(2)}, u32[]{:S(2)}) %collective-permute-start.11) | collective-permute-done | bytes 131104 | tf_op jit(solution)/shard_map/ppermute | solution.py:842
  35.7 2.0 %collective-permute-start.13 = (bf16[1,2,4,8,2048]{4,3,2,1,0:T(8,128)(2,1)S(1)}, bf16[1,2,4,8,2048]{4,3,2,1,0:T(8,128)(2,1)S(1)}, u32[]{:S(2)}, u32[]{:S(2)}) collective-permute-start(bf16[1,2,4,8,2048]{4,3,2,1,0:T(8,128)(2,1)S(1)} %get-tuple-element.192), channel_id=1, source_target_pairs={{8,0},{16,8},{24,16},{0,24},{9,1},{17,9},{25,17},{1,25},{10,2},{18... | collective-permute-start | bytes 786440 | tf_op jit(solution)/shard_map/ppermute | solution.py:842
  37.7 3.6 %ghost_start.1 = (bf16[64,128]{1,0:T(8,128)(2,1)S(1)}, bf16[1024,512]{1,0:T(8,128)(2,1)S(1)}, bf16[1024,64]{1,0:T(8,128)(2,1)S(1)}, bf16[64,1024]{1,0:T(8,128)(2...) custom-call(bf16[128,1280]{1,0:T(8,128)(2,1)S(1)} %bitcast.37, ...), custom_call_target="tpu_custom_call" | custom-call | flops 1024 | bytes 1024 | tf_op jit(solution)/shard_map/ghost_start/pallas_call | solution.py:57
  41.2 4.4 %pairs_a.1 = (bf16[64,1024]{1,0:T(8,128)(2,1)S(1)}, f32[64,128]{1,0:T(8,128)S(1)}, bf16[64,1024]{1,0:T(8,128)(2,1)}, bf16[1024,128]{1,0:T(8,128)(2,1)S(1)}, bf16...) custom-call(bf16[128,1280]{1,0:T(8,128)(2,1)S(1)} %bitcast.38, ...), custom_call_target="tpu_custom_call" | custom-call | flops 1024 | bytes 1024 | tf_op jit(solution)/shard_map/pairs_a/pallas_call | solution.py:57
  45.8 7.7 %third_group.1 = (bf16[64,3200]{1,0:T(8,128)(2,1)}, f32[1,64]{1,0:T(1,128)}, f32[64,128]{1,0:T(8,128)S(1)}, f32[8,64]{1,0:T(8,128)S(1)}, f32[8,128]{1,0:T(8,128)...) custom-call(bf16[64,2048]{1,0:T(8,128)(2,1)S(1)} %bitcast.44, ...), custom_call_target="tpu_custom_call" | custom-call | flops 1024 | bytes 1024 | tf_op jit(solution)/shard_map/third_group/pallas_call | solution.py:57
  54.1 1.5 %collective-permute-start.15 = (f32[8,128]{1,0:T(8,128)S(1)}, f32[8,128]{1,0:T(8,128)S(1)}, u32[]{:S(2)}, u32[]{:S(2)}) collective-permute-start(f32[8,128]{1,0:T(8,128)S(1)} %get-tuple-element.160), channel_id=1, source_target_pairs={{8,0},{16,8},{24,16},{0,24},{9,1},{17,9},{25,17},{1,25},{10,2},{18... | collective-permute-start | bytes 12296 | tf_op jit(solution)/shard_map/ppermute | solution.py:885
  55.6 2.2 %own_backward_b.1 = (bf16[1024,128]{1,0:T(8,128)(2,1)S(1)}, bf16[1024,128]{1,0:T(8,128)(2,1)S(1)}, bf16[1024,128]{1,0:T(8,128)(2,1)S(1)}) custom-call(bf16[5,128,128]{2,1,0:T(8,128)(2,1)S(1)} %copy-done.2, bf16[64,2048]{1,0:T(8,128)(2,1)S(1)} %get-tuple-element.161.gs_ref, bf16[1024,128]{1,0:T(8,128)(2,1)S(1)} %get-tuple-element.120.refs_8_.refs_12_.gate_ref, ...), custom_call_target="tpu_custom_call" | custom-call | flops 1024 | bytes 1024 | tf_op jit(solution)/shard_map/own_backward_b/pallas_call | solution.py:57
  57.9 3.8 %collective-permute-start.17 = (f32[8,256]{1,0:T(8,128)S(1)}, f32[8,256]{1,0:T(8,128)S(1)}, u32[]{:S(2)}, u32[]{:S(2)}) collective-permute-start(f32[8,256]{1,0:T(8,128)S(1)} %add.3.mid_ref), channel_id=1, source_target_pairs={{2,0},{4,2},{6,4},{0,6},{3,1},{5,3},{7,5},{1,7},{10,8},{12,10},{14... | collective-permute-start | bytes 24584 | tf_op jit(solution)/shard_map/ppermute | solution.py:891
  61.7 1.5 %own_back.2 = (f32[64,128]{1,0:T(8,128)S(1)}, f32[8,64]{1,0:T(8,128)S(1)}) custom-call(bf16[1024,64]{1,0:T(8,128)(2,1)S(1)} %get-tuple-element.113.refs_2_.oh_own, bf16[1024,128]{1,0:T(8,128)(2,1)S(1)} %get-tuple-element.166.pre_own, f32[1024,128]{1,0:T(8,128)S(1)} %get-tuple-element.167.unit_own, bf16[640,128]{1,0:T(8,128)(2,1)S(1)} %get-tuple-element.135.radt_ref, ...), custom_call_target="tpu_custom_call" | custom-call | flops 1024 | bytes 1024 | tf_op jit(solution)/shard_map/own_back/pallas_call | solution.py:57
  63.4 1.5 %collective-permute-start.18 = (f32[8,256]{1,0:T(8,128)S(1)}, f32[8,256]{1,0:T(8,128)S(1)}, u32[]{:S(2)}, u32[]{:S(2)}) collective-permute-start(f32[8,256]{1,0:T(8,128)S(1)} %fold.1.mid_ref), channel_id=1, source_target_pairs={{0,1},{1,0},{2,3},{3,2},{4,5},{5,4},{6,7},{7,6},{8,9},{9,8},{10,11... | collective-permute-start | bytes 24584 | tf_op jit(solution)/shard_map/ppermute | solution.py:900
  64.9 1.5 %own_back.3 = (f32[64,128]{1,0:T(8,128)S(1)}, f32[8,64]{1,0:T(8,128)S(1)}) custom-call(bf16[1024,64]{1,0:T(8,128)(2,1)S(1)} %get-tuple-element.113.refs_2_.oh_own, bf16[1024,128]{1,0:T(8,128)(2,1)S(1)} %get-tuple-element.166.pre_own, f32[1024,128]{1,0:T(8,128)S(1)} %get-tuple-element.167.unit_own, bf16[640,128]{1,0:T(8,128)(2,1)S(1)} %get-tuple-element.135.radt_ref, ...), custom_call_target="tpu_custom_call" | custom-call | flops 1024 | bytes 1024 | tf_op jit(solution)/shard_map/own_back/pallas_call | solution.py:57
  (68 shorter events, 9.3 us)
Async XLA Ops:
  3.4 8.1 %collective-permute-start.3 = (bf16[2,2,2,8,1280]{4,3,2,1,0:T(8,128)(2,1)S(1)}, bf16[2,2,2,8,1280]{4,3,2,1,0:T(8,128)(2,1)S(1)}, u32[]{:S(2)}, u32[]{:S(2)}) collective-permute-start(bf16[2,2,2,8,1280]{4,3,2,1,0:T(8,128)(2,1)S(1)} %bitcast.41), channel_id=1, source_target_pairs={{0,1},{1,0},{2,3},{3,2},{4,5},{5,4},{6,7},{7,6},{8,9},{9,8},{10,11... | collective-permute-start | bytes 491528 | tf_op jit(solution)/shard_map/ppermute | solution.py:836
  6.6 13.9 %collective-permute-start = (bf16[2,2,2,8,2048]{4,3,2,1,0:T(8,128)(2,1)S(1)}, bf16[2,2,2,8,2048]{4,3,2,1,0:T(8,128)(2,1)S(1)}, u32[]{:S(2)}, u32[]{:S(2)}) collective-permute-start(bf16[2,2,2,8,2048]{4,3,2,1,0:T(8,128)(2,1)S(1)} %bitcast.33), channel_id=1, source_target_pairs={{0,1},{1,0},{2,3},{3,2},{4,5},{5,4},{6,7},{7,6},{8,9},{9,8},{10,11... | collective-permute-start | bytes 786440 | tf_op jit(solution)/shard_map/ppermute | solution.py:836
  6.8 22.7 %copy-start.1 = (bf16[1,1,1,64,3200]{4,3,2,1,0:T(8,128)(2,1)S(1)}, bf16[1,1,1,64,3200]{4,3,2,1,0:T(8,128)(2,1)}, u32[]{:S(2)}) copy-start(bf16[1,1,1,64,3200]{4,3,2,1,0:T(8,128)(2,1)} %param.11) | copy-start | bytes 1228804
  6.8 22.7 %copy-start.2 = (bf16[5,128,128]{2,1,0:T(8,128)(2,1)S(1)}, bf16[5,128,128]{2,1,0:T(8,128)(2,1)}, u32[]{:S(2)}) copy-start(bf16[5,128,128]{2,1,0:T(8,128)(2,1)} %mix_ref.9) | copy-start | bytes 491524
  6.8 13.8 %collective-permute-start.1 = (bf16[2,1,2,8,2048]{4,3,2,1,0:T(8,128)(2,1)S(1)}, bf16[2,1,2,8,2048]{4,3,2,1,0:T(8,128)(2,1)S(1)}, u32[]{:S(2)}, u32[]{:S(2)}) collective-permute-start(bf16[2,1,2,8,2048]{4,3,2,1,0:T(8,128)(2,1)S(1)} %get-tuple-element.201), channel_id=1, source_target_pairs={{0,2},{2,4},{4,6},{6,0},{1,3},{3,5},{5,7},{7,1},{8,10},{10,12},{12... | collective-permute-start | bytes 393224 | tf_op jit(solution)/shard_map/ppermute | solution.py:841
  8.9 11.7 %collective-permute-start.2 = (bf16[2,1,2,8,2048]{4,3,2,1,0:T(8,128)(2,1)S(1)}, bf16[2,1,2,8,2048]{4,3,2,1,0:T(8,128)(2,1)S(1)}, u32[]{:S(2)}, u32[]{:S(2)}) collective-permute-start(bf16[2,1,2,8,2048]{4,3,2,1,0:T(8,128)(2,1)S(1)} %get-tuple-element.200), channel_id=1, source_target_pairs={{2,0},{4,2},{6,4},{0,6},{3,1},{5,3},{7,5},{1,7},{10,8},{12,10},{14... | collective-permute-start | bytes 393224 | tf_op jit(solution)/shard_map/ppermute | solution.py:842
  11.6 10.9 %collective-permute-start.6 = (bf16[2,1,4,8,1280]{4,3,2,1,0:T(8,128)(2,1)S(1)}, bf16[2,1,4,8,1280]{4,3,2,1,0:T(8,128)(2,1)S(1)}, u32[]{:S(2)}, u32[]{:S(2)}) collective-permute-start(bf16[2,1,4,8,1280]{4,3,2,1,0:T(8,128)(2,1)S(1)} %get-tuple-element.197), channel_id=1, source_target_pairs={{0,2},{2,4},{4,6},{6,0},{1,3},{3,5},{5,7},{7,1},{8,10},{10,12},{12... | collective-permute-start | bytes 491528 | tf_op jit(solution)/shard_map/ppermute | solution.py:841
  13.7 9.4 %collective-permute-start.7 = (bf16[2,1,4,8,1280]{4,3,2,1,0:T(8,128)(2,1)S(1)}, bf16[2,1,4,8,1280]{4,3,2,1,0:T(8,128)(2,1)S(1)}, u32[]{:S(2)}, u32[]{:S(2)}) collective-permute-start(bf16[2,1,4,8,1280]{4,3,2,1,0:T(8,128)(2,1)S(1)} %get-tuple-element.196), channel_id=1, source_target_pairs={{2,0},{4,2},{6,4},{0,6},{3,1},{5,3},{7,5},{1,7},{10,8},{12,10},{14... | collective-permute-start | bytes 491528 | tf_op jit(solution)/shard_map/ppermute | solution.py:842
  20.7 6.7 %collective-permute-start.4 = (bf16[1,2,4,8,2048]{4,3,2,1,0:T(8,128)(2,1)S(1)}, bf16[1,2,4,8,2048]{4,3,2,1,0:T(8,128)(2,1)S(1)}, u32[]{:S(2)}, u32[]{:S(2)}) collective-permute-start(bf16[1,2,4,8,2048]{4,3,2,1,0:T(8,128)(2,1)S(1)} %get-tuple-element.195), channel_id=1, source_target_pairs={{0,8},{8,16},{16,24},{24,0},{1,9},{9,17},{17,25},{25,1},{2,10},{10... | collective-permute-start | bytes 786440 | tf_op jit(solution)/shard_map/ppermute | solution.py:841
  20.8 8.7 %collective-permute-start.5 = (bf16[1,2,4,8,2048]{4,3,2,1,0:T(8,128)(2,1)S(1)}, bf16[1,2,4,8,2048]{4,3,2,1,0:T(8,128)(2,1)S(1)}, u32[]{:S(2)}, u32[]{:S(2)}) collective-permute-start(bf16[1,2,4,8,2048]{4,3,2,1,0:T(8,128)(2,1)S(1)} %get-tuple-element.194), channel_id=1, source_target_pairs={{8,0},{16,8},{24,16},{0,24},{9,1},{17,9},{25,17},{1,25},{10,2},{18... | collective-permute-start | bytes 786440 | tf_op jit(solution)/shard_map/ppermute | solution.py:842
  23.3 14.3 %copy-start.3 = (bf16[5,128,128]{2,1,0:T(8,128)(2,1)S(1)}, bf16[5,128,128]{2,1,0:T(8,128)(2,1)}, u32[]{:S(2)}) copy-start(bf16[5,128,128]{2,1,0:T(8,128)(2,1)} %out_ref.3) | copy-start | bytes 491524
  23.3 14.3 %copy-start.5 = (bf16[128,640]{1,0:T(8,128)(2,1)S(1)}, bf16[128,640]{1,0:T(8,128)(2,1)}, u32[]{:S(2)}) copy-start(bf16[128,640]{1,0:T(8,128)(2,1)} %rad_ref.3) | copy-start | bytes 491524
  23.3 14.3 %copy-start.7 = (bf16[512,128]{1,0:T(8,128)(2,1)S(1)}, bf16[512,128]{1,0:T(8,128)(2,1)}, u32[]{:S(2)}) copy-start(bf16[512,128]{1,0:T(8,128)(2,1)} %rbf_ref.3) | copy-start | bytes 393220
  23.3 11.9 %collective-permute-start.8 = (bf16[1,4,4,8,1280]{4,3,2,1,0:T(8,128)(2,1)S(1)}, bf16[1,4,4,8,1280]{4,3,2,1,0:T(8,128)(2,1)S(1)}, u32[]{:S(2)}, u32[]{:S(2)}) collective-permute-start(bf16[1,4,4,8,1280]{4,3,2,1,0:T(8,128)(2,1)S(1)} %get-tuple-element.191), channel_id=1, source_target_pairs={{0,8},{8,16},{16,24},{24,0},{1,9},{9,17},{17,25},{25,1},{2,10},{10... | collective-permute-start | bytes 983048 | tf_op jit(solution)/shard_map/ppermute | solution.py:841
  23.4 12.1 %collective-permute-start.9 = (bf16[1,4,4,8,1280]{4,3,2,1,0:T(8,128)(2,1)S(1)}, bf16[1,4,4,8,1280]{4,3,2,1,0:T(8,128)(2,1)S(1)}, u32[]{:S(2)}, u32[]{:S(2)}) collective-permute-start(bf16[1,4,4,8,1280]{4,3,2,1,0:T(8,128)(2,1)S(1)} %get-tuple-element.190), channel_id=1, source_target_pairs={{8,0},{16,8},{24,16},{0,24},{9,1},{17,9},{25,17},{1,25},{10,2},{18... | collective-permute-start | bytes 983048 | tf_op jit(solution)/shard_map/ppermute | solution.py:842
  25.2 8.3 %collective-permute-start.10 = (bf16[2,1,2,8,2048]{4,3,2,1,0:T(8,128)(2,1)S(1)}, bf16[2,1,2,8,2048]{4,3,2,1,0:T(8,128)(2,1)S(1)}, u32[]{:S(2)}, u32[]{:S(2)}) collective-permute-start(bf16[2,1,2,8,2048]{4,3,2,1,0:T(8,128)(2,1)S(1)} %get-tuple-element.199), channel_id=1, source_target_pairs={{0,2},{2,4},{4,6},{6,0},{1,3},{3,5},{5,7},{7,1},{8,10},{10,12},{12... | collective-permute-start | bytes 393224 | tf_op jit(solution)/shard_map/ppermute | solution.py:841
  27.4 7.8 %collective-permute-start.11 = (bf16[2,1,2,8,2048]{4,3,2,1,0:T(8,128)(2,1)S(1)}, bf16[2,1,2,8,2048]{4,3,2,1,0:T(8,128)(2,1)S(1)}, u32[]{:S(2)}, u32[]{:S(2)}) collective-permute-start(bf16[2,1,2,8,2048]{4,3,2,1,0:T(8,128)(2,1)S(1)} %get-tuple-element.198), channel_id=1, source_target_pairs={{2,0},{4,2},{6,4},{0,6},{3,1},{5,3},{7,5},{1,7},{10,8},{12,10},{14... | collective-permute-start | bytes 393224 | tf_op jit(solution)/shard_map/ppermute | solution.py:842
  35.7 10.1 %collective-permute-start.13 = (bf16[1,2,4,8,2048]{4,3,2,1,0:T(8,128)(2,1)S(1)}, bf16[1,2,4,8,2048]{4,3,2,1,0:T(8,128)(2,1)S(1)}, u32[]{:S(2)}, u32[]{:S(2)}) collective-permute-start(bf16[1,2,4,8,2048]{4,3,2,1,0:T(8,128)(2,1)S(1)} %get-tuple-element.192), channel_id=1, source_target_pairs={{8,0},{16,8},{24,16},{0,24},{9,1},{17,9},{25,17},{1,25},{10,2},{18... | collective-permute-start | bytes 786440 | tf_op jit(solution)/shard_map/ppermute | solution.py:842
  37.6 8.2 %collective-permute-start.12 = (bf16[1,2,4,8,2048]{4,3,2,1,0:T(8,128)(2,1)S(1)}, bf16[1,2,4,8,2048]{4,3,2,1,0:T(8,128)(2,1)S(1)}, u32[]{:S(2)}, u32[]{:S(2)}) collective-permute-start(bf16[1,2,4,8,2048]{4,3,2,1,0:T(8,128)(2,1)S(1)} %get-tuple-element.193), channel_id=1, source_target_pairs={{0,8},{8,16},{16,24},{24,0},{1,9},{9,17},{17,25},{25,1},{2,10},{10... | collective-permute-start | bytes 786440 | tf_op jit(solution)/shard_map/ppermute | solution.py:841
  53.5 4.2 %collective-permute-start.14 = (f32[8,128]{1,0:T(8,128)S(1)}, f32[8,128]{1,0:T(8,128)S(1)}, u32[]{:S(2)}, u32[]{:S(2)}) collective-permute-start(f32[8,128]{1,0:T(8,128)S(1)} %get-tuple-element.159), channel_id=1, source_target_pairs={{0,8},{8,16},{16,24},{24,0},{1,9},{9,17},{17,25},{25,1},{2,10},{10... | collective-permute-start | bytes 12296 | tf_op jit(solution)/shard_map/ppermute | solution.py:884
  54.1 3.7 %collective-permute-start.15 = (f32[8,128]{1,0:T(8,128)S(1)}, f32[8,128]{1,0:T(8,128)S(1)}, u32[]{:S(2)}, u32[]{:S(2)}) collective-permute-start(f32[8,128]{1,0:T(8,128)S(1)} %get-tuple-element.160), channel_id=1, source_target_pairs={{8,0},{16,8},{24,16},{0,24},{9,1},{17,9},{25,17},{1,25},{10,2},{18... | collective-permute-start | bytes 12296 | tf_op jit(solution)/shard_map/ppermute | solution.py:885
  57.8 5.5 %collective-permute-start.16 = (f32[8,256]{1,0:T(8,128)S(1)}, f32[8,256]{1,0:T(8,128)S(1)}, u32[]{:S(2)}, u32[]{:S(2)}) collective-permute-start(f32[8,256]{1,0:T(8,128)S(1)} %add.3.mid_ref), channel_id=1, source_target_pairs={{0,2},{2,4},{4,6},{6,0},{1,3},{3,5},{5,7},{7,1},{8,10},{10,12},{12... | collective-permute-start | bytes 24584 | tf_op jit(solution)/shard_map/ppermute | solution.py:891
  57.9 5.4 %collective-permute-start.17 = (f32[8,256]{1,0:T(8,128)S(1)}, f32[8,256]{1,0:T(8,128)S(1)}, u32[]{:S(2)}, u32[]{:S(2)}) collective-permute-start(f32[8,256]{1,0:T(8,128)S(1)} %add.3.mid_ref), channel_id=1, source_target_pairs={{2,0},{4,2},{6,4},{0,6},{3,1},{5,3},{7,5},{1,7},{10,8},{12,10},{14... | collective-permute-start | bytes 24584 | tf_op jit(solution)/shard_map/ppermute | solution.py:891
  63.4 3.7 %collective-permute-start.18 = (f32[8,256]{1,0:T(8,128)S(1)}, f32[8,256]{1,0:T(8,128)S(1)}, u32[]{:S(2)}, u32[]{:S(2)}) collective-permute-start(f32[8,256]{1,0:T(8,128)S(1)} %fold.1.mid_ref), channel_id=1, source_target_pairs={{0,1},{1,0},{2,3},{3,2},{4,5},{5,4},{6,7},{7,6},{8,9},{9,8},{10,11... | collective-permute-start | bytes 24584 | tf_op jit(solution)/shard_map/ppermute | solution.py:900
  (6 other events, 28.1 us)

commit v14 on v13

--- a/solution.py
+++ b/solution.py
@@ -23,7 +23,7 @@
     (3, 3), (3, 3), (3, 3), (3, 4),
     (4, 4), (4, 4), (4, 4), (4, 4),
 )
-GROUPS = ((0, 4), (4, 12))
+GROUPS = ((0, 3), (3, 12))
 KINDS = tuple(sorted({PAIR_DEGREES[pair] for pair in range(*group)}) for group in GROUPS)
 DEGREES = tuple(sorted({d for both in kinds for d in both}) for kinds in KINDS)
 GROUP_COLS = tuple(2 * CH * (end - begin) for begin, end in GROUPS)

time: 68.1 us -> 70.6 us (1.037)
  waiting for transfers between devices: 4.84 us -> 9.98 us
  local copies, waits for them, and re-layouts: 3.8 us -> 1.97 us
    ppermute x6, waiting for transfers between devices: 1.01 us -> 6.92 us  [neighbours_of(): lax.ppermute(lax.slice_in_dim(block, length - 1, length, axis=dim), axis,...]
    unnamed x23 -> x19, local copies, waits for them, and re-layouts: 3.55 us -> 1.73 us
  transfers between devices with their start and end apart: 19 -> 19, of which waited for: 7 -> 8; matrix products, arithmetic and copies ran while one was open for 1% -> 1% of each run, Pallas kernels for 30% -> 27%
where the time goes in v14:
time: 70.6 us; the launch traced here: 70.4 us
  Pallas kernels  29 us (41%)
  starting transfers between devices  27.2 us (39%)
  waiting for transfers between devices  9.98 us (14%)
  local copies, waits for them, and re-layouts  1.97 us (3%)
  other arithmetic  1.16 us (2%)
  between operations  0.95 us (1%)
    pallas_call x13, Pallas kernels, call(): pl.pallas_call(kernel, out_shape=out_shape, in_specs=specs or [pl.BlockSp...  29 us
    ppermute x6, starting transfers between devices, neighbours_of(): after = lax.ppermute(lax.slice_in_dim(block, 0, 1, axis=dim), axis, down)  11.6 us
    ppermute x6, waiting for transfers between devices, neighbours_of(): lax.ppermute(lax.slice_in_dim(block, length - 1, length, axis=dim), axis,...  6.92 us
    ppermute x6, starting transfers between devices, neighbours_of(): lax.ppermute(lax.slice_in_dim(block, length - 1, length, axis=dim), axis,...  5.35 us
    ppermute x2, starting transfers between devices, give_back_y(): return (mid, lax.ppermute(mid, 'gy', up), lax.ppermute(mid, 'gy', down))  3.88 us
    ppermute x2, starting transfers between devices, neighbours_of(): other = lax.ppermute(block, axis, up)  3.13 us
    ppermute x6, waiting for transfers between devices, neighbours_of(): after = lax.ppermute(lax.slice_in_dim(block, 0, 1, axis=dim), axis, down)  2.33 us
    ppermute x1, starting transfers between devices, give_back_x(): from_high = lax.ppermute(low, 'gx', down)  1.73 us
  transfers between devices with their start and end apart: 19, of which 8 were waited for; matrix products, arithmetic and copies ran while one was open for 1% of the time, Pallas kernels for 27%

profile of v14, /device:TPU:0, one launch (start us, length us, event | category | flops | bytes accessed | tf_op | source)
XLA Modules:
  0.0 70.4 jit_solution(14137380409804304224)
XLA Ops:
  3.4 3.0 %collective-permute-start.3 = (bf16[2,2,2,8,1024]{4,3,2,1,0:T(8,128)(2,1)S(1)}, bf16[2,2,2,8,1024]{4,3,2,1,0:T(8,128)(2,1)S(1)}, u32[]{:S(2)}, u32[]{:S(2)}) collective-permute-start(bf16[2,2,2,8,1024]{4,3,2,1,0:T(8,128)(2,1)S(1)} %bitcast.41), channel_id=1, source_target_pairs={{0,1},{1,0},{2,3},{3,2},{4,5},{5,4},{6,7},{7,6},{8,9},{9,8},{10,11... | collective-permute-start | bytes 393224 | tf_op jit(solution)/shard_map/ppermute | solution.py:836
  6.8 2.1 %collective-permute-start.1 = (bf16[2,1,2,8,2304]{4,3,2,1,0:T(8,128)(2,1)S(1)}, bf16[2,1,2,8,2304]{4,3,2,1,0:T(8,128)(2,1)S(1)}, u32[]{:S(2)}, u32[]{:S(2)}) collective-permute-start(bf16[2,1,2,8,2304]{4,3,2,1,0:T(8,128)(2,1)S(1)} %get-tuple-element.201), channel_id=1, source_target_pairs={{0,2},{2,4},{4,6},{6,0},{1,3},{3,5},{5,7},{7,1},{8,10},{10,12},{12... | collective-permute-start | bytes 442376 | tf_op jit(solution)/shard_map/ppermute | solution.py:841
  8.9 2.1 %collective-permute-start.2 = (bf16[2,1,2,8,2304]{4,3,2,1,0:T(8,128)(2,1)S(1)}, bf16[2,1,2,8,2304]{4,3,2,1,0:T(8,128)(2,1)S(1)}, u32[]{:S(2)}, u32[]{:S(2)}) collective-permute-start(bf16[2,1,2,8,2304]{4,3,2,1,0:T(8,128)(2,1)S(1)} %get-tuple-element.200), channel_id=1, source_target_pairs={{2,0},{4,2},{6,4},{0,6},{3,1},{5,3},{7,5},{1,7},{10,8},{12,10},{14... | collective-permute-start | bytes 442376 | tf_op jit(solution)/shard_map/ppermute | solution.py:842
  11.1 1.9 %collective-permute-start.6 = (bf16[2,1,4,8,1024]{4,3,2,1,0:T(8,128)(2,1)S(1)}, bf16[2,1,4,8,1024]{4,3,2,1,0:T(8,128)(2,1)S(1)}, u32[]{:S(2)}, u32[]{:S(2)}) collective-permute-start(bf16[2,1,4,8,1024]{4,3,2,1,0:T(8,128)(2,1)S(1)} %get-tuple-element.205), channel_id=1, source_target_pairs={{0,2},{2,4},{4,6},{6,0},{1,3},{3,5},{5,7},{7,1},{8,10},{10,12},{12... | collective-permute-start | bytes 393224 | tf_op jit(solution)/shard_map/ppermute | solution.py:841
  13.0 2.1 %collective-permute-start.7 = (bf16[2,1,4,8,1024]{4,3,2,1,0:T(8,128)(2,1)S(1)}, bf16[2,1,4,8,1024]{4,3,2,1,0:T(8,128)(2,1)S(1)}, u32[]{:S(2)}, u32[]{:S(2)}) collective-permute-start(bf16[2,1,4,8,1024]{4,3,2,1,0:T(8,128)(2,1)S(1)} %get-tuple-element.204), channel_id=1, source_target_pairs={{2,0},{4,2},{6,4},{0,6},{3,1},{5,3},{7,5},{1,7},{10,8},{12,10},{14... | collective-permute-start | bytes 393224 | tf_op jit(solution)/shard_map/ppermute | solution.py:842
  15.1 2.9 %own_edges.1 = (bf16[1024,64]{1,0:T(8,128)(2,1)S(1)}, bf16[1024,128]{1,0:T(8,128)(2,1)S(1)}, f32[1024,128]{1,0:T(8,128)S(1)}, bf16[640,128]{1,0:T(8,128)(2,1)S(1...) custom-call(f32[64,128]{1,0:T(8,128)S(1)} %get-tuple-element.100.met, ...), custom_call_target="tpu_custom_call" | custom-call | flops 1024 | bytes 1024 | tf_op jit(solution)/shard_map/own_edges/pallas_call | solution.py:57
  19.2 2.4 %collective-permute-done.6 = bf16[2,1,4,8,1024]{4,3,2,1,0:T(8,128)(2,1)S(1)} collective-permute-done((bf16[2,1,4,8,1024]{4,3,2,1,0:T(8,128)(2,1)S(1)}, bf16[2,1,4,8,1024]{4,3,2,1,0:T(8,128)(2,1)S(1)}, u32[]{:S(2)}, u32[]{:S(2)}) %collective-permute-start.6) | collective-permute-done | bytes 131104 | tf_op jit(solution)/shard_map/ppermute | solution.py:841
  22.5 1.7 %collective-permute-start.5 = (bf16[1,2,4,8,2304]{4,3,2,1,0:T(8,128)(2,1)S(1)}, bf16[1,2,4,8,2304]{4,3,2,1,0:T(8,128)(2,1)S(1)}, u32[]{:S(2)}, u32[]{:S(2)}) collective-permute-start(bf16[1,2,4,8,2304]{4,3,2,1,0:T(8,128)(2,1)S(1)} %get-tuple-element.194), channel_id=1, source_target_pairs={{8,0},{16,8},{24,16},{0,24},{9,1},{17,9},{25,17},{1,25},{10,2},{18... | collective-permute-start | bytes 884744 | tf_op jit(solution)/shard_map/ppermute | solution.py:842
  24.5 1.7 %collective-permute-start.9 = (bf16[1,4,4,8,1024]{4,3,2,1,0:T(8,128)(2,1)S(1)}, bf16[1,4,4,8,1024]{4,3,2,1,0:T(8,128)(2,1)S(1)}, u32[]{:S(2)}, u32[]{:S(2)}) collective-permute-start(bf16[1,4,4,8,1024]{4,3,2,1,0:T(8,128)(2,1)S(1)} %get-tuple-element.196), channel_id=1, source_target_pairs={{8,0},{16,8},{24,16},{0,24},{9,1},{17,9},{25,17},{1,25},{10,2},{18... | collective-permute-start | bytes 786440 | tf_op jit(solution)/shard_map/ppermute | solution.py:842
  27.4 2.5 %collective-permute-done.4 = bf16[1,2,4,8,2304]{4,3,2,1,0:T(8,128)(2,1)S(1)} collective-permute-done((bf16[1,2,4,8,2304]{4,3,2,1,0:T(8,128)(2,1)S(1)}, bf16[1,2,4,8,2304]{4,3,2,1,0:T(8,128)(2,1)S(1)}, u32[]{:S(2)}, u32[]{:S(2)}) %collective-permute-start.4) | collective-permute-done | bytes 294944 | tf_op jit(solution)/shard_map/ppermute | solution.py:841
  30.0 2.4 %collective-permute-start.11 = (bf16[2,1,2,8,2304]{4,3,2,1,0:T(8,128)(2,1)S(1)}, bf16[2,1,2,8,2304]{4,3,2,1,0:T(8,128)(2,1)S(1)}, u32[]{:S(2)}, u32[]{:S(2)}) collective-permute-start(bf16[2,1,2,8,2304]{4,3,2,1,0:T(8,128)(2,1)S(1)} %get-tuple-element.198), channel_id=1, source_target_pairs={{2,0},{4,2},{6,4},{0,6},{3,1},{5,3},{7,5},{1,7},{10,8},{12,10},{14... | collective-permute-start | bytes 442376 | tf_op jit(solution)/shard_map/ppermute | solution.py:842
  32.4 1.3 %own_forward_a.1 = (bf16[1024,128]{1,0:T(8,128)(2,1)S(1)}, bf16[1024,128]{1,0:T(8,128)(2,1)S(1)}, bf16[1024,128]{1,0:T(8,128)(2,1)S(1)}, f32[64,128]{1,0:T(8,128...) custom-call(bf16[64,3200]{1,0:T(8,128)(2,1)S(1)} %bitcast.25, ...), custom_call_target="tpu_custom_call" | custom-call | flops 1024 | bytes 1024 | tf_op jit(solution)/shard_map/own_forward_a/pallas_call | solution.py:57
  33.7 2.7 %own_forward_b.1 = (bf16[1024,2304]{1,0:T(8,128)(2,1)S(1)}, bf16[1024,2304]{1,0:T(8,128)(2,1)S(1)}, f32[64,2304]{1,0:T(8,128)S(1)}) custom-call(bf16[64,3200]{1,0:T(8,128)(2,1)S(1)} %bitcast.26, bf16[5,128,128]{2,1,0:T(8,128)(2,1)S(1)} %copy-done.2, bf16[1024,64]{1,0:T(8,128)(2,1)S(1)} %get-tuple-element.114.refs_2_.oh_own, ...), custom_call_target="tpu_custom_call" | custom-call | flops 1024 | bytes 1024 | tf_op jit(solution)/shard_map/own_forward_b/pallas_call | solution.py:57
  37.1 1.5 %collective-permute-start.13 = (bf16[1,2,4,8,2304]{4,3,2,1,0:T(8,128)(2,1)S(1)}, bf16[1,2,4,8,2304]{4,3,2,1,0:T(8,128)(2,1)S(1)}, u32[]{:S(2)}, u32[]{:S(2)}) collective-permute-start(bf16[1,2,4,8,2304]{4,3,2,1,0:T(8,128)(2,1)S(1)} %get-tuple-element.192), channel_id=1, source_target_pairs={{8,0},{16,8},{24,16},{0,24},{9,1},{17,9},{25,17},{1,25},{10,2},{18... | collective-permute-start | bytes 884744 | tf_op jit(solution)/shard_map/ppermute | solution.py:842
  38.6 3.6 %ghost_start.1 = (bf16[64,128]{1,0:T(8,128)(2,1)S(1)}, bf16[1024,512]{1,0:T(8,128)(2,1)S(1)}, bf16[1024,64]{1,0:T(8,128)(2,1)S(1)}, bf16[64,1024]{1,0:T(8,128)(2...) custom-call(bf16[128,1024]{1,0:T(8,128)(2,1)S(1)} %bitcast.37, ...), custom_call_target="tpu_custom_call" | custom-call | flops 1024 | bytes 1024 | tf_op jit(solution)/shard_map/ghost_start/pallas_call | solution.py:57
  42.2 3.3 %pairs_a.1 = (bf16[64,768]{1,0:T(8,128)(2,1)S(1)}, f32[64,128]{1,0:T(8,128)S(1)}, bf16[64,768]{1,0:T(8,128)(2,1)}, bf16[1024,128]{1,0:T(8,128)(2,1)S(1)}, bf16[1...) custom-call(bf16[128,1024]{1,0:T(8,128)(2,1)S(1)} %bitcast.38, ...), custom_call_target="tpu_custom_call" | custom-call | flops 1024 | bytes 1024 | tf_op jit(solution)/shard_map/pairs_a/pallas_call | solution.py:57
  45.6 2.0 %collective-permute-done.12 = bf16[1,2,4,8,2304]{4,3,2,1,0:T(8,128)(2,1)S(1)} collective-permute-done((bf16[1,2,4,8,2304]{4,3,2,1,0:T(8,128)(2,1)S(1)}, bf16[1,2,4,8,2304]{4,3,2,1,0:T(8,128)(2,1)S(1)}, u32[]{:S(2)}, u32[]{:S(2)}) %collective-permute-start.12) | collective-permute-done | bytes 294944 | tf_op jit(solution)/shard_map/ppermute | solution.py:841
  47.6 8.5 %third_group.1 = (bf16[64,3200]{1,0:T(8,128)(2,1)}, f32[1,64]{1,0:T(1,128)}, f32[64,128]{1,0:T(8,128)S(1)}, f32[8,64]{1,0:T(8,128)S(1)}, f32[8,128]{1,0:T(8,128)...) custom-call(bf16[64,2304]{1,0:T(8,128)(2,1)S(1)} %bitcast.44, ...), custom_call_target="tpu_custom_call" | custom-call | flops 1024 | bytes 1024 | tf_op jit(solution)/shard_map/third_group/pallas_call | solution.py:57
  56.2 1.7 %collective-permute-start.15 = (f32[8,128]{1,0:T(8,128)S(1)}, f32[8,128]{1,0:T(8,128)S(1)}, u32[]{:S(2)}, u32[]{:S(2)}) collective-permute-start(f32[8,128]{1,0:T(8,128)S(1)} %get-tuple-element.161), channel_id=1, source_target_pairs={{8,0},{16,8},{24,16},{0,24},{9,1},{17,9},{25,17},{1,25},{10,2},{18... | collective-permute-start | bytes 12296 | tf_op jit(solution)/shard_map/ppermute | solution.py:885
  58.0 2.3 %own_backward_b.1 = (bf16[1024,128]{1,0:T(8,128)(2,1)S(1)}, bf16[1024,128]{1,0:T(8,128)(2,1)S(1)}, bf16[1024,128]{1,0:T(8,128)(2,1)S(1)}, bf16[1024,128]{1,0:T(8,128)(2,1)S(1)}) custom-call(bf16[5,128,128]{2,1,0:T(8,128)(2,1)S(1)} %copy-done.2, bf16[64,2304]{1,0:T(8,128)(2,1)S(1)} %get-tuple-element.162.gs_ref, ...), custom_call_target="tpu_custom_call" | custom-call | flops 1024 | bytes 1024 | tf_op jit(solution)/shard_map/own_backward_b/pallas_call | solution.py:57
  61.5 2.7 %collective-permute-start.17 = (f32[8,256]{1,0:T(8,128)S(1)}, f32[8,256]{1,0:T(8,128)S(1)}, u32[]{:S(2)}, u32[]{:S(2)}) collective-permute-start(f32[8,256]{1,0:T(8,128)S(1)} %add.3.mid_ref), channel_id=1, source_target_pairs={{2,0},{4,2},{6,4},{0,6},{3,1},{5,3},{7,5},{1,7},{10,8},{12,10},{14... | collective-permute-start | bytes 24584 | tf_op jit(solution)/shard_map/ppermute | solution.py:891
  64.2 1.5 %own_back.2 = (f32[64,128]{1,0:T(8,128)S(1)}, f32[8,64]{1,0:T(8,128)S(1)}) custom-call(bf16[1024,64]{1,0:T(8,128)(2,1)S(1)} %get-tuple-element.114.refs_2_.oh_own, bf16[1024,128]{1,0:T(8,128)(2,1)S(1)} %get-tuple-element.167.pre_own, f32[1024,128]{1,0:T(8,128)S(1)} %get-tuple-element.168.unit_own, bf16[640,128]{1,0:T(8,128)(2,1)S(1)} %get-tuple-element.136.radt_ref, ...), custom_call_target="tpu_custom_call" | custom-call | flops 1024 | bytes 1024 | tf_op jit(solution)/shard_map/own_back/pallas_call | solution.py:57
  65.9 1.5 %collective-permute-start.18 = (f32[8,256]{1,0:T(8,128)S(1)}, f32[8,256]{1,0:T(8,128)S(1)}, u32[]{:S(2)}, u32[]{:S(2)}) collective-permute-start(f32[8,256]{1,0:T(8,128)S(1)} %fold.1.mid_ref), channel_id=1, source_target_pairs={{0,1},{1,0},{2,3},{3,2},{4,5},{5,4},{6,7},{7,6},{8,9},{9,8},{10,11... | collective-permute-start | bytes 24584 | tf_op jit(solution)/shard_map/ppermute | solution.py:900
  67.5 1.5 %own_back.3 = (f32[64,128]{1,0:T(8,128)S(1)}, f32[8,64]{1,0:T(8,128)S(1)}) custom-call(bf16[1024,64]{1,0:T(8,128)(2,1)S(1)} %get-tuple-element.114.refs_2_.oh_own, bf16[1024,128]{1,0:T(8,128)(2,1)S(1)} %get-tuple-element.167.pre_own, f32[1024,128]{1,0:T(8,128)S(1)} %get-tuple-element.168.unit_own, bf16[640,128]{1,0:T(8,128)(2,1)S(1)} %get-tuple-element.136.radt_ref, ...), custom_call_target="tpu_custom_call" | custom-call | flops 1024 | bytes 1024 | tf_op jit(solution)/shard_map/own_back/pallas_call | solution.py:57
  (64 shorter events, 10.2 us)
Async XLA Ops:
  3.4 7.6 %collective-permute-start.3 = (bf16[2,2,2,8,1024]{4,3,2,1,0:T(8,128)(2,1)S(1)}, bf16[2,2,2,8,1024]{4,3,2,1,0:T(8,128)(2,1)S(1)}, u32[]{:S(2)}, u32[]{:S(2)}) collective-permute-start(bf16[2,2,2,8,1024]{4,3,2,1,0:T(8,128)(2,1)S(1)} %bitcast.41), channel_id=1, source_target_pairs={{0,1},{1,0},{2,3},{3,2},{4,5},{5,4},{6,7},{7,6},{8,9},{9,8},{10,11... | collective-permute-start | bytes 393224 | tf_op jit(solution)/shard_map/ppermute | solution.py:836
  6.4 8.7 %copy-start.4 = (bf16[128,640]{1,0:T(8,128)(2,1)S(1)}, bf16[128,640]{1,0:T(8,128)(2,1)}, u32[]{:S(2)}) copy-start(bf16[128,640]{1,0:T(8,128)(2,1)} %rad_ref.3) | copy-start | bytes 491524
  6.4 8.7 %copy-start.5 = (bf16[512,128]{1,0:T(8,128)(2,1)S(1)}, bf16[512,128]{1,0:T(8,128)(2,1)}, u32[]{:S(2)}) copy-start(bf16[512,128]{1,0:T(8,128)(2,1)} %rbf_ref.3) | copy-start | bytes 393220
  6.7 11.3 %collective-permute-start = (bf16[2,2,2,8,2304]{4,3,2,1,0:T(8,128)(2,1)S(1)}, bf16[2,2,2,8,2304]{4,3,2,1,0:T(8,128)(2,1)S(1)}, u32[]{:S(2)}, u32[]{:S(2)}) collective-permute-start(bf16[2,2,2,8,2304]{4,3,2,1,0:T(8,128)(2,1)S(1)} %bitcast.33), channel_id=1, source_target_pairs={{0,1},{1,0},{2,3},{3,2},{4,5},{5,4},{6,7},{7,6},{8,9},{9,8},{10,11... | collective-permute-start | bytes 884744 | tf_op jit(solution)/shard_map/ppermute | solution.py:836
  6.8 11.2 %collective-permute-start.1 = (bf16[2,1,2,8,2304]{4,3,2,1,0:T(8,128)(2,1)S(1)}, bf16[2,1,2,8,2304]{4,3,2,1,0:T(8,128)(2,1)S(1)}, u32[]{:S(2)}, u32[]{:S(2)}) collective-permute-start(bf16[2,1,2,8,2304]{4,3,2,1,0:T(8,128)(2,1)S(1)} %get-tuple-element.201), channel_id=1, source_target_pairs={{0,2},{2,4},{4,6},{6,0},{1,3},{3,5},{5,7},{7,1},{8,10},{10,12},{12... | collective-permute-start | bytes 442376 | tf_op jit(solution)/shard_map/ppermute | solution.py:841
  8.9 10.2 %collective-permute-start.2 = (bf16[2,1,2,8,2304]{4,3,2,1,0:T(8,128)(2,1)S(1)}, bf16[2,1,2,8,2304]{4,3,2,1,0:T(8,128)(2,1)S(1)}, u32[]{:S(2)}, u32[]{:S(2)}) collective-permute-start(bf16[2,1,2,8,2304]{4,3,2,1,0:T(8,128)(2,1)S(1)} %get-tuple-element.200), channel_id=1, source_target_pairs={{2,0},{4,2},{6,4},{0,6},{3,1},{5,3},{7,5},{1,7},{10,8},{12,10},{14... | collective-permute-start | bytes 442376 | tf_op jit(solution)/shard_map/ppermute | solution.py:842
  11.1 10.5 %collective-permute-start.6 = (bf16[2,1,4,8,1024]{4,3,2,1,0:T(8,128)(2,1)S(1)}, bf16[2,1,4,8,1024]{4,3,2,1,0:T(8,128)(2,1)S(1)}, u32[]{:S(2)}, u32[]{:S(2)}) collective-permute-start(bf16[2,1,4,8,1024]{4,3,2,1,0:T(8,128)(2,1)S(1)} %get-tuple-element.205), channel_id=1, source_target_pairs={{0,2},{2,4},{4,6},{6,0},{1,3},{3,5},{5,7},{7,1},{8,10},{10,12},{12... | collective-permute-start | bytes 393224 | tf_op jit(solution)/shard_map/ppermute | solution.py:841
  13.0 9.4 %collective-permute-start.7 = (bf16[2,1,4,8,1024]{4,3,2,1,0:T(8,128)(2,1)S(1)}, bf16[2,1,4,8,1024]{4,3,2,1,0:T(8,128)(2,1)S(1)}, u32[]{:S(2)}, u32[]{:S(2)}) collective-permute-start(bf16[2,1,4,8,1024]{4,3,2,1,0:T(8,128)(2,1)S(1)} %get-tuple-element.204), channel_id=1, source_target_pairs={{2,0},{4,2},{6,4},{0,6},{3,1},{5,3},{7,5},{1,7},{10,8},{12,10},{14... | collective-permute-start | bytes 393224 | tf_op jit(solution)/shard_map/ppermute | solution.py:842
  22.5 7.5 %collective-permute-start.4 = (bf16[1,2,4,8,2304]{4,3,2,1,0:T(8,128)(2,1)S(1)}, bf16[1,2,4,8,2304]{4,3,2,1,0:T(8,128)(2,1)S(1)}, u32[]{:S(2)}, u32[]{:S(2)}) collective-permute-start(bf16[1,2,4,8,2304]{4,3,2,1,0:T(8,128)(2,1)S(1)} %get-tuple-element.195), channel_id=1, source_target_pairs={{0,8},{8,16},{16,24},{24,0},{1,9},{9,17},{17,25},{25,1},{2,10},{10... | collective-permute-start | bytes 884744 | tf_op jit(solution)/shard_map/ppermute | solution.py:841
  22.5 9.9 %collective-permute-start.5 = (bf16[1,2,4,8,2304]{4,3,2,1,0:T(8,128)(2,1)S(1)}, bf16[1,2,4,8,2304]{4,3,2,1,0:T(8,128)(2,1)S(1)}, u32[]{:S(2)}, u32[]{:S(2)}) collective-permute-start(bf16[1,2,4,8,2304]{4,3,2,1,0:T(8,128)(2,1)S(1)} %get-tuple-element.194), channel_id=1, source_target_pairs={{8,0},{16,8},{24,16},{0,24},{9,1},{17,9},{25,17},{1,25},{10,2},{18... | collective-permute-start | bytes 884744 | tf_op jit(solution)/shard_map/ppermute | solution.py:842
  24.3 8.0 %copy-start.1 = (bf16[1,1,1,64,3200]{4,3,2,1,0:T(8,128)(2,1)S(1)}, bf16[1,1,1,64,3200]{4,3,2,1,0:T(8,128)(2,1)}, u32[]{:S(2)}) copy-start(bf16[1,1,1,64,3200]{4,3,2,1,0:T(8,128)(2,1)} %param.11) | copy-start | bytes 1228804
  24.4 8.0 %copy-start.2 = (bf16[5,128,128]{2,1,0:T(8,128)(2,1)S(1)}, bf16[5,128,128]{2,1,0:T(8,128)(2,1)}, u32[]{:S(2)}) copy-start(bf16[5,128,128]{2,1,0:T(8,128)(2,1)} %mix_ref.9) | copy-start | bytes 491524
  24.4 12.5 %collective-permute-start.8 = (bf16[1,4,4,8,1024]{4,3,2,1,0:T(8,128)(2,1)S(1)}, bf16[1,4,4,8,1024]{4,3,2,1,0:T(8,128)(2,1)S(1)}, u32[]{:S(2)}, u32[]{:S(2)}) collective-permute-start(bf16[1,4,4,8,1024]{4,3,2,1,0:T(8,128)(2,1)S(1)} %get-tuple-element.197), channel_id=1, source_target_pairs={{0,8},{8,16},{16,24},{24,0},{1,9},{9,17},{17,25},{25,1},{2,10},{10... | collective-permute-start | bytes 786440 | tf_op jit(solution)/shard_map/ppermute | solution.py:841
  24.5 12.4 %collective-permute-start.9 = (bf16[1,4,4,8,1024]{4,3,2,1,0:T(8,128)(2,1)S(1)}, bf16[1,4,4,8,1024]{4,3,2,1,0:T(8,128)(2,1)S(1)}, u32[]{:S(2)}, u32[]{:S(2)}) collective-permute-start(bf16[1,4,4,8,1024]{4,3,2,1,0:T(8,128)(2,1)S(1)} %get-tuple-element.196), channel_id=1, source_target_pairs={{8,0},{16,8},{24,16},{0,24},{9,1},{17,9},{25,17},{1,25},{10,2},{18... | collective-permute-start | bytes 786440 | tf_op jit(solution)/shard_map/ppermute | solution.py:842
  26.3 10.2 %collective-permute-start.10 = (bf16[2,1,2,8,2304]{4,3,2,1,0:T(8,128)(2,1)S(1)}, bf16[2,1,2,8,2304]{4,3,2,1,0:T(8,128)(2,1)S(1)}, u32[]{:S(2)}, u32[]{:S(2)}) collective-permute-start(bf16[2,1,2,8,2304]{4,3,2,1,0:T(8,128)(2,1)S(1)} %get-tuple-element.199), channel_id=1, source_target_pairs={{0,2},{2,4},{4,6},{6,0},{1,3},{3,5},{5,7},{7,1},{8,10},{10,12},{12... | collective-permute-start | bytes 442376 | tf_op jit(solution)/shard_map/ppermute | solution.py:841
  30.0 6.9 %collective-permute-start.11 = (bf16[2,1,2,8,2304]{4,3,2,1,0:T(8,128)(2,1)S(1)}, bf16[2,1,2,8,2304]{4,3,2,1,0:T(8,128)(2,1)S(1)}, u32[]{:S(2)}, u32[]{:S(2)}) collective-permute-start(bf16[2,1,2,8,2304]{4,3,2,1,0:T(8,128)(2,1)S(1)} %get-tuple-element.198), channel_id=1, source_target_pairs={{2,0},{4,2},{6,4},{0,6},{3,1},{5,3},{7,5},{1,7},{10,8},{12,10},{14... | collective-permute-start | bytes 442376 | tf_op jit(solution)/shard_map/ppermute | solution.py:842
  37.1 5.1 %copy-start.6 = (f32[4,128]{1,0:T(4,128)S(1)}, f32[4,128]{1,0:T(4,128)}, u32[]{:S(2)}) copy-start(f32[4,128]{1,0:T(4,128)} %nw_ref.1) | copy-start | bytes 6148
  37.1 8.5 %collective-permute-start.13 = (bf16[1,2,4,8,2304]{4,3,2,1,0:T(8,128)(2,1)S(1)}, bf16[1,2,4,8,2304]{4,3,2,1,0:T(8,128)(2,1)S(1)}, u32[]{:S(2)}, u32[]{:S(2)}) collective-permute-start(bf16[1,2,4,8,2304]{4,3,2,1,0:T(8,128)(2,1)S(1)} %get-tuple-element.192), channel_id=1, source_target_pairs={{8,0},{16,8},{24,16},{0,24},{9,1},{17,9},{25,17},{1,25},{10,2},{18... | collective-permute-start | bytes 884744 | tf_op jit(solution)/shard_map/ppermute | solution.py:842
  38.6 9.0 %collective-permute-start.12 = (bf16[1,2,4,8,2304]{4,3,2,1,0:T(8,128)(2,1)S(1)}, bf16[1,2,4,8,2304]{4,3,2,1,0:T(8,128)(2,1)S(1)}, u32[]{:S(2)}, u32[]{:S(2)}) collective-permute-start(bf16[1,2,4,8,2304]{4,3,2,1,0:T(8,128)(2,1)S(1)} %get-tuple-element.193), channel_id=1, source_target_pairs={{0,8},{8,16},{16,24},{24,0},{1,9},{9,17},{17,25},{25,1},{2,10},{10... | collective-permute-start | bytes 884744 | tf_op jit(solution)/shard_map/ppermute | solution.py:841
  56.2 4.1 %collective-permute-start.14 = (f32[8,128]{1,0:T(8,128)S(1)}, f32[8,128]{1,0:T(8,128)S(1)}, u32[]{:S(2)}, u32[]{:S(2)}) collective-permute-start(f32[8,128]{1,0:T(8,128)S(1)} %get-tuple-element.160), channel_id=1, source_target_pairs={{0,8},{8,16},{16,24},{24,0},{1,9},{9,17},{17,25},{25,1},{2,10},{10... | collective-permute-start | bytes 12296 | tf_op jit(solution)/shard_map/ppermute | solution.py:884
  56.2 4.1 %collective-permute-start.15 = (f32[8,128]{1,0:T(8,128)S(1)}, f32[8,128]{1,0:T(8,128)S(1)}, u32[]{:S(2)}, u32[]{:S(2)}) collective-permute-start(f32[8,128]{1,0:T(8,128)S(1)} %get-tuple-element.161), channel_id=1, source_target_pairs={{8,0},{16,8},{24,16},{0,24},{9,1},{17,9},{25,17},{1,25},{10,2},{18... | collective-permute-start | bytes 12296 | tf_op jit(solution)/shard_map/ppermute | solution.py:885
  60.3 5.5 %collective-permute-start.16 = (f32[8,256]{1,0:T(8,128)S(1)}, f32[8,256]{1,0:T(8,128)S(1)}, u32[]{:S(2)}, u32[]{:S(2)}) collective-permute-start(f32[8,256]{1,0:T(8,128)S(1)} %add.3.mid_ref), channel_id=1, source_target_pairs={{0,2},{2,4},{4,6},{6,0},{1,3},{3,5},{5,7},{7,1},{8,10},{10,12},{12... | collective-permute-start | bytes 24584 | tf_op jit(solution)/shard_map/ppermute | solution.py:891
  61.5 4.3 %collective-permute-start.17 = (f32[8,256]{1,0:T(8,128)S(1)}, f32[8,256]{1,0:T(8,128)S(1)}, u32[]{:S(2)}, u32[]{:S(2)}) collective-permute-start(f32[8,256]{1,0:T(8,128)S(1)} %add.3.mid_ref), channel_id=1, source_target_pairs={{2,0},{4,2},{6,4},{0,6},{3,1},{5,3},{7,5},{1,7},{10,8},{12,10},{14... | collective-permute-start | bytes 24584 | tf_op jit(solution)/shard_map/ppermute | solution.py:891
  65.9 3.7 %collective-permute-start.18 = (f32[8,256]{1,0:T(8,128)S(1)}, f32[8,256]{1,0:T(8,128)S(1)}, u32[]{:S(2)}, u32[]{:S(2)}) collective-permute-start(f32[8,256]{1,0:T(8,128)S(1)} %fold.1.mid_ref), channel_id=1, source_target_pairs={{0,1},{1,0},{2,3},{3,2},{4,5},{5,4},{6,7},{7,6},{8,9},{9,8},{10,11... | collective-permute-start | bytes 24584 | tf_op jit(solution)/shard_map/ppermute | solution.py:900
  (4 other events, 5.0 us)

commit v15 on v13

--- a/solution.py
+++ b/solution.py
@@ -53,7 +53,7 @@
     return jax.ShapeDtypeStruct(shape, dtype)
 
 
-def call(kernel, name, out_shape, scratch, args, specs=None, limit=16):
+def call(kernel, name, out_shape, scratch, args, specs=None, limit=16, work=1024):
     return pl.pallas_call(
         kernel,
         out_shape=out_shape,
@@ -61,7 +61,7 @@
         out_specs=tuple(pl.BlockSpec(memory_space=SPACE) for _ in out_shape),
         scratch_shapes=scratch,
         compiler_params=pltpu.CompilerParams(vmem_limit_bytes=limit * MIB),
-        cost_estimate=pl.CostEstimate(flops=1024, bytes_accessed=1024, transcendentals=0),
+        cost_estimate=pl.CostEstimate(flops=work, bytes_accessed=1024, transcendentals=0),
         name=name,
     )(*args)
 
@@ -112,7 +112,7 @@
     scratch = [pltpu.VMEM((CH, atoms), F32), pltpu.VMEM((CH, atoms), F32)]
     first, own_pos, meta, pick = call(cells_kernel, "cells", out_shape, scratch, args)
     out_shape = (struct(atoms, GROUP_COLS[1], dtype=BF16),)
-    rest = call(rest_kernel, "cells_rest", out_shape, [], (feats, pick))[0]
+    rest = call(rest_kernel, "cells_rest", out_shape, [], (feats, pick), work=1 << 32)[0]
     return first, rest, own_pos, meta
 
 

time: 68.1 us -> 66.2 us (0.972)
  local copies, waits for them, and re-layouts: 3.8 us -> 1.97 us
    unnamed x23 -> x19, local copies, waits for them, and re-layouts: 3.55 us -> 1.73 us
  transfers between devices with their start and end apart: 19 -> 19, of which waited for: 7 -> 9; matrix products, arithmetic and copies ran while one was open for 1% -> 1% of each run, Pallas kernels for 30% -> 31%
where the time goes in v15:
time: 66.2 us; the launch traced here: 66 us
  Pallas kernels  29.1 us (44%)
  starting transfers between devices  28 us (42%)
  waiting for transfers between devices  4.76 us (7%)
  local copies, waits for them, and re-layouts  1.97 us (3%)
  other arithmetic  1.16 us (2%)
  between operations  0.95 us (1%)
    pallas_call x13, Pallas kernels, call(): pl.pallas_call(kernel, out_shape=out_shape, in_specs=specs or [pl.BlockSp...  29.1 us
    ppermute x6, starting transfers between devices, neighbours_of(): after = lax.ppermute(lax.slice_in_dim(block, 0, 1, axis=dim), axis, down)  11.8 us
    ppermute x6, starting transfers between devices, neighbours_of(): lax.ppermute(lax.slice_in_dim(block, length - 1, length, axis=dim), axis,...  5.57 us
    ppermute x2, starting transfers between devices, give_back_y(): return (mid, lax.ppermute(mid, 'gy', up), lax.ppermute(mid, 'gy', down))  3.88 us
    ppermute x2, starting transfers between devices, neighbours_of(): other = lax.ppermute(block, axis, up)  3.13 us
    ppermute x6, waiting for transfers between devices, neighbours_of(): after = lax.ppermute(lax.slice_in_dim(block, 0, 1, axis=dim), axis, down)  2.79 us
    unnamed x19, local copies, waits for them, and re-layouts  1.73 us
    ppermute x1, starting transfers between devices, give_back_z(): from_low = lax.ppermute(mid, 'gz', up)  1.56 us
  transfers between devices with their start and end apart: 19, of which 9 were waited for; matrix products, arithmetic and copies ran while one was open for 1% of the time, Pallas kernels for 31%

profile of v15, /device:TPU:0, one launch (start us, length us, event | category | flops | bytes accessed | tf_op | source)
XLA Modules:
  0.0 66.0 jit_solution(15457143771134301572)
XLA Ops:
  3.4 3.0 %collective-permute-start.3 = (bf16[2,2,2,8,1280]{4,3,2,1,0:T(8,128)(2,1)S(1)}, bf16[2,2,2,8,1280]{4,3,2,1,0:T(8,128)(2,1)S(1)}, u32[]{:S(2)}, u32[]{:S(2)}) collective-permute-start(bf16[2,2,2,8,1280]{4,3,2,1,0:T(8,128)(2,1)S(1)} %bitcast.41), channel_id=1, source_target_pairs={{0,1},{1,0},{2,3},{3,2},{4,5},{5,4},{6,7},{7,6},{8,9},{9,8},{10,11... | collective-permute-start | bytes 491528 | tf_op jit(solution)/shard_map/ppermute | solution.py:836
  6.8 2.1 %collective-permute-start.1 = (bf16[2,1,2,8,2048]{4,3,2,1,0:T(8,128)(2,1)S(1)}, bf16[2,1,2,8,2048]{4,3,2,1,0:T(8,128)(2,1)S(1)}, u32[]{:S(2)}, u32[]{:S(2)}) collective-permute-start(bf16[2,1,2,8,2048]{4,3,2,1,0:T(8,128)(2,1)S(1)} %get-tuple-element.201), channel_id=1, source_target_pairs={{0,2},{2,4},{4,6},{6,0},{1,3},{3,5},{5,7},{7,1},{8,10},{10,12},{12... | collective-permute-start | bytes 393224 | tf_op jit(solution)/shard_map/ppermute | solution.py:841
  8.9 2.1 %collective-permute-start.2 = (bf16[2,1,2,8,2048]{4,3,2,1,0:T(8,128)(2,1)S(1)}, bf16[2,1,2,8,2048]{4,3,2,1,0:T(8,128)(2,1)S(1)}, u32[]{:S(2)}, u32[]{:S(2)}) collective-permute-start(bf16[2,1,2,8,2048]{4,3,2,1,0:T(8,128)(2,1)S(1)} %get-tuple-element.200), channel_id=1, source_target_pairs={{2,0},{4,2},{6,4},{0,6},{3,1},{5,3},{7,5},{1,7},{10,8},{12,10},{14... | collective-permute-start | bytes 393224 | tf_op jit(solution)/shard_map/ppermute | solution.py:842
  11.6 2.2 %collective-permute-start.6 = (bf16[2,1,4,8,1280]{4,3,2,1,0:T(8,128)(2,1)S(1)}, bf16[2,1,4,8,1280]{4,3,2,1,0:T(8,128)(2,1)S(1)}, u32[]{:S(2)}, u32[]{:S(2)}) collective-permute-start(bf16[2,1,4,8,1280]{4,3,2,1,0:T(8,128)(2,1)S(1)} %get-tuple-element.197), channel_id=1, source_target_pairs={{0,2},{2,4},{4,6},{6,0},{1,3},{3,5},{5,7},{7,1},{8,10},{10,12},{12... | collective-permute-start | bytes 491528 | tf_op jit(solution)/shard_map/ppermute | solution.py:841
  13.7 2.1 %collective-permute-start.7 = (bf16[2,1,4,8,1280]{4,3,2,1,0:T(8,128)(2,1)S(1)}, bf16[2,1,4,8,1280]{4,3,2,1,0:T(8,128)(2,1)S(1)}, u32[]{:S(2)}, u32[]{:S(2)}) collective-permute-start(bf16[2,1,4,8,1280]{4,3,2,1,0:T(8,128)(2,1)S(1)} %get-tuple-element.196), channel_id=1, source_target_pairs={{2,0},{4,2},{6,4},{0,6},{3,1},{5,3},{7,5},{1,7},{10,8},{12,10},{14... | collective-permute-start | bytes 491528 | tf_op jit(solution)/shard_map/ppermute | solution.py:842
  15.8 2.9 %own_edges.1 = (bf16[1024,64]{1,0:T(8,128)(2,1)S(1)}, bf16[1024,128]{1,0:T(8,128)(2,1)S(1)}, f32[1024,128]{1,0:T(8,128)S(1)}, bf16[640,128]{1,0:T(8,128)(2,1)S(1...) custom-call(f32[64,128]{1,0:T(8,128)S(1)} %get-tuple-element.99.meta, ...), custom_call_target="tpu_custom_call" | custom-call | flops 1024 | bytes 1024 | tf_op jit(solution)/shard_map/own_edges/pallas_call | solution.py:57
  19.4 1.7 %collective-permute-start.5 = (bf16[1,2,4,8,2048]{4,3,2,1,0:T(8,128)(2,1)S(1)}, bf16[1,2,4,8,2048]{4,3,2,1,0:T(8,128)(2,1)S(1)}, u32[]{:S(2)}, u32[]{:S(2)}) collective-permute-start(bf16[1,2,4,8,2048]{4,3,2,1,0:T(8,128)(2,1)S(1)} %get-tuple-element.194), channel_id=1, source_target_pairs={{8,0},{16,8},{24,16},{0,24},{9,1},{17,9},{25,17},{1,25},{10,2},{18... | collective-permute-start | bytes 786440 | tf_op jit(solution)/shard_map/ppermute | solution.py:842
  21.5 1.6 %collective-permute-done.7 = bf16[2,1,4,8,1280]{4,3,2,1,0:T(8,128)(2,1)S(1)} collective-permute-done((bf16[2,1,4,8,1280]{4,3,2,1,0:T(8,128)(2,1)S(1)}, bf16[2,1,4,8,1280]{4,3,2,1,0:T(8,128)(2,1)S(1)}, u32[]{:S(2)}, u32[]{:S(2)}) %collective-permute-start.7) | collective-permute-done | bytes 163872 | tf_op jit(solution)/shard_map/ppermute | solution.py:842
  23.4 1.7 %collective-permute-start.9 = (bf16[1,4,4,8,1280]{4,3,2,1,0:T(8,128)(2,1)S(1)}, bf16[1,4,4,8,1280]{4,3,2,1,0:T(8,128)(2,1)S(1)}, u32[]{:S(2)}, u32[]{:S(2)}) collective-permute-start(bf16[1,4,4,8,1280]{4,3,2,1,0:T(8,128)(2,1)S(1)} %get-tuple-element.190), channel_id=1, source_target_pairs={{8,0},{16,8},{24,16},{0,24},{9,1},{17,9},{25,17},{1,25},{10,2},{18... | collective-permute-start | bytes 983048 | tf_op jit(solution)/shard_map/ppermute | solution.py:842
  25.2 1.2 %collective-permute-start.10 = (bf16[2,1,2,8,2048]{4,3,2,1,0:T(8,128)(2,1)S(1)}, bf16[2,1,2,8,2048]{4,3,2,1,0:T(8,128)(2,1)S(1)}, u32[]{:S(2)}, u32[]{:S(2)}) collective-permute-start(bf16[2,1,2,8,2048]{4,3,2,1,0:T(8,128)(2,1)S(1)} %get-tuple-element.199), channel_id=1, source_target_pairs={{0,2},{2,4},{4,6},{6,0},{1,3},{3,5},{5,7},{7,1},{8,10},{10,12},{12... | collective-permute-start | bytes 393224 | tf_op jit(solution)/shard_map/ppermute | solution.py:841
  26.4 2.6 %collective-permute-start.11 = (bf16[2,1,2,8,2048]{4,3,2,1,0:T(8,128)(2,1)S(1)}, bf16[2,1,2,8,2048]{4,3,2,1,0:T(8,128)(2,1)S(1)}, u32[]{:S(2)}, u32[]{:S(2)}) collective-permute-start(bf16[2,1,2,8,2048]{4,3,2,1,0:T(8,128)(2,1)S(1)} %get-tuple-element.198), channel_id=1, source_target_pairs={{2,0},{4,2},{6,4},{0,6},{3,1},{5,3},{7,5},{1,7},{10,8},{12,10},{14... | collective-permute-start | bytes 393224 | tf_op jit(solution)/shard_map/ppermute | solution.py:842
  29.0 1.5 %own_forward_a.1 = (bf16[1024,128]{1,0:T(8,128)(2,1)S(1)}, bf16[1024,128]{1,0:T(8,128)(2,1)S(1)}, bf16[1024,128]{1,0:T(8,128)(2,1)S(1)}, f32[64,128]{1,0:T(8,128...) custom-call(bf16[64,3200]{1,0:T(8,128)(2,1)S(1)} %bitcast.25, ...), custom_call_target="tpu_custom_call" | custom-call | flops 1024 | bytes 1024 | tf_op jit(solution)/shard_map/own_forward_a/pallas_call | solution.py:57
  30.6 2.5 %own_forward_b.1 = (bf16[1024,2048]{1,0:T(8,128)(2,1)S(1)}, bf16[1024,2048]{1,0:T(8,128)(2,1)S(1)}, f32[64,2048]{1,0:T(8,128)S(1)}) custom-call(bf16[64,3200]{1,0:T(8,128)(2,1)S(1)} %bitcast.26, bf16[5,128,128]{2,1,0:T(8,128)(2,1)S(1)} %copy-done.2, bf16[1024,64]{1,0:T(8,128)(2,1)S(1)} %get-tuple-element.113.refs_2_.oh_own, ...), custom_call_target="tpu_custom_call" | custom-call | flops 1024 | bytes 1024 | tf_op jit(solution)/shard_map/own_forward_b/pallas_call | solution.py:57
  34.3 1.5 %collective-permute-start.13 = (bf16[1,2,4,8,2048]{4,3,2,1,0:T(8,128)(2,1)S(1)}, bf16[1,2,4,8,2048]{4,3,2,1,0:T(8,128)(2,1)S(1)}, u32[]{:S(2)}, u32[]{:S(2)}) collective-permute-start(bf16[1,2,4,8,2048]{4,3,2,1,0:T(8,128)(2,1)S(1)} %get-tuple-element.192), channel_id=1, source_target_pairs={{8,0},{16,8},{24,16},{0,24},{9,1},{17,9},{25,17},{1,25},{10,2},{18... | collective-permute-start | bytes 786440 | tf_op jit(solution)/shard_map/ppermute | solution.py:842
  35.8 3.6 %ghost_start.1 = (bf16[64,128]{1,0:T(8,128)(2,1)S(1)}, bf16[1024,512]{1,0:T(8,128)(2,1)S(1)}, bf16[1024,64]{1,0:T(8,128)(2,1)S(1)}, bf16[64,1024]{1,0:T(8,128)(2...) custom-call(bf16[128,1280]{1,0:T(8,128)(2,1)S(1)} %bitcast.37, ...), custom_call_target="tpu_custom_call" | custom-call | flops 1024 | bytes 1024 | tf_op jit(solution)/shard_map/ghost_start/pallas_call | solution.py:57
  39.4 4.4 %pairs_a.1 = (bf16[64,1024]{1,0:T(8,128)(2,1)S(1)}, f32[64,128]{1,0:T(8,128)S(1)}, bf16[64,1024]{1,0:T(8,128)(2,1)}, bf16[1024,128]{1,0:T(8,128)(2,1)S(1)}, bf16...) custom-call(bf16[128,1280]{1,0:T(8,128)(2,1)S(1)} %bitcast.38, ...), custom_call_target="tpu_custom_call" | custom-call | flops 1024 | bytes 1024 | tf_op jit(solution)/shard_map/pairs_a/pallas_call | solution.py:57
  44.0 7.7 %third_group.1 = (bf16[64,3200]{1,0:T(8,128)(2,1)}, f32[1,64]{1,0:T(1,128)}, f32[64,128]{1,0:T(8,128)S(1)}, f32[8,64]{1,0:T(8,128)S(1)}, f32[8,128]{1,0:T(8,128)...) custom-call(bf16[64,2048]{1,0:T(8,128)(2,1)S(1)} %bitcast.44, ...), custom_call_target="tpu_custom_call" | custom-call | flops 1024 | bytes 1024 | tf_op jit(solution)/shard_map/third_group/pallas_call | solution.py:57
  52.7 1.1 %collective-permute-start.15 = (f32[8,128]{1,0:T(8,128)S(1)}, f32[8,128]{1,0:T(8,128)S(1)}, u32[]{:S(2)}, u32[]{:S(2)}) collective-permute-start(f32[8,128]{1,0:T(8,128)S(1)} %get-tuple-element.160), channel_id=1, source_target_pairs={{8,0},{16,8},{24,16},{0,24},{9,1},{17,9},{25,17},{1,25},{10,2},{18... | collective-permute-start | bytes 12296 | tf_op jit(solution)/shard_map/ppermute | solution.py:885
  53.7 2.2 %own_backward_b.1 = (bf16[1024,128]{1,0:T(8,128)(2,1)S(1)}, bf16[1024,128]{1,0:T(8,128)(2,1)S(1)}, bf16[1024,128]{1,0:T(8,128)(2,1)S(1)}) custom-call(bf16[5,128,128]{2,1,0:T(8,128)(2,1)S(1)} %copy-done.2, bf16[64,2048]{1,0:T(8,128)(2,1)S(1)} %get-tuple-element.161.gs_ref, bf16[1024,128]{1,0:T(8,128)(2,1)S(1)} %get-tuple-element.120.refs_8_.refs_12_.gate_ref, ...), custom_call_target="tpu_custom_call" | custom-call | flops 1024 | bytes 1024 | tf_op jit(solution)/shard_map/own_backward_b/pallas_call | solution.py:57
  56.0 1.6 %collective-permute-start.16 = (f32[8,256]{1,0:T(8,128)S(1)}, f32[8,256]{1,0:T(8,128)S(1)}, u32[]{:S(2)}, u32[]{:S(2)}) collective-permute-start(f32[8,256]{1,0:T(8,128)S(1)} %add.3.mid_ref), channel_id=1, source_target_pairs={{0,2},{2,4},{4,6},{6,0},{1,3},{3,5},{5,7},{7,1},{8,10},{10,12},{12... | collective-permute-start | bytes 24584 | tf_op jit(solution)/shard_map/ppermute | solution.py:891
  57.6 2.3 %collective-permute-start.17 = (f32[8,256]{1,0:T(8,128)S(1)}, f32[8,256]{1,0:T(8,128)S(1)}, u32[]{:S(2)}, u32[]{:S(2)}) collective-permute-start(f32[8,256]{1,0:T(8,128)S(1)} %add.3.mid_ref), channel_id=1, source_target_pairs={{2,0},{4,2},{6,4},{0,6},{3,1},{5,3},{7,5},{1,7},{10,8},{12,10},{14... | collective-permute-start | bytes 24584 | tf_op jit(solution)/shard_map/ppermute | solution.py:891
  59.8 1.5 %own_back.2 = (f32[64,128]{1,0:T(8,128)S(1)}, f32[8,64]{1,0:T(8,128)S(1)}) custom-call(bf16[1024,64]{1,0:T(8,128)(2,1)S(1)} %get-tuple-element.113.refs_2_.oh_own, bf16[1024,128]{1,0:T(8,128)(2,1)S(1)} %get-tuple-element.166.pre_own, f32[1024,128]{1,0:T(8,128)S(1)} %get-tuple-element.167.unit_own, bf16[640,128]{1,0:T(8,128)(2,1)S(1)} %get-tuple-element.135.radt_ref, ...), custom_call_target="tpu_custom_call" | custom-call | flops 1024 | bytes 1024 | tf_op jit(solution)/shard_map/own_back/pallas_call | solution.py:57
  61.5 1.6 %collective-permute-start.18 = (f32[8,256]{1,0:T(8,128)S(1)}, f32[8,256]{1,0:T(8,128)S(1)}, u32[]{:S(2)}, u32[]{:S(2)}) collective-permute-start(f32[8,256]{1,0:T(8,128)S(1)} %fold.1.mid_ref), channel_id=1, source_target_pairs={{0,1},{1,0},{2,3},{3,2},{4,5},{5,4},{6,7},{7,6},{8,9},{9,8},{10,11... | collective-permute-start | bytes 24584 | tf_op jit(solution)/shard_map/ppermute | solution.py:900
  63.1 1.5 %own_back.3 = (f32[64,128]{1,0:T(8,128)S(1)}, f32[8,64]{1,0:T(8,128)S(1)}) custom-call(bf16[1024,64]{1,0:T(8,128)(2,1)S(1)} %get-tuple-element.113.refs_2_.oh_own, bf16[1024,128]{1,0:T(8,128)(2,1)S(1)} %get-tuple-element.166.pre_own, f32[1024,128]{1,0:T(8,128)S(1)} %get-tuple-element.167.unit_own, bf16[640,128]{1,0:T(8,128)(2,1)S(1)} %get-tuple-element.135.radt_ref, ...), custom_call_target="tpu_custom_call" | custom-call | flops 1024 | bytes 1024 | tf_op jit(solution)/shard_map/own_back/pallas_call | solution.py:57
  (64 shorter events, 8.9 us)
Async XLA Ops:
  3.4 8.1 %collective-permute-start.3 = (bf16[2,2,2,8,1280]{4,3,2,1,0:T(8,128)(2,1)S(1)}, bf16[2,2,2,8,1280]{4,3,2,1,0:T(8,128)(2,1)S(1)}, u32[]{:S(2)}, u32[]{:S(2)}) collective-permute-start(bf16[2,2,2,8,1280]{4,3,2,1,0:T(8,128)(2,1)S(1)} %bitcast.41), channel_id=1, source_target_pairs={{0,1},{1,0},{2,3},{3,2},{4,5},{5,4},{6,7},{7,6},{8,9},{9,8},{10,11... | collective-permute-start | bytes 491528 | tf_op jit(solution)/shard_map/ppermute | solution.py:836
  6.4 9.4 %copy-start.5 = (bf16[512,128]{1,0:T(8,128)(2,1)S(1)}, bf16[512,128]{1,0:T(8,128)(2,1)}, u32[]{:S(2)}) copy-start(bf16[512,128]{1,0:T(8,128)(2,1)} %rbf_ref.3) | copy-start | bytes 393220
  6.7 12.0 %collective-permute-start = (bf16[2,2,2,8,2048]{4,3,2,1,0:T(8,128)(2,1)S(1)}, bf16[2,2,2,8,2048]{4,3,2,1,0:T(8,128)(2,1)S(1)}, u32[]{:S(2)}, u32[]{:S(2)}) collective-permute-start(bf16[2,2,2,8,2048]{4,3,2,1,0:T(8,128)(2,1)S(1)} %bitcast.33), channel_id=1, source_target_pairs={{0,1},{1,0},{2,3},{3,2},{4,5},{5,4},{6,7},{7,6},{8,9},{9,8},{10,11... | collective-permute-start | bytes 786440 | tf_op jit(solution)/shard_map/ppermute | solution.py:836
  6.8 22.3 %copy-start.1 = (bf16[1,1,1,64,3200]{4,3,2,1,0:T(8,128)(2,1)S(1)}, bf16[1,1,1,64,3200]{4,3,2,1,0:T(8,128)(2,1)}, u32[]{:S(2)}) copy-start(bf16[1,1,1,64,3200]{4,3,2,1,0:T(8,128)(2,1)} %param.11) | copy-start | bytes 1228804
  6.8 22.3 %copy-start.2 = (bf16[5,128,128]{2,1,0:T(8,128)(2,1)S(1)}, bf16[5,128,128]{2,1,0:T(8,128)(2,1)}, u32[]{:S(2)}) copy-start(bf16[5,128,128]{2,1,0:T(8,128)(2,1)} %mix_ref.9) | copy-start | bytes 491524
  6.8 11.9 %collective-permute-start.1 = (bf16[2,1,2,8,2048]{4,3,2,1,0:T(8,128)(2,1)S(1)}, bf16[2,1,2,8,2048]{4,3,2,1,0:T(8,128)(2,1)S(1)}, u32[]{:S(2)}, u32[]{:S(2)}) collective-permute-start(bf16[2,1,2,8,2048]{4,3,2,1,0:T(8,128)(2,1)S(1)} %get-tuple-element.201), channel_id=1, source_target_pairs={{0,2},{2,4},{4,6},{6,0},{1,3},{3,5},{5,7},{7,1},{8,10},{10,12},{12... | collective-permute-start | bytes 393224 | tf_op jit(solution)/shard_map/ppermute | solution.py:841
  8.9 10.3 %collective-permute-start.2 = (bf16[2,1,2,8,2048]{4,3,2,1,0:T(8,128)(2,1)S(1)}, bf16[2,1,2,8,2048]{4,3,2,1,0:T(8,128)(2,1)S(1)}, u32[]{:S(2)}, u32[]{:S(2)}) collective-permute-start(bf16[2,1,2,8,2048]{4,3,2,1,0:T(8,128)(2,1)S(1)} %get-tuple-element.200), channel_id=1, source_target_pairs={{2,0},{4,2},{6,4},{0,6},{3,1},{5,3},{7,5},{1,7},{10,8},{12,10},{14... | collective-permute-start | bytes 393224 | tf_op jit(solution)/shard_map/ppermute | solution.py:842
  11.6 10.0 %collective-permute-start.6 = (bf16[2,1,4,8,1280]{4,3,2,1,0:T(8,128)(2,1)S(1)}, bf16[2,1,4,8,1280]{4,3,2,1,0:T(8,128)(2,1)S(1)}, u32[]{:S(2)}, u32[]{:S(2)}) collective-permute-start(bf16[2,1,4,8,1280]{4,3,2,1,0:T(8,128)(2,1)S(1)} %get-tuple-element.197), channel_id=1, source_target_pairs={{0,2},{2,4},{4,6},{6,0},{1,3},{3,5},{5,7},{7,1},{8,10},{10,12},{12... | collective-permute-start | bytes 491528 | tf_op jit(solution)/shard_map/ppermute | solution.py:841
  13.7 9.4 %collective-permute-start.7 = (bf16[2,1,4,8,1280]{4,3,2,1,0:T(8,128)(2,1)S(1)}, bf16[2,1,4,8,1280]{4,3,2,1,0:T(8,128)(2,1)S(1)}, u32[]{:S(2)}, u32[]{:S(2)}) collective-permute-start(bf16[2,1,4,8,1280]{4,3,2,1,0:T(8,128)(2,1)S(1)} %get-tuple-element.196), channel_id=1, source_target_pairs={{2,0},{4,2},{6,4},{0,6},{3,1},{5,3},{7,5},{1,7},{10,8},{12,10},{14... | collective-permute-start | bytes 491528 | tf_op jit(solution)/shard_map/ppermute | solution.py:842
  19.3 7.1 %collective-permute-start.4 = (bf16[1,2,4,8,2048]{4,3,2,1,0:T(8,128)(2,1)S(1)}, bf16[1,2,4,8,2048]{4,3,2,1,0:T(8,128)(2,1)S(1)}, u32[]{:S(2)}, u32[]{:S(2)}) collective-permute-start(bf16[1,2,4,8,2048]{4,3,2,1,0:T(8,128)(2,1)S(1)} %get-tuple-element.195), channel_id=1, source_target_pairs={{0,8},{8,16},{16,24},{24,0},{1,9},{9,17},{17,25},{25,1},{2,10},{10... | collective-permute-start | bytes 786440 | tf_op jit(solution)/shard_map/ppermute | solution.py:841
  19.4 9.7 %collective-permute-start.5 = (bf16[1,2,4,8,2048]{4,3,2,1,0:T(8,128)(2,1)S(1)}, bf16[1,2,4,8,2048]{4,3,2,1,0:T(8,128)(2,1)S(1)}, u32[]{:S(2)}, u32[]{:S(2)}) collective-permute-start(bf16[1,2,4,8,2048]{4,3,2,1,0:T(8,128)(2,1)S(1)} %get-tuple-element.194), channel_id=1, source_target_pairs={{8,0},{16,8},{24,16},{0,24},{9,1},{17,9},{25,17},{1,25},{10,2},{18... | collective-permute-start | bytes 786440 | tf_op jit(solution)/shard_map/ppermute | solution.py:842
  23.3 12.5 %copy-start.3 = (bf16[5,128,128]{2,1,0:T(8,128)(2,1)S(1)}, bf16[5,128,128]{2,1,0:T(8,128)(2,1)}, u32[]{:S(2)}) copy-start(bf16[5,128,128]{2,1,0:T(8,128)(2,1)} %out_ref.3) | copy-start | bytes 491524
  23.3 12.5 %copy-start.8 = (f32[128]{0:T(128)S(1)}, f32[128]{0:T(128)}, u32[]{:S(2)}) copy-start(f32[128]{0:T(128)} %param.20) | copy-start | bytes 1540
  23.3 10.8 %collective-permute-start.8 = (bf16[1,4,4,8,1280]{4,3,2,1,0:T(8,128)(2,1)S(1)}, bf16[1,4,4,8,1280]{4,3,2,1,0:T(8,128)(2,1)S(1)}, u32[]{:S(2)}, u32[]{:S(2)}) collective-permute-start(bf16[1,4,4,8,1280]{4,3,2,1,0:T(8,128)(2,1)S(1)} %get-tuple-element.191), channel_id=1, source_target_pairs={{0,8},{8,16},{16,24},{24,0},{1,9},{9,17},{17,25},{25,1},{2,10},{10... | collective-permute-start | bytes 983048 | tf_op jit(solution)/shard_map/ppermute | solution.py:841
  23.4 10.8 %collective-permute-start.9 = (bf16[1,4,4,8,1280]{4,3,2,1,0:T(8,128)(2,1)S(1)}, bf16[1,4,4,8,1280]{4,3,2,1,0:T(8,128)(2,1)S(1)}, u32[]{:S(2)}, u32[]{:S(2)}) collective-permute-start(bf16[1,4,4,8,1280]{4,3,2,1,0:T(8,128)(2,1)S(1)} %get-tuple-element.190), channel_id=1, source_target_pairs={{8,0},{16,8},{24,16},{0,24},{9,1},{17,9},{25,17},{1,25},{10,2},{18... | collective-permute-start | bytes 983048 | tf_op jit(solution)/shard_map/ppermute | solution.py:842
  25.2 8.2 %collective-permute-start.10 = (bf16[2,1,2,8,2048]{4,3,2,1,0:T(8,128)(2,1)S(1)}, bf16[2,1,2,8,2048]{4,3,2,1,0:T(8,128)(2,1)S(1)}, u32[]{:S(2)}, u32[]{:S(2)}) collective-permute-start(bf16[2,1,2,8,2048]{4,3,2,1,0:T(8,128)(2,1)S(1)} %get-tuple-element.199), channel_id=1, source_target_pairs={{0,2},{2,4},{4,6},{6,0},{1,3},{3,5},{5,7},{7,1},{8,10},{10,12},{12... | collective-permute-start | bytes 393224 | tf_op jit(solution)/shard_map/ppermute | solution.py:841
  26.4 7.7 %collective-permute-start.11 = (bf16[2,1,2,8,2048]{4,3,2,1,0:T(8,128)(2,1)S(1)}, bf16[2,1,2,8,2048]{4,3,2,1,0:T(8,128)(2,1)S(1)}, u32[]{:S(2)}, u32[]{:S(2)}) collective-permute-start(bf16[2,1,2,8,2048]{4,3,2,1,0:T(8,128)(2,1)S(1)} %get-tuple-element.198), channel_id=1, source_target_pairs={{2,0},{4,2},{6,4},{0,6},{3,1},{5,3},{7,5},{1,7},{10,8},{12,10},{14... | collective-permute-start | bytes 393224 | tf_op jit(solution)/shard_map/ppermute | solution.py:842
  34.3 9.7 %collective-permute-start.13 = (bf16[1,2,4,8,2048]{4,3,2,1,0:T(8,128)(2,1)S(1)}, bf16[1,2,4,8,2048]{4,3,2,1,0:T(8,128)(2,1)S(1)}, u32[]{:S(2)}, u32[]{:S(2)}) collective-permute-start(bf16[1,2,4,8,2048]{4,3,2,1,0:T(8,128)(2,1)S(1)} %get-tuple-element.192), channel_id=1, source_target_pairs={{8,0},{16,8},{24,16},{0,24},{9,1},{17,9},{25,17},{1,25},{10,2},{18... | collective-permute-start | bytes 786440 | tf_op jit(solution)/shard_map/ppermute | solution.py:842
  35.8 8.2 %collective-permute-start.12 = (bf16[1,2,4,8,2048]{4,3,2,1,0:T(8,128)(2,1)S(1)}, bf16[1,2,4,8,2048]{4,3,2,1,0:T(8,128)(2,1)S(1)}, u32[]{:S(2)}, u32[]{:S(2)}) collective-permute-start(bf16[1,2,4,8,2048]{4,3,2,1,0:T(8,128)(2,1)S(1)} %get-tuple-element.193), channel_id=1, source_target_pairs={{0,8},{8,16},{16,24},{24,0},{1,9},{9,17},{17,25},{25,1},{2,10},{10... | collective-permute-start | bytes 786440 | tf_op jit(solution)/shard_map/ppermute | solution.py:841
  51.7 4.2 %collective-permute-start.14 = (f32[8,128]{1,0:T(8,128)S(1)}, f32[8,128]{1,0:T(8,128)S(1)}, u32[]{:S(2)}, u32[]{:S(2)}) collective-permute-start(f32[8,128]{1,0:T(8,128)S(1)} %get-tuple-element.159), channel_id=1, source_target_pairs={{0,8},{8,16},{16,24},{24,0},{1,9},{9,17},{17,25},{25,1},{2,10},{10... | collective-permute-start | bytes 12296 | tf_op jit(solution)/shard_map/ppermute | solution.py:884
  52.7 3.3 %collective-permute-start.15 = (f32[8,128]{1,0:T(8,128)S(1)}, f32[8,128]{1,0:T(8,128)S(1)}, u32[]{:S(2)}, u32[]{:S(2)}) collective-permute-start(f32[8,128]{1,0:T(8,128)S(1)} %get-tuple-element.160), channel_id=1, source_target_pairs={{8,0},{16,8},{24,16},{0,24},{9,1},{17,9},{25,17},{1,25},{10,2},{18... | collective-permute-start | bytes 12296 | tf_op jit(solution)/shard_map/ppermute | solution.py:885
  56.0 5.5 %collective-permute-start.16 = (f32[8,256]{1,0:T(8,128)S(1)}, f32[8,256]{1,0:T(8,128)S(1)}, u32[]{:S(2)}, u32[]{:S(2)}) collective-permute-start(f32[8,256]{1,0:T(8,128)S(1)} %add.3.mid_ref), channel_id=1, source_target_pairs={{0,2},{2,4},{4,6},{6,0},{1,3},{3,5},{5,7},{7,1},{8,10},{10,12},{12... | collective-permute-start | bytes 24584 | tf_op jit(solution)/shard_map/ppermute | solution.py:891
  57.6 3.9 %collective-permute-start.17 = (f32[8,256]{1,0:T(8,128)S(1)}, f32[8,256]{1,0:T(8,128)S(1)}, u32[]{:S(2)}, u32[]{:S(2)}) collective-permute-start(f32[8,256]{1,0:T(8,128)S(1)} %add.3.mid_ref), channel_id=1, source_target_pairs={{2,0},{4,2},{6,4},{0,6},{3,1},{5,3},{7,5},{1,7},{10,8},{12,10},{14... | collective-permute-start | bytes 24584 | tf_op jit(solution)/shard_map/ppermute | solution.py:891
  61.5 3.7 %collective-permute-start.18 = (f32[8,256]{1,0:T(8,128)S(1)}, f32[8,256]{1,0:T(8,128)S(1)}, u32[]{:S(2)}, u32[]{:S(2)}) collective-permute-start(f32[8,256]{1,0:T(8,128)S(1)} %fold.1.mid_ref), channel_id=1, source_target_pairs={{0,1},{1,0},{2,3},{3,2},{4,5},{5,4},{6,7},{7,6},{8,9},{9,8},{10,11... | collective-permute-start | bytes 24584 | tf_op jit(solution)/shard_map/ppermute | solution.py:900
  (4 other events, 19.9 us)

commit v16 on v15

--- a/solution.py
+++ b/solution.py
@@ -213,26 +213,14 @@
                         across[kind, part, part] = flipped
 
 
-def fetch(pieces, cols, table, sems):
-    low, high, ghosts = 0, 0, table.shape[0]
+def joined(pieces, cols):
     if len(pieces) == 3:
-        rows = [(piece, 0, piece.shape[0]) for piece in pieces]
-    else:
-        low_in, low_out, mid, high_in, high_out = pieces
-        half = low_out.shape[0] // 2
-        rows = [(low_out, 0, half), (low_in, 0, low_in.shape[0]), (low_out, half, half)]
-        rows += [(mid, 0, mid.shape[0])]
-        rows += [(high_out, 0, half), (high_in, 0, high_in.shape[0]), (high_out, half, half)]
-    copies = []
-    at = 0
-    for index, (piece, start, count) in enumerate(rows):
-        source = piece.at[pl.ds(start, count), cols]
-        target = table.at[pl.ds(at, count), :]
-        copies.append(pltpu.make_async_copy(source, target, sems.at[index]))
-        at += count
-    for copy in copies:
-        copy.start()
-    return copies
+        return jnp.concatenate([piece[:, cols] for piece in pieces], axis=0)
+    low_in, low_out, mid, high_in, high_out = pieces
+    half = low_out.shape[0] // 2
+    parts = [low_out[0:half, cols], low_in[:, cols], low_out[half:, cols], mid[:, cols]]
+    parts += [high_out[0:half, cols], high_in[:, cols], high_out[half:, cols]]
+    return jnp.concatenate(parts, axis=0)
 
 
 def infos_of(group):
@@ -312,16 +300,18 @@
 
 
 def ghost_pairs(
-    group, own_ref, table, new_ref, new_base, oh_gh, d_gh, dt_gh, gate_ref, radials, nw_ref,
+    group, own_ref, pieces, skip, new_ref, new_base, oh_gh, d_gh, dt_gh, gate_ref, radials, nw_ref,
     steps, wm, wmt, wo, wot, nf_s, mx_s, acc_in, acc_s, gs_ref, dot_ref, grad_refs, en_ref,
 ):
     norm = 1.0 / math.sqrt(SLOTS)
+    cols = slice(skip, skip + GROUP_COLS[group])
     acc_s[...] = acc_in[...]
 
     def ghost_forward(step):
         here, _ = ghost_rows(step)
         messages = forward(
-            group, here, oh_gh[here, :], table[...], radials, gate_ref, wm, nf_s, mx_s, False
+            group, here, oh_gh[here, :], joined(pieces, cols), radials, gate_ref, wm, nf_s, mx_s,
+            False,
         )
         acc_s[...] += mm(dt_gh[:, here], jnp.concatenate(messages, axis=1))
 
@@ -350,11 +340,10 @@
     over_ghost_steps(steps, ghost_backward)
 
 
-def pair_scratch(atoms, half, ghosts, group):
+def pair_scratch(atoms, half, group):
     count, width = len(KINDS[group]), GROUP_COLS[group]
     return (
-        [pltpu.VMEM((ghosts, width), BF16), pltpu.SemaphoreType.DMA((7,))]
-        + [pltpu.VMEM((count, 2 * CH, 2 * CH), BF16) for _ in range(4)]
+        [pltpu.VMEM((count, 2 * CH, 2 * CH), BF16) for _ in range(4)]
         + [
             pltpu.VMEM((half, width), BF16),
             pltpu.VMEM((half, width), BF16),
@@ -477,12 +466,12 @@
     acc0_ref,
     new_ref, oh_gh, d_gh, dt_gh, pre_ref, unit_ref, gs0_ref, en_ref, m0_gh, gate_gh, nf0_gh,
     radial_gh1, radial_gh2, radial_gh3, radial_gh4,
-    table, sems, ghpos, acc_s,
+    ghpos, acc_s,
 ):
     radial_gh = (None, radial_gh1, radial_gh2, radial_gh3, radial_gh4)
-    copies = fetch((p0, p1, p2), slice(0, 2 * CH), table, sems)
+    pieces = (p0, p1, p2)
     atoms = own_ref.shape[0]
-    ghosts = table.shape[0]
+    ghosts = ghpos.shape[0]
     spacing = spacing_of(atoms, rbf_ref.shape[0])
     norm = 1.0 / math.sqrt(SLOTS)
 
@@ -519,9 +508,7 @@
     shift = jnp.where(lane == 14, side_of(ext_z, zcells + 1, 2.0 * zcells), shift)
     own0 = own_ref[:, 0:CH]
     acc_s[...] = acc0_ref[...]
-    for copy in copies:
-        copy.wait()
-    ghpos[...] = (table[:, CH:].astype(F32) + shift).astype(BF16)
+    ghpos[...] = (joined(pieces, slice(CH, 2 * CH)).astype(F32) + shift).astype(BF16)
 
     def ghost_start(step):
         here, _ = ghost_rows(step)
@@ -549,7 +536,7 @@
         for degree in range(1, 5):
             radial_gh[degree][here, :] = radial[:, degree * CH : (degree + 1) * CH]
         message = scalar_forward(
-            here, mm(onehot, table[:, 0:CH]), radial[:, 0:CH], mix_ref, m0_gh, gate_gh, nf0_gh
+            here, mm(onehot, joined(pieces, slice(0, CH))), radial[:, 0:CH], mix_ref, m0_gh, gate_gh, nf0_gh
         )
         acc_s[...] += mm(spread, message.astype(BF16))
 
@@ -563,12 +550,6 @@
     en_ref[...] = weight0 * updated0 * logistic
     grad0 = (weight0 * logistic * (1.0 + updated0 * (1.0 - logistic))).astype(BF16)
     gs0_ref[...] = mm_nt(grad0, out_ref[0]) * norm
-
-
-def any_specs(count, total):
-    return [pl.BlockSpec(memory_space=pl.ANY)] * count + [
-        pl.BlockSpec(memory_space=SPACE)
-    ] * (total - count)
 
 
 def start_stage(pieces, feats, *rest):
@@ -586,15 +567,12 @@
         struct(atoms, CH),
     ) + (struct(half, CH, dtype=BF16),) * 7
     scratch = [
-        pltpu.VMEM((ghosts, 2 * CH), BF16),
-        pltpu.SemaphoreType.DMA((7,)),
         pltpu.VMEM((ghosts, CH), BF16),
         pltpu.VMEM((atoms, CH), F32),
     ]
     args = tuple(pieces) + (feats,) + rest
     return call(
-        start_kernel, "ghost_start", out_shape, scratch, args,
-        any_specs(len(pieces), len(args)), 24,
+        start_kernel, "ghost_start", out_shape, scratch, args, limit=24
     )
 
 
@@ -610,15 +588,12 @@
     if group == 0:
         dot_own, refs = refs[0], refs[1:]
         grads_own, refs = dict(zip(degrees, refs)), refs[len(degrees) :]
-    table, sems, wm, wmt, wo, wot, nf_s, mx_s, acc_s = refs
-    copies = fetch(pieces, slice(skip, skip + GROUP_COLS[group]), table, sems)
+    wm, wmt, wo, wot, nf_s, mx_s, acc_s = refs
     block_diagonal(KINDS[group], mix_ref, wm, wmt)
     block_diagonal(KINDS[group], out_ref, wo, wot)
     en_ref[...] = jnp.zeros_like(en_ref)
-    for copy in copies:
-        copy.wait()
     ghost_pairs(
-        group, own_ref, table, new_ref, group_cols(group).start, oh_gh, d_gh, dt_gh, gate_gh,
+        group, own_ref, pieces, skip, new_ref, group_cols(group).start, oh_gh, d_gh, dt_gh, gate_gh,
         radials, nw_ref, step_count(meta_ref), wm, wmt, wo, wot, nf_s, mx_s, acc_own, acc_s,
         gs_ref, dot_gh, grads, en_ref,
     )
@@ -642,8 +617,7 @@
     args += tuple(radial_gh[degree - 1] for degree in degrees)
     new, energy, gs, *rest = call(
         functools.partial(pairs_kernel, group, len(pieces), skip), "pairs_" + "abc"[group],
-        out_shape, pair_scratch(atoms, half, ghosts, group), args,
-        any_specs(len(pieces), len(args)), 24,
+        out_shape, pair_scratch(atoms, half, group), args, limit=24,
     )
     return new, energy, gs, rest[: 1 + len(degrees)], rest[1 + len(degrees) :]
 
@@ -715,9 +689,9 @@
     gr_a, refs = refs[:before], refs[before:]
     radials, refs = dict(zip(degrees, refs)), refs[len(degrees) :]
     new_ref, energy_ref, src_ref, onto_ref, flow_ref, fmid_ref, fhigh_ref, gs_ref = refs[:8]
-    table, sems, wm, wmt, wo, wot, nf_s, mx_s, acc_s, dot_c, en_s, fgh_s = refs[8:20]
-    grads = dict(zip(degrees, refs[20:]))
-    copies = fetch((p0, p1, p2, p3, p4), slice(0, GROUP_COLS[group]), table, sems)
+    wm, wmt, wo, wot, nf_s, mx_s, acc_s, dot_c, en_s, fgh_s = refs[8:18]
+    grads = dict(zip(degrees, refs[18:]))
+    pieces = (p0, p1, p2, p3, p4)
     atoms = own_ref.shape[0]
     spacing = spacing_of(atoms, rbft_ref.shape[1])
     block_diagonal(KINDS[group], mix_ref, wm, wmt)
@@ -729,10 +703,8 @@
         at += part.shape[1]
     steps = step_count(meta_ref)
 
-    for copy in copies:
-        copy.wait()
     ghost_pairs(
-        group, own_ref, table, new_ref, 0, oh_gh, d_gh, dt_gh, gate_gh, radials, nw_ref,
+        group, own_ref, pieces, 0, new_ref, 0, oh_gh, d_gh, dt_gh, gate_gh, radials, nw_ref,
         steps, wm, wmt, wo, wot, nf_s, mx_s, acc_own, acc_s, gs_ref, dot_c, grads, en_s,
     )
     energy_ref[...] = jnp.sum(en_s[...].T, axis=0, keepdims=True)
@@ -748,7 +720,7 @@
         grad = mm(d_gh[here, :], gs0_low)
         pull, top, rest = finish(
             grad, m0_ref[here, :], nf0_ref[here, :], sum_of((dot_a, dot_c), here),
-            degree_parts(gr_a + refs[20:], here), pre_gh[here, :], unit_gh[here, :], spacing,
+            degree_parts(gr_a + refs[18:], here), pre_gh[here, :], unit_gh[here, :], spacing,
             radt_ref, rbft_ref, mix_t,
         )
         pull_top = pull.astype(BF16)
@@ -778,7 +750,7 @@
     ) + tuple(struct(8, size) for size in sizes) + (
         struct(atoms, GROUP_COLS[1], dtype=BF16),
     )
-    scratch = pair_scratch(atoms, half, ghosts, 1) + [
+    scratch = pair_scratch(atoms, half, 1) + [
         pltpu.VMEM((half, CH), BF16),
         pltpu.VMEM((atoms, CH), F32),
         pltpu.VMEM((8, ghosts), F32),
@@ -786,8 +758,7 @@
     scratch += [pltpu.VMEM((half, CH), BF16)] * len(DEGREES[1])
     args = tuple(pieces) + (feats,) + rest
     return call(
-        third_kernel, "third_group", out_shape, scratch, args,
-        any_specs(len(pieces), len(args)), 28,
+        third_kernel, "third_group", out_shape, scratch, args, limit=28
     )
 
 
@@ -932,14 +903,14 @@
     z1, y1_in, oh_own = hold((z1, y1_in, oh_own))
     block1 = jnp.concatenate([z1[0], block1, z1[1]], axis=2)
     x1_in = neighbours_of(block1, "gx", 0)
-    y0, z1, oh_own = hold((y0, z1, oh_own))
+    (m0_own, gate_own, nf0_own, acc0), (own_a,) = own_forward_stage(
+        (0,), feats, mix_weight, oh_own, radial_own
+    )
+    y0, z1, gate_own = hold((y0, z1, gate_own))
     middle = jnp.concatenate([y0[0], block0, y0[1]], axis=1)
     x0 = neighbours_of(middle, "gx", 0)
     y1_out = neighbours_of(jnp.concatenate(z1, axis=2), "gy", 1)
-    x1_in, oh_own = hold((x1_in, oh_own))
-    (m0_own, gate_own, nf0_own, acc0), (own_a,) = own_forward_stage(
-        (0,), feats, mix_weight, oh_own, radial_own
-    )
+    x1_in, gate_own = hold((x1_in, gate_own))
     _, (own_b,) = own_forward_stage((1,), feats, mix_weight, oh_own, radial_own, gate_own)
     x0, y1_out, acc0, acc_b = hold((x0, y1_out, acc0, own_b[2]))
     pieces0 = tuple(flat_rows(piece) for piece in (x0[0], middle, x0[1]))

time: 66.2 us -> 64.7 us (0.977)
  Pallas kernels: 29.1 us -> 27.5 us
  waiting for transfers between devices: 4.76 us -> 5.43 us
    pallas_call x13, Pallas kernels: 29.1 us -> 27.5 us  [call(): pl.pallas_call(kernel, out_shape=out_shape, in_specs=specs or [pl.BlockSp...]
    ppermute x6, waiting for transfers between devices: 0.82 us -> 2.28 us  [neighbours_of(): lax.ppermute(lax.slice_in_dim(block, length - 1, length, axis=dim), axis,...]
    ppermute x6, waiting for transfers between devices: 2.79 us -> 1.69 us  [neighbours_of(): after = lax.ppermute(lax.slice_in_dim(block, 0, 1, axis=dim), axis, down)]
where the time goes in v16:
time: 64.7 us; the launch traced here: 64.4 us
  Pallas kernels  27.5 us (43%)
  starting transfers between devices  27.4 us (42%)
  waiting for transfers between devices  5.43 us (8%)
  local copies, waits for them, and re-layouts  1.97 us (3%)
  other arithmetic  1.15 us (2%)
  between operations  0.92 us (1%)
    pallas_call x13, Pallas kernels, call(): pl.pallas_call(kernel, out_shape=out_shape, in_specs=specs or [pl.BlockSp...  27.5 us
    ppermute x6, starting transfers between devices, neighbours_of(): after = lax.ppermute(lax.slice_in_dim(block, 0, 1, axis=dim), axis, down)  11.8 us
    ppermute x6, starting transfers between devices, neighbours_of(): lax.ppermute(lax.slice_in_dim(block, length - 1, length, axis=dim), axis,...  5.57 us
    ppermute x2, starting transfers between devices, give_back_y(): return (mid, lax.ppermute(mid, 'gy', up), lax.ppermute(mid, 'gy', down))  3.89 us
    ppermute x2, starting transfers between devices, neighbours_of(): other = lax.ppermute(block, axis, up)  3.13 us
    ppermute x6, waiting for transfers between devices, neighbours_of(): lax.ppermute(lax.slice_in_dim(block, length - 1, length, axis=dim), axis,...  2.28 us
    unnamed x19, local copies, waits for them, and re-layouts  1.73 us
    ppermute x6, waiting for transfers between devices, neighbours_of(): after = lax.ppermute(lax.slice_in_dim(block, 0, 1, axis=dim), axis, down)  1.69 us
  transfers between devices with their start and end apart: 19, of which 9 were waited for; matrix products, arithmetic and copies ran while one was open for 1% of the time, Pallas kernels for 31%

profile of v16, /device:TPU:0, one launch (start us, length us, event | category | flops | bytes accessed | tf_op | source)
XLA Modules:
  0.0 64.4 jit_solution(18340453588905757240)
XLA Ops:
  3.4 3.0 %collective-permute-start.3 = (bf16[2,2,2,8,1280]{4,3,2,1,0:T(8,128)(2,1)S(1)}, bf16[2,2,2,8,1280]{4,3,2,1,0:T(8,128)(2,1)S(1)}, u32[]{:S(2)}, u32[]{:S(2)}) collective-permute-start(bf16[2,2,2,8,1280]{4,3,2,1,0:T(8,128)(2,1)S(1)} %bitcast.41), channel_id=1, source_target_pairs={{0,1},{1,0},{2,3},{3,2},{4,5},{5,4},{6,7},{7,6},{8,9},{9,8},{10,11... | collective-permute-start | bytes 491528 | tf_op jit(solution)/shard_map/ppermute | solution.py:807
  6.8 2.1 %collective-permute-start.1 = (bf16[2,1,2,8,2048]{4,3,2,1,0:T(8,128)(2,1)S(1)}, bf16[2,1,2,8,2048]{4,3,2,1,0:T(8,128)(2,1)S(1)}, u32[]{:S(2)}, u32[]{:S(2)}) collective-permute-start(bf16[2,1,2,8,2048]{4,3,2,1,0:T(8,128)(2,1)S(1)} %get-tuple-element.201), channel_id=1, source_target_pairs={{0,2},{2,4},{4,6},{6,0},{1,3},{3,5},{5,7},{7,1},{8,10},{10,12},{12... | collective-permute-start | bytes 393224 | tf_op jit(solution)/shard_map/ppermute | solution.py:812
  8.9 2.1 %collective-permute-start.2 = (bf16[2,1,2,8,2048]{4,3,2,1,0:T(8,128)(2,1)S(1)}, bf16[2,1,2,8,2048]{4,3,2,1,0:T(8,128)(2,1)S(1)}, u32[]{:S(2)}, u32[]{:S(2)}) collective-permute-start(bf16[2,1,2,8,2048]{4,3,2,1,0:T(8,128)(2,1)S(1)} %get-tuple-element.200), channel_id=1, source_target_pairs={{2,0},{4,2},{6,4},{0,6},{3,1},{5,3},{7,5},{1,7},{10,8},{12,10},{14... | collective-permute-start | bytes 393224 | tf_op jit(solution)/shard_map/ppermute | solution.py:813
  11.6 2.2 %collective-permute-start.6 = (bf16[2,1,4,8,1280]{4,3,2,1,0:T(8,128)(2,1)S(1)}, bf16[2,1,4,8,1280]{4,3,2,1,0:T(8,128)(2,1)S(1)}, u32[]{:S(2)}, u32[]{:S(2)}) collective-permute-start(bf16[2,1,4,8,1280]{4,3,2,1,0:T(8,128)(2,1)S(1)} %get-tuple-element.197), channel_id=1, source_target_pairs={{0,2},{2,4},{4,6},{6,0},{1,3},{3,5},{5,7},{7,1},{8,10},{10,12},{12... | collective-permute-start | bytes 491528 | tf_op jit(solution)/shard_map/ppermute | solution.py:812
  13.7 2.1 %collective-permute-start.7 = (bf16[2,1,4,8,1280]{4,3,2,1,0:T(8,128)(2,1)S(1)}, bf16[2,1,4,8,1280]{4,3,2,1,0:T(8,128)(2,1)S(1)}, u32[]{:S(2)}, u32[]{:S(2)}) collective-permute-start(bf16[2,1,4,8,1280]{4,3,2,1,0:T(8,128)(2,1)S(1)} %get-tuple-element.196), channel_id=1, source_target_pairs={{2,0},{4,2},{6,4},{0,6},{3,1},{5,3},{7,5},{1,7},{10,8},{12,10},{14... | collective-permute-start | bytes 491528 | tf_op jit(solution)/shard_map/ppermute | solution.py:813
  15.8 2.9 %own_edges.1 = (bf16[1024,64]{1,0:T(8,128)(2,1)S(1)}, bf16[1024,128]{1,0:T(8,128)(2,1)S(1)}, f32[1024,128]{1,0:T(8,128)S(1)}, bf16[640,128]{1,0:T(8,128)(2,1)S(1...) custom-call(f32[64,128]{1,0:T(8,128)S(1)} %get-tuple-element.99.meta, ...), custom_call_target="tpu_custom_call" | custom-call | flops 1024 | bytes 1024 | tf_op jit(solution)/shard_map/own_edges/pallas_call | solution.py:57
  19.4 1.7 %collective-permute-start.5 = (bf16[1,2,4,8,2048]{4,3,2,1,0:T(8,128)(2,1)S(1)}, bf16[1,2,4,8,2048]{4,3,2,1,0:T(8,128)(2,1)S(1)}, u32[]{:S(2)}, u32[]{:S(2)}) collective-permute-start(bf16[1,2,4,8,2048]{4,3,2,1,0:T(8,128)(2,1)S(1)} %get-tuple-element.194), channel_id=1, source_target_pairs={{8,0},{16,8},{24,16},{0,24},{9,1},{17,9},{25,17},{1,25},{10,2},{18... | collective-permute-start | bytes 786440 | tf_op jit(solution)/shard_map/ppermute | solution.py:813
  21.1 1.5 %own_forward_a.1 = (bf16[1024,128]{1,0:T(8,128)(2,1)S(1)}, bf16[1024,128]{1,0:T(8,128)(2,1)S(1)}, bf16[1024,128]{1,0:T(8,128)(2,1)S(1)}, f32[64,128]{1,0:T(8,128...) custom-call(bf16[64,3200]{1,0:T(8,128)(2,1)S(1)} %bitcast.25, ...), custom_call_target="tpu_custom_call" | custom-call | flops 1024 | bytes 1024 | tf_op jit(solution)/shard_map/own_forward_a/pallas_call | solution.py:57
  23.4 1.7 %collective-permute-start.9 = (bf16[1,4,4,8,1280]{4,3,2,1,0:T(8,128)(2,1)S(1)}, bf16[1,4,4,8,1280]{4,3,2,1,0:T(8,128)(2,1)S(1)}, u32[]{:S(2)}, u32[]{:S(2)}) collective-permute-start(bf16[1,4,4,8,1280]{4,3,2,1,0:T(8,128)(2,1)S(1)} %get-tuple-element.190), channel_id=1, source_target_pairs={{8,0},{16,8},{24,16},{0,24},{9,1},{17,9},{25,17},{1,25},{10,2},{18... | collective-permute-start | bytes 983048 | tf_op jit(solution)/shard_map/ppermute | solution.py:813
  25.2 1.2 %collective-permute-start.10 = (bf16[2,1,2,8,2048]{4,3,2,1,0:T(8,128)(2,1)S(1)}, bf16[2,1,2,8,2048]{4,3,2,1,0:T(8,128)(2,1)S(1)}, u32[]{:S(2)}, u32[]{:S(2)}) collective-permute-start(bf16[2,1,2,8,2048]{4,3,2,1,0:T(8,128)(2,1)S(1)} %get-tuple-element.199), channel_id=1, source_target_pairs={{0,2},{2,4},{4,6},{6,0},{1,3},{3,5},{5,7},{7,1},{8,10},{10,12},{12... | collective-permute-start | bytes 393224 | tf_op jit(solution)/shard_map/ppermute | solution.py:812
  26.4 2.6 %collective-permute-start.11 = (bf16[2,1,2,8,2048]{4,3,2,1,0:T(8,128)(2,1)S(1)}, bf16[2,1,2,8,2048]{4,3,2,1,0:T(8,128)(2,1)S(1)}, u32[]{:S(2)}, u32[]{:S(2)}) collective-permute-start(bf16[2,1,2,8,2048]{4,3,2,1,0:T(8,128)(2,1)S(1)} %get-tuple-element.198), channel_id=1, source_target_pairs={{2,0},{4,2},{6,4},{0,6},{3,1},{5,3},{7,5},{1,7},{10,8},{12,10},{14... | collective-permute-start | bytes 393224 | tf_op jit(solution)/shard_map/ppermute | solution.py:813
  29.0 2.5 %own_forward_b.1 = (bf16[1024,2048]{1,0:T(8,128)(2,1)S(1)}, bf16[1024,2048]{1,0:T(8,128)(2,1)S(1)}, f32[64,2048]{1,0:T(8,128)S(1)}) custom-call(bf16[64,3200]{1,0:T(8,128)(2,1)S(1)} %bitcast.26, bf16[5,128,128]{2,1,0:T(8,128)(2,1)S(1)} %copy-done.2, bf16[1024,64]{1,0:T(8,128)(2,1)S(1)} %get-tuple-element.106.refs_2_.oh_own, ...), custom_call_target="tpu_custom_call" | custom-call | flops 1024 | bytes 1024 | tf_op jit(solution)/shard_map/own_forward_b/pallas_call | solution.py:57
  31.6 1.9 %collective-permute-done.10 = bf16[2,1,2,8,2048]{4,3,2,1,0:T(8,128)(2,1)S(1)} collective-permute-done((bf16[2,1,2,8,2048]{4,3,2,1,0:T(8,128)(2,1)S(1)}, bf16[2,1,2,8,2048]{4,3,2,1,0:T(8,128)(2,1)S(1)}, u32[]{:S(2)}, u32[]{:S(2)}) %collective-permute-start.10) | collective-permute-done | bytes 131104 | tf_op jit(solution)/shard_map/ppermute | solution.py:812
  34.3 1.5 %collective-permute-start.13 = (bf16[1,2,4,8,2048]{4,3,2,1,0:T(8,128)(2,1)S(1)}, bf16[1,2,4,8,2048]{4,3,2,1,0:T(8,128)(2,1)S(1)}, u32[]{:S(2)}, u32[]{:S(2)}) collective-permute-start(bf16[1,2,4,8,2048]{4,3,2,1,0:T(8,128)(2,1)S(1)} %get-tuple-element.192), channel_id=1, source_target_pairs={{8,0},{16,8},{24,16},{0,24},{9,1},{17,9},{25,17},{1,25},{10,2},{18... | collective-permute-start | bytes 786440 | tf_op jit(solution)/shard_map/ppermute | solution.py:813
  35.8 3.3 %ghost_start.1 = (bf16[64,128]{1,0:T(8,128)(2,1)S(1)}, bf16[1024,512]{1,0:T(8,128)(2,1)S(1)}, bf16[1024,64]{1,0:T(8,128)(2,1)S(1)}, bf16[64,1024]{1,0:T(8,128)(2...) custom-call(bf16[128,1280]{1,0:T(8,128)(2,1)S(1)} %bitcast.37, ...), custom_call_target="tpu_custom_call" | custom-call | flops 1024 | bytes 1024 | tf_op jit(solution)/shard_map/ghost_start/pallas_call | solution.py:57
  39.2 4.1 %pairs_a.1 = (bf16[64,1024]{1,0:T(8,128)(2,1)S(1)}, f32[64,128]{1,0:T(8,128)S(1)}, bf16[64,1024]{1,0:T(8,128)(2,1)}, bf16[1024,128]{1,0:T(8,128)(2,1)S(1)}, bf16...) custom-call(bf16[128,1280]{1,0:T(8,128)(2,1)S(1)} %bitcast.38, ...), custom_call_target="tpu_custom_call" | custom-call | flops 1024 | bytes 1024 | tf_op jit(solution)/shard_map/pairs_a/pallas_call | solution.py:57
  43.8 6.6 %third_group.1 = (bf16[64,3200]{1,0:T(8,128)(2,1)}, f32[1,64]{1,0:T(1,128)}, f32[64,128]{1,0:T(8,128)S(1)}, f32[8,64]{1,0:T(8,128)S(1)}, f32[8,128]{1,0:T(8,128)...) custom-call(bf16[64,2048]{1,0:T(8,128)(2,1)S(1)} %bitcast.44, ...), custom_call_target="tpu_custom_call" | custom-call | flops 1024 | bytes 1024 | tf_op jit(solution)/shard_map/third_group/pallas_call | solution.py:57
  51.0 1.1 %collective-permute-start.15 = (f32[8,128]{1,0:T(8,128)S(1)}, f32[8,128]{1,0:T(8,128)S(1)}, u32[]{:S(2)}, u32[]{:S(2)}) collective-permute-start(f32[8,128]{1,0:T(8,128)S(1)} %get-tuple-element.160), channel_id=1, source_target_pairs={{8,0},{16,8},{24,16},{0,24},{9,1},{17,9},{25,17},{1,25},{10,2},{18... | collective-permute-start | bytes 12296 | tf_op jit(solution)/shard_map/ppermute | solution.py:856
  52.2 2.2 %own_backward_b.1 = (bf16[1024,128]{1,0:T(8,128)(2,1)S(1)}, bf16[1024,128]{1,0:T(8,128)(2,1)S(1)}, bf16[1024,128]{1,0:T(8,128)(2,1)S(1)}) custom-call(bf16[5,128,128]{2,1,0:T(8,128)(2,1)S(1)} %copy-done.2, bf16[64,2048]{1,0:T(8,128)(2,1)S(1)} %get-tuple-element.161.gs_ref, bf16[1024,128]{1,0:T(8,128)(2,1)S(1)} %get-tuple-element.120.refs_8_.refs_12_.gate_ref, ...), custom_call_target="tpu_custom_call" | custom-call | flops 1024 | bytes 1024 | tf_op jit(solution)/shard_map/own_backward_b/pallas_call | solution.py:57
  54.4 1.3 %collective-permute-start.16 = (f32[8,256]{1,0:T(8,128)S(1)}, f32[8,256]{1,0:T(8,128)S(1)}, u32[]{:S(2)}, u32[]{:S(2)}) collective-permute-start(f32[8,256]{1,0:T(8,128)S(1)} %add.3.mid_ref), channel_id=1, source_target_pairs={{0,2},{2,4},{4,6},{6,0},{1,3},{3,5},{5,7},{7,1},{8,10},{10,12},{12... | collective-permute-start | bytes 24584 | tf_op jit(solution)/shard_map/ppermute | solution.py:862
  55.7 2.6 %collective-permute-start.17 = (f32[8,256]{1,0:T(8,128)S(1)}, f32[8,256]{1,0:T(8,128)S(1)}, u32[]{:S(2)}, u32[]{:S(2)}) collective-permute-start(f32[8,256]{1,0:T(8,128)S(1)} %add.3.mid_ref), channel_id=1, source_target_pairs={{2,0},{4,2},{6,4},{0,6},{3,1},{5,3},{7,5},{1,7},{10,8},{12,10},{14... | collective-permute-start | bytes 24584 | tf_op jit(solution)/shard_map/ppermute | solution.py:862
  58.3 1.5 %own_back.2 = (f32[64,128]{1,0:T(8,128)S(1)}, f32[8,64]{1,0:T(8,128)S(1)}) custom-call(bf16[1024,64]{1,0:T(8,128)(2,1)S(1)} %get-tuple-element.106.refs_2_.oh_own, bf16[1024,128]{1,0:T(8,128)(2,1)S(1)} %get-tuple-element.166.pre_own, f32[1024,128]{1,0:T(8,128)S(1)} %get-tuple-element.167.unit_own, bf16[640,128]{1,0:T(8,128)(2,1)S(1)} %get-tuple-element.135.radt_ref, ...), custom_call_target="tpu_custom_call" | custom-call | flops 1024 | bytes 1024 | tf_op jit(solution)/shard_map/own_back/pallas_call | solution.py:57
  60.0 1.2 %collective-permute-start.18 = (f32[8,256]{1,0:T(8,128)S(1)}, f32[8,256]{1,0:T(8,128)S(1)}, u32[]{:S(2)}, u32[]{:S(2)}) collective-permute-start(f32[8,256]{1,0:T(8,128)S(1)} %fold.1.mid_ref), channel_id=1, source_target_pairs={{0,1},{1,0},{2,3},{3,2},{4,5},{5,4},{6,7},{7,6},{8,9},{9,8},{10,11... | collective-permute-start | bytes 24584 | tf_op jit(solution)/shard_map/ppermute | solution.py:871
  61.2 1.5 %own_back.3 = (f32[64,128]{1,0:T(8,128)S(1)}, f32[8,64]{1,0:T(8,128)S(1)}) custom-call(bf16[1024,64]{1,0:T(8,128)(2,1)S(1)} %get-tuple-element.106.refs_2_.oh_own, bf16[1024,128]{1,0:T(8,128)(2,1)S(1)} %get-tuple-element.166.pre_own, f32[1024,128]{1,0:T(8,128)S(1)} %get-tuple-element.167.unit_own, bf16[640,128]{1,0:T(8,128)(2,1)S(1)} %get-tuple-element.135.radt_ref, ...), custom_call_target="tpu_custom_call" | custom-call | flops 1024 | bytes 1024 | tf_op jit(solution)/shard_map/own_back/pallas_call | solution.py:57
  (64 shorter events, 8.9 us)
Async XLA Ops:
  3.4 8.1 %collective-permute-start.3 = (bf16[2,2,2,8,1280]{4,3,2,1,0:T(8,128)(2,1)S(1)}, bf16[2,2,2,8,1280]{4,3,2,1,0:T(8,128)(2,1)S(1)}, u32[]{:S(2)}, u32[]{:S(2)}) collective-permute-start(bf16[2,2,2,8,1280]{4,3,2,1,0:T(8,128)(2,1)S(1)} %bitcast.41), channel_id=1, source_target_pairs={{0,1},{1,0},{2,3},{3,2},{4,5},{5,4},{6,7},{7,6},{8,9},{9,8},{10,11... | collective-permute-start | bytes 491528 | tf_op jit(solution)/shard_map/ppermute | solution.py:807
  6.7 14.5 %copy-start.1 = (bf16[1,1,1,64,3200]{4,3,2,1,0:T(8,128)(2,1)S(1)}, bf16[1,1,1,64,3200]{4,3,2,1,0:T(8,128)(2,1)}, u32[]{:S(2)}) copy-start(bf16[1,1,1,64,3200]{4,3,2,1,0:T(8,128)(2,1)} %param.11) | copy-start | bytes 1228804
  6.7 14.5 %copy-start.2 = (bf16[5,128,128]{2,1,0:T(8,128)(2,1)S(1)}, bf16[5,128,128]{2,1,0:T(8,128)(2,1)}, u32[]{:S(2)}) copy-start(bf16[5,128,128]{2,1,0:T(8,128)(2,1)} %mix_ref.9) | copy-start | bytes 491524
  6.7 12.0 %collective-permute-start = (bf16[2,2,2,8,2048]{4,3,2,1,0:T(8,128)(2,1)S(1)}, bf16[2,2,2,8,2048]{4,3,2,1,0:T(8,128)(2,1)S(1)}, u32[]{:S(2)}, u32[]{:S(2)}) collective-permute-start(bf16[2,2,2,8,2048]{4,3,2,1,0:T(8,128)(2,1)S(1)} %bitcast.33), channel_id=1, source_target_pairs={{0,1},{1,0},{2,3},{3,2},{4,5},{5,4},{6,7},{7,6},{8,9},{9,8},{10,11... | collective-permute-start | bytes 786440 | tf_op jit(solution)/shard_map/ppermute | solution.py:807
  6.8 11.9 %collective-permute-start.1 = (bf16[2,1,2,8,2048]{4,3,2,1,0:T(8,128)(2,1)S(1)}, bf16[2,1,2,8,2048]{4,3,2,1,0:T(8,128)(2,1)S(1)}, u32[]{:S(2)}, u32[]{:S(2)}) collective-permute-start(bf16[2,1,2,8,2048]{4,3,2,1,0:T(8,128)(2,1)S(1)} %get-tuple-element.201), channel_id=1, source_target_pairs={{0,2},{2,4},{4,6},{6,0},{1,3},{3,5},{5,7},{7,1},{8,10},{10,12},{12... | collective-permute-start | bytes 393224 | tf_op jit(solution)/shard_map/ppermute | solution.py:812
  8.9 10.3 %collective-permute-start.2 = (bf16[2,1,2,8,2048]{4,3,2,1,0:T(8,128)(2,1)S(1)}, bf16[2,1,2,8,2048]{4,3,2,1,0:T(8,128)(2,1)S(1)}, u32[]{:S(2)}, u32[]{:S(2)}) collective-permute-start(bf16[2,1,2,8,2048]{4,3,2,1,0:T(8,128)(2,1)S(1)} %get-tuple-element.200), channel_id=1, source_target_pairs={{2,0},{4,2},{6,4},{0,6},{3,1},{5,3},{7,5},{1,7},{10,8},{12,10},{14... | collective-permute-start | bytes 393224 | tf_op jit(solution)/shard_map/ppermute | solution.py:813
  11.6 11.1 %collective-permute-start.6 = (bf16[2,1,4,8,1280]{4,3,2,1,0:T(8,128)(2,1)S(1)}, bf16[2,1,4,8,1280]{4,3,2,1,0:T(8,128)(2,1)S(1)}, u32[]{:S(2)}, u32[]{:S(2)}) collective-permute-start(bf16[2,1,4,8,1280]{4,3,2,1,0:T(8,128)(2,1)S(1)} %get-tuple-element.197), channel_id=1, source_target_pairs={{0,2},{2,4},{4,6},{6,0},{1,3},{3,5},{5,7},{7,1},{8,10},{10,12},{12... | collective-permute-start | bytes 491528 | tf_op jit(solution)/shard_map/ppermute | solution.py:812
  13.7 9.4 %collective-permute-start.7 = (bf16[2,1,4,8,1280]{4,3,2,1,0:T(8,128)(2,1)S(1)}, bf16[2,1,4,8,1280]{4,3,2,1,0:T(8,128)(2,1)S(1)}, u32[]{:S(2)}, u32[]{:S(2)}) collective-permute-start(bf16[2,1,4,8,1280]{4,3,2,1,0:T(8,128)(2,1)S(1)} %get-tuple-element.196), channel_id=1, source_target_pairs={{2,0},{4,2},{6,4},{0,6},{3,1},{5,3},{7,5},{1,7},{10,8},{12,10},{14... | collective-permute-start | bytes 491528 | tf_op jit(solution)/shard_map/ppermute | solution.py:813
  19.3 7.1 %collective-permute-start.4 = (bf16[1,2,4,8,2048]{4,3,2,1,0:T(8,128)(2,1)S(1)}, bf16[1,2,4,8,2048]{4,3,2,1,0:T(8,128)(2,1)S(1)}, u32[]{:S(2)}, u32[]{:S(2)}) collective-permute-start(bf16[1,2,4,8,2048]{4,3,2,1,0:T(8,128)(2,1)S(1)} %get-tuple-element.195), channel_id=1, source_target_pairs={{0,8},{8,16},{16,24},{24,0},{1,9},{9,17},{17,25},{25,1},{2,10},{10... | collective-permute-start | bytes 786440 | tf_op jit(solution)/shard_map/ppermute | solution.py:812
  19.4 9.7 %collective-permute-start.5 = (bf16[1,2,4,8,2048]{4,3,2,1,0:T(8,128)(2,1)S(1)}, bf16[1,2,4,8,2048]{4,3,2,1,0:T(8,128)(2,1)S(1)}, u32[]{:S(2)}, u32[]{:S(2)}) collective-permute-start(bf16[1,2,4,8,2048]{4,3,2,1,0:T(8,128)(2,1)S(1)} %get-tuple-element.194), channel_id=1, source_target_pairs={{8,0},{16,8},{24,16},{0,24},{9,1},{17,9},{25,17},{1,25},{10,2},{18... | collective-permute-start | bytes 786440 | tf_op jit(solution)/shard_map/ppermute | solution.py:813
  23.1 12.7 %copy-start.3 = (bf16[5,128,128]{2,1,0:T(8,128)(2,1)S(1)}, bf16[5,128,128]{2,1,0:T(8,128)(2,1)}, u32[]{:S(2)}) copy-start(bf16[5,128,128]{2,1,0:T(8,128)(2,1)} %out_ref.3) | copy-start | bytes 491524
  23.1 12.7 %copy-start.8 = (f32[128]{0:T(128)S(1)}, f32[128]{0:T(128)}, u32[]{:S(2)}) copy-start(f32[128]{0:T(128)} %param.20) | copy-start | bytes 1540
  23.3 15.8 %copy-start.6 = (f32[4,128]{1,0:T(4,128)S(1)}, f32[4,128]{1,0:T(4,128)}, u32[]{:S(2)}) copy-start(f32[4,128]{1,0:T(4,128)} %nw_ref.1) | copy-start | bytes 6148
  23.3 10.8 %collective-permute-start.8 = (bf16[1,4,4,8,1280]{4,3,2,1,0:T(8,128)(2,1)S(1)}, bf16[1,4,4,8,1280]{4,3,2,1,0:T(8,128)(2,1)S(1)}, u32[]{:S(2)}, u32[]{:S(2)}) collective-permute-start(bf16[1,4,4,8,1280]{4,3,2,1,0:T(8,128)(2,1)S(1)} %get-tuple-element.191), channel_id=1, source_target_pairs={{0,8},{8,16},{16,24},{24,0},{1,9},{9,17},{17,25},{25,1},{2,10},{10... | collective-permute-start | bytes 983048 | tf_op jit(solution)/shard_map/ppermute | solution.py:812
  23.4 10.8 %collective-permute-start.9 = (bf16[1,4,4,8,1280]{4,3,2,1,0:T(8,128)(2,1)S(1)}, bf16[1,4,4,8,1280]{4,3,2,1,0:T(8,128)(2,1)S(1)}, u32[]{:S(2)}, u32[]{:S(2)}) collective-permute-start(bf16[1,4,4,8,1280]{4,3,2,1,0:T(8,128)(2,1)S(1)} %get-tuple-element.190), channel_id=1, source_target_pairs={{8,0},{16,8},{24,16},{0,24},{9,1},{17,9},{25,17},{1,25},{10,2},{18... | collective-permute-start | bytes 983048 | tf_op jit(solution)/shard_map/ppermute | solution.py:813
  25.2 8.2 %collective-permute-start.10 = (bf16[2,1,2,8,2048]{4,3,2,1,0:T(8,128)(2,1)S(1)}, bf16[2,1,2,8,2048]{4,3,2,1,0:T(8,128)(2,1)S(1)}, u32[]{:S(2)}, u32[]{:S(2)}) collective-permute-start(bf16[2,1,2,8,2048]{4,3,2,1,0:T(8,128)(2,1)S(1)} %get-tuple-element.199), channel_id=1, source_target_pairs={{0,2},{2,4},{4,6},{6,0},{1,3},{3,5},{5,7},{7,1},{8,10},{10,12},{12... | collective-permute-start | bytes 393224 | tf_op jit(solution)/shard_map/ppermute | solution.py:812
  26.4 7.7 %collective-permute-start.11 = (bf16[2,1,2,8,2048]{4,3,2,1,0:T(8,128)(2,1)S(1)}, bf16[2,1,2,8,2048]{4,3,2,1,0:T(8,128)(2,1)S(1)}, u32[]{:S(2)}, u32[]{:S(2)}) collective-permute-start(bf16[2,1,2,8,2048]{4,3,2,1,0:T(8,128)(2,1)S(1)} %get-tuple-element.198), channel_id=1, source_target_pairs={{2,0},{4,2},{6,4},{0,6},{3,1},{5,3},{7,5},{1,7},{10,8},{12,10},{14... | collective-permute-start | bytes 393224 | tf_op jit(solution)/shard_map/ppermute | solution.py:813
  34.3 9.1 %collective-permute-start.13 = (bf16[1,2,4,8,2048]{4,3,2,1,0:T(8,128)(2,1)S(1)}, bf16[1,2,4,8,2048]{4,3,2,1,0:T(8,128)(2,1)S(1)}, u32[]{:S(2)}, u32[]{:S(2)}) collective-permute-start(bf16[1,2,4,8,2048]{4,3,2,1,0:T(8,128)(2,1)S(1)} %get-tuple-element.192), channel_id=1, source_target_pairs={{8,0},{16,8},{24,16},{0,24},{9,1},{17,9},{25,17},{1,25},{10,2},{18... | collective-permute-start | bytes 786440 | tf_op jit(solution)/shard_map/ppermute | solution.py:813
  35.8 8.0 %collective-permute-start.12 = (bf16[1,2,4,8,2048]{4,3,2,1,0:T(8,128)(2,1)S(1)}, bf16[1,2,4,8,2048]{4,3,2,1,0:T(8,128)(2,1)S(1)}, u32[]{:S(2)}, u32[]{:S(2)}) collective-permute-start(bf16[1,2,4,8,2048]{4,3,2,1,0:T(8,128)(2,1)S(1)} %get-tuple-element.193), channel_id=1, source_target_pairs={{0,8},{8,16},{16,24},{24,0},{1,9},{9,17},{17,25},{25,1},{2,10},{10... | collective-permute-start | bytes 786440 | tf_op jit(solution)/shard_map/ppermute | solution.py:812
  50.4 3.9 %collective-permute-start.14 = (f32[8,128]{1,0:T(8,128)S(1)}, f32[8,128]{1,0:T(8,128)S(1)}, u32[]{:S(2)}, u32[]{:S(2)}) collective-permute-start(f32[8,128]{1,0:T(8,128)S(1)} %get-tuple-element.159), channel_id=1, source_target_pairs={{0,8},{8,16},{16,24},{24,0},{1,9},{9,17},{17,25},{25,1},{2,10},{10... | collective-permute-start | bytes 12296 | tf_op jit(solution)/shard_map/ppermute | solution.py:855
  51.0 3.3 %collective-permute-start.15 = (f32[8,128]{1,0:T(8,128)S(1)}, f32[8,128]{1,0:T(8,128)S(1)}, u32[]{:S(2)}, u32[]{:S(2)}) collective-permute-start(f32[8,128]{1,0:T(8,128)S(1)} %get-tuple-element.160), channel_id=1, source_target_pairs={{8,0},{16,8},{24,16},{0,24},{9,1},{17,9},{25,17},{1,25},{10,2},{18... | collective-permute-start | bytes 12296 | tf_op jit(solution)/shard_map/ppermute | solution.py:856
  54.4 5.5 %collective-permute-start.16 = (f32[8,256]{1,0:T(8,128)S(1)}, f32[8,256]{1,0:T(8,128)S(1)}, u32[]{:S(2)}, u32[]{:S(2)}) collective-permute-start(f32[8,256]{1,0:T(8,128)S(1)} %add.3.mid_ref), channel_id=1, source_target_pairs={{0,2},{2,4},{4,6},{6,0},{1,3},{3,5},{5,7},{7,1},{8,10},{10,12},{12... | collective-permute-start | bytes 24584 | tf_op jit(solution)/shard_map/ppermute | solution.py:862
  55.7 4.2 %collective-permute-start.17 = (f32[8,256]{1,0:T(8,128)S(1)}, f32[8,256]{1,0:T(8,128)S(1)}, u32[]{:S(2)}, u32[]{:S(2)}) collective-permute-start(f32[8,256]{1,0:T(8,128)S(1)} %add.3.mid_ref), channel_id=1, source_target_pairs={{2,0},{4,2},{6,4},{0,6},{3,1},{5,3},{7,5},{1,7},{10,8},{12,10},{14... | collective-permute-start | bytes 24584 | tf_op jit(solution)/shard_map/ppermute | solution.py:862
  60.0 3.7 %collective-permute-start.18 = (f32[8,256]{1,0:T(8,128)S(1)}, f32[8,256]{1,0:T(8,128)S(1)}, u32[]{:S(2)}, u32[]{:S(2)}) collective-permute-start(f32[8,256]{1,0:T(8,128)S(1)} %fold.1.mid_ref), channel_id=1, source_target_pairs={{0,1},{1,0},{2,3},{3,2},{4,5},{5,4},{6,7},{7,6},{8,9},{9,8},{10,11... | collective-permute-start | bytes 24584 | tf_op jit(solution)/shard_map/ppermute | solution.py:871
  (4 other events, 20.4 us)

commit v17 on v16

--- a/solution.py
+++ b/solution.py
@@ -341,15 +341,29 @@
 
 
 def pair_scratch(atoms, half, group):
-    count, width = len(KINDS[group]), GROUP_COLS[group]
+    width = GROUP_COLS[group]
     return (
-        [pltpu.VMEM((count, 2 * CH, 2 * CH), BF16) for _ in range(4)]
-        + [
+        [
             pltpu.VMEM((half, width), BF16),
             pltpu.VMEM((half, width), BF16),
             pltpu.VMEM((atoms, width), F32),
         ]
     )
+
+
+def weights_kernel(mix_ref, out_ref, *refs):
+    for group, kinds in enumerate(KINDS):
+        wm, wmt, wo, wot = refs[4 * group : 4 * group + 4]
+        block_diagonal(kinds, mix_ref, wm, wmt)
+        block_diagonal(kinds, out_ref, wo, wot)
+
+
+def weights_stage(mix, out):
+    out_shape = ()
+    for kinds in KINDS:
+        out_shape += (struct(len(kinds), 2 * CH, 2 * CH, dtype=BF16),) * 4
+    outs = call(weights_kernel, "weights", out_shape, [], (mix, out))
+    return outs[:4], outs[4:]
 
 
 def own_kernel(
@@ -583,14 +597,13 @@
     refs = refs[13:]
     degrees = DEGREES[group]
     radials, refs = dict(zip(degrees, refs)), refs[len(degrees) :]
+    (wm, wmt, wo, wot), refs = refs[:4], refs[4:]
     new_ref, en_ref, gs_ref, dot_gh = refs[:4]
     grads, refs = dict(zip(degrees, refs[4:])), refs[4 + len(degrees) :]
     if group == 0:
         dot_own, refs = refs[0], refs[1:]
         grads_own, refs = dict(zip(degrees, refs)), refs[len(degrees) :]
-    wm, wmt, wo, wot, nf_s, mx_s, acc_s = refs
-    block_diagonal(KINDS[group], mix_ref, wm, wmt)
-    block_diagonal(KINDS[group], out_ref, wo, wot)
+    nf_s, mx_s, acc_s = refs
     en_ref[...] = jnp.zeros_like(en_ref)
     ghost_pairs(
         group, own_ref, pieces, skip, new_ref, group_cols(group).start, oh_gh, d_gh, dt_gh, gate_gh,
@@ -601,7 +614,7 @@
         own_backward(group, gs_ref, gate_own, wmt, nf_own, mx_own, dot_own, grads_own)
 
 
-def pairs_stage(group, skip, pieces, shared, own_parts, radial_gh):
+def pairs_stage(group, skip, pieces, shared, own_parts, radial_gh, weights):
     feats = shared[0]
     atoms = feats.shape[0]
     half = atoms * HALF
@@ -614,7 +627,7 @@
         struct(atoms, GROUP_COLS[group], dtype=BF16),
     ) + (struct(half, CH, dtype=BF16),) * (sides * (1 + len(degrees)))
     args = tuple(pieces) + tuple(shared) + tuple(own_parts)
-    args += tuple(radial_gh[degree - 1] for degree in degrees)
+    args += tuple(radial_gh[degree - 1] for degree in degrees) + tuple(weights)
     new, energy, gs, *rest = call(
         functools.partial(pairs_kernel, group, len(pieces), skip), "pairs_" + "abc"[group],
         out_shape, pair_scratch(atoms, half, group), args, limit=24,
@@ -622,19 +635,17 @@
     return new, energy, gs, rest[: 1 + len(degrees)], rest[1 + len(degrees) :]
 
 
-def own_backward_kernel(group, mix_ref, gs_ref, gate_ref, nf_ref, mx_ref, *refs):
-    dot_ref, grads, wmt = refs[0], dict(zip(DEGREES[group], refs[1:-1])), refs[-1]
-    block_diagonal(KINDS[group], mix_ref, None, wmt)
+def own_backward_kernel(group, wmt, gs_ref, gate_ref, nf_ref, mx_ref, *refs):
+    dot_ref, grads = refs[0], dict(zip(DEGREES[group], refs[1:]))
     own_backward(group, gs_ref, gate_ref, wmt, nf_ref, mx_ref, dot_ref, grads)
 
 
-def own_backward_stage(group, mix, gs, gate, nf, mx):
+def own_backward_stage(group, wmt, gs, gate, nf, mx):
     half = nf.shape[0]
     out_shape = (struct(half, CH, dtype=BF16),) * (1 + len(DEGREES[group]))
-    scratch = [pltpu.VMEM((len(KINDS[group]), 2 * CH, 2 * CH), BF16)]
     kernel = functools.partial(own_backward_kernel, group)
     name = "own_backward_" + "abc"[group]
-    return call(kernel, name, out_shape, scratch, (mix, gs, gate, nf, mx))
+    return call(kernel, name, out_shape, [], (wmt, gs, gate, nf, mx))
 
 
 def finish(
@@ -688,14 +699,13 @@
     before, degrees = len(DEGREES[0]), DEGREES[group]
     gr_a, refs = refs[:before], refs[before:]
     radials, refs = dict(zip(degrees, refs)), refs[len(degrees) :]
+    (wm, wmt, wo, wot), refs = refs[:4], refs[4:]
     new_ref, energy_ref, src_ref, onto_ref, flow_ref, fmid_ref, fhigh_ref, gs_ref = refs[:8]
-    wm, wmt, wo, wot, nf_s, mx_s, acc_s, dot_c, en_s, fgh_s = refs[8:18]
-    grads = dict(zip(degrees, refs[18:]))
+    nf_s, mx_s, acc_s, dot_c, en_s, fgh_s = refs[8:14]
+    grads = dict(zip(degrees, refs[14:]))
     pieces = (p0, p1, p2, p3, p4)
     atoms = own_ref.shape[0]
     spacing = spacing_of(atoms, rbft_ref.shape[1])
-    block_diagonal(KINDS[group], mix_ref, wm, wmt)
-    block_diagonal(KINDS[group], out_ref, wo, wot)
     en_s[...] = en_0[...] + en_a[...]
     at = 0
     for part in (new_0, new_a):
@@ -720,7 +730,7 @@
         grad = mm(d_gh[here, :], gs0_low)
         pull, top, rest = finish(
             grad, m0_ref[here, :], nf0_ref[here, :], sum_of((dot_a, dot_c), here),
-            degree_parts(gr_a + refs[18:], here), pre_gh[here, :], unit_gh[here, :], spacing,
+            degree_parts(gr_a + refs[14:], here), pre_gh[here, :], unit_gh[here, :], spacing,
             radt_ref, rbft_ref, mix_t,
         )
         pull_top = pull.astype(BF16)
@@ -910,7 +920,8 @@
     middle = jnp.concatenate([y0[0], block0, y0[1]], axis=1)
     x0 = neighbours_of(middle, "gx", 0)
     y1_out = neighbours_of(jnp.concatenate(z1, axis=2), "gy", 1)
-    x1_in, gate_own = hold((x1_in, gate_own))
+    weights_a, weights_b = weights_stage(mix_weight, out_weight)
+    x1_in, gate_own, weights_a = hold((x1_in, gate_own, weights_a))
     _, (own_b,) = own_forward_stage((1,), feats, mix_weight, oh_own, radial_own, gate_own)
     x0, y1_out, acc0, acc_b = hold((x0, y1_out, acc0, own_b[2]))
     pieces0 = tuple(flat_rows(piece) for piece in (x0[0], middle, x0[1]))
@@ -931,15 +942,15 @@
     )
     shared = (feats, meta, mix_weight, out_weight, norm_weight, oh_gh, d_gh, dt_gh, gate_gh)
     new_a, en_a, _, (dot_gh_a, *gr_gh_a), (dot_own_a, *gr_own_a) = pairs_stage(
-        0, 2 * CH, pieces0, shared, (gate_own, *own_a), radial_gh
+        0, 2 * CH, pieces0, shared, (gate_own, *own_a), radial_gh, weights_a
     )
     new, energy, src, onto, low, mid, high, gs_b = third_stage(
         pieces1, *shared, acc_b, radt, rbft, gs0, en_0, en_a, new_0, new_a, pre_gh,
         unit_gh, m0_gh, nf0_gh, dot_gh_a, *gr_gh_a,
-        *[radial_gh[degree - 1] for degree in DEGREES[1]],
+        *[radial_gh[degree - 1] for degree in DEGREES[1]], *weights_b,
     )
     mid, arrived = give_back_x(low, mid, high)
-    dot_own_b, *gr_own_b = own_backward_stage(1, mix_weight, gs_b, gate_own, *own_b[:2])
+    dot_own_b, *gr_own_b = own_backward_stage(1, weights_b[1], gs_b, gate_own, *own_b[:2])
     arrived, gs0, dot_own_b = hold((arrived, gs0, dot_own_b))
     mid, from_low, from_high = give_back_y(mid + arrived)
     back = (oh_own, pre_own, unit_own, radt, rbft, mix_weight, gs0, m0_own, nf0_own)

time: 64.7 us -> 64.7 us (level)
    pallas_call x13 -> x14, Pallas kernels: 27.5 us -> 27.9 us  [call(): pl.pallas_call(kernel, out_shape=out_shape, in_specs=specs or [pl.BlockSp...]
where the time goes in v17:
time: 64.7 us; the launch traced here: 64.4 us
  Pallas kernels  27.9 us (43%)
  starting transfers between devices  27.4 us (42%)
  waiting for transfers between devices  5.05 us (8%)
  local copies, waits for them, and re-layouts  1.97 us (3%)
  other arithmetic  1.15 us (2%)
  between operations  0.93 us (1%)
    pallas_call x14, Pallas kernels, call(): pl.pallas_call(kernel, out_shape=out_shape, in_specs=specs or [pl.BlockSp...  27.9 us
    ppermute x6, starting transfers between devices, neighbours_of(): after = lax.ppermute(lax.slice_in_dim(block, 0, 1, axis=dim), axis, down)  11.8 us
    ppermute x6, starting transfers between devices, neighbours_of(): lax.ppermute(lax.slice_in_dim(block, length - 1, length, axis=dim), axis,...  5.57 us
    ppermute x2, starting transfers between devices, give_back_y(): return (mid, lax.ppermute(mid, 'gy', up), lax.ppermute(mid, 'gy', down))  3.91 us
    ppermute x2, starting transfers between devices, neighbours_of(): other = lax.ppermute(block, axis, up)  3.13 us
    ppermute x6, waiting for transfers between devices, neighbours_of(): lax.ppermute(lax.slice_in_dim(block, length - 1, length, axis=dim), axis,...  1.91 us
    unnamed x19, local copies, waits for them, and re-layouts  1.73 us
    ppermute x6, waiting for transfers between devices, neighbours_of(): after = lax.ppermute(lax.slice_in_dim(block, 0, 1, axis=dim), axis, down)  1.67 us
  transfers between devices with their start and end apart: 19, of which 9 were waited for; matrix products, arithmetic and copies ran while one was open for 1% of the time, Pallas kernels for 31%

profile of v17, /device:TPU:0, one launch (start us, length us, event | category | flops | bytes accessed | tf_op | source)
XLA Modules:
  0.0 64.4 jit_solution(17723589068757835019)
XLA Ops:
  3.4 3.0 %collective-permute-start.3 = (bf16[2,2,2,8,1280]{4,3,2,1,0:T(8,128)(2,1)S(1)}, bf16[2,2,2,8,1280]{4,3,2,1,0:T(8,128)(2,1)S(1)}, u32[]{:S(2)}, u32[]{:S(2)}) collective-permute-start(bf16[2,2,2,8,1280]{4,3,2,1,0:T(8,128)(2,1)S(1)} %bitcast.41), channel_id=1, source_target_pairs={{0,1},{1,0},{2,3},{3,2},{4,5},{5,4},{6,7},{7,6},{8,9},{9,8},{10,11... | collective-permute-start | bytes 491528 | tf_op jit(solution)/shard_map/ppermute | solution.py:817
  6.8 2.1 %collective-permute-start.1 = (bf16[2,1,2,8,2048]{4,3,2,1,0:T(8,128)(2,1)S(1)}, bf16[2,1,2,8,2048]{4,3,2,1,0:T(8,128)(2,1)S(1)}, u32[]{:S(2)}, u32[]{:S(2)}) collective-permute-start(bf16[2,1,2,8,2048]{4,3,2,1,0:T(8,128)(2,1)S(1)} %get-tuple-element.225), channel_id=1, source_target_pairs={{0,2},{2,4},{4,6},{6,0},{1,3},{3,5},{5,7},{7,1},{8,10},{10,12},{12... | collective-permute-start | bytes 393224 | tf_op jit(solution)/shard_map/ppermute | solution.py:822
  8.9 2.1 %collective-permute-start.2 = (bf16[2,1,2,8,2048]{4,3,2,1,0:T(8,128)(2,1)S(1)}, bf16[2,1,2,8,2048]{4,3,2,1,0:T(8,128)(2,1)S(1)}, u32[]{:S(2)}, u32[]{:S(2)}) collective-permute-start(bf16[2,1,2,8,2048]{4,3,2,1,0:T(8,128)(2,1)S(1)} %get-tuple-element.224), channel_id=1, source_target_pairs={{2,0},{4,2},{6,4},{0,6},{3,1},{5,3},{7,5},{1,7},{10,8},{12,10},{14... | collective-permute-start | bytes 393224 | tf_op jit(solution)/shard_map/ppermute | solution.py:823
  11.6 2.2 %collective-permute-start.6 = (bf16[2,1,4,8,1280]{4,3,2,1,0:T(8,128)(2,1)S(1)}, bf16[2,1,4,8,1280]{4,3,2,1,0:T(8,128)(2,1)S(1)}, u32[]{:S(2)}, u32[]{:S(2)}) collective-permute-start(bf16[2,1,4,8,1280]{4,3,2,1,0:T(8,128)(2,1)S(1)} %get-tuple-element.221), channel_id=1, source_target_pairs={{0,2},{2,4},{4,6},{6,0},{1,3},{3,5},{5,7},{7,1},{8,10},{10,12},{12... | collective-permute-start | bytes 491528 | tf_op jit(solution)/shard_map/ppermute | solution.py:822
  13.7 2.1 %collective-permute-start.7 = (bf16[2,1,4,8,1280]{4,3,2,1,0:T(8,128)(2,1)S(1)}, bf16[2,1,4,8,1280]{4,3,2,1,0:T(8,128)(2,1)S(1)}, u32[]{:S(2)}, u32[]{:S(2)}) collective-permute-start(bf16[2,1,4,8,1280]{4,3,2,1,0:T(8,128)(2,1)S(1)} %get-tuple-element.220), channel_id=1, source_target_pairs={{2,0},{4,2},{6,4},{0,6},{3,1},{5,3},{7,5},{1,7},{10,8},{12,10},{14... | collective-permute-start | bytes 491528 | tf_op jit(solution)/shard_map/ppermute | solution.py:823
  15.8 2.9 %own_edges.1 = (bf16[1024,64]{1,0:T(8,128)(2,1)S(1)}, bf16[1024,128]{1,0:T(8,128)(2,1)S(1)}, f32[1024,128]{1,0:T(8,128)S(1)}, bf16[640,128]{1,0:T(8,128)(2,1)S(1...) custom-call(f32[64,128]{1,0:T(8,128)S(1)} %get-tuple-element.111.met, ...), custom_call_target="tpu_custom_call" | custom-call | flops 1024 | bytes 1024 | tf_op jit(solution)/shard_map/own_edges/pallas_call | solution.py:57
  19.4 1.7 %collective-permute-start.5 = (bf16[1,2,4,8,2048]{4,3,2,1,0:T(8,128)(2,1)S(1)}, bf16[1,2,4,8,2048]{4,3,2,1,0:T(8,128)(2,1)S(1)}, u32[]{:S(2)}, u32[]{:S(2)}) collective-permute-start(bf16[1,2,4,8,2048]{4,3,2,1,0:T(8,128)(2,1)S(1)} %get-tuple-element.218), channel_id=1, source_target_pairs={{8,0},{16,8},{24,16},{0,24},{9,1},{17,9},{25,17},{1,25},{10,2},{18... | collective-permute-start | bytes 786440 | tf_op jit(solution)/shard_map/ppermute | solution.py:823
  21.1 1.5 %own_forward_a.1 = (bf16[1024,128]{1,0:T(8,128)(2,1)S(1)}, bf16[1024,128]{1,0:T(8,128)(2,1)S(1)}, bf16[1024,128]{1,0:T(8,128)(2,1)S(1)}, f32[64,128]{1,0:T(8,128...) custom-call(bf16[64,3200]{1,0:T(8,128)(2,1)S(1)} %bitcast.25, ...), custom_call_target="tpu_custom_call" | custom-call | flops 1024 | bytes 1024 | tf_op jit(solution)/shard_map/own_forward_a/pallas_call | solution.py:57
  23.4 1.7 %collective-permute-start.9 = (bf16[1,4,4,8,1280]{4,3,2,1,0:T(8,128)(2,1)S(1)}, bf16[1,4,4,8,1280]{4,3,2,1,0:T(8,128)(2,1)S(1)}, u32[]{:S(2)}, u32[]{:S(2)}) collective-permute-start(bf16[1,4,4,8,1280]{4,3,2,1,0:T(8,128)(2,1)S(1)} %get-tuple-element.214), channel_id=1, source_target_pairs={{8,0},{16,8},{24,16},{0,24},{9,1},{17,9},{25,17},{1,25},{10,2},{18... | collective-permute-start | bytes 983048 | tf_op jit(solution)/shard_map/ppermute | solution.py:823
  25.2 1.2 %collective-permute-start.10 = (bf16[2,1,2,8,2048]{4,3,2,1,0:T(8,128)(2,1)S(1)}, bf16[2,1,2,8,2048]{4,3,2,1,0:T(8,128)(2,1)S(1)}, u32[]{:S(2)}, u32[]{:S(2)}) collective-permute-start(bf16[2,1,2,8,2048]{4,3,2,1,0:T(8,128)(2,1)S(1)} %get-tuple-element.223), channel_id=1, source_target_pairs={{0,2},{2,4},{4,6},{6,0},{1,3},{3,5},{5,7},{7,1},{8,10},{10,12},{12... | collective-permute-start | bytes 393224 | tf_op jit(solution)/shard_map/ppermute | solution.py:822
  26.4 2.6 %collective-permute-start.11 = (bf16[2,1,2,8,2048]{4,3,2,1,0:T(8,128)(2,1)S(1)}, bf16[2,1,2,8,2048]{4,3,2,1,0:T(8,128)(2,1)S(1)}, u32[]{:S(2)}, u32[]{:S(2)}) collective-permute-start(bf16[2,1,2,8,2048]{4,3,2,1,0:T(8,128)(2,1)S(1)} %get-tuple-element.222), channel_id=1, source_target_pairs={{2,0},{4,2},{6,4},{0,6},{3,1},{5,3},{7,5},{1,7},{10,8},{12,10},{14... | collective-permute-start | bytes 393224 | tf_op jit(solution)/shard_map/ppermute | solution.py:823
  29.5 2.5 %own_forward_b.1 = (bf16[1024,2048]{1,0:T(8,128)(2,1)S(1)}, bf16[1024,2048]{1,0:T(8,128)(2,1)S(1)}, f32[64,2048]{1,0:T(8,128)S(1)}) custom-call(bf16[64,3200]{1,0:T(8,128)(2,1)S(1)} %bitcast.26, bf16[5,128,128]{2,1,0:T(8,128)(2,1)S(1)} %copy-done.2, bf16[1024,64]{1,0:T(8,128)(2,1)S(1)} %get-tuple-element.118.refs_2_.oh_own, ...), custom_call_target="tpu_custom_call" | custom-call | flops 1024 | bytes 1024 | tf_op jit(solution)/shard_map/own_forward_b/pallas_call | solution.py:57
  32.0 1.4 %collective-permute-done.10 = bf16[2,1,2,8,2048]{4,3,2,1,0:T(8,128)(2,1)S(1)} collective-permute-done((bf16[2,1,2,8,2048]{4,3,2,1,0:T(8,128)(2,1)S(1)}, bf16[2,1,2,8,2048]{4,3,2,1,0:T(8,128)(2,1)S(1)}, u32[]{:S(2)}, u32[]{:S(2)}) %collective-permute-start.10) | collective-permute-done | bytes 131104 | tf_op jit(solution)/shard_map/ppermute | solution.py:822
  34.3 1.5 %collective-permute-start.13 = (bf16[1,2,4,8,2048]{4,3,2,1,0:T(8,128)(2,1)S(1)}, bf16[1,2,4,8,2048]{4,3,2,1,0:T(8,128)(2,1)S(1)}, u32[]{:S(2)}, u32[]{:S(2)}) collective-permute-start(bf16[1,2,4,8,2048]{4,3,2,1,0:T(8,128)(2,1)S(1)} %get-tuple-element.216), channel_id=1, source_target_pairs={{8,0},{16,8},{24,16},{0,24},{9,1},{17,9},{25,17},{1,25},{10,2},{18... | collective-permute-start | bytes 786440 | tf_op jit(solution)/shard_map/ppermute | solution.py:823
  35.8 3.3 %ghost_start.1 = (bf16[64,128]{1,0:T(8,128)(2,1)S(1)}, bf16[1024,512]{1,0:T(8,128)(2,1)S(1)}, bf16[1024,64]{1,0:T(8,128)(2,1)S(1)}, bf16[64,1024]{1,0:T(8,128)(2...) custom-call(bf16[128,1280]{1,0:T(8,128)(2,1)S(1)} %bitcast.37, ...), custom_call_target="tpu_custom_call" | custom-call | flops 1024 | bytes 1024 | tf_op jit(solution)/shard_map/ghost_start/pallas_call | solution.py:57
  39.1 4.1 %pairs_a.1 = (bf16[64,1024]{1,0:T(8,128)(2,1)S(1)}, f32[64,128]{1,0:T(8,128)S(1)}, bf16[64,1024]{1,0:T(8,128)(2,1)}, bf16[1024,128]{1,0:T(8,128)(2,1)S(1)}, bf16...) custom-call(bf16[128,1280]{1,0:T(8,128)(2,1)S(1)} %bitcast.38, ...), custom_call_target="tpu_custom_call" | custom-call | flops 1024 | bytes 1024 | tf_op jit(solution)/shard_map/pairs_a/pallas_call | solution.py:57
  43.8 6.7 %third_group.1 = (bf16[64,3200]{1,0:T(8,128)(2,1)}, f32[1,64]{1,0:T(1,128)}, f32[64,128]{1,0:T(8,128)S(1)}, f32[8,64]{1,0:T(8,128)S(1)}, f32[8,128]{1,0:T(8,128)...) custom-call(bf16[64,2048]{1,0:T(8,128)(2,1)S(1)} %bitcast.44, ...), custom_call_target="tpu_custom_call" | custom-call | flops 1024 | bytes 1024 | tf_op jit(solution)/shard_map/third_group/pallas_call | solution.py:57
  51.0 1.2 %collective-permute-start.15 = (f32[8,128]{1,0:T(8,128)S(1)}, f32[8,128]{1,0:T(8,128)S(1)}, u32[]{:S(2)}, u32[]{:S(2)}) collective-permute-start(f32[8,128]{1,0:T(8,128)S(1)} %get-tuple-element.184), channel_id=1, source_target_pairs={{8,0},{16,8},{24,16},{0,24},{9,1},{17,9},{25,17},{1,25},{10,2},{18... | collective-permute-start | bytes 12296 | tf_op jit(solution)/shard_map/ppermute | solution.py:866
  52.2 2.1 %own_backward_b.1 = (bf16[1024,128]{1,0:T(8,128)(2,1)S(1)}, bf16[1024,128]{1,0:T(8,128)(2,1)S(1)}, bf16[1024,128]{1,0:T(8,128)(2,1)S(1)}) custom-call(bf16[3,256,256]{2,1,0:T(8,128)(2,1)S(1)} %get-tuple-element.177.refs_5_.wmt, bf16[64,2048]{1,0:T(8,128)(2,1)S(1)} %get-tuple-element.185.gs_ref, ...), custom_call_target="tpu_custom_call" | custom-call | flops 1024 | bytes 1024 | tf_op jit(solution)/shard_map/own_backward_b/pallas_call | solution.py:57
  54.4 1.3 %collective-permute-start.16 = (f32[8,256]{1,0:T(8,128)S(1)}, f32[8,256]{1,0:T(8,128)S(1)}, u32[]{:S(2)}, u32[]{:S(2)}) collective-permute-start(f32[8,256]{1,0:T(8,128)S(1)} %add.3.mid_ref), channel_id=1, source_target_pairs={{0,2},{2,4},{4,6},{6,0},{1,3},{3,5},{5,7},{7,1},{8,10},{10,12},{12... | collective-permute-start | bytes 24584 | tf_op jit(solution)/shard_map/ppermute | solution.py:872
  55.7 2.6 %collective-permute-start.17 = (f32[8,256]{1,0:T(8,128)S(1)}, f32[8,256]{1,0:T(8,128)S(1)}, u32[]{:S(2)}, u32[]{:S(2)}) collective-permute-start(f32[8,256]{1,0:T(8,128)S(1)} %add.3.mid_ref), channel_id=1, source_target_pairs={{2,0},{4,2},{6,4},{0,6},{3,1},{5,3},{7,5},{1,7},{10,8},{12,10},{14... | collective-permute-start | bytes 24584 | tf_op jit(solution)/shard_map/ppermute | solution.py:872
  58.3 1.5 %own_back.2 = (f32[64,128]{1,0:T(8,128)S(1)}, f32[8,64]{1,0:T(8,128)S(1)}) custom-call(bf16[1024,64]{1,0:T(8,128)(2,1)S(1)} %get-tuple-element.118.refs_2_.oh_own, bf16[1024,128]{1,0:T(8,128)(2,1)S(1)} %get-tuple-element.190.pre_own, f32[1024,128]{1,0:T(8,128)S(1)} %get-tuple-element.191.unit_own, bf16[640,128]{1,0:T(8,128)(2,1)S(1)} %get-tuple-element.151.radt_ref, ...), custom_call_target="tpu_custom_call" | custom-call | flops 1024 | bytes 1024 | tf_op jit(solution)/shard_map/own_back/pallas_call | solution.py:57
  60.0 1.2 %collective-permute-start.18 = (f32[8,256]{1,0:T(8,128)S(1)}, f32[8,256]{1,0:T(8,128)S(1)}, u32[]{:S(2)}, u32[]{:S(2)}) collective-permute-start(f32[8,256]{1,0:T(8,128)S(1)} %fold.1.mid_ref), channel_id=1, source_target_pairs={{0,1},{1,0},{2,3},{3,2},{4,5},{5,4},{6,7},{7,6},{8,9},{9,8},{10,11... | collective-permute-start | bytes 24584 | tf_op jit(solution)/shard_map/ppermute | solution.py:881
  61.2 1.5 %own_back.3 = (f32[64,128]{1,0:T(8,128)S(1)}, f32[8,64]{1,0:T(8,128)S(1)}) custom-call(bf16[1024,64]{1,0:T(8,128)(2,1)S(1)} %get-tuple-element.118.refs_2_.oh_own, bf16[1024,128]{1,0:T(8,128)(2,1)S(1)} %get-tuple-element.190.pre_own, f32[1024,128]{1,0:T(8,128)S(1)} %get-tuple-element.191.unit_own, bf16[640,128]{1,0:T(8,128)(2,1)S(1)} %get-tuple-element.151.radt_ref, ...), custom_call_target="tpu_custom_call" | custom-call | flops 1024 | bytes 1024 | tf_op jit(solution)/shard_map/own_back/pallas_call | solution.py:57
  (65 shorter events, 9.4 us)
Async XLA Ops:
  3.4 8.1 %collective-permute-start.3 = (bf16[2,2,2,8,1280]{4,3,2,1,0:T(8,128)(2,1)S(1)}, bf16[2,2,2,8,1280]{4,3,2,1,0:T(8,128)(2,1)S(1)}, u32[]{:S(2)}, u32[]{:S(2)}) collective-permute-start(bf16[2,2,2,8,1280]{4,3,2,1,0:T(8,128)(2,1)S(1)} %bitcast.41), channel_id=1, source_target_pairs={{0,1},{1,0},{2,3},{3,2},{4,5},{5,4},{6,7},{7,6},{8,9},{9,8},{10,11... | collective-permute-start | bytes 491528 | tf_op jit(solution)/shard_map/ppermute | solution.py:817
  6.7 14.5 %copy-start.1 = (bf16[1,1,1,64,3200]{4,3,2,1,0:T(8,128)(2,1)S(1)}, bf16[1,1,1,64,3200]{4,3,2,1,0:T(8,128)(2,1)}, u32[]{:S(2)}) copy-start(bf16[1,1,1,64,3200]{4,3,2,1,0:T(8,128)(2,1)} %param.11) | copy-start | bytes 1228804
  6.7 14.5 %copy-start.2 = (bf16[5,128,128]{2,1,0:T(8,128)(2,1)S(1)}, bf16[5,128,128]{2,1,0:T(8,128)(2,1)}, u32[]{:S(2)}) copy-start(bf16[5,128,128]{2,1,0:T(8,128)(2,1)} %mix_ref.9) | copy-start | bytes 491524
  6.7 12.0 %collective-permute-start = (bf16[2,2,2,8,2048]{4,3,2,1,0:T(8,128)(2,1)S(1)}, bf16[2,2,2,8,2048]{4,3,2,1,0:T(8,128)(2,1)S(1)}, u32[]{:S(2)}, u32[]{:S(2)}) collective-permute-start(bf16[2,2,2,8,2048]{4,3,2,1,0:T(8,128)(2,1)S(1)} %bitcast.33), channel_id=1, source_target_pairs={{0,1},{1,0},{2,3},{3,2},{4,5},{5,4},{6,7},{7,6},{8,9},{9,8},{10,11... | collective-permute-start | bytes 786440 | tf_op jit(solution)/shard_map/ppermute | solution.py:817
  6.8 12.0 %collective-permute-start.1 = (bf16[2,1,2,8,2048]{4,3,2,1,0:T(8,128)(2,1)S(1)}, bf16[2,1,2,8,2048]{4,3,2,1,0:T(8,128)(2,1)S(1)}, u32[]{:S(2)}, u32[]{:S(2)}) collective-permute-start(bf16[2,1,2,8,2048]{4,3,2,1,0:T(8,128)(2,1)S(1)} %get-tuple-element.225), channel_id=1, source_target_pairs={{0,2},{2,4},{4,6},{6,0},{1,3},{3,5},{5,7},{7,1},{8,10},{10,12},{12... | collective-permute-start | bytes 393224 | tf_op jit(solution)/shard_map/ppermute | solution.py:822
  8.9 10.3 %collective-permute-start.2 = (bf16[2,1,2,8,2048]{4,3,2,1,0:T(8,128)(2,1)S(1)}, bf16[2,1,2,8,2048]{4,3,2,1,0:T(8,128)(2,1)S(1)}, u32[]{:S(2)}, u32[]{:S(2)}) collective-permute-start(bf16[2,1,2,8,2048]{4,3,2,1,0:T(8,128)(2,1)S(1)} %get-tuple-element.224), channel_id=1, source_target_pairs={{2,0},{4,2},{6,4},{0,6},{3,1},{5,3},{7,5},{1,7},{10,8},{12,10},{14... | collective-permute-start | bytes 393224 | tf_op jit(solution)/shard_map/ppermute | solution.py:823
  11.6 11.1 %collective-permute-start.6 = (bf16[2,1,4,8,1280]{4,3,2,1,0:T(8,128)(2,1)S(1)}, bf16[2,1,4,8,1280]{4,3,2,1,0:T(8,128)(2,1)S(1)}, u32[]{:S(2)}, u32[]{:S(2)}) collective-permute-start(bf16[2,1,4,8,1280]{4,3,2,1,0:T(8,128)(2,1)S(1)} %get-tuple-element.221), channel_id=1, source_target_pairs={{0,2},{2,4},{4,6},{6,0},{1,3},{3,5},{5,7},{7,1},{8,10},{10,12},{12... | collective-permute-start | bytes 491528 | tf_op jit(solution)/shard_map/ppermute | solution.py:822
  13.7 9.4 %collective-permute-start.7 = (bf16[2,1,4,8,1280]{4,3,2,1,0:T(8,128)(2,1)S(1)}, bf16[2,1,4,8,1280]{4,3,2,1,0:T(8,128)(2,1)S(1)}, u32[]{:S(2)}, u32[]{:S(2)}) collective-permute-start(bf16[2,1,4,8,1280]{4,3,2,1,0:T(8,128)(2,1)S(1)} %get-tuple-element.220), channel_id=1, source_target_pairs={{2,0},{4,2},{6,4},{0,6},{3,1},{5,3},{7,5},{1,7},{10,8},{12,10},{14... | collective-permute-start | bytes 491528 | tf_op jit(solution)/shard_map/ppermute | solution.py:823
  18.7 10.3 %copy-start.3 = (bf16[5,128,128]{2,1,0:T(8,128)(2,1)S(1)}, bf16[5,128,128]{2,1,0:T(8,128)(2,1)}, u32[]{:S(2)}) copy-start(bf16[5,128,128]{2,1,0:T(8,128)(2,1)} %out_ref.5) | copy-start | bytes 491524
  19.3 7.1 %collective-permute-start.4 = (bf16[1,2,4,8,2048]{4,3,2,1,0:T(8,128)(2,1)S(1)}, bf16[1,2,4,8,2048]{4,3,2,1,0:T(8,128)(2,1)S(1)}, u32[]{:S(2)}, u32[]{:S(2)}) collective-permute-start(bf16[1,2,4,8,2048]{4,3,2,1,0:T(8,128)(2,1)S(1)} %get-tuple-element.219), channel_id=1, source_target_pairs={{0,8},{8,16},{16,24},{24,0},{1,9},{9,17},{17,25},{25,1},{2,10},{10... | collective-permute-start | bytes 786440 | tf_op jit(solution)/shard_map/ppermute | solution.py:822
  19.4 10.1 %collective-permute-start.5 = (bf16[1,2,4,8,2048]{4,3,2,1,0:T(8,128)(2,1)S(1)}, bf16[1,2,4,8,2048]{4,3,2,1,0:T(8,128)(2,1)S(1)}, u32[]{:S(2)}, u32[]{:S(2)}) collective-permute-start(bf16[1,2,4,8,2048]{4,3,2,1,0:T(8,128)(2,1)S(1)} %get-tuple-element.218), channel_id=1, source_target_pairs={{8,0},{16,8},{24,16},{0,24},{9,1},{17,9},{25,17},{1,25},{10,2},{18... | collective-permute-start | bytes 786440 | tf_op jit(solution)/shard_map/ppermute | solution.py:823
  23.1 12.7 %copy-start.8 = (f32[128]{0:T(128)S(1)}, f32[128]{0:T(128)}, u32[]{:S(2)}) copy-start(f32[128]{0:T(128)} %param.20) | copy-start | bytes 1540
  23.3 10.8 %collective-permute-start.8 = (bf16[1,4,4,8,1280]{4,3,2,1,0:T(8,128)(2,1)S(1)}, bf16[1,4,4,8,1280]{4,3,2,1,0:T(8,128)(2,1)S(1)}, u32[]{:S(2)}, u32[]{:S(2)}) collective-permute-start(bf16[1,4,4,8,1280]{4,3,2,1,0:T(8,128)(2,1)S(1)} %get-tuple-element.215), channel_id=1, source_target_pairs={{0,8},{8,16},{16,24},{24,0},{1,9},{9,17},{17,25},{25,1},{2,10},{10... | collective-permute-start | bytes 983048 | tf_op jit(solution)/shard_map/ppermute | solution.py:822
  23.4 10.8 %collective-permute-start.9 = (bf16[1,4,4,8,1280]{4,3,2,1,0:T(8,128)(2,1)S(1)}, bf16[1,4,4,8,1280]{4,3,2,1,0:T(8,128)(2,1)S(1)}, u32[]{:S(2)}, u32[]{:S(2)}) collective-permute-start(bf16[1,4,4,8,1280]{4,3,2,1,0:T(8,128)(2,1)S(1)} %get-tuple-element.214), channel_id=1, source_target_pairs={{8,0},{16,8},{24,16},{0,24},{9,1},{17,9},{25,17},{1,25},{10,2},{18... | collective-permute-start | bytes 983048 | tf_op jit(solution)/shard_map/ppermute | solution.py:823
  25.1 14.0 %copy-start.6 = (f32[4,128]{1,0:T(4,128)S(1)}, f32[4,128]{1,0:T(4,128)}, u32[]{:S(2)}) copy-start(f32[4,128]{1,0:T(4,128)} %nw_ref.1) | copy-start | bytes 6148
  25.2 8.2 %collective-permute-start.10 = (bf16[2,1,2,8,2048]{4,3,2,1,0:T(8,128)(2,1)S(1)}, bf16[2,1,2,8,2048]{4,3,2,1,0:T(8,128)(2,1)S(1)}, u32[]{:S(2)}, u32[]{:S(2)}) collective-permute-start(bf16[2,1,2,8,2048]{4,3,2,1,0:T(8,128)(2,1)S(1)} %get-tuple-element.223), channel_id=1, source_target_pairs={{0,2},{2,4},{4,6},{6,0},{1,3},{3,5},{5,7},{7,1},{8,10},{10,12},{12... | collective-permute-start | bytes 393224 | tf_op jit(solution)/shard_map/ppermute | solution.py:822
  26.4 7.7 %collective-permute-start.11 = (bf16[2,1,2,8,2048]{4,3,2,1,0:T(8,128)(2,1)S(1)}, bf16[2,1,2,8,2048]{4,3,2,1,0:T(8,128)(2,1)S(1)}, u32[]{:S(2)}, u32[]{:S(2)}) collective-permute-start(bf16[2,1,2,8,2048]{4,3,2,1,0:T(8,128)(2,1)S(1)} %get-tuple-element.222), channel_id=1, source_target_pairs={{2,0},{4,2},{6,4},{0,6},{3,1},{5,3},{7,5},{1,7},{10,8},{12,10},{14... | collective-permute-start | bytes 393224 | tf_op jit(solution)/shard_map/ppermute | solution.py:823
  34.3 9.1 %collective-permute-start.13 = (bf16[1,2,4,8,2048]{4,3,2,1,0:T(8,128)(2,1)S(1)}, bf16[1,2,4,8,2048]{4,3,2,1,0:T(8,128)(2,1)S(1)}, u32[]{:S(2)}, u32[]{:S(2)}) collective-permute-start(bf16[1,2,4,8,2048]{4,3,2,1,0:T(8,128)(2,1)S(1)} %get-tuple-element.216), channel_id=1, source_target_pairs={{8,0},{16,8},{24,16},{0,24},{9,1},{17,9},{25,17},{1,25},{10,2},{18... | collective-permute-start | bytes 786440 | tf_op jit(solution)/shard_map/ppermute | solution.py:823
  35.8 8.0 %collective-permute-start.12 = (bf16[1,2,4,8,2048]{4,3,2,1,0:T(8,128)(2,1)S(1)}, bf16[1,2,4,8,2048]{4,3,2,1,0:T(8,128)(2,1)S(1)}, u32[]{:S(2)}, u32[]{:S(2)}) collective-permute-start(bf16[1,2,4,8,2048]{4,3,2,1,0:T(8,128)(2,1)S(1)} %get-tuple-element.217), channel_id=1, source_target_pairs={{0,8},{8,16},{16,24},{24,0},{1,9},{9,17},{17,25},{25,1},{2,10},{10... | collective-permute-start | bytes 786440 | tf_op jit(solution)/shard_map/ppermute | solution.py:822
  50.5 3.9 %collective-permute-start.14 = (f32[8,128]{1,0:T(8,128)S(1)}, f32[8,128]{1,0:T(8,128)S(1)}, u32[]{:S(2)}, u32[]{:S(2)}) collective-permute-start(f32[8,128]{1,0:T(8,128)S(1)} %get-tuple-element.183), channel_id=1, source_target_pairs={{0,8},{8,16},{16,24},{24,0},{1,9},{9,17},{17,25},{25,1},{2,10},{10... | collective-permute-start | bytes 12296 | tf_op jit(solution)/shard_map/ppermute | solution.py:865
  51.0 3.3 %collective-permute-start.15 = (f32[8,128]{1,0:T(8,128)S(1)}, f32[8,128]{1,0:T(8,128)S(1)}, u32[]{:S(2)}, u32[]{:S(2)}) collective-permute-start(f32[8,128]{1,0:T(8,128)S(1)} %get-tuple-element.184), channel_id=1, source_target_pairs={{8,0},{16,8},{24,16},{0,24},{9,1},{17,9},{25,17},{1,25},{10,2},{18... | collective-permute-start | bytes 12296 | tf_op jit(solution)/shard_map/ppermute | solution.py:866
  54.4 5.5 %collective-permute-start.16 = (f32[8,256]{1,0:T(8,128)S(1)}, f32[8,256]{1,0:T(8,128)S(1)}, u32[]{:S(2)}, u32[]{:S(2)}) collective-permute-start(f32[8,256]{1,0:T(8,128)S(1)} %add.3.mid_ref), channel_id=1, source_target_pairs={{0,2},{2,4},{4,6},{6,0},{1,3},{3,5},{5,7},{7,1},{8,10},{10,12},{12... | collective-permute-start | bytes 24584 | tf_op jit(solution)/shard_map/ppermute | solution.py:872
  55.7 4.2 %collective-permute-start.17 = (f32[8,256]{1,0:T(8,128)S(1)}, f32[8,256]{1,0:T(8,128)S(1)}, u32[]{:S(2)}, u32[]{:S(2)}) collective-permute-start(f32[8,256]{1,0:T(8,128)S(1)} %add.3.mid_ref), channel_id=1, source_target_pairs={{2,0},{4,2},{6,4},{0,6},{3,1},{5,3},{7,5},{1,7},{10,8},{12,10},{14... | collective-permute-start | bytes 24584 | tf_op jit(solution)/shard_map/ppermute | solution.py:872
  60.0 3.7 %collective-permute-start.18 = (f32[8,256]{1,0:T(8,128)S(1)}, f32[8,256]{1,0:T(8,128)S(1)}, u32[]{:S(2)}, u32[]{:S(2)}) collective-permute-start(f32[8,256]{1,0:T(8,128)S(1)} %fold.1.mid_ref), channel_id=1, source_target_pairs={{0,1},{1,0},{2,3},{3,2},{4,5},{5,4},{6,7},{7,6},{8,9},{9,8},{10,11... | collective-permute-start | bytes 24584 | tf_op jit(solution)/shard_map/ppermute | solution.py:881
  (4 other events, 20.4 us)

commit v18 on v16

--- a/solution.py
+++ b/solution.py
@@ -152,7 +152,7 @@
     basis = jnp.exp(-0.5 * centred * centred)
     pre = mm(basis.astype(BF16), rbf_ref[...])
     hidden = (pre * jax.nn.sigmoid(pre)).astype(BF16)
-    return pre, mm(hidden, rad_ref[...]).astype(BF16)
+    return pre, mm(hidden, rad_ref[...]).astype(BF16), basis * centred
 
 
 def tiled(values, size=STEP):
@@ -354,7 +354,7 @@
 
 def own_kernel(
     meta_ref, own_pos_ref, rbf_ref, rad_ref,
-    oh_own, pre_ref, unit_ref, radt_ref, rbft_ref, home_ref, *radial_refs
+    oh_own, pre_ref, unit_ref, radt_ref, rbft_ref, home_ref, slope_ref, *radial_refs
 ):
     atoms = meta_ref.shape[0]
     nbasis = rbft_ref.shape[1]
@@ -365,7 +365,8 @@
         rows = own_rows(step)
         unit, dist = geometry(mm(oh_own[rows, :], own_pos_ref[...]), here)
         unit_ref[rows, :] = unit
-        pre, radial = radial_net(dist, spacing, rbf_ref, rad_ref)
+        pre, radial, slope = radial_net(dist, spacing, rbf_ref, rad_ref)
+        slope_ref[rows, :] = slope.astype(BF16)
         pre_ref[rows, :] = pre.astype(BF16)
         for degree, ref in enumerate(radial_refs):
             ref[rows, :] = radial[:, degree * CH : (degree + 1) * CH]
@@ -399,6 +400,7 @@
         struct(5 * CH, CH, dtype=BF16),
         struct(CH, rbf.shape[0], dtype=BF16),
         struct(atoms, 256, dtype=BF16),
+        struct(edges, rbf.shape[0], dtype=BF16),
     ) + (struct(edges, CH, dtype=BF16),) * 5
     return call(own_kernel, "own_edges", out_shape, [], (meta, own_pos, rbf, rad))
 
@@ -531,7 +533,7 @@
         oh_gh[here, :] = onehot
         unit, dist = geometry(mm(onehot, ghpos[...]), mm(source, own_pos_ref[...]))
         unit_ref[here, :] = unit
-        pre, radial = radial_net(dist, spacing, rbf_ref, rad_ref)
+        pre, radial, _ = radial_net(dist, spacing, rbf_ref, rad_ref)
         pre_ref[here, :] = pre.astype(BF16)
         for degree in range(1, 5):
             radial_gh[degree][here, :] = radial[:, degree * CH : (degree + 1) * CH]
@@ -638,7 +640,8 @@
 
 
 def finish(
-    grad, mixed, near, dots, parts, pre, unit, spacing, radt_ref, rbft_ref, mix_t
+    grad, mixed, near, dots, parts, pre, unit, spacing, radt_ref, rbft_ref, mix_t,
+    slope=None,
 ):
     mixed = mixed.astype(F32)
     gate = jax.nn.sigmoid(mixed)
@@ -649,8 +652,9 @@
     pre = pre.astype(F32)
     logistic = jax.nn.sigmoid(pre)
     pre_grad = (hidden_grad * logistic * (1.0 + pre * (1.0 - logistic))).astype(BF16)
-    centred = centred_of(unit[:, 3:4], spacing, rbft_ref.shape[1])
-    slope = jnp.exp(-0.5 * centred * centred) * centred
+    if slope is None:
+        centred = centred_of(unit[:, 3:4], spacing, rbft_ref.shape[1])
+        slope = jnp.exp(-0.5 * centred * centred) * centred
     basis_grad = mm(pre_grad, rbft_ref[...])
     dist_grad = jnp.sum(basis_grad * slope, axis=1, keepdims=True) * (-1.0 / spacing)
     pull = unit * dist_grad
@@ -763,7 +767,7 @@
 
 
 def own_back_kernel(
-    steps, oh_own, pre_own, unit_own, radt_ref, rbft_ref, mix_ref, gs0_ref,
+    steps, oh_own, pre_own, unit_own, slope_ref, radt_ref, rbft_ref, mix_ref, gs0_ref,
     m0_ref, nf0_ref, dot_a, dot_c, *refs
 ):
     gr_own, (src_in, onto_in, src_out, onto_out) = refs[:PARTIALS], refs[PARTIALS:]
@@ -778,7 +782,7 @@
         pull, top, rest = finish(
             grad, m0_ref[rows, :], nf0_ref[rows, :], sum_of((dot_a, dot_c), rows),
             degree_parts(gr_own, rows), pre_own[rows, :], unit_own[rows, :], spacing, radt_ref,
-            rbft_ref, mix_t,
+            rbft_ref, mix_t, slope_ref[rows, :].astype(F32),
         )
         src += over_slots(pull, atoms)
         onehot = oh_own[rows, :]
@@ -897,7 +901,7 @@
     z0, own_pos, meta = hold((z0, own_pos, meta))
     block0 = jnp.concatenate([z0[0], block0, z0[1]], axis=2)
     y0 = neighbours_of(block0, "gy", 1)
-    oh_own, pre_own, unit_own, radt, rbft, home, *radial_own = own_stage(
+    oh_own, pre_own, unit_own, radt, rbft, home, slope, *radial_own = own_stage(
         meta, own_pos, rbf_weight, radial_weight
     )
     z1, y1_in, oh_own = hold((z1, y1_in, oh_own))
@@ -942,7 +946,7 @@
     dot_own_b, *gr_own_b = own_backward_stage(1, mix_weight, gs_b, gate_own, *own_b[:2])
     arrived, gs0, dot_own_b = hold((arrived, gs0, dot_own_b))
     mid, from_low, from_high = give_back_y(mid + arrived)
-    back = (oh_own, pre_own, unit_own, radt, rbft, mix_weight, gs0, m0_own, nf0_own)
+    back = (oh_own, pre_own, unit_own, slope, radt, rbft, mix_weight, gs0, m0_own, nf0_own)
     back += (dot_own_a, dot_own_b, *gr_own_a, *gr_own_b)
     src, onto = own_back_stage(range(2), *back, src, onto)
     from_low, from_high, src = hold((from_low, from_high, src))

time: 64.7 us -> 64.7 us (level)
  transfers between devices with their start and end apart: 19 -> 19, of which waited for: 9 -> 8; matrix products, arithmetic and copies ran while one was open for 1% -> 1% of each run, Pallas kernels for 31% -> 30%
where the time goes in v18:
time: 64.7 us; the launch traced here: 64.5 us
  Pallas kernels  27.5 us (43%)
  starting transfers between devices  27.5 us (43%)
  waiting for transfers between devices  5.4 us (8%)
  local copies, waits for them, and re-layouts  1.97 us (3%)
  other arithmetic  1.15 us (2%)
  between operations  0.92 us (1%)
    pallas_call x13, Pallas kernels, call(): pl.pallas_call(kernel, out_shape=out_shape, in_specs=specs or [pl.BlockSp...  27.5 us
    ppermute x6, starting transfers between devices, neighbours_of(): after = lax.ppermute(lax.slice_in_dim(block, 0, 1, axis=dim), axis, down)  11.9 us
    ppermute x6, starting transfers between devices, neighbours_of(): lax.ppermute(lax.slice_in_dim(block, length - 1, length, axis=dim), axis,...  5.57 us
    ppermute x2, starting transfers between devices, give_back_y(): return (mid, lax.ppermute(mid, 'gy', up), lax.ppermute(mid, 'gy', down))  3.91 us
    ppermute x2, starting transfers between devices, neighbours_of(): other = lax.ppermute(block, axis, up)  3.13 us
    ppermute x6, waiting for transfers between devices, neighbours_of(): lax.ppermute(lax.slice_in_dim(block, length - 1, length, axis=dim), axis,...  2.22 us
    unnamed x19, local copies, waits for them, and re-layouts  1.73 us
    ppermute x6, waiting for transfers between devices, neighbours_of(): after = lax.ppermute(lax.slice_in_dim(block, 0, 1, axis=dim), axis, down)  1.64 us
  transfers between devices with their start and end apart: 19, of which 8 were waited for; matrix products, arithmetic and copies ran while one was open for 1% of the time, Pallas kernels for 30%

profile of v18, /device:TPU:0, one launch (start us, length us, event | category | flops | bytes accessed | tf_op | source)
XLA Modules:
  0.0 64.5 jit_solution(17491390234258551926)
XLA Ops:
  3.4 3.0 %collective-permute-start.3 = (bf16[2,2,2,8,1280]{4,3,2,1,0:T(8,128)(2,1)S(1)}, bf16[2,2,2,8,1280]{4,3,2,1,0:T(8,128)(2,1)S(1)}, u32[]{:S(2)}, u32[]{:S(2)}) collective-permute-start(bf16[2,2,2,8,1280]{4,3,2,1,0:T(8,128)(2,1)S(1)} %bitcast.41), channel_id=1, source_target_pairs={{0,1},{1,0},{2,3},{3,2},{4,5},{5,4},{6,7},{7,6},{8,9},{9,8},{10,11... | collective-permute-start | bytes 491528 | tf_op jit(solution)/shard_map/ppermute | solution.py:811
  6.8 2.1 %collective-permute-start.1 = (bf16[2,1,2,8,2048]{4,3,2,1,0:T(8,128)(2,1)S(1)}, bf16[2,1,2,8,2048]{4,3,2,1,0:T(8,128)(2,1)S(1)}, u32[]{:S(2)}, u32[]{:S(2)}) collective-permute-start(bf16[2,1,2,8,2048]{4,3,2,1,0:T(8,128)(2,1)S(1)} %get-tuple-element.203), channel_id=1, source_target_pairs={{0,2},{2,4},{4,6},{6,0},{1,3},{3,5},{5,7},{7,1},{8,10},{10,12},{12... | collective-permute-start | bytes 393224 | tf_op jit(solution)/shard_map/ppermute | solution.py:816
  8.9 2.1 %collective-permute-start.2 = (bf16[2,1,2,8,2048]{4,3,2,1,0:T(8,128)(2,1)S(1)}, bf16[2,1,2,8,2048]{4,3,2,1,0:T(8,128)(2,1)S(1)}, u32[]{:S(2)}, u32[]{:S(2)}) collective-permute-start(bf16[2,1,2,8,2048]{4,3,2,1,0:T(8,128)(2,1)S(1)} %get-tuple-element.202), channel_id=1, source_target_pairs={{2,0},{4,2},{6,4},{0,6},{3,1},{5,3},{7,5},{1,7},{10,8},{12,10},{14... | collective-permute-start | bytes 393224 | tf_op jit(solution)/shard_map/ppermute | solution.py:817
  11.6 2.2 %collective-permute-start.6 = (bf16[2,1,4,8,1280]{4,3,2,1,0:T(8,128)(2,1)S(1)}, bf16[2,1,4,8,1280]{4,3,2,1,0:T(8,128)(2,1)S(1)}, u32[]{:S(2)}, u32[]{:S(2)}) collective-permute-start(bf16[2,1,4,8,1280]{4,3,2,1,0:T(8,128)(2,1)S(1)} %get-tuple-element.199), channel_id=1, source_target_pairs={{0,2},{2,4},{4,6},{6,0},{1,3},{3,5},{5,7},{7,1},{8,10},{10,12},{12... | collective-permute-start | bytes 491528 | tf_op jit(solution)/shard_map/ppermute | solution.py:816
  13.7 2.1 %collective-permute-start.7 = (bf16[2,1,4,8,1280]{4,3,2,1,0:T(8,128)(2,1)S(1)}, bf16[2,1,4,8,1280]{4,3,2,1,0:T(8,128)(2,1)S(1)}, u32[]{:S(2)}, u32[]{:S(2)}) collective-permute-start(bf16[2,1,4,8,1280]{4,3,2,1,0:T(8,128)(2,1)S(1)} %get-tuple-element.198), channel_id=1, source_target_pairs={{2,0},{4,2},{6,4},{0,6},{3,1},{5,3},{7,5},{1,7},{10,8},{12,10},{14... | collective-permute-start | bytes 491528 | tf_op jit(solution)/shard_map/ppermute | solution.py:817
  15.8 2.9 %own_edges.1 = (bf16[1024,64]{1,0:T(8,128)(2,1)S(1)}, bf16[1024,128]{1,0:T(8,128)(2,1)S(1)}, f32[1024,128]{1,0:T(8,128)S(1)}, bf16[640,128]{1,0:T(8,128)(2,1)S(1...) custom-call(f32[64,128]{1,0:T(8,128)S(1)} %get-tuple-element.100.met, ...), custom_call_target="tpu_custom_call" | custom-call | flops 1024 | bytes 1024 | tf_op jit(solution)/shard_map/own_edges/pallas_call | solution.py:57
  19.4 1.7 %collective-permute-start.5 = (bf16[1,2,4,8,2048]{4,3,2,1,0:T(8,128)(2,1)S(1)}, bf16[1,2,4,8,2048]{4,3,2,1,0:T(8,128)(2,1)S(1)}, u32[]{:S(2)}, u32[]{:S(2)}) collective-permute-start(bf16[1,2,4,8,2048]{4,3,2,1,0:T(8,128)(2,1)S(1)} %get-tuple-element.196), channel_id=1, source_target_pairs={{8,0},{16,8},{24,16},{0,24},{9,1},{17,9},{25,17},{1,25},{10,2},{18... | collective-permute-start | bytes 786440 | tf_op jit(solution)/shard_map/ppermute | solution.py:817
  21.1 1.5 %own_forward_a.1 = (bf16[1024,128]{1,0:T(8,128)(2,1)S(1)}, bf16[1024,128]{1,0:T(8,128)(2,1)S(1)}, bf16[1024,128]{1,0:T(8,128)(2,1)S(1)}, f32[64,128]{1,0:T(8,128...) custom-call(bf16[64,3200]{1,0:T(8,128)(2,1)S(1)} %bitcast.25, ...), custom_call_target="tpu_custom_call" | custom-call | flops 1024 | bytes 1024 | tf_op jit(solution)/shard_map/own_forward_a/pallas_call | solution.py:57
  23.4 1.7 %collective-permute-start.9 = (bf16[1,4,4,8,1280]{4,3,2,1,0:T(8,128)(2,1)S(1)}, bf16[1,4,4,8,1280]{4,3,2,1,0:T(8,128)(2,1)S(1)}, u32[]{:S(2)}, u32[]{:S(2)}) collective-permute-start(bf16[1,4,4,8,1280]{4,3,2,1,0:T(8,128)(2,1)S(1)} %get-tuple-element.192), channel_id=1, source_target_pairs={{8,0},{16,8},{24,16},{0,24},{9,1},{17,9},{25,17},{1,25},{10,2},{18... | collective-permute-start | bytes 983048 | tf_op jit(solution)/shard_map/ppermute | solution.py:817
  25.2 1.2 %collective-permute-start.10 = (bf16[2,1,2,8,2048]{4,3,2,1,0:T(8,128)(2,1)S(1)}, bf16[2,1,2,8,2048]{4,3,2,1,0:T(8,128)(2,1)S(1)}, u32[]{:S(2)}, u32[]{:S(2)}) collective-permute-start(bf16[2,1,2,8,2048]{4,3,2,1,0:T(8,128)(2,1)S(1)} %get-tuple-element.201), channel_id=1, source_target_pairs={{0,2},{2,4},{4,6},{6,0},{1,3},{3,5},{5,7},{7,1},{8,10},{10,12},{12... | collective-permute-start | bytes 393224 | tf_op jit(solution)/shard_map/ppermute | solution.py:816
  26.4 2.7 %collective-permute-start.11 = (bf16[2,1,2,8,2048]{4,3,2,1,0:T(8,128)(2,1)S(1)}, bf16[2,1,2,8,2048]{4,3,2,1,0:T(8,128)(2,1)S(1)}, u32[]{:S(2)}, u32[]{:S(2)}) collective-permute-start(bf16[2,1,2,8,2048]{4,3,2,1,0:T(8,128)(2,1)S(1)} %get-tuple-element.200), channel_id=1, source_target_pairs={{2,0},{4,2},{6,4},{0,6},{3,1},{5,3},{7,5},{1,7},{10,8},{12,10},{14... | collective-permute-start | bytes 393224 | tf_op jit(solution)/shard_map/ppermute | solution.py:817
  29.0 2.5 %own_forward_b.1 = (bf16[1024,2048]{1,0:T(8,128)(2,1)S(1)}, bf16[1024,2048]{1,0:T(8,128)(2,1)S(1)}, f32[64,2048]{1,0:T(8,128)S(1)}) custom-call(bf16[64,3200]{1,0:T(8,128)(2,1)S(1)} %bitcast.26, bf16[5,128,128]{2,1,0:T(8,128)(2,1)S(1)} %copy-done.2, bf16[1024,64]{1,0:T(8,128)(2,1)S(1)} %get-tuple-element.107.refs_2_.oh_own, ...), custom_call_target="tpu_custom_call" | custom-call | flops 1024 | bytes 1024 | tf_op jit(solution)/shard_map/own_forward_b/pallas_call | solution.py:57
  31.5 1.9 %collective-permute-done.10 = bf16[2,1,2,8,2048]{4,3,2,1,0:T(8,128)(2,1)S(1)} collective-permute-done((bf16[2,1,2,8,2048]{4,3,2,1,0:T(8,128)(2,1)S(1)}, bf16[2,1,2,8,2048]{4,3,2,1,0:T(8,128)(2,1)S(1)}, u32[]{:S(2)}, u32[]{:S(2)}) %collective-permute-start.10) | collective-permute-done | bytes 131104 | tf_op jit(solution)/shard_map/ppermute | solution.py:816
  34.3 1.6 %collective-permute-start.13 = (bf16[1,2,4,8,2048]{4,3,2,1,0:T(8,128)(2,1)S(1)}, bf16[1,2,4,8,2048]{4,3,2,1,0:T(8,128)(2,1)S(1)}, u32[]{:S(2)}, u32[]{:S(2)}) collective-permute-start(bf16[1,2,4,8,2048]{4,3,2,1,0:T(8,128)(2,1)S(1)} %get-tuple-element.194), channel_id=1, source_target_pairs={{8,0},{16,8},{24,16},{0,24},{9,1},{17,9},{25,17},{1,25},{10,2},{18... | collective-permute-start | bytes 786440 | tf_op jit(solution)/shard_map/ppermute | solution.py:817
  35.9 3.3 %ghost_start.1 = (bf16[64,128]{1,0:T(8,128)(2,1)S(1)}, bf16[1024,512]{1,0:T(8,128)(2,1)S(1)}, bf16[1024,64]{1,0:T(8,128)(2,1)S(1)}, bf16[64,1024]{1,0:T(8,128)(2...) custom-call(bf16[128,1280]{1,0:T(8,128)(2,1)S(1)} %bitcast.37, ...), custom_call_target="tpu_custom_call" | custom-call | flops 1024 | bytes 1024 | tf_op jit(solution)/shard_map/ghost_start/pallas_call | solution.py:57
  39.2 4.1 %pairs_a.1 = (bf16[64,1024]{1,0:T(8,128)(2,1)S(1)}, f32[64,128]{1,0:T(8,128)S(1)}, bf16[64,1024]{1,0:T(8,128)(2,1)}, bf16[1024,128]{1,0:T(8,128)(2,1)S(1)}, bf16...) custom-call(bf16[128,1280]{1,0:T(8,128)(2,1)S(1)} %bitcast.38, ...), custom_call_target="tpu_custom_call" | custom-call | flops 1024 | bytes 1024 | tf_op jit(solution)/shard_map/pairs_a/pallas_call | solution.py:57
  43.8 6.7 %third_group.1 = (bf16[64,3200]{1,0:T(8,128)(2,1)}, f32[1,64]{1,0:T(1,128)}, f32[64,128]{1,0:T(8,128)S(1)}, f32[8,64]{1,0:T(8,128)S(1)}, f32[8,128]{1,0:T(8,128)...) custom-call(bf16[64,2048]{1,0:T(8,128)(2,1)S(1)} %bitcast.44, ...), custom_call_target="tpu_custom_call" | custom-call | flops 1024 | bytes 1024 | tf_op jit(solution)/shard_map/third_group/pallas_call | solution.py:57
  51.1 1.2 %collective-permute-start.15 = (f32[8,128]{1,0:T(8,128)S(1)}, f32[8,128]{1,0:T(8,128)S(1)}, u32[]{:S(2)}, u32[]{:S(2)}) collective-permute-start(f32[8,128]{1,0:T(8,128)S(1)} %get-tuple-element.161), channel_id=1, source_target_pairs={{8,0},{16,8},{24,16},{0,24},{9,1},{17,9},{25,17},{1,25},{10,2},{18... | collective-permute-start | bytes 12296 | tf_op jit(solution)/shard_map/ppermute | solution.py:860
  52.2 2.2 %own_backward_b.1 = (bf16[1024,128]{1,0:T(8,128)(2,1)S(1)}, bf16[1024,128]{1,0:T(8,128)(2,1)S(1)}, bf16[1024,128]{1,0:T(8,128)(2,1)S(1)}) custom-call(bf16[5,128,128]{2,1,0:T(8,128)(2,1)S(1)} %copy-done.2, bf16[64,2048]{1,0:T(8,128)(2,1)S(1)} %get-tuple-element.162.gs_ref, bf16[1024,128]{1,0:T(8,128)(2,1)S(1)} %get-tuple-element.121.refs_8_.refs_12_.gate_ref, ...), custom_call_target="tpu_custom_call" | custom-call | flops 1024 | bytes 1024 | tf_op jit(solution)/shard_map/own_backward_b/pallas_call | solution.py:57
  54.4 1.3 %collective-permute-start.16 = (f32[8,256]{1,0:T(8,128)S(1)}, f32[8,256]{1,0:T(8,128)S(1)}, u32[]{:S(2)}, u32[]{:S(2)}) collective-permute-start(f32[8,256]{1,0:T(8,128)S(1)} %add.3.mid_ref), channel_id=1, source_target_pairs={{0,2},{2,4},{4,6},{6,0},{1,3},{3,5},{5,7},{7,1},{8,10},{10,12},{12... | collective-permute-start | bytes 24584 | tf_op jit(solution)/shard_map/ppermute | solution.py:866
  55.7 2.6 %collective-permute-start.17 = (f32[8,256]{1,0:T(8,128)S(1)}, f32[8,256]{1,0:T(8,128)S(1)}, u32[]{:S(2)}, u32[]{:S(2)}) collective-permute-start(f32[8,256]{1,0:T(8,128)S(1)} %add.3.mid_ref), channel_id=1, source_target_pairs={{2,0},{4,2},{6,4},{0,6},{3,1},{5,3},{7,5},{1,7},{10,8},{12,10},{14... | collective-permute-start | bytes 24584 | tf_op jit(solution)/shard_map/ppermute | solution.py:866
  58.3 1.5 %own_back.2 = (f32[64,128]{1,0:T(8,128)S(1)}, f32[8,64]{1,0:T(8,128)S(1)}) custom-call(bf16[1024,64]{1,0:T(8,128)(2,1)S(1)} %get-tuple-element.107.refs_2_.oh_own, bf16[1024,128]{1,0:T(8,128)(2,1)S(1)} %get-tuple-element.167.pre_own, f32[1024,128]{1,0:T(8,128)S(1)} %get-tuple-element.168.unit_own, bf16[1024,512]{1,0:T(8,128)(2,1)S(1)} %get-tuple-element.169.slope_ref, ...), custom_call_target="tpu_custom_call" | custom-call | flops 1024 | bytes 1024 | tf_op jit(solution)/shard_map/own_back/pallas_call | solution.py:57
  60.0 1.3 %collective-permute-start.18 = (f32[8,256]{1,0:T(8,128)S(1)}, f32[8,256]{1,0:T(8,128)S(1)}, u32[]{:S(2)}, u32[]{:S(2)}) collective-permute-start(f32[8,256]{1,0:T(8,128)S(1)} %fold.1.mid_ref), channel_id=1, source_target_pairs={{0,1},{1,0},{2,3},{3,2},{4,5},{5,4},{6,7},{7,6},{8,9},{9,8},{10,11... | collective-permute-start | bytes 24584 | tf_op jit(solution)/shard_map/ppermute | solution.py:875
  61.3 1.5 %own_back.3 = (f32[64,128]{1,0:T(8,128)S(1)}, f32[8,64]{1,0:T(8,128)S(1)}) custom-call(bf16[1024,64]{1,0:T(8,128)(2,1)S(1)} %get-tuple-element.107.refs_2_.oh_own, bf16[1024,128]{1,0:T(8,128)(2,1)S(1)} %get-tuple-element.167.pre_own, f32[1024,128]{1,0:T(8,128)S(1)} %get-tuple-element.168.unit_own, bf16[1024,512]{1,0:T(8,128)(2,1)S(1)} %get-tuple-element.169.slope_ref, ...), custom_call_target="tpu_custom_call" | custom-call | flops 1024 | bytes 1024 | tf_op jit(solution)/shard_map/own_back/pallas_call | solution.py:57
  (64 shorter events, 8.8 us)
Async XLA Ops:
  3.4 8.1 %collective-permute-start.3 = (bf16[2,2,2,8,1280]{4,3,2,1,0:T(8,128)(2,1)S(1)}, bf16[2,2,2,8,1280]{4,3,2,1,0:T(8,128)(2,1)S(1)}, u32[]{:S(2)}, u32[]{:S(2)}) collective-permute-start(bf16[2,2,2,8,1280]{4,3,2,1,0:T(8,128)(2,1)S(1)} %bitcast.41), channel_id=1, source_target_pairs={{0,1},{1,0},{2,3},{3,2},{4,5},{5,4},{6,7},{7,6},{8,9},{9,8},{10,11... | collective-permute-start | bytes 491528 | tf_op jit(solution)/shard_map/ppermute | solution.py:811
  6.7 14.5 %copy-start.1 = (bf16[1,1,1,64,3200]{4,3,2,1,0:T(8,128)(2,1)S(1)}, bf16[1,1,1,64,3200]{4,3,2,1,0:T(8,128)(2,1)}, u32[]{:S(2)}) copy-start(bf16[1,1,1,64,3200]{4,3,2,1,0:T(8,128)(2,1)} %param.11) | copy-start | bytes 1228804
  6.7 14.5 %copy-start.2 = (bf16[5,128,128]{2,1,0:T(8,128)(2,1)S(1)}, bf16[5,128,128]{2,1,0:T(8,128)(2,1)}, u32[]{:S(2)}) copy-start(bf16[5,128,128]{2,1,0:T(8,128)(2,1)} %mix_ref.9) | copy-start | bytes 491524
  6.7 12.1 %collective-permute-start = (bf16[2,2,2,8,2048]{4,3,2,1,0:T(8,128)(2,1)S(1)}, bf16[2,2,2,8,2048]{4,3,2,1,0:T(8,128)(2,1)S(1)}, u32[]{:S(2)}, u32[]{:S(2)}) collective-permute-start(bf16[2,2,2,8,2048]{4,3,2,1,0:T(8,128)(2,1)S(1)} %bitcast.33), channel_id=1, source_target_pairs={{0,1},{1,0},{2,3},{3,2},{4,5},{5,4},{6,7},{7,6},{8,9},{9,8},{10,11... | collective-permute-start | bytes 786440 | tf_op jit(solution)/shard_map/ppermute | solution.py:811
  6.8 12.0 %collective-permute-start.1 = (bf16[2,1,2,8,2048]{4,3,2,1,0:T(8,128)(2,1)S(1)}, bf16[2,1,2,8,2048]{4,3,2,1,0:T(8,128)(2,1)S(1)}, u32[]{:S(2)}, u32[]{:S(2)}) collective-permute-start(bf16[2,1,2,8,2048]{4,3,2,1,0:T(8,128)(2,1)S(1)} %get-tuple-element.203), channel_id=1, source_target_pairs={{0,2},{2,4},{4,6},{6,0},{1,3},{3,5},{5,7},{7,1},{8,10},{10,12},{12... | collective-permute-start | bytes 393224 | tf_op jit(solution)/shard_map/ppermute | solution.py:816
  8.9 10.3 %collective-permute-start.2 = (bf16[2,1,2,8,2048]{4,3,2,1,0:T(8,128)(2,1)S(1)}, bf16[2,1,2,8,2048]{4,3,2,1,0:T(8,128)(2,1)S(1)}, u32[]{:S(2)}, u32[]{:S(2)}) collective-permute-start(bf16[2,1,2,8,2048]{4,3,2,1,0:T(8,128)(2,1)S(1)} %get-tuple-element.202), channel_id=1, source_target_pairs={{2,0},{4,2},{6,4},{0,6},{3,1},{5,3},{7,5},{1,7},{10,8},{12,10},{14... | collective-permute-start | bytes 393224 | tf_op jit(solution)/shard_map/ppermute | solution.py:817
  11.6 11.1 %collective-permute-start.6 = (bf16[2,1,4,8,1280]{4,3,2,1,0:T(8,128)(2,1)S(1)}, bf16[2,1,4,8,1280]{4,3,2,1,0:T(8,128)(2,1)S(1)}, u32[]{:S(2)}, u32[]{:S(2)}) collective-permute-start(bf16[2,1,4,8,1280]{4,3,2,1,0:T(8,128)(2,1)S(1)} %get-tuple-element.199), channel_id=1, source_target_pairs={{0,2},{2,4},{4,6},{6,0},{1,3},{3,5},{5,7},{7,1},{8,10},{10,12},{12... | collective-permute-start | bytes 491528 | tf_op jit(solution)/shard_map/ppermute | solution.py:816
  13.7 9.4 %collective-permute-start.7 = (bf16[2,1,4,8,1280]{4,3,2,1,0:T(8,128)(2,1)S(1)}, bf16[2,1,4,8,1280]{4,3,2,1,0:T(8,128)(2,1)S(1)}, u32[]{:S(2)}, u32[]{:S(2)}) collective-permute-start(bf16[2,1,4,8,1280]{4,3,2,1,0:T(8,128)(2,1)S(1)} %get-tuple-element.198), channel_id=1, source_target_pairs={{2,0},{4,2},{6,4},{0,6},{3,1},{5,3},{7,5},{1,7},{10,8},{12,10},{14... | collective-permute-start | bytes 491528 | tf_op jit(solution)/shard_map/ppermute | solution.py:817
  19.3 7.0 %collective-permute-start.4 = (bf16[1,2,4,8,2048]{4,3,2,1,0:T(8,128)(2,1)S(1)}, bf16[1,2,4,8,2048]{4,3,2,1,0:T(8,128)(2,1)S(1)}, u32[]{:S(2)}, u32[]{:S(2)}) collective-permute-start(bf16[1,2,4,8,2048]{4,3,2,1,0:T(8,128)(2,1)S(1)} %get-tuple-element.197), channel_id=1, source_target_pairs={{0,8},{8,16},{16,24},{24,0},{1,9},{9,17},{17,25},{25,1},{2,10},{10... | collective-permute-start | bytes 786440 | tf_op jit(solution)/shard_map/ppermute | solution.py:816
  19.4 9.7 %collective-permute-start.5 = (bf16[1,2,4,8,2048]{4,3,2,1,0:T(8,128)(2,1)S(1)}, bf16[1,2,4,8,2048]{4,3,2,1,0:T(8,128)(2,1)S(1)}, u32[]{:S(2)}, u32[]{:S(2)}) collective-permute-start(bf16[1,2,4,8,2048]{4,3,2,1,0:T(8,128)(2,1)S(1)} %get-tuple-element.196), channel_id=1, source_target_pairs={{8,0},{16,8},{24,16},{0,24},{9,1},{17,9},{25,17},{1,25},{10,2},{18... | collective-permute-start | bytes 786440 | tf_op jit(solution)/shard_map/ppermute | solution.py:817
  23.1 12.7 %copy-start.3 = (bf16[5,128,128]{2,1,0:T(8,128)(2,1)S(1)}, bf16[5,128,128]{2,1,0:T(8,128)(2,1)}, u32[]{:S(2)}) copy-start(bf16[5,128,128]{2,1,0:T(8,128)(2,1)} %out_ref.3) | copy-start | bytes 491524
  23.1 12.7 %copy-start.8 = (f32[128]{0:T(128)S(1)}, f32[128]{0:T(128)}, u32[]{:S(2)}) copy-start(f32[128]{0:T(128)} %param.20) | copy-start | bytes 1540
  23.3 15.9 %copy-start.6 = (f32[4,128]{1,0:T(4,128)S(1)}, f32[4,128]{1,0:T(4,128)}, u32[]{:S(2)}) copy-start(f32[4,128]{1,0:T(4,128)} %nw_ref.1) | copy-start | bytes 6148
  23.3 10.8 %collective-permute-start.8 = (bf16[1,4,4,8,1280]{4,3,2,1,0:T(8,128)(2,1)S(1)}, bf16[1,4,4,8,1280]{4,3,2,1,0:T(8,128)(2,1)S(1)}, u32[]{:S(2)}, u32[]{:S(2)}) collective-permute-start(bf16[1,4,4,8,1280]{4,3,2,1,0:T(8,128)(2,1)S(1)} %get-tuple-element.193), channel_id=1, source_target_pairs={{0,8},{8,16},{16,24},{24,0},{1,9},{9,17},{17,25},{25,1},{2,10},{10... | collective-permute-start | bytes 983048 | tf_op jit(solution)/shard_map/ppermute | solution.py:816
  23.4 10.8 %collective-permute-start.9 = (bf16[1,4,4,8,1280]{4,3,2,1,0:T(8,128)(2,1)S(1)}, bf16[1,4,4,8,1280]{4,3,2,1,0:T(8,128)(2,1)S(1)}, u32[]{:S(2)}, u32[]{:S(2)}) collective-permute-start(bf16[1,4,4,8,1280]{4,3,2,1,0:T(8,128)(2,1)S(1)} %get-tuple-element.192), channel_id=1, source_target_pairs={{8,0},{16,8},{24,16},{0,24},{9,1},{17,9},{25,17},{1,25},{10,2},{18... | collective-permute-start | bytes 983048 | tf_op jit(solution)/shard_map/ppermute | solution.py:817
  25.2 8.2 %collective-permute-start.10 = (bf16[2,1,2,8,2048]{4,3,2,1,0:T(8,128)(2,1)S(1)}, bf16[2,1,2,8,2048]{4,3,2,1,0:T(8,128)(2,1)S(1)}, u32[]{:S(2)}, u32[]{:S(2)}) collective-permute-start(bf16[2,1,2,8,2048]{4,3,2,1,0:T(8,128)(2,1)S(1)} %get-tuple-element.201), channel_id=1, source_target_pairs={{0,2},{2,4},{4,6},{6,0},{1,3},{3,5},{5,7},{7,1},{8,10},{10,12},{12... | collective-permute-start | bytes 393224 | tf_op jit(solution)/shard_map/ppermute | solution.py:816
  26.4 7.8 %collective-permute-start.11 = (bf16[2,1,2,8,2048]{4,3,2,1,0:T(8,128)(2,1)S(1)}, bf16[2,1,2,8,2048]{4,3,2,1,0:T(8,128)(2,1)S(1)}, u32[]{:S(2)}, u32[]{:S(2)}) collective-permute-start(bf16[2,1,2,8,2048]{4,3,2,1,0:T(8,128)(2,1)S(1)} %get-tuple-element.200), channel_id=1, source_target_pairs={{2,0},{4,2},{6,4},{0,6},{3,1},{5,3},{7,5},{1,7},{10,8},{12,10},{14... | collective-permute-start | bytes 393224 | tf_op jit(solution)/shard_map/ppermute | solution.py:817
  34.3 9.2 %collective-permute-start.13 = (bf16[1,2,4,8,2048]{4,3,2,1,0:T(8,128)(2,1)S(1)}, bf16[1,2,4,8,2048]{4,3,2,1,0:T(8,128)(2,1)S(1)}, u32[]{:S(2)}, u32[]{:S(2)}) collective-permute-start(bf16[1,2,4,8,2048]{4,3,2,1,0:T(8,128)(2,1)S(1)} %get-tuple-element.194), channel_id=1, source_target_pairs={{8,0},{16,8},{24,16},{0,24},{9,1},{17,9},{25,17},{1,25},{10,2},{18... | collective-permute-start | bytes 786440 | tf_op jit(solution)/shard_map/ppermute | solution.py:817
  35.9 7.9 %collective-permute-start.12 = (bf16[1,2,4,8,2048]{4,3,2,1,0:T(8,128)(2,1)S(1)}, bf16[1,2,4,8,2048]{4,3,2,1,0:T(8,128)(2,1)S(1)}, u32[]{:S(2)}, u32[]{:S(2)}) collective-permute-start(bf16[1,2,4,8,2048]{4,3,2,1,0:T(8,128)(2,1)S(1)} %get-tuple-element.195), channel_id=1, source_target_pairs={{0,8},{8,16},{16,24},{24,0},{1,9},{9,17},{17,25},{25,1},{2,10},{10... | collective-permute-start | bytes 786440 | tf_op jit(solution)/shard_map/ppermute | solution.py:816
  50.5 3.9 %collective-permute-start.14 = (f32[8,128]{1,0:T(8,128)S(1)}, f32[8,128]{1,0:T(8,128)S(1)}, u32[]{:S(2)}, u32[]{:S(2)}) collective-permute-start(f32[8,128]{1,0:T(8,128)S(1)} %get-tuple-element.160), channel_id=1, source_target_pairs={{0,8},{8,16},{16,24},{24,0},{1,9},{9,17},{17,25},{25,1},{2,10},{10... | collective-permute-start | bytes 12296 | tf_op jit(solution)/shard_map/ppermute | solution.py:859
  51.1 3.3 %collective-permute-start.15 = (f32[8,128]{1,0:T(8,128)S(1)}, f32[8,128]{1,0:T(8,128)S(1)}, u32[]{:S(2)}, u32[]{:S(2)}) collective-permute-start(f32[8,128]{1,0:T(8,128)S(1)} %get-tuple-element.161), channel_id=1, source_target_pairs={{8,0},{16,8},{24,16},{0,24},{9,1},{17,9},{25,17},{1,25},{10,2},{18... | collective-permute-start | bytes 12296 | tf_op jit(solution)/shard_map/ppermute | solution.py:860
  54.4 5.5 %collective-permute-start.16 = (f32[8,256]{1,0:T(8,128)S(1)}, f32[8,256]{1,0:T(8,128)S(1)}, u32[]{:S(2)}, u32[]{:S(2)}) collective-permute-start(f32[8,256]{1,0:T(8,128)S(1)} %add.3.mid_ref), channel_id=1, source_target_pairs={{0,2},{2,4},{4,6},{6,0},{1,3},{3,5},{5,7},{7,1},{8,10},{10,12},{12... | collective-permute-start | bytes 24584 | tf_op jit(solution)/shard_map/ppermute | solution.py:866
  55.7 4.2 %collective-permute-start.17 = (f32[8,256]{1,0:T(8,128)S(1)}, f32[8,256]{1,0:T(8,128)S(1)}, u32[]{:S(2)}, u32[]{:S(2)}) collective-permute-start(f32[8,256]{1,0:T(8,128)S(1)} %add.3.mid_ref), channel_id=1, source_target_pairs={{2,0},{4,2},{6,4},{0,6},{3,1},{5,3},{7,5},{1,7},{10,8},{12,10},{14... | collective-permute-start | bytes 24584 | tf_op jit(solution)/shard_map/ppermute | solution.py:866
  60.0 3.7 %collective-permute-start.18 = (f32[8,256]{1,0:T(8,128)S(1)}, f32[8,256]{1,0:T(8,128)S(1)}, u32[]{:S(2)}, u32[]{:S(2)}) collective-permute-start(f32[8,256]{1,0:T(8,128)S(1)} %fold.1.mid_ref), channel_id=1, source_target_pairs={{0,1},{1,0},{2,3},{3,2},{4,5},{5,4},{6,7},{7,6},{8,9},{9,8},{10,11... | collective-permute-start | bytes 24584 | tf_op jit(solution)/shard_map/ppermute | solution.py:875
  (4 other events, 20.5 us)
